TPU v7x, 32 devices: a whole 2x2x4 slice. The times are simulated.
32 devices in a mesh: parts: 2 (over x), blk: 8 (over z, y), helper: 2 (over core).
Axes of the slice: x: 2, y: 2, z: 4, core: 2. Of those that a mesh axis runs over, the one named last changes fastest.
Arguments:
- queries: bfloat16 [16384, 768], P(('parts', 'blk', 'helper')), parts along dimension 0, may hold values from -6 to 6
- query_block_cluster: int32 [128], P(('parts', 'blk', 'helper')), parts along dimension 0, may hold values from 0 to 63
- block_count: int32 [32], P(('parts', 'blk', 'helper')), parts along dimension 0, may hold values from 1 to 4, 40 in all
- references: bfloat16 [8192, 768], P(('parts', 'blk')), parts along dimension 0, may hold values from -6 to 6
- ref_cluster: int32 [8192], P(('parts', 'blk')), parts along dimension 0, may hold values from 0 to 63
- ref_rows: int32 [16], P(('parts', 'blk')), parts along dimension 0, may hold values from 1 to 512, 3072 in all
- cluster_beta: float32 [128], P('parts'), parts along dimension 0, may hold values from 0.5 to 2
- cluster_member_count: int32 [128], P('parts'), parts along dimension 0, may hold values from 24 to 97
Outputs:
- log_density: float32 [16384], P(('parts', 'blk', 'helper')), parts along dimension 0
There are 2 independent parts, one for each index of `parts`. A program takes and returns all parts, laid end to end along the dimension named above; each array names one. Nothing has to cross between parts.
All inputs are finite; a program needn't handle non-finite values. No bound on the sum of `block_count` or of `ref_rows` on one device may be relied on, other than what follows from the above.
Results may differ from a plain program's by a relative error of at most 0.0003.
Values may be sent and summed in bfloat16 or wider, within the bound.
No kernel may reach another device: no remote copies, remote signals or barrier semaphores. Data moves between devices by JAX's collectives and lax.ppermute only.
A program may use at most 64 MiB of HBM per device.

v0:
```python
import math

import jax
import jax.numpy as jnp
from jax import lax
from jax.sharding import PartitionSpec as P


def from_behind(shard, axis, by):
    length = lax.axis_size(axis)
    return lax.ppermute(shard, axis, [(i, (i + by) % length) for i in range(length)])


def table_lookup(table, keys):
    columns = jnp.arange(table.shape[0], dtype=jnp.int32)
    onehot = keys[:, None] == columns[None, :]
    return jnp.sum(jnp.where(onehot, table[None, :].astype(jnp.float32), 0.0), axis=1)


def score_prefix(acc, live, embedding_blocks, block_ids, betas, device_portion, shard_ids):
    factor = 1.0 / math.sqrt(embedding_blocks.shape[2])
    shard_keys = shard_ids.astype(jnp.int32)
    most = embedding_blocks.shape[0]

    def make_branch(smoothing_width):

        def branch(switch_operand):
            if smoothing_width == 0:
                return switch_operand
            score = (
                jnp.einsum(
                    "neg,wg->new",
                    embedding_blocks[:smoothing_width],
                    device_portion,
                    preferred_element_type=jnp.float32,
                )
                * factor
            )
            beta = betas[:smoothing_width, None, None]
            same = block_ids[:smoothing_width, None, None] == shard_keys[None, None, :]
            weights = jnp.where(shard_keys[None, None, :] < 0, 0.0, jnp.where(same, 1.0, 0.0625))
            gaussian_kernel = weights * jnp.exp(beta * score - 0.5 * beta * beta)
            return switch_operand.at[:smoothing_width].add(jnp.sum(gaussian_kernel, axis=2))

        return branch

    branches = [make_branch(smoothing_width) for smoothing_width in range(most + 1)]
    return lax.switch(jnp.clip(live, 0, most), branches, acc)


def per_device(
    queries,
    query_block_cluster,
    block_count,
    references,
    ref_cluster,
    ref_rows,
    cluster_beta,
    cluster_member_count,
):
    nblk = lax.axis_size("blk")
    slot_count = query_block_cluster.shape[0]
    half_steps = slot_count // 2
    query_rows = queries.shape[0]
    rows_per_block = query_rows // slot_count
    kernel_spread_width = queries.shape[1]
    query_blocks = queries.reshape(slot_count, rows_per_block, kernel_spread_width)
    count = block_count[0]
    rows_live = jnp.arange(references.shape[0], dtype=jnp.int32) < ref_rows[0]
    own_ids = jnp.where(rows_live, ref_cluster, -1).astype(jnp.bfloat16)
    own_betas = table_lookup(cluster_beta, query_block_cluster)
    own_sizes = table_lookup(cluster_member_count, query_block_cluster)
    zeroed_totals = jnp.zeros((slot_count, rows_per_block), jnp.float32)
    zero_extra = jnp.zeros((half_steps, rows_per_block), jnp.float32)

    def work(accs, device_portion, shard_ids):
        first = score_prefix(
            accs[0], count, query_blocks, query_block_cluster, own_betas, device_portion, shard_ids
        )
        return (first, accs[1])

    accs = (zeroed_totals, zero_extra)

    def one_turn(turn, carry):
        device_portion, shard_ids, totals = carry
        totals = work(totals, device_portion, shard_ids)
        device_portion, shard_ids = from_behind((device_portion, shard_ids), "blk", 1)
        return (device_portion, shard_ids, totals)

    state = lax.fori_loop(0, nblk - 1, one_turn, (references, own_ids, accs))
    accs = work(state[2], state[0], state[1])
    totals = accs[0]
    density = jnp.log1p(totals / own_sizes[:, None])
    return density.reshape(query_rows)


def solution(mesh):
    in_specs = (
        P(("parts", "blk", "helper"), None),
        P(("parts", "blk", "helper")),
        P(("parts", "blk", "helper")),
        P(("parts", "blk"), None),
        P(("parts", "blk")),
        P(("parts", "blk")),
        P("parts"),
        P("parts"),
    )
    out_specs = P(("parts", "blk", "helper"))
    return jax.shard_map(
        per_device, mesh=mesh, in_specs=in_specs, out_specs=out_specs, check_vma=False
    )
```

profile of v0, /device:TPU:0, one launch (start us, length us, event | category | flops | bytes accessed | tf_op | source)
XLA Modules:
  0.0 150.4 jit_solution(7851131462556096369)
XLA Ops:
  3.6 145.4 %while.32 = (s32[]{:T(128)}, bf16[512,768]{1,0:T(8,128)(2,1)S(1)}, bf16[512]{0:T(512)(128)(2,1)S(1)}, f32[4,128]{1,0:T(4,128)S(1)}, s32[4]{0:T(128)S(1)}, /*inde...) while((s32[]{:T(128)}, bf16[512,768]{1,0:T(8,128)(2,1)S(1)}, ...), condition=%wide.region_11.12_spmd, body=%wide.region_1.11_spmd.sunk | while | flops 403709440 | bytes 6329717 | solution.py:90
  4.5 3.0 %collective-permute-start = (bf16[512,768]{1,0:T(8,128)(2,1)}, bf16[512,768]{1,0:T(8,128)(2,1)S(1)}, u32[]{:S(2)}, u32[]{:S(2)}) collective-permute-start(bf16[512,768]{1,0:T(8,128)(2,1)} %copy.25), channel_id=1, source_target_pairs={{0,2},{2,4},{4,6},{6,8},{8,10},{10,12},{12,14},{14,0},{1,3},{3,5},... | collective-permute-start | bytes 2359304 | tf_op jit(solution)/shard_map/while/body/eval_jaxpr/ppermute | solution.py:11
  8.1 1.5 %collective-permute-start.1 = (bf16[512]{0:T(512)(128)(2,1)}, bf16[512]{0:T(512)(128)(2,1)S(1)}, u32[]{:S(2)}, u32[]{:S(2)}) collective-permute-start(bf16[512]{0:T(512)(128)(2,1)} %copy.26), channel_id=1, source_target_pairs={{0,2},{2,4},{4,6},{6,8},{8,10},{10,12},{12,14},{14,0},{1,3},{3,5},... | collective-permute-start | bytes 3080 | tf_op jit(solution)/shard_map/while/body/eval_jaxpr/ppermute | solution.py:11
  9.6 3.2 %conditional.4 = (f32[4,128]{1,0:T(4,128)S(1)}) conditional(s32[]{:T(128)} %get-tuple-element.490, f32[4,128]{1,0:T(4,128)S(1)} %get-tuple-element.477, (f32[4,128]{1,0:T(4,128)S(1)}, bf16[512]{0:T(512)(128)(2,1)}, s32[4]{0:T(128)S(1)}, bf16[4,128,768]{2,1,0:T(8,128)(2,1)S(1)}, bf16[512,768]{1,0:T(8,128)(2,1)}, ...), branch_computations={%region_2.2_spmd, %region_3.4_spmd, %region_5.6_spmd, %region_7.8_... | conditional | flops 403709440 | bytes 1604712 | solution.py:48
  11.1 1.7 %fusion.9 = f32[2,128]{1,0:T(2,128)S(1)} fusion(bf16[4,128,768]{2,1,0:T(8,128)(2,1)S(1)} %get-tuple-element.332, bf16[512,768]{1,0:T(8,128)(2,1)} %get-tuple-element.333, f32[2]{0:T(128)S(1)} %get-tuple-element.405, f32[2]{0:T(128)S(1)} %get-tuple-element.404, f32[2,512]{1,0:T(2,128)S(1)} %fusion.11), kind=kOutput, calls=%fused_computation.15 | convolution fusion | flops 201850624 | bytes 1578000 | tf_op jit(solution)/shard_map/while/body/eval_jaxpr/cond/branch_2_fun/neg,wg->new/dot_general | solution.py:31
  12.8 15.6 %collective-permute-done.1 = bf16[512]{0:T(512)(128)(2,1)S(1)} collective-permute-done((bf16[512]{0:T(512)(128)(2,1)}, bf16[512]{0:T(512)(128)(2,1)S(1)}, u32[]{:S(2)}, u32[]{:S(2)}) %collective-permute-start.1) | collective-permute-done | bytes 1056 | tf_op jit(solution)/shard_map/while/body/eval_jaxpr/ppermute | solution.py:11
  30.9 3.2 %conditional.4 = (f32[4,128]{1,0:T(4,128)S(1)}) conditional(s32[]{:T(128)} %get-tuple-element.490, f32[4,128]{1,0:T(4,128)S(1)} %get-tuple-element.477, (f32[4,128]{1,0:T(4,128)S(1)}, bf16[512]{0:T(512)(128)(2,1)}, s32[4]{0:T(128)S(1)}, bf16[4,128,768]{2,1,0:T(8,128)(2,1)S(1)}, bf16[512,768]{1,0:T(8,128)(2,1)}, ...), branch_computations={%region_2.2_spmd, %region_3.4_spmd, %region_5.6_spmd, %region_7.8_... | conditional | flops 403709440 | bytes 1604712 | solution.py:48
  32.4 1.7 %fusion.9 = f32[2,128]{1,0:T(2,128)S(1)} fusion(bf16[4,128,768]{2,1,0:T(8,128)(2,1)S(1)} %get-tuple-element.332, bf16[512,768]{1,0:T(8,128)(2,1)} %get-tuple-element.333, f32[2]{0:T(128)S(1)} %get-tuple-element.405, f32[2]{0:T(128)S(1)} %get-tuple-element.404, f32[2,512]{1,0:T(2,128)S(1)} %fusion.11), kind=kOutput, calls=%fused_computation.15 | convolution fusion | flops 201850624 | bytes 1578000 | tf_op jit(solution)/shard_map/while/body/eval_jaxpr/cond/branch_2_fun/neg,wg->new/dot_general | solution.py:31
  34.1 16.8 %collective-permute-done.1 = bf16[512]{0:T(512)(128)(2,1)S(1)} collective-permute-done((bf16[512]{0:T(512)(128)(2,1)}, bf16[512]{0:T(512)(128)(2,1)S(1)}, u32[]{:S(2)}, u32[]{:S(2)}) %collective-permute-start.1) | collective-permute-done | bytes 1056 | tf_op jit(solution)/shard_map/while/body/eval_jaxpr/ppermute | solution.py:11
  52.3 3.2 %conditional.4 = (f32[4,128]{1,0:T(4,128)S(1)}) conditional(s32[]{:T(128)} %get-tuple-element.490, f32[4,128]{1,0:T(4,128)S(1)} %get-tuple-element.477, (f32[4,128]{1,0:T(4,128)S(1)}, bf16[512]{0:T(512)(128)(2,1)}, s32[4]{0:T(128)S(1)}, bf16[4,128,768]{2,1,0:T(8,128)(2,1)S(1)}, bf16[512,768]{1,0:T(8,128)(2,1)}, ...), branch_computations={%region_2.2_spmd, %region_3.4_spmd, %region_5.6_spmd, %region_7.8_... | conditional | flops 403709440 | bytes 1604712 | solution.py:48
  53.8 1.7 %fusion.9 = f32[2,128]{1,0:T(2,128)S(1)} fusion(bf16[4,128,768]{2,1,0:T(8,128)(2,1)S(1)} %get-tuple-element.332, bf16[512,768]{1,0:T(8,128)(2,1)} %get-tuple-element.333, f32[2]{0:T(128)S(1)} %get-tuple-element.405, f32[2]{0:T(128)S(1)} %get-tuple-element.404, f32[2,512]{1,0:T(2,128)S(1)} %fusion.11), kind=kOutput, calls=%fused_computation.15 | convolution fusion | flops 201850624 | bytes 1578000 | tf_op jit(solution)/shard_map/while/body/eval_jaxpr/cond/branch_2_fun/neg,wg->new/dot_general | solution.py:31
  55.5 16.9 %collective-permute-done.1 = bf16[512]{0:T(512)(128)(2,1)S(1)} collective-permute-done((bf16[512]{0:T(512)(128)(2,1)}, bf16[512]{0:T(512)(128)(2,1)S(1)}, u32[]{:S(2)}, u32[]{:S(2)}) %collective-permute-start.1) | collective-permute-done | bytes 1056 | tf_op jit(solution)/shard_map/while/body/eval_jaxpr/ppermute | solution.py:11
  73.9 3.2 %conditional.4 = (f32[4,128]{1,0:T(4,128)S(1)}) conditional(s32[]{:T(128)} %get-tuple-element.490, f32[4,128]{1,0:T(4,128)S(1)} %get-tuple-element.477, (f32[4,128]{1,0:T(4,128)S(1)}, bf16[512]{0:T(512)(128)(2,1)}, s32[4]{0:T(128)S(1)}, bf16[4,128,768]{2,1,0:T(8,128)(2,1)S(1)}, bf16[512,768]{1,0:T(8,128)(2,1)}, ...), branch_computations={%region_2.2_spmd, %region_3.4_spmd, %region_5.6_spmd, %region_7.8_... | conditional | flops 403709440 | bytes 1604712 | solution.py:48
  75.4 1.7 %fusion.9 = f32[2,128]{1,0:T(2,128)S(1)} fusion(bf16[4,128,768]{2,1,0:T(8,128)(2,1)S(1)} %get-tuple-element.332, bf16[512,768]{1,0:T(8,128)(2,1)} %get-tuple-element.333, f32[2]{0:T(128)S(1)} %get-tuple-element.405, f32[2]{0:T(128)S(1)} %get-tuple-element.404, f32[2,512]{1,0:T(2,128)S(1)} %fusion.11), kind=kOutput, calls=%fused_computation.15 | convolution fusion | flops 201850624 | bytes 1578000 | tf_op jit(solution)/shard_map/while/body/eval_jaxpr/cond/branch_2_fun/neg,wg->new/dot_general | solution.py:31
  77.1 16.0 %collective-permute-done.1 = bf16[512]{0:T(512)(128)(2,1)S(1)} collective-permute-done((bf16[512]{0:T(512)(128)(2,1)}, bf16[512]{0:T(512)(128)(2,1)S(1)}, u32[]{:S(2)}, u32[]{:S(2)}) %collective-permute-start.1) | collective-permute-done | bytes 1056 | tf_op jit(solution)/shard_map/while/body/eval_jaxpr/ppermute | solution.py:11
  94.5 3.2 %conditional.4 = (f32[4,128]{1,0:T(4,128)S(1)}) conditional(s32[]{:T(128)} %get-tuple-element.490, f32[4,128]{1,0:T(4,128)S(1)} %get-tuple-element.477, (f32[4,128]{1,0:T(4,128)S(1)}, bf16[512]{0:T(512)(128)(2,1)}, s32[4]{0:T(128)S(1)}, bf16[4,128,768]{2,1,0:T(8,128)(2,1)S(1)}, bf16[512,768]{1,0:T(8,128)(2,1)}, ...), branch_computations={%region_2.2_spmd, %region_3.4_spmd, %region_5.6_spmd, %region_7.8_... | conditional | flops 403709440 | bytes 1604712 | solution.py:48
  96.0 1.7 %fusion.9 = f32[2,128]{1,0:T(2,128)S(1)} fusion(bf16[4,128,768]{2,1,0:T(8,128)(2,1)S(1)} %get-tuple-element.332, bf16[512,768]{1,0:T(8,128)(2,1)} %get-tuple-element.333, f32[2]{0:T(128)S(1)} %get-tuple-element.405, f32[2]{0:T(128)S(1)} %get-tuple-element.404, f32[2,512]{1,0:T(2,128)S(1)} %fusion.11), kind=kOutput, calls=%fused_computation.15 | convolution fusion | flops 201850624 | bytes 1578000 | tf_op jit(solution)/shard_map/while/body/eval_jaxpr/cond/branch_2_fun/neg,wg->new/dot_general | solution.py:31
  97.7 15.0 %collective-permute-done.1 = bf16[512]{0:T(512)(128)(2,1)S(1)} collective-permute-done((bf16[512]{0:T(512)(128)(2,1)}, bf16[512]{0:T(512)(128)(2,1)S(1)}, u32[]{:S(2)}, u32[]{:S(2)}) %collective-permute-start.1) | collective-permute-done | bytes 1056 | tf_op jit(solution)/shard_map/while/body/eval_jaxpr/ppermute | solution.py:11
  114.1 3.2 %conditional.4 = (f32[4,128]{1,0:T(4,128)S(1)}) conditional(s32[]{:T(128)} %get-tuple-element.490, f32[4,128]{1,0:T(4,128)S(1)} %get-tuple-element.477, (f32[4,128]{1,0:T(4,128)S(1)}, bf16[512]{0:T(512)(128)(2,1)}, s32[4]{0:T(128)S(1)}, bf16[4,128,768]{2,1,0:T(8,128)(2,1)S(1)}, bf16[512,768]{1,0:T(8,128)(2,1)}, ...), branch_computations={%region_2.2_spmd, %region_3.4_spmd, %region_5.6_spmd, %region_7.8_... | conditional | flops 403709440 | bytes 1604712 | solution.py:48
  115.6 1.7 %fusion.9 = f32[2,128]{1,0:T(2,128)S(1)} fusion(bf16[4,128,768]{2,1,0:T(8,128)(2,1)S(1)} %get-tuple-element.332, bf16[512,768]{1,0:T(8,128)(2,1)} %get-tuple-element.333, f32[2]{0:T(128)S(1)} %get-tuple-element.405, f32[2]{0:T(128)S(1)} %get-tuple-element.404, f32[2,512]{1,0:T(2,128)S(1)} %fusion.11), kind=kOutput, calls=%fused_computation.15 | convolution fusion | flops 201850624 | bytes 1578000 | tf_op jit(solution)/shard_map/while/body/eval_jaxpr/cond/branch_2_fun/neg,wg->new/dot_general | solution.py:31
  117.3 14.1 %collective-permute-done.1 = bf16[512]{0:T(512)(128)(2,1)S(1)} collective-permute-done((bf16[512]{0:T(512)(128)(2,1)}, bf16[512]{0:T(512)(128)(2,1)S(1)}, u32[]{:S(2)}, u32[]{:S(2)}) %collective-permute-start.1) | collective-permute-done | bytes 1056 | tf_op jit(solution)/shard_map/while/body/eval_jaxpr/ppermute | solution.py:11
  132.8 3.2 %conditional.4 = (f32[4,128]{1,0:T(4,128)S(1)}) conditional(s32[]{:T(128)} %get-tuple-element.490, f32[4,128]{1,0:T(4,128)S(1)} %get-tuple-element.477, (f32[4,128]{1,0:T(4,128)S(1)}, bf16[512]{0:T(512)(128)(2,1)}, s32[4]{0:T(128)S(1)}, bf16[4,128,768]{2,1,0:T(8,128)(2,1)S(1)}, bf16[512,768]{1,0:T(8,128)(2,1)}, ...), branch_computations={%region_2.2_spmd, %region_3.4_spmd, %region_5.6_spmd, %region_7.8_... | conditional | flops 403709440 | bytes 1604712 | solution.py:48
  134.3 1.7 %fusion.9 = f32[2,128]{1,0:T(2,128)S(1)} fusion(bf16[4,128,768]{2,1,0:T(8,128)(2,1)S(1)} %get-tuple-element.332, bf16[512,768]{1,0:T(8,128)(2,1)} %get-tuple-element.333, f32[2]{0:T(128)S(1)} %get-tuple-element.405, f32[2]{0:T(128)S(1)} %get-tuple-element.404, f32[2,512]{1,0:T(2,128)S(1)} %fusion.11), kind=kOutput, calls=%fused_computation.15 | convolution fusion | flops 201850624 | bytes 1578000 | tf_op jit(solution)/shard_map/while/body/eval_jaxpr/cond/branch_2_fun/neg,wg->new/dot_general | solution.py:31
  136.0 13.1 %collective-permute-done.1 = bf16[512]{0:T(512)(128)(2,1)S(1)} collective-permute-done((bf16[512]{0:T(512)(128)(2,1)}, bf16[512]{0:T(512)(128)(2,1)S(1)}, u32[]{:S(2)}, u32[]{:S(2)}) %collective-permute-start.1) | collective-permute-done | bytes 1056 | tf_op jit(solution)/shard_map/while/body/eval_jaxpr/ppermute | solution.py:11
  (92 shorter events, 25.8 us)
Async XLA Ops:
  0.0 3.6 %copy-start.4 = (bf16[512,768]{1,0:T(8,128)(2,1)S(1)}, bf16[512,768]{1,0:T(8,128)(2,1)}, u32[]{:S(2)}) copy-start(bf16[512,768]{1,0:T(8,128)(2,1)} %param.40) | copy-start | bytes 2359300
  0.0 3.6 %copy-start = (bf16[512,768]{1,0:T(8,128)(2,1)S(1)}, bf16[512,768]{1,0:T(8,128)(2,1)}, u32[]{:S(2)}) copy-start(bf16[512,768]{1,0:T(8,128)(2,1)} %param.43) | copy-start | bytes 2359300
  1.4 0.7 copy-start.2
  2.1 0.7 copy-start.5
  2.8 0.7 copy-start.1
  2.8 0.7 copy-start.3
  4.5 23.8 %collective-permute-start = (bf16[512,768]{1,0:T(8,128)(2,1)}, bf16[512,768]{1,0:T(8,128)(2,1)S(1)}, u32[]{:S(2)}, u32[]{:S(2)}) collective-permute-start(bf16[512,768]{1,0:T(8,128)(2,1)} %copy.25), channel_id=1, source_target_pairs={{0,2},{2,4},{4,6},{6,8},{8,10},{10,12},{12,14},{14,0},{1,3},{3,5},... | collective-permute-start | bytes 2359304 | tf_op jit(solution)/shard_map/while/body/eval_jaxpr/ppermute | solution.py:11
  8.1 20.3 %collective-permute-start.1 = (bf16[512]{0:T(512)(128)(2,1)}, bf16[512]{0:T(512)(128)(2,1)S(1)}, u32[]{:S(2)}, u32[]{:S(2)}) collective-permute-start(bf16[512]{0:T(512)(128)(2,1)} %copy.26), channel_id=1, source_target_pairs={{0,2},{2,4},{4,6},{6,8},{8,10},{10,12},{12,14},{14,0},{1,3},{3,5},... | collective-permute-start | bytes 3080 | tf_op jit(solution)/shard_map/while/body/eval_jaxpr/ppermute | solution.py:11
  29.2 21.7 %collective-permute-start = (bf16[512,768]{1,0:T(8,128)(2,1)}, bf16[512,768]{1,0:T(8,128)(2,1)S(1)}, u32[]{:S(2)}, u32[]{:S(2)}) collective-permute-start(bf16[512,768]{1,0:T(8,128)(2,1)} %copy.25), channel_id=1, source_target_pairs={{0,2},{2,4},{4,6},{6,8},{8,10},{10,12},{12,14},{14,0},{1,3},{3,5},... | collective-permute-start | bytes 2359304 | tf_op jit(solution)/shard_map/while/body/eval_jaxpr/ppermute | solution.py:11
  29.8 21.1 %collective-permute-start.1 = (bf16[512]{0:T(512)(128)(2,1)}, bf16[512]{0:T(512)(128)(2,1)S(1)}, u32[]{:S(2)}, u32[]{:S(2)}) collective-permute-start(bf16[512]{0:T(512)(128)(2,1)} %copy.26), channel_id=1, source_target_pairs={{0,2},{2,4},{4,6},{6,8},{8,10},{10,12},{12,14},{14,0},{1,3},{3,5},... | collective-permute-start | bytes 3080 | tf_op jit(solution)/shard_map/while/body/eval_jaxpr/ppermute | solution.py:11
  51.8 20.7 %collective-permute-start = (bf16[512,768]{1,0:T(8,128)(2,1)}, bf16[512,768]{1,0:T(8,128)(2,1)S(1)}, u32[]{:S(2)}, u32[]{:S(2)}) collective-permute-start(bf16[512,768]{1,0:T(8,128)(2,1)} %copy.25), channel_id=1, source_target_pairs={{0,2},{2,4},{4,6},{6,8},{8,10},{10,12},{12,14},{14,0},{1,3},{3,5},... | collective-permute-start | bytes 2359304 | tf_op jit(solution)/shard_map/while/body/eval_jaxpr/ppermute | solution.py:11
  52.3 20.1 %collective-permute-start.1 = (bf16[512]{0:T(512)(128)(2,1)}, bf16[512]{0:T(512)(128)(2,1)S(1)}, u32[]{:S(2)}, u32[]{:S(2)}) collective-permute-start(bf16[512]{0:T(512)(128)(2,1)} %copy.26), channel_id=1, source_target_pairs={{0,2},{2,4},{4,6},{6,8},{8,10},{10,12},{12,14},{14,0},{1,3},{3,5},... | collective-permute-start | bytes 3080 | tf_op jit(solution)/shard_map/while/body/eval_jaxpr/ppermute | solution.py:11
  73.3 19.7 %collective-permute-start = (bf16[512,768]{1,0:T(8,128)(2,1)}, bf16[512,768]{1,0:T(8,128)(2,1)S(1)}, u32[]{:S(2)}, u32[]{:S(2)}) collective-permute-start(bf16[512,768]{1,0:T(8,128)(2,1)} %copy.25), channel_id=1, source_target_pairs={{0,2},{2,4},{4,6},{6,8},{8,10},{10,12},{12,14},{14,0},{1,3},{3,5},... | collective-permute-start | bytes 2359304 | tf_op jit(solution)/shard_map/while/body/eval_jaxpr/ppermute | solution.py:11
  73.9 19.2 %collective-permute-start.1 = (bf16[512]{0:T(512)(128)(2,1)}, bf16[512]{0:T(512)(128)(2,1)S(1)}, u32[]{:S(2)}, u32[]{:S(2)}) collective-permute-start(bf16[512]{0:T(512)(128)(2,1)} %copy.26), channel_id=1, source_target_pairs={{0,2},{2,4},{4,6},{6,8},{8,10},{10,12},{12,14},{14,0},{1,3},{3,5},... | collective-permute-start | bytes 3080 | tf_op jit(solution)/shard_map/while/body/eval_jaxpr/ppermute | solution.py:11
  93.9 18.8 %collective-permute-start = (bf16[512,768]{1,0:T(8,128)(2,1)}, bf16[512,768]{1,0:T(8,128)(2,1)S(1)}, u32[]{:S(2)}, u32[]{:S(2)}) collective-permute-start(bf16[512,768]{1,0:T(8,128)(2,1)} %copy.25), channel_id=1, source_target_pairs={{0,2},{2,4},{4,6},{6,8},{8,10},{10,12},{12,14},{14,0},{1,3},{3,5},... | collective-permute-start | bytes 2359304 | tf_op jit(solution)/shard_map/while/body/eval_jaxpr/ppermute | solution.py:11
  94.5 18.2 %collective-permute-start.1 = (bf16[512]{0:T(512)(128)(2,1)}, bf16[512]{0:T(512)(128)(2,1)S(1)}, u32[]{:S(2)}, u32[]{:S(2)}) collective-permute-start(bf16[512]{0:T(512)(128)(2,1)} %copy.26), channel_id=1, source_target_pairs={{0,2},{2,4},{4,6},{6,8},{8,10},{10,12},{12,14},{14,0},{1,3},{3,5},... | collective-permute-start | bytes 3080 | tf_op jit(solution)/shard_map/while/body/eval_jaxpr/ppermute | solution.py:11
  113.6 17.8 %collective-permute-start = (bf16[512,768]{1,0:T(8,128)(2,1)}, bf16[512,768]{1,0:T(8,128)(2,1)S(1)}, u32[]{:S(2)}, u32[]{:S(2)}) collective-permute-start(bf16[512,768]{1,0:T(8,128)(2,1)} %copy.25), channel_id=1, source_target_pairs={{0,2},{2,4},{4,6},{6,8},{8,10},{10,12},{12,14},{14,0},{1,3},{3,5},... | collective-permute-start | bytes 2359304 | tf_op jit(solution)/shard_map/while/body/eval_jaxpr/ppermute | solution.py:11
  114.1 17.2 %collective-permute-start.1 = (bf16[512]{0:T(512)(128)(2,1)}, bf16[512]{0:T(512)(128)(2,1)S(1)}, u32[]{:S(2)}, u32[]{:S(2)}) collective-permute-start(bf16[512]{0:T(512)(128)(2,1)} %copy.26), channel_id=1, source_target_pairs={{0,2},{2,4},{4,6},{6,8},{8,10},{10,12},{12,14},{14,0},{1,3},{3,5},... | collective-permute-start | bytes 3080 | tf_op jit(solution)/shard_map/while/body/eval_jaxpr/ppermute | solution.py:11
  132.2 16.8 %collective-permute-start = (bf16[512,768]{1,0:T(8,128)(2,1)}, bf16[512,768]{1,0:T(8,128)(2,1)S(1)}, u32[]{:S(2)}, u32[]{:S(2)}) collective-permute-start(bf16[512,768]{1,0:T(8,128)(2,1)} %copy.25), channel_id=1, source_target_pairs={{0,2},{2,4},{4,6},{6,8},{8,10},{10,12},{12,14},{14,0},{1,3},{3,5},... | collective-permute-start | bytes 2359304 | tf_op jit(solution)/shard_map/while/body/eval_jaxpr/ppermute | solution.py:11
  132.8 16.3 %collective-permute-start.1 = (bf16[512]{0:T(512)(128)(2,1)}, bf16[512]{0:T(512)(128)(2,1)S(1)}, u32[]{:S(2)}, u32[]{:S(2)}) collective-permute-start(bf16[512]{0:T(512)(128)(2,1)} %copy.26), channel_id=1, source_target_pairs={{0,2},{2,4},{4,6},{6,8},{8,10},{10,12},{12,14},{14,0},{1,3},{3,5},... | collective-permute-start | bytes 3080 | tf_op jit(solution)/shard_map/while/body/eval_jaxpr/ppermute | solution.py:11
where the time goes:
time: 151 us; the launch traced here: 150 us
  waiting for transfers between devices  108 us (72%)
  local copies, waits for them, and re-layouts  12.1 us (8%)
  matrix products  12.1 us (8%)
  other arithmetic  11.4 us (8%)
  starting transfers between devices  5.64 us (4%)
    ppermute x14, waiting for transfers between devices, from_behind(): lax.ppermute(shard, axis, [(i, (i + by) % length) for i in range(length)])  108 us
    dot_general x8, matrix products, branch(): jnp.einsum('neg,wg->new', embedding_blocks[:smoothing_width], device_port...  12.1 us
    another operation x14, local copies, waits for them, and re-layouts  10.1 us
    ppermute x14, starting transfers between devices, from_behind(): lax.ppermute(shard, axis, [(i, (i + by) % length) for i in range(length)])  5.64 us
    lt x8, other arithmetic, branch(): shard_keys[None, None, :] < 0  5.04 us
    convert_element_type x8, other arithmetic, score_prefix(): shard_keys = shard_ids.astype(jnp.int32)  4.78 us
  transfers between devices with their start and end apart: 14, of which 7 were waited for; matrix products, arithmetic and copies ran while one was open for 17% of the time, Pallas kernels for 0%

commit v1 on v0

v1 whole, which is shorter than its diff:
```python
import functools
import math

import jax
import jax.numpy as jnp
from jax import lax
from jax.experimental import pallas as pl
from jax.experimental.pallas import tpu as pltpu
from jax.sharding import PartitionSpec as P

LANES = 128
LOG2E = 1.4426950408889634
DEAD = -1.0e30


def turn(value, by):
    length = lax.axis_size("blk")
    return lax.ppermute(value, "blk", [(i, (i + by) % length) for i in range(length)])


def swap(value, axis):
    length = lax.axis_size(axis)
    return lax.ppermute(value, axis, [(i, i ^ 1) for i in range(length)])


def swap_both(value):
    nblk, nhelper = lax.axis_size("blk"), lax.axis_size("helper")
    pairs = [(i, (i ^ nhelper) ^ 1) for i in range(nblk * nhelper)]
    return lax.ppermute(value, ("blk", "helper"), pairs)


def rows_of(index, count=1):
    return pl.ds(pl.multiple_of(index * LANES, LANES), count * LANES)


def score_kernel(plan, chunks, qblocks, first, info_ref, beta_ref, ids_ref, *refs):
    ntiles = len(plan)
    if first:
        q_refs, refs = refs[:4], refs[4:]
        r_refs, (out_ref, qv, rv, q_list, r_list) = refs[:ntiles], refs[ntiles:]
    else:
        (qv, prev_ref), refs = refs[:2], refs[2:]
        r_refs, (out_ref, rv, q_list, r_list) = refs[:ntiles], refs[ntiles:]
    width = qv.shape[1]
    slots = 4 * qblocks
    helper = info_ref[slots + 4]

    q_count = jnp.int32(0)
    for source in range(4):
        blocks = info_ref[slots + source]

        def one_block(block, carry, source=source, q_count=q_count):
            if first:
                qv[rows_of(q_count + block), :] = q_refs[source][rows_of(block), :]
            q_list[q_count + block] = source * qblocks + block
            return carry

        lax.fori_loop(0, blocks, one_block, 0)
        q_count = q_count + blocks

    r_count = jnp.int32(0)
    for operand, (source, chunk) in enumerate(plan):
        tile = helper + 2 * chunk
        live = info_ref[slots + 5 + source] > tile * LANES

        @pl.when(live)
        def _(operand=operand, source=source, chunk=chunk, r_count=r_count):
            rv[rows_of(r_count), :] = r_refs[operand][...]
            r_list[r_count] = source * chunks + chunk

        r_count = r_count + live.astype(jnp.int32)
    odd = lax.rem(r_count, 2)

    @pl.when(odd == 1)
    def _():
        rv[rows_of(r_count), :] = r_refs[0][...]
        r_list[r_count] = ids_ref.shape[0] - 1

    r_pairs = (r_count + odd) // 2
    factor = LOG2E / math.sqrt(width)
    if first:
        out_ref[...] = jnp.zeros_like(out_ref)
    else:
        out_ref[...] = prev_ref[...]

    def two_query_blocks(group, carry):
        parts = []
        for side in range(2):
            slot = q_list[jnp.minimum(2 * group + side, q_count - 1)]
            cluster = info_ref[slot]
            beta = beta_ref[cluster]
            parts.append((slot, cluster, beta * factor, beta * beta * (0.5 * LOG2E)))
        blocks = qv[rows_of(2 * group, 2), :]

        def two_tiles(pair, accs):
            score = lax.dot_general(
                blocks,
                rv[rows_of(2 * pair, 2), :],
                (((1,), (1,)), ((), ())),
                preferred_element_type=jnp.float32,
            )
            accs = list(accs)
            for t in range(2):
                ids = ids_ref[pl.ds(r_list[2 * pair + t], 1), :]
                for side, (_, cluster, scale, offset) in enumerate(parts):
                    weight = jnp.where(ids == cluster, 0.0, -4.0)
                    bias = jnp.where(ids < 0, DEAD, weight) - offset
                    part = score[
                        side * LANES : (side + 1) * LANES, t * LANES : (t + 1) * LANES
                    ]
                    accs[side] = accs[side] + jnp.exp2(part * scale + bias)
            return tuple(accs)

        zero = jnp.zeros((LANES, LANES), jnp.float32)
        accs = lax.fori_loop(0, r_pairs, two_tiles, (zero, zero))
        for side in range(2):
            total = jnp.sum(accs[side].T, axis=0, keepdims=True)

            @pl.when(2 * group + side < q_count)
            def _(side=side, total=total):
                row = pl.ds(parts[side][0], 1)
                out_ref[row, :] = out_ref[row, :] + total

        return carry

    @pl.when(r_pairs > 0)
    def _():
        lax.fori_loop(0, (q_count + 1) // 2, two_query_blocks, 0)


def score_call(plan, chunks, qblocks, info, beta, ids, queries, packed, prev, tiles):
    first = packed is None
    width = tiles[0].shape[1]
    slots = 4 * qblocks
    ntiles = len(tiles)
    pad = ntiles + ntiles % 2
    smem = pl.BlockSpec(memory_space=pltpu.SMEM)
    vmem = pl.BlockSpec(memory_space=pltpu.VMEM)
    totals_shape = jax.ShapeDtypeStruct((slots, LANES), jnp.float32)
    packed_shape = jax.ShapeDtypeStruct((slots * LANES, width), jnp.bfloat16)
    given = queries if first else (packed, prev)
    return pl.pallas_call(
        functools.partial(score_kernel, plan, chunks, qblocks, first),
        out_shape=(totals_shape, packed_shape) if first else totals_shape,
        in_specs=[smem, smem] + [vmem] * (1 + len(given) + ntiles),
        out_specs=(vmem, vmem) if first else vmem,
        scratch_shapes=[
            pltpu.VMEM((pad * LANES, width), jnp.bfloat16),
            pltpu.SMEM((slots,), jnp.int32),
            pltpu.SMEM((pad,), jnp.int32),
        ],
        compiler_params=pltpu.CompilerParams(vmem_limit_bytes=24 * 1024 * 1024),
        cost_estimate=pl.CostEstimate(flops=1, bytes_accessed=1, transcendentals=0),
    )(info, beta, ids, *given, *tiles)


def per_device(
    queries,
    query_block_cluster,
    block_count,
    references,
    ref_cluster,
    ref_rows,
    cluster_beta,
    cluster_member_count,
):
    nblk, nhelper = lax.axis_size("blk"), lax.axis_size("helper")
    helper = lax.axis_index("helper").astype(jnp.int32)
    qblocks = query_block_cluster.shape[0]
    rows, width = references.shape
    tiles = rows // LANES
    chunks = tiles // nhelper
    sources = nblk // 2

    by_tile = references.reshape(tiles, LANES, width)
    own = [
        lax.dynamic_index_in_dim(by_tile, helper + nhelper * c, 0, keepdims=False)
        for c in range(chunks)
    ]
    own, queries, ref_cluster, query_block_cluster, block_count, ref_rows = (
        lax.optimization_barrier(
            (own, queries, ref_cluster, query_block_cluster, block_count, ref_rows)
        )
    )
    held = [own, [turn(x, 2) for x in own]]
    q_partner = swap(queries, "blk")
    q_helper = swap(queries, "helper")

    live = jnp.arange(rows, dtype=jnp.int32) < ref_rows[0]
    ids = jnp.where(live, ref_cluster, -1).reshape(chunks, nhelper, LANES)
    ids = lax.dynamic_index_in_dim(ids, helper, 1, keepdims=False)
    scalars = jnp.concatenate([query_block_cluster, block_count, ref_rows])
    scalars = jnp.pad(scalars, (0, LANES - scalars.shape[0]))
    meta = jnp.concatenate([ids, scalars[None, :]])
    along = [meta] + [turn(meta, 2 * s) for s in range(1, sources)]
    around = [meta, swap(meta, "helper"), swap(meta, "blk"), swap_both(meta)]
    none = jnp.full((1, LANES), -1, jnp.int32)
    all_ids = jnp.concatenate([m[:chunks] for m in along] + [none])
    info = jnp.concatenate(
        [m[chunks, :qblocks] for m in around]
        + [m[chunks, qblocks : qblocks + 1] for m in around]
        + [helper[None]]
        + [m[chunks, qblocks + 1 : qblocks + 2] for m in along]
    )

    for _ in range(2, sources):
        held.append([turn(x, 2) for x in held[-1]])
    q_partner, held[-2] = lax.optimization_barrier((q_partner, held[-2]))
    q_both = swap(q_partner, "helper")
    all_queries = (queries, q_helper, q_partner, q_both)

    def operands(steps):
        plan = tuple((s, c) for s in steps for c in range(chunks))
        return plan, [held[s][c] for s, c in plan]

    plan, operand = operands(range(sources - 1))
    totals, packed = score_call(
        plan, chunks, qblocks, info, cluster_beta, all_ids, all_queries, None, None, operand
    )
    plan, operand = operands([sources - 1])
    totals = score_call(
        plan, chunks, qblocks, info, cluster_beta, all_ids, None, packed, totals, operand
    )
    totals = totals.reshape(4, qblocks, LANES)
    total = totals[0] + swap(totals[1], "helper") + swap(totals[2], "blk") + swap_both(totals[3])
    columns = jnp.arange(cluster_member_count.shape[0], dtype=jnp.int32)
    onehot = query_block_cluster[:, None] == columns[None, :]
    sizes = jnp.sum(jnp.where(onehot, cluster_member_count[None, :], 0), axis=1)
    density = jnp.log1p(total / sizes.astype(jnp.float32)[:, None])
    return density.reshape(queries.shape[0])


def solution(mesh):
    in_specs = (
        P(("parts", "blk", "helper"), None),
        P(("parts", "blk", "helper")),
        P(("parts", "blk", "helper")),
        P(("parts", "blk"), None),
        P(("parts", "blk")),
        P(("parts", "blk")),
        P("parts"),
        P("parts"),
    )
    out_specs = P(("parts", "blk", "helper"))
    return jax.shard_map(
        per_device, mesh=mesh, in_specs=in_specs, out_specs=out_specs, check_vma=False
    )
```

time: 151 us -> 69.3 us (0.46)
  waiting for transfers between devices: 108 us -> 11.2 us
  Pallas kernels: 0 us -> 12.9 us
  matrix products: 12.1 us -> 0 us
  local copies, waits for them, and re-layouts: 12.1 us -> 23.6 us
  starting transfers between devices: 5.64 us -> 16.8 us
  other arithmetic: 11.4 us -> 2.85 us
    ppermute x14 -> x18, waiting for transfers between devices: 108 us -> 11.2 us  [the longest x9 9.47 us: turn(): lax.ppermute(value, 'blk', [(i, (i + by) % length) for i in range(length)])]
    pallas_call x0 -> x2, Pallas kernels: none -> 12.9 us  [score_call(): pl.pallas_call(functools.partial(score_kernel, plan, chunks, qblocks, fir...]
    dot_general x8 -> x0, matrix products: 12.1 us -> none  [branch(): jnp.einsum('neg,wg->new', embedding_blocks[:smoothing_width], device_port...]
    ppermute x14 -> x18, starting transfers between devices: 5.64 us -> 16.8 us  [the longest x9 9.45 us: turn(): lax.ppermute(value, 'blk', [(i, (i + by) % length) for i in range(length)])]
    another operation x14 -> x0, local copies, waits for them, and re-layouts: 10.1 us -> none
    slice x0 -> x11, local copies, waits for them, and re-layouts: none -> 9.51 us  [the longest x4 4.56 us: per_device(): m[chunks, qblocks + 1:qblocks + 2]]
    concatenate x0 -> x2, local copies, waits for them, and re-layouts: none -> 7.09 us  [the longest x1 5.72 us: per_device(): jnp.concatenate([m[chunks, :qblocks] for m in around] + [m[chunks, qblock...]
    lt x8 -> x0, other arithmetic: 5.04 us -> none  [branch(): shard_keys[None, None, :] < 0]
  transfers between devices with their start and end apart: 14 -> 18, of which waited for: 7 -> 5; matrix products, arithmetic and copies ran while one was open for 17% -> 33% of each run, Pallas kernels for 0% -> 12%
where the time goes in v1:
time: 69.3 us; the launch traced here: 68.7 us
  local copies, waits for them, and re-layouts  23.6 us (34%)
  starting transfers between devices  16.8 us (24%)
  Pallas kernels  12.9 us (19%)
  waiting for transfers between devices  11.2 us (16%)
  other arithmetic  2.85 us (4%)
  between operations  1.42 us (2%)
    pallas_call x2, Pallas kernels, score_call(): pl.pallas_call(functools.partial(score_kernel, plan, chunks, qblocks, fir...  12.9 us
    ppermute x9, waiting for transfers between devices, turn(): lax.ppermute(value, 'blk', [(i, (i + by) % length) for i in range(length)])  9.47 us
    ppermute x9, starting transfers between devices, turn(): lax.ppermute(value, 'blk', [(i, (i + by) % length) for i in range(length)])  9.45 us
    concatenate x1, local copies, waits for them, and re-layouts, per_device(): jnp.concatenate([m[chunks, :qblocks] for m in around] + [m[chunks, qblock...  5.72 us
    ppermute x7, starting transfers between devices, swap(): return lax.ppermute(value, axis, [(i, i ^ 1) for i in range(length)])  4.61 us
    slice x4, local copies, waits for them, and re-layouts, per_device(): m[chunks, qblocks + 1:qblocks + 2]  4.56 us
    slice x3, local copies, waits for them, and re-layouts, per_device(): m[chunks, qblocks:qblocks + 1]  3.81 us
    squeeze x4, local copies, waits for them, and re-layouts, per_device(): m[chunks, :qblocks]  3.56 us
  transfers between devices with their start and end apart: 18, of which 5 were waited for; matrix products, arithmetic and copies ran while one was open for 33% of the time, Pallas kernels for 12%

profile of v1, /device:TPU:0, one launch (start us, length us, event | category | flops | bytes accessed | tf_op | source)
XLA Modules:
  0.0 68.7 jit_solution(4420382941630574889)
XLA Ops:
  1.1 3.0 %collective-permute-start.7 = (bf16[512,768]{1,0:T(8,128)(2,1)}, bf16[512,768]{1,0:T(8,128)(2,1)S(1)}, u32[]{:S(2)}, u32[]{:S(2)}) collective-permute-start(bf16[512,768]{1,0:T(8,128)(2,1)} %refs_0_), channel_id=1, source_target_pairs={{0,2},{2,0},{4,6},{6,4},{8,10},{10,8},{12,14},{14,12},{1,3},{3,1},... | collective-permute-start | bytes 2359304 | tf_op jit(solution)/shard_map/ppermute | solution.py:23
  4.1 1.6 %collective-permute-start.10 = (bf16[128,768]{1,0:T(8,128)(2,1)S(1)}, bf16[128,768]{1,0:T(8,128)(2,1)S(1)}, u32[]{:S(2)}, u32[]{:S(2)}) collective-permute-start(bf16[128,768]{1,0:T(8,128)(2,1)S(1)} %get-tuple-element.23.refs_5_), channel_id=1, source_target_pairs={{0,4},{2,6},{4,8},{6,10},{8,12},{10,14},{12,0},{14,2},{1,5},{3,7},... | collective-permute-start | bytes 589832 | tf_op jit(solution)/shard_map/ppermute | solution.py:18
  5.7 1.6 %collective-permute-start.8 = (bf16[128,768]{1,0:T(8,128)(2,1)S(1)}, bf16[128,768]{1,0:T(8,128)(2,1)S(1)}, u32[]{:S(2)}, u32[]{:S(2)}) collective-permute-start(bf16[128,768]{1,0:T(8,128)(2,1)S(1)} %get-tuple-element.22.refs_4_), channel_id=1, source_target_pairs={{0,4},{2,6},{4,8},{6,10},{8,12},{10,14},{12,0},{14,2},{1,5},{3,7},... | collective-permute-start | bytes 589832 | tf_op jit(solution)/shard_map/ppermute | solution.py:18
  10.0 3.7 %collective-permute-done.10.refs_7_ = bf16[128,768]{1,0:T(8,128)(2,1)S(1)} collective-permute-done((bf16[128,768]{1,0:T(8,128)(2,1)S(1)}, bf16[128,768]{1,0:T(8,128)(2,1)S(1)}, u32[]{:S(2)}, u32[]{:S(2)}) %collective-permute-start.10) | collective-permute-done | bytes 196640 | tf_op jit(solution)/shard_map/ppermute | solution.py:18
  13.7 3.9 %collective-permute-done.8.refs_6_ = bf16[128,768]{1,0:T(8,128)(2,1)S(1)} collective-permute-done((bf16[128,768]{1,0:T(8,128)(2,1)S(1)}, bf16[128,768]{1,0:T(8,128)(2,1)S(1)}, u32[]{:S(2)}, u32[]{:S(2)}) %collective-permute-start.8) | collective-permute-done | bytes 196640 | tf_op jit(solution)/shard_map/ppermute | solution.py:18
  18.3 1.6 %collective-permute-start.3 = (s32[3,128]{1,0:T(4,128)}, s32[3,128]{1,0:T(4,128)S(1)}, u32[]{:S(2)}, u32[]{:S(2)}) collective-permute-start(s32[3,128]{1,0:T(4,128)} %pad_add_fusion), channel_id=1, source_target_pairs={{0,4},{2,6},{4,8},{6,10},{8,12},{10,14},{12,0},{14,2},{1,5},{3,7},... | collective-permute-start | bytes 4616 | tf_op jit(solution)/shard_map/ppermute | solution.py:18
  19.9 2.7 %collective-permute-start.4 = (s32[3,128]{1,0:T(4,128)}, s32[3,128]{1,0:T(4,128)S(1)}, u32[]{:S(2)}, u32[]{:S(2)}) collective-permute-start(s32[3,128]{1,0:T(4,128)} %pad_add_fusion), channel_id=1, source_target_pairs={{0,8},{2,10},{4,12},{6,14},{8,0},{10,2},{12,4},{14,6},{1,9},{3,11}... | collective-permute-start | bytes 4616 | tf_op jit(solution)/shard_map/ppermute | solution.py:18
  23.9 1.6 %collective-permute-done.9.refs_8_ = bf16[128,768]{1,0:T(8,128)(2,1)S(1)} collective-permute-done((bf16[128,768]{1,0:T(8,128)(2,1)S(1)}, bf16[128,768]{1,0:T(8,128)(2,1)S(1)}, u32[]{:S(2)}, u32[]{:S(2)}) %collective-permute-start.9) | collective-permute-done | bytes 196640 | tf_op jit(solution)/shard_map/ppermute | solution.py:18
  26.9 1.5 %collective-permute-start.2 = (s32[3,128]{1,0:T(4,128)}, s32[3,128]{1,0:T(4,128)}, u32[]{:S(2)}, u32[]{:S(2)}) collective-permute-start(s32[3,128]{1,0:T(4,128)} %pad_add_fusion), channel_id=1, source_target_pairs={{0,3},{1,2},{2,1},{3,0},{4,7},{5,6},{6,5},{7,4},{8,11},{9,10},{10,... | collective-permute-start | bytes 4616 | tf_op jit(solution)/shard_map/ppermute | solution.py:29
  30.8 1.4 %concatenate.15.ids_ref = s32[9,128]{1,0:T(8,128)S(1)} concatenate(s32[2,128]{1,0:T(2,128)S(1)} %bitcast.32, s32[2,128]{1,0:T(2,128)S(1)} %slice.73, s32[2,128]{1,0:T(2,128)} %slice.74, s32[2,128]{1,0:T(2,128)} %slice.75, s32[1,128]{1,0:T(1,128)} %broadcast_in_dim.32), dimensions={0} | concatenate | bytes 9216 | tf_op jit(solution)/shard_map/concatenate | solution.py:198
  32.2 1.3 %slice.70 = s32[1,1]{1,0:T(1,128)} slice(s32[3,128]{1,0:T(4,128)} %copy-done.2), slice={[2:3], [5:6]} | slice | bytes 8 | tf_op jit(solution)/shard_map/slice | solution.py:203
  33.5 1.3 %slice.71 = s32[1,1]{1,0:T(1,128)} slice(s32[3,128]{1,0:T(4,128)} %copy-done.3), slice={[2:3], [5:6]} | slice | bytes 8 | tf_op jit(solution)/shard_map/slice | solution.py:203
  34.8 1.3 %slice.72 = s32[1,1]{1,0:T(1,128)} slice(s32[3,128]{1,0:T(4,128)} %copy-done.4), slice={[2:3], [5:6]} | slice | bytes 8 | tf_op jit(solution)/shard_map/slice | solution.py:203
  36.1 1.3 %slice.66 = s32[1,1]{1,0:T(1,128)} slice(s32[3,128]{1,0:T(4,128)} %collective-permute-done), slice={[2:3], [4:5]} | slice | bytes 8 | tf_op jit(solution)/shard_map/slice | solution.py:201
  37.4 1.3 %slice.67 = s32[1,1]{1,0:T(1,128)} slice(s32[3,128]{1,0:T(4,128)} %collective-permute-done.1), slice={[2:3], [4:5]} | slice | bytes 8 | tf_op jit(solution)/shard_map/slice | solution.py:201
  38.7 1.2 %slice.68 = s32[1,1]{1,0:T(1,128)} slice(s32[3,128]{1,0:T(4,128)} %collective-permute-done.2), slice={[2:3], [4:5]} | slice | bytes 8 | tf_op jit(solution)/shard_map/slice | solution.py:201
  40.6 1.2 %slice_bitcast_fusion.1 = s32[4]{0:T(128)} fusion(s32[3,128]{1,0:T(4,128)} %collective-permute-done.1), kind=kLoop, calls=%fused_computation.15 | loop fusion | bytes 32 | tf_op jit(solution)/shard_map/squeeze | solution.py:200
  42.6 1.2 %slice_bitcast_fusion.2 = s32[4]{0:T(128)} fusion(s32[3,128]{1,0:T(4,128)} %collective-permute-done), kind=kLoop, calls=%fused_computation.16 | loop fusion | bytes 32 | tf_op jit(solution)/shard_map/squeeze | solution.py:200
  43.8 5.7 %concatenate.14.info_ref = s32[25]{0:T(128)S(1)} concatenate(s32[4]{0:T(128)} %slice_bitcast_fusion.3, s32[4]{0:T(128)} %slice_bitcast_fusion.2, s32[4]{0:T(128)} %slice_bitcast_fusion.1, s32[4]{0:T(128)S(1)} %slice_bitcast_fusion, s32[1]{0:T(128)} %bitcast.11, s32[1]{0:T(128)} %bitcast.12, s32[1]{0:T(128)} %bitcast.13, s32[1]{0:T(128)} %bitcast.14, s32[1]{0:T(128)} %bitcast.15, ...), dimensions={0} | concatenate | bytes 200 | tf_op jit(solution)/shard_map/concatenate | solution.py:199
  49.5 1.1 %copy-done = bf16[512,768]{1,0:T(8,128)(2,1)S(1)} copy-done((bf16[512,768]{1,0:T(8,128)(2,1)S(1)}, bf16[512,768]{1,0:T(8,128)(2,1)}, u32[]{:S(2)}) %copy-start) | copy-done | bytes 786456
  51.3 8.3 %shard_map.82 = (f32[16,128]{1,0:T(8,128)S(1)}, bf16[2048,768]{1,0:T(8,128)(2,1)S(1)}) custom-call(s32[25]{0:T(128)S(1)} %concatenate.14.info_ref, f32[64]{0:T(128)S(1)} %copy-done.1, s32[9,128]{1,0:T(8,128)S(1)} %concatenate.15.ids_ref, bf16[512,768]{1,0:T(8,128)(2,1)S(1)} %copy-done, bf16[512,768]{1,0:T(8,128)(2,1)S(1)} %collective-permute-done.6.refs_1_, ...), custom_call_target="tpu_custom_call" | custom-call | flops 1 | bytes 1 | tf_op jit(solution)/shard_map/pallas_call | solution.py:142
  59.6 4.6 %shard_map.83 = f32[16,128]{1,0:T(8,128)S(1)} custom-call(s32[25]{0:T(128)S(1)} %concatenate.14.info_ref, f32[64]{0:T(128)S(1)} %copy-done.1, s32[9,128]{1,0:T(8,128)S(1)} %concatenate.15.ids_ref, bf16[2048,768]{1,0:T(8,128)(2,1)S(1)} %get-tuple-element.27.refs_0_, f32[16,128]{1,0:T(8,128)S(1)} %get-tuple-element.28.refs_1_, ...), custom_call_target="tpu_custom_call" | custom-call | flops 1 | bytes 1 | tf_op jit(solution)/shard_map/pallas_call | solution.py:142
  65.0 1.2 %collective-permute-start.17 = (f32[4,128]{1,0:T(4,128)S(1)}, f32[4,128]{1,0:T(4,128)S(1)}, u32[]{:S(2)}, u32[]{:S(2)}) collective-permute-start(f32[4,128]{1,0:T(4,128)S(1)} %get-tuple-element.32), channel_id=1, source_target_pairs={{0,3},{1,2},{2,1},{3,0},{4,7},{5,6},{6,5},{7,4},{8,11},{9,10},{10,... | collective-permute-start | bytes 6152 | tf_op jit(solution)/shard_map/ppermute | solution.py:29
  66.4 1.7 %collective-permute-done.16 = f32[4,128]{1,0:T(4,128)S(1)} collective-permute-done((f32[4,128]{1,0:T(4,128)S(1)}, f32[4,128]{1,0:T(4,128)S(1)}, u32[]{:S(2)}, u32[]{:S(2)}) %collective-permute-start.16) | collective-permute-done | bytes 2080 | tf_op jit(solution)/shard_map/ppermute | solution.py:23
  (55 shorter events, 12.1 us)
Async XLA Ops:
  1.1 24.4 %collective-permute-start.7 = (bf16[512,768]{1,0:T(8,128)(2,1)}, bf16[512,768]{1,0:T(8,128)(2,1)S(1)}, u32[]{:S(2)}, u32[]{:S(2)}) collective-permute-start(bf16[512,768]{1,0:T(8,128)(2,1)} %refs_0_), channel_id=1, source_target_pairs={{0,2},{2,0},{4,6},{6,4},{8,10},{10,8},{12,14},{14,12},{1,3},{3,1},... | collective-permute-start | bytes 2359304 | tf_op jit(solution)/shard_map/ppermute | solution.py:23
  4.1 9.6 %collective-permute-start.10 = (bf16[128,768]{1,0:T(8,128)(2,1)S(1)}, bf16[128,768]{1,0:T(8,128)(2,1)S(1)}, u32[]{:S(2)}, u32[]{:S(2)}) collective-permute-start(bf16[128,768]{1,0:T(8,128)(2,1)S(1)} %get-tuple-element.23.refs_5_), channel_id=1, source_target_pairs={{0,4},{2,6},{4,8},{6,10},{8,12},{10,14},{12,0},{14,2},{1,5},{3,7},... | collective-permute-start | bytes 589832 | tf_op jit(solution)/shard_map/ppermute | solution.py:18
  5.7 11.9 %collective-permute-start.8 = (bf16[128,768]{1,0:T(8,128)(2,1)S(1)}, bf16[128,768]{1,0:T(8,128)(2,1)S(1)}, u32[]{:S(2)}, u32[]{:S(2)}) collective-permute-start(bf16[128,768]{1,0:T(8,128)(2,1)S(1)} %get-tuple-element.22.refs_4_), channel_id=1, source_target_pairs={{0,4},{2,6},{4,8},{6,10},{8,12},{10,14},{12,0},{14,2},{1,5},{3,7},... | collective-permute-start | bytes 589832 | tf_op jit(solution)/shard_map/ppermute | solution.py:18
  13.7 9.1 %collective-permute-start.11 = (bf16[128,768]{1,0:T(8,128)(2,1)S(1)}, bf16[128,768]{1,0:T(8,128)(2,1)S(1)}, u32[]{:S(2)}, u32[]{:S(2)}) collective-permute-start(bf16[128,768]{1,0:T(8,128)(2,1)S(1)} %collective-permute-done.10.refs_7_), channel_id=1, source_target_pairs={{0,4},{2,6},{4,8},{6,10},{8,12},{10,14},{12,0},{14,2},{1,5},{3,7},... | collective-permute-start | bytes 589832 | tf_op jit(solution)/shard_map/ppermute | solution.py:18
  17.6 7.9 %collective-permute-start.9 = (bf16[128,768]{1,0:T(8,128)(2,1)S(1)}, bf16[128,768]{1,0:T(8,128)(2,1)S(1)}, u32[]{:S(2)}, u32[]{:S(2)}) collective-permute-start(bf16[128,768]{1,0:T(8,128)(2,1)S(1)} %collective-permute-done.8.refs_6_), channel_id=1, source_target_pairs={{0,4},{2,6},{4,8},{6,10},{8,12},{10,14},{12,0},{14,2},{1,5},{3,7},... | collective-permute-start | bytes 589832 | tf_op jit(solution)/shard_map/ppermute | solution.py:18
  18.3 8.3 %collective-permute-start.3 = (s32[3,128]{1,0:T(4,128)}, s32[3,128]{1,0:T(4,128)S(1)}, u32[]{:S(2)}, u32[]{:S(2)}) collective-permute-start(s32[3,128]{1,0:T(4,128)} %pad_add_fusion), channel_id=1, source_target_pairs={{0,4},{2,6},{4,8},{6,10},{8,12},{10,14},{12,0},{14,2},{1,5},{3,7},... | collective-permute-start | bytes 4616 | tf_op jit(solution)/shard_map/ppermute | solution.py:18
  19.9 6.7 %collective-permute-start.4 = (s32[3,128]{1,0:T(4,128)}, s32[3,128]{1,0:T(4,128)S(1)}, u32[]{:S(2)}, u32[]{:S(2)}) collective-permute-start(s32[3,128]{1,0:T(4,128)} %pad_add_fusion), channel_id=1, source_target_pairs={{0,8},{2,10},{4,12},{6,14},{8,0},{10,2},{12,4},{14,6},{1,9},{3,11}... | collective-permute-start | bytes 4616 | tf_op jit(solution)/shard_map/ppermute | solution.py:18
  22.9 4.0 %collective-permute-start.5 = (s32[3,128]{1,0:T(4,128)}, s32[3,128]{1,0:T(4,128)S(1)}, u32[]{:S(2)}, u32[]{:S(2)}) collective-permute-start(s32[3,128]{1,0:T(4,128)} %pad_add_fusion), channel_id=1, source_target_pairs={{0,12},{2,14},{4,0},{6,2},{8,4},{10,6},{12,8},{14,10},{1,13},{3,15... | collective-permute-start | bytes 4616 | tf_op jit(solution)/shard_map/ppermute | solution.py:18
  25.5 24.0 %collective-permute-start.6 = (bf16[512,768]{1,0:T(8,128)(2,1)}, bf16[512,768]{1,0:T(8,128)(2,1)S(1)}, u32[]{:S(2)}, u32[]{:S(2)}) collective-permute-start(bf16[512,768]{1,0:T(8,128)(2,1)} %refs_0_), channel_id=1, source_target_pairs={{0,1},{1,0},{2,3},{3,2},{4,5},{5,4},{6,7},{7,6},{8,9},{9,8},{10,11... | collective-permute-start | bytes 2359304 | tf_op jit(solution)/shard_map/ppermute | solution.py:23
  25.5 24.0 %collective-permute-start.12 = (bf16[512,768]{1,0:T(8,128)(2,1)S(1)}, bf16[512,768]{1,0:T(8,128)(2,1)S(1)}, u32[]{:S(2)}, u32[]{:S(2)}) collective-permute-start(bf16[512,768]{1,0:T(8,128)(2,1)S(1)} %collective-permute-done.7.refs_2_), channel_id=1, source_target_pairs={{0,1},{1,0},{2,3},{3,2},{4,5},{5,4},{6,7},{7,6},{8,9},{9,8},{10,11... | collective-permute-start | bytes 2359304 | tf_op jit(solution)/shard_map/ppermute | solution.py:23
  26.5 3.7 %copy-start.2 = (s32[3,128]{1,0:T(4,128)}, s32[3,128]{1,0:T(4,128)S(1)}, u32[]{:S(2)}) copy-start(s32[3,128]{1,0:T(4,128)S(1)} %collective-permute-done.3) | copy-start | bytes 4612
  26.5 9.6 %collective-permute-start = (s32[3,128]{1,0:T(4,128)}, s32[3,128]{1,0:T(4,128)}, u32[]{:S(2)}, u32[]{:S(2)}) collective-permute-start(s32[3,128]{1,0:T(4,128)} %pad_add_fusion), channel_id=1, source_target_pairs={{0,1},{1,0},{2,3},{3,2},{4,5},{5,4},{6,7},{7,6},{8,9},{9,8},{10,11... | collective-permute-start | bytes 4616 | tf_op jit(solution)/shard_map/ppermute | solution.py:23
  26.6 3.7 %copy-start.3 = (s32[3,128]{1,0:T(4,128)}, s32[3,128]{1,0:T(4,128)S(1)}, u32[]{:S(2)}) copy-start(s32[3,128]{1,0:T(4,128)S(1)} %collective-permute-done.4) | copy-start | bytes 4612
  26.6 10.8 %collective-permute-start.1 = (s32[3,128]{1,0:T(4,128)}, s32[3,128]{1,0:T(4,128)}, u32[]{:S(2)}, u32[]{:S(2)}) collective-permute-start(s32[3,128]{1,0:T(4,128)} %pad_add_fusion), channel_id=1, source_target_pairs={{0,2},{2,0},{4,6},{6,4},{8,10},{10,8},{12,14},{14,12},{1,3},{3,1},... | collective-permute-start | bytes 4616 | tf_op jit(solution)/shard_map/ppermute | solution.py:23
  26.9 3.3 %copy-start.4 = (s32[3,128]{1,0:T(4,128)}, s32[3,128]{1,0:T(4,128)S(1)}, u32[]{:S(2)}) copy-start(s32[3,128]{1,0:T(4,128)S(1)} %collective-permute-done.5) | copy-start | bytes 4612
  26.9 11.8 %collective-permute-start.2 = (s32[3,128]{1,0:T(4,128)}, s32[3,128]{1,0:T(4,128)}, u32[]{:S(2)}, u32[]{:S(2)}) collective-permute-start(s32[3,128]{1,0:T(4,128)} %pad_add_fusion), channel_id=1, source_target_pairs={{0,3},{1,2},{2,1},{3,0},{4,7},{5,6},{6,5},{7,4},{8,11},{9,10},{10,... | collective-permute-start | bytes 4616 | tf_op jit(solution)/shard_map/ppermute | solution.py:29
  41.8 17.8 %collective-permute-start.13 = (bf16[128,768]{1,0:T(8,128)(2,1)S(1)}, bf16[128,768]{1,0:T(8,128)(2,1)}, u32[]{:S(2)}, u32[]{:S(2)}) collective-permute-start(bf16[128,768]{1,0:T(8,128)(2,1)S(1)} %collective-permute-done.9.refs_8_), channel_id=1, source_target_pairs={{0,4},{2,6},{4,8},{6,10},{8,12},{10,14},{12,0},{14,2},{1,5},{3,7},... | collective-permute-start | bytes 589832 | tf_op jit(solution)/shard_map/ppermute | solution.py:18
  41.8 17.8 %collective-permute-start.14 = (bf16[128,768]{1,0:T(8,128)(2,1)S(1)}, bf16[128,768]{1,0:T(8,128)(2,1)}, u32[]{:S(2)}, u32[]{:S(2)}) collective-permute-start(bf16[128,768]{1,0:T(8,128)(2,1)S(1)} %collective-permute-done.11.refs_9_), channel_id=1, source_target_pairs={{0,4},{2,6},{4,8},{6,10},{8,12},{10,14},{12,0},{14,2},{1,5},{3,7},... | collective-permute-start | bytes 589832 | tf_op jit(solution)/shard_map/ppermute | solution.py:18
  49.5 1.1 %copy-start = (bf16[512,768]{1,0:T(8,128)(2,1)S(1)}, bf16[512,768]{1,0:T(8,128)(2,1)}, u32[]{:S(2)}) copy-start(bf16[512,768]{1,0:T(8,128)(2,1)} %refs_0_) | copy-start | bytes 2359300
  51.3 14.9 %copy-start.5 = (s32[4]{0:T(128)S(1)}, s32[4]{0:T(128)}, u32[]{:S(2)}) copy-start(s32[4]{0:T(128)} %param.9) | copy-start | bytes 52
  51.3 14.9 %copy-start.6 = (s32[64]{0:T(128)S(1)}, s32[64]{0:T(128)}, u32[]{:S(2)}) copy-start(s32[64]{0:T(128)} %param.15) | copy-start | bytes 772
  64.2 2.1 %collective-permute-start.15 = (f32[4,128]{1,0:T(4,128)S(1)}, f32[4,128]{1,0:T(4,128)S(1)}, u32[]{:S(2)}, u32[]{:S(2)}) collective-permute-start(f32[4,128]{1,0:T(4,128)S(1)} %get-tuple-element.31), channel_id=1, source_target_pairs={{0,1},{1,0},{2,3},{3,2},{4,5},{5,4},{6,7},{7,6},{8,9},{9,8},{10,11... | collective-permute-start | bytes 6152 | tf_op jit(solution)/shard_map/ppermute | solution.py:23
  64.4 3.6 %collective-permute-start.16 = (f32[4,128]{1,0:T(4,128)S(1)}, f32[4,128]{1,0:T(4,128)S(1)}, u32[]{:S(2)}, u32[]{:S(2)}) collective-permute-start(f32[4,128]{1,0:T(4,128)S(1)} %get-tuple-element.33), channel_id=1, source_target_pairs={{0,2},{2,0},{4,6},{6,4},{8,10},{10,8},{12,14},{14,12},{1,3},{3,1},... | collective-permute-start | bytes 6152 | tf_op jit(solution)/shard_map/ppermute | solution.py:23
  65.0 3.1 %collective-permute-start.17 = (f32[4,128]{1,0:T(4,128)S(1)}, f32[4,128]{1,0:T(4,128)S(1)}, u32[]{:S(2)}, u32[]{:S(2)}) collective-permute-start(f32[4,128]{1,0:T(4,128)S(1)} %get-tuple-element.32), channel_id=1, source_target_pairs={{0,3},{1,2},{2,1},{3,0},{4,7},{5,6},{6,5},{7,4},{8,11},{9,10},{10,... | collective-permute-start | bytes 6152 | tf_op jit(solution)/shard_map/ppermute | solution.py:29
  (1 other events, 0.7 us)

commit v2 on v1

v2 whole, which is shorter than its diff:
```python
import functools
import math

import jax
import jax.numpy as jnp
from jax import lax
from jax.experimental import pallas as pl
from jax.experimental.pallas import tpu as pltpu
from jax.sharding import PartitionSpec as P

LANES = 128
LOG2E = 1.4426950408889634
DEAD = -1.0e30
SMEM = pl.BlockSpec(memory_space=pltpu.SMEM)
VMEM = pl.BlockSpec(memory_space=pltpu.VMEM)
PARAMS = pltpu.CompilerParams(vmem_limit_bytes=24 * 1024 * 1024)
COST = pl.CostEstimate(flops=1, bytes_accessed=1, transcendentals=0)


def turn(value, by):
    length = lax.axis_size("blk")
    return lax.ppermute(value, "blk", [(i, (i + by) % length) for i in range(length)])


def swap(value, axis):
    length = lax.axis_size(axis)
    return lax.ppermute(value, axis, [(i, i ^ 1) for i in range(length)])


def swap_both(value):
    nblk, nhelper = lax.axis_size("blk"), lax.axis_size("helper")
    pairs = [(i, (i ^ nhelper) ^ 1) for i in range(nblk * nhelper)]
    return lax.ppermute(value, ("blk", "helper"), pairs)


def rows_of(index, count=1):
    return pl.ds(pl.multiple_of(index * LANES, LANES), count * LANES)


def table_kernel(
    nhelper, chunks, helper_ref, clusters_ref, count_ref, rows_ref, ids_ref, out_ref
):
    lane = lax.broadcasted_iota(jnp.int32, (1, LANES), 1)
    live_rows = rows_ref[0]
    out_ref[...] = jnp.zeros_like(out_ref)
    for c in range(chunks):
        tile = helper_ref[0] + nhelper * c
        ids = ids_ref[pl.ds(tile, 1), :]
        out_ref[c : c + 1, :] = jnp.where(tile * LANES + lane < live_rows, ids, -1)
    qblocks = clusters_ref.shape[0]
    row = jnp.where(lane == qblocks, count_ref[0], 0)
    for k in range(qblocks):
        row = jnp.where(lane == k, clusters_ref[k], row)
    out_ref[chunks : chunks + 1, :] = row


def spread_kernel(chunks, nalong, *refs):
    tables, (info_ref, ids_ref, weight_ref) = refs[:-3], refs[-3:]
    info_ref[...] = jnp.zeros_like(info_ref)
    for k, table in enumerate((tables[0],) + tables[nalong:]):
        info_ref[k : k + 1, :] = table[chunks : chunks + 1, :]
    for s in range(nalong):
        for c in range(chunks):
            ids = jnp.broadcast_to(tables[s][c : c + 1, :], (LANES, LANES)).T
            rows = pl.ds((s * chunks + c) * LANES, LANES)
            ids_ref[rows, :] = ids
            weight_ref[rows, :] = jnp.where(ids < 0, DEAD, -4.0)


def score_kernel(
    chunks, base, qblocks, first, info_ref, beta_ref, ids_ref, weight_ref, *refs
):
    if first:
        q_refs, r_refs, (out_ref, qv, q_list) = refs[:4], refs[4:-3], refs[-3:]
    else:
        (qv, prev_ref), r_refs, (out_ref, q_list) = refs[:2], refs[2:-2], refs[-2:]
    width = qv.shape[1]

    q_count = jnp.int32(0)
    for source in range(4):
        blocks = info_ref[source, qblocks]

        def one_block(block, carry, source=source, q_count=q_count):
            if first:
                qv[rows_of(q_count + block), :] = q_refs[source][rows_of(block), :]
            q_list[q_count + block, 0] = source * qblocks + block
            q_list[q_count + block, 1] = info_ref[source, block]
            return carry

        lax.fori_loop(0, blocks, one_block, 0)
        q_count = q_count + blocks

    factor = LOG2E / math.sqrt(width)
    out_ref[...] = jnp.zeros_like(out_ref) if first else prev_ref[...]

    def two_query_blocks(group, carry):
        parts = []
        for side in range(2):
            entry = jnp.minimum(2 * group + side, q_count - 1)
            slot, cluster = q_list[entry, 0], q_list[entry, 1]
            beta = beta_ref[cluster]
            parts.append((slot, cluster, beta * factor, beta * beta * (0.5 * LOG2E)))
        blocks = qv[rows_of(2 * group, 2), :]
        accs = [jnp.zeros((8, LANES), jnp.float32) for _ in range(2)]
        for s in range(len(r_refs) // chunks):
            held = r_refs[s * chunks : (s + 1) * chunks]
            tile = jnp.concatenate([r[...] for r in held], axis=0)
            score = lax.dot_general(
                tile,
                blocks,
                (((1,), (1,)), ((), ())),
                preferred_element_type=jnp.float32,
            )
            height = tile.shape[0]
            rows = pl.ds((base + s) * height, height)
            ids, other = ids_ref[rows, :], weight_ref[rows, :]
            for side, (_, cluster, scale, offset) in enumerate(parts):
                part = score[:, side * LANES : (side + 1) * LANES]
                weight = jnp.where(ids == cluster, 0.0, other)
                value = jnp.exp2((part * scale - offset) + weight)
                accs[side] = accs[side] + jnp.sum(value.reshape(height // 8, 8, LANES), axis=0)
        for side in range(2):
            total = jnp.sum(accs[side], axis=0, keepdims=True)

            @pl.when(2 * group + side < q_count)
            def _(side=side, total=total):
                row = pl.ds(parts[side][0], 1)
                out_ref[row, :] = out_ref[row, :] + total

        return carry

    lax.fori_loop(0, (q_count + 1) // 2, two_query_blocks, 0)


def score_call(chunks, base, qblocks, info, beta, spread, queries, packed, prev, tiles):
    first = packed is None
    width = tiles[0].shape[1]
    slots = 4 * qblocks
    totals_shape = jax.ShapeDtypeStruct((slots, LANES), jnp.float32)
    packed_shape = jax.ShapeDtypeStruct((slots * LANES, width), jnp.bfloat16)
    given = queries if first else (packed, prev)
    return pl.pallas_call(
        functools.partial(score_kernel, chunks, base, qblocks, first),
        out_shape=(totals_shape, packed_shape) if first else totals_shape,
        in_specs=[SMEM, SMEM] + [VMEM] * (2 + len(given) + len(tiles)),
        out_specs=(VMEM, VMEM) if first else VMEM,
        scratch_shapes=[pltpu.SMEM((slots, 2), jnp.int32)],
        compiler_params=PARAMS,
        cost_estimate=COST,
    )(info, beta, *spread, *given, *tiles)


def per_device(
    queries,
    query_block_cluster,
    block_count,
    references,
    ref_cluster,
    ref_rows,
    cluster_beta,
    cluster_member_count,
):
    nblk, nhelper = lax.axis_size("blk"), lax.axis_size("helper")
    helper = lax.axis_index("helper").astype(jnp.int32)
    qblocks = query_block_cluster.shape[0]
    rows, width = references.shape
    tiles = rows // LANES
    chunks = tiles // nhelper
    sources = nblk // 2

    by_tile = references.reshape(tiles, LANES, width)
    own = [
        lax.dynamic_index_in_dim(by_tile, helper + nhelper * c, 0, keepdims=False)
        for c in range(chunks)
    ]
    own, queries, ref_cluster = lax.optimization_barrier((own, queries, ref_cluster))
    held = [own, [turn(x, 2) for x in own]]
    q_partner = swap(queries, "blk")
    q_helper = swap(queries, "helper")

    table = pl.pallas_call(
        functools.partial(table_kernel, nhelper, chunks),
        out_shape=jax.ShapeDtypeStruct((8 * ((chunks + 8) // 8), LANES), jnp.int32),
        in_specs=[SMEM] * 4 + [VMEM],
        out_specs=VMEM,
        compiler_params=PARAMS,
        cost_estimate=COST,
    )(
        helper[None],
        query_block_cluster,
        block_count,
        ref_rows,
        ref_cluster.reshape(tiles, LANES),
    )
    along = [table] + [turn(table, 2 * s) for s in range(1, sources)]
    around = [swap(table, "helper"), swap(table, "blk"), swap_both(table)]
    spread_shape = (sources * rows // nhelper, LANES)
    info, *spread = pl.pallas_call(
        functools.partial(spread_kernel, chunks, sources),
        out_shape=(
            jax.ShapeDtypeStruct((8, LANES), jnp.int32),
            jax.ShapeDtypeStruct(spread_shape, jnp.int32),
            jax.ShapeDtypeStruct(spread_shape, jnp.float32),
        ),
        in_specs=[VMEM] * (sources + 3),
        out_specs=(VMEM, VMEM, VMEM),
        compiler_params=PARAMS,
        cost_estimate=COST,
    )(*along, *around)

    for step in range(2, sources):
        ready = table if step == 2 else info
        if step == 2 or step == sources - 1:
            held[-1][0], ready = lax.optimization_barrier((held[-1][0], ready))
        if step == sources - 1:
            info = ready
        held.append([turn(x, 2) for x in held[-1]])
    q_partner, held[-2][-1] = lax.optimization_barrier((q_partner, held[-2][-1]))
    q_both = swap(q_partner, "helper")
    all_queries = (queries, q_helper, q_partner, q_both)

    early = [x for step in held[:-1] for x in step]
    totals, packed = score_call(
        chunks, 0, qblocks, info, cluster_beta, spread, all_queries, None, None, early
    )
    totals = score_call(
        chunks, sources - 1, qblocks, info, cluster_beta, spread, None, packed, totals, held[-1]
    )
    totals = totals.reshape(4, qblocks, LANES)
    total = totals[0] + swap(totals[1], "helper") + swap(totals[2], "blk") + swap_both(totals[3])
    columns = jnp.arange(cluster_member_count.shape[0], dtype=jnp.int32)
    onehot = query_block_cluster[:, None] == columns[None, :]
    sizes = jnp.sum(jnp.where(onehot, cluster_member_count[None, :], 0), axis=1)
    density = jnp.log1p(total / sizes.astype(jnp.float32)[:, None])
    return density.reshape(queries.shape[0])


def solution(mesh):
    in_specs = (
        P(("parts", "blk", "helper"), None),
        P(("parts", "blk", "helper")),
        P(("parts", "blk", "helper")),
        P(("parts", "blk"), None),
        P(("parts", "blk")),
        P(("parts", "blk")),
        P("parts"),
        P("parts"),
    )
    out_specs = P(("parts", "blk", "helper"))
    return jax.shard_map(
        per_device, mesh=mesh, in_specs=in_specs, out_specs=out_specs, check_vma=False
    )
```

time: 69.3 us -> 68.5 us (0.988)
  waiting for transfers between devices: 11.2 us -> 41.2 us
  local copies, waits for them, and re-layouts: 23.6 us -> 4.18 us
  Pallas kernels: 12.9 us -> 5.91 us
  starting transfers between devices: 16.8 us -> 14.3 us
  other arithmetic: 2.85 us -> 0.85 us
    ppermute x9, waiting for transfers between devices: 9.47 us -> 33.6 us  [turn(): lax.ppermute(value, 'blk', [(i, (i + by) % length) for i in range(length)])]
    slice x10 -> x0, local copies, waits for them, and re-layouts: 9.51 us -> none  [the longest x4 4.56 us: per_device(): m[chunks, qblocks + 1:qblocks + 2]]
    concatenate x2 -> x0, local copies, waits for them, and re-layouts: 7.09 us -> none  [the longest x1 5.72 us: per_device(): jnp.concatenate([m[chunks, :qblocks] for m in around] + [m[chunks, qblock...]
    pallas_call x2 -> x4, Pallas kernels: 12.9 us -> 5.91 us  [the longest x2 5.17 us: score_call(): pl.pallas_call(functools.partial(score_kernel, chunks, base, qblocks, fir...]
    ppermute x7, waiting for transfers between devices: 1.69 us -> 5.86 us  [swap(): return lax.ppermute(value, axis, [(i, i ^ 1) for i in range(length)])]
    squeeze x4 -> x0, local copies, waits for them, and re-layouts: 3.56 us -> none  [per_device(): m[chunks, :qblocks]]
    ppermute x2, starting transfers between devices: 2.72 us -> 0.33 us  [swap_both(): return lax.ppermute(value, ('blk', 'helper'), pairs)]
    ppermute x2, waiting for transfers between devices: 0.01 us -> 1.72 us  [swap_both(): return lax.ppermute(value, ('blk', 'helper'), pairs)]
  transfers between devices with their start and end apart: 18 -> 18, of which waited for: 5 -> 12; matrix products, arithmetic and copies ran while one was open for 33% -> 0% of each run, Pallas kernels for 12% -> 6%
where the time goes in v2:
time: 68.5 us; the launch traced here: 67.9 us
  waiting for transfers between devices  41.2 us (60%)
  starting transfers between devices  14.3 us (21%)
  Pallas kernels  5.91 us (9%)
  local copies, waits for them, and re-layouts  4.18 us (6%)
  between operations  1.45 us (2%)
  other arithmetic  0.85 us (1%)
    ppermute x9, waiting for transfers between devices, turn(): lax.ppermute(value, 'blk', [(i, (i + by) % length) for i in range(length)])  33.6 us
    ppermute x9, starting transfers between devices, turn(): lax.ppermute(value, 'blk', [(i, (i + by) % length) for i in range(length)])  7.88 us
    ppermute x7, starting transfers between devices, swap(): return lax.ppermute(value, axis, [(i, i ^ 1) for i in range(length)])  6.04 us
    ppermute x7, waiting for transfers between devices, swap(): return lax.ppermute(value, axis, [(i, i ^ 1) for i in range(length)])  5.86 us
    pallas_call x2, Pallas kernels, score_call(): pl.pallas_call(functools.partial(score_kernel, chunks, base, qblocks, fir...  5.17 us
    unnamed x12, local copies, waits for them, and re-layouts  3.13 us
    ppermute x2, waiting for transfers between devices, swap_both(): return lax.ppermute(value, ('blk', 'helper'), pairs)  1.72 us
  transfers between devices with their start and end apart: 18, of which 12 were waited for; matrix products, arithmetic and copies ran while one was open for 0% of the time, Pallas kernels for 6%

profile of v2, /device:TPU:0, one launch (start us, length us, event | category | flops | bytes accessed | tf_op | source)
XLA Modules:
  0.0 67.9 jit_solution(15920584927099612935)
XLA Ops:
  0.0 1.0 %dynamic-slice_bitcast_fusion = (bf16[128,768]{1,0:T(8,128)(2,1)S(1)}, bf16[128,768]{1,0:T(8,128)(2,1)S(1)}) fusion(bf16[4,128,768]{2,1,0:T(8,128)(2,1)} %bitcast.10, s32[]{:T(128)S(6)} %select_n.12, s32[]{:T(128)S(6)} %select_n.11), kind=kLoop, calls=%fused_computation | loop fusion | bytes 786440 | tf_op jit(solution)/shard_map/jit(dynamic_index_in_dim)/squeeze | solution.py:173
  1.1 3.0 %collective-permute-start.9 = (bf16[512,768]{1,0:T(8,128)(2,1)}, bf16[512,768]{1,0:T(8,128)(2,1)S(1)}, u32[]{:S(2)}, u32[]{:S(2)}) collective-permute-start(bf16[512,768]{1,0:T(8,128)(2,1)} %refs_0_), channel_id=1, source_target_pairs={{0,2},{2,0},{4,6},{6,4},{8,10},{10,8},{12,14},{14,12},{1,3},{3,1},... | collective-permute-start | bytes 2359304 | tf_op jit(solution)/shard_map/ppermute | solution.py:27
  4.1 1.6 %collective-permute-start.10 = (bf16[128,768]{1,0:T(8,128)(2,1)S(1)}, bf16[128,768]{1,0:T(8,128)(2,1)S(1)}, u32[]{:S(2)}, u32[]{:S(2)}) collective-permute-start(bf16[128,768]{1,0:T(8,128)(2,1)S(1)} %get-tuple-element.27.refs_5_), channel_id=1, source_target_pairs={{0,4},{2,6},{4,8},{6,10},{8,12},{10,14},{12,0},{14,2},{1,5},{3,7},... | collective-permute-start | bytes 589832 | tf_op jit(solution)/shard_map/ppermute | solution.py:22
  5.7 6.6 %collective-permute-done.10.refs_7_ = bf16[128,768]{1,0:T(8,128)(2,1)S(1)} collective-permute-done((bf16[128,768]{1,0:T(8,128)(2,1)S(1)}, bf16[128,768]{1,0:T(8,128)(2,1)S(1)}, u32[]{:S(2)}, u32[]{:S(2)}) %collective-permute-start.10) | collective-permute-done | bytes 196640 | tf_op jit(solution)/shard_map/ppermute | solution.py:22
  12.3 7.5 %collective-permute-done.11.refs_9_ = bf16[128,768]{1,0:T(8,128)(2,1)S(1)} collective-permute-done((bf16[128,768]{1,0:T(8,128)(2,1)S(1)}, bf16[128,768]{1,0:T(8,128)(2,1)S(1)}, u32[]{:S(2)}, u32[]{:S(2)}) %collective-permute-start.11) | collective-permute-done | bytes 196640 | tf_op jit(solution)/shard_map/ppermute | solution.py:22
  19.8 2.1 %collective-permute-done.9.refs_2_ = bf16[512,768]{1,0:T(8,128)(2,1)S(1)} collective-permute-done((bf16[512,768]{1,0:T(8,128)(2,1)}, bf16[512,768]{1,0:T(8,128)(2,1)S(1)}, u32[]{:S(2)}, u32[]{:S(2)}) %collective-permute-start.9) | collective-permute-done | bytes 786464 | tf_op jit(solution)/shard_map/ppermute | solution.py:27
  21.8 1.8 %collective-permute-start = (bf16[128,768]{1,0:T(8,128)(2,1)S(1)}, bf16[128,768]{1,0:T(8,128)(2,1)S(1)}, u32[]{:S(2)}, u32[]{:S(2)}) collective-permute-start(bf16[128,768]{1,0:T(8,128)(2,1)S(1)} %get-tuple-element.19.refs_4_), channel_id=1, source_target_pairs={{0,4},{2,6},{4,8},{6,10},{8,12},{10,14},{12,0},{14,2},{1,5},{3,7},... | collective-permute-start | bytes 589832 | tf_op jit(solution)/shard_map/ppermute | solution.py:22
  24.9 0.7 copy-done.2
  26.8 4.4 %collective-permute-done.refs_6_ = bf16[128,768]{1,0:T(8,128)(2,1)S(1)} collective-permute-done((bf16[128,768]{1,0:T(8,128)(2,1)S(1)}, bf16[128,768]{1,0:T(8,128)(2,1)S(1)}, u32[]{:S(2)}, u32[]{:S(2)}) %collective-permute-start) | collective-permute-done | bytes 196640 | tf_op jit(solution)/shard_map/ppermute | solution.py:22
  31.2 1.3 %collective-permute-start.2 = (s32[8,128]{1,0:T(8,128)S(1)}, s32[8,128]{1,0:T(8,128)S(1)}, u32[]{:S(2)}, u32[]{:S(2)}) collective-permute-start(s32[8,128]{1,0:T(8,128)S(1)} %shard_map.82.refs_0_), channel_id=1, source_target_pairs={{0,4},{2,6},{4,8},{6,10},{8,12},{10,14},{12,0},{14,2},{1,5},{3,7},... | collective-permute-start | bytes 12296 | tf_op jit(solution)/shard_map/ppermute | solution.py:22
  32.5 3.1 %collective-permute-start.3 = (s32[8,128]{1,0:T(8,128)S(1)}, s32[8,128]{1,0:T(8,128)S(1)}, u32[]{:S(2)}, u32[]{:S(2)}) collective-permute-start(s32[8,128]{1,0:T(8,128)S(1)} %shard_map.82.refs_0_), channel_id=1, source_target_pairs={{0,8},{2,10},{4,12},{6,14},{8,0},{10,2},{12,4},{14,6},{1,9},{3,11}... | collective-permute-start | bytes 12296 | tf_op jit(solution)/shard_map/ppermute | solution.py:22
  35.6 4.4 %collective-permute-done.2.refs_1_ = s32[8,128]{1,0:T(8,128)S(1)} collective-permute-done((s32[8,128]{1,0:T(8,128)S(1)}, s32[8,128]{1,0:T(8,128)S(1)}, u32[]{:S(2)}, u32[]{:S(2)}) %collective-permute-start.2) | collective-permute-done | bytes 4128 | tf_op jit(solution)/shard_map/ppermute | solution.py:22
  40.0 3.6 %collective-permute-done.4.refs_3_ = s32[8,128]{1,0:T(8,128)S(1)} collective-permute-done((s32[8,128]{1,0:T(8,128)S(1)}, s32[8,128]{1,0:T(8,128)S(1)}, u32[]{:S(2)}, u32[]{:S(2)}) %collective-permute-start.4) | collective-permute-done | bytes 4128 | tf_op jit(solution)/shard_map/ppermute | solution.py:22
  43.6 1.4 %collective-permute-start.6 = (s32[8,128]{1,0:T(8,128)S(1)}, s32[8,128]{1,0:T(8,128)S(1)}, u32[]{:S(2)}, u32[]{:S(2)}) collective-permute-start(s32[8,128]{1,0:T(8,128)S(1)} %shard_map.82.refs_0_), channel_id=1, source_target_pairs={{0,2},{2,0},{4,6},{6,4},{8,10},{10,8},{12,14},{14,12},{1,3},{3,1},... | collective-permute-start | bytes 12296 | tf_op jit(solution)/shard_map/ppermute | solution.py:27
  45.0 2.2 %collective-permute-done.6.refs_5_ = s32[8,128]{1,0:T(8,128)S(1)} collective-permute-done((s32[8,128]{1,0:T(8,128)S(1)}, s32[8,128]{1,0:T(8,128)S(1)}, u32[]{:S(2)}, u32[]{:S(2)}) %collective-permute-start.6) | collective-permute-done | bytes 4128 | tf_op jit(solution)/shard_map/ppermute | solution.py:27
  47.2 0.8 %collective-permute-done.7.refs_6_ = s32[8,128]{1,0:T(8,128)S(1)} collective-permute-done((s32[8,128]{1,0:T(8,128)S(1)}, s32[8,128]{1,0:T(8,128)S(1)}, u32[]{:S(2)}, u32[]{:S(2)}) %collective-permute-start.7) | collective-permute-done | bytes 4128 | tf_op jit(solution)/shard_map/ppermute | solution.py:33
  48.4 1.1 %copy-done = bf16[512,768]{1,0:T(8,128)(2,1)S(1)} copy-done((bf16[512,768]{1,0:T(8,128)(2,1)S(1)}, bf16[512,768]{1,0:T(8,128)(2,1)}, u32[]{:S(2)}) %copy-start) | copy-done | bytes 786456
  50.2 3.0 %shard_map.84 = (f32[16,128]{1,0:T(8,128)S(1)}, bf16[2048,768]{1,0:T(8,128)(2,1)S(1)}) custom-call(s32[8,128]{1,0:T(8,128)S(1)} %get-tuple-element.23.info_ref, f32[64]{0:T(128)S(1)} %copy-done.1, s32[1024,128]{1,0:T(8,128)S(1)} %get-tuple-element.24.ids_ref, f32[1024,128]{1,0:T(8,128)S(1)} %get-tuple-element.25.weight_ref, bf16[512,768]{1,0:T(8,128)(2,1)S(1)} %copy-done, ...), custom_call_target="tpu_custom_call" | custom-call | flops 1 | bytes 1 | tf_op jit(solution)/shard_map/pallas_call | solution.py:142
  53.3 4.7 %collective-permute-done.13.refs_2_ = bf16[128,768]{1,0:T(8,128)(2,1)S(1)} collective-permute-done((bf16[128,768]{1,0:T(8,128)(2,1)S(1)}, bf16[128,768]{1,0:T(8,128)(2,1)S(1)}, u32[]{:S(2)}, u32[]{:S(2)}) %collective-permute-start.13) | collective-permute-done | bytes 196640 | tf_op jit(solution)/shard_map/ppermute | solution.py:22
  58.0 2.5 %collective-permute-done.14.refs_3_ = bf16[128,768]{1,0:T(8,128)(2,1)S(1)} collective-permute-done((bf16[128,768]{1,0:T(8,128)(2,1)S(1)}, bf16[128,768]{1,0:T(8,128)(2,1)S(1)}, u32[]{:S(2)}, u32[]{:S(2)}) %collective-permute-start.14) | collective-permute-done | bytes 196640 | tf_op jit(solution)/shard_map/ppermute | solution.py:22
  60.4 2.1 %shard_map.85 = f32[16,128]{1,0:T(8,128)S(1)} custom-call(s32[8,128]{1,0:T(8,128)S(1)} %get-tuple-element.23.info_ref, f32[64]{0:T(128)S(1)} %copy-done.1, s32[1024,128]{1,0:T(8,128)S(1)} %get-tuple-element.24.ids_ref, f32[1024,128]{1,0:T(8,128)S(1)} %get-tuple-element.25.weight_ref, bf16[2048,768]{1,0:T(8,128)(2,1)S(1)} %get-tuple-element.31.refs_0_, ...), custom_call_target="tpu_custom_call" | custom-call | flops 1 | bytes 1 | tf_op jit(solution)/shard_map/pallas_call | solution.py:142
  62.7 1.5 %collective-permute-start.16 = (f32[4,128]{1,0:T(4,128)S(1)}, f32[4,128]{1,0:T(4,128)S(1)}, u32[]{:S(2)}, u32[]{:S(2)}) collective-permute-start(f32[4,128]{1,0:T(4,128)S(1)} %get-tuple-element.37), channel_id=1, source_target_pairs={{0,2},{2,0},{4,6},{6,4},{8,10},{10,8},{12,14},{14,12},{1,3},{3,1},... | collective-permute-start | bytes 6152 | tf_op jit(solution)/shard_map/ppermute | solution.py:27
  64.7 1.6 %collective-permute-done.16 = f32[4,128]{1,0:T(4,128)S(1)} collective-permute-done((f32[4,128]{1,0:T(4,128)S(1)}, f32[4,128]{1,0:T(4,128)S(1)}, u32[]{:S(2)}, u32[]{:S(2)}) %collective-permute-start.16) | collective-permute-done | bytes 2080 | tf_op jit(solution)/shard_map/ppermute | solution.py:27
  66.3 0.9 %collective-permute-done.17 = f32[4,128]{1,0:T(4,128)S(1)} collective-permute-done((f32[4,128]{1,0:T(4,128)S(1)}, f32[4,128]{1,0:T(4,128)S(1)}, u32[]{:S(2)}, u32[]{:S(2)}) %collective-permute-start.17) | collective-permute-done | bytes 2080 | tf_op jit(solution)/shard_map/ppermute | solution.py:33
  (33 shorter events, 3.5 us)
Async XLA Ops:
  1.1 20.8 %collective-permute-start.9 = (bf16[512,768]{1,0:T(8,128)(2,1)}, bf16[512,768]{1,0:T(8,128)(2,1)S(1)}, u32[]{:S(2)}, u32[]{:S(2)}) collective-permute-start(bf16[512,768]{1,0:T(8,128)(2,1)} %refs_0_), channel_id=1, source_target_pairs={{0,2},{2,0},{4,6},{6,4},{8,10},{10,8},{12,14},{14,12},{1,3},{3,1},... | collective-permute-start | bytes 2359304 | tf_op jit(solution)/shard_map/ppermute | solution.py:27
  4.1 8.2 %collective-permute-start.10 = (bf16[128,768]{1,0:T(8,128)(2,1)S(1)}, bf16[128,768]{1,0:T(8,128)(2,1)S(1)}, u32[]{:S(2)}, u32[]{:S(2)}) collective-permute-start(bf16[128,768]{1,0:T(8,128)(2,1)S(1)} %get-tuple-element.27.refs_5_), channel_id=1, source_target_pairs={{0,4},{2,6},{4,8},{6,10},{8,12},{10,14},{12,0},{14,2},{1,5},{3,7},... | collective-permute-start | bytes 589832 | tf_op jit(solution)/shard_map/ppermute | solution.py:22
  12.3 7.5 %collective-permute-start.11 = (bf16[128,768]{1,0:T(8,128)(2,1)S(1)}, bf16[128,768]{1,0:T(8,128)(2,1)S(1)}, u32[]{:S(2)}, u32[]{:S(2)}) collective-permute-start(bf16[128,768]{1,0:T(8,128)(2,1)S(1)} %collective-permute-done.10.refs_7_), channel_id=1, source_target_pairs={{0,4},{2,6},{4,8},{6,10},{8,12},{10,14},{12,0},{14,2},{1,5},{3,7},... | collective-permute-start | bytes 589832 | tf_op jit(solution)/shard_map/ppermute | solution.py:22
  12.3 36.1 %collective-permute-start.8 = (bf16[512,768]{1,0:T(8,128)(2,1)}, bf16[512,768]{1,0:T(8,128)(2,1)S(1)}, u32[]{:S(2)}, u32[]{:S(2)}) collective-permute-start(bf16[512,768]{1,0:T(8,128)(2,1)} %refs_0_), channel_id=1, source_target_pairs={{0,1},{1,0},{2,3},{3,2},{4,5},{5,4},{6,7},{7,6},{8,9},{9,8},{10,11... | collective-permute-start | bytes 2359304 | tf_op jit(solution)/shard_map/ppermute | solution.py:27
  21.8 26.6 %collective-permute-start.12 = (bf16[512,768]{1,0:T(8,128)(2,1)S(1)}, bf16[512,768]{1,0:T(8,128)(2,1)S(1)}, u32[]{:S(2)}, u32[]{:S(2)}) collective-permute-start(bf16[512,768]{1,0:T(8,128)(2,1)S(1)} %collective-permute-done.9.refs_2_), channel_id=1, source_target_pairs={{0,1},{1,0},{2,3},{3,2},{4,5},{5,4},{6,7},{7,6},{8,9},{9,8},{10,11... | collective-permute-start | bytes 2359304 | tf_op jit(solution)/shard_map/ppermute | solution.py:27
  21.8 9.4 %collective-permute-start = (bf16[128,768]{1,0:T(8,128)(2,1)S(1)}, bf16[128,768]{1,0:T(8,128)(2,1)S(1)}, u32[]{:S(2)}, u32[]{:S(2)}) collective-permute-start(bf16[128,768]{1,0:T(8,128)(2,1)S(1)} %get-tuple-element.19.refs_4_), channel_id=1, source_target_pairs={{0,4},{2,6},{4,8},{6,10},{8,12},{10,14},{12,0},{14,2},{1,5},{3,7},... | collective-permute-start | bytes 589832 | tf_op jit(solution)/shard_map/ppermute | solution.py:22
  24.9 0.7 %copy-start.2 = (s32[512]{0:T(512)S(1)}, s32[512]{0:T(512)}, u32[]{:S(2)}) copy-start(s32[512]{0:T(512)} %param.12) | copy-start | bytes 6148
  25.6 0.7 copy-start.3
  31.2 17.0 %collective-permute-start.1 = (bf16[128,768]{1,0:T(8,128)(2,1)S(1)}, bf16[128,768]{1,0:T(8,128)(2,1)S(1)}, u32[]{:S(2)}, u32[]{:S(2)}) collective-permute-start(bf16[128,768]{1,0:T(8,128)(2,1)S(1)} %collective-permute-done.refs_6_), channel_id=1, source_target_pairs={{0,4},{2,6},{4,8},{6,10},{8,12},{10,14},{12,0},{14,2},{1,5},{3,7},... | collective-permute-start | bytes 589832 | tf_op jit(solution)/shard_map/ppermute | solution.py:22
  31.2 8.8 %collective-permute-start.2 = (s32[8,128]{1,0:T(8,128)S(1)}, s32[8,128]{1,0:T(8,128)S(1)}, u32[]{:S(2)}, u32[]{:S(2)}) collective-permute-start(s32[8,128]{1,0:T(8,128)S(1)} %shard_map.82.refs_0_), channel_id=1, source_target_pairs={{0,4},{2,6},{4,8},{6,10},{8,12},{10,14},{12,0},{14,2},{1,5},{3,7},... | collective-permute-start | bytes 12296 | tf_op jit(solution)/shard_map/ppermute | solution.py:22
  32.5 7.5 %collective-permute-start.3 = (s32[8,128]{1,0:T(8,128)S(1)}, s32[8,128]{1,0:T(8,128)S(1)}, u32[]{:S(2)}, u32[]{:S(2)}) collective-permute-start(s32[8,128]{1,0:T(8,128)S(1)} %shard_map.82.refs_0_), channel_id=1, source_target_pairs={{0,8},{2,10},{4,12},{6,14},{8,0},{10,2},{12,4},{14,6},{1,9},{3,11}... | collective-permute-start | bytes 12296 | tf_op jit(solution)/shard_map/ppermute | solution.py:22
  40.0 3.6 %collective-permute-start.4 = (s32[8,128]{1,0:T(8,128)S(1)}, s32[8,128]{1,0:T(8,128)S(1)}, u32[]{:S(2)}, u32[]{:S(2)}) collective-permute-start(s32[8,128]{1,0:T(8,128)S(1)} %shard_map.82.refs_0_), channel_id=1, source_target_pairs={{0,12},{2,14},{4,0},{6,2},{8,4},{10,6},{12,8},{14,10},{1,13},{3,15... | collective-permute-start | bytes 12296 | tf_op jit(solution)/shard_map/ppermute | solution.py:22
  40.0 5.0 %collective-permute-start.5 = (s32[8,128]{1,0:T(8,128)S(1)}, s32[8,128]{1,0:T(8,128)S(1)}, u32[]{:S(2)}, u32[]{:S(2)}) collective-permute-start(s32[8,128]{1,0:T(8,128)S(1)} %shard_map.82.refs_0_), channel_id=1, source_target_pairs={{0,1},{1,0},{2,3},{3,2},{4,5},{5,4},{6,7},{7,6},{8,9},{9,8},{10,11... | collective-permute-start | bytes 12296 | tf_op jit(solution)/shard_map/ppermute | solution.py:27
  43.6 3.6 %collective-permute-start.6 = (s32[8,128]{1,0:T(8,128)S(1)}, s32[8,128]{1,0:T(8,128)S(1)}, u32[]{:S(2)}, u32[]{:S(2)}) collective-permute-start(s32[8,128]{1,0:T(8,128)S(1)} %shard_map.82.refs_0_), channel_id=1, source_target_pairs={{0,2},{2,0},{4,6},{6,4},{8,10},{10,8},{12,14},{14,12},{1,3},{3,1},... | collective-permute-start | bytes 12296 | tf_op jit(solution)/shard_map/ppermute | solution.py:27
  45.0 3.0 %collective-permute-start.7 = (s32[8,128]{1,0:T(8,128)S(1)}, s32[8,128]{1,0:T(8,128)S(1)}, u32[]{:S(2)}, u32[]{:S(2)}) collective-permute-start(s32[8,128]{1,0:T(8,128)S(1)} %shard_map.82.refs_0_), channel_id=1, source_target_pairs={{0,3},{1,2},{2,1},{3,0},{4,7},{5,6},{6,5},{7,4},{8,11},{9,10},{10,... | collective-permute-start | bytes 12296 | tf_op jit(solution)/shard_map/ppermute | solution.py:33
  48.3 9.7 %collective-permute-start.13 = (bf16[128,768]{1,0:T(8,128)(2,1)S(1)}, bf16[128,768]{1,0:T(8,128)(2,1)S(1)}, u32[]{:S(2)}, u32[]{:S(2)}) collective-permute-start(bf16[128,768]{1,0:T(8,128)(2,1)S(1)} %collective-permute-done.1.refs_8_), channel_id=1, source_target_pairs={{0,4},{2,6},{4,8},{6,10},{8,12},{10,14},{12,0},{14,2},{1,5},{3,7},... | collective-permute-start | bytes 589832 | tf_op jit(solution)/shard_map/ppermute | solution.py:22
  48.3 12.1 %collective-permute-start.14 = (bf16[128,768]{1,0:T(8,128)(2,1)S(1)}, bf16[128,768]{1,0:T(8,128)(2,1)S(1)}, u32[]{:S(2)}, u32[]{:S(2)}) collective-permute-start(bf16[128,768]{1,0:T(8,128)(2,1)S(1)} %collective-permute-done.11.refs_9_), channel_id=1, source_target_pairs={{0,4},{2,6},{4,8},{6,10},{8,12},{10,14},{12,0},{14,2},{1,5},{3,7},... | collective-permute-start | bytes 589832 | tf_op jit(solution)/shard_map/ppermute | solution.py:22
  48.4 1.1 %copy-start = (bf16[512,768]{1,0:T(8,128)(2,1)S(1)}, bf16[512,768]{1,0:T(8,128)(2,1)}, u32[]{:S(2)}) copy-start(bf16[512,768]{1,0:T(8,128)(2,1)} %refs_0_) | copy-start | bytes 2359300
  49.6 0.7 copy-start.1
  53.3 11.2 %copy-start.4 = (s32[4]{0:T(128)S(1)}, s32[4]{0:T(128)}, u32[]{:S(2)}) copy-start(s32[4]{0:T(128)} %clusters_ref.1) | copy-start | bytes 52
  53.3 11.2 %copy-start.5 = (s32[64]{0:T(128)S(1)}, s32[64]{0:T(128)}, u32[]{:S(2)}) copy-start(s32[64]{0:T(128)} %param.15) | copy-start | bytes 772
  62.6 2.1 %collective-permute-start.15 = (f32[4,128]{1,0:T(4,128)S(1)}, f32[4,128]{1,0:T(4,128)S(1)}, u32[]{:S(2)}, u32[]{:S(2)}) collective-permute-start(f32[4,128]{1,0:T(4,128)S(1)} %get-tuple-element.35), channel_id=1, source_target_pairs={{0,1},{1,0},{2,3},{3,2},{4,5},{5,4},{6,7},{7,6},{8,9},{9,8},{10,11... | collective-permute-start | bytes 6152 | tf_op jit(solution)/shard_map/ppermute | solution.py:27
  62.7 3.7 %collective-permute-start.16 = (f32[4,128]{1,0:T(4,128)S(1)}, f32[4,128]{1,0:T(4,128)S(1)}, u32[]{:S(2)}, u32[]{:S(2)}) collective-permute-start(f32[4,128]{1,0:T(4,128)S(1)} %get-tuple-element.37), channel_id=1, source_target_pairs={{0,2},{2,0},{4,6},{6,4},{8,10},{10,8},{12,14},{14,12},{1,3},{3,1},... | collective-permute-start | bytes 6152 | tf_op jit(solution)/shard_map/ppermute | solution.py:27
  64.2 3.0 %collective-permute-start.17 = (f32[4,128]{1,0:T(4,128)S(1)}, f32[4,128]{1,0:T(4,128)S(1)}, u32[]{:S(2)}, u32[]{:S(2)}) collective-permute-start(f32[4,128]{1,0:T(4,128)S(1)} %get-tuple-element.36), channel_id=1, source_target_pairs={{0,3},{1,2},{2,1},{3,0},{4,7},{5,6},{6,5},{7,4},{8,11},{9,10},{10,... | collective-permute-start | bytes 6152 | tf_op jit(solution)/shard_map/ppermute | solution.py:33

commit v3 on v2

v3 whole, which is shorter than its diff:
```python
import functools
import math

import jax
import jax.numpy as jnp
from jax import lax
from jax.experimental import pallas as pl
from jax.experimental.pallas import tpu as pltpu
from jax.sharding import PartitionSpec as P

LANES = 128
TABLE = 16
LOG2E = 1.4426950408889634
DEAD = -1.0e30
SMEM = pl.BlockSpec(memory_space=pltpu.SMEM)
VMEM = pl.BlockSpec(memory_space=pltpu.VMEM)
HBM = pl.BlockSpec(memory_space=pltpu.HBM)
WHOLE = pltpu.CompilerParams(vmem_limit_bytes=60 * 1024 * 1024)
PARAMS = pltpu.CompilerParams(vmem_limit_bytes=24 * 1024 * 1024)
COST = pl.CostEstimate(flops=1, bytes_accessed=1, transcendentals=0)


def turn(value, by):
    length = lax.axis_size("blk")
    return lax.ppermute(value, "blk", [(i, (i + by) % length) for i in range(length)])


def swap(value, axis):
    length = lax.axis_size(axis)
    return lax.ppermute(value, axis, [(i, i ^ 1) for i in range(length)])


def swap_both(value):
    nblk, nhelper = lax.axis_size("blk"), lax.axis_size("helper")
    pairs = [(i, (i ^ nhelper) ^ 1) for i in range(nblk * nhelper)]
    return lax.ppermute(value, ("blk", "helper"), pairs)


def after(value, *others):
    return lax.optimization_barrier((value, *others))[0]


def rows_of(index, count=1):
    return pl.ds(pl.multiple_of(index * LANES, LANES), count * LANES)


def pack_refs_kernel(nhelper, helper_ref, r_ref, ids_ref, live_ref, *refs):
    outs, (ids, live, sem) = refs[:-3], refs[-3:]
    n = len(outs)
    copies = [
        pltpu.make_async_copy(ids_ref, ids, sem.at[n]),
        pltpu.make_async_copy(live_ref, live, sem.at[n + 1]),
    ]
    for c, out in enumerate(outs):
        rows = rows_of(helper_ref[0] + nhelper * c)
        copies.append(pltpu.make_async_copy(r_ref.at[rows], out.at[pl.ds(0, LANES)], sem.at[c]))
    for copy in copies:
        copy.start()
    copies[0].wait()
    copies[1].wait()
    lane = lax.broadcasted_iota(jnp.int32, (TABLE, LANES), 1)
    row = lax.broadcasted_iota(jnp.int32, (TABLE, LANES), 0)
    table = jnp.full((TABLE, LANES), -1, jnp.int32)
    for c in range(n):
        tile = helper_ref[0] + nhelper * c
        here = jnp.where(tile * LANES + lane < live[0], ids[pl.ds(tile, 1), :], -1)
        table = jnp.where(row == c, here, table)
    outs[0][pl.ds(LANES, TABLE), pl.ds(0, LANES)] = table.astype(jnp.float32).astype(jnp.bfloat16)
    for copy in copies[2:]:
        copy.wait()


def pack_queries_kernel(q_ref, clusters_ref, count_ref, out, clusters, count, sem):
    copies = (
        pltpu.make_async_copy(clusters_ref, clusters, sem.at[0]),
        pltpu.make_async_copy(count_ref, count, sem.at[1]),
        pltpu.make_async_copy(q_ref, out.at[pl.ds(0, q_ref.shape[0])], sem.at[2]),
    )
    for copy in copies:
        copy.start()
    copies[0].wait()
    copies[1].wait()
    lane = lax.broadcasted_iota(jnp.int32, (TABLE, LANES), 1)
    qblocks = clusters_ref.shape[0]
    table = jnp.where(lane == qblocks, count[0], 0)
    for k in range(qblocks):
        table = jnp.where(lane == k, clusters[k], table)
    out[pl.ds(q_ref.shape[0], TABLE), pl.ds(0, LANES)] = table.astype(jnp.float32).astype(
        jnp.bfloat16
    )
    copies[2].wait()


def score_kernel(chunks, qblocks, first, wide, beta_ref, *refs):
    if first:
        q_refs, refs = refs[:4], refs[4:]
        r_refs, (out_ref, qv, info_out, q_list, info, ids_ref, other_ref, sem) = refs[:-8], refs[-8:]
    else:
        (info, qv, prev_ref), refs = refs[:3], refs[3:]
        r_refs, (out_ref, q_list, ids_ref, other_ref) = refs[:-4], refs[-4:]
    width = qv.shape[1]
    sources = len(r_refs) // chunks
    if first:
        for s, q_ref in enumerate(q_refs):
            table = q_ref[pl.ds(qblocks * LANES, TABLE), pl.ds(0, LANES)].astype(jnp.float32)
            info_out[s : s + 1, :] = table[0:1, :].astype(jnp.int32)
        copy = pltpu.make_async_copy(info_out, info, sem)
        copy.start()

    for s in range(sources):
        table = r_refs[s * chunks][pl.ds(LANES, TABLE), pl.ds(0, LANES)].astype(jnp.float32)
        for c in range(chunks):
            ids = jnp.broadcast_to(table[c : c + 1, :], (LANES, LANES)).T
            rows = pl.ds((s * chunks + c) * LANES, LANES)
            ids_ref[rows, :] = ids
            other_ref[rows, :] = jnp.where(ids < 0.0, DEAD, -4.0)
    if first:
        copy.wait()

    q_count = jnp.int32(0)
    for source in range(4):
        blocks = info[source, qblocks]

        def one_block(block, carry, source=source, q_count=q_count):
            if first:
                qv[rows_of(q_count + block), :] = q_refs[source][rows_of(block), :]
            q_list[q_count + block, 0] = source * qblocks + block
            q_list[q_count + block, 1] = info[source, block]
            return carry

        lax.fori_loop(0, blocks, one_block, 0)
        q_count = q_count + blocks

    factor = LOG2E / math.sqrt(width)
    out_ref[...] = jnp.zeros_like(out_ref) if first else prev_ref[...]

    def query_blocks(group, carry):
        parts = []
        for side in range(wide):
            entry = jnp.minimum(wide * group + side, q_count - 1)
            slot, cluster = q_list[entry, 0], q_list[entry, 1]
            beta = beta_ref[cluster]
            parts.append(
                (slot, cluster.astype(jnp.float32), beta * factor, beta * beta * (0.5 * LOG2E))
            )
        accs = [jnp.zeros((8, LANES), jnp.float32) for _ in range(wide)]
        for s in range(sources):
            held = r_refs[s * chunks : (s + 1) * chunks]
            tile = jnp.concatenate([r[pl.ds(0, LANES), :] for r in held], axis=0)
            height = tile.shape[0]
            rows = pl.ds(s * height, height)
            for pair in range(wide // 2):
                score = lax.dot_general(
                    tile,
                    qv[rows_of(wide * group + 2 * pair, 2), :],
                    (((1,), (1,)), ((), ())),
                    preferred_element_type=jnp.float32,
                )
                for half in range(2):
                    side = 2 * pair + half
                    _, cluster, scale, offset = parts[side]
                    part = score[:, half * LANES : (half + 1) * LANES]
                    weight = jnp.where(ids_ref[rows, :] == cluster, 0.0, other_ref[rows, :])
                    value = jnp.exp2((part * scale - offset) + weight)
                    accs[side] += jnp.sum(value.reshape(height // 8, 8, LANES), axis=0)
        for side in range(wide):
            total = jnp.sum(accs[side], axis=0, keepdims=True)

            @pl.when(wide * group + side < q_count)
            def _(side=side, total=total):
                row = pl.ds(parts[side][0], 1)
                out_ref[row, :] = out_ref[row, :] + total

        return carry

    lax.fori_loop(0, (q_count + wide - 1) // wide, query_blocks, 0)


def score_call(chunks, qblocks, wide, beta, given, tiles, first):
    width = tiles[0].shape[1]
    slots = 4 * qblocks
    totals_shape = jax.ShapeDtypeStruct((slots, LANES), jnp.float32)
    packed_shape = jax.ShapeDtypeStruct((slots * LANES, width), jnp.bfloat16)
    info_shape = jax.ShapeDtypeStruct((8, LANES), jnp.int32)
    q_list = pltpu.SMEM((slots, 2), jnp.int32)
    spread = pltpu.VMEM((len(tiles) * LANES, LANES), jnp.float32)
    info = pltpu.SMEM((8, LANES), jnp.int32)
    return pl.pallas_call(
        functools.partial(score_kernel, chunks, qblocks, first, wide),
        out_shape=(totals_shape, packed_shape, info_shape) if first else totals_shape,
        in_specs=[SMEM, VMEM if first else SMEM] + [VMEM] * (len(given) - 1 + len(tiles)),
        out_specs=(VMEM, VMEM, VMEM) if first else VMEM,
        scratch_shapes=[q_list, info, spread, spread, pltpu.SemaphoreType.DMA]
        if first
        else [q_list, spread, spread],
        compiler_params=PARAMS,
        cost_estimate=COST,
    )(beta, *given, *tiles)


def per_device(
    queries,
    query_block_cluster,
    block_count,
    references,
    ref_cluster,
    ref_rows,
    cluster_beta,
    cluster_member_count,
):
    nblk, nhelper = lax.axis_size("blk"), lax.axis_size("helper")
    helper = lax.axis_index("helper").astype(jnp.int32)
    qblocks = query_block_cluster.shape[0]
    q_rows, (rows, width) = queries.shape[0], references.shape
    tiles = rows // LANES
    chunks = tiles // nhelper
    sources = nblk // 2

    own = pl.pallas_call(
        functools.partial(pack_refs_kernel, nhelper),
        out_shape=[
            jax.ShapeDtypeStruct((LANES + (TABLE if c == 0 else 0), width), jnp.bfloat16)
            for c in range(chunks)
        ],
        in_specs=[SMEM] + [HBM] * 3,
        out_specs=[VMEM] * chunks,
        scratch_shapes=[
            pltpu.VMEM((tiles, LANES), jnp.int32),
            pltpu.SMEM((1,), jnp.int32),
            pltpu.SemaphoreType.DMA((chunks + 2,)),
        ],
        compiler_params=WHOLE,
        cost_estimate=COST,
    )(helper[None], references, ref_cluster.reshape(tiles, LANES), ref_rows)
    q_own = pl.pallas_call(
        pack_queries_kernel,
        out_shape=jax.ShapeDtypeStruct((q_rows + TABLE, width), jnp.bfloat16),
        in_specs=[HBM] * 3,
        out_specs=VMEM,
        scratch_shapes=[
            pltpu.SMEM((qblocks,), jnp.int32),
            pltpu.SMEM((1,), jnp.int32),
            pltpu.SemaphoreType.DMA((3,)),
        ],
        compiler_params=WHOLE,
        cost_estimate=COST,
    )(after(queries, *own), query_block_cluster, block_count)
    q_partner = swap(q_own, "blk")
    q_helper = swap(q_own, "helper")
    held = [own]
    for step in range(1, sources):
        sent = []
        for c in range(chunks):
            if c > 0 and step > 1:
                waits = [held[step - 1][c - 1]]
            elif c == 0 and step > 2:
                waits = [held[step - 2][-1]]
            else:
                waits = []
            sent.append(turn(after(held[step - 1][c], *waits), 2))
        held.append(sent)
    q_both = swap(after(q_partner, *held[-2]), "helper")

    early = [x for step in held[:-1] for x in step]
    totals, packed, info = score_call(
        chunks, qblocks, 2, cluster_beta, (q_own, q_helper, q_partner, q_both), early, True
    )
    totals = score_call(
        chunks, qblocks, 4, cluster_beta, (info, packed, totals), held[-1], False
    )
    totals = totals.reshape(4, qblocks, LANES)
    total = totals[0] + swap(totals[1], "helper") + swap(totals[2], "blk") + swap_both(totals[3])
    columns = jnp.arange(cluster_member_count.shape[0], dtype=jnp.int32)
    onehot = query_block_cluster[:, None] == columns[None, :]
    sizes = jnp.sum(jnp.where(onehot, cluster_member_count[None, :], 0), axis=1)
    density = jnp.log1p(total / sizes.astype(jnp.float32)[:, None])
    return density.reshape(queries.shape[0])


def solution(mesh):
    in_specs = (
        P(("parts", "blk", "helper"), None),
        P(("parts", "blk", "helper")),
        P(("parts", "blk", "helper")),
        P(("parts", "blk"), None),
        P(("parts", "blk")),
        P(("parts", "blk")),
        P("parts"),
        P("parts"),
    )
    out_specs = P(("parts", "blk", "helper"))
    return jax.shard_map(
        per_device, mesh=mesh, in_specs=in_specs, out_specs=out_specs, check_vma=False
    )
```

time: 68.5 us -> 51 us (0.74)
  waiting for transfers between devices: 41.2 us -> 25.6 us
  starting transfers between devices: 14.3 us -> 9.7 us
  Pallas kernels: 5.91 us -> 9.25 us
    ppermute x9 -> x6, waiting for transfers between devices: 33.6 us -> 23.2 us  [turn(): lax.ppermute(value, 'blk', [(i, (i + by) % length) for i in range(length)])]
    ppermute x7 -> x5, waiting for transfers between devices: 5.86 us -> 2.4 us  [swap(): return lax.ppermute(value, axis, [(i, i ^ 1) for i in range(length)])]
    ppermute x9 -> x6, starting transfers between devices: 7.88 us -> 4.46 us  [turn(): lax.ppermute(value, 'blk', [(i, (i + by) % length) for i in range(length)])]
    pallas_call x4, Pallas kernels: 5.91 us -> 9.25 us  [the longest x2 5.36 us: score_call(): pl.pallas_call(functools.partial(score_kernel, chunks, qblocks, first, wi...]
    ppermute x2 -> x1, waiting for transfers between devices: 1.72 us -> 0.01 us  [swap_both(): return lax.ppermute(value, ('blk', 'helper'), pairs)]
    ppermute x7 -> x5, starting transfers between devices: 6.04 us -> 4.56 us  [swap(): return lax.ppermute(value, axis, [(i, i ^ 1) for i in range(length)])]
    squeeze x1 -> x0, local copies, waits for them, and re-layouts: 1.05 us -> none  [per_device(): lax.dynamic_index_in_dim(by_tile, helper + nhelper * c, 0, keepdims=False)]
  transfers between devices with their start and end apart: 18 -> 12, of which waited for: 12 -> 6; matrix products, arithmetic and copies ran while one was open for 0% -> 0% of each run, Pallas kernels for 6% -> 7%
where the time goes in v3:
time: 51 us; the launch traced here: 50.5 us
  waiting for transfers between devices  25.6 us (50%)
  starting transfers between devices  9.7 us (19%)
  Pallas kernels  9.25 us (18%)
  local copies, waits for them, and re-layouts  3.68 us (7%)
  between operations  1.39 us (3%)
  other arithmetic  0.85 us (2%)
    ppermute x6, waiting for transfers between devices, turn(): lax.ppermute(value, 'blk', [(i, (i + by) % length) for i in range(length)])  23.2 us
    pallas_call x2, Pallas kernels, score_call(): pl.pallas_call(functools.partial(score_kernel, chunks, qblocks, first, wi...  5.36 us
    ppermute x5, starting transfers between devices, swap(): return lax.ppermute(value, axis, [(i, i ^ 1) for i in range(length)])  4.56 us
    ppermute x6, starting transfers between devices, turn(): lax.ppermute(value, 'blk', [(i, (i + by) % length) for i in range(length)])  4.46 us
    unnamed x12, local copies, waits for them, and re-layouts  3.67 us
    ppermute x5, waiting for transfers between devices, swap(): return lax.ppermute(value, axis, [(i, i ^ 1) for i in range(length)])  2.4 us
    pallas_call x1, Pallas kernels, per_device(): pl.pallas_call(pack_queries_kernel, out_shape=jax.ShapeDtypeStruct((q_row...  2.07 us
    pallas_call x1, Pallas kernels, per_device(): pl.pallas_call(functools.partial(pack_refs_kernel, nhelper), out_shape=[j...  1.83 us
  transfers between devices with their start and end apart: 12, of which 6 were waited for; matrix products, arithmetic and copies ran while one was open for 0% of the time, Pallas kernels for 7%

profile of v3, /device:TPU:0, one launch (start us, length us, event | category | flops | bytes accessed | tf_op | source)
XLA Modules:
  0.0 50.5 jit_solution(5094998319214519144)
XLA Ops:
  0.7 1.8 %shard_map.82 = (bf16[144,768]{1,0:T(8,128)(2,1)}, bf16[128,768]{1,0:T(8,128)(2,1)}) custom-call(s32[1]{0:T(128)} %bitcast.helper_ref, bf16[512,768]{1,0:T(8,128)(2,1)} %r_ref.1, s32[4,128]{1,0:T(4,128)} %bitcast.4, s32[1]{0:T(128)S(6)} %copy.10.live_ref), custom_call_target="tpu_custom_call" | custom-call | flops 1 | bytes 1 | tf_op jit(solution)/shard_map/pallas_call | solution.py:219
  3.2 2.1 %shard_map.83.refs_0_ = bf16[528,768]{1,0:T(8,128)(2,1)} custom-call(bf16[512,768]{1,0:T(8,128)(2,1)} %q_ref, s32[4]{0:T(128)} %clusters_ref.1, s32[1]{0:T(128)S(6)} %copy.9.count_ref), custom_call_target="tpu_custom_call" | custom-call | flops 1 | bytes 1 | tf_op jit(solution)/shard_map/pallas_call | solution.py:235
  5.2 3.0 %collective-permute-start.1 = (bf16[528,768]{1,0:T(8,128)(2,1)}, bf16[528,768]{1,0:T(8,128)(2,1)S(1)}, u32[]{:S(2)}, u32[]{:S(2)}) collective-permute-start(bf16[528,768]{1,0:T(8,128)(2,1)} %shard_map.83.refs_0_), channel_id=1, source_target_pairs={{0,2},{2,0},{4,6},{6,4},{8,10},{10,8},{12,14},{14,12},{1,3},{3,1},... | collective-permute-start | bytes 2433032 | tf_op jit(solution)/shard_map/ppermute | solution.py:30
  8.3 1.6 %collective-permute-start.2 = (bf16[144,768]{1,0:T(8,128)(2,1)}, bf16[144,768]{1,0:T(8,128)(2,1)S(1)}, u32[]{:S(2)}, u32[]{:S(2)}) collective-permute-start(bf16[144,768]{1,0:T(8,128)(2,1)} %get-tuple-element.15.refs_4_), channel_id=1, source_target_pairs={{0,4},{2,6},{4,8},{6,10},{8,12},{10,14},{12,0},{14,2},{1,5},{3,7},... | collective-permute-start | bytes 663560 | tf_op jit(solution)/shard_map/ppermute | solution.py:25
  9.8 1.6 %collective-permute-start.4 = (bf16[128,768]{1,0:T(8,128)(2,1)}, bf16[128,768]{1,0:T(8,128)(2,1)S(1)}, u32[]{:S(2)}, u32[]{:S(2)}) collective-permute-start(bf16[128,768]{1,0:T(8,128)(2,1)} %get-tuple-element.16.refs_5_), channel_id=1, source_target_pairs={{0,4},{2,6},{4,8},{6,10},{8,12},{10,14},{12,0},{14,2},{1,5},{3,7},... | collective-permute-start | bytes 589832 | tf_op jit(solution)/shard_map/ppermute | solution.py:25
  11.4 7.2 %collective-permute-done.2.refs_6_ = bf16[144,768]{1,0:T(8,128)(2,1)S(1)} collective-permute-done((bf16[144,768]{1,0:T(8,128)(2,1)}, bf16[144,768]{1,0:T(8,128)(2,1)S(1)}, u32[]{:S(2)}, u32[]{:S(2)}) %collective-permute-start.2) | collective-permute-done | bytes 221216 | tf_op jit(solution)/shard_map/ppermute | solution.py:25
  18.6 3.9 %collective-permute-done.4.refs_7_ = bf16[128,768]{1,0:T(8,128)(2,1)S(1)} collective-permute-done((bf16[128,768]{1,0:T(8,128)(2,1)}, bf16[128,768]{1,0:T(8,128)(2,1)S(1)}, u32[]{:S(2)}, u32[]{:S(2)}) %collective-permute-start.4) | collective-permute-done | bytes 196640 | tf_op jit(solution)/shard_map/ppermute | solution.py:25
  22.5 0.1 collective-permute-start.5
  22.6 7.9 %collective-permute-done.5.refs_9_ = bf16[128,768]{1,0:T(8,128)(2,1)S(1)} collective-permute-done((bf16[128,768]{1,0:T(8,128)(2,1)S(1)}, bf16[128,768]{1,0:T(8,128)(2,1)S(1)}, u32[]{:S(2)}, u32[]{:S(2)}) %collective-permute-start.5) | collective-permute-done | bytes 196640 | tf_op jit(solution)/shard_map/ppermute | solution.py:25
  30.6 1.1 %collective-permute-start.8 = (bf16[128,768]{1,0:T(8,128)(2,1)S(1)}, bf16[128,768]{1,0:T(8,128)(2,1)S(1)}, u32[]{:S(2)}, u32[]{:S(2)}) collective-permute-start(bf16[128,768]{1,0:T(8,128)(2,1)S(1)} %collective-permute-done.5.refs_9_), channel_id=1, source_target_pairs={{0,4},{2,6},{4,8},{6,10},{8,12},{10,14},{12,0},{14,2},{1,5},{3,7},... | collective-permute-start | bytes 589832 | tf_op jit(solution)/shard_map/ppermute | solution.py:25
  31.8 1.1 %collective-permute-done.6.refs_3_ = bf16[528,768]{1,0:T(8,128)(2,1)S(1)} collective-permute-done((bf16[528,768]{1,0:T(8,128)(2,1)S(1)}, bf16[528,768]{1,0:T(8,128)(2,1)S(1)}, u32[]{:S(2)}, u32[]{:S(2)}) %collective-permute-start.6) | collective-permute-done | bytes 811040 | tf_op jit(solution)/shard_map/ppermute | solution.py:30
  32.9 1.1 %copy-done = bf16[528,768]{1,0:T(8,128)(2,1)S(1)} copy-done((bf16[528,768]{1,0:T(8,128)(2,1)S(1)}, bf16[528,768]{1,0:T(8,128)(2,1)}, u32[]{:S(2)}) %copy-start) | copy-done | bytes 811032
  34.0 0.9 %copy-done.1 = bf16[144,768]{1,0:T(8,128)(2,1)S(1)} copy-done((bf16[144,768]{1,0:T(8,128)(2,1)S(1)}, bf16[144,768]{1,0:T(8,128)(2,1)}, u32[]{:S(2)}) %copy-start.1) | copy-done | bytes 221208
  35.0 0.9 %copy-done.2 = bf16[128,768]{1,0:T(8,128)(2,1)S(1)} copy-done((bf16[128,768]{1,0:T(8,128)(2,1)S(1)}, bf16[128,768]{1,0:T(8,128)(2,1)}, u32[]{:S(2)}) %copy-start.2) | copy-done | bytes 196632
  35.9 0.7 %copy-done.3 = f32[64]{0:T(128)S(1)} copy-done((f32[64]{0:T(128)S(1)}, f32[64]{0:T(128)}, u32[]{:S(2)}) %copy-start.3) | copy-done | bytes 280
  36.6 3.6 %shard_map.84 = (f32[16,128]{1,0:T(8,128)S(1)}, bf16[2048,768]{1,0:T(8,128)(2,1)S(1)}, s32[8,128]{1,0:T(8,128)S(1)}) custom-call(f32[64]{0:T(128)S(1)} %copy-done.3, bf16[528,768]{1,0:T(8,128)(2,1)S(1)} %copy-done, bf16[528,768]{1,0:T(8,128)(2,1)S(1)} %collective-permute-done.refs_1_, bf16[528,768]{1,0:T(8,128)(2,1)S(1)} %collective-permute-done.1.refs_2_, ...), custom_call_target="tpu_custom_call" | custom-call | flops 1 | bytes 1 | tf_op jit(solution)/shard_map/pallas_call | solution.py:188
  40.2 4.2 %collective-permute-done.8.refs_4_ = bf16[128,768]{1,0:T(8,128)(2,1)S(1)} collective-permute-done((bf16[128,768]{1,0:T(8,128)(2,1)S(1)}, bf16[128,768]{1,0:T(8,128)(2,1)S(1)}, u32[]{:S(2)}, u32[]{:S(2)}) %collective-permute-start.8) | collective-permute-done | bytes 196640 | tf_op jit(solution)/shard_map/ppermute | solution.py:25
  44.4 1.7 %shard_map.85 = f32[16,128]{1,0:T(8,128)S(1)} custom-call(f32[64]{0:T(128)S(1)} %copy-done.3, s32[8,128]{1,0:T(8,128)S(1)} %get-tuple-element.20.refs_0_, bf16[2048,768]{1,0:T(8,128)(2,1)S(1)} %get-tuple-element.21.refs_1_, f32[16,128]{1,0:T(8,128)S(1)} %get-tuple-element.22.refs_2_, bf16[144,768]{1,0:T(8,128)(2,1)S(1)} %collective-permute-done.7.refs_3_, ...), custom_call_target="tpu_custom_call" | custom-call | flops 1 | bytes 1 | tf_op jit(solution)/shard_map/pallas_call | solution.py:188
  46.2 0.4 collective-permute-start.10
  46.6 0.7 %collective-permute-start.11 = (f32[4,128]{1,0:T(4,128)S(1)}, f32[4,128]{1,0:T(4,128)S(1)}, u32[]{:S(2)}, u32[]{:S(2)}) collective-permute-start(f32[4,128]{1,0:T(4,128)S(1)} %get-tuple-element.26), channel_id=1, source_target_pairs={{0,3},{1,2},{2,1},{3,0},{4,7},{5,6},{6,5},{7,4},{8,11},{9,10},{10,... | collective-permute-start | bytes 6152 | tf_op jit(solution)/shard_map/ppermute | solution.py:36
  47.2 1.1 %collective-permute-start.9 = (f32[4,128]{1,0:T(4,128)S(1)}, f32[4,128]{1,0:T(4,128)S(1)}, u32[]{:S(2)}, u32[]{:S(2)}) collective-permute-start(f32[4,128]{1,0:T(4,128)S(1)} %get-tuple-element.25), channel_id=1, source_target_pairs={{0,1},{1,0},{2,3},{3,2},{4,5},{5,4},{6,7},{7,6},{8,9},{9,8},{10,11... | collective-permute-start | bytes 6152 | tf_op jit(solution)/shard_map/ppermute | solution.py:30
  48.4 0.2 select_reduce_fusion
  48.6 1.2 %collective-permute-done.10 = f32[4,128]{1,0:T(4,128)S(1)} collective-permute-done((f32[4,128]{1,0:T(4,128)S(1)}, f32[4,128]{1,0:T(4,128)S(1)}, u32[]{:S(2)}, u32[]{:S(2)}) %collective-permute-start.10) | collective-permute-done | bytes 2080 | tf_op jit(solution)/shard_map/ppermute | solution.py:30
  49.8 0.7 %log-plus-one_bitcast_fusion = f32[512]{0:T(512)} fusion(f32[4,128]{1,0:T(4,128)S(1)} %collective-permute-done.11, f32[4,128]{1,0:T(4,128)S(1)} %collective-permute-done.10, f32[4,128]{1,0:T(4,128)S(1)} %collective-permute-done.9, f32[16,128]{1,0:T(8,128)S(1)} %shard_map.85, f32[4]{0:T(128)S(1)} %convert_element_type.7), kind=kLoop, calls=%fused_computation.4 | loop fusion | flops 2048 | bytes 10256 | tf_op jit(solution)/shard_map/reshape | solution.py:277
  (20 shorter events, 0.1 us)
Async XLA Ops:
  3.1 45.2 %copy-start.4 = (s32[4]{0:T(128)S(1)}, s32[4]{0:T(128)}, u32[]{:S(2)}) copy-start(s32[4]{0:T(128)} %clusters_ref.1) | copy-start | bytes 52
  3.1 45.2 %copy-start.5 = (s32[64]{0:T(128)S(1)}, s32[64]{0:T(128)}, u32[]{:S(2)}) copy-start(s32[64]{0:T(128)} %param.15) | copy-start | bytes 772
  5.2 25.3 %collective-permute-start.1 = (bf16[528,768]{1,0:T(8,128)(2,1)}, bf16[528,768]{1,0:T(8,128)(2,1)S(1)}, u32[]{:S(2)}, u32[]{:S(2)}) collective-permute-start(bf16[528,768]{1,0:T(8,128)(2,1)} %shard_map.83.refs_0_), channel_id=1, source_target_pairs={{0,2},{2,0},{4,6},{6,4},{8,10},{10,8},{12,14},{14,12},{1,3},{3,1},... | collective-permute-start | bytes 2433032 | tf_op jit(solution)/shard_map/ppermute | solution.py:30
  8.3 10.4 %collective-permute-start.2 = (bf16[144,768]{1,0:T(8,128)(2,1)}, bf16[144,768]{1,0:T(8,128)(2,1)S(1)}, u32[]{:S(2)}, u32[]{:S(2)}) collective-permute-start(bf16[144,768]{1,0:T(8,128)(2,1)} %get-tuple-element.15.refs_4_), channel_id=1, source_target_pairs={{0,4},{2,6},{4,8},{6,10},{8,12},{10,14},{12,0},{14,2},{1,5},{3,7},... | collective-permute-start | bytes 663560 | tf_op jit(solution)/shard_map/ppermute | solution.py:25
  9.8 12.6 %collective-permute-start.4 = (bf16[128,768]{1,0:T(8,128)(2,1)}, bf16[128,768]{1,0:T(8,128)(2,1)S(1)}, u32[]{:S(2)}, u32[]{:S(2)}) collective-permute-start(bf16[128,768]{1,0:T(8,128)(2,1)} %get-tuple-element.16.refs_5_), channel_id=1, source_target_pairs={{0,4},{2,6},{4,8},{6,10},{8,12},{10,14},{12,0},{14,2},{1,5},{3,7},... | collective-permute-start | bytes 589832 | tf_op jit(solution)/shard_map/ppermute | solution.py:25
  18.6 11.9 %collective-permute-start.3 = (bf16[144,768]{1,0:T(8,128)(2,1)S(1)}, bf16[144,768]{1,0:T(8,128)(2,1)S(1)}, u32[]{:S(2)}, u32[]{:S(2)}) collective-permute-start(bf16[144,768]{1,0:T(8,128)(2,1)S(1)} %collective-permute-done.2.refs_6_), channel_id=1, source_target_pairs={{0,4},{2,6},{4,8},{6,10},{8,12},{10,14},{12,0},{14,2},{1,5},{3,7},... | collective-permute-start | bytes 663560 | tf_op jit(solution)/shard_map/ppermute | solution.py:25
  22.5 8.1 %collective-permute-start.5 = (bf16[128,768]{1,0:T(8,128)(2,1)S(1)}, bf16[128,768]{1,0:T(8,128)(2,1)S(1)}, u32[]{:S(2)}, u32[]{:S(2)}) collective-permute-start(bf16[128,768]{1,0:T(8,128)(2,1)S(1)} %collective-permute-done.4.refs_7_), channel_id=1, source_target_pairs={{0,4},{2,6},{4,8},{6,10},{8,12},{10,14},{12,0},{14,2},{1,5},{3,7},... | collective-permute-start | bytes 589832 | tf_op jit(solution)/shard_map/ppermute | solution.py:25
  22.6 9.1 %collective-permute-start = (bf16[528,768]{1,0:T(8,128)(2,1)}, bf16[528,768]{1,0:T(8,128)(2,1)S(1)}, u32[]{:S(2)}, u32[]{:S(2)}) collective-permute-start(bf16[528,768]{1,0:T(8,128)(2,1)} %shard_map.83.refs_0_), channel_id=1, source_target_pairs={{0,1},{1,0},{2,3},{3,2},{4,5},{5,4},{6,7},{7,6},{8,9},{9,8},{10,11... | collective-permute-start | bytes 2433032 | tf_op jit(solution)/shard_map/ppermute | solution.py:30
  30.6 2.3 %collective-permute-start.6 = (bf16[528,768]{1,0:T(8,128)(2,1)S(1)}, bf16[528,768]{1,0:T(8,128)(2,1)S(1)}, u32[]{:S(2)}, u32[]{:S(2)}) collective-permute-start(bf16[528,768]{1,0:T(8,128)(2,1)S(1)} %collective-permute-done.1.refs_2_), channel_id=1, source_target_pairs={{0,1},{1,0},{2,3},{3,2},{4,5},{5,4},{6,7},{7,6},{8,9},{9,8},{10,11... | collective-permute-start | bytes 2433032 | tf_op jit(solution)/shard_map/ppermute | solution.py:30
  30.6 13.9 %collective-permute-start.7 = (bf16[144,768]{1,0:T(8,128)(2,1)S(1)}, bf16[144,768]{1,0:T(8,128)(2,1)S(1)}, u32[]{:S(2)}, u32[]{:S(2)}) collective-permute-start(bf16[144,768]{1,0:T(8,128)(2,1)S(1)} %collective-permute-done.3.refs_8_), channel_id=1, source_target_pairs={{0,4},{2,6},{4,8},{6,10},{8,12},{10,14},{12,0},{14,2},{1,5},{3,7},... | collective-permute-start | bytes 663560 | tf_op jit(solution)/shard_map/ppermute | solution.py:25
  30.6 13.8 %collective-permute-start.8 = (bf16[128,768]{1,0:T(8,128)(2,1)S(1)}, bf16[128,768]{1,0:T(8,128)(2,1)S(1)}, u32[]{:S(2)}, u32[]{:S(2)}) collective-permute-start(bf16[128,768]{1,0:T(8,128)(2,1)S(1)} %collective-permute-done.5.refs_9_), channel_id=1, source_target_pairs={{0,4},{2,6},{4,8},{6,10},{8,12},{10,14},{12,0},{14,2},{1,5},{3,7},... | collective-permute-start | bytes 589832 | tf_op jit(solution)/shard_map/ppermute | solution.py:25
  32.9 1.1 %copy-start = (bf16[528,768]{1,0:T(8,128)(2,1)S(1)}, bf16[528,768]{1,0:T(8,128)(2,1)}, u32[]{:S(2)}) copy-start(bf16[528,768]{1,0:T(8,128)(2,1)} %shard_map.83.refs_0_) | copy-start | bytes 2433028
  34.0 0.9 %copy-start.1 = (bf16[144,768]{1,0:T(8,128)(2,1)S(1)}, bf16[144,768]{1,0:T(8,128)(2,1)}, u32[]{:S(2)}) copy-start(bf16[144,768]{1,0:T(8,128)(2,1)} %get-tuple-element.15.refs_4_) | copy-start | bytes 663556
  35.0 0.9 %copy-start.2 = (bf16[128,768]{1,0:T(8,128)(2,1)S(1)}, bf16[128,768]{1,0:T(8,128)(2,1)}, u32[]{:S(2)}) copy-start(bf16[128,768]{1,0:T(8,128)(2,1)} %get-tuple-element.16.refs_5_) | copy-start | bytes 589828
  35.9 0.7 %copy-start.3 = (f32[64]{0:T(128)S(1)}, f32[64]{0:T(128)}, u32[]{:S(2)}) copy-start(f32[64]{0:T(128)} %beta_ref.3) | copy-start | bytes 772
  46.2 3.7 %collective-permute-start.10 = (f32[4,128]{1,0:T(4,128)S(1)}, f32[4,128]{1,0:T(4,128)S(1)}, u32[]{:S(2)}, u32[]{:S(2)}) collective-permute-start(f32[4,128]{1,0:T(4,128)S(1)} %get-tuple-element.27), channel_id=1, source_target_pairs={{0,2},{2,0},{4,6},{6,4},{8,10},{10,8},{12,14},{14,12},{1,3},{3,1},... | collective-permute-start | bytes 6152 | tf_op jit(solution)/shard_map/ppermute | solution.py:30
  46.6 3.3 %collective-permute-start.11 = (f32[4,128]{1,0:T(4,128)S(1)}, f32[4,128]{1,0:T(4,128)S(1)}, u32[]{:S(2)}, u32[]{:S(2)}) collective-permute-start(f32[4,128]{1,0:T(4,128)S(1)} %get-tuple-element.26), channel_id=1, source_target_pairs={{0,3},{1,2},{2,1},{3,0},{4,7},{5,6},{6,5},{7,4},{8,11},{9,10},{10,... | collective-permute-start | bytes 6152 | tf_op jit(solution)/shard_map/ppermute | solution.py:36
  47.2 2.6 %collective-permute-start.9 = (f32[4,128]{1,0:T(4,128)S(1)}, f32[4,128]{1,0:T(4,128)S(1)}, u32[]{:S(2)}, u32[]{:S(2)}) collective-permute-start(f32[4,128]{1,0:T(4,128)S(1)} %get-tuple-element.25), channel_id=1, source_target_pairs={{0,1},{1,0},{2,3},{3,2},{4,5},{5,4},{6,7},{7,6},{8,9},{9,8},{10,11... | collective-permute-start | bytes 6152 | tf_op jit(solution)/shard_map/ppermute | solution.py:30

commit v4 on v3

--- a/solution.py
+++ b/solution.py
@@ -17,7 +17,6 @@
 HBM = pl.BlockSpec(memory_space=pltpu.HBM)
 WHOLE = pltpu.CompilerParams(vmem_limit_bytes=60 * 1024 * 1024)
 PARAMS = pltpu.CompilerParams(vmem_limit_bytes=24 * 1024 * 1024)
-COST = pl.CostEstimate(flops=1, bytes_accessed=1, transcendentals=0)
 
 
 def turn(value, by):
@@ -38,6 +37,10 @@
 
 def after(value, *others):
     return lax.optimization_barrier((value, *others))[0]
+
+
+def cost(flops, moved):
+    return pl.CostEstimate(flops=flops, bytes_accessed=moved, transcendentals=0)
 
 
 def rows_of(index, count=1):
@@ -63,7 +66,7 @@
     table = jnp.full((TABLE, LANES), -1, jnp.int32)
     for c in range(n):
         tile = helper_ref[0] + nhelper * c
-        here = jnp.where(tile * LANES + lane < live[0], ids[pl.ds(tile, 1), :], -1)
+        here = jnp.where(tile * LANES + lane < live[0, 0], ids[pl.ds(tile, 1), :], -1)
         table = jnp.where(row == c, here, table)
     outs[0][pl.ds(LANES, TABLE), pl.ds(0, LANES)] = table.astype(jnp.float32).astype(jnp.bfloat16)
     for copy in copies[2:]:
@@ -82,7 +85,7 @@
     copies[1].wait()
     lane = lax.broadcasted_iota(jnp.int32, (TABLE, LANES), 1)
     qblocks = clusters_ref.shape[0]
-    table = jnp.where(lane == qblocks, count[0], 0)
+    table = jnp.where(lane == qblocks, count[0, 0], 0)
     for k in range(qblocks):
         table = jnp.where(lane == k, clusters[k], table)
     out[pl.ds(q_ref.shape[0], TABLE), pl.ds(0, LANES)] = table.astype(jnp.float32).astype(
@@ -194,7 +197,7 @@
         if first
         else [q_list, spread, spread],
         compiler_params=PARAMS,
-        cost_estimate=COST,
+        cost_estimate=cost(2 * slots * len(tiles) * LANES**2 * width, 2 * slots * LANES * width),
     )(beta, *given, *tiles)
 
 
@@ -226,12 +229,12 @@
         out_specs=[VMEM] * chunks,
         scratch_shapes=[
             pltpu.VMEM((tiles, LANES), jnp.int32),
-            pltpu.SMEM((1,), jnp.int32),
+            pltpu.SMEM((1, 1), jnp.int32),
             pltpu.SemaphoreType.DMA((chunks + 2,)),
         ],
         compiler_params=WHOLE,
-        cost_estimate=COST,
-    )(helper[None], references, ref_cluster.reshape(tiles, LANES), ref_rows)
+        cost_estimate=cost(1, 4 * rows * width),
+    )(helper[None], references, ref_cluster.reshape(tiles, LANES), ref_rows.reshape(1, 1))
     q_own = pl.pallas_call(
         pack_queries_kernel,
         out_shape=jax.ShapeDtypeStruct((q_rows + TABLE, width), jnp.bfloat16),
@@ -239,34 +242,29 @@
         out_specs=VMEM,
         scratch_shapes=[
             pltpu.SMEM((qblocks,), jnp.int32),
-            pltpu.SMEM((1,), jnp.int32),
+            pltpu.SMEM((1, 1), jnp.int32),
             pltpu.SemaphoreType.DMA((3,)),
         ],
         compiler_params=WHOLE,
-        cost_estimate=COST,
-    )(after(queries, *own), query_block_cluster, block_count)
+        cost_estimate=cost(1, 8 * q_rows * width),
+    )(after(queries, *own), query_block_cluster, block_count.reshape(1, 1))
     q_partner = swap(q_own, "blk")
     q_helper = swap(q_own, "helper")
-    held = [own]
-    for step in range(1, sources):
-        sent = []
-        for c in range(chunks):
-            if c > 0 and step > 1:
-                waits = [held[step - 1][c - 1]]
-            elif c == 0 and step > 2:
-                waits = [held[step - 2][-1]]
-            else:
-                waits = []
-            sent.append(turn(after(held[step - 1][c], *waits), 2))
-        held.append(sent)
-    q_both = swap(after(q_partner, *held[-2]), "helper")
-
-    early = [x for step in held[:-1] for x in step]
+
+    above, below = [own], [own]
+    for step in range(1, (sources + 1) // 2):
+        above.append([turn(x, 2) for x in above[-1]])
+        below.append([turn(x, -2) for x in below[-1]])
+    early = [x for step in [own] + above[1:] + below[1:] for x in step]
+    half = chunks // 2
+    last = [turn(x, 2) for x in above[-1][:half]] + [turn(x, -2) for x in below[-1][half:]]
+    q_both = swap(after(q_partner, *above[-1], *below[-1]), "helper")
+
     totals, packed, info = score_call(
         chunks, qblocks, 2, cluster_beta, (q_own, q_helper, q_partner, q_both), early, True
     )
     totals = score_call(
-        chunks, qblocks, 4, cluster_beta, (info, packed, totals), held[-1], False
+        chunks, qblocks, 4, cluster_beta, (info, packed, totals), last, False
     )
     totals = totals.reshape(4, qblocks, LANES)
     total = totals[0] + swap(totals[1], "helper") + swap(totals[2], "blk") + swap_both(totals[3])

time: 51 us -> 49.2 us (0.965)
  waiting for transfers between devices: 25.6 us -> 20.3 us
  starting transfers between devices: 9.7 us -> 13.2 us
    ppermute x6, waiting for transfers between devices: 23.2 us -> 18.8 us  [turn(): lax.ppermute(value, 'blk', [(i, (i + by) % length) for i in range(length)])]
    ppermute x6, starting transfers between devices: 4.46 us -> 7.93 us  [turn(): lax.ppermute(value, 'blk', [(i, (i + by) % length) for i in range(length)])]
    ppermute x5, waiting for transfers between devices: 2.4 us -> 1.48 us  [swap(): return lax.ppermute(value, axis, [(i, i ^ 1) for i in range(length)])]
  transfers between devices with their start and end apart: 12 -> 12, of which waited for: 6 -> 5; matrix products, arithmetic and copies ran while one was open for 0% -> 0% of each run, Pallas kernels for 7% -> 8%
where the time goes in v4:
time: 49.2 us; the launch traced here: 48.7 us
  waiting for transfers between devices  20.3 us (41%)
  starting transfers between devices  13.2 us (27%)
  Pallas kernels  9.29 us (19%)
  local copies, waits for them, and re-layouts  3.68 us (7%)
  between operations  1.39 us (3%)
  other arithmetic  0.85 us (2%)
    ppermute x6, waiting for transfers between devices, turn(): lax.ppermute(value, 'blk', [(i, (i + by) % length) for i in range(length)])  18.8 us
    ppermute x6, starting transfers between devices, turn(): lax.ppermute(value, 'blk', [(i, (i + by) % length) for i in range(length)])  7.93 us
    pallas_call x2, Pallas kernels, score_call(): pl.pallas_call(functools.partial(score_kernel, chunks, qblocks, first, wi...  5.4 us
    ppermute x5, starting transfers between devices, swap(): return lax.ppermute(value, axis, [(i, i ^ 1) for i in range(length)])  4.81 us
    unnamed x12, local copies, waits for them, and re-layouts  3.67 us
    pallas_call x1, Pallas kernels, per_device(): pl.pallas_call(pack_queries_kernel, out_shape=jax.ShapeDtypeStruct((q_row...  2.06 us
    pallas_call x1, Pallas kernels, per_device(): pl.pallas_call(functools.partial(pack_refs_kernel, nhelper), out_shape=[j...  1.83 us
    ppermute x5, waiting for transfers between devices, swap(): return lax.ppermute(value, axis, [(i, i ^ 1) for i in range(length)])  1.48 us
  transfers between devices with their start and end apart: 12, of which 5 were waited for; matrix products, arithmetic and copies ran while one was open for 0% of the time, Pallas kernels for 8%

profile of v4, /device:TPU:0, one launch (start us, length us, event | category | flops | bytes accessed | tf_op | source)
XLA Modules:
  0.0 48.7 jit_solution(8781101471544631574)
XLA Ops:
  0.7 1.8 %shard_map.82 = (bf16[144,768]{1,0:T(8,128)(2,1)}, bf16[128,768]{1,0:T(8,128)(2,1)}) custom-call(s32[1]{0:T(128)} %bitcast.helper_ref, bf16[512,768]{1,0:T(8,128)(2,1)} %r_ref.1, s32[4,128]{1,0:T(4,128)} %bitcast.8, s32[1,1]{1,0:T(1,128)} %bitcast.7.live_ref), custom_call_target="tpu_custom_call" | custom-call | flops 1 | bytes 1572864 | tf_op jit(solution)/shard_map/pallas_call | solution.py:222
  3.1 2.1 %shard_map.83.refs_0_ = bf16[528,768]{1,0:T(8,128)(2,1)} custom-call(bf16[512,768]{1,0:T(8,128)(2,1)} %q_ref, s32[4]{0:T(128)} %clusters_ref.1, s32[1,1]{1,0:T(1,128)} %bitcast.6.count_ref), custom_call_target="tpu_custom_call" | custom-call | flops 1 | bytes 3145728 | tf_op jit(solution)/shard_map/pallas_call | solution.py:238
  5.2 3.0 %collective-permute-start.1 = (bf16[528,768]{1,0:T(8,128)(2,1)}, bf16[528,768]{1,0:T(8,128)(2,1)S(1)}, u32[]{:S(2)}, u32[]{:S(2)}) collective-permute-start(bf16[528,768]{1,0:T(8,128)(2,1)} %shard_map.83.refs_0_), channel_id=1, source_target_pairs={{0,2},{2,0},{4,6},{6,4},{8,10},{10,8},{12,14},{14,12},{1,3},{3,1},... | collective-permute-start | bytes 2433032 | tf_op jit(solution)/shard_map/ppermute | solution.py:29
  8.2 1.6 %collective-permute-start.2 = (bf16[144,768]{1,0:T(8,128)(2,1)}, bf16[144,768]{1,0:T(8,128)(2,1)S(1)}, u32[]{:S(2)}, u32[]{:S(2)}) collective-permute-start(bf16[144,768]{1,0:T(8,128)(2,1)} %get-tuple-element.12.refs_4_), channel_id=1, source_target_pairs={{0,4},{2,6},{4,8},{6,10},{8,12},{10,14},{12,0},{14,2},{1,5},{3,7},... | collective-permute-start | bytes 663560 | tf_op jit(solution)/shard_map/ppermute | solution.py:24
  9.8 2.2 %collective-permute-start.4 = (bf16[144,768]{1,0:T(8,128)(2,1)}, bf16[144,768]{1,0:T(8,128)(2,1)S(1)}, u32[]{:S(2)}, u32[]{:S(2)}) collective-permute-start(bf16[144,768]{1,0:T(8,128)(2,1)} %get-tuple-element.12.refs_4_), channel_id=1, source_target_pairs={{0,12},{2,14},{4,0},{6,2},{8,4},{10,6},{12,8},{14,10},{1,13},{3,15... | collective-permute-start | bytes 663560 | tf_op jit(solution)/shard_map/ppermute | solution.py:24
  12.1 1.8 %collective-permute-start.5 = (bf16[128,768]{1,0:T(8,128)(2,1)}, bf16[128,768]{1,0:T(8,128)(2,1)S(1)}, u32[]{:S(2)}, u32[]{:S(2)}) collective-permute-start(bf16[128,768]{1,0:T(8,128)(2,1)} %get-tuple-element.13.refs_5_), channel_id=1, source_target_pairs={{0,12},{2,14},{4,0},{6,2},{8,4},{10,6},{12,8},{14,10},{1,13},{3,15... | collective-permute-start | bytes 589832 | tf_op jit(solution)/shard_map/ppermute | solution.py:24
  13.9 0.2 collective-permute-start.3
  14.1 12.3 %collective-permute-done.5.refs_9_ = bf16[128,768]{1,0:T(8,128)(2,1)S(1)} collective-permute-done((bf16[128,768]{1,0:T(8,128)(2,1)}, bf16[128,768]{1,0:T(8,128)(2,1)S(1)}, u32[]{:S(2)}, u32[]{:S(2)}) %collective-permute-start.5) | collective-permute-done | bytes 196640 | tf_op jit(solution)/shard_map/ppermute | solution.py:24
  26.4 4.0 %collective-permute-done.3.refs_7_ = bf16[128,768]{1,0:T(8,128)(2,1)S(1)} collective-permute-done((bf16[128,768]{1,0:T(8,128)(2,1)}, bf16[128,768]{1,0:T(8,128)(2,1)S(1)}, u32[]{:S(2)}, u32[]{:S(2)}) %collective-permute-start.3) | collective-permute-done | bytes 196640 | tf_op jit(solution)/shard_map/ppermute | solution.py:24
  30.5 1.8 %collective-permute-start.8 = (bf16[128,768]{1,0:T(8,128)(2,1)S(1)}, bf16[128,768]{1,0:T(8,128)(2,1)S(1)}, u32[]{:S(2)}, u32[]{:S(2)}) collective-permute-start(bf16[128,768]{1,0:T(8,128)(2,1)S(1)} %collective-permute-done.5.refs_9_), channel_id=1, source_target_pairs={{0,12},{2,14},{4,0},{6,2},{8,4},{10,6},{12,8},{14,10},{1,13},{3,15... | collective-permute-start | bytes 589832 | tf_op jit(solution)/shard_map/ppermute | solution.py:24
  32.2 0.3 collective-permute-start.7
  32.6 0.2 collective-permute-done.6.refs_3_
  32.8 1.1 %copy-done = bf16[528,768]{1,0:T(8,128)(2,1)S(1)} copy-done((bf16[528,768]{1,0:T(8,128)(2,1)S(1)}, bf16[528,768]{1,0:T(8,128)(2,1)}, u32[]{:S(2)}) %copy-start) | copy-done | bytes 811032
  33.9 0.7 %copy-done.1 = f32[64]{0:T(128)S(1)} copy-done((f32[64]{0:T(128)S(1)}, f32[64]{0:T(128)}, u32[]{:S(2)}) %copy-start.1) | copy-done | bytes 280
  34.6 0.9 %copy-done.2 = bf16[144,768]{1,0:T(8,128)(2,1)S(1)} copy-done((bf16[144,768]{1,0:T(8,128)(2,1)S(1)}, bf16[144,768]{1,0:T(8,128)(2,1)}, u32[]{:S(2)}) %copy-start.2) | copy-done | bytes 221208
  35.5 0.9 %copy-done.3 = bf16[128,768]{1,0:T(8,128)(2,1)S(1)} copy-done((bf16[128,768]{1,0:T(8,128)(2,1)S(1)}, bf16[128,768]{1,0:T(8,128)(2,1)}, u32[]{:S(2)}) %copy-start.3) | copy-done | bytes 196632
  36.5 3.7 %shard_map.84 = (f32[16,128]{1,0:T(8,128)S(1)}, bf16[2048,768]{1,0:T(8,128)(2,1)S(1)}, s32[8,128]{1,0:T(8,128)S(1)}) custom-call(f32[64]{0:T(128)S(1)} %copy-done.1, bf16[528,768]{1,0:T(8,128)(2,1)S(1)} %copy-done, bf16[528,768]{1,0:T(8,128)(2,1)S(1)} %collective-permute-done.refs_1_, bf16[528,768]{1,0:T(8,128)(2,1)S(1)} %collective-permute-done.1.refs_2_, ...), custom_call_target="tpu_custom_call" | custom-call | flops 2415919104 | bytes 3145728 | tf_op jit(solution)/shard_map/pallas_call | solution.py:191
  40.2 2.5 %collective-permute-done.7.refs_3_ = bf16[144,768]{1,0:T(8,128)(2,1)S(1)} collective-permute-done((bf16[144,768]{1,0:T(8,128)(2,1)S(1)}, bf16[144,768]{1,0:T(8,128)(2,1)S(1)}, u32[]{:S(2)}, u32[]{:S(2)}) %collective-permute-start.7) | collective-permute-done | bytes 221216 | tf_op jit(solution)/shard_map/ppermute | solution.py:24
  42.7 1.7 %shard_map.85 = f32[16,128]{1,0:T(8,128)S(1)} custom-call(f32[64]{0:T(128)S(1)} %copy-done.1, s32[8,128]{1,0:T(8,128)S(1)} %get-tuple-element.16.refs_0_, bf16[2048,768]{1,0:T(8,128)(2,1)S(1)} %get-tuple-element.17.refs_1_, f32[16,128]{1,0:T(8,128)S(1)} %get-tuple-element.18.refs_2_, bf16[144,768]{1,0:T(8,128)(2,1)S(1)} %collective-permute-done.7.refs_3_, ...), custom_call_target="tpu_custom_call" | custom-call | flops 805306368 | bytes 3145728 | tf_op jit(solution)/shard_map/pallas_call | solution.py:191
  44.4 0.6 %collective-permute-start.10 = (f32[4,128]{1,0:T(4,128)S(1)}, f32[4,128]{1,0:T(4,128)S(1)}, u32[]{:S(2)}, u32[]{:S(2)}) collective-permute-start(f32[4,128]{1,0:T(4,128)S(1)} %get-tuple-element.21), channel_id=1, source_target_pairs={{0,2},{2,0},{4,6},{6,4},{8,10},{10,8},{12,14},{14,12},{1,3},{3,1},... | collective-permute-start | bytes 6152 | tf_op jit(solution)/shard_map/ppermute | solution.py:29
  45.0 0.5 %collective-permute-start.11 = (f32[4,128]{1,0:T(4,128)S(1)}, f32[4,128]{1,0:T(4,128)S(1)}, u32[]{:S(2)}, u32[]{:S(2)}) collective-permute-start(f32[4,128]{1,0:T(4,128)S(1)} %get-tuple-element.20), channel_id=1, source_target_pairs={{0,3},{1,2},{2,1},{3,0},{4,7},{5,6},{6,5},{7,4},{8,11},{9,10},{10,... | collective-permute-start | bytes 6152 | tf_op jit(solution)/shard_map/ppermute | solution.py:35
  45.5 1.1 %collective-permute-start.9 = (f32[4,128]{1,0:T(4,128)S(1)}, f32[4,128]{1,0:T(4,128)S(1)}, u32[]{:S(2)}, u32[]{:S(2)}) collective-permute-start(f32[4,128]{1,0:T(4,128)S(1)} %get-tuple-element.19), channel_id=1, source_target_pairs={{0,1},{1,0},{2,3},{3,2},{4,5},{5,4},{6,7},{7,6},{8,9},{9,8},{10,11... | collective-permute-start | bytes 6152 | tf_op jit(solution)/shard_map/ppermute | solution.py:29
  46.8 1.2 %collective-permute-done.10 = f32[4,128]{1,0:T(4,128)S(1)} collective-permute-done((f32[4,128]{1,0:T(4,128)S(1)}, f32[4,128]{1,0:T(4,128)S(1)}, u32[]{:S(2)}, u32[]{:S(2)}) %collective-permute-start.10) | collective-permute-done | bytes 2080 | tf_op jit(solution)/shard_map/ppermute | solution.py:29
  48.1 0.7 %log-plus-one_bitcast_fusion = f32[512]{0:T(512)} fusion(f32[4,128]{1,0:T(4,128)S(1)} %collective-permute-done.11, f32[4,128]{1,0:T(4,128)S(1)} %collective-permute-done.10, f32[4,128]{1,0:T(4,128)S(1)} %collective-permute-done.9, f32[16,128]{1,0:T(8,128)S(1)} %shard_map.85, f32[4]{0:T(128)S(1)} %convert_element_type.7), kind=kLoop, calls=%fused_computation.4 | loop fusion | flops 2048 | bytes 10256 | tf_op jit(solution)/shard_map/reshape | solution.py:275
  (20 shorter events, 0.3 us)
Async XLA Ops:
  5.2 25.2 %collective-permute-start.1 = (bf16[528,768]{1,0:T(8,128)(2,1)}, bf16[528,768]{1,0:T(8,128)(2,1)S(1)}, u32[]{:S(2)}, u32[]{:S(2)}) collective-permute-start(bf16[528,768]{1,0:T(8,128)(2,1)} %shard_map.83.refs_0_), channel_id=1, source_target_pairs={{0,2},{2,0},{4,6},{6,4},{8,10},{10,8},{12,14},{14,12},{1,3},{3,1},... | collective-permute-start | bytes 2433032 | tf_op jit(solution)/shard_map/ppermute | solution.py:29
  8.2 22.2 %collective-permute-start.2 = (bf16[144,768]{1,0:T(8,128)(2,1)}, bf16[144,768]{1,0:T(8,128)(2,1)S(1)}, u32[]{:S(2)}, u32[]{:S(2)}) collective-permute-start(bf16[144,768]{1,0:T(8,128)(2,1)} %get-tuple-element.12.refs_4_), channel_id=1, source_target_pairs={{0,4},{2,6},{4,8},{6,10},{8,12},{10,14},{12,0},{14,2},{1,5},{3,7},... | collective-permute-start | bytes 663560 | tf_op jit(solution)/shard_map/ppermute | solution.py:24
  9.8 20.6 %collective-permute-start.4 = (bf16[144,768]{1,0:T(8,128)(2,1)}, bf16[144,768]{1,0:T(8,128)(2,1)S(1)}, u32[]{:S(2)}, u32[]{:S(2)}) collective-permute-start(bf16[144,768]{1,0:T(8,128)(2,1)} %get-tuple-element.12.refs_4_), channel_id=1, source_target_pairs={{0,12},{2,14},{4,0},{6,2},{8,4},{10,6},{12,8},{14,10},{1,13},{3,15... | collective-permute-start | bytes 663560 | tf_op jit(solution)/shard_map/ppermute | solution.py:24
  12.1 14.3 %collective-permute-start.5 = (bf16[128,768]{1,0:T(8,128)(2,1)}, bf16[128,768]{1,0:T(8,128)(2,1)S(1)}, u32[]{:S(2)}, u32[]{:S(2)}) collective-permute-start(bf16[128,768]{1,0:T(8,128)(2,1)} %get-tuple-element.13.refs_5_), channel_id=1, source_target_pairs={{0,12},{2,14},{4,0},{6,2},{8,4},{10,6},{12,8},{14,10},{1,13},{3,15... | collective-permute-start | bytes 589832 | tf_op jit(solution)/shard_map/ppermute | solution.py:24
  13.9 16.5 %collective-permute-start.3 = (bf16[128,768]{1,0:T(8,128)(2,1)}, bf16[128,768]{1,0:T(8,128)(2,1)S(1)}, u32[]{:S(2)}, u32[]{:S(2)}) collective-permute-start(bf16[128,768]{1,0:T(8,128)(2,1)} %get-tuple-element.13.refs_5_), channel_id=1, source_target_pairs={{0,4},{2,6},{4,8},{6,10},{8,12},{10,14},{12,0},{14,2},{1,5},{3,7},... | collective-permute-start | bytes 589832 | tf_op jit(solution)/shard_map/ppermute | solution.py:24
  26.4 6.2 %collective-permute-start = (bf16[528,768]{1,0:T(8,128)(2,1)}, bf16[528,768]{1,0:T(8,128)(2,1)S(1)}, u32[]{:S(2)}, u32[]{:S(2)}) collective-permute-start(bf16[528,768]{1,0:T(8,128)(2,1)} %shard_map.83.refs_0_), channel_id=1, source_target_pairs={{0,1},{1,0},{2,3},{3,2},{4,5},{5,4},{6,7},{7,6},{8,9},{9,8},{10,11... | collective-permute-start | bytes 2433032 | tf_op jit(solution)/shard_map/ppermute | solution.py:29
  30.4 2.4 %collective-permute-start.6 = (bf16[528,768]{1,0:T(8,128)(2,1)S(1)}, bf16[528,768]{1,0:T(8,128)(2,1)S(1)}, u32[]{:S(2)}, u32[]{:S(2)}) collective-permute-start(bf16[528,768]{1,0:T(8,128)(2,1)S(1)} %collective-permute-done.1.refs_2_), channel_id=1, source_target_pairs={{0,1},{1,0},{2,3},{3,2},{4,5},{5,4},{6,7},{7,6},{8,9},{9,8},{10,11... | collective-permute-start | bytes 2433032 | tf_op jit(solution)/shard_map/ppermute | solution.py:29
  30.5 9.7 %collective-permute-start.8 = (bf16[128,768]{1,0:T(8,128)(2,1)S(1)}, bf16[128,768]{1,0:T(8,128)(2,1)S(1)}, u32[]{:S(2)}, u32[]{:S(2)}) collective-permute-start(bf16[128,768]{1,0:T(8,128)(2,1)S(1)} %collective-permute-done.5.refs_9_), channel_id=1, source_target_pairs={{0,12},{2,14},{4,0},{6,2},{8,4},{10,6},{12,8},{14,10},{1,13},{3,15... | collective-permute-start | bytes 589832 | tf_op jit(solution)/shard_map/ppermute | solution.py:24
  32.2 10.4 %collective-permute-start.7 = (bf16[144,768]{1,0:T(8,128)(2,1)S(1)}, bf16[144,768]{1,0:T(8,128)(2,1)S(1)}, u32[]{:S(2)}, u32[]{:S(2)}) collective-permute-start(bf16[144,768]{1,0:T(8,128)(2,1)S(1)} %collective-permute-done.2.refs_6_), channel_id=1, source_target_pairs={{0,4},{2,6},{4,8},{6,10},{8,12},{10,14},{12,0},{14,2},{1,5},{3,7},... | collective-permute-start | bytes 663560 | tf_op jit(solution)/shard_map/ppermute | solution.py:24
  32.8 1.1 %copy-start = (bf16[528,768]{1,0:T(8,128)(2,1)S(1)}, bf16[528,768]{1,0:T(8,128)(2,1)}, u32[]{:S(2)}) copy-start(bf16[528,768]{1,0:T(8,128)(2,1)} %shard_map.83.refs_0_) | copy-start | bytes 2433028
  33.9 0.7 %copy-start.1 = (f32[64]{0:T(128)S(1)}, f32[64]{0:T(128)}, u32[]{:S(2)}) copy-start(f32[64]{0:T(128)} %beta_ref.3) | copy-start | bytes 772
  34.6 0.9 %copy-start.2 = (bf16[144,768]{1,0:T(8,128)(2,1)S(1)}, bf16[144,768]{1,0:T(8,128)(2,1)}, u32[]{:S(2)}) copy-start(bf16[144,768]{1,0:T(8,128)(2,1)} %get-tuple-element.12.refs_4_) | copy-start | bytes 663556
  35.5 0.9 %copy-start.3 = (bf16[128,768]{1,0:T(8,128)(2,1)S(1)}, bf16[128,768]{1,0:T(8,128)(2,1)}, u32[]{:S(2)}) copy-start(bf16[128,768]{1,0:T(8,128)(2,1)} %get-tuple-element.13.refs_5_) | copy-start | bytes 589828
  40.2 6.5 %copy-start.4 = (s32[4]{0:T(128)S(1)}, s32[4]{0:T(128)}, u32[]{:S(2)}) copy-start(s32[4]{0:T(128)} %clusters_ref.1) | copy-start | bytes 52
  40.2 6.4 %copy-start.5 = (s32[64]{0:T(128)S(1)}, s32[64]{0:T(128)}, u32[]{:S(2)}) copy-start(s32[64]{0:T(128)} %param.15) | copy-start | bytes 772
  44.4 3.7 %collective-permute-start.10 = (f32[4,128]{1,0:T(4,128)S(1)}, f32[4,128]{1,0:T(4,128)S(1)}, u32[]{:S(2)}, u32[]{:S(2)}) collective-permute-start(f32[4,128]{1,0:T(4,128)S(1)} %get-tuple-element.21), channel_id=1, source_target_pairs={{0,2},{2,0},{4,6},{6,4},{8,10},{10,8},{12,14},{14,12},{1,3},{3,1},... | collective-permute-start | bytes 6152 | tf_op jit(solution)/shard_map/ppermute | solution.py:29
  45.0 3.1 %collective-permute-start.11 = (f32[4,128]{1,0:T(4,128)S(1)}, f32[4,128]{1,0:T(4,128)S(1)}, u32[]{:S(2)}, u32[]{:S(2)}) collective-permute-start(f32[4,128]{1,0:T(4,128)S(1)} %get-tuple-element.20), channel_id=1, source_target_pairs={{0,3},{1,2},{2,1},{3,0},{4,7},{5,6},{6,5},{7,4},{8,11},{9,10},{10,... | collective-permute-start | bytes 6152 | tf_op jit(solution)/shard_map/ppermute | solution.py:35
  45.5 2.6 %collective-permute-start.9 = (f32[4,128]{1,0:T(4,128)S(1)}, f32[4,128]{1,0:T(4,128)S(1)}, u32[]{:S(2)}, u32[]{:S(2)}) collective-permute-start(f32[4,128]{1,0:T(4,128)S(1)} %get-tuple-element.19), channel_id=1, source_target_pairs={{0,1},{1,0},{2,3},{3,2},{4,5},{5,4},{6,7},{7,6},{8,9},{9,8},{10,11... | collective-permute-start | bytes 6152 | tf_op jit(solution)/shard_map/ppermute | solution.py:29

commit v5 on v4

--- a/solution.py
+++ b/solution.py
@@ -14,8 +14,6 @@
 DEAD = -1.0e30
 SMEM = pl.BlockSpec(memory_space=pltpu.SMEM)
 VMEM = pl.BlockSpec(memory_space=pltpu.VMEM)
-HBM = pl.BlockSpec(memory_space=pltpu.HBM)
-WHOLE = pltpu.CompilerParams(vmem_limit_bytes=60 * 1024 * 1024)
 PARAMS = pltpu.CompilerParams(vmem_limit_bytes=24 * 1024 * 1024)
 
 
@@ -47,56 +45,30 @@
     return pl.ds(pl.multiple_of(index * LANES, LANES), count * LANES)
 
 
-def pack_refs_kernel(nhelper, helper_ref, r_ref, ids_ref, live_ref, *refs):
-    outs, (ids, live, sem) = refs[:-3], refs[-3:]
-    n = len(outs)
-    copies = [
-        pltpu.make_async_copy(ids_ref, ids, sem.at[n]),
-        pltpu.make_async_copy(live_ref, live, sem.at[n + 1]),
-    ]
-    for c, out in enumerate(outs):
-        rows = rows_of(helper_ref[0] + nhelper * c)
-        copies.append(pltpu.make_async_copy(r_ref.at[rows], out.at[pl.ds(0, LANES)], sem.at[c]))
-    for copy in copies:
-        copy.start()
-    copies[0].wait()
-    copies[1].wait()
+def cut_kernel(nhelper, helper_ref, live_ref, ids_ref, r_ref, *outs):
     lane = lax.broadcasted_iota(jnp.int32, (TABLE, LANES), 1)
     row = lax.broadcasted_iota(jnp.int32, (TABLE, LANES), 0)
     table = jnp.full((TABLE, LANES), -1, jnp.int32)
-    for c in range(n):
+    for c, out in enumerate(outs):
         tile = helper_ref[0] + nhelper * c
-        here = jnp.where(tile * LANES + lane < live[0, 0], ids[pl.ds(tile, 1), :], -1)
+        here = jnp.where(tile * LANES + lane < live_ref[0], ids_ref[pl.ds(tile, 1), :], -1)
         table = jnp.where(row == c, here, table)
-    outs[0][pl.ds(LANES, TABLE), pl.ds(0, LANES)] = table.astype(jnp.float32).astype(jnp.bfloat16)
-    for copy in copies[2:]:
-        copy.wait()
-
-
-def pack_queries_kernel(q_ref, clusters_ref, count_ref, out, clusters, count, sem):
-    copies = (
-        pltpu.make_async_copy(clusters_ref, clusters, sem.at[0]),
-        pltpu.make_async_copy(count_ref, count, sem.at[1]),
-        pltpu.make_async_copy(q_ref, out.at[pl.ds(0, q_ref.shape[0])], sem.at[2]),
-    )
-    for copy in copies:
-        copy.start()
-    copies[0].wait()
-    copies[1].wait()
-    lane = lax.broadcasted_iota(jnp.int32, (TABLE, LANES), 1)
+        out[pl.ds(0, LANES), :] = r_ref[rows_of(tile), :]
+    outs[-1][pl.ds(LANES, TABLE), pl.ds(0, LANES)] = table.astype(jnp.float32).astype(jnp.bfloat16)
+
+
+def table_kernel(clusters_ref, count_ref, out):
     qblocks = clusters_ref.shape[0]
-    table = jnp.where(lane == qblocks, count[0, 0], 0)
+    lane = lax.broadcasted_iota(jnp.int32, out.shape, 1)
+    table = jnp.where(lane == qblocks, count_ref[0], 0)
     for k in range(qblocks):
-        table = jnp.where(lane == k, clusters[k], table)
-    out[pl.ds(q_ref.shape[0], TABLE), pl.ds(0, LANES)] = table.astype(jnp.float32).astype(
-        jnp.bfloat16
-    )
-    copies[2].wait()
+        table = jnp.where(lane == k, clusters_ref[k], table)
+    out[...] = table
 
 
 def score_kernel(chunks, qblocks, first, wide, beta_ref, *refs):
     if first:
-        q_refs, refs = refs[:4], refs[4:]
+        q_refs, t_refs, refs = refs[:4], refs[4:8], refs[8:]
         r_refs, (out_ref, qv, info_out, q_list, info, ids_ref, other_ref, sem) = refs[:-8], refs[-8:]
     else:
         (info, qv, prev_ref), refs = refs[:3], refs[3:]
@@ -104,14 +76,14 @@
     width = qv.shape[1]
     sources = len(r_refs) // chunks
     if first:
-        for s, q_ref in enumerate(q_refs):
-            table = q_ref[pl.ds(qblocks * LANES, TABLE), pl.ds(0, LANES)].astype(jnp.float32)
-            info_out[s : s + 1, :] = table[0:1, :].astype(jnp.int32)
+        for s, t_ref in enumerate(t_refs):
+            info_out[s : s + 1, :] = t_ref[0:1, :]
         copy = pltpu.make_async_copy(info_out, info, sem)
         copy.start()
 
     for s in range(sources):
-        table = r_refs[s * chunks][pl.ds(LANES, TABLE), pl.ds(0, LANES)].astype(jnp.float32)
+        last = r_refs[(s + 1) * chunks - 1]
+        table = last[pl.ds(LANES, TABLE), pl.ds(0, LANES)].astype(jnp.float32)
         for c in range(chunks):
             ids = jnp.broadcast_to(table[c : c + 1, :], (LANES, LANES)).T
             rows = pl.ds((s * chunks + c) * LANES, LANES)
@@ -214,42 +186,33 @@
     nblk, nhelper = lax.axis_size("blk"), lax.axis_size("helper")
     helper = lax.axis_index("helper").astype(jnp.int32)
     qblocks = query_block_cluster.shape[0]
-    q_rows, (rows, width) = queries.shape[0], references.shape
+    rows, width = references.shape
     tiles = rows // LANES
     chunks = tiles // nhelper
     sources = nblk // 2
 
+    q_partner = swap(queries, "blk")
     own = pl.pallas_call(
-        functools.partial(pack_refs_kernel, nhelper),
+        functools.partial(cut_kernel, nhelper),
         out_shape=[
-            jax.ShapeDtypeStruct((LANES + (TABLE if c == 0 else 0), width), jnp.bfloat16)
+            jax.ShapeDtypeStruct((LANES + (TABLE if c == chunks - 1 else 0), width), jnp.bfloat16)
             for c in range(chunks)
         ],
-        in_specs=[SMEM] + [HBM] * 3,
+        in_specs=[SMEM] * 2 + [VMEM] * 2,
         out_specs=[VMEM] * chunks,
-        scratch_shapes=[
-            pltpu.VMEM((tiles, LANES), jnp.int32),
-            pltpu.SMEM((1, 1), jnp.int32),
-            pltpu.SemaphoreType.DMA((chunks + 2,)),
-        ],
-        compiler_params=WHOLE,
-        cost_estimate=cost(1, 4 * rows * width),
-    )(helper[None], references, ref_cluster.reshape(tiles, LANES), ref_rows.reshape(1, 1))
-    q_own = pl.pallas_call(
-        pack_queries_kernel,
-        out_shape=jax.ShapeDtypeStruct((q_rows + TABLE, width), jnp.bfloat16),
-        in_specs=[HBM] * 3,
+        compiler_params=PARAMS,
+        cost_estimate=cost(1, 4 * LANES * width),
+    )(helper[None], ref_rows, ref_cluster.reshape(tiles, LANES), references)
+    table = pl.pallas_call(
+        table_kernel,
+        out_shape=jax.ShapeDtypeStruct((8, LANES), jnp.int32),
+        in_specs=[SMEM] * 2,
         out_specs=VMEM,
-        scratch_shapes=[
-            pltpu.SMEM((qblocks,), jnp.int32),
-            pltpu.SMEM((1, 1), jnp.int32),
-            pltpu.SemaphoreType.DMA((3,)),
-        ],
-        compiler_params=WHOLE,
-        cost_estimate=cost(1, 8 * q_rows * width),
-    )(after(queries, *own), query_block_cluster, block_count.reshape(1, 1))
-    q_partner = swap(q_own, "blk")
-    q_helper = swap(q_own, "helper")
+        compiler_params=PARAMS,
+        cost_estimate=cost(1, 4 * LANES * width),
+    )(after(query_block_cluster, *own), block_count)
+    q_helper = swap(queries, "helper")
+    tables = (table, swap(table, "helper"), swap(table, "blk"), swap_both(table))
 
     above, below = [own], [own]
     for step in range(1, (sources + 1) // 2):
@@ -258,10 +221,10 @@
     early = [x for step in [own] + above[1:] + below[1:] for x in step]
     half = chunks // 2
     last = [turn(x, 2) for x in above[-1][:half]] + [turn(x, -2) for x in below[-1][half:]]
-    q_both = swap(after(q_partner, *above[-1], *below[-1]), "helper")
+    q_both = swap(after(q_partner, *above[-1], *below[-1], *tables), "helper")
 
     totals, packed, info = score_call(
-        chunks, qblocks, 2, cluster_beta, (q_own, q_helper, q_partner, q_both), early, True
+        chunks, qblocks, 2, cluster_beta, (queries, q_helper, q_partner, q_both, *tables), early, True
     )
     totals = score_call(
         chunks, qblocks, 4, cluster_beta, (info, packed, totals), last, False

time: 49.2 us -> 52.9 us (1.075)
  starting transfers between devices: 13.2 us -> 17.7 us
  Pallas kernels: 9.29 us -> 7.68 us
  waiting for transfers between devices: 20.3 us -> 20.9 us
  local copies, waits for them, and re-layouts: 3.68 us -> 4.26 us
    ppermute x6, waiting for transfers between devices: 18.8 us -> 9.94 us  [turn(): lax.ppermute(value, 'blk', [(i, (i + by) % length) for i in range(length)])]
    ppermute x5 -> x7, waiting for transfers between devices: 1.48 us -> 10.1 us  [swap(): return lax.ppermute(value, axis, [(i, i ^ 1) for i in range(length)])]
    ppermute x6, starting transfers between devices: 7.93 us -> 11.4 us  [turn(): lax.ppermute(value, 'blk', [(i, (i + by) % length) for i in range(length)])]
    pallas_call x2, Pallas kernels: 3.89 us -> 0.58 us  [the longest x1 0.55 us: per_device(): pl.pallas_call(table_kernel, out_shape=jax.ShapeDtypeStruct((8, LANES), j...]
    pallas_call x2, Pallas kernels: 5.4 us -> 7.1 us  [score_call(): pl.pallas_call(functools.partial(score_kernel, chunks, qblocks, first, wi...]
    ppermute x1 -> x2, waiting for transfers between devices: 0.01 us -> 0.91 us  [swap_both(): return lax.ppermute(value, ('blk', 'helper'), pairs)]
    unnamed x12 -> x14, local copies, waits for them, and re-layouts: 3.67 us -> 4.26 us
    ppermute x5 -> x7, starting transfers between devices: 4.81 us -> 5.3 us  [swap(): return lax.ppermute(value, axis, [(i, i ^ 1) for i in range(length)])]
  transfers between devices with their start and end apart: 12 -> 15, of which waited for: 5 -> 7; matrix products, arithmetic and copies ran while one was open for 0% -> 0% of each run, Pallas kernels for 8% -> 10%
where the time goes in v5:
time: 52.9 us
  waiting for transfers between devices  20.9 us (40%)
  starting transfers between devices  17.7 us (33%)
  Pallas kernels  7.68 us (15%)
  local copies, waits for them, and re-layouts  4.26 us (8%)
  between operations  1.43 us (3%)
  other arithmetic  0.85 us (2%)
    ppermute x6, starting transfers between devices, turn(): lax.ppermute(value, 'blk', [(i, (i + by) % length) for i in range(length)])  11.4 us
    ppermute x7, waiting for transfers between devices, swap(): return lax.ppermute(value, axis, [(i, i ^ 1) for i in range(length)])  10.1 us
    ppermute x6, waiting for transfers between devices, turn(): lax.ppermute(value, 'blk', [(i, (i + by) % length) for i in range(length)])  9.94 us
    pallas_call x2, Pallas kernels, score_call(): pl.pallas_call(functools.partial(score_kernel, chunks, qblocks, first, wi...  7.1 us
    ppermute x7, starting transfers between devices, swap(): return lax.ppermute(value, axis, [(i, i ^ 1) for i in range(length)])  5.3 us
    unnamed x14, local copies, waits for them, and re-layouts  4.26 us
  transfers between devices with their start and end apart: 15, of which 7 were waited for; matrix products, arithmetic and copies ran while one was open for 0% of the time, Pallas kernels for 10%

profile of v5, /device:TPU:0, one launch (start us, length us, event | category | flops | bytes accessed | tf_op | source)
XLA Modules:
  0.0 52.9 jit_solution(8354680529983116282)
XLA Ops:
  0.0 3.0 %collective-permute-start.1 = (bf16[512,768]{1,0:T(8,128)(2,1)}, bf16[512,768]{1,0:T(8,128)(2,1)S(1)}, u32[]{:S(2)}, u32[]{:S(2)}) collective-permute-start(bf16[512,768]{1,0:T(8,128)(2,1)} %refs_0_.1), channel_id=1, source_target_pairs={{0,2},{2,0},{4,6},{6,4},{8,10},{10,8},{12,14},{14,12},{1,3},{3,1},... | collective-permute-start | bytes 2359304 | tf_op jit(solution)/shard_map/ppermute | solution.py:27
  3.6 1.1 %copy-done = bf16[512,768]{1,0:T(8,128)(2,1)S(1)} copy-done((bf16[512,768]{1,0:T(8,128)(2,1)S(1)}, bf16[512,768]{1,0:T(8,128)(2,1)}, u32[]{:S(2)}) %copy-start) | copy-done | bytes 786456
  4.8 0.7 %copy-done.1 = s32[512]{0:T(512)S(1)} copy-done((s32[512]{0:T(512)S(1)}, s32[512]{0:T(512)}, u32[]{:S(2)}) %copy-start.1) | copy-done | bytes 2072
  5.5 3.7 %collective-permute-start.5 = (bf16[144,768]{1,0:T(8,128)(2,1)S(1)}, bf16[144,768]{1,0:T(8,128)(2,1)S(1)}, u32[]{:S(2)}, u32[]{:S(2)}) collective-permute-start(bf16[144,768]{1,0:T(8,128)(2,1)S(1)} %get-tuple-element.13.refs_9_), channel_id=1, source_target_pairs={{0,12},{2,14},{4,0},{6,2},{8,4},{10,6},{12,8},{14,10},{1,13},{3,15... | collective-permute-start | bytes 663560 | tf_op jit(solution)/shard_map/ppermute | solution.py:22
  9.8 0.6 %copy-done.3 = s32[4]{0:T(128)S(1)} copy-done((s32[4]{0:T(128)S(1)}, s32[4]{0:T(128)}, u32[]{:S(2)}) %copy-start.3) | copy-done | bytes 40
  11.1 0.6 %collective-permute-start.7 = (s32[8,128]{1,0:T(8,128)S(1)}, s32[8,128]{1,0:T(8,128)S(1)}, u32[]{:S(2)}, u32[]{:S(2)}) collective-permute-start(s32[8,128]{1,0:T(8,128)S(1)} %shard_map.83.refs_4_), channel_id=1, source_target_pairs={{0,2},{2,0},{4,6},{6,4},{8,10},{10,8},{12,14},{14,12},{1,3},{3,1},... | collective-permute-start | bytes 12296 | tf_op jit(solution)/shard_map/ppermute | solution.py:27
  11.6 0.6 %collective-permute-done.6.refs_5_ = s32[8,128]{1,0:T(8,128)S(1)} collective-permute-done((s32[8,128]{1,0:T(8,128)S(1)}, s32[8,128]{1,0:T(8,128)S(1)}, u32[]{:S(2)}, u32[]{:S(2)}) %collective-permute-start.6) | collective-permute-done | bytes 4128 | tf_op jit(solution)/shard_map/ppermute | solution.py:27
  12.2 0.7 %collective-permute-start.8 = (s32[8,128]{1,0:T(8,128)S(1)}, s32[8,128]{1,0:T(8,128)S(1)}, u32[]{:S(2)}, u32[]{:S(2)}) collective-permute-start(s32[8,128]{1,0:T(8,128)S(1)} %shard_map.83.refs_4_), channel_id=1, source_target_pairs={{0,3},{1,2},{2,1},{3,0},{4,7},{5,6},{6,5},{7,4},{8,11},{9,10},{10,... | collective-permute-start | bytes 12296 | tf_op jit(solution)/shard_map/ppermute | solution.py:33
  12.9 7.9 %collective-permute-done.7.refs_6_ = s32[8,128]{1,0:T(8,128)S(1)} collective-permute-done((s32[8,128]{1,0:T(8,128)S(1)}, s32[8,128]{1,0:T(8,128)S(1)}, u32[]{:S(2)}, u32[]{:S(2)}) %collective-permute-start.7) | collective-permute-done | bytes 4128 | tf_op jit(solution)/shard_map/ppermute | solution.py:27
  20.8 1.8 %collective-permute-start.2 = (bf16[128,768]{1,0:T(8,128)(2,1)S(1)}, bf16[128,768]{1,0:T(8,128)(2,1)S(1)}, u32[]{:S(2)}, u32[]{:S(2)}) collective-permute-start(bf16[128,768]{1,0:T(8,128)(2,1)S(1)} %get-tuple-element.12.refs_8_), channel_id=1, source_target_pairs={{0,4},{2,6},{4,8},{6,10},{8,12},{10,14},{12,0},{14,2},{1,5},{3,7},... | collective-permute-start | bytes 589832 | tf_op jit(solution)/shard_map/ppermute | solution.py:22
  22.7 2.0 %collective-permute-start.4 = (bf16[128,768]{1,0:T(8,128)(2,1)S(1)}, bf16[128,768]{1,0:T(8,128)(2,1)S(1)}, u32[]{:S(2)}, u32[]{:S(2)}) collective-permute-start(bf16[128,768]{1,0:T(8,128)(2,1)S(1)} %get-tuple-element.12.refs_8_), channel_id=1, source_target_pairs={{0,12},{2,14},{4,0},{6,2},{8,4},{10,6},{12,8},{14,10},{1,13},{3,15... | collective-permute-start | bytes 589832 | tf_op jit(solution)/shard_map/ppermute | solution.py:22
  24.7 5.9 %collective-permute-done.2.refs_10_ = bf16[128,768]{1,0:T(8,128)(2,1)S(1)} collective-permute-done((bf16[128,768]{1,0:T(8,128)(2,1)S(1)}, bf16[128,768]{1,0:T(8,128)(2,1)S(1)}, u32[]{:S(2)}, u32[]{:S(2)}) %collective-permute-start.2) | collective-permute-done | bytes 196640 | tf_op jit(solution)/shard_map/ppermute | solution.py:22
  30.5 1.8 %collective-permute-done.4.refs_12_ = bf16[128,768]{1,0:T(8,128)(2,1)S(1)} collective-permute-done((bf16[128,768]{1,0:T(8,128)(2,1)S(1)}, bf16[128,768]{1,0:T(8,128)(2,1)S(1)}, u32[]{:S(2)}, u32[]{:S(2)}) %collective-permute-start.4) | collective-permute-done | bytes 196640 | tf_op jit(solution)/shard_map/ppermute | solution.py:22
  32.4 1.2 %collective-permute-start.10 = (bf16[128,768]{1,0:T(8,128)(2,1)S(1)}, bf16[128,768]{1,0:T(8,128)(2,1)S(1)}, u32[]{:S(2)}, u32[]{:S(2)}) collective-permute-start(bf16[128,768]{1,0:T(8,128)(2,1)S(1)} %collective-permute-done.2.refs_10_), channel_id=1, source_target_pairs={{0,4},{2,6},{4,8},{6,10},{8,12},{10,14},{12,0},{14,2},{1,5},{3,7},... | collective-permute-start | bytes 589832 | tf_op jit(solution)/shard_map/ppermute | solution.py:22
  33.6 2.7 %collective-permute-start.11 = (bf16[144,768]{1,0:T(8,128)(2,1)S(1)}, bf16[144,768]{1,0:T(8,128)(2,1)S(1)}, u32[]{:S(2)}, u32[]{:S(2)}) collective-permute-start(bf16[144,768]{1,0:T(8,128)(2,1)S(1)} %collective-permute-done.5.refs_13_), channel_id=1, source_target_pairs={{0,12},{2,14},{4,0},{6,2},{8,4},{10,6},{12,8},{14,10},{1,13},{3,15... | collective-permute-start | bytes 663560 | tf_op jit(solution)/shard_map/ppermute | solution.py:22
  36.3 0.7 %copy-done.2 = f32[64]{0:T(128)S(1)} copy-done((f32[64]{0:T(128)S(1)}, f32[64]{0:T(128)}, u32[]{:S(2)}) %copy-start.2) | copy-done | bytes 280
  36.9 1.1 %copy-done.5 = bf16[512,768]{1,0:T(8,128)(2,1)S(1)} copy-done((bf16[512,768]{1,0:T(8,128)(2,1)S(1)}, bf16[512,768]{1,0:T(8,128)(2,1)}, u32[]{:S(2)}) %copy-start.5) | copy-done | bytes 786456
  38.1 4.9 %shard_map.84 = (f32[16,128]{1,0:T(8,128)S(1)}, bf16[2048,768]{1,0:T(8,128)(2,1)S(1)}, s32[8,128]{1,0:T(8,128)S(1)}) custom-call(f32[64]{0:T(128)S(1)} %copy-done.2, bf16[512,768]{1,0:T(8,128)(2,1)S(1)} %copy-done.5, bf16[512,768]{1,0:T(8,128)(2,1)S(1)} %collective-permute-done.refs_1_, bf16[512,768]{1,0:T(8,128)(2,1)S(1)} %collective-permute-done.1.refs_2_, ...), custom_call_target="tpu_custom_call" | custom-call | flops 2415919104 | bytes 3145728 | tf_op jit(solution)/shard_map/pallas_call | solution.py:163
  43.0 2.3 %collective-permute-done.11.refs_4_ = bf16[144,768]{1,0:T(8,128)(2,1)S(1)} collective-permute-done((bf16[144,768]{1,0:T(8,128)(2,1)S(1)}, bf16[144,768]{1,0:T(8,128)(2,1)S(1)}, u32[]{:S(2)}, u32[]{:S(2)}) %collective-permute-start.11) | collective-permute-done | bytes 221216 | tf_op jit(solution)/shard_map/ppermute | solution.py:22
  45.3 2.2 %shard_map.85 = f32[16,128]{1,0:T(8,128)S(1)} custom-call(f32[64]{0:T(128)S(1)} %copy-done.2, s32[8,128]{1,0:T(8,128)S(1)} %get-tuple-element.16.refs_0_, bf16[2048,768]{1,0:T(8,128)(2,1)S(1)} %get-tuple-element.17.refs_1_, f32[16,128]{1,0:T(8,128)S(1)} %get-tuple-element.18.refs_2_, bf16[128,768]{1,0:T(8,128)(2,1)S(1)} %collective-permute-done.10.refs_3_, ...), custom_call_target="tpu_custom_call" | custom-call | flops 805306368 | bytes 3145728 | tf_op jit(solution)/shard_map/pallas_call | solution.py:163
  47.6 1.5 %collective-permute-start.13 = (f32[4,128]{1,0:T(4,128)S(1)}, f32[4,128]{1,0:T(4,128)S(1)}, u32[]{:S(2)}, u32[]{:S(2)}) collective-permute-start(f32[4,128]{1,0:T(4,128)S(1)} %get-tuple-element.21), channel_id=1, source_target_pairs={{0,2},{2,0},{4,6},{6,4},{8,10},{10,8},{12,14},{14,12},{1,3},{3,1},... | collective-permute-start | bytes 6152 | tf_op jit(solution)/shard_map/ppermute | solution.py:27
  49.7 1.6 %collective-permute-done.13 = f32[4,128]{1,0:T(4,128)S(1)} collective-permute-done((f32[4,128]{1,0:T(4,128)S(1)}, f32[4,128]{1,0:T(4,128)S(1)}, u32[]{:S(2)}, u32[]{:S(2)}) %collective-permute-start.13) | collective-permute-done | bytes 2080 | tf_op jit(solution)/shard_map/ppermute | solution.py:27
  51.3 0.9 %collective-permute-done.14 = f32[4,128]{1,0:T(4,128)S(1)} collective-permute-done((f32[4,128]{1,0:T(4,128)S(1)}, f32[4,128]{1,0:T(4,128)S(1)}, u32[]{:S(2)}, u32[]{:S(2)}) %collective-permute-start.14) | collective-permute-done | bytes 2080 | tf_op jit(solution)/shard_map/ppermute | solution.py:33
  52.2 0.7 %log-plus-one_bitcast_fusion = f32[512]{0:T(512)} fusion(f32[4,128]{1,0:T(4,128)S(1)} %collective-permute-done.14, f32[4,128]{1,0:T(4,128)S(1)} %collective-permute-done.13, f32[4,128]{1,0:T(4,128)S(1)} %collective-permute-done.12, f32[16,128]{1,0:T(8,128)S(1)} %shard_map.85, f32[4]{0:T(128)S(1)} %convert_element_type.7), kind=kLoop, calls=%fused_computation.4 | loop fusion | flops 2048 | bytes 10256 | tf_op jit(solution)/shard_map/reshape | solution.py:238
  (28 shorter events, 1.3 us)
Async XLA Ops:
  0.0 32.3 %collective-permute-start.1 = (bf16[512,768]{1,0:T(8,128)(2,1)}, bf16[512,768]{1,0:T(8,128)(2,1)S(1)}, u32[]{:S(2)}, u32[]{:S(2)}) collective-permute-start(bf16[512,768]{1,0:T(8,128)(2,1)} %refs_0_.1), channel_id=1, source_target_pairs={{0,2},{2,0},{4,6},{6,4},{8,10},{10,8},{12,14},{14,12},{1,3},{3,1},... | collective-permute-start | bytes 2359304 | tf_op jit(solution)/shard_map/ppermute | solution.py:27
  3.6 1.1 %copy-start = (bf16[512,768]{1,0:T(8,128)(2,1)S(1)}, bf16[512,768]{1,0:T(8,128)(2,1)}, u32[]{:S(2)}) copy-start(bf16[512,768]{1,0:T(8,128)(2,1)} %r_ref.1) | copy-start | bytes 2359300
  4.8 0.7 %copy-start.1 = (s32[512]{0:T(512)S(1)}, s32[512]{0:T(512)}, u32[]{:S(2)}) copy-start(s32[512]{0:T(512)} %param.12) | copy-start | bytes 6148
  5.5 26.8 %collective-permute-start.5 = (bf16[144,768]{1,0:T(8,128)(2,1)S(1)}, bf16[144,768]{1,0:T(8,128)(2,1)S(1)}, u32[]{:S(2)}, u32[]{:S(2)}) collective-permute-start(bf16[144,768]{1,0:T(8,128)(2,1)S(1)} %get-tuple-element.13.refs_9_), channel_id=1, source_target_pairs={{0,12},{2,14},{4,0},{6,2},{8,4},{10,6},{12,8},{14,10},{1,13},{3,15... | collective-permute-start | bytes 663560 | tf_op jit(solution)/shard_map/ppermute | solution.py:22
  9.1 23.2 %collective-permute-start.3 = (bf16[144,768]{1,0:T(8,128)(2,1)S(1)}, bf16[144,768]{1,0:T(8,128)(2,1)S(1)}, u32[]{:S(2)}, u32[]{:S(2)}) collective-permute-start(bf16[144,768]{1,0:T(8,128)(2,1)S(1)} %get-tuple-element.13.refs_9_), channel_id=1, source_target_pairs={{0,4},{2,6},{4,8},{6,10},{8,12},{10,14},{12,0},{14,2},{1,5},{3,7},... | collective-permute-start | bytes 663560 | tf_op jit(solution)/shard_map/ppermute | solution.py:22
  9.8 0.7 %copy-start.3 = (s32[4]{0:T(128)S(1)}, s32[4]{0:T(128)}, u32[]{:S(2)}) copy-start(s32[4]{0:T(128)} %clusters_ref) | copy-start | bytes 52
  11.0 1.2 %collective-permute-start.6 = (s32[8,128]{1,0:T(8,128)S(1)}, s32[8,128]{1,0:T(8,128)S(1)}, u32[]{:S(2)}, u32[]{:S(2)}) collective-permute-start(s32[8,128]{1,0:T(8,128)S(1)} %shard_map.83.refs_4_), channel_id=1, source_target_pairs={{0,1},{1,0},{2,3},{3,2},{4,5},{5,4},{6,7},{7,6},{8,9},{9,8},{10,11... | collective-permute-start | bytes 12296 | tf_op jit(solution)/shard_map/ppermute | solution.py:27
  11.1 9.8 %collective-permute-start.7 = (s32[8,128]{1,0:T(8,128)S(1)}, s32[8,128]{1,0:T(8,128)S(1)}, u32[]{:S(2)}, u32[]{:S(2)}) collective-permute-start(s32[8,128]{1,0:T(8,128)S(1)} %shard_map.83.refs_4_), channel_id=1, source_target_pairs={{0,2},{2,0},{4,6},{6,4},{8,10},{10,8},{12,14},{14,12},{1,3},{3,1},... | collective-permute-start | bytes 12296 | tf_op jit(solution)/shard_map/ppermute | solution.py:27
  12.2 10.4 %collective-permute-start.8 = (s32[8,128]{1,0:T(8,128)S(1)}, s32[8,128]{1,0:T(8,128)S(1)}, u32[]{:S(2)}, u32[]{:S(2)}) collective-permute-start(s32[8,128]{1,0:T(8,128)S(1)} %shard_map.83.refs_4_), channel_id=1, source_target_pairs={{0,3},{1,2},{2,1},{3,0},{4,7},{5,6},{6,5},{7,4},{8,11},{9,10},{10,... | collective-permute-start | bytes 12296 | tf_op jit(solution)/shard_map/ppermute | solution.py:33
  20.8 9.7 %collective-permute-start.2 = (bf16[128,768]{1,0:T(8,128)(2,1)S(1)}, bf16[128,768]{1,0:T(8,128)(2,1)S(1)}, u32[]{:S(2)}, u32[]{:S(2)}) collective-permute-start(bf16[128,768]{1,0:T(8,128)(2,1)S(1)} %get-tuple-element.12.refs_8_), channel_id=1, source_target_pairs={{0,4},{2,6},{4,8},{6,10},{8,12},{10,14},{12,0},{14,2},{1,5},{3,7},... | collective-permute-start | bytes 589832 | tf_op jit(solution)/shard_map/ppermute | solution.py:22
  22.7 9.7 %collective-permute-start.4 = (bf16[128,768]{1,0:T(8,128)(2,1)S(1)}, bf16[128,768]{1,0:T(8,128)(2,1)S(1)}, u32[]{:S(2)}, u32[]{:S(2)}) collective-permute-start(bf16[128,768]{1,0:T(8,128)(2,1)S(1)} %get-tuple-element.12.refs_8_), channel_id=1, source_target_pairs={{0,12},{2,14},{4,0},{6,2},{8,4},{10,6},{12,8},{14,10},{1,13},{3,15... | collective-permute-start | bytes 589832 | tf_op jit(solution)/shard_map/ppermute | solution.py:22
  30.5 5.7 %collective-permute-start = (bf16[512,768]{1,0:T(8,128)(2,1)}, bf16[512,768]{1,0:T(8,128)(2,1)S(1)}, u32[]{:S(2)}, u32[]{:S(2)}) collective-permute-start(bf16[512,768]{1,0:T(8,128)(2,1)} %refs_0_.1), channel_id=1, source_target_pairs={{0,1},{1,0},{2,3},{3,2},{4,5},{5,4},{6,7},{7,6},{8,9},{9,8},{10,11... | collective-permute-start | bytes 2359304 | tf_op jit(solution)/shard_map/ppermute | solution.py:27
  32.3 4.0 %collective-permute-start.9 = (bf16[512,768]{1,0:T(8,128)(2,1)S(1)}, bf16[512,768]{1,0:T(8,128)(2,1)S(1)}, u32[]{:S(2)}, u32[]{:S(2)}) collective-permute-start(bf16[512,768]{1,0:T(8,128)(2,1)S(1)} %collective-permute-done.1.refs_2_), channel_id=1, source_target_pairs={{0,1},{1,0},{2,3},{3,2},{4,5},{5,4},{6,7},{7,6},{8,9},{9,8},{10,11... | collective-permute-start | bytes 2359304 | tf_op jit(solution)/shard_map/ppermute | solution.py:27
  32.4 10.6 %collective-permute-start.10 = (bf16[128,768]{1,0:T(8,128)(2,1)S(1)}, bf16[128,768]{1,0:T(8,128)(2,1)S(1)}, u32[]{:S(2)}, u32[]{:S(2)}) collective-permute-start(bf16[128,768]{1,0:T(8,128)(2,1)S(1)} %collective-permute-done.2.refs_10_), channel_id=1, source_target_pairs={{0,4},{2,6},{4,8},{6,10},{8,12},{10,14},{12,0},{14,2},{1,5},{3,7},... | collective-permute-start | bytes 589832 | tf_op jit(solution)/shard_map/ppermute | solution.py:22
  33.6 11.7 %collective-permute-start.11 = (bf16[144,768]{1,0:T(8,128)(2,1)S(1)}, bf16[144,768]{1,0:T(8,128)(2,1)S(1)}, u32[]{:S(2)}, u32[]{:S(2)}) collective-permute-start(bf16[144,768]{1,0:T(8,128)(2,1)S(1)} %collective-permute-done.5.refs_13_), channel_id=1, source_target_pairs={{0,12},{2,14},{4,0},{6,2},{8,4},{10,6},{12,8},{14,10},{1,13},{3,15... | collective-permute-start | bytes 663560 | tf_op jit(solution)/shard_map/ppermute | solution.py:22
  36.3 0.7 %copy-start.2 = (f32[64]{0:T(128)S(1)}, f32[64]{0:T(128)}, u32[]{:S(2)}) copy-start(f32[64]{0:T(128)} %beta_ref.3) | copy-start | bytes 772
  36.9 1.1 %copy-start.5 = (bf16[512,768]{1,0:T(8,128)(2,1)S(1)}, bf16[512,768]{1,0:T(8,128)(2,1)}, u32[]{:S(2)}) copy-start(bf16[512,768]{1,0:T(8,128)(2,1)} %refs_0_.1) | copy-start | bytes 2359300
  43.0 6.5 %copy-start.4 = (s32[4]{0:T(128)S(1)}, s32[4]{0:T(128)}, u32[]{:S(2)}) copy-start(s32[4]{0:T(128)} %clusters_ref) | copy-start | bytes 52
  43.0 6.5 %copy-start.6 = (s32[64]{0:T(128)S(1)}, s32[64]{0:T(128)}, u32[]{:S(2)}) copy-start(s32[64]{0:T(128)} %param.15) | copy-start | bytes 772
  47.6 2.1 %collective-permute-start.12 = (f32[4,128]{1,0:T(4,128)S(1)}, f32[4,128]{1,0:T(4,128)S(1)}, u32[]{:S(2)}, u32[]{:S(2)}) collective-permute-start(f32[4,128]{1,0:T(4,128)S(1)} %get-tuple-element.19), channel_id=1, source_target_pairs={{0,1},{1,0},{2,3},{3,2},{4,5},{5,4},{6,7},{7,6},{8,9},{9,8},{10,11... | collective-permute-start | bytes 6152 | tf_op jit(solution)/shard_map/ppermute | solution.py:27
  47.6 3.7 %collective-permute-start.13 = (f32[4,128]{1,0:T(4,128)S(1)}, f32[4,128]{1,0:T(4,128)S(1)}, u32[]{:S(2)}, u32[]{:S(2)}) collective-permute-start(f32[4,128]{1,0:T(4,128)S(1)} %get-tuple-element.21), channel_id=1, source_target_pairs={{0,2},{2,0},{4,6},{6,4},{8,10},{10,8},{12,14},{14,12},{1,3},{3,1},... | collective-permute-start | bytes 6152 | tf_op jit(solution)/shard_map/ppermute | solution.py:27
  49.2 3.0 %collective-permute-start.14 = (f32[4,128]{1,0:T(4,128)S(1)}, f32[4,128]{1,0:T(4,128)S(1)}, u32[]{:S(2)}, u32[]{:S(2)}) collective-permute-start(f32[4,128]{1,0:T(4,128)S(1)} %get-tuple-element.20), channel_id=1, source_target_pairs={{0,3},{1,2},{2,1},{3,0},{4,7},{5,6},{6,5},{7,4},{8,11},{9,10},{10,... | collective-permute-start | bytes 6152 | tf_op jit(solution)/shard_map/ppermute | solution.py:33

commit v6 on v5

v6 whole, which is shorter than its diff:
```python
import functools
import math

import jax
import jax.numpy as jnp
from jax import lax
from jax.experimental import pallas as pl
from jax.experimental.pallas import tpu as pltpu
from jax.sharding import PartitionSpec as P

LANES = 128
TABLE = 16
LOG2E = 1.4426950408889634
DEAD = -1.0e30
SMEM = pl.BlockSpec(memory_space=pltpu.SMEM)
VMEM = pl.BlockSpec(memory_space=pltpu.VMEM)
ANY = pl.BlockSpec(memory_space=pl.ANY)
WHOLE = pltpu.CompilerParams(vmem_limit_bytes=60 * 1024 * 1024)
PARAMS = pltpu.CompilerParams(vmem_limit_bytes=24 * 1024 * 1024)


def turn(value, by):
    length = lax.axis_size("blk")
    return lax.ppermute(value, "blk", [(i, (i + by) % length) for i in range(length)])


def swap(value, axis):
    length = lax.axis_size(axis)
    return lax.ppermute(value, axis, [(i, i ^ 1) for i in range(length)])


def swap_both(value):
    nblk, nhelper = lax.axis_size("blk"), lax.axis_size("helper")
    pairs = [(i, (i ^ nhelper) ^ 1) for i in range(nblk * nhelper)]
    return lax.ppermute(value, ("blk", "helper"), pairs)


def after(value, *others):
    return lax.optimization_barrier((value, *others))[0]


def cost(flops, moved):
    return pl.CostEstimate(flops=flops, bytes_accessed=moved, transcendentals=0)


def rows_of(index, count=1):
    return pl.ds(pl.multiple_of(index * LANES, LANES), count * LANES)


def pack_kernel(
    nhelper, helper_ref, r_ref, q_ref, ids_ref, clusters_ref, live_ref, count_ref, r_out, q_out, *scratch
):
    ids, clusters, live, count, sem = scratch
    chunks = ids_ref.shape[0] // nhelper
    qblocks = clusters_ref.shape[0]
    small = [
        pltpu.make_async_copy(ids_ref, ids, sem.at[0]),
        pltpu.make_async_copy(clusters_ref, clusters, sem.at[1]),
        pltpu.make_async_copy(live_ref, live, sem.at[2]),
        pltpu.make_async_copy(count_ref, count, sem.at[3]),
    ]
    large = [pltpu.make_async_copy(q_ref, q_out.at[pl.ds(0, qblocks * LANES)], sem.at[4])]
    for c in range(chunks):
        rows = rows_of(helper_ref[0] + nhelper * c)
        large.append(pltpu.make_async_copy(r_ref.at[rows], r_out.at[rows_of(c)], sem.at[5 + c]))
    for copy in small + large:
        copy.start()
    for copy in small:
        copy.wait()
    lane = lax.broadcasted_iota(jnp.int32, (TABLE, LANES), 1)
    row = lax.broadcasted_iota(jnp.int32, (TABLE, LANES), 0)
    table = jnp.full((TABLE, LANES), -1, jnp.int32)
    for c in range(chunks):
        tile = helper_ref[0] + nhelper * c
        here = jnp.where(tile * LANES + lane < live[0], ids[pl.ds(tile, 1), :], -1)
        table = jnp.where(row == c, here, table)
    columns = pl.ds(0, LANES)
    r_out[pl.ds(chunks * LANES, TABLE), columns] = table.astype(jnp.float32).astype(jnp.bfloat16)
    table = jnp.where(lane == qblocks, count[0], 0)
    for k in range(qblocks):
        table = jnp.where(lane == k, clusters[k], table)
    q_out[pl.ds(qblocks * LANES, TABLE), columns] = table.astype(jnp.float32).astype(jnp.bfloat16)
    for copy in large:
        copy.wait()


def score_kernel(chunks, qblocks, first, wide, beta_ref, *refs):
    if first:
        q_refs, r_refs, refs = list(refs[:4]), list(refs[4:-11]), refs[-11:]
        out_ref, qv, info_out, q_list, ids_ref, other_ref, info, q_own, r_own, sem, info_sem = refs
        fetch = (
            pltpu.make_async_copy(r_refs[0], r_own, sem.at[0]),
            pltpu.make_async_copy(q_refs[0], q_own, sem.at[1]),
        )
        q_refs[0], r_refs[0] = q_own, r_own
    else:
        info, qv, prev_ref, *r_refs, out_ref, q_list, ids_ref, other_ref = refs
        fetch = ()
    width = qv.shape[1]
    height = chunks * LANES
    for copy in fetch:
        copy.start()

    def spread(s):
        table = r_refs[s][pl.ds(height, TABLE), pl.ds(0, LANES)].astype(jnp.float32)
        for c in range(chunks):
            ids = jnp.broadcast_to(table[c : c + 1, :], (LANES, LANES)).T
            rows = pl.ds(s * height + c * LANES, LANES)
            ids_ref[rows, :] = ids
            other_ref[rows, :] = jnp.where(ids < 0.0, DEAD, -4.0)

    for s in range(len(fetch) // 2, len(r_refs)):
        spread(s)
    for copy in fetch:
        copy.wait()
    if first:
        spread(0)
        for s, q_ref in enumerate(q_refs):
            table = q_ref[pl.ds(qblocks * LANES, TABLE), pl.ds(0, LANES)].astype(jnp.float32)
            info_out[s : s + 1, :] = table[0:1, :].astype(jnp.int32)
        copy = pltpu.make_async_copy(info_out, info, info_sem)
        copy.start()
        copy.wait()

    q_count = jnp.int32(0)
    for source in range(4):
        blocks = info[source, qblocks]

        def one_block(block, carry, source=source, q_count=q_count):
            if first:
                qv[rows_of(q_count + block), :] = q_refs[source][rows_of(block), :]
            q_list[q_count + block, 0] = source * qblocks + block
            q_list[q_count + block, 1] = info[source, block]
            return carry

        lax.fori_loop(0, blocks, one_block, 0)
        q_count = q_count + blocks

    factor = LOG2E / math.sqrt(width)
    out_ref[...] = jnp.zeros_like(out_ref) if first else prev_ref[...]

    def query_blocks(group, carry):
        parts = []
        for side in range(wide):
            entry = jnp.minimum(wide * group + side, q_count - 1)
            slot, cluster = q_list[entry, 0], q_list[entry, 1]
            beta = beta_ref[cluster]
            parts.append(
                (slot, cluster.astype(jnp.float32), beta * factor, beta * beta * (0.5 * LOG2E))
            )
        accs = [jnp.zeros((8, LANES), jnp.float32) for _ in range(wide)]
        for s, r_ref in enumerate(r_refs):
            tile = r_ref[pl.ds(0, height), :]
            rows = pl.ds(s * height, height)
            for pair in range(wide // 2):
                score = lax.dot_general(
                    tile,
                    qv[rows_of(wide * group + 2 * pair, 2), :],
                    (((1,), (1,)), ((), ())),
                    preferred_element_type=jnp.float32,
                )
                for half in range(2):
                    side = 2 * pair + half
                    _, cluster, scale, offset = parts[side]
                    part = score[:, half * LANES : (half + 1) * LANES]
                    weight = jnp.where(ids_ref[rows, :] == cluster, 0.0, other_ref[rows, :])
                    value = jnp.exp2((part * scale - offset) + weight)
                    accs[side] += jnp.sum(value.reshape(height // 8, 8, LANES), axis=0)
        for side in range(wide):
            total = jnp.sum(accs[side], axis=0, keepdims=True)

            @pl.when(wide * group + side < q_count)
            def _(side=side, total=total):
                row = pl.ds(parts[side][0], 1)
                out_ref[row, :] = out_ref[row, :] + total

        return carry

    lax.fori_loop(0, (q_count + wide - 1) // wide, query_blocks, 0)


def score_call(chunks, qblocks, wide, beta, given, payloads, first):
    width = payloads[0].shape[1]
    slots = 4 * qblocks
    height = chunks * LANES
    totals_shape = jax.ShapeDtypeStruct((slots, LANES), jnp.float32)
    packed_shape = jax.ShapeDtypeStruct((slots * LANES, width), jnp.bfloat16)
    info_shape = jax.ShapeDtypeStruct((8, LANES), jnp.int32)
    spread = pltpu.VMEM((len(payloads) * height, LANES), jnp.float32)
    scratch = [pltpu.SMEM((slots, 2), jnp.int32), spread, spread]
    specs = [VMEM] * (len(given) + len(payloads))
    if first:
        specs[0] = specs[len(given)] = ANY
        scratch += [
            pltpu.SMEM((8, LANES), jnp.int32),
            pltpu.VMEM(given[0].shape, jnp.bfloat16),
            pltpu.VMEM(payloads[0].shape, jnp.bfloat16),
            pltpu.SemaphoreType.DMA((2,)),
            pltpu.SemaphoreType.DMA,
        ]
    else:
        specs[0] = SMEM
    return pl.pallas_call(
        functools.partial(score_kernel, chunks, qblocks, first, wide),
        out_shape=(totals_shape, packed_shape, info_shape) if first else totals_shape,
        in_specs=[SMEM] + specs,
        out_specs=(VMEM, VMEM, VMEM) if first else VMEM,
        scratch_shapes=scratch,
        compiler_params=PARAMS,
        cost_estimate=cost(
            2 * slots * LANES * len(payloads) * height * width, 2 * slots * LANES * width
        ),
    )(beta, *given, *payloads)


def per_device(
    queries,
    query_block_cluster,
    block_count,
    references,
    ref_cluster,
    ref_rows,
    cluster_beta,
    cluster_member_count,
):
    nblk, nhelper = lax.axis_size("blk"), lax.axis_size("helper")
    helper = lax.axis_index("helper").astype(jnp.int32)
    qblocks = query_block_cluster.shape[0]
    rows, width = references.shape
    tiles = rows // LANES
    chunks = tiles // nhelper
    sources = nblk // 2

    own, q_own = pl.pallas_call(
        functools.partial(pack_kernel, nhelper),
        out_shape=(
            jax.ShapeDtypeStruct((chunks * LANES + TABLE, width), jnp.bfloat16),
            jax.ShapeDtypeStruct((queries.shape[0] + TABLE, width), jnp.bfloat16),
        ),
        in_specs=[SMEM] + [ANY] * 6,
        out_specs=(VMEM, VMEM),
        scratch_shapes=[
            pltpu.VMEM((tiles, LANES), jnp.int32),
            pltpu.SMEM((qblocks,), jnp.int32),
            pltpu.SMEM((1,), jnp.int32),
            pltpu.SMEM((1,), jnp.int32),
            pltpu.SemaphoreType.DMA((5 + chunks,)),
        ],
        compiler_params=WHOLE,
        cost_estimate=cost(1, 4 * rows * width),
    )(
        helper[None],
        references,
        queries,
        ref_cluster.reshape(tiles, LANES),
        query_block_cluster,
        ref_rows,
        block_count,
    )
    q_partner = swap(q_own, "blk")
    q_helper = swap(q_own, "helper")

    above, below = [own], [own]
    for step in range(1, sources // 2 + 1):
        above.append(turn(above[-1], 2))
        if step < (sources + 1) // 2:
            below.append(turn(below[-1], -2))
    early = [own] + above[1:-1] + below[1:]
    q_both = swap(after(q_partner, above[-2], below[-1]), "helper")

    totals, packed, info = score_call(
        chunks, qblocks, 2, cluster_beta, (q_own, q_helper, q_partner, q_both), early, True
    )
    totals = score_call(
        chunks, qblocks, 4, cluster_beta, (info, packed, totals), above[-1:], False
    )
    totals = totals.reshape(4, qblocks, LANES)
    total = totals[0] + swap(totals[1], "helper") + swap(totals[2], "blk") + swap_both(totals[3])
    columns = jnp.arange(cluster_member_count.shape[0], dtype=jnp.int32)
    onehot = query_block_cluster[:, None] == columns[None, :]
    sizes = jnp.sum(jnp.where(onehot, cluster_member_count[None, :], 0), axis=1)
    density = jnp.log1p(total / sizes.astype(jnp.float32)[:, None])
    return density.reshape(queries.shape[0])


def solution(mesh):
    in_specs = (
        P(("parts", "blk", "helper"), None),
        P(("parts", "blk", "helper")),
        P(("parts", "blk", "helper")),
        P(("parts", "blk"), None),
        P(("parts", "blk")),
        P(("parts", "blk")),
        P("parts"),
        P("parts"),
    )
    out_specs = P(("parts", "blk", "helper"))
    return jax.shard_map(
        per_device, mesh=mesh, in_specs=in_specs, out_specs=out_specs, check_vma=False
    )
```

time: 52.9 us -> 49.2 us (0.930)
  starting transfers between devices: 17.7 us -> 9.93 us
  Pallas kernels: 7.68 us -> 10.9 us
  waiting for transfers between devices: 20.9 us -> 23.4 us
  local copies, waits for them, and re-layouts: 4.26 us -> 2.82 us
    ppermute x6 -> x3, waiting for transfers between devices: 9.94 us -> 20.6 us  [turn(): lax.ppermute(value, 'blk', [(i, (i + by) % length) for i in range(length)])]
    ppermute x7 -> x5, waiting for transfers between devices: 10.1 us -> 2.77 us  [swap(): return lax.ppermute(value, axis, [(i, i ^ 1) for i in range(length)])]
    ppermute x6 -> x3, starting transfers between devices: 11.4 us -> 4.96 us  [turn(): lax.ppermute(value, 'blk', [(i, (i + by) % length) for i in range(length)])]
    pallas_call x2 -> x1, Pallas kernels: 0.58 us -> 2.38 us  [per_device(): pl.pallas_call(functools.partial(pack_kernel, nhelper), out_shape=(jax.Sh...]
    ppermute x7 -> x5, starting transfers between devices: 5.3 us -> 3.68 us  [swap(): return lax.ppermute(value, axis, [(i, i ^ 1) for i in range(length)])]
    unnamed x14 -> x10, local copies, waits for them, and re-layouts: 4.26 us -> 2.81 us
    pallas_call x2, Pallas kernels: 7.1 us -> 8.5 us  [score_call(): pl.pallas_call(functools.partial(score_kernel, chunks, qblocks, first, wi...]
    ppermute x2 -> x1, waiting for transfers between devices: 0.91 us -> 0.01 us  [swap_both(): return lax.ppermute(value, ('blk', 'helper'), pairs)]
  transfers between devices with their start and end apart: 15 -> 9, of which waited for: 7 -> 5; matrix products, arithmetic and copies ran while one was open for 0% -> 0% of each run, Pallas kernels for 10% -> 12%
where the time goes in v6:
time: 49.2 us
  waiting for transfers between devices  23.4 us (48%)
  Pallas kernels  10.9 us (22%)
  starting transfers between devices  9.93 us (20%)
  local copies, waits for them, and re-layouts  2.82 us (6%)
  between operations  1.37 us (3%)
  other arithmetic  0.85 us (2%)
    ppermute x3, waiting for transfers between devices, turn(): lax.ppermute(value, 'blk', [(i, (i + by) % length) for i in range(length)])  20.6 us
    pallas_call x2, Pallas kernels, score_call(): pl.pallas_call(functools.partial(score_kernel, chunks, qblocks, first, wi...  8.5 us
    ppermute x3, starting transfers between devices, turn(): lax.ppermute(value, 'blk', [(i, (i + by) % length) for i in range(length)])  4.96 us
    ppermute x5, starting transfers between devices, swap(): return lax.ppermute(value, axis, [(i, i ^ 1) for i in range(length)])  3.68 us
    unnamed x10, local copies, waits for them, and re-layouts  2.81 us
    ppermute x5, waiting for transfers between devices, swap(): return lax.ppermute(value, axis, [(i, i ^ 1) for i in range(length)])  2.77 us
    pallas_call x1, Pallas kernels, per_device(): pl.pallas_call(functools.partial(pack_kernel, nhelper), out_shape=(jax.Sh...  2.38 us
    ppermute x1, starting transfers between devices, swap_both(): return lax.ppermute(value, ('blk', 'helper'), pairs)  1.29 us
  transfers between devices with their start and end apart: 9, of which 5 were waited for; matrix products, arithmetic and copies ran while one was open for 0% of the time, Pallas kernels for 12%

profile of v6, /device:TPU:0, one launch (start us, length us, event | category | flops | bytes accessed | tf_op | source)
XLA Modules:
  0.0 49.2 jit_solution(741484207765419350)
XLA Ops:
  1.3 2.4 %shard_map.82 = (bf16[272,768]{1,0:T(8,128)(2,1)}, bf16[528,768]{1,0:T(8,128)(2,1)}) custom-call(s32[1]{0:T(128)} %bitcast.helper_ref, bf16[512,768]{1,0:T(8,128)(2,1)} %r_ref.1, bf16[512,768]{1,0:T(8,128)(2,1)} %q_ref.1, s32[4,128]{1,0:T(4,128)} %bitcast.4, s32[4]{0:T(128)} %clusters_ref.1, s32[1]{0:T(128)S(6)} %copy.10.live_ref, s32[1]{0:T(128)S(6)} %copy.9.count_ref), custom_call_target="tpu_custom_call" | custom-call | flops 1 | bytes 1572864 | tf_op jit(solution)/shard_map/pallas_call | solution.py:234
  3.7 3.0 %collective-permute-start.1 = (bf16[528,768]{1,0:T(8,128)(2,1)}, bf16[528,768]{1,0:T(8,128)(2,1)S(1)}, u32[]{:S(2)}, u32[]{:S(2)}) collective-permute-start(bf16[528,768]{1,0:T(8,128)(2,1)} %get-tuple-element.11.refs_0_), channel_id=1, source_target_pairs={{0,2},{2,0},{4,6},{6,4},{8,10},{10,8},{12,14},{14,12},{1,3},{3,1},... | collective-permute-start | bytes 2433032 | tf_op jit(solution)/shard_map/ppermute | solution.py:29
  6.7 1.6 %collective-permute-start.2 = (bf16[272,768]{1,0:T(8,128)(2,1)}, bf16[272,768]{1,0:T(8,128)(2,1)S(1)}, u32[]{:S(2)}, u32[]{:S(2)}) collective-permute-start(bf16[272,768]{1,0:T(8,128)(2,1)} %get-tuple-element.12.refs_4_), channel_id=1, source_target_pairs={{0,4},{2,6},{4,8},{6,10},{8,12},{10,14},{12,0},{14,2},{1,5},{3,7},... | collective-permute-start | bytes 1253384 | tf_op jit(solution)/shard_map/ppermute | solution.py:24
  8.3 2.2 %collective-permute-start.3 = (bf16[272,768]{1,0:T(8,128)(2,1)}, bf16[272,768]{1,0:T(8,128)(2,1)S(1)}, u32[]{:S(2)}, u32[]{:S(2)}) collective-permute-start(bf16[272,768]{1,0:T(8,128)(2,1)} %get-tuple-element.12.refs_4_), channel_id=1, source_target_pairs={{0,12},{2,14},{4,0},{6,2},{8,4},{10,6},{12,8},{14,10},{1,13},{3,15... | collective-permute-start | bytes 1253384 | tf_op jit(solution)/shard_map/ppermute | solution.py:24
  10.5 10.8 %collective-permute-done.2.refs_5_ = bf16[272,768]{1,0:T(8,128)(2,1)S(1)} collective-permute-done((bf16[272,768]{1,0:T(8,128)(2,1)}, bf16[272,768]{1,0:T(8,128)(2,1)S(1)}, u32[]{:S(2)}, u32[]{:S(2)}) %collective-permute-start.2) | collective-permute-done | bytes 417824 | tf_op jit(solution)/shard_map/ppermute | solution.py:24
  21.3 6.9 %collective-permute-done.3.refs_6_ = bf16[272,768]{1,0:T(8,128)(2,1)S(1)} collective-permute-done((bf16[272,768]{1,0:T(8,128)(2,1)}, bf16[272,768]{1,0:T(8,128)(2,1)S(1)}, u32[]{:S(2)}, u32[]{:S(2)}) %collective-permute-start.3) | collective-permute-done | bytes 417824 | tf_op jit(solution)/shard_map/ppermute | solution.py:24
  28.3 0.0 collective-permute-done.1.refs_2_
  28.3 0.0 collective-permute-start.4
  28.3 1.1 %collective-permute-start.5 = (bf16[272,768]{1,0:T(8,128)(2,1)S(1)}, bf16[272,768]{1,0:T(8,128)(2,1)S(1)}, u32[]{:S(2)}, u32[]{:S(2)}) collective-permute-start(bf16[272,768]{1,0:T(8,128)(2,1)S(1)} %collective-permute-done.2.refs_5_), channel_id=1, source_target_pairs={{0,4},{2,6},{4,8},{6,10},{8,12},{10,14},{12,0},{14,2},{1,5},{3,7},... | collective-permute-start | bytes 1253384 | tf_op jit(solution)/shard_map/ppermute | solution.py:24
  29.4 1.2 %collective-permute-done.4.refs_3_ = bf16[528,768]{1,0:T(8,128)(2,1)S(1)} collective-permute-done((bf16[528,768]{1,0:T(8,128)(2,1)S(1)}, bf16[528,768]{1,0:T(8,128)(2,1)S(1)}, u32[]{:S(2)}, u32[]{:S(2)}) %collective-permute-start.4) | collective-permute-done | bytes 811040 | tf_op jit(solution)/shard_map/ppermute | solution.py:29
  30.6 0.7 %copy-done = f32[64]{0:T(128)S(1)} copy-done((f32[64]{0:T(128)S(1)}, f32[64]{0:T(128)}, u32[]{:S(2)}) %copy-start) | copy-done | bytes 280
  31.3 1.1 %copy-done.1 = bf16[528,768]{1,0:T(8,128)(2,1)S(1)} copy-done((bf16[528,768]{1,0:T(8,128)(2,1)S(1)}, bf16[528,768]{1,0:T(8,128)(2,1)}, u32[]{:S(2)}) %copy-start.1) | copy-done | bytes 811032
  32.4 1.0 %copy-done.2 = bf16[272,768]{1,0:T(8,128)(2,1)S(1)} copy-done((bf16[272,768]{1,0:T(8,128)(2,1)S(1)}, bf16[272,768]{1,0:T(8,128)(2,1)}, u32[]{:S(2)}) %copy-start.2) | copy-done | bytes 417816
  33.4 5.8 %shard_map.83 = (f32[16,128]{1,0:T(8,128)S(1)}, bf16[2048,768]{1,0:T(8,128)(2,1)S(1)}, s32[8,128]{1,0:T(8,128)S(1)}) custom-call(f32[64]{0:T(128)S(1)} %copy-done, bf16[528,768]{1,0:T(8,128)(2,1)S(1)} %copy-done.1, bf16[528,768]{1,0:T(8,128)(2,1)S(1)} %collective-permute-done.refs_1_, bf16[528,768]{1,0:T(8,128)(2,1)S(1)} %collective-permute-done.1.refs_2_, ...), custom_call_target="tpu_custom_call" | custom-call | flops 2415919104 | bytes 3145728 | tf_op jit(solution)/shard_map/pallas_call | solution.py:203
  39.2 0.0 copy-start.3
  39.2 0.0 copy-start.4
  39.3 2.9 %collective-permute-done.5.refs_3_ = bf16[272,768]{1,0:T(8,128)(2,1)S(1)} collective-permute-done((bf16[272,768]{1,0:T(8,128)(2,1)S(1)}, bf16[272,768]{1,0:T(8,128)(2,1)S(1)}, u32[]{:S(2)}, u32[]{:S(2)}) %collective-permute-start.5) | collective-permute-done | bytes 417824 | tf_op jit(solution)/shard_map/ppermute | solution.py:24
  42.1 2.7 %shard_map.84 = f32[16,128]{1,0:T(8,128)S(1)} custom-call(f32[64]{0:T(128)S(1)} %copy-done, s32[8,128]{1,0:T(8,128)S(1)} %get-tuple-element.14.refs_0_, bf16[2048,768]{1,0:T(8,128)(2,1)S(1)} %get-tuple-element.15.refs_1_, f32[16,128]{1,0:T(8,128)S(1)} %get-tuple-element.16.refs_2_, bf16[272,768]{1,0:T(8,128)(2,1)S(1)} %collective-permute-done.5.refs_3_), custom_call_target="tpu_custom_call" | custom-call | flops 805306368 | bytes 3145728 | tf_op jit(solution)/shard_map/pallas_call | solution.py:203
  44.8 0.1 collective-permute-start.6
  44.9 0.6 %collective-permute-start.7 = (f32[4,128]{1,0:T(4,128)S(1)}, f32[4,128]{1,0:T(4,128)S(1)}, u32[]{:S(2)}, u32[]{:S(2)}) collective-permute-start(f32[4,128]{1,0:T(4,128)S(1)} %get-tuple-element.19), channel_id=1, source_target_pairs={{0,2},{2,0},{4,6},{6,4},{8,10},{10,8},{12,14},{14,12},{1,3},{3,1},... | collective-permute-start | bytes 6152 | tf_op jit(solution)/shard_map/ppermute | solution.py:29
  45.5 1.3 %collective-permute-start.8 = (f32[4,128]{1,0:T(4,128)S(1)}, f32[4,128]{1,0:T(4,128)S(1)}, u32[]{:S(2)}, u32[]{:S(2)}) collective-permute-start(f32[4,128]{1,0:T(4,128)S(1)} %get-tuple-element.18), channel_id=1, source_target_pairs={{0,3},{1,2},{2,1},{3,0},{4,7},{5,6},{6,5},{7,4},{8,11},{9,10},{10,... | collective-permute-start | bytes 6152 | tf_op jit(solution)/shard_map/ppermute | solution.py:35
  46.8 0.2 select_reduce_fusion
  47.0 1.6 %collective-permute-done.7 = f32[4,128]{1,0:T(4,128)S(1)} collective-permute-done((f32[4,128]{1,0:T(4,128)S(1)}, f32[4,128]{1,0:T(4,128)S(1)}, u32[]{:S(2)}, u32[]{:S(2)}) %collective-permute-start.7) | collective-permute-done | bytes 2080 | tf_op jit(solution)/shard_map/ppermute | solution.py:29
  48.6 0.7 %log-plus-one_bitcast_fusion = f32[512]{0:T(512)} fusion(f32[4,128]{1,0:T(4,128)S(1)} %collective-permute-done.8, f32[4,128]{1,0:T(4,128)S(1)} %collective-permute-done.7, f32[4,128]{1,0:T(4,128)S(1)} %collective-permute-done.6, f32[16,128]{1,0:T(8,128)S(1)} %shard_map.84, f32[4]{0:T(128)S(1)} %convert_element_type.7), kind=kLoop, calls=%fused_computation.4 | loop fusion | flops 2048 | bytes 10256 | tf_op jit(solution)/shard_map/reshape | solution.py:283
  (11 shorter events, 0.0 us)
Async XLA Ops:
  3.7 24.6 %collective-permute-start.1 = (bf16[528,768]{1,0:T(8,128)(2,1)}, bf16[528,768]{1,0:T(8,128)(2,1)S(1)}, u32[]{:S(2)}, u32[]{:S(2)}) collective-permute-start(bf16[528,768]{1,0:T(8,128)(2,1)} %get-tuple-element.11.refs_0_), channel_id=1, source_target_pairs={{0,2},{2,0},{4,6},{6,4},{8,10},{10,8},{12,14},{14,12},{1,3},{3,1},... | collective-permute-start | bytes 2433032 | tf_op jit(solution)/shard_map/ppermute | solution.py:29
  6.7 14.6 %collective-permute-start.2 = (bf16[272,768]{1,0:T(8,128)(2,1)}, bf16[272,768]{1,0:T(8,128)(2,1)S(1)}, u32[]{:S(2)}, u32[]{:S(2)}) collective-permute-start(bf16[272,768]{1,0:T(8,128)(2,1)} %get-tuple-element.12.refs_4_), channel_id=1, source_target_pairs={{0,4},{2,6},{4,8},{6,10},{8,12},{10,14},{12,0},{14,2},{1,5},{3,7},... | collective-permute-start | bytes 1253384 | tf_op jit(solution)/shard_map/ppermute | solution.py:24
  8.3 20.0 %collective-permute-start.3 = (bf16[272,768]{1,0:T(8,128)(2,1)}, bf16[272,768]{1,0:T(8,128)(2,1)S(1)}, u32[]{:S(2)}, u32[]{:S(2)}) collective-permute-start(bf16[272,768]{1,0:T(8,128)(2,1)} %get-tuple-element.12.refs_4_), channel_id=1, source_target_pairs={{0,12},{2,14},{4,0},{6,2},{8,4},{10,6},{12,8},{14,10},{1,13},{3,15... | collective-permute-start | bytes 1253384 | tf_op jit(solution)/shard_map/ppermute | solution.py:24
  10.5 18.9 %collective-permute-start = (bf16[528,768]{1,0:T(8,128)(2,1)}, bf16[528,768]{1,0:T(8,128)(2,1)S(1)}, u32[]{:S(2)}, u32[]{:S(2)}) collective-permute-start(bf16[528,768]{1,0:T(8,128)(2,1)} %get-tuple-element.11.refs_0_), channel_id=1, source_target_pairs={{0,1},{1,0},{2,3},{3,2},{4,5},{5,4},{6,7},{7,6},{8,9},{9,8},{10,11... | collective-permute-start | bytes 2433032 | tf_op jit(solution)/shard_map/ppermute | solution.py:29
  28.3 2.3 %collective-permute-start.4 = (bf16[528,768]{1,0:T(8,128)(2,1)S(1)}, bf16[528,768]{1,0:T(8,128)(2,1)S(1)}, u32[]{:S(2)}, u32[]{:S(2)}) collective-permute-start(bf16[528,768]{1,0:T(8,128)(2,1)S(1)} %collective-permute-done.1.refs_2_), channel_id=1, source_target_pairs={{0,1},{1,0},{2,3},{3,2},{4,5},{5,4},{6,7},{7,6},{8,9},{9,8},{10,11... | collective-permute-start | bytes 2433032 | tf_op jit(solution)/shard_map/ppermute | solution.py:29
  28.3 13.9 %collective-permute-start.5 = (bf16[272,768]{1,0:T(8,128)(2,1)S(1)}, bf16[272,768]{1,0:T(8,128)(2,1)S(1)}, u32[]{:S(2)}, u32[]{:S(2)}) collective-permute-start(bf16[272,768]{1,0:T(8,128)(2,1)S(1)} %collective-permute-done.2.refs_5_), channel_id=1, source_target_pairs={{0,4},{2,6},{4,8},{6,10},{8,12},{10,14},{12,0},{14,2},{1,5},{3,7},... | collective-permute-start | bytes 1253384 | tf_op jit(solution)/shard_map/ppermute | solution.py:24
  30.6 0.7 %copy-start = (f32[64]{0:T(128)S(1)}, f32[64]{0:T(128)}, u32[]{:S(2)}) copy-start(f32[64]{0:T(128)} %beta_ref.3) | copy-start | bytes 772
  31.3 1.1 %copy-start.1 = (bf16[528,768]{1,0:T(8,128)(2,1)S(1)}, bf16[528,768]{1,0:T(8,128)(2,1)}, u32[]{:S(2)}) copy-start(bf16[528,768]{1,0:T(8,128)(2,1)} %get-tuple-element.11.refs_0_) | copy-start | bytes 2433028
  32.4 1.0 %copy-start.2 = (bf16[272,768]{1,0:T(8,128)(2,1)S(1)}, bf16[272,768]{1,0:T(8,128)(2,1)}, u32[]{:S(2)}) copy-start(bf16[272,768]{1,0:T(8,128)(2,1)} %get-tuple-element.12.refs_4_) | copy-start | bytes 1253380
  39.2 7.5 %copy-start.3 = (s32[4]{0:T(128)S(1)}, s32[4]{0:T(128)}, u32[]{:S(2)}) copy-start(s32[4]{0:T(128)} %clusters_ref.1) | copy-start | bytes 52
  39.2 7.5 %copy-start.4 = (s32[64]{0:T(128)S(1)}, s32[64]{0:T(128)}, u32[]{:S(2)}) copy-start(s32[64]{0:T(128)} %param.15) | copy-start | bytes 772
  44.8 2.1 %collective-permute-start.6 = (f32[4,128]{1,0:T(4,128)S(1)}, f32[4,128]{1,0:T(4,128)S(1)}, u32[]{:S(2)}, u32[]{:S(2)}) collective-permute-start(f32[4,128]{1,0:T(4,128)S(1)} %get-tuple-element.17), channel_id=1, source_target_pairs={{0,1},{1,0},{2,3},{3,2},{4,5},{5,4},{6,7},{7,6},{8,9},{9,8},{10,11... | collective-permute-start | bytes 6152 | tf_op jit(solution)/shard_map/ppermute | solution.py:29
  44.9 3.7 %collective-permute-start.7 = (f32[4,128]{1,0:T(4,128)S(1)}, f32[4,128]{1,0:T(4,128)S(1)}, u32[]{:S(2)}, u32[]{:S(2)}) collective-permute-start(f32[4,128]{1,0:T(4,128)S(1)} %get-tuple-element.19), channel_id=1, source_target_pairs={{0,2},{2,0},{4,6},{6,4},{8,10},{10,8},{12,14},{14,12},{1,3},{3,1},... | collective-permute-start | bytes 6152 | tf_op jit(solution)/shard_map/ppermute | solution.py:29
  45.5 3.1 %collective-permute-start.8 = (f32[4,128]{1,0:T(4,128)S(1)}, f32[4,128]{1,0:T(4,128)S(1)}, u32[]{:S(2)}, u32[]{:S(2)}) collective-permute-start(f32[4,128]{1,0:T(4,128)S(1)} %get-tuple-element.18), channel_id=1, source_target_pairs={{0,3},{1,2},{2,1},{3,0},{4,7},{5,6},{6,5},{7,4},{8,11},{9,10},{10,... | collective-permute-start | bytes 6152 | tf_op jit(solution)/shard_map/ppermute | solution.py:35

commit v7 on v6

--- a/solution.py
+++ b/solution.py
@@ -48,9 +48,9 @@
 
 
 def pack_kernel(
-    nhelper, helper_ref, r_ref, q_ref, ids_ref, clusters_ref, live_ref, count_ref, r_out, q_out, *scratch
+    nhelper, helper_ref, r_ref, q_ref, ids_ref, clusters_ref, live_ref, count_ref, r_out, *outs
 ):
-    ids, clusters, live, count, sem = scratch
+    q_outs, (ids, clusters, live, count, sem) = outs[:-5], outs[-5:]
     chunks = ids_ref.shape[0] // nhelper
     qblocks = clusters_ref.shape[0]
     small = [
@@ -59,10 +59,15 @@
         pltpu.make_async_copy(live_ref, live, sem.at[2]),
         pltpu.make_async_copy(count_ref, count, sem.at[3]),
     ]
-    large = [pltpu.make_async_copy(q_ref, q_out.at[pl.ds(0, qblocks * LANES)], sem.at[4])]
+    large, height = [], qblocks * LANES // len(q_outs)
+    for p, q_out in enumerate(q_outs):
+        source = q_ref.at[pl.ds(p * height, height)]
+        large.append(
+            pltpu.make_async_copy(source, q_out.at[pl.ds(0, height)], sem.at[4 + chunks + p])
+        )
     for c in range(chunks):
         rows = rows_of(helper_ref[0] + nhelper * c)
-        large.append(pltpu.make_async_copy(r_ref.at[rows], r_out.at[rows_of(c)], sem.at[5 + c]))
+        large.append(pltpu.make_async_copy(r_ref.at[rows], r_out.at[rows_of(c)], sem.at[4 + c]))
     for copy in small + large:
         copy.start()
     for copy in small:
@@ -79,19 +84,19 @@
     table = jnp.where(lane == qblocks, count[0], 0)
     for k in range(qblocks):
         table = jnp.where(lane == k, clusters[k], table)
-    q_out[pl.ds(qblocks * LANES, TABLE), columns] = table.astype(jnp.float32).astype(jnp.bfloat16)
+    q_outs[0][pl.ds(height, TABLE), columns] = table.astype(jnp.float32).astype(jnp.bfloat16)
     for copy in large:
         copy.wait()
 
 
-def score_kernel(chunks, qblocks, first, wide, beta_ref, *refs):
+def score_kernel(chunks, qblocks, parts, first, wide, beta_ref, *refs):
     if first:
-        q_refs, r_refs, refs = list(refs[:4]), list(refs[4:-11]), refs[-11:]
-        out_ref, qv, info_out, q_list, ids_ref, other_ref, info, q_own, r_own, sem, info_sem = refs
-        fetch = (
-            pltpu.make_async_copy(r_refs[0], r_own, sem.at[0]),
-            pltpu.make_async_copy(q_refs[0], q_own, sem.at[1]),
-        )
+        q_refs = [list(refs[i : i + parts]) for i in range(0, 4 * parts, parts)]
+        r_refs, refs = list(refs[4 * parts : -10 - parts]), refs[-10 - parts :]
+        out_ref, qv, info_out, q_list, ids_ref, other_ref, info, sem, info_sem, r_own, *q_own = refs
+        fetch = [pltpu.make_async_copy(r_refs[0], r_own, sem.at[parts])]
+        for p in range(parts):
+            fetch.append(pltpu.make_async_copy(q_refs[0][p], q_own[p], sem.at[p]))
         q_refs[0], r_refs[0] = q_own, r_own
     else:
         info, qv, prev_ref, *r_refs, out_ref, q_list, ids_ref, other_ref = refs
@@ -109,14 +114,15 @@
             ids_ref[rows, :] = ids
             other_ref[rows, :] = jnp.where(ids < 0.0, DEAD, -4.0)
 
-    for s in range(len(fetch) // 2, len(r_refs)):
+    for s in range(1 if first else 0, len(r_refs)):
         spread(s)
     for copy in fetch:
         copy.wait()
     if first:
         spread(0)
         for s, q_ref in enumerate(q_refs):
-            table = q_ref[pl.ds(qblocks * LANES, TABLE), pl.ds(0, LANES)].astype(jnp.float32)
+            behind = pl.ds(qblocks * LANES // parts, TABLE)
+            table = q_ref[0][behind, pl.ds(0, LANES)].astype(jnp.float32)
             info_out[s : s + 1, :] = table[0:1, :].astype(jnp.int32)
         copy = pltpu.make_async_copy(info_out, info, info_sem)
         copy.start()
@@ -127,25 +133,32 @@
         blocks = info[source, qblocks]
 
         def one_block(block, carry, source=source, q_count=q_count):
-            if first:
-                qv[rows_of(q_count + block), :] = q_refs[source][rows_of(block), :]
             q_list[q_count + block, 0] = source * qblocks + block
             q_list[q_count + block, 1] = info[source, block]
             return carry
 
         lax.fori_loop(0, blocks, one_block, 0)
+        each = qblocks // parts
+        for p in range(parts if first else 0):
+
+            def move(block, carry, source=source, q_count=q_count, p=p):
+                place = rows_of(q_count + p * each + block)
+                qv[place, :] = q_refs[source][p][rows_of(block), :]
+                return carry
+
+            lax.fori_loop(0, jnp.clip(blocks - p * each, 0, each), move, 0)
         q_count = q_count + blocks
 
     factor = LOG2E / math.sqrt(width)
     out_ref[...] = jnp.zeros_like(out_ref) if first else prev_ref[...]
 
     def query_blocks(group, carry):
-        parts = []
+        sides = []
         for side in range(wide):
             entry = jnp.minimum(wide * group + side, q_count - 1)
             slot, cluster = q_list[entry, 0], q_list[entry, 1]
             beta = beta_ref[cluster]
-            parts.append(
+            sides.append(
                 (slot, cluster.astype(jnp.float32), beta * factor, beta * beta * (0.5 * LOG2E))
             )
         accs = [jnp.zeros((8, LANES), jnp.float32) for _ in range(wide)]
@@ -161,7 +174,7 @@
                 )
                 for half in range(2):
                     side = 2 * pair + half
-                    _, cluster, scale, offset = parts[side]
+                    _, cluster, scale, offset = sides[side]
                     part = score[:, half * LANES : (half + 1) * LANES]
                     weight = jnp.where(ids_ref[rows, :] == cluster, 0.0, other_ref[rows, :])
                     value = jnp.exp2((part * scale - offset) + weight)
@@ -171,7 +184,7 @@
 
             @pl.when(wide * group + side < q_count)
             def _(side=side, total=total):
-                row = pl.ds(parts[side][0], 1)
+                row = pl.ds(sides[side][0], 1)
                 out_ref[row, :] = out_ref[row, :] + total
 
         return carry
@@ -179,7 +192,7 @@
     lax.fori_loop(0, (q_count + wide - 1) // wide, query_blocks, 0)
 
 
-def score_call(chunks, qblocks, wide, beta, given, payloads, first):
+def score_call(chunks, qblocks, parts, wide, beta, given, payloads, first):
     width = payloads[0].shape[1]
     slots = 4 * qblocks
     height = chunks * LANES
@@ -190,26 +203,25 @@
     scratch = [pltpu.SMEM((slots, 2), jnp.int32), spread, spread]
     specs = [VMEM] * (len(given) + len(payloads))
     if first:
-        specs[0] = specs[len(given)] = ANY
+        for i in (*range(parts), len(given)):
+            specs[i] = ANY
         scratch += [
             pltpu.SMEM((8, LANES), jnp.int32),
-            pltpu.VMEM(given[0].shape, jnp.bfloat16),
+            pltpu.SemaphoreType.DMA((parts + 1,)),
+            pltpu.SemaphoreType.DMA,
             pltpu.VMEM(payloads[0].shape, jnp.bfloat16),
-            pltpu.SemaphoreType.DMA((2,)),
-            pltpu.SemaphoreType.DMA,
+            *[pltpu.VMEM(q.shape, jnp.bfloat16) for q in given[:parts]],
         ]
     else:
         specs[0] = SMEM
     return pl.pallas_call(
-        functools.partial(score_kernel, chunks, qblocks, first, wide),
+        functools.partial(score_kernel, chunks, qblocks, parts, first, wide),
         out_shape=(totals_shape, packed_shape, info_shape) if first else totals_shape,
         in_specs=[SMEM] + specs,
         out_specs=(VMEM, VMEM, VMEM) if first else VMEM,
         scratch_shapes=scratch,
         compiler_params=PARAMS,
-        cost_estimate=cost(
-            2 * slots * LANES * len(payloads) * height * width, 2 * slots * LANES * width
-        ),
+        cost_estimate=cost(1, 1),
     )(beta, *given, *payloads)
 
 
@@ -231,20 +243,23 @@
     chunks = tiles // nhelper
     sources = nblk // 2
 
-    own, q_own = pl.pallas_call(
+    parts = 2
+    q_height = queries.shape[0] // parts
+    own, *q_own = pl.pallas_call(
         functools.partial(pack_kernel, nhelper),
-        out_shape=(
-            jax.ShapeDtypeStruct((chunks * LANES + TABLE, width), jnp.bfloat16),
-            jax.ShapeDtypeStruct((queries.shape[0] + TABLE, width), jnp.bfloat16),
-        ),
+        out_shape=[jax.ShapeDtypeStruct((chunks * LANES + TABLE, width), jnp.bfloat16)]
+        + [
+            jax.ShapeDtypeStruct((q_height + (TABLE if p == 0 else 0), width), jnp.bfloat16)
+            for p in range(parts)
+        ],
         in_specs=[SMEM] + [ANY] * 6,
-        out_specs=(VMEM, VMEM),
+        out_specs=[VMEM] * (1 + parts),
         scratch_shapes=[
             pltpu.VMEM((tiles, LANES), jnp.int32),
             pltpu.SMEM((qblocks,), jnp.int32),
             pltpu.SMEM((1,), jnp.int32),
             pltpu.SMEM((1,), jnp.int32),
-            pltpu.SemaphoreType.DMA((5 + chunks,)),
+            pltpu.SemaphoreType.DMA((4 + chunks + parts,)),
         ],
         compiler_params=WHOLE,
         cost_estimate=cost(1, 4 * rows * width),
@@ -257,8 +272,8 @@
         ref_rows,
         block_count,
     )
-    q_partner = swap(q_own, "blk")
-    q_helper = swap(q_own, "helper")
+    q_partner = [swap(q, "blk") for q in q_own]
+    q_helper = [swap(q, "helper") for q in q_own]
 
     above, below = [own], [own]
     for step in range(1, sources // 2 + 1):
@@ -266,13 +281,15 @@
         if step < (sources + 1) // 2:
             below.append(turn(below[-1], -2))
     early = [own] + above[1:-1] + below[1:]
-    q_both = swap(after(q_partner, above[-2], below[-1]), "helper")
+    q_both = [swap(after(q, above[-2]), "helper") for q in q_partner[:-1]]
+    q_both.append(swap(after(q_partner[-1], below[-1]), "helper"))
+    all_queries = (*q_own, *q_helper, *q_partner, *q_both)
 
     totals, packed, info = score_call(
-        chunks, qblocks, 2, cluster_beta, (q_own, q_helper, q_partner, q_both), early, True
+        chunks, qblocks, parts, 2, cluster_beta, all_queries, early, True
     )
     totals = score_call(
-        chunks, qblocks, 4, cluster_beta, (info, packed, totals), above[-1:], False
+        chunks, qblocks, parts, 4, cluster_beta, (info, packed, totals), above[-1:], False
     )
     totals = totals.reshape(4, qblocks, LANES)
     total = totals[0] + swap(totals[1], "helper") + swap(totals[2], "blk") + swap_both(totals[3])

time: 49.2 us -> 46 us (0.935)
  waiting for transfers between devices: 23.4 us -> 20.2 us
  Pallas kernels: 10.9 us -> 8.55 us
  starting transfers between devices: 9.93 us -> 11 us
  local copies, waits for them, and re-layouts: 2.82 us -> 3.67 us
    ppermute x3, waiting for transfers between devices: 20.6 us -> 10.9 us  [turn(): lax.ppermute(value, 'blk', [(i, (i + by) % length) for i in range(length)])]
    ppermute x5 -> x8, waiting for transfers between devices: 2.77 us -> 8.38 us  [swap(): return lax.ppermute(value, axis, [(i, i ^ 1) for i in range(length)])]
    pallas_call x3, Pallas kernels: 10.9 us -> 8.55 us  [the longest x2 6.21 us: score_call(): pl.pallas_call(functools.partial(score_kernel, chunks, qblocks, parts, fi...]
    ppermute x3, starting transfers between devices: 4.96 us -> 6.9 us  [turn(): lax.ppermute(value, 'blk', [(i, (i + by) % length) for i in range(length)])]
    ppermute x1, starting transfers between devices: 1.29 us -> 0.01 us  [swap_both(): return lax.ppermute(value, ('blk', 'helper'), pairs)]
    ppermute x1, waiting for transfers between devices: 0.01 us -> 0.94 us  [swap_both(): return lax.ppermute(value, ('blk', 'helper'), pairs)]
    unnamed x10 -> x12, local copies, waits for them, and re-layouts: 2.81 us -> 3.67 us
    ppermute x5 -> x8, starting transfers between devices: 3.68 us -> 4.1 us  [swap(): return lax.ppermute(value, axis, [(i, i ^ 1) for i in range(length)])]
  transfers between devices with their start and end apart: 9 -> 12, of which waited for: 5 -> 8; matrix products, arithmetic and copies ran while one was open for 0% -> 0% of each run, Pallas kernels for 12% -> 10%
where the time goes in v7:
time: 46 us; the launch traced here: 45.6 us
  waiting for transfers between devices  20.2 us (44%)
  starting transfers between devices  11 us (24%)
  Pallas kernels  8.55 us (19%)
  local copies, waits for them, and re-layouts  3.67 us (8%)
  between operations  1.35 us (3%)
  other arithmetic  0.85 us (2%)
    ppermute x3, waiting for transfers between devices, turn(): lax.ppermute(value, 'blk', [(i, (i + by) % length) for i in range(length)])  10.9 us
    ppermute x8, waiting for transfers between devices, swap(): return lax.ppermute(value, axis, [(i, i ^ 1) for i in range(length)])  8.38 us
    ppermute x3, starting transfers between devices, turn(): lax.ppermute(value, 'blk', [(i, (i + by) % length) for i in range(length)])  6.9 us
    pallas_call x2, Pallas kernels, score_call(): pl.pallas_call(functools.partial(score_kernel, chunks, qblocks, parts, fi...  6.21 us
    ppermute x8, starting transfers between devices, swap(): return lax.ppermute(value, axis, [(i, i ^ 1) for i in range(length)])  4.1 us
    unnamed x12, local copies, waits for them, and re-layouts  3.67 us
    pallas_call x1, Pallas kernels, per_device(): pl.pallas_call(functools.partial(pack_kernel, nhelper), out_shape=[jax.Sh...  2.34 us
    ppermute x1, waiting for transfers between devices, swap_both(): return lax.ppermute(value, ('blk', 'helper'), pairs)  0.94 us
  transfers between devices with their start and end apart: 12, of which 8 were waited for; matrix products, arithmetic and copies ran while one was open for 0% of the time, Pallas kernels for 10%

profile of v7, /device:TPU:0, one launch (start us, length us, event | category | flops | bytes accessed | tf_op | source)
XLA Modules:
  0.0 45.6 jit_solution(14990922466420361519)
XLA Ops:
  1.3 2.3 %shard_map.82 = (bf16[272,768]{1,0:T(8,128)(2,1)}, bf16[272,768]{1,0:T(8,128)(2,1)}, bf16[256,768]{1,0:T(8,128)(2,1)}) custom-call(s32[1]{0:T(128)} %bitcast.helper_ref, bf16[512,768]{1,0:T(8,128)(2,1)} %r_ref.1, bf16[512,768]{1,0:T(8,128)(2,1)} %q_ref.1, s32[4,128]{1,0:T(4,128)} %bitcast.4, s32[4]{0:T(128)} %clusters_ref.1, s32[1]{0:T(128)S(6)} %copy.10.live_ref, ...), custom_call_target="tpu_custom_call" | custom-call | flops 1 | bytes 1572864 | tf_op jit(solution)/shard_map/pallas_call | solution.py:248
  3.6 3.1 %collective-permute-start.4 = (bf16[272,768]{1,0:T(8,128)(2,1)}, bf16[272,768]{1,0:T(8,128)(2,1)S(1)}, u32[]{:S(2)}, u32[]{:S(2)}) collective-permute-start(bf16[272,768]{1,0:T(8,128)(2,1)} %get-tuple-element.15.refs_8_), channel_id=1, source_target_pairs={{0,4},{2,6},{4,8},{6,10},{8,12},{10,14},{12,0},{14,2},{1,5},{3,7},... | collective-permute-start | bytes 1253384 | tf_op jit(solution)/shard_map/ppermute | solution.py:24
  6.7 1.5 %collective-permute-start.2 = (bf16[272,768]{1,0:T(8,128)(2,1)}, bf16[272,768]{1,0:T(8,128)(2,1)S(1)}, u32[]{:S(2)}, u32[]{:S(2)}) collective-permute-start(bf16[272,768]{1,0:T(8,128)(2,1)} %get-tuple-element.13.refs_0_), channel_id=1, source_target_pairs={{0,2},{2,0},{4,6},{6,4},{8,10},{10,8},{12,14},{14,12},{1,3},{3,1},... | collective-permute-start | bytes 1253384 | tf_op jit(solution)/shard_map/ppermute | solution.py:29
  8.2 2.2 %collective-permute-start.6 = (bf16[272,768]{1,0:T(8,128)(2,1)}, bf16[272,768]{1,0:T(8,128)(2,1)S(1)}, u32[]{:S(2)}, u32[]{:S(2)}) collective-permute-start(bf16[272,768]{1,0:T(8,128)(2,1)} %get-tuple-element.15.refs_8_), channel_id=1, source_target_pairs={{0,12},{2,14},{4,0},{6,2},{8,4},{10,6},{12,8},{14,10},{1,13},{3,15... | collective-permute-start | bytes 1253384 | tf_op jit(solution)/shard_map/ppermute | solution.py:24
  10.5 0.4 collective-permute-start.3
  10.9 8.6 %collective-permute-done.4.refs_9_ = bf16[272,768]{1,0:T(8,128)(2,1)S(1)} collective-permute-done((bf16[272,768]{1,0:T(8,128)(2,1)}, bf16[272,768]{1,0:T(8,128)(2,1)S(1)}, u32[]{:S(2)}, u32[]{:S(2)}) %collective-permute-start.4) | collective-permute-done | bytes 417824 | tf_op jit(solution)/shard_map/ppermute | solution.py:24
  19.5 1.6 %collective-permute-start.8 = (bf16[272,768]{1,0:T(8,128)(2,1)S(1)}, bf16[272,768]{1,0:T(8,128)(2,1)S(1)}, u32[]{:S(2)}, u32[]{:S(2)}) collective-permute-start(bf16[272,768]{1,0:T(8,128)(2,1)S(1)} %collective-permute-done.4.refs_9_), channel_id=1, source_target_pairs={{0,4},{2,6},{4,8},{6,10},{8,12},{10,14},{12,0},{14,2},{1,5},{3,7},... | collective-permute-start | bytes 1253384 | tf_op jit(solution)/shard_map/ppermute | solution.py:24
  21.1 5.4 %collective-permute-done.3.refs_5_ = bf16[256,768]{1,0:T(8,128)(2,1)S(1)} collective-permute-done((bf16[256,768]{1,0:T(8,128)(2,1)}, bf16[256,768]{1,0:T(8,128)(2,1)S(1)}, u32[]{:S(2)}, u32[]{:S(2)}) %collective-permute-start.3) | collective-permute-done | bytes 393248 | tf_op jit(solution)/shard_map/ppermute | solution.py:29
  26.5 1.1 %collective-permute-done.6.refs_10_ = bf16[272,768]{1,0:T(8,128)(2,1)S(1)} collective-permute-done((bf16[272,768]{1,0:T(8,128)(2,1)}, bf16[272,768]{1,0:T(8,128)(2,1)S(1)}, u32[]{:S(2)}, u32[]{:S(2)}) %collective-permute-start.6) | collective-permute-done | bytes 417824 | tf_op jit(solution)/shard_map/ppermute | solution.py:24
  27.6 0.8 %collective-permute-done.1.refs_3_ = bf16[256,768]{1,0:T(8,128)(2,1)S(1)} collective-permute-done((bf16[256,768]{1,0:T(8,128)(2,1)}, bf16[256,768]{1,0:T(8,128)(2,1)S(1)}, u32[]{:S(2)}, u32[]{:S(2)}) %collective-permute-start.1) | collective-permute-done | bytes 393248 | tf_op jit(solution)/shard_map/ppermute | solution.py:29
  28.4 0.9 %collective-permute-done.7.refs_7_ = bf16[256,768]{1,0:T(8,128)(2,1)S(1)} collective-permute-done((bf16[256,768]{1,0:T(8,128)(2,1)S(1)}, bf16[256,768]{1,0:T(8,128)(2,1)S(1)}, u32[]{:S(2)}, u32[]{:S(2)}) %collective-permute-start.7) | collective-permute-done | bytes 393248 | tf_op jit(solution)/shard_map/ppermute | solution.py:29
  29.3 1.0 %copy-done = bf16[272,768]{1,0:T(8,128)(2,1)S(1)} copy-done((bf16[272,768]{1,0:T(8,128)(2,1)S(1)}, bf16[272,768]{1,0:T(8,128)(2,1)}, u32[]{:S(2)}) %copy-start) | copy-done | bytes 417816
  30.3 1.0 %copy-done.1 = bf16[272,768]{1,0:T(8,128)(2,1)S(1)} copy-done((bf16[272,768]{1,0:T(8,128)(2,1)S(1)}, bf16[272,768]{1,0:T(8,128)(2,1)}, u32[]{:S(2)}) %copy-start.1) | copy-done | bytes 417816
  31.3 1.0 %copy-done.2 = bf16[256,768]{1,0:T(8,128)(2,1)S(1)} copy-done((bf16[256,768]{1,0:T(8,128)(2,1)S(1)}, bf16[256,768]{1,0:T(8,128)(2,1)}, u32[]{:S(2)}) %copy-start.2) | copy-done | bytes 393240
  32.3 0.7 %copy-done.3 = f32[64]{0:T(128)S(1)} copy-done((f32[64]{0:T(128)S(1)}, f32[64]{0:T(128)}, u32[]{:S(2)}) %copy-start.3) | copy-done | bytes 280
  32.9 4.5 %shard_map.83 = (f32[16,128]{1,0:T(8,128)S(1)}, bf16[2048,768]{1,0:T(8,128)(2,1)S(1)}, s32[8,128]{1,0:T(8,128)S(1)}) custom-call(f32[64]{0:T(128)S(1)} %copy-done.3, bf16[272,768]{1,0:T(8,128)(2,1)S(1)} %copy-done.1, bf16[256,768]{1,0:T(8,128)(2,1)S(1)} %copy-done.2, bf16[272,768]{1,0:T(8,128)(2,1)S(1)} %collective-permute-done.refs_2_, ...), custom_call_target="tpu_custom_call" | custom-call | flops 1 | bytes 1 | tf_op jit(solution)/shard_map/pallas_call | solution.py:217
  37.4 1.2 %collective-permute-done.8.refs_3_ = bf16[272,768]{1,0:T(8,128)(2,1)S(1)} collective-permute-done((bf16[272,768]{1,0:T(8,128)(2,1)S(1)}, bf16[272,768]{1,0:T(8,128)(2,1)S(1)}, u32[]{:S(2)}, u32[]{:S(2)}) %collective-permute-start.8) | collective-permute-done | bytes 417824 | tf_op jit(solution)/shard_map/ppermute | solution.py:24
  38.6 1.7 %shard_map.84 = f32[16,128]{1,0:T(8,128)S(1)} custom-call(f32[64]{0:T(128)S(1)} %copy-done.3, s32[8,128]{1,0:T(8,128)S(1)} %get-tuple-element.18.refs_0_, bf16[2048,768]{1,0:T(8,128)(2,1)S(1)} %get-tuple-element.19.refs_1_, f32[16,128]{1,0:T(8,128)S(1)} %get-tuple-element.20.refs_2_, bf16[272,768]{1,0:T(8,128)(2,1)S(1)} %collective-permute-done.8.refs_3_), custom_call_target="tpu_custom_call" | custom-call | flops 1 | bytes 1 | tf_op jit(solution)/shard_map/pallas_call | solution.py:217
  40.4 1.6 %collective-permute-start.10 = (f32[4,128]{1,0:T(4,128)S(1)}, f32[4,128]{1,0:T(4,128)S(1)}, u32[]{:S(2)}, u32[]{:S(2)}) collective-permute-start(f32[4,128]{1,0:T(4,128)S(1)} %get-tuple-element.23), channel_id=1, source_target_pairs={{0,2},{2,0},{4,6},{6,4},{8,10},{10,8},{12,14},{14,12},{1,3},{3,1},... | collective-permute-start | bytes 6152 | tf_op jit(solution)/shard_map/ppermute | solution.py:29
  42.0 0.6 %collective-permute-start.9 = (f32[4,128]{1,0:T(4,128)S(1)}, f32[4,128]{1,0:T(4,128)S(1)}, u32[]{:S(2)}, u32[]{:S(2)}) collective-permute-start(f32[4,128]{1,0:T(4,128)S(1)} %get-tuple-element.21), channel_id=1, source_target_pairs={{0,1},{1,0},{2,3},{3,2},{4,5},{5,4},{6,7},{7,6},{8,9},{9,8},{10,11... | collective-permute-start | bytes 6152 | tf_op jit(solution)/shard_map/ppermute | solution.py:29
  42.6 0.2 select_reduce_fusion
  42.8 1.2 %collective-permute-done.10 = f32[4,128]{1,0:T(4,128)S(1)} collective-permute-done((f32[4,128]{1,0:T(4,128)S(1)}, f32[4,128]{1,0:T(4,128)S(1)}, u32[]{:S(2)}, u32[]{:S(2)}) %collective-permute-start.10) | collective-permute-done | bytes 2080 | tf_op jit(solution)/shard_map/ppermute | solution.py:29
  44.0 0.9 %collective-permute-done.11 = f32[4,128]{1,0:T(4,128)S(1)} collective-permute-done((f32[4,128]{1,0:T(4,128)S(1)}, f32[4,128]{1,0:T(4,128)S(1)}, u32[]{:S(2)}, u32[]{:S(2)}) %collective-permute-start.11) | collective-permute-done | bytes 2080 | tf_op jit(solution)/shard_map/ppermute | solution.py:35
  45.0 0.7 %log-plus-one_bitcast_fusion = f32[512]{0:T(512)} fusion(f32[4,128]{1,0:T(4,128)S(1)} %collective-permute-done.11, f32[4,128]{1,0:T(4,128)S(1)} %collective-permute-done.10, f32[4,128]{1,0:T(4,128)S(1)} %collective-permute-done.9, f32[16,128]{1,0:T(8,128)S(1)} %shard_map.84, f32[4]{0:T(128)S(1)} %convert_element_type.7), kind=kLoop, calls=%fused_computation.4 | loop fusion | flops 2048 | bytes 10256 | tf_op jit(solution)/shard_map/reshape | solution.py:300
  (19 shorter events, 0.1 us)
Async XLA Ops:
  3.6 15.8 %collective-permute-start.4 = (bf16[272,768]{1,0:T(8,128)(2,1)}, bf16[272,768]{1,0:T(8,128)(2,1)S(1)}, u32[]{:S(2)}, u32[]{:S(2)}) collective-permute-start(bf16[272,768]{1,0:T(8,128)(2,1)} %get-tuple-element.15.refs_8_), channel_id=1, source_target_pairs={{0,4},{2,6},{4,8},{6,10},{8,12},{10,14},{12,0},{14,2},{1,5},{3,7},... | collective-permute-start | bytes 1253384 | tf_op jit(solution)/shard_map/ppermute | solution.py:24
  6.7 12.8 %collective-permute-start.2 = (bf16[272,768]{1,0:T(8,128)(2,1)}, bf16[272,768]{1,0:T(8,128)(2,1)S(1)}, u32[]{:S(2)}, u32[]{:S(2)}) collective-permute-start(bf16[272,768]{1,0:T(8,128)(2,1)} %get-tuple-element.13.refs_0_), channel_id=1, source_target_pairs={{0,2},{2,0},{4,6},{6,4},{8,10},{10,8},{12,14},{14,12},{1,3},{3,1},... | collective-permute-start | bytes 1253384 | tf_op jit(solution)/shard_map/ppermute | solution.py:29
  8.2 19.3 %collective-permute-start.6 = (bf16[272,768]{1,0:T(8,128)(2,1)}, bf16[272,768]{1,0:T(8,128)(2,1)S(1)}, u32[]{:S(2)}, u32[]{:S(2)}) collective-permute-start(bf16[272,768]{1,0:T(8,128)(2,1)} %get-tuple-element.15.refs_8_), channel_id=1, source_target_pairs={{0,12},{2,14},{4,0},{6,2},{8,4},{10,6},{12,8},{14,10},{1,13},{3,15... | collective-permute-start | bytes 1253384 | tf_op jit(solution)/shard_map/ppermute | solution.py:24
  10.5 32.1 %copy-start.4 = (s32[4]{0:T(128)S(1)}, s32[4]{0:T(128)}, u32[]{:S(2)}) copy-start(s32[4]{0:T(128)} %clusters_ref.1) | copy-start | bytes 52
  10.5 32.1 %copy-start.5 = (s32[64]{0:T(128)S(1)}, s32[64]{0:T(128)}, u32[]{:S(2)}) copy-start(s32[64]{0:T(128)} %param.15) | copy-start | bytes 772
  10.5 16.0 %collective-permute-start.3 = (bf16[256,768]{1,0:T(8,128)(2,1)}, bf16[256,768]{1,0:T(8,128)(2,1)S(1)}, u32[]{:S(2)}, u32[]{:S(2)}) collective-permute-start(bf16[256,768]{1,0:T(8,128)(2,1)} %get-tuple-element.14.refs_1_), channel_id=1, source_target_pairs={{0,2},{2,0},{4,6},{6,4},{8,10},{10,8},{12,14},{14,12},{1,3},{3,1},... | collective-permute-start | bytes 1179656 | tf_op jit(solution)/shard_map/ppermute | solution.py:29
  10.9 17.5 %collective-permute-start = (bf16[272,768]{1,0:T(8,128)(2,1)}, bf16[272,768]{1,0:T(8,128)(2,1)S(1)}, u32[]{:S(2)}, u32[]{:S(2)}) collective-permute-start(bf16[272,768]{1,0:T(8,128)(2,1)} %get-tuple-element.13.refs_0_), channel_id=1, source_target_pairs={{0,1},{1,0},{2,3},{3,2},{4,5},{5,4},{6,7},{7,6},{8,9},{9,8},{10,11... | collective-permute-start | bytes 1253384 | tf_op jit(solution)/shard_map/ppermute | solution.py:29
  19.5 9.8 %collective-permute-start.5 = (bf16[272,768]{1,0:T(8,128)(2,1)S(1)}, bf16[272,768]{1,0:T(8,128)(2,1)S(1)}, u32[]{:S(2)}, u32[]{:S(2)}) collective-permute-start(bf16[272,768]{1,0:T(8,128)(2,1)S(1)} %collective-permute-done.2.refs_4_), channel_id=1, source_target_pairs={{0,1},{1,0},{2,3},{3,2},{4,5},{5,4},{6,7},{7,6},{8,9},{9,8},{10,11... | collective-permute-start | bytes 1253384 | tf_op jit(solution)/shard_map/ppermute | solution.py:29
  19.5 19.1 %collective-permute-start.8 = (bf16[272,768]{1,0:T(8,128)(2,1)S(1)}, bf16[272,768]{1,0:T(8,128)(2,1)S(1)}, u32[]{:S(2)}, u32[]{:S(2)}) collective-permute-start(bf16[272,768]{1,0:T(8,128)(2,1)S(1)} %collective-permute-done.4.refs_9_), channel_id=1, source_target_pairs={{0,4},{2,6},{4,8},{6,10},{8,12},{10,14},{12,0},{14,2},{1,5},{3,7},... | collective-permute-start | bytes 1253384 | tf_op jit(solution)/shard_map/ppermute | solution.py:24
  26.5 1.9 %collective-permute-start.1 = (bf16[256,768]{1,0:T(8,128)(2,1)}, bf16[256,768]{1,0:T(8,128)(2,1)S(1)}, u32[]{:S(2)}, u32[]{:S(2)}) collective-permute-start(bf16[256,768]{1,0:T(8,128)(2,1)} %get-tuple-element.14.refs_1_), channel_id=1, source_target_pairs={{0,1},{1,0},{2,3},{3,2},{4,5},{5,4},{6,7},{7,6},{8,9},{9,8},{10,11... | collective-permute-start | bytes 1179656 | tf_op jit(solution)/shard_map/ppermute | solution.py:29
  27.5 1.7 %collective-permute-start.7 = (bf16[256,768]{1,0:T(8,128)(2,1)S(1)}, bf16[256,768]{1,0:T(8,128)(2,1)S(1)}, u32[]{:S(2)}, u32[]{:S(2)}) collective-permute-start(bf16[256,768]{1,0:T(8,128)(2,1)S(1)} %collective-permute-done.3.refs_5_), channel_id=1, source_target_pairs={{0,1},{1,0},{2,3},{3,2},{4,5},{5,4},{6,7},{7,6},{8,9},{9,8},{10,11... | collective-permute-start | bytes 1179656 | tf_op jit(solution)/shard_map/ppermute | solution.py:29
  29.3 1.0 %copy-start = (bf16[272,768]{1,0:T(8,128)(2,1)S(1)}, bf16[272,768]{1,0:T(8,128)(2,1)}, u32[]{:S(2)}) copy-start(bf16[272,768]{1,0:T(8,128)(2,1)} %get-tuple-element.15.refs_8_) | copy-start | bytes 1253380
  30.3 1.0 %copy-start.1 = (bf16[272,768]{1,0:T(8,128)(2,1)S(1)}, bf16[272,768]{1,0:T(8,128)(2,1)}, u32[]{:S(2)}) copy-start(bf16[272,768]{1,0:T(8,128)(2,1)} %get-tuple-element.13.refs_0_) | copy-start | bytes 1253380
  31.3 1.0 %copy-start.2 = (bf16[256,768]{1,0:T(8,128)(2,1)S(1)}, bf16[256,768]{1,0:T(8,128)(2,1)}, u32[]{:S(2)}) copy-start(bf16[256,768]{1,0:T(8,128)(2,1)} %get-tuple-element.14.refs_1_) | copy-start | bytes 1179652
  32.3 0.7 %copy-start.3 = (f32[64]{0:T(128)S(1)}, f32[64]{0:T(128)}, u32[]{:S(2)}) copy-start(f32[64]{0:T(128)} %beta_ref.3) | copy-start | bytes 772
  40.4 3.7 %collective-permute-start.10 = (f32[4,128]{1,0:T(4,128)S(1)}, f32[4,128]{1,0:T(4,128)S(1)}, u32[]{:S(2)}, u32[]{:S(2)}) collective-permute-start(f32[4,128]{1,0:T(4,128)S(1)} %get-tuple-element.23), channel_id=1, source_target_pairs={{0,2},{2,0},{4,6},{6,4},{8,10},{10,8},{12,14},{14,12},{1,3},{3,1},... | collective-permute-start | bytes 6152 | tf_op jit(solution)/shard_map/ppermute | solution.py:29
  42.0 3.0 %collective-permute-start.11 = (f32[4,128]{1,0:T(4,128)S(1)}, f32[4,128]{1,0:T(4,128)S(1)}, u32[]{:S(2)}, u32[]{:S(2)}) collective-permute-start(f32[4,128]{1,0:T(4,128)S(1)} %get-tuple-element.22), channel_id=1, source_target_pairs={{0,3},{1,2},{2,1},{3,0},{4,7},{5,6},{6,5},{7,4},{8,11},{9,10},{10,... | collective-permute-start | bytes 6152 | tf_op jit(solution)/shard_map/ppermute | solution.py:35
  42.0 3.0 %collective-permute-start.9 = (f32[4,128]{1,0:T(4,128)S(1)}, f32[4,128]{1,0:T(4,128)S(1)}, u32[]{:S(2)}, u32[]{:S(2)}) collective-permute-start(f32[4,128]{1,0:T(4,128)S(1)} %get-tuple-element.21), channel_id=1, source_target_pairs={{0,1},{1,0},{2,3},{3,2},{4,5},{5,4},{6,7},{7,6},{8,9},{9,8},{10,11... | collective-permute-start | bytes 6152 | tf_op jit(solution)/shard_map/ppermute | solution.py:29

commit v8 on v7

--- a/solution.py
+++ b/solution.py
@@ -48,78 +48,71 @@
 
 
 def pack_kernel(
-    nhelper, helper_ref, r_ref, q_ref, ids_ref, clusters_ref, live_ref, count_ref, r_out, *outs
+    nhelper, helper_ref, r_ref, q_ref, ids_ref, clusters_ref, live_ref, count_ref, r_out, *refs
 ):
-    q_outs, (ids, clusters, live, count, sem) = outs[:-5], outs[-5:]
+    q_outs, (ids, clusters, live, count, r_table, q_table, sem) = refs[:-7], refs[-7:]
     chunks = ids_ref.shape[0] // nhelper
     qblocks = clusters_ref.shape[0]
-    small = [
-        pltpu.make_async_copy(ids_ref, ids, sem.at[0]),
-        pltpu.make_async_copy(clusters_ref, clusters, sem.at[1]),
-        pltpu.make_async_copy(live_ref, live, sem.at[2]),
-        pltpu.make_async_copy(count_ref, count, sem.at[3]),
-    ]
-    large, height = [], qblocks * LANES // len(q_outs)
-    for p, q_out in enumerate(q_outs):
-        source = q_ref.at[pl.ds(p * height, height)]
-        large.append(
-            pltpu.make_async_copy(source, q_out.at[pl.ds(0, height)], sem.at[4 + chunks + p])
-        )
+    pairs = [(ids_ref, ids), (live_ref, live), (clusters_ref, clusters), (count_ref, count)]
     for c in range(chunks):
         rows = rows_of(helper_ref[0] + nhelper * c)
-        large.append(pltpu.make_async_copy(r_ref.at[rows], r_out.at[rows_of(c)], sem.at[4 + c]))
-    for copy in small + large:
+        pairs.append((r_ref.at[rows], r_out.at[rows_of(c)]))
+    start = 0
+    for out in q_outs:
+        height = out.shape[0] // LANES * LANES
+        pairs.append((q_ref.at[pl.ds(start, height)], out.at[pl.ds(0, height)]))
+        start += height
+    pairs.append((r_table, r_out.at[pl.ds(chunks * LANES, TABLE)]))
+    pairs.append((q_table, q_outs[0].at[pl.ds(q_outs[0].shape[0] - TABLE, TABLE)]))
+    copies = [pltpu.make_async_copy(*pair, sem.at[i]) for i, pair in enumerate(pairs)]
+    for copy in copies[:-2]:
         copy.start()
-    for copy in small:
+    for copy in copies[:4]:
         copy.wait()
     lane = lax.broadcasted_iota(jnp.int32, (TABLE, LANES), 1)
     row = lax.broadcasted_iota(jnp.int32, (TABLE, LANES), 0)
-    table = jnp.full((TABLE, LANES), -1, jnp.int32)
+    rows = jnp.full((TABLE, LANES), -1, jnp.int32)
     for c in range(chunks):
         tile = helper_ref[0] + nhelper * c
         here = jnp.where(tile * LANES + lane < live[0], ids[pl.ds(tile, 1), :], -1)
-        table = jnp.where(row == c, here, table)
-    columns = pl.ds(0, LANES)
-    r_out[pl.ds(chunks * LANES, TABLE), columns] = table.astype(jnp.float32).astype(jnp.bfloat16)
-    table = jnp.where(lane == qblocks, count[0], 0)
+        rows = jnp.where(row == c, here, rows)
+    r_table[...] = jnp.zeros_like(r_table)
+    r_table[:, pl.ds(0, LANES)] = rows.astype(jnp.float32).astype(jnp.bfloat16)
+    copies[-2].start()
+    rows = jnp.where(lane == qblocks, count[0], 0)
     for k in range(qblocks):
-        table = jnp.where(lane == k, clusters[k], table)
-    q_outs[0][pl.ds(height, TABLE), columns] = table.astype(jnp.float32).astype(jnp.bfloat16)
-    for copy in large:
+        rows = jnp.where(lane == k, clusters[k], rows)
+    q_table[...] = jnp.zeros_like(q_table)
+    q_table[:, pl.ds(0, LANES)] = rows.astype(jnp.float32).astype(jnp.bfloat16)
+    copies[-1].start()
+    for copy in copies[4:]:
         copy.wait()
+
+
+def stage_kernel(*refs):
+    half = len(refs) // 2
+    for source, out in zip(refs[:half], refs[half:]):
+        out[...] = source[...]
 
 
 def score_kernel(chunks, qblocks, parts, first, wide, beta_ref, *refs):
     if first:
-        q_refs = [list(refs[i : i + parts]) for i in range(0, 4 * parts, parts)]
-        r_refs, refs = list(refs[4 * parts : -10 - parts]), refs[-10 - parts :]
-        out_ref, qv, info_out, q_list, ids_ref, other_ref, info, sem, info_sem, r_own, *q_own = refs
-        fetch = [pltpu.make_async_copy(r_refs[0], r_own, sem.at[parts])]
-        for p in range(parts):
-            fetch.append(pltpu.make_async_copy(q_refs[0][p], q_own[p], sem.at[p]))
-        q_refs[0], r_refs[0] = q_own, r_own
+        q_refs = [refs[i : i + parts] for i in range(0, 4 * parts, parts)]
+        r_refs, refs = refs[4 * parts : -8], refs[-8:]
+        out_ref, qv, info_out, q_list, ids_ref, other_ref, info, info_sem = refs
     else:
         info, qv, prev_ref, *r_refs, out_ref, q_list, ids_ref, other_ref = refs
-        fetch = ()
     width = qv.shape[1]
     height = chunks * LANES
-    for copy in fetch:
-        copy.start()
-
-    def spread(s):
+
+    for s in range(len(r_refs)):
         table = r_refs[s][pl.ds(height, TABLE), pl.ds(0, LANES)].astype(jnp.float32)
         for c in range(chunks):
             ids = jnp.broadcast_to(table[c : c + 1, :], (LANES, LANES)).T
             rows = pl.ds(s * height + c * LANES, LANES)
             ids_ref[rows, :] = ids
             other_ref[rows, :] = jnp.where(ids < 0.0, DEAD, -4.0)
-
-    for s in range(1 if first else 0, len(r_refs)):
-        spread(s)
-    for copy in fetch:
-        copy.wait()
     if first:
-        spread(0)
         for s, q_ref in enumerate(q_refs):
             behind = pl.ds(qblocks * LANES // parts, TABLE)
             table = q_ref[0][behind, pl.ds(0, LANES)].astype(jnp.float32)
@@ -157,7 +150,7 @@
         for side in range(wide):
             entry = jnp.minimum(wide * group + side, q_count - 1)
             slot, cluster = q_list[entry, 0], q_list[entry, 1]
-            beta = beta_ref[cluster]
+            beta = beta_ref[0, cluster]
             sides.append(
                 (slot, cluster.astype(jnp.float32), beta * factor, beta * beta * (0.5 * LOG2E))
             )
@@ -203,15 +196,7 @@
     scratch = [pltpu.SMEM((slots, 2), jnp.int32), spread, spread]
     specs = [VMEM] * (len(given) + len(payloads))
     if first:
-        for i in (*range(parts), len(given)):
-            specs[i] = ANY
-        scratch += [
-            pltpu.SMEM((8, LANES), jnp.int32),
-            pltpu.SemaphoreType.DMA((parts + 1,)),
-            pltpu.SemaphoreType.DMA,
-            pltpu.VMEM(payloads[0].shape, jnp.bfloat16),
-            *[pltpu.VMEM(q.shape, jnp.bfloat16) for q in given[:parts]],
-        ]
+        scratch += [pltpu.SMEM((8, LANES), jnp.int32), pltpu.SemaphoreType.DMA]
     else:
         specs[0] = SMEM
     return pl.pallas_call(
@@ -243,26 +228,28 @@
     chunks = tiles // nhelper
     sources = nblk // 2
 
-    parts = 2
-    q_height = queries.shape[0] // parts
+    split = (qblocks // 2, qblocks - qblocks // 2)
+    parts = len(split)
     own, *q_own = pl.pallas_call(
         functools.partial(pack_kernel, nhelper),
         out_shape=[jax.ShapeDtypeStruct((chunks * LANES + TABLE, width), jnp.bfloat16)]
         + [
-            jax.ShapeDtypeStruct((q_height + (TABLE if p == 0 else 0), width), jnp.bfloat16)
-            for p in range(parts)
+            jax.ShapeDtypeStruct((n * LANES + (TABLE if p == 0 else 0), width), jnp.bfloat16)
+            for p, n in enumerate(split)
         ],
         in_specs=[SMEM] + [ANY] * 6,
-        out_specs=[VMEM] * (1 + parts),
+        out_specs=[ANY] * (1 + parts),
         scratch_shapes=[
             pltpu.VMEM((tiles, LANES), jnp.int32),
             pltpu.SMEM((qblocks,), jnp.int32),
             pltpu.SMEM((1,), jnp.int32),
             pltpu.SMEM((1,), jnp.int32),
-            pltpu.SemaphoreType.DMA((4 + chunks + parts,)),
+            pltpu.VMEM((TABLE, width), jnp.bfloat16),
+            pltpu.VMEM((TABLE, width), jnp.bfloat16),
+            pltpu.SemaphoreType.DMA((6 + chunks + parts,)),
         ],
         compiler_params=WHOLE,
-        cost_estimate=cost(1, 4 * rows * width),
+        cost_estimate=cost(1, 1),
     )(
         helper[None],
         references,
@@ -272,24 +259,33 @@
         ref_rows,
         block_count,
     )
+    beta = cluster_beta.reshape(1, -1)
+    staged_own, *staged_q, beta = staged = pl.pallas_call(
+        stage_kernel,
+        out_shape=[jax.ShapeDtypeStruct(x.shape, x.dtype) for x in (own, *q_own, beta)],
+        in_specs=[VMEM] * (2 + parts),
+        out_specs=[VMEM] * (2 + parts),
+        compiler_params=PARAMS,
+        cost_estimate=cost(1, 1),
+    )(own, *q_own, beta)
     q_partner = [swap(q, "blk") for q in q_own]
     q_helper = [swap(q, "helper") for q in q_own]
 
     above, below = [own], [own]
     for step in range(1, sources // 2 + 1):
-        above.append(turn(above[-1], 2))
+        above.append(turn(after(above[-1], *staged) if step > 1 else own, 2))
         if step < (sources + 1) // 2:
             below.append(turn(below[-1], -2))
-    early = [own] + above[1:-1] + below[1:]
+    early = [staged_own] + above[1:-1] + below[1:]
     q_both = [swap(after(q, above[-2]), "helper") for q in q_partner[:-1]]
     q_both.append(swap(after(q_partner[-1], below[-1]), "helper"))
-    all_queries = (*q_own, *q_helper, *q_partner, *q_both)
+    all_queries = (*staged_q, *q_helper, *q_partner, *q_both)
 
     totals, packed, info = score_call(
-        chunks, qblocks, parts, 2, cluster_beta, all_queries, early, True
+        chunks, qblocks, parts, 2, beta, all_queries, early, True
     )
     totals = score_call(
-        chunks, qblocks, parts, 4, cluster_beta, (info, packed, totals), above[-1:], False
+        chunks, qblocks, parts, 4, beta, (info, packed, totals), above[-1:], False
     )
     totals = totals.reshape(4, qblocks, LANES)
     total = totals[0] + swap(totals[1], "helper") + swap(totals[2], "blk") + swap_both(totals[3])

time: 46 us -> 81.1 us (1.76)
  Pallas kernels: 8.55 us -> 44.2 us
  starting transfers between devices: 11 us -> 9.13 us
  waiting for transfers between devices: 20.2 us -> 21.6 us
    pallas_call x1, Pallas kernels: 2.34 us -> 36.9 us  [per_device(): pl.pallas_call(functools.partial(pack_kernel, nhelper), out_shape=[jax.Sh...]
    ppermute x3, starting transfers between devices: 6.9 us -> 3.88 us  [turn(): lax.ppermute(value, 'blk', [(i, (i + by) % length) for i in range(length)])]
    ppermute x8, starting transfers between devices: 4.1 us -> 5.18 us  [swap(): return lax.ppermute(value, axis, [(i, i ^ 1) for i in range(length)])]
    ppermute x3, waiting for transfers between devices: 10.9 us -> 11.9 us  [turn(): lax.ppermute(value, 'blk', [(i, (i + by) % length) for i in range(length)])]
    pallas_call x2, Pallas kernels: 6.21 us -> 7.15 us  [score_call(): pl.pallas_call(functools.partial(score_kernel, chunks, qblocks, parts, fi...]
  transfers between devices with their start and end apart: 12 -> 12, of which waited for: 8 -> 8; matrix products, arithmetic and copies ran while one was open for 0% -> 0% of each run, Pallas kernels for 10% -> 6%
where the time goes in v8:
time: 81.1 us; the launch traced here: 80.8 us
  Pallas kernels  44.2 us (55%)
  waiting for transfers between devices  21.6 us (27%)
  starting transfers between devices  9.13 us (11%)
  local copies, waits for them, and re-layouts  3.67 us (5%)
  between operations  1.37 us (2%)
  other arithmetic  0.85 us (1%)
    pallas_call x1, Pallas kernels, per_device(): pl.pallas_call(functools.partial(pack_kernel, nhelper), out_shape=[jax.Sh...  36.9 us
    ppermute x3, waiting for transfers between devices, turn(): lax.ppermute(value, 'blk', [(i, (i + by) % length) for i in range(length)])  11.9 us
    ppermute x8, waiting for transfers between devices, swap(): return lax.ppermute(value, axis, [(i, i ^ 1) for i in range(length)])  8.78 us
    pallas_call x2, Pallas kernels, score_call(): pl.pallas_call(functools.partial(score_kernel, chunks, qblocks, parts, fi...  7.15 us
    ppermute x8, starting transfers between devices, swap(): return lax.ppermute(value, axis, [(i, i ^ 1) for i in range(length)])  5.18 us
    ppermute x3, starting transfers between devices, turn(): lax.ppermute(value, 'blk', [(i, (i + by) % length) for i in range(length)])  3.88 us
    unnamed x12, local copies, waits for them, and re-layouts  3.67 us
  transfers between devices with their start and end apart: 12, of which 8 were waited for; matrix products, arithmetic and copies ran while one was open for 0% of the time, Pallas kernels for 6%

profile of v8, /device:TPU:0, one launch (start us, length us, event | category | flops | bytes accessed | tf_op | source)
XLA Modules:
  0.0 80.8 jit_solution(2094468869990790684)
XLA Ops:
  1.3 36.9 %shard_map.82 = (bf16[272,768]{1,0:T(8,128)(2,1)}, bf16[272,768]{1,0:T(8,128)(2,1)}, bf16[256,768]{1,0:T(8,128)(2,1)}) custom-call(s32[1]{0:T(128)} %bitcast.helper_ref, bf16[512,768]{1,0:T(8,128)(2,1)} %r_ref.1, bf16[512,768]{1,0:T(8,128)(2,1)} %q_ref.1, s32[4,128]{1,0:T(4,128)} %bitcast.6, s32[4]{0:T(128)} %clusters_ref.1, s32[1]{0:T(128)S(6)} %copy.10.live_ref, ...), custom_call_target="tpu_custom_call" | custom-call | flops 1 | bytes 1 | tf_op jit(solution)/shard_map/pallas_call | solution.py:233
  38.2 3.0 %collective-permute-start.2 = (bf16[272,768]{1,0:T(8,128)(2,1)}, bf16[272,768]{1,0:T(8,128)(2,1)S(1)}, u32[]{:S(2)}, u32[]{:S(2)}) collective-permute-start(bf16[272,768]{1,0:T(8,128)(2,1)} %get-tuple-element.19.refs_1_), channel_id=1, source_target_pairs={{0,2},{2,0},{4,6},{6,4},{8,10},{10,8},{12,14},{14,12},{1,3},{3,1},... | collective-permute-start | bytes 1253384 | tf_op jit(solution)/shard_map/ppermute | solution.py:29
  41.3 1.6 %collective-permute-start.4 = (bf16[272,768]{1,0:T(8,128)(2,1)}, bf16[272,768]{1,0:T(8,128)(2,1)S(1)}, u32[]{:S(2)}, u32[]{:S(2)}) collective-permute-start(bf16[272,768]{1,0:T(8,128)(2,1)} %get-tuple-element.18.refs_0_), channel_id=1, source_target_pairs={{0,4},{2,6},{4,8},{6,10},{8,12},{10,14},{12,0},{14,2},{1,5},{3,7},... | collective-permute-start | bytes 1253384 | tf_op jit(solution)/shard_map/ppermute | solution.py:24
  42.8 2.2 %collective-permute-start.6 = (bf16[272,768]{1,0:T(8,128)(2,1)}, bf16[272,768]{1,0:T(8,128)(2,1)S(1)}, u32[]{:S(2)}, u32[]{:S(2)}) collective-permute-start(bf16[272,768]{1,0:T(8,128)(2,1)} %get-tuple-element.18.refs_0_), channel_id=1, source_target_pairs={{0,12},{2,14},{4,0},{6,2},{8,4},{10,6},{12,8},{14,10},{1,13},{3,15... | collective-permute-start | bytes 1253384 | tf_op jit(solution)/shard_map/ppermute | solution.py:24
  45.1 0.3 collective-permute-start.3
  45.4 1.0 %copy-done = bf16[272,768]{1,0:T(8,128)(2,1)S(1)} copy-done((bf16[272,768]{1,0:T(8,128)(2,1)S(1)}, bf16[272,768]{1,0:T(8,128)(2,1)}, u32[]{:S(2)}) %copy-start) | copy-done | bytes 417816
  46.4 1.0 %copy-done.1 = bf16[272,768]{1,0:T(8,128)(2,1)S(1)} copy-done((bf16[272,768]{1,0:T(8,128)(2,1)S(1)}, bf16[272,768]{1,0:T(8,128)(2,1)}, u32[]{:S(2)}) %copy-start.1) | copy-done | bytes 417816
  47.4 1.0 %copy-done.2 = bf16[256,768]{1,0:T(8,128)(2,1)S(1)} copy-done((bf16[256,768]{1,0:T(8,128)(2,1)S(1)}, bf16[256,768]{1,0:T(8,128)(2,1)}, u32[]{:S(2)}) %copy-start.2) | copy-done | bytes 393240
  48.4 0.7 copy-done.3
  49.0 0.1 shard_map.83
  49.1 2.8 %collective-permute-done.2.refs_4_ = bf16[272,768]{1,0:T(8,128)(2,1)S(1)} collective-permute-done((bf16[272,768]{1,0:T(8,128)(2,1)}, bf16[272,768]{1,0:T(8,128)(2,1)S(1)}, u32[]{:S(2)}, u32[]{:S(2)}) %collective-permute-start.2) | collective-permute-done | bytes 417824 | tf_op jit(solution)/shard_map/ppermute | solution.py:29
  52.0 3.9 %collective-permute-done.4.refs_9_ = bf16[272,768]{1,0:T(8,128)(2,1)S(1)} collective-permute-done((bf16[272,768]{1,0:T(8,128)(2,1)}, bf16[272,768]{1,0:T(8,128)(2,1)S(1)}, u32[]{:S(2)}, u32[]{:S(2)}) %collective-permute-start.4) | collective-permute-done | bytes 417824 | tf_op jit(solution)/shard_map/ppermute | solution.py:24
  56.0 3.6 %collective-permute-done.3.refs_5_ = bf16[256,768]{1,0:T(8,128)(2,1)S(1)} collective-permute-done((bf16[256,768]{1,0:T(8,128)(2,1)}, bf16[256,768]{1,0:T(8,128)(2,1)S(1)}, u32[]{:S(2)}, u32[]{:S(2)}) %collective-permute-start.3) | collective-permute-done | bytes 393248 | tf_op jit(solution)/shard_map/ppermute | solution.py:29
  59.6 3.3 %collective-permute-done.6.refs_10_ = bf16[272,768]{1,0:T(8,128)(2,1)S(1)} collective-permute-done((bf16[272,768]{1,0:T(8,128)(2,1)}, bf16[272,768]{1,0:T(8,128)(2,1)S(1)}, u32[]{:S(2)}, u32[]{:S(2)}) %collective-permute-start.6) | collective-permute-done | bytes 417824 | tf_op jit(solution)/shard_map/ppermute | solution.py:24
  62.8 1.7 %collective-permute-done.7.refs_7_ = bf16[256,768]{1,0:T(8,128)(2,1)S(1)} collective-permute-done((bf16[256,768]{1,0:T(8,128)(2,1)S(1)}, bf16[256,768]{1,0:T(8,128)(2,1)S(1)}, u32[]{:S(2)}, u32[]{:S(2)}) %collective-permute-start.7) | collective-permute-done | bytes 393248 | tf_op jit(solution)/shard_map/ppermute | solution.py:29
  64.6 4.9 %shard_map.84 = (f32[16,128]{1,0:T(8,128)S(1)}, bf16[2048,768]{1,0:T(8,128)(2,1)S(1)}, s32[8,128]{1,0:T(8,128)S(1)}) custom-call(f32[1,64]{1,0:T(1,128)S(1)} %get-tuple-element.21.beta_ref, bf16[272,768]{1,0:T(8,128)(2,1)S(1)} %get-tuple-element.22.refs_0_, bf16[256,768]{1,0:T(8,128)(2,1)S(1)} %get-tuple-element.23.refs_1_, ...), custom_call_target="tpu_custom_call" | custom-call | flops 1 | bytes 1 | tf_op jit(solution)/shard_map/pallas_call | solution.py:202
  69.5 4.6 %collective-permute-done.8.refs_3_ = bf16[272,768]{1,0:T(8,128)(2,1)S(1)} collective-permute-done((bf16[272,768]{1,0:T(8,128)(2,1)S(1)}, bf16[272,768]{1,0:T(8,128)(2,1)S(1)}, u32[]{:S(2)}, u32[]{:S(2)}) %collective-permute-start.8) | collective-permute-done | bytes 417824 | tf_op jit(solution)/shard_map/ppermute | solution.py:24
  74.2 2.2 %shard_map.85 = f32[16,128]{1,0:T(8,128)S(1)} custom-call(f32[1,64]{1,0:T(1,128)S(1)} %get-tuple-element.21.beta_ref, s32[8,128]{1,0:T(8,128)S(1)} %get-tuple-element.27.refs_0_, bf16[2048,768]{1,0:T(8,128)(2,1)S(1)} %get-tuple-element.28.refs_1_, f32[16,128]{1,0:T(8,128)S(1)} %get-tuple-element.29.refs_2_, bf16[272,768]{1,0:T(8,128)(2,1)S(1)} %collective-permute-done.8.refs_3_), custom_call_target="tpu_custom_call" | custom-call | flops 1 | bytes 1 | tf_op jit(solution)/shard_map/pallas_call | solution.py:202
  76.5 1.5 %collective-permute-start.10 = (f32[4,128]{1,0:T(4,128)S(1)}, f32[4,128]{1,0:T(4,128)S(1)}, u32[]{:S(2)}, u32[]{:S(2)}) collective-permute-start(f32[4,128]{1,0:T(4,128)S(1)} %get-tuple-element.33), channel_id=1, source_target_pairs={{0,2},{2,0},{4,6},{6,4},{8,10},{10,8},{12,14},{14,12},{1,3},{3,1},... | collective-permute-start | bytes 6152 | tf_op jit(solution)/shard_map/ppermute | solution.py:29
  78.0 0.4 collective-permute-start.9
  78.3 0.2 select_reduce_fusion
  78.5 1.0 %collective-permute-done.11 = f32[4,128]{1,0:T(4,128)S(1)} collective-permute-done((f32[4,128]{1,0:T(4,128)S(1)}, f32[4,128]{1,0:T(4,128)S(1)}, u32[]{:S(2)}, u32[]{:S(2)}) %collective-permute-start.11) | collective-permute-done | bytes 2080 | tf_op jit(solution)/shard_map/ppermute | solution.py:35
  79.5 0.7 collective-permute-done.10
  80.1 0.7 log-plus-one_bitcast_fusion
  (20 shorter events, 0.2 us)
Async XLA Ops:
  38.2 13.7 %collective-permute-start.2 = (bf16[272,768]{1,0:T(8,128)(2,1)}, bf16[272,768]{1,0:T(8,128)(2,1)S(1)}, u32[]{:S(2)}, u32[]{:S(2)}) collective-permute-start(bf16[272,768]{1,0:T(8,128)(2,1)} %get-tuple-element.19.refs_1_), channel_id=1, source_target_pairs={{0,2},{2,0},{4,6},{6,4},{8,10},{10,8},{12,14},{14,12},{1,3},{3,1},... | collective-permute-start | bytes 1253384 | tf_op jit(solution)/shard_map/ppermute | solution.py:29
  41.3 14.6 %collective-permute-start.4 = (bf16[272,768]{1,0:T(8,128)(2,1)}, bf16[272,768]{1,0:T(8,128)(2,1)S(1)}, u32[]{:S(2)}, u32[]{:S(2)}) collective-permute-start(bf16[272,768]{1,0:T(8,128)(2,1)} %get-tuple-element.18.refs_0_), channel_id=1, source_target_pairs={{0,4},{2,6},{4,8},{6,10},{8,12},{10,14},{12,0},{14,2},{1,5},{3,7},... | collective-permute-start | bytes 1253384 | tf_op jit(solution)/shard_map/ppermute | solution.py:24
  42.8 20.0 %collective-permute-start.6 = (bf16[272,768]{1,0:T(8,128)(2,1)}, bf16[272,768]{1,0:T(8,128)(2,1)S(1)}, u32[]{:S(2)}, u32[]{:S(2)}) collective-permute-start(bf16[272,768]{1,0:T(8,128)(2,1)} %get-tuple-element.18.refs_0_), channel_id=1, source_target_pairs={{0,12},{2,14},{4,0},{6,2},{8,4},{10,6},{12,8},{14,10},{1,13},{3,15... | collective-permute-start | bytes 1253384 | tf_op jit(solution)/shard_map/ppermute | solution.py:24
  45.1 14.5 %collective-permute-start.3 = (bf16[256,768]{1,0:T(8,128)(2,1)}, bf16[256,768]{1,0:T(8,128)(2,1)S(1)}, u32[]{:S(2)}, u32[]{:S(2)}) collective-permute-start(bf16[256,768]{1,0:T(8,128)(2,1)} %get-tuple-element.20.refs_2_), channel_id=1, source_target_pairs={{0,2},{2,0},{4,6},{6,4},{8,10},{10,8},{12,14},{14,12},{1,3},{3,1},... | collective-permute-start | bytes 1179656 | tf_op jit(solution)/shard_map/ppermute | solution.py:29
  45.4 17.5 %collective-permute-start = (bf16[272,768]{1,0:T(8,128)(2,1)}, bf16[272,768]{1,0:T(8,128)(2,1)S(1)}, u32[]{:S(2)}, u32[]{:S(2)}) collective-permute-start(bf16[272,768]{1,0:T(8,128)(2,1)} %get-tuple-element.19.refs_1_), channel_id=1, source_target_pairs={{0,1},{1,0},{2,3},{3,2},{4,5},{5,4},{6,7},{7,6},{8,9},{9,8},{10,11... | collective-permute-start | bytes 1253384 | tf_op jit(solution)/shard_map/ppermute | solution.py:29
  45.4 1.0 %copy-start = (bf16[272,768]{1,0:T(8,128)(2,1)S(1)}, bf16[272,768]{1,0:T(8,128)(2,1)}, u32[]{:S(2)}) copy-start(bf16[272,768]{1,0:T(8,128)(2,1)} %get-tuple-element.19.refs_1_) | copy-start | bytes 1253380
  46.4 1.0 %copy-start.1 = (bf16[272,768]{1,0:T(8,128)(2,1)S(1)}, bf16[272,768]{1,0:T(8,128)(2,1)}, u32[]{:S(2)}) copy-start(bf16[272,768]{1,0:T(8,128)(2,1)} %get-tuple-element.18.refs_0_) | copy-start | bytes 1253380
  47.4 1.0 %copy-start.2 = (bf16[256,768]{1,0:T(8,128)(2,1)S(1)}, bf16[256,768]{1,0:T(8,128)(2,1)}, u32[]{:S(2)}) copy-start(bf16[256,768]{1,0:T(8,128)(2,1)} %get-tuple-element.20.refs_2_) | copy-start | bytes 1179652
  48.4 0.7 copy-start.3
  55.9 8.7 %collective-permute-start.5 = (bf16[272,768]{1,0:T(8,128)(2,1)S(1)}, bf16[272,768]{1,0:T(8,128)(2,1)S(1)}, u32[]{:S(2)}, u32[]{:S(2)}) collective-permute-start(bf16[272,768]{1,0:T(8,128)(2,1)S(1)} %collective-permute-done.2.refs_4_), channel_id=1, source_target_pairs={{0,1},{1,0},{2,3},{3,2},{4,5},{5,4},{6,7},{7,6},{8,9},{9,8},{10,11... | collective-permute-start | bytes 1253384 | tf_op jit(solution)/shard_map/ppermute | solution.py:29
  55.9 22.4 %copy-start.4 = (s32[4]{0:T(128)S(1)}, s32[4]{0:T(128)}, u32[]{:S(2)}) copy-start(s32[4]{0:T(128)} %clusters_ref.1) | copy-start | bytes 52
  55.9 22.4 %copy-start.5 = (s32[64]{0:T(128)S(1)}, s32[64]{0:T(128)}, u32[]{:S(2)}) copy-start(s32[64]{0:T(128)} %param.15) | copy-start | bytes 772
  55.9 18.3 %collective-permute-start.8 = (bf16[272,768]{1,0:T(8,128)(2,1)S(1)}, bf16[272,768]{1,0:T(8,128)(2,1)S(1)}, u32[]{:S(2)}, u32[]{:S(2)}) collective-permute-start(bf16[272,768]{1,0:T(8,128)(2,1)S(1)} %collective-permute-done.4.refs_9_), channel_id=1, source_target_pairs={{0,4},{2,6},{4,8},{6,10},{8,12},{10,14},{12,0},{14,2},{1,5},{3,7},... | collective-permute-start | bytes 1253384 | tf_op jit(solution)/shard_map/ppermute | solution.py:24
  59.5 3.3 %collective-permute-start.1 = (bf16[256,768]{1,0:T(8,128)(2,1)S(1)}, bf16[256,768]{1,0:T(8,128)(2,1)S(1)}, u32[]{:S(2)}, u32[]{:S(2)}) collective-permute-start(bf16[256,768]{1,0:T(8,128)(2,1)S(1)} %copy-done.2), channel_id=1, source_target_pairs={{0,1},{1,0},{2,3},{3,2},{4,5},{5,4},{6,7},{7,6},{8,9},{9,8},{10,11... | collective-permute-start | bytes 1179656 | tf_op jit(solution)/shard_map/ppermute | solution.py:29
  62.8 1.7 %collective-permute-start.7 = (bf16[256,768]{1,0:T(8,128)(2,1)S(1)}, bf16[256,768]{1,0:T(8,128)(2,1)S(1)}, u32[]{:S(2)}, u32[]{:S(2)}) collective-permute-start(bf16[256,768]{1,0:T(8,128)(2,1)S(1)} %collective-permute-done.3.refs_5_), channel_id=1, source_target_pairs={{0,1},{1,0},{2,3},{3,2},{4,5},{5,4},{6,7},{7,6},{8,9},{9,8},{10,11... | collective-permute-start | bytes 1179656 | tf_op jit(solution)/shard_map/ppermute | solution.py:29
  76.4 3.1 %collective-permute-start.11 = (f32[4,128]{1,0:T(4,128)S(1)}, f32[4,128]{1,0:T(4,128)S(1)}, u32[]{:S(2)}, u32[]{:S(2)}) collective-permute-start(f32[4,128]{1,0:T(4,128)S(1)} %get-tuple-element.32), channel_id=1, source_target_pairs={{0,3},{1,2},{2,1},{3,0},{4,7},{5,6},{6,5},{7,4},{8,11},{9,10},{10,... | collective-permute-start | bytes 6152 | tf_op jit(solution)/shard_map/ppermute | solution.py:35
  76.5 3.7 %collective-permute-start.10 = (f32[4,128]{1,0:T(4,128)S(1)}, f32[4,128]{1,0:T(4,128)S(1)}, u32[]{:S(2)}, u32[]{:S(2)}) collective-permute-start(f32[4,128]{1,0:T(4,128)S(1)} %get-tuple-element.33), channel_id=1, source_target_pairs={{0,2},{2,0},{4,6},{6,4},{8,10},{10,8},{12,14},{14,12},{1,3},{3,1},... | collective-permute-start | bytes 6152 | tf_op jit(solution)/shard_map/ppermute | solution.py:29
  78.0 2.2 %collective-permute-start.9 = (f32[4,128]{1,0:T(4,128)S(1)}, f32[4,128]{1,0:T(4,128)S(1)}, u32[]{:S(2)}, u32[]{:S(2)}) collective-permute-start(f32[4,128]{1,0:T(4,128)S(1)} %get-tuple-element.31), channel_id=1, source_target_pairs={{0,1},{1,0},{2,3},{3,2},{4,5},{5,4},{6,7},{7,6},{8,9},{9,8},{10,11... | collective-permute-start | bytes 6152 | tf_op jit(solution)/shard_map/ppermute | solution.py:29

commit v9 on v8

--- a/solution.py
+++ b/solution.py
@@ -50,7 +50,7 @@
 def pack_kernel(
     nhelper, helper_ref, r_ref, q_ref, ids_ref, clusters_ref, live_ref, count_ref, r_out, *refs
 ):
-    q_outs, (ids, clusters, live, count, r_table, q_table, sem) = refs[:-7], refs[-7:]
+    q_outs, (ids, clusters, live, count, sem) = refs[:-5], refs[-5:]
     chunks = ids_ref.shape[0] // nhelper
     qblocks = clusters_ref.shape[0]
     pairs = [(ids_ref, ids), (live_ref, live), (clusters_ref, clusters), (count_ref, count)]
@@ -62,10 +62,8 @@
         height = out.shape[0] // LANES * LANES
         pairs.append((q_ref.at[pl.ds(start, height)], out.at[pl.ds(0, height)]))
         start += height
-    pairs.append((r_table, r_out.at[pl.ds(chunks * LANES, TABLE)]))
-    pairs.append((q_table, q_outs[0].at[pl.ds(q_outs[0].shape[0] - TABLE, TABLE)]))
     copies = [pltpu.make_async_copy(*pair, sem.at[i]) for i, pair in enumerate(pairs)]
-    for copy in copies[:-2]:
+    for copy in copies:
         copy.start()
     for copy in copies[:4]:
         copy.wait()
@@ -76,15 +74,15 @@
         tile = helper_ref[0] + nhelper * c
         here = jnp.where(tile * LANES + lane < live[0], ids[pl.ds(tile, 1), :], -1)
         rows = jnp.where(row == c, here, rows)
-    r_table[...] = jnp.zeros_like(r_table)
-    r_table[:, pl.ds(0, LANES)] = rows.astype(jnp.float32).astype(jnp.bfloat16)
-    copies[-2].start()
+    r_out[pl.ds(chunks * LANES, TABLE), pl.ds(0, LANES)] = rows.astype(jnp.float32).astype(
+        jnp.bfloat16
+    )
     rows = jnp.where(lane == qblocks, count[0], 0)
     for k in range(qblocks):
         rows = jnp.where(lane == k, clusters[k], rows)
-    q_table[...] = jnp.zeros_like(q_table)
-    q_table[:, pl.ds(0, LANES)] = rows.astype(jnp.float32).astype(jnp.bfloat16)
-    copies[-1].start()
+    q_outs[0][pl.ds(q_outs[0].shape[0] - TABLE, TABLE), pl.ds(0, LANES)] = rows.astype(
+        jnp.float32
+    ).astype(jnp.bfloat16)
     for copy in copies[4:]:
         copy.wait()
 
@@ -150,7 +148,7 @@
         for side in range(wide):
             entry = jnp.minimum(wide * group + side, q_count - 1)
             slot, cluster = q_list[entry, 0], q_list[entry, 1]
-            beta = beta_ref[0, cluster]
+            beta = beta_ref[cluster]
             sides.append(
                 (slot, cluster.astype(jnp.float32), beta * factor, beta * beta * (0.5 * LOG2E))
             )
@@ -238,15 +236,13 @@
             for p, n in enumerate(split)
         ],
         in_specs=[SMEM] + [ANY] * 6,
-        out_specs=[ANY] * (1 + parts),
+        out_specs=[VMEM] * (1 + parts),
         scratch_shapes=[
             pltpu.VMEM((tiles, LANES), jnp.int32),
             pltpu.SMEM((qblocks,), jnp.int32),
             pltpu.SMEM((1,), jnp.int32),
             pltpu.SMEM((1,), jnp.int32),
-            pltpu.VMEM((TABLE, width), jnp.bfloat16),
-            pltpu.VMEM((TABLE, width), jnp.bfloat16),
-            pltpu.SemaphoreType.DMA((6 + chunks + parts,)),
+            pltpu.SemaphoreType.DMA((4 + chunks + parts,)),
         ],
         compiler_params=WHOLE,
         cost_estimate=cost(1, 1),
@@ -259,15 +255,14 @@
         ref_rows,
         block_count,
     )
-    beta = cluster_beta.reshape(1, -1)
-    staged_own, *staged_q, beta = staged = pl.pallas_call(
+    staged_own, *staged_q = staged = pl.pallas_call(
         stage_kernel,
-        out_shape=[jax.ShapeDtypeStruct(x.shape, x.dtype) for x in (own, *q_own, beta)],
-        in_specs=[VMEM] * (2 + parts),
-        out_specs=[VMEM] * (2 + parts),
+        out_shape=[jax.ShapeDtypeStruct(x.shape, x.dtype) for x in (own, *q_own)],
+        in_specs=[VMEM] * (1 + parts),
+        out_specs=[VMEM] * (1 + parts),
         compiler_params=PARAMS,
         cost_estimate=cost(1, 1),
-    )(own, *q_own, beta)
+    )(own, *q_own)
     q_partner = [swap(q, "blk") for q in q_own]
     q_helper = [swap(q, "helper") for q in q_own]
 
@@ -282,10 +277,10 @@
     all_queries = (*staged_q, *q_helper, *q_partner, *q_both)
 
     totals, packed, info = score_call(
-        chunks, qblocks, parts, 2, beta, all_queries, early, True
+        chunks, qblocks, parts, 2, cluster_beta, all_queries, early, True
     )
     totals = score_call(
-        chunks, qblocks, parts, 4, beta, (info, packed, totals), above[-1:], False
+        chunks, qblocks, parts, 4, cluster_beta, (info, packed, totals), above[-1:], False
     )
     totals = totals.reshape(4, qblocks, LANES)
     total = totals[0] + swap(totals[1], "helper") + swap(totals[2], "blk") + swap_both(totals[3])

time: 81.1 us -> 46.5 us (0.57)
  Pallas kernels: 44.2 us -> 9.68 us
  waiting for transfers between devices: 21.6 us -> 19.6 us
  starting transfers between devices: 9.13 us -> 11 us
    pallas_call x1, Pallas kernels: 36.9 us -> 2.44 us  [per_device(): pl.pallas_call(functools.partial(pack_kernel, nhelper), out_shape=[jax.Sh...]
    ppermute x3, starting transfers between devices: 3.88 us -> 6.95 us  [turn(): lax.ppermute(value, 'blk', [(i, (i + by) % length) for i in range(length)])]
    ppermute x3, waiting for transfers between devices: 11.9 us -> 10.4 us  [turn(): lax.ppermute(value, 'blk', [(i, (i + by) % length) for i in range(length)])]
    ppermute x8, starting transfers between devices: 5.18 us -> 4.1 us  [swap(): return lax.ppermute(value, axis, [(i, i ^ 1) for i in range(length)])]
  transfers between devices with their start and end apart: 12 -> 12, of which waited for: 8 -> 8; matrix products, arithmetic and copies ran while one was open for 0% -> 0% of each run, Pallas kernels for 6% -> 11%
where the time goes in v9:
time: 46.5 us; the launch traced here: 46.2 us
  waiting for transfers between devices  19.6 us (42%)
  starting transfers between devices  11 us (24%)
  Pallas kernels  9.68 us (21%)
  local copies, waits for them, and re-layouts  3.67 us (8%)
  between operations  1.35 us (3%)
  other arithmetic  0.85 us (2%)
    ppermute x3, waiting for transfers between devices, turn(): lax.ppermute(value, 'blk', [(i, (i + by) % length) for i in range(length)])  10.4 us
    ppermute x8, waiting for transfers between devices, swap(): return lax.ppermute(value, axis, [(i, i ^ 1) for i in range(length)])  8.33 us
    pallas_call x2, Pallas kernels, score_call(): pl.pallas_call(functools.partial(score_kernel, chunks, qblocks, parts, fi...  7.15 us
    ppermute x3, starting transfers between devices, turn(): lax.ppermute(value, 'blk', [(i, (i + by) % length) for i in range(length)])  6.95 us
    ppermute x8, starting transfers between devices, swap(): return lax.ppermute(value, axis, [(i, i ^ 1) for i in range(length)])  4.1 us
    unnamed x12, local copies, waits for them, and re-layouts  3.67 us
    pallas_call x1, Pallas kernels, per_device(): pl.pallas_call(functools.partial(pack_kernel, nhelper), out_shape=[jax.Sh...  2.44 us
    ppermute x1, waiting for transfers between devices, swap_both(): return lax.ppermute(value, ('blk', 'helper'), pairs)  0.95 us
  transfers between devices with their start and end apart: 12, of which 8 were waited for; matrix products, arithmetic and copies ran while one was open for 0% of the time, Pallas kernels for 11%

profile of v9, /device:TPU:0, one launch (start us, length us, event | category | flops | bytes accessed | tf_op | source)
XLA Modules:
  0.0 46.2 jit_solution(14239575634704580606)
XLA Ops:
  1.3 2.4 %shard_map.82 = (bf16[272,768]{1,0:T(8,128)(2,1)}, bf16[272,768]{1,0:T(8,128)(2,1)}, bf16[256,768]{1,0:T(8,128)(2,1)}) custom-call(s32[1]{0:T(128)} %bitcast.helper_ref, bf16[512,768]{1,0:T(8,128)(2,1)} %r_ref.1, bf16[512,768]{1,0:T(8,128)(2,1)} %q_ref.1, s32[4,128]{1,0:T(4,128)} %bitcast.4, s32[4]{0:T(128)} %clusters_ref.1, s32[1]{0:T(128)S(6)} %copy.10.live_ref, ...), custom_call_target="tpu_custom_call" | custom-call | flops 1 | bytes 1 | tf_op jit(solution)/shard_map/pallas_call | solution.py:231
  3.7 3.1 %collective-permute-start.4 = (bf16[272,768]{1,0:T(8,128)(2,1)}, bf16[272,768]{1,0:T(8,128)(2,1)S(1)}, u32[]{:S(2)}, u32[]{:S(2)}) collective-permute-start(bf16[272,768]{1,0:T(8,128)(2,1)} %get-tuple-element.17.refs_0_), channel_id=1, source_target_pairs={{0,4},{2,6},{4,8},{6,10},{8,12},{10,14},{12,0},{14,2},{1,5},{3,7},... | collective-permute-start | bytes 1253384 | tf_op jit(solution)/shard_map/ppermute | solution.py:24
  6.8 1.5 %collective-permute-start.2 = (bf16[272,768]{1,0:T(8,128)(2,1)}, bf16[272,768]{1,0:T(8,128)(2,1)S(1)}, u32[]{:S(2)}, u32[]{:S(2)}) collective-permute-start(bf16[272,768]{1,0:T(8,128)(2,1)} %get-tuple-element.18.refs_1_), channel_id=1, source_target_pairs={{0,2},{2,0},{4,6},{6,4},{8,10},{10,8},{12,14},{14,12},{1,3},{3,1},... | collective-permute-start | bytes 1253384 | tf_op jit(solution)/shard_map/ppermute | solution.py:29
  8.3 2.2 %collective-permute-start.6 = (bf16[272,768]{1,0:T(8,128)(2,1)}, bf16[272,768]{1,0:T(8,128)(2,1)S(1)}, u32[]{:S(2)}, u32[]{:S(2)}) collective-permute-start(bf16[272,768]{1,0:T(8,128)(2,1)} %get-tuple-element.17.refs_0_), channel_id=1, source_target_pairs={{0,12},{2,14},{4,0},{6,2},{8,4},{10,6},{12,8},{14,10},{1,13},{3,15... | collective-permute-start | bytes 1253384 | tf_op jit(solution)/shard_map/ppermute | solution.py:24
  10.6 0.4 collective-permute-start.3
  11.0 1.0 %copy-done = bf16[272,768]{1,0:T(8,128)(2,1)S(1)} copy-done((bf16[272,768]{1,0:T(8,128)(2,1)S(1)}, bf16[272,768]{1,0:T(8,128)(2,1)}, u32[]{:S(2)}) %copy-start) | copy-done | bytes 417816
  12.0 1.0 %copy-done.1 = bf16[272,768]{1,0:T(8,128)(2,1)S(1)} copy-done((bf16[272,768]{1,0:T(8,128)(2,1)S(1)}, bf16[272,768]{1,0:T(8,128)(2,1)}, u32[]{:S(2)}) %copy-start.1) | copy-done | bytes 417816
  13.0 1.0 %copy-done.2 = bf16[256,768]{1,0:T(8,128)(2,1)S(1)} copy-done((bf16[256,768]{1,0:T(8,128)(2,1)S(1)}, bf16[256,768]{1,0:T(8,128)(2,1)}, u32[]{:S(2)}) %copy-start.2) | copy-done | bytes 393240
  14.0 5.5 %collective-permute-done.4.refs_9_ = bf16[272,768]{1,0:T(8,128)(2,1)S(1)} collective-permute-done((bf16[272,768]{1,0:T(8,128)(2,1)}, bf16[272,768]{1,0:T(8,128)(2,1)S(1)}, u32[]{:S(2)}, u32[]{:S(2)}) %collective-permute-start.4) | collective-permute-done | bytes 417824 | tf_op jit(solution)/shard_map/ppermute | solution.py:24
  19.6 1.6 %collective-permute-start.8 = (bf16[272,768]{1,0:T(8,128)(2,1)S(1)}, bf16[272,768]{1,0:T(8,128)(2,1)S(1)}, u32[]{:S(2)}, u32[]{:S(2)}) collective-permute-start(bf16[272,768]{1,0:T(8,128)(2,1)S(1)} %collective-permute-done.4.refs_9_), channel_id=1, source_target_pairs={{0,4},{2,6},{4,8},{6,10},{8,12},{10,14},{12,0},{14,2},{1,5},{3,7},... | collective-permute-start | bytes 1253384 | tf_op jit(solution)/shard_map/ppermute | solution.py:24
  21.2 5.3 %collective-permute-done.3.refs_5_ = bf16[256,768]{1,0:T(8,128)(2,1)S(1)} collective-permute-done((bf16[256,768]{1,0:T(8,128)(2,1)}, bf16[256,768]{1,0:T(8,128)(2,1)S(1)}, u32[]{:S(2)}, u32[]{:S(2)}) %collective-permute-start.3) | collective-permute-done | bytes 393248 | tf_op jit(solution)/shard_map/ppermute | solution.py:29
  26.6 1.1 %collective-permute-done.6.refs_10_ = bf16[272,768]{1,0:T(8,128)(2,1)S(1)} collective-permute-done((bf16[272,768]{1,0:T(8,128)(2,1)}, bf16[272,768]{1,0:T(8,128)(2,1)S(1)}, u32[]{:S(2)}, u32[]{:S(2)}) %collective-permute-start.6) | collective-permute-done | bytes 417824 | tf_op jit(solution)/shard_map/ppermute | solution.py:24
  27.7 0.6 %collective-permute-done.1.refs_3_ = bf16[256,768]{1,0:T(8,128)(2,1)S(1)} collective-permute-done((bf16[256,768]{1,0:T(8,128)(2,1)S(1)}, bf16[256,768]{1,0:T(8,128)(2,1)S(1)}, u32[]{:S(2)}, u32[]{:S(2)}) %collective-permute-start.1) | collective-permute-done | bytes 393248 | tf_op jit(solution)/shard_map/ppermute | solution.py:29
  28.3 1.1 %collective-permute-done.7.refs_7_ = bf16[256,768]{1,0:T(8,128)(2,1)S(1)} collective-permute-done((bf16[256,768]{1,0:T(8,128)(2,1)S(1)}, bf16[256,768]{1,0:T(8,128)(2,1)S(1)}, u32[]{:S(2)}, u32[]{:S(2)}) %collective-permute-start.7) | collective-permute-done | bytes 393248 | tf_op jit(solution)/shard_map/ppermute | solution.py:29
  29.4 0.7 %copy-done.3 = f32[64]{0:T(128)S(1)} copy-done((f32[64]{0:T(128)S(1)}, f32[64]{0:T(128)}, u32[]{:S(2)}) %copy-start.3) | copy-done | bytes 280
  30.0 5.0 %shard_map.84 = (f32[16,128]{1,0:T(8,128)S(1)}, bf16[2048,768]{1,0:T(8,128)(2,1)S(1)}, s32[8,128]{1,0:T(8,128)S(1)}) custom-call(f32[64]{0:T(128)S(1)} %copy-done.3, bf16[272,768]{1,0:T(8,128)(2,1)S(1)} %get-tuple-element.20.refs_0_, bf16[256,768]{1,0:T(8,128)(2,1)S(1)} %get-tuple-element.21.refs_1_, bf16[272,768]{1,0:T(8,128)(2,1)S(1)} %collective-permute-done.refs_2_, ...), custom_call_target="tpu_custom_call" | custom-call | flops 1 | bytes 1 | tf_op jit(solution)/shard_map/pallas_call | solution.py:200
  35.0 3.7 %collective-permute-done.8.refs_3_ = bf16[272,768]{1,0:T(8,128)(2,1)S(1)} collective-permute-done((bf16[272,768]{1,0:T(8,128)(2,1)S(1)}, bf16[272,768]{1,0:T(8,128)(2,1)S(1)}, u32[]{:S(2)}, u32[]{:S(2)}) %collective-permute-start.8) | collective-permute-done | bytes 417824 | tf_op jit(solution)/shard_map/ppermute | solution.py:24
  38.7 2.2 %shard_map.85 = f32[16,128]{1,0:T(8,128)S(1)} custom-call(f32[64]{0:T(128)S(1)} %copy-done.3, s32[8,128]{1,0:T(8,128)S(1)} %get-tuple-element.25.refs_0_, bf16[2048,768]{1,0:T(8,128)(2,1)S(1)} %get-tuple-element.26.refs_1_, f32[16,128]{1,0:T(8,128)S(1)} %get-tuple-element.27.refs_2_, bf16[272,768]{1,0:T(8,128)(2,1)S(1)} %collective-permute-done.8.refs_3_), custom_call_target="tpu_custom_call" | custom-call | flops 1 | bytes 1 | tf_op jit(solution)/shard_map/pallas_call | solution.py:200
  41.0 1.6 %collective-permute-start.10 = (f32[4,128]{1,0:T(4,128)S(1)}, f32[4,128]{1,0:T(4,128)S(1)}, u32[]{:S(2)}, u32[]{:S(2)}) collective-permute-start(f32[4,128]{1,0:T(4,128)S(1)} %get-tuple-element.31), channel_id=1, source_target_pairs={{0,2},{2,0},{4,6},{6,4},{8,10},{10,8},{12,14},{14,12},{1,3},{3,1},... | collective-permute-start | bytes 6152 | tf_op jit(solution)/shard_map/ppermute | solution.py:29
  42.6 0.6 %collective-permute-start.9 = (f32[4,128]{1,0:T(4,128)S(1)}, f32[4,128]{1,0:T(4,128)S(1)}, u32[]{:S(2)}, u32[]{:S(2)}) collective-permute-start(f32[4,128]{1,0:T(4,128)S(1)} %get-tuple-element.29), channel_id=1, source_target_pairs={{0,1},{1,0},{2,3},{3,2},{4,5},{5,4},{6,7},{7,6},{8,9},{9,8},{10,11... | collective-permute-start | bytes 6152 | tf_op jit(solution)/shard_map/ppermute | solution.py:29
  43.2 0.2 select_reduce_fusion
  43.4 1.2 %collective-permute-done.10 = f32[4,128]{1,0:T(4,128)S(1)} collective-permute-done((f32[4,128]{1,0:T(4,128)S(1)}, f32[4,128]{1,0:T(4,128)S(1)}, u32[]{:S(2)}, u32[]{:S(2)}) %collective-permute-start.10) | collective-permute-done | bytes 2080 | tf_op jit(solution)/shard_map/ppermute | solution.py:29
  44.6 0.9 %collective-permute-done.11 = f32[4,128]{1,0:T(4,128)S(1)} collective-permute-done((f32[4,128]{1,0:T(4,128)S(1)}, f32[4,128]{1,0:T(4,128)S(1)}, u32[]{:S(2)}, u32[]{:S(2)}) %collective-permute-start.11) | collective-permute-done | bytes 2080 | tf_op jit(solution)/shard_map/ppermute | solution.py:35
  45.6 0.7 %log-plus-one_bitcast_fusion = f32[512]{0:T(512)} fusion(f32[4,128]{1,0:T(4,128)S(1)} %collective-permute-done.11, f32[4,128]{1,0:T(4,128)S(1)} %collective-permute-done.10, f32[4,128]{1,0:T(4,128)S(1)} %collective-permute-done.9, f32[16,128]{1,0:T(8,128)S(1)} %shard_map.85, f32[4]{0:T(128)S(1)} %convert_element_type.7), kind=kLoop, calls=%fused_computation.4 | loop fusion | flops 2048 | bytes 10256 | tf_op jit(solution)/shard_map/reshape | solution.py:291
  (20 shorter events, 0.2 us)
Async XLA Ops:
  3.7 15.8 %collective-permute-start.4 = (bf16[272,768]{1,0:T(8,128)(2,1)}, bf16[272,768]{1,0:T(8,128)(2,1)S(1)}, u32[]{:S(2)}, u32[]{:S(2)}) collective-permute-start(bf16[272,768]{1,0:T(8,128)(2,1)} %get-tuple-element.17.refs_0_), channel_id=1, source_target_pairs={{0,4},{2,6},{4,8},{6,10},{8,12},{10,14},{12,0},{14,2},{1,5},{3,7},... | collective-permute-start | bytes 1253384 | tf_op jit(solution)/shard_map/ppermute | solution.py:24
  6.8 12.8 %collective-permute-start.2 = (bf16[272,768]{1,0:T(8,128)(2,1)}, bf16[272,768]{1,0:T(8,128)(2,1)S(1)}, u32[]{:S(2)}, u32[]{:S(2)}) collective-permute-start(bf16[272,768]{1,0:T(8,128)(2,1)} %get-tuple-element.18.refs_1_), channel_id=1, source_target_pairs={{0,2},{2,0},{4,6},{6,4},{8,10},{10,8},{12,14},{14,12},{1,3},{3,1},... | collective-permute-start | bytes 1253384 | tf_op jit(solution)/shard_map/ppermute | solution.py:29
  8.3 19.3 %collective-permute-start.6 = (bf16[272,768]{1,0:T(8,128)(2,1)}, bf16[272,768]{1,0:T(8,128)(2,1)S(1)}, u32[]{:S(2)}, u32[]{:S(2)}) collective-permute-start(bf16[272,768]{1,0:T(8,128)(2,1)} %get-tuple-element.17.refs_0_), channel_id=1, source_target_pairs={{0,12},{2,14},{4,0},{6,2},{8,4},{10,6},{12,8},{14,10},{1,13},{3,15... | collective-permute-start | bytes 1253384 | tf_op jit(solution)/shard_map/ppermute | solution.py:24
  10.6 16.0 %collective-permute-start.3 = (bf16[256,768]{1,0:T(8,128)(2,1)}, bf16[256,768]{1,0:T(8,128)(2,1)S(1)}, u32[]{:S(2)}, u32[]{:S(2)}) collective-permute-start(bf16[256,768]{1,0:T(8,128)(2,1)} %get-tuple-element.19.refs_2_), channel_id=1, source_target_pairs={{0,2},{2,0},{4,6},{6,4},{8,10},{10,8},{12,14},{14,12},{1,3},{3,1},... | collective-permute-start | bytes 1179656 | tf_op jit(solution)/shard_map/ppermute | solution.py:29
  11.0 17.3 %collective-permute-start = (bf16[272,768]{1,0:T(8,128)(2,1)}, bf16[272,768]{1,0:T(8,128)(2,1)S(1)}, u32[]{:S(2)}, u32[]{:S(2)}) collective-permute-start(bf16[272,768]{1,0:T(8,128)(2,1)} %get-tuple-element.18.refs_1_), channel_id=1, source_target_pairs={{0,1},{1,0},{2,3},{3,2},{4,5},{5,4},{6,7},{7,6},{8,9},{9,8},{10,11... | collective-permute-start | bytes 1253384 | tf_op jit(solution)/shard_map/ppermute | solution.py:29
  11.0 1.0 %copy-start = (bf16[272,768]{1,0:T(8,128)(2,1)S(1)}, bf16[272,768]{1,0:T(8,128)(2,1)}, u32[]{:S(2)}) copy-start(bf16[272,768]{1,0:T(8,128)(2,1)} %get-tuple-element.18.refs_1_) | copy-start | bytes 1253380
  12.0 1.0 %copy-start.1 = (bf16[272,768]{1,0:T(8,128)(2,1)S(1)}, bf16[272,768]{1,0:T(8,128)(2,1)}, u32[]{:S(2)}) copy-start(bf16[272,768]{1,0:T(8,128)(2,1)} %get-tuple-element.17.refs_0_) | copy-start | bytes 1253380
  13.0 1.0 %copy-start.2 = (bf16[256,768]{1,0:T(8,128)(2,1)S(1)}, bf16[256,768]{1,0:T(8,128)(2,1)}, u32[]{:S(2)}) copy-start(bf16[256,768]{1,0:T(8,128)(2,1)} %get-tuple-element.19.refs_2_) | copy-start | bytes 1179652
  19.6 9.8 %collective-permute-start.5 = (bf16[272,768]{1,0:T(8,128)(2,1)S(1)}, bf16[272,768]{1,0:T(8,128)(2,1)S(1)}, u32[]{:S(2)}, u32[]{:S(2)}) collective-permute-start(bf16[272,768]{1,0:T(8,128)(2,1)S(1)} %collective-permute-done.2.refs_4_), channel_id=1, source_target_pairs={{0,1},{1,0},{2,3},{3,2},{4,5},{5,4},{6,7},{7,6},{8,9},{9,8},{10,11... | collective-permute-start | bytes 1253384 | tf_op jit(solution)/shard_map/ppermute | solution.py:29
  19.6 23.6 %copy-start.4 = (s32[4]{0:T(128)S(1)}, s32[4]{0:T(128)}, u32[]{:S(2)}) copy-start(s32[4]{0:T(128)} %clusters_ref.1) | copy-start | bytes 52
  19.6 23.6 %copy-start.5 = (s32[64]{0:T(128)S(1)}, s32[64]{0:T(128)}, u32[]{:S(2)}) copy-start(s32[64]{0:T(128)} %param.15) | copy-start | bytes 772
  19.6 19.1 %collective-permute-start.8 = (bf16[272,768]{1,0:T(8,128)(2,1)S(1)}, bf16[272,768]{1,0:T(8,128)(2,1)S(1)}, u32[]{:S(2)}, u32[]{:S(2)}) collective-permute-start(bf16[272,768]{1,0:T(8,128)(2,1)S(1)} %collective-permute-done.4.refs_9_), channel_id=1, source_target_pairs={{0,4},{2,6},{4,8},{6,10},{8,12},{10,14},{12,0},{14,2},{1,5},{3,7},... | collective-permute-start | bytes 1253384 | tf_op jit(solution)/shard_map/ppermute | solution.py:24
  26.6 1.7 %collective-permute-start.1 = (bf16[256,768]{1,0:T(8,128)(2,1)S(1)}, bf16[256,768]{1,0:T(8,128)(2,1)S(1)}, u32[]{:S(2)}, u32[]{:S(2)}) collective-permute-start(bf16[256,768]{1,0:T(8,128)(2,1)S(1)} %copy-done.2), channel_id=1, source_target_pairs={{0,1},{1,0},{2,3},{3,2},{4,5},{5,4},{6,7},{7,6},{8,9},{9,8},{10,11... | collective-permute-start | bytes 1179656 | tf_op jit(solution)/shard_map/ppermute | solution.py:29
  27.7 1.7 %collective-permute-start.7 = (bf16[256,768]{1,0:T(8,128)(2,1)S(1)}, bf16[256,768]{1,0:T(8,128)(2,1)S(1)}, u32[]{:S(2)}, u32[]{:S(2)}) collective-permute-start(bf16[256,768]{1,0:T(8,128)(2,1)S(1)} %collective-permute-done.3.refs_5_), channel_id=1, source_target_pairs={{0,1},{1,0},{2,3},{3,2},{4,5},{5,4},{6,7},{7,6},{8,9},{9,8},{10,11... | collective-permute-start | bytes 1179656 | tf_op jit(solution)/shard_map/ppermute | solution.py:29
  29.4 0.7 %copy-start.3 = (f32[64]{0:T(128)S(1)}, f32[64]{0:T(128)}, u32[]{:S(2)}) copy-start(f32[64]{0:T(128)} %beta_ref.3) | copy-start | bytes 772
  41.0 3.7 %collective-permute-start.10 = (f32[4,128]{1,0:T(4,128)S(1)}, f32[4,128]{1,0:T(4,128)S(1)}, u32[]{:S(2)}, u32[]{:S(2)}) collective-permute-start(f32[4,128]{1,0:T(4,128)S(1)} %get-tuple-element.31), channel_id=1, source_target_pairs={{0,2},{2,0},{4,6},{6,4},{8,10},{10,8},{12,14},{14,12},{1,3},{3,1},... | collective-permute-start | bytes 6152 | tf_op jit(solution)/shard_map/ppermute | solution.py:29
  42.5 3.0 %collective-permute-start.11 = (f32[4,128]{1,0:T(4,128)S(1)}, f32[4,128]{1,0:T(4,128)S(1)}, u32[]{:S(2)}, u32[]{:S(2)}) collective-permute-start(f32[4,128]{1,0:T(4,128)S(1)} %get-tuple-element.30), channel_id=1, source_target_pairs={{0,3},{1,2},{2,1},{3,0},{4,7},{5,6},{6,5},{7,4},{8,11},{9,10},{10,... | collective-permute-start | bytes 6152 | tf_op jit(solution)/shard_map/ppermute | solution.py:35
  42.6 3.0 %collective-permute-start.9 = (f32[4,128]{1,0:T(4,128)S(1)}, f32[4,128]{1,0:T(4,128)S(1)}, u32[]{:S(2)}, u32[]{:S(2)}) collective-permute-start(f32[4,128]{1,0:T(4,128)S(1)} %get-tuple-element.29), channel_id=1, source_target_pairs={{0,1},{1,0},{2,3},{3,2},{4,5},{5,4},{6,7},{7,6},{8,9},{9,8},{10,11... | collective-permute-start | bytes 6152 | tf_op jit(solution)/shard_map/ppermute | solution.py:29

commit v10 on v9

--- a/solution.py
+++ b/solution.py
@@ -19,9 +19,9 @@
 PARAMS = pltpu.CompilerParams(vmem_limit_bytes=24 * 1024 * 1024)
 
 
-def turn(value, by):
+def trade(value, mask):
     length = lax.axis_size("blk")
-    return lax.ppermute(value, "blk", [(i, (i + by) % length) for i in range(length)])
+    return lax.ppermute(value, "blk", [(i, i ^ mask) for i in range(length)])
 
 
 def swap(value, axis):
@@ -266,21 +266,20 @@
     q_partner = [swap(q, "blk") for q in q_own]
     q_helper = [swap(q, "helper") for q in q_own]
 
-    above, below = [own], [own]
-    for step in range(1, sources // 2 + 1):
-        above.append(turn(after(above[-1], *staged) if step > 1 else own, 2))
-        if step < (sources + 1) // 2:
-            below.append(turn(below[-1], -2))
-    early = [staged_own] + above[1:-1] + below[1:]
-    q_both = [swap(after(q, above[-2]), "helper") for q in q_partner[:-1]]
-    q_both.append(swap(after(q_partner[-1], below[-1]), "helper"))
+    held, mask = [own], sources - 1
+    while mask:
+        fresh = [trade(after(x, *staged) if x is not own else x, 2 * mask) for x in held]
+        held, mask = held + fresh, mask // 2
+    early = [staged_own] + held[1:-1]
+    q_both = [swap(after(q, held[-3]), "helper") for q in q_partner[:-1]]
+    q_both.append(swap(after(q_partner[-1], held[-2]), "helper"))
     all_queries = (*staged_q, *q_helper, *q_partner, *q_both)
 
     totals, packed, info = score_call(
         chunks, qblocks, parts, 2, cluster_beta, all_queries, early, True
     )
     totals = score_call(
-        chunks, qblocks, parts, 4, cluster_beta, (info, packed, totals), above[-1:], False
+        chunks, qblocks, parts, 4, cluster_beta, (info, packed, totals), held[-1:], False
     )
     totals = totals.reshape(4, qblocks, LANES)
     total = totals[0] + swap(totals[1], "helper") + swap(totals[2], "blk") + swap_both(totals[3])

time: 46.5 us -> 45.2 us (0.972)
  starting transfers between devices: 11 us -> 15.7 us
  waiting for transfers between devices: 19.6 us -> 15.1 us
  Pallas kernels: 9.68 us -> 7.99 us
    ppermute x3, starting transfers between devices: 6.95 us -> 10.9 us  [trade(): return lax.ppermute(value, 'blk', [(i, i ^ mask) for i in range(length)])]
    ppermute x3, waiting for transfers between devices: 10.4 us -> 8.04 us  [trade(): return lax.ppermute(value, 'blk', [(i, i ^ mask) for i in range(length)])]
    ppermute x8, waiting for transfers between devices: 8.33 us -> 6.16 us  [swap(): return lax.ppermute(value, axis, [(i, i ^ 1) for i in range(length)])]
    pallas_call x2, Pallas kernels: 7.15 us -> 5.47 us  [score_call(): pl.pallas_call(functools.partial(score_kernel, chunks, qblocks, parts, fi...]
    ppermute x8, starting transfers between devices: 4.1 us -> 4.75 us  [swap(): return lax.ppermute(value, axis, [(i, i ^ 1) for i in range(length)])]
  transfers between devices with their start and end apart: 12 -> 12, of which waited for: 8 -> 8; matrix products, arithmetic and copies ran while one was open for 0% -> 0% of each run, Pallas kernels for 11% -> 9%
where the time goes in v10:
time: 45.2 us; the launch traced here: 44.7 us
  starting transfers between devices  15.7 us (35%)
  waiting for transfers between devices  15.1 us (33%)
  Pallas kernels  7.99 us (18%)
  local copies, waits for them, and re-layouts  3.67 us (8%)
  between operations  1.35 us (3%)
  other arithmetic  0.85 us (2%)
    ppermute x3, starting transfers between devices, trade(): return lax.ppermute(value, 'blk', [(i, i ^ mask) for i in range(length)])  10.9 us
    ppermute x3, waiting for transfers between devices, trade(): return lax.ppermute(value, 'blk', [(i, i ^ mask) for i in range(length)])  8.04 us
    ppermute x8, waiting for transfers between devices, swap(): return lax.ppermute(value, axis, [(i, i ^ 1) for i in range(length)])  6.16 us
    pallas_call x2, Pallas kernels, score_call(): pl.pallas_call(functools.partial(score_kernel, chunks, qblocks, parts, fi...  5.47 us
    ppermute x8, starting transfers between devices, swap(): return lax.ppermute(value, axis, [(i, i ^ 1) for i in range(length)])  4.75 us
    unnamed x12, local copies, waits for them, and re-layouts  3.67 us
    pallas_call x1, Pallas kernels, per_device(): pl.pallas_call(functools.partial(pack_kernel, nhelper), out_shape=[jax.Sh...  2.44 us
    ppermute x1, waiting for transfers between devices, swap_both(): return lax.ppermute(value, ('blk', 'helper'), pairs)  0.95 us
  transfers between devices with their start and end apart: 12, of which 8 were waited for; matrix products, arithmetic and copies ran while one was open for 0% of the time, Pallas kernels for 9%

profile of v10, /device:TPU:0, one launch (start us, length us, event | category | flops | bytes accessed | tf_op | source)
XLA Modules:
  0.0 44.7 jit_solution(18052617338588685937)
XLA Ops:
  1.3 2.4 %shard_map.82 = (bf16[272,768]{1,0:T(8,128)(2,1)}, bf16[272,768]{1,0:T(8,128)(2,1)}, bf16[256,768]{1,0:T(8,128)(2,1)}) custom-call(s32[1]{0:T(128)} %bitcast.helper_ref, bf16[512,768]{1,0:T(8,128)(2,1)} %r_ref.1, bf16[512,768]{1,0:T(8,128)(2,1)} %q_ref.1, s32[4,128]{1,0:T(4,128)} %bitcast.4, s32[4]{0:T(128)} %clusters_ref.1, s32[1]{0:T(128)S(6)} %copy.10.live_ref, ...), custom_call_target="tpu_custom_call" | custom-call | flops 1 | bytes 1 | tf_op jit(solution)/shard_map/pallas_call | solution.py:231
  3.7 5.1 %collective-permute-start.4 = (bf16[272,768]{1,0:T(8,128)(2,1)}, bf16[272,768]{1,0:T(8,128)(2,1)S(1)}, u32[]{:S(2)}, u32[]{:S(2)}) collective-permute-start(bf16[272,768]{1,0:T(8,128)(2,1)} %get-tuple-element.17.refs_0_), channel_id=1, source_target_pairs={{0,12},{2,14},{4,8},{6,10},{8,4},{10,6},{12,0},{14,2},{1,13},{3,15... | collective-permute-start | bytes 1253384 | tf_op jit(solution)/shard_map/ppermute | solution.py:24
  8.9 1.5 %collective-permute-start.2 = (bf16[272,768]{1,0:T(8,128)(2,1)}, bf16[272,768]{1,0:T(8,128)(2,1)S(1)}, u32[]{:S(2)}, u32[]{:S(2)}) collective-permute-start(bf16[272,768]{1,0:T(8,128)(2,1)} %get-tuple-element.18.refs_1_), channel_id=1, source_target_pairs={{0,2},{2,0},{4,6},{6,4},{8,10},{10,8},{12,14},{14,12},{1,3},{3,1},... | collective-permute-start | bytes 1253384 | tf_op jit(solution)/shard_map/ppermute | solution.py:29
  10.4 0.5 %collective-permute-start.3 = (bf16[256,768]{1,0:T(8,128)(2,1)}, bf16[256,768]{1,0:T(8,128)(2,1)S(1)}, u32[]{:S(2)}, u32[]{:S(2)}) collective-permute-start(bf16[256,768]{1,0:T(8,128)(2,1)} %get-tuple-element.19.refs_2_), channel_id=1, source_target_pairs={{0,2},{2,0},{4,6},{6,4},{8,10},{10,8},{12,14},{14,12},{1,3},{3,1},... | collective-permute-start | bytes 1179656 | tf_op jit(solution)/shard_map/ppermute | solution.py:29
  10.9 1.0 %copy-done = bf16[272,768]{1,0:T(8,128)(2,1)S(1)} copy-done((bf16[272,768]{1,0:T(8,128)(2,1)S(1)}, bf16[272,768]{1,0:T(8,128)(2,1)}, u32[]{:S(2)}) %copy-start) | copy-done | bytes 417816
  11.9 1.0 %copy-done.1 = bf16[272,768]{1,0:T(8,128)(2,1)S(1)} copy-done((bf16[272,768]{1,0:T(8,128)(2,1)S(1)}, bf16[272,768]{1,0:T(8,128)(2,1)}, u32[]{:S(2)}) %copy-start.1) | copy-done | bytes 417816
  12.9 1.0 %copy-done.2 = bf16[256,768]{1,0:T(8,128)(2,1)S(1)} copy-done((bf16[256,768]{1,0:T(8,128)(2,1)S(1)}, bf16[256,768]{1,0:T(8,128)(2,1)}, u32[]{:S(2)}) %copy-start.2) | copy-done | bytes 393240
  14.0 5.6 %collective-permute-done.4.refs_9_ = bf16[272,768]{1,0:T(8,128)(2,1)S(1)} collective-permute-done((bf16[272,768]{1,0:T(8,128)(2,1)}, bf16[272,768]{1,0:T(8,128)(2,1)S(1)}, u32[]{:S(2)}, u32[]{:S(2)}) %collective-permute-start.4) | collective-permute-done | bytes 417824 | tf_op jit(solution)/shard_map/ppermute | solution.py:24
  19.6 2.0 %collective-permute-done.2.refs_4_ = bf16[272,768]{1,0:T(8,128)(2,1)S(1)} collective-permute-done((bf16[272,768]{1,0:T(8,128)(2,1)}, bf16[272,768]{1,0:T(8,128)(2,1)S(1)}, u32[]{:S(2)}, u32[]{:S(2)}) %collective-permute-start.2) | collective-permute-done | bytes 417824 | tf_op jit(solution)/shard_map/ppermute | solution.py:29
  21.6 5.8 %collective-permute-start.8 = (bf16[272,768]{1,0:T(8,128)(2,1)S(1)}, bf16[272,768]{1,0:T(8,128)(2,1)S(1)}, u32[]{:S(2)}, u32[]{:S(2)}) collective-permute-start(bf16[272,768]{1,0:T(8,128)(2,1)S(1)} %collective-permute-done.4.refs_9_), channel_id=1, source_target_pairs={{0,4},{2,6},{4,0},{6,2},{8,12},{10,14},{12,8},{14,10},{1,5},{3,7},... | collective-permute-start | bytes 1253384 | tf_op jit(solution)/shard_map/ppermute | solution.py:24
  27.5 1.1 %collective-permute-done.3.refs_5_ = bf16[256,768]{1,0:T(8,128)(2,1)S(1)} collective-permute-done((bf16[256,768]{1,0:T(8,128)(2,1)}, bf16[256,768]{1,0:T(8,128)(2,1)S(1)}, u32[]{:S(2)}, u32[]{:S(2)}) %collective-permute-start.3) | collective-permute-done | bytes 393248 | tf_op jit(solution)/shard_map/ppermute | solution.py:29
  28.6 0.5 %collective-permute-start.7 = (bf16[256,768]{1,0:T(8,128)(2,1)S(1)}, bf16[256,768]{1,0:T(8,128)(2,1)S(1)}, u32[]{:S(2)}, u32[]{:S(2)}) collective-permute-start(bf16[256,768]{1,0:T(8,128)(2,1)S(1)} %collective-permute-done.3.refs_5_), channel_id=1, source_target_pairs={{0,1},{1,0},{2,3},{3,2},{4,5},{5,4},{6,7},{7,6},{8,9},{9,8},{10,11... | collective-permute-start | bytes 1179656 | tf_op jit(solution)/shard_map/ppermute | solution.py:29
  29.1 1.2 %collective-permute-done.1.refs_3_ = bf16[256,768]{1,0:T(8,128)(2,1)S(1)} collective-permute-done((bf16[256,768]{1,0:T(8,128)(2,1)S(1)}, bf16[256,768]{1,0:T(8,128)(2,1)S(1)}, u32[]{:S(2)}, u32[]{:S(2)}) %collective-permute-start.1) | collective-permute-done | bytes 393248 | tf_op jit(solution)/shard_map/ppermute | solution.py:29
  30.3 0.6 %collective-permute-done.7.refs_7_ = bf16[256,768]{1,0:T(8,128)(2,1)S(1)} collective-permute-done((bf16[256,768]{1,0:T(8,128)(2,1)S(1)}, bf16[256,768]{1,0:T(8,128)(2,1)S(1)}, u32[]{:S(2)}, u32[]{:S(2)}) %collective-permute-start.7) | collective-permute-done | bytes 393248 | tf_op jit(solution)/shard_map/ppermute | solution.py:29
  30.9 0.7 %copy-done.3 = f32[64]{0:T(128)S(1)} copy-done((f32[64]{0:T(128)S(1)}, f32[64]{0:T(128)}, u32[]{:S(2)}) %copy-start.3) | copy-done | bytes 280
  31.5 3.8 %shard_map.84 = (f32[16,128]{1,0:T(8,128)S(1)}, bf16[2048,768]{1,0:T(8,128)(2,1)S(1)}, s32[8,128]{1,0:T(8,128)S(1)}) custom-call(f32[64]{0:T(128)S(1)} %copy-done.3, bf16[272,768]{1,0:T(8,128)(2,1)S(1)} %get-tuple-element.20.refs_0_, bf16[256,768]{1,0:T(8,128)(2,1)S(1)} %get-tuple-element.21.refs_1_, bf16[272,768]{1,0:T(8,128)(2,1)S(1)} %collective-permute-done.refs_2_, ...), custom_call_target="tpu_custom_call" | custom-call | flops 1 | bytes 1 | tf_op jit(solution)/shard_map/pallas_call | solution.py:200
  35.3 2.4 %collective-permute-done.8.refs_3_ = bf16[272,768]{1,0:T(8,128)(2,1)S(1)} collective-permute-done((bf16[272,768]{1,0:T(8,128)(2,1)S(1)}, bf16[272,768]{1,0:T(8,128)(2,1)S(1)}, u32[]{:S(2)}, u32[]{:S(2)}) %collective-permute-start.8) | collective-permute-done | bytes 417824 | tf_op jit(solution)/shard_map/ppermute | solution.py:24
  37.7 1.7 %shard_map.85 = f32[16,128]{1,0:T(8,128)S(1)} custom-call(f32[64]{0:T(128)S(1)} %copy-done.3, s32[8,128]{1,0:T(8,128)S(1)} %get-tuple-element.25.refs_0_, bf16[2048,768]{1,0:T(8,128)(2,1)S(1)} %get-tuple-element.26.refs_1_, f32[16,128]{1,0:T(8,128)S(1)} %get-tuple-element.27.refs_2_, bf16[272,768]{1,0:T(8,128)(2,1)S(1)} %collective-permute-done.8.refs_3_), custom_call_target="tpu_custom_call" | custom-call | flops 1 | bytes 1 | tf_op jit(solution)/shard_map/pallas_call | solution.py:200
  39.4 1.6 %collective-permute-start.10 = (f32[4,128]{1,0:T(4,128)S(1)}, f32[4,128]{1,0:T(4,128)S(1)}, u32[]{:S(2)}, u32[]{:S(2)}) collective-permute-start(f32[4,128]{1,0:T(4,128)S(1)} %get-tuple-element.31), channel_id=1, source_target_pairs={{0,2},{2,0},{4,6},{6,4},{8,10},{10,8},{12,14},{14,12},{1,3},{3,1},... | collective-permute-start | bytes 6152 | tf_op jit(solution)/shard_map/ppermute | solution.py:29
  41.0 0.6 %collective-permute-start.9 = (f32[4,128]{1,0:T(4,128)S(1)}, f32[4,128]{1,0:T(4,128)S(1)}, u32[]{:S(2)}, u32[]{:S(2)}) collective-permute-start(f32[4,128]{1,0:T(4,128)S(1)} %get-tuple-element.29), channel_id=1, source_target_pairs={{0,1},{1,0},{2,3},{3,2},{4,5},{5,4},{6,7},{7,6},{8,9},{9,8},{10,11... | collective-permute-start | bytes 6152 | tf_op jit(solution)/shard_map/ppermute | solution.py:29
  41.7 0.2 select_reduce_fusion
  41.8 1.2 %collective-permute-done.10 = f32[4,128]{1,0:T(4,128)S(1)} collective-permute-done((f32[4,128]{1,0:T(4,128)S(1)}, f32[4,128]{1,0:T(4,128)S(1)}, u32[]{:S(2)}, u32[]{:S(2)}) %collective-permute-start.10) | collective-permute-done | bytes 2080 | tf_op jit(solution)/shard_map/ppermute | solution.py:29
  43.1 0.9 %collective-permute-done.11 = f32[4,128]{1,0:T(4,128)S(1)} collective-permute-done((f32[4,128]{1,0:T(4,128)S(1)}, f32[4,128]{1,0:T(4,128)S(1)}, u32[]{:S(2)}, u32[]{:S(2)}) %collective-permute-start.11) | collective-permute-done | bytes 2080 | tf_op jit(solution)/shard_map/ppermute | solution.py:35
  44.0 0.7 %log-plus-one_bitcast_fusion = f32[512]{0:T(512)} fusion(f32[4,128]{1,0:T(4,128)S(1)} %collective-permute-done.11, f32[4,128]{1,0:T(4,128)S(1)} %collective-permute-done.10, f32[4,128]{1,0:T(4,128)S(1)} %collective-permute-done.9, f32[16,128]{1,0:T(8,128)S(1)} %shard_map.85, f32[4]{0:T(128)S(1)} %convert_element_type.7), kind=kLoop, calls=%fused_computation.4 | loop fusion | flops 2048 | bytes 10256 | tf_op jit(solution)/shard_map/reshape | solution.py:290
  (20 shorter events, 0.1 us)
Async XLA Ops:
  3.7 15.9 %collective-permute-start.4 = (bf16[272,768]{1,0:T(8,128)(2,1)}, bf16[272,768]{1,0:T(8,128)(2,1)S(1)}, u32[]{:S(2)}, u32[]{:S(2)}) collective-permute-start(bf16[272,768]{1,0:T(8,128)(2,1)} %get-tuple-element.17.refs_0_), channel_id=1, source_target_pairs={{0,12},{2,14},{4,8},{6,10},{8,4},{10,6},{12,0},{14,2},{1,13},{3,15... | collective-permute-start | bytes 1253384 | tf_op jit(solution)/shard_map/ppermute | solution.py:24
  8.9 12.8 %collective-permute-start.2 = (bf16[272,768]{1,0:T(8,128)(2,1)}, bf16[272,768]{1,0:T(8,128)(2,1)S(1)}, u32[]{:S(2)}, u32[]{:S(2)}) collective-permute-start(bf16[272,768]{1,0:T(8,128)(2,1)} %get-tuple-element.18.refs_1_), channel_id=1, source_target_pairs={{0,2},{2,0},{4,6},{6,4},{8,10},{10,8},{12,14},{14,12},{1,3},{3,1},... | collective-permute-start | bytes 1253384 | tf_op jit(solution)/shard_map/ppermute | solution.py:29
  10.4 18.2 %collective-permute-start.6 = (bf16[272,768]{1,0:T(8,128)(2,1)}, bf16[272,768]{1,0:T(8,128)(2,1)S(1)}, u32[]{:S(2)}, u32[]{:S(2)}) collective-permute-start(bf16[272,768]{1,0:T(8,128)(2,1)} %get-tuple-element.17.refs_0_), channel_id=1, source_target_pairs={{0,4},{2,6},{4,0},{6,2},{8,12},{10,14},{12,8},{14,10},{1,5},{3,7},... | collective-permute-start | bytes 1253384 | tf_op jit(solution)/shard_map/ppermute | solution.py:24
  10.4 18.2 %collective-permute-start.3 = (bf16[256,768]{1,0:T(8,128)(2,1)}, bf16[256,768]{1,0:T(8,128)(2,1)S(1)}, u32[]{:S(2)}, u32[]{:S(2)}) collective-permute-start(bf16[256,768]{1,0:T(8,128)(2,1)} %get-tuple-element.19.refs_2_), channel_id=1, source_target_pairs={{0,2},{2,0},{4,6},{6,4},{8,10},{10,8},{12,14},{14,12},{1,3},{3,1},... | collective-permute-start | bytes 1179656 | tf_op jit(solution)/shard_map/ppermute | solution.py:29
  10.9 19.4 %collective-permute-start = (bf16[272,768]{1,0:T(8,128)(2,1)}, bf16[272,768]{1,0:T(8,128)(2,1)S(1)}, u32[]{:S(2)}, u32[]{:S(2)}) collective-permute-start(bf16[272,768]{1,0:T(8,128)(2,1)} %get-tuple-element.18.refs_1_), channel_id=1, source_target_pairs={{0,1},{1,0},{2,3},{3,2},{4,5},{5,4},{6,7},{7,6},{8,9},{9,8},{10,11... | collective-permute-start | bytes 1253384 | tf_op jit(solution)/shard_map/ppermute | solution.py:29
  10.9 1.0 %copy-start = (bf16[272,768]{1,0:T(8,128)(2,1)S(1)}, bf16[272,768]{1,0:T(8,128)(2,1)}, u32[]{:S(2)}) copy-start(bf16[272,768]{1,0:T(8,128)(2,1)} %get-tuple-element.18.refs_1_) | copy-start | bytes 1253380
  11.9 1.0 %copy-start.1 = (bf16[272,768]{1,0:T(8,128)(2,1)S(1)}, bf16[272,768]{1,0:T(8,128)(2,1)}, u32[]{:S(2)}) copy-start(bf16[272,768]{1,0:T(8,128)(2,1)} %get-tuple-element.17.refs_0_) | copy-start | bytes 1253380
  12.9 1.0 %copy-start.2 = (bf16[256,768]{1,0:T(8,128)(2,1)S(1)}, bf16[256,768]{1,0:T(8,128)(2,1)}, u32[]{:S(2)}) copy-start(bf16[256,768]{1,0:T(8,128)(2,1)} %get-tuple-element.19.refs_2_) | copy-start | bytes 1179652
  21.6 9.3 %collective-permute-start.5 = (bf16[272,768]{1,0:T(8,128)(2,1)S(1)}, bf16[272,768]{1,0:T(8,128)(2,1)S(1)}, u32[]{:S(2)}, u32[]{:S(2)}) collective-permute-start(bf16[272,768]{1,0:T(8,128)(2,1)S(1)} %collective-permute-done.2.refs_4_), channel_id=1, source_target_pairs={{0,1},{1,0},{2,3},{3,2},{4,5},{5,4},{6,7},{7,6},{8,9},{9,8},{10,11... | collective-permute-start | bytes 1253384 | tf_op jit(solution)/shard_map/ppermute | solution.py:29
  21.6 20.0 %copy-start.4 = (s32[4]{0:T(128)S(1)}, s32[4]{0:T(128)}, u32[]{:S(2)}) copy-start(s32[4]{0:T(128)} %clusters_ref.1) | copy-start | bytes 52
  21.6 20.0 %copy-start.5 = (s32[64]{0:T(128)S(1)}, s32[64]{0:T(128)}, u32[]{:S(2)}) copy-start(s32[64]{0:T(128)} %param.15) | copy-start | bytes 772
  21.6 16.1 %collective-permute-start.8 = (bf16[272,768]{1,0:T(8,128)(2,1)S(1)}, bf16[272,768]{1,0:T(8,128)(2,1)S(1)}, u32[]{:S(2)}, u32[]{:S(2)}) collective-permute-start(bf16[272,768]{1,0:T(8,128)(2,1)S(1)} %collective-permute-done.4.refs_9_), channel_id=1, source_target_pairs={{0,4},{2,6},{4,0},{6,2},{8,12},{10,14},{12,8},{14,10},{1,5},{3,7},... | collective-permute-start | bytes 1253384 | tf_op jit(solution)/shard_map/ppermute | solution.py:24
  28.6 1.7 %collective-permute-start.1 = (bf16[256,768]{1,0:T(8,128)(2,1)S(1)}, bf16[256,768]{1,0:T(8,128)(2,1)S(1)}, u32[]{:S(2)}, u32[]{:S(2)}) collective-permute-start(bf16[256,768]{1,0:T(8,128)(2,1)S(1)} %copy-done.2), channel_id=1, source_target_pairs={{0,1},{1,0},{2,3},{3,2},{4,5},{5,4},{6,7},{7,6},{8,9},{9,8},{10,11... | collective-permute-start | bytes 1179656 | tf_op jit(solution)/shard_map/ppermute | solution.py:29
  28.6 2.3 %collective-permute-start.7 = (bf16[256,768]{1,0:T(8,128)(2,1)S(1)}, bf16[256,768]{1,0:T(8,128)(2,1)S(1)}, u32[]{:S(2)}, u32[]{:S(2)}) collective-permute-start(bf16[256,768]{1,0:T(8,128)(2,1)S(1)} %collective-permute-done.3.refs_5_), channel_id=1, source_target_pairs={{0,1},{1,0},{2,3},{3,2},{4,5},{5,4},{6,7},{7,6},{8,9},{9,8},{10,11... | collective-permute-start | bytes 1179656 | tf_op jit(solution)/shard_map/ppermute | solution.py:29
  30.9 0.7 %copy-start.3 = (f32[64]{0:T(128)S(1)}, f32[64]{0:T(128)}, u32[]{:S(2)}) copy-start(f32[64]{0:T(128)} %beta_ref.3) | copy-start | bytes 772
  39.4 3.7 %collective-permute-start.10 = (f32[4,128]{1,0:T(4,128)S(1)}, f32[4,128]{1,0:T(4,128)S(1)}, u32[]{:S(2)}, u32[]{:S(2)}) collective-permute-start(f32[4,128]{1,0:T(4,128)S(1)} %get-tuple-element.31), channel_id=1, source_target_pairs={{0,2},{2,0},{4,6},{6,4},{8,10},{10,8},{12,14},{14,12},{1,3},{3,1},... | collective-permute-start | bytes 6152 | tf_op jit(solution)/shard_map/ppermute | solution.py:29
  41.0 3.0 %collective-permute-start.11 = (f32[4,128]{1,0:T(4,128)S(1)}, f32[4,128]{1,0:T(4,128)S(1)}, u32[]{:S(2)}, u32[]{:S(2)}) collective-permute-start(f32[4,128]{1,0:T(4,128)S(1)} %get-tuple-element.30), channel_id=1, source_target_pairs={{0,3},{1,2},{2,1},{3,0},{4,7},{5,6},{6,5},{7,4},{8,11},{9,10},{10,... | collective-permute-start | bytes 6152 | tf_op jit(solution)/shard_map/ppermute | solution.py:35
  41.0 3.0 %collective-permute-start.9 = (f32[4,128]{1,0:T(4,128)S(1)}, f32[4,128]{1,0:T(4,128)S(1)}, u32[]{:S(2)}, u32[]{:S(2)}) collective-permute-start(f32[4,128]{1,0:T(4,128)S(1)} %get-tuple-element.29), channel_id=1, source_target_pairs={{0,1},{1,0},{2,3},{3,2},{4,5},{5,4},{6,7},{7,6},{8,9},{9,8},{10,11... | collective-permute-start | bytes 6152 | tf_op jit(solution)/shard_map/ppermute | solution.py:29

commit v11 on v10

v11 whole, which is shorter than its diff:
```python
import functools
import math

import jax
import jax.numpy as jnp
from jax import lax
from jax.experimental import pallas as pl
from jax.experimental.pallas import tpu as pltpu
from jax.sharding import PartitionSpec as P

LANES = 128
LOG2E = 1.4426950408889634
DEAD = -1.0e30
SMEM = pl.BlockSpec(memory_space=pltpu.SMEM)
VMEM = pl.BlockSpec(memory_space=pltpu.VMEM)
PARAMS = pltpu.CompilerParams(vmem_limit_bytes=24 * 1024 * 1024)


def trade(value, mask):
    length = lax.axis_size("blk")
    return lax.ppermute(value, "blk", [(i, i ^ mask) for i in range(length)])


def swap(value, axis):
    length = lax.axis_size(axis)
    return lax.ppermute(value, axis, [(i, i ^ 1) for i in range(length)])


def swap_both(value):
    nblk, nhelper = lax.axis_size("blk"), lax.axis_size("helper")
    pairs = [(i, (i ^ nhelper) ^ 1) for i in range(nblk * nhelper)]
    return lax.ppermute(value, ("blk", "helper"), pairs)


def after(value, *others):
    return lax.optimization_barrier((value, *others))[0]


def cost(flops, moved):
    return pl.CostEstimate(flops=flops, bytes_accessed=moved, transcendentals=0)


def rows_of(index, count=1):
    return pl.ds(pl.multiple_of(index * LANES, LANES), count * LANES)


def table_kernel(
    nhelper, helper_ref, clusters_ref, count_ref, live_ref, ids_ref, out_ref
):
    lane = lax.broadcasted_iota(jnp.int32, (1, LANES), 1)
    chunks = ids_ref.shape[0] // nhelper
    out_ref[...] = jnp.zeros_like(out_ref)
    for c in range(chunks):
        tile = helper_ref[0] + nhelper * c
        ids = ids_ref[pl.ds(tile, 1), :]
        out_ref[c : c + 1, :] = jnp.where(tile * LANES + lane < live_ref[0], ids, -1)
    qblocks = clusters_ref.shape[0]
    row = jnp.where(lane == qblocks, count_ref[0], 0)
    for k in range(qblocks):
        row = jnp.where(lane == k, clusters_ref[k], row)
    out_ref[chunks : chunks + 1, :] = row


def stage_kernel(*refs):
    half = len(refs) // 2
    for source, out in zip(refs[:half], refs[half:]):
        out[...] = source[...]


def score_kernel(chunks, qblocks, first, wide, beta_ref, *refs):
    if first:
        (*given, out_ref, qv, info_out, q_list, ids_ref, other_ref, info, info_sem) = refs
        q_refs, t_refs, given = given[:4], given[4:8], given[8:]
    else:
        (info, qv, prev_ref, *given, out_ref, q_list, ids_ref, other_ref) = refs
    r_refs, i_refs = given[: len(given) // 2], given[len(given) // 2 :]
    width = qv.shape[1]
    height = chunks * LANES
    if first:
        for s, t_ref in enumerate(t_refs):
            info_out[s : s + 1, :] = t_ref[chunks : chunks + 1, :]
        copy = pltpu.make_async_copy(info_out, info, info_sem)
        copy.start()

    for s, i_ref in enumerate(i_refs):
        for c in range(chunks):
            ids = i_ref[c : c + 1, :].astype(jnp.float32)
            ids = jnp.broadcast_to(ids, (LANES, LANES)).T
            rows = pl.ds(s * height + c * LANES, LANES)
            ids_ref[rows, :] = ids
            other_ref[rows, :] = jnp.where(ids < 0.0, DEAD, -4.0)
    if first:
        copy.wait()

    q_count = jnp.int32(0)
    for source in range(4):
        blocks = info[source, qblocks]

        def one_block(block, carry, source=source, q_count=q_count):
            if first:
                qv[rows_of(q_count + block), :] = q_refs[source][rows_of(block), :]
            q_list[q_count + block, 0] = source * qblocks + block
            q_list[q_count + block, 1] = info[source, block]
            return carry

        lax.fori_loop(0, blocks, one_block, 0)
        q_count = q_count + blocks

    factor = LOG2E / math.sqrt(width)
    out_ref[...] = jnp.zeros_like(out_ref) if first else prev_ref[...]

    def query_blocks(group, carry):
        sides = []
        for side in range(wide):
            entry = jnp.minimum(wide * group + side, q_count - 1)
            slot, cluster = q_list[entry, 0], q_list[entry, 1]
            beta = beta_ref[cluster]
            sides.append(
                (slot, cluster.astype(jnp.float32), beta * factor, beta * beta * (0.5 * LOG2E))
            )
        accs = [jnp.zeros((8, LANES), jnp.float32) for _ in range(wide)]
        for s, r_ref in enumerate(r_refs):
            tile = r_ref[pl.ds(0, height), :]
            rows = pl.ds(s * height, height)
            for pair in range(wide // 2):
                score = lax.dot_general(
                    tile,
                    qv[rows_of(wide * group + 2 * pair, 2), :],
                    (((1,), (1,)), ((), ())),
                    preferred_element_type=jnp.float32,
                )
                for half in range(2):
                    side = 2 * pair + half
                    _, cluster, scale, offset = sides[side]
                    part = score[:, half * LANES : (half + 1) * LANES]
                    weight = jnp.where(ids_ref[rows, :] == cluster, 0.0, other_ref[rows, :])
                    value = jnp.exp2((part * scale - offset) + weight)
                    accs[side] += jnp.sum(value.reshape(height // 8, 8, LANES), axis=0)
        for side in range(wide):
            total = jnp.sum(accs[side], axis=0, keepdims=True)

            @pl.when(wide * group + side < q_count)
            def _(side=side, total=total):
                row = pl.ds(sides[side][0], 1)
                out_ref[row, :] = out_ref[row, :] + total

        return carry

    lax.fori_loop(0, (q_count + wide - 1) // wide, query_blocks, 0)


def score_call(chunks, qblocks, wide, beta, given, payloads, tables, first):
    width = payloads[0].shape[1]
    slots = 4 * qblocks
    height = chunks * LANES
    totals_shape = jax.ShapeDtypeStruct((slots, LANES), jnp.float32)
    packed_shape = jax.ShapeDtypeStruct((slots * LANES, width), jnp.bfloat16)
    info_shape = jax.ShapeDtypeStruct((8, LANES), jnp.int32)
    spread = pltpu.VMEM((len(payloads) * height, LANES), jnp.float32)
    scratch = [pltpu.SMEM((slots, 2), jnp.int32), spread, spread]
    specs = [VMEM] * (len(given) + len(payloads) + len(tables))
    if first:
        scratch += [pltpu.SMEM((8, LANES), jnp.int32), pltpu.SemaphoreType.DMA]
    else:
        specs[0] = SMEM
    return pl.pallas_call(
        functools.partial(score_kernel, chunks, qblocks, first, wide),
        out_shape=(totals_shape, packed_shape, info_shape) if first else totals_shape,
        in_specs=[SMEM] + specs,
        out_specs=(VMEM, VMEM, VMEM) if first else VMEM,
        scratch_shapes=scratch,
        compiler_params=PARAMS,
        cost_estimate=cost(1, 1),
    )(beta, *given, *payloads, *tables)


def per_device(
    queries,
    query_block_cluster,
    block_count,
    references,
    ref_cluster,
    ref_rows,
    cluster_beta,
    cluster_member_count,
):
    nblk, nhelper = lax.axis_size("blk"), lax.axis_size("helper")
    helper = lax.axis_index("helper").astype(jnp.int32)
    qblocks = query_block_cluster.shape[0]
    rows, width = references.shape
    tiles = rows // LANES
    chunks = tiles // nhelper
    sources = nblk // 2

    q_partner = swap(queries, "blk")
    by_chunk = references.reshape(chunks, nhelper, LANES, width)
    own = lax.dynamic_index_in_dim(by_chunk, helper, 1, keepdims=False)
    own = own.reshape(chunks * LANES, width)

    held, masks, mask = [own], [0], sources - 1
    while mask:
        held = held + [trade(x, 2 * mask) for x in held]
        masks, mask = masks + [m ^ mask for m in masks], mask // 2
    q_helper = swap(queries, "helper")

    table = pl.pallas_call(
        functools.partial(table_kernel, nhelper),
        out_shape=jax.ShapeDtypeStruct((8 * ((chunks + 8) // 8), LANES), jnp.int32),
        in_specs=[SMEM] * 4 + [VMEM],
        out_specs=VMEM,
        compiler_params=PARAMS,
        cost_estimate=cost(1, 1),
    )(
        helper[None],
        after(query_block_cluster, own),
        block_count,
        ref_rows,
        ref_cluster.reshape(tiles, LANES),
    )
    r_tables = [table] + [trade(table, 2 * m) for m in masks[1:]]
    q_tables = [table, swap(table, "helper"), swap(table, "blk"), swap_both(table)]
    staged = pl.pallas_call(
        stage_kernel,
        out_shape=jax.ShapeDtypeStruct(queries.shape, queries.dtype),
        in_specs=[VMEM],
        out_specs=VMEM,
        compiler_params=PARAMS,
        cost_estimate=cost(1, 1),
    )(queries)
    q_both = swap(after(q_partner, staged, *held[1:-1], *r_tables, *q_tables), "helper")

    totals, packed, info = score_call(
        chunks,
        qblocks,
        2,
        cluster_beta,
        (staged, q_helper, q_partner, q_both, *q_tables),
        held[:-1],
        r_tables[:-1],
        True,
    )
    totals = score_call(
        chunks,
        qblocks,
        4,
        cluster_beta,
        (info, packed, totals),
        held[-1:],
        r_tables[-1:],
        False,
    )
    totals = totals.reshape(4, qblocks, LANES)
    total = totals[0] + swap(totals[1], "helper") + swap(totals[2], "blk") + swap_both(totals[3])
    columns = jnp.arange(cluster_member_count.shape[0], dtype=jnp.int32)
    onehot = query_block_cluster[:, None] == columns[None, :]
    sizes = jnp.sum(jnp.where(onehot, cluster_member_count[None, :], 0), axis=1)
    density = jnp.log1p(total / sizes.astype(jnp.float32)[:, None])
    return density.reshape(queries.shape[0])


def solution(mesh):
    in_specs = (
        P(("parts", "blk", "helper"), None),
        P(("parts", "blk", "helper")),
        P(("parts", "blk", "helper")),
        P(("parts", "blk"), None),
        P(("parts", "blk")),
        P(("parts", "blk")),
        P("parts"),
        P("parts"),
    )
    out_specs = P(("parts", "blk", "helper"))
    return jax.shard_map(
        per_device, mesh=mesh, in_specs=in_specs, out_specs=out_specs, check_vma=False
    )
```

time: 45.2 us -> 51.4 us (1.14)
  waiting for transfers between devices: 15.1 us -> 25.7 us
  Pallas kernels: 7.99 us -> 6 us
  starting transfers between devices: 15.7 us -> 13.9 us
    ppermute x3 -> x6, waiting for transfers between devices: 8.04 us -> 20.8 us  [trade(): return lax.ppermute(value, 'blk', [(i, i ^ mask) for i in range(length)])]
    ppermute x3 -> x6, starting transfers between devices: 10.9 us -> 7.52 us  [trade(): return lax.ppermute(value, 'blk', [(i, i ^ mask) for i in range(length)])]
    ppermute x8 -> x7, waiting for transfers between devices: 6.16 us -> 3.93 us  [swap(): return lax.ppermute(value, axis, [(i, i ^ 1) for i in range(length)])]
    pallas_call x4, Pallas kernels: 7.99 us -> 6 us  [the longest x2 5.4 us: score_call(): pl.pallas_call(functools.partial(score_kernel, chunks, qblocks, first, wi...]
    ppermute x1 -> x2, starting transfers between devices: 0.01 us -> 1.15 us  [swap_both(): return lax.ppermute(value, ('blk', 'helper'), pairs)]
    unnamed x12 -> x14, local copies, waits for them, and re-layouts: 3.67 us -> 3.13 us
    ppermute x8 -> x7, starting transfers between devices: 4.75 us -> 5.23 us  [swap(): return lax.ppermute(value, axis, [(i, i ^ 1) for i in range(length)])]
  transfers between devices with their start and end apart: 12 -> 15, of which waited for: 8 -> 9; matrix products, arithmetic and copies ran while one was open for 0% -> 0% of each run, Pallas kernels for 9% -> 8%
where the time goes in v11:
time: 51.4 us; the launch traced here: 51 us
  waiting for transfers between devices  25.7 us (50%)
  starting transfers between devices  13.9 us (27%)
  Pallas kernels  6 us (12%)
  local copies, waits for them, and re-layouts  3.16 us (6%)
  between operations  1.39 us (3%)
  other arithmetic  0.85 us (2%)
    ppermute x6, waiting for transfers between devices, trade(): return lax.ppermute(value, 'blk', [(i, i ^ mask) for i in range(length)])  20.8 us
    ppermute x6, starting transfers between devices, trade(): return lax.ppermute(value, 'blk', [(i, i ^ mask) for i in range(length)])  7.52 us
    pallas_call x2, Pallas kernels, score_call(): pl.pallas_call(functools.partial(score_kernel, chunks, qblocks, first, wi...  5.4 us
    ppermute x7, starting transfers between devices, swap(): return lax.ppermute(value, axis, [(i, i ^ 1) for i in range(length)])  5.23 us
    ppermute x7, waiting for transfers between devices, swap(): return lax.ppermute(value, axis, [(i, i ^ 1) for i in range(length)])  3.93 us
    unnamed x14, local copies, waits for them, and re-layouts  3.13 us
    ppermute x2, starting transfers between devices, swap_both(): return lax.ppermute(value, ('blk', 'helper'), pairs)  1.15 us
  transfers between devices with their start and end apart: 15, of which 9 were waited for; matrix products, arithmetic and copies ran while one was open for 0% of the time, Pallas kernels for 8%

profile of v11, /device:TPU:0, one launch (start us, length us, event | category | flops | bytes accessed | tf_op | source)
XLA Modules:
  0.0 51.0 jit_solution(16305673755540404340)
XLA Ops:
  0.0 3.0 %collective-permute-start.1 = (bf16[512,768]{1,0:T(8,128)(2,1)}, bf16[512,768]{1,0:T(8,128)(2,1)S(1)}, u32[]{:S(2)}, u32[]{:S(2)}) collective-permute-start(bf16[512,768]{1,0:T(8,128)(2,1)} %refs_0_.1), channel_id=1, source_target_pairs={{0,2},{2,0},{4,6},{6,4},{8,10},{10,8},{12,14},{14,12},{1,3},{3,1},... | collective-permute-start | bytes 2359304 | tf_op jit(solution)/shard_map/ppermute | solution.py:26
  3.0 3.7 %collective-permute-start.2 = (bf16[256,768]{1,0:T(8,128)(2,1)S(1)}, bf16[256,768]{1,0:T(8,128)(2,1)S(1)}, u32[]{:S(2)}, u32[]{:S(2)}) collective-permute-start(bf16[256,768]{1,0:T(8,128)(2,1)S(1)} %bitcast.9), channel_id=1, source_target_pairs={{0,12},{2,14},{4,8},{6,10},{8,4},{10,6},{12,0},{14,2},{1,13},{3,15... | collective-permute-start | bytes 1179656 | tf_op jit(solution)/shard_map/ppermute | solution.py:21
  8.0 0.7 %copy-done.2 = s32[512]{0:T(512)S(1)} copy-done((s32[512]{0:T(512)S(1)}, s32[512]{0:T(512)}, u32[]{:S(2)}) %copy-start.2) | copy-done | bytes 2072
  8.7 0.7 %copy-done.4 = s32[4]{0:T(128)S(1)} copy-done((s32[4]{0:T(128)S(1)}, s32[4]{0:T(128)}, u32[]{:S(2)}) %copy-start.4) | copy-done | bytes 40
  9.3 0.5 %shard_map.83.refs_4_.refs_11_ = s32[8,128]{1,0:T(8,128)S(1)} custom-call(s32[1]{0:T(128)} %bitcast.2.helper_ref, s32[4]{0:T(128)S(1)} %copy-done.4, s32[1]{0:T(128)S(6)} %copy.12.count_ref, s32[1]{0:T(128)S(6)} %copy.13.live_ref, s32[4,128]{1,0:T(4,128)S(1)} %bitcast.12), custom_call_target="tpu_custom_call" | custom-call | flops 1 | bytes 1 | tf_op jit(solution)/shard_map/pallas_call | solution.py:206
  9.9 1.0 %collective-permute-start.4 = (s32[8,128]{1,0:T(8,128)S(1)}, s32[8,128]{1,0:T(8,128)S(1)}, u32[]{:S(2)}, u32[]{:S(2)}) collective-permute-start(s32[8,128]{1,0:T(8,128)S(1)} %shard_map.83.refs_4_.refs_11_), channel_id=1, source_target_pairs={{0,12},{2,14},{4,8},{6,10},{8,4},{10,6},{12,0},{14,2},{1,13},{3,15... | collective-permute-start | bytes 12296 | tf_op jit(solution)/shard_map/ppermute | solution.py:21
  10.8 1.2 %collective-permute-start.5 = (s32[8,128]{1,0:T(8,128)S(1)}, s32[8,128]{1,0:T(8,128)S(1)}, u32[]{:S(2)}, u32[]{:S(2)}) collective-permute-start(s32[8,128]{1,0:T(8,128)S(1)} %shard_map.83.refs_4_.refs_11_), channel_id=1, source_target_pairs={{0,4},{2,6},{4,0},{6,2},{8,12},{10,14},{12,8},{14,10},{1,5},{3,7},... | collective-permute-start | bytes 12296 | tf_op jit(solution)/shard_map/ppermute | solution.py:21
  12.0 12.2 %collective-permute-done.4.refs_12_ = s32[8,128]{1,0:T(8,128)S(1)} collective-permute-done((s32[8,128]{1,0:T(8,128)S(1)}, s32[8,128]{1,0:T(8,128)S(1)}, u32[]{:S(2)}, u32[]{:S(2)}) %collective-permute-start.4) | collective-permute-done | bytes 4128 | tf_op jit(solution)/shard_map/ppermute | solution.py:21
  24.2 0.5 %collective-permute-start.6 = (s32[8,128]{1,0:T(8,128)S(1)}, s32[8,128]{1,0:T(8,128)S(1)}, u32[]{:S(2)}, u32[]{:S(2)}) collective-permute-start(s32[8,128]{1,0:T(8,128)S(1)} %shard_map.83.refs_4_.refs_11_), channel_id=1, source_target_pairs={{0,8},{2,10},{4,12},{6,14},{8,0},{10,2},{12,4},{14,6},{1,9},{3,11}... | collective-permute-start | bytes 12296 | tf_op jit(solution)/shard_map/ppermute | solution.py:21
  24.8 4.0 %collective-permute-done.6.refs_4_ = s32[8,128]{1,0:T(8,128)S(1)} collective-permute-done((s32[8,128]{1,0:T(8,128)S(1)}, s32[8,128]{1,0:T(8,128)S(1)}, u32[]{:S(2)}, u32[]{:S(2)}) %collective-permute-start.6) | collective-permute-done | bytes 4128 | tf_op jit(solution)/shard_map/ppermute | solution.py:21
  28.7 1.4 %collective-permute-start.8 = (s32[8,128]{1,0:T(8,128)S(1)}, s32[8,128]{1,0:T(8,128)S(1)}, u32[]{:S(2)}, u32[]{:S(2)}) collective-permute-start(s32[8,128]{1,0:T(8,128)S(1)} %shard_map.83.refs_4_.refs_11_), channel_id=1, source_target_pairs={{0,2},{2,0},{4,6},{6,4},{8,10},{10,8},{12,14},{14,12},{1,3},{3,1},... | collective-permute-start | bytes 12296 | tf_op jit(solution)/shard_map/ppermute | solution.py:26
  30.1 1.1 %copy-done.1 = bf16[512,768]{1,0:T(8,128)(2,1)S(1)} copy-done((bf16[512,768]{1,0:T(8,128)(2,1)S(1)}, bf16[512,768]{1,0:T(8,128)(2,1)}, u32[]{:S(2)}) %copy-start.1) | copy-done | bytes 786456
  31.3 1.0 %collective-permute-done.8.refs_6_ = s32[8,128]{1,0:T(8,128)S(1)} collective-permute-done((s32[8,128]{1,0:T(8,128)S(1)}, s32[8,128]{1,0:T(8,128)S(1)}, u32[]{:S(2)}, u32[]{:S(2)}) %collective-permute-start.8) | collective-permute-done | bytes 4128 | tf_op jit(solution)/shard_map/ppermute | solution.py:26
  32.3 0.8 %collective-permute-done.9.refs_7_ = s32[8,128]{1,0:T(8,128)S(1)} collective-permute-done((s32[8,128]{1,0:T(8,128)S(1)}, s32[8,128]{1,0:T(8,128)S(1)}, u32[]{:S(2)}, u32[]{:S(2)}) %collective-permute-start.9) | collective-permute-done | bytes 4128 | tf_op jit(solution)/shard_map/ppermute | solution.py:32
  33.3 1.1 %collective-permute-start.11 = (bf16[256,768]{1,0:T(8,128)(2,1)S(1)}, bf16[256,768]{1,0:T(8,128)(2,1)S(1)}, u32[]{:S(2)}, u32[]{:S(2)}) collective-permute-start(bf16[256,768]{1,0:T(8,128)(2,1)S(1)} %collective-permute-done.2.refs_9_), channel_id=1, source_target_pairs={{0,4},{2,6},{4,0},{6,2},{8,12},{10,14},{12,8},{14,10},{1,5},{3,7},... | collective-permute-start | bytes 1179656 | tf_op jit(solution)/shard_map/ppermute | solution.py:21
  34.6 1.1 %collective-permute-done.10.refs_3_ = bf16[512,768]{1,0:T(8,128)(2,1)S(1)} collective-permute-done((bf16[512,768]{1,0:T(8,128)(2,1)S(1)}, bf16[512,768]{1,0:T(8,128)(2,1)S(1)}, u32[]{:S(2)}, u32[]{:S(2)}) %collective-permute-start.10) | collective-permute-done | bytes 786464 | tf_op jit(solution)/shard_map/ppermute | solution.py:26
  35.7 0.7 %copy-done.3 = f32[64]{0:T(128)S(1)} copy-done((f32[64]{0:T(128)S(1)}, f32[64]{0:T(128)}, u32[]{:S(2)}) %copy-start.3) | copy-done | bytes 280
  36.4 3.7 %shard_map.84 = (f32[16,128]{1,0:T(8,128)S(1)}, bf16[2048,768]{1,0:T(8,128)(2,1)S(1)}, s32[8,128]{1,0:T(8,128)S(1)}) custom-call(f32[64]{0:T(128)S(1)} %copy-done.3, bf16[512,768]{1,0:T(8,128)(2,1)S(1)} %shard_map.82.refs_0_, bf16[512,768]{1,0:T(8,128)(2,1)S(1)} %collective-permute-done.refs_1_, bf16[512,768]{1,0:T(8,128)(2,1)S(1)} %collective-permute-done.1.refs_2_, ...), custom_call_target="tpu_custom_call" | custom-call | flops 1 | bytes 1 | tf_op jit(solution)/shard_map/pallas_call | solution.py:166
  40.1 4.7 %collective-permute-done.11.refs_3_ = bf16[256,768]{1,0:T(8,128)(2,1)S(1)} collective-permute-done((bf16[256,768]{1,0:T(8,128)(2,1)S(1)}, bf16[256,768]{1,0:T(8,128)(2,1)S(1)}, u32[]{:S(2)}, u32[]{:S(2)}) %collective-permute-start.11) | collective-permute-done | bytes 393248 | tf_op jit(solution)/shard_map/ppermute | solution.py:21
  44.8 1.7 %shard_map.85 = f32[16,128]{1,0:T(8,128)S(1)} custom-call(f32[64]{0:T(128)S(1)} %copy-done.3, s32[8,128]{1,0:T(8,128)S(1)} %get-tuple-element.12.refs_0_, bf16[2048,768]{1,0:T(8,128)(2,1)S(1)} %get-tuple-element.13.refs_1_, f32[16,128]{1,0:T(8,128)S(1)} %get-tuple-element.14.refs_2_, bf16[256,768]{1,0:T(8,128)(2,1)S(1)} %collective-permute-done.11.refs_3_, ...), custom_call_target="tpu_custom_call" | custom-call | flops 1 | bytes 1 | tf_op jit(solution)/shard_map/pallas_call | solution.py:166
  46.6 0.7 %collective-permute-start.13 = (f32[4,128]{1,0:T(4,128)S(1)}, f32[4,128]{1,0:T(4,128)S(1)}, u32[]{:S(2)}, u32[]{:S(2)}) collective-permute-start(f32[4,128]{1,0:T(4,128)S(1)} %get-tuple-element.17), channel_id=1, source_target_pairs={{0,2},{2,0},{4,6},{6,4},{8,10},{10,8},{12,14},{14,12},{1,3},{3,1},... | collective-permute-start | bytes 6152 | tf_op jit(solution)/shard_map/ppermute | solution.py:26
  47.3 1.1 %collective-permute-start.14 = (f32[4,128]{1,0:T(4,128)S(1)}, f32[4,128]{1,0:T(4,128)S(1)}, u32[]{:S(2)}, u32[]{:S(2)}) collective-permute-start(f32[4,128]{1,0:T(4,128)S(1)} %get-tuple-element.16), channel_id=1, source_target_pairs={{0,3},{1,2},{2,1},{3,0},{4,7},{5,6},{6,5},{7,4},{8,11},{9,10},{10,... | collective-permute-start | bytes 6152 | tf_op jit(solution)/shard_map/ppermute | solution.py:32
  48.7 1.6 %collective-permute-done.13 = f32[4,128]{1,0:T(4,128)S(1)} collective-permute-done((f32[4,128]{1,0:T(4,128)S(1)}, f32[4,128]{1,0:T(4,128)S(1)}, u32[]{:S(2)}, u32[]{:S(2)}) %collective-permute-start.13) | collective-permute-done | bytes 2080 | tf_op jit(solution)/shard_map/ppermute | solution.py:26
  50.3 0.7 %log-plus-one_bitcast_fusion = f32[512]{0:T(512)} fusion(f32[4,128]{1,0:T(4,128)S(1)} %collective-permute-done.14, f32[4,128]{1,0:T(4,128)S(1)} %collective-permute-done.13, f32[4,128]{1,0:T(4,128)S(1)} %collective-permute-done.12, f32[16,128]{1,0:T(8,128)S(1)} %shard_map.85, f32[4]{0:T(128)S(1)} %convert_element_type.7), kind=kLoop, calls=%fused_computation.4 | loop fusion | flops 2048 | bytes 10256 | tf_op jit(solution)/shard_map/reshape | solution.py:258
  (29 shorter events, 0.7 us)
Async XLA Ops:
  0.0 3.0 %copy-start = (bf16[512,768]{1,0:T(8,128)(2,1)S(1)}, bf16[512,768]{1,0:T(8,128)(2,1)}, u32[]{:S(2)}) copy-start(bf16[512,768]{1,0:T(8,128)(2,1)} %param.11) | copy-start | bytes 2359300
  0.0 33.2 %collective-permute-start.1 = (bf16[512,768]{1,0:T(8,128)(2,1)}, bf16[512,768]{1,0:T(8,128)(2,1)S(1)}, u32[]{:S(2)}, u32[]{:S(2)}) collective-permute-start(bf16[512,768]{1,0:T(8,128)(2,1)} %refs_0_.1), channel_id=1, source_target_pairs={{0,2},{2,0},{4,6},{6,4},{8,10},{10,8},{12,14},{14,12},{1,3},{3,1},... | collective-permute-start | bytes 2359304 | tf_op jit(solution)/shard_map/ppermute | solution.py:26
  3.0 30.2 %collective-permute-start.2 = (bf16[256,768]{1,0:T(8,128)(2,1)S(1)}, bf16[256,768]{1,0:T(8,128)(2,1)S(1)}, u32[]{:S(2)}, u32[]{:S(2)}) collective-permute-start(bf16[256,768]{1,0:T(8,128)(2,1)S(1)} %bitcast.9), channel_id=1, source_target_pairs={{0,12},{2,14},{4,8},{6,10},{8,4},{10,6},{12,0},{14,2},{1,13},{3,15... | collective-permute-start | bytes 1179656 | tf_op jit(solution)/shard_map/ppermute | solution.py:21
  6.7 26.5 %collective-permute-start.3 = (bf16[256,768]{1,0:T(8,128)(2,1)S(1)}, bf16[256,768]{1,0:T(8,128)(2,1)S(1)}, u32[]{:S(2)}, u32[]{:S(2)}) collective-permute-start(bf16[256,768]{1,0:T(8,128)(2,1)S(1)} %bitcast.10), channel_id=1, source_target_pairs={{0,4},{2,6},{4,0},{6,2},{8,12},{10,14},{12,8},{14,10},{1,5},{3,7},... | collective-permute-start | bytes 1179656 | tf_op jit(solution)/shard_map/ppermute | solution.py:21
  8.0 0.7 %copy-start.2 = (s32[512]{0:T(512)S(1)}, s32[512]{0:T(512)}, u32[]{:S(2)}) copy-start(s32[512]{0:T(512)} %param.12) | copy-start | bytes 6148
  8.7 0.7 %copy-start.4 = (s32[4]{0:T(128)S(1)}, s32[4]{0:T(128)}, u32[]{:S(2)}) copy-start(s32[4]{0:T(128)} %clusters_ref) | copy-start | bytes 52
  9.9 14.3 %collective-permute-start.4 = (s32[8,128]{1,0:T(8,128)S(1)}, s32[8,128]{1,0:T(8,128)S(1)}, u32[]{:S(2)}, u32[]{:S(2)}) collective-permute-start(s32[8,128]{1,0:T(8,128)S(1)} %shard_map.83.refs_4_.refs_11_), channel_id=1, source_target_pairs={{0,12},{2,14},{4,8},{6,10},{8,4},{10,6},{12,0},{14,2},{1,13},{3,15... | collective-permute-start | bytes 12296 | tf_op jit(solution)/shard_map/ppermute | solution.py:21
  10.8 13.9 %collective-permute-start.5 = (s32[8,128]{1,0:T(8,128)S(1)}, s32[8,128]{1,0:T(8,128)S(1)}, u32[]{:S(2)}, u32[]{:S(2)}) collective-permute-start(s32[8,128]{1,0:T(8,128)S(1)} %shard_map.83.refs_4_.refs_11_), channel_id=1, source_target_pairs={{0,4},{2,6},{4,0},{6,2},{8,12},{10,14},{12,8},{14,10},{1,5},{3,7},... | collective-permute-start | bytes 12296 | tf_op jit(solution)/shard_map/ppermute | solution.py:21
  24.2 4.5 %collective-permute-start.6 = (s32[8,128]{1,0:T(8,128)S(1)}, s32[8,128]{1,0:T(8,128)S(1)}, u32[]{:S(2)}, u32[]{:S(2)}) collective-permute-start(s32[8,128]{1,0:T(8,128)S(1)} %shard_map.83.refs_4_.refs_11_), channel_id=1, source_target_pairs={{0,8},{2,10},{4,12},{6,14},{8,0},{10,2},{12,4},{14,6},{1,9},{3,11}... | collective-permute-start | bytes 12296 | tf_op jit(solution)/shard_map/ppermute | solution.py:21
  24.8 5.4 %collective-permute-start.7 = (s32[8,128]{1,0:T(8,128)S(1)}, s32[8,128]{1,0:T(8,128)S(1)}, u32[]{:S(2)}, u32[]{:S(2)}) collective-permute-start(s32[8,128]{1,0:T(8,128)S(1)} %shard_map.83.refs_4_.refs_11_), channel_id=1, source_target_pairs={{0,1},{1,0},{2,3},{3,2},{4,5},{5,4},{6,7},{7,6},{8,9},{9,8},{10,11... | collective-permute-start | bytes 12296 | tf_op jit(solution)/shard_map/ppermute | solution.py:26
  28.7 3.6 %collective-permute-start.8 = (s32[8,128]{1,0:T(8,128)S(1)}, s32[8,128]{1,0:T(8,128)S(1)}, u32[]{:S(2)}, u32[]{:S(2)}) collective-permute-start(s32[8,128]{1,0:T(8,128)S(1)} %shard_map.83.refs_4_.refs_11_), channel_id=1, source_target_pairs={{0,2},{2,0},{4,6},{6,4},{8,10},{10,8},{12,14},{14,12},{1,3},{3,1},... | collective-permute-start | bytes 12296 | tf_op jit(solution)/shard_map/ppermute | solution.py:26
  30.1 3.0 %collective-permute-start.9 = (s32[8,128]{1,0:T(8,128)S(1)}, s32[8,128]{1,0:T(8,128)S(1)}, u32[]{:S(2)}, u32[]{:S(2)}) collective-permute-start(s32[8,128]{1,0:T(8,128)S(1)} %shard_map.83.refs_4_.refs_11_), channel_id=1, source_target_pairs={{0,3},{1,2},{2,1},{3,0},{4,7},{5,6},{6,5},{7,4},{8,11},{9,10},{10,... | collective-permute-start | bytes 12296 | tf_op jit(solution)/shard_map/ppermute | solution.py:32
  30.1 1.1 %copy-start.1 = (bf16[512,768]{1,0:T(8,128)(2,1)S(1)}, bf16[512,768]{1,0:T(8,128)(2,1)}, u32[]{:S(2)}) copy-start(bf16[512,768]{1,0:T(8,128)(2,1)} %refs_0_.1) | copy-start | bytes 2359300
  31.3 17.2 %copy-start.5 = (s32[4]{0:T(128)S(1)}, s32[4]{0:T(128)}, u32[]{:S(2)}) copy-start(s32[4]{0:T(128)} %clusters_ref) | copy-start | bytes 52
  31.3 17.2 %copy-start.6 = (s32[64]{0:T(128)S(1)}, s32[64]{0:T(128)}, u32[]{:S(2)}) copy-start(s32[64]{0:T(128)} %param.15) | copy-start | bytes 772
  32.3 2.3 %collective-permute-start = (bf16[512,768]{1,0:T(8,128)(2,1)S(1)}, bf16[512,768]{1,0:T(8,128)(2,1)S(1)}, u32[]{:S(2)}, u32[]{:S(2)}) collective-permute-start(bf16[512,768]{1,0:T(8,128)(2,1)S(1)} %copy-done.1), channel_id=1, source_target_pairs={{0,1},{1,0},{2,3},{3,2},{4,5},{5,4},{6,7},{7,6},{8,9},{9,8},{10,11... | collective-permute-start | bytes 2359304 | tf_op jit(solution)/shard_map/ppermute | solution.py:26
  33.2 2.6 %collective-permute-start.10 = (bf16[512,768]{1,0:T(8,128)(2,1)S(1)}, bf16[512,768]{1,0:T(8,128)(2,1)S(1)}, u32[]{:S(2)}, u32[]{:S(2)}) collective-permute-start(bf16[512,768]{1,0:T(8,128)(2,1)S(1)} %collective-permute-done.1.refs_2_), channel_id=1, source_target_pairs={{0,1},{1,0},{2,3},{3,2},{4,5},{5,4},{6,7},{7,6},{8,9},{9,8},{10,11... | collective-permute-start | bytes 2359304 | tf_op jit(solution)/shard_map/ppermute | solution.py:26
  33.3 11.5 %collective-permute-start.11 = (bf16[256,768]{1,0:T(8,128)(2,1)S(1)}, bf16[256,768]{1,0:T(8,128)(2,1)S(1)}, u32[]{:S(2)}, u32[]{:S(2)}) collective-permute-start(bf16[256,768]{1,0:T(8,128)(2,1)S(1)} %collective-permute-done.2.refs_9_), channel_id=1, source_target_pairs={{0,4},{2,6},{4,0},{6,2},{8,12},{10,14},{12,8},{14,10},{1,5},{3,7},... | collective-permute-start | bytes 1179656 | tf_op jit(solution)/shard_map/ppermute | solution.py:21
  35.7 0.7 %copy-start.3 = (f32[64]{0:T(128)S(1)}, f32[64]{0:T(128)}, u32[]{:S(2)}) copy-start(f32[64]{0:T(128)} %beta_ref.3) | copy-start | bytes 772
  46.5 2.1 %collective-permute-start.12 = (f32[4,128]{1,0:T(4,128)S(1)}, f32[4,128]{1,0:T(4,128)S(1)}, u32[]{:S(2)}, u32[]{:S(2)}) collective-permute-start(f32[4,128]{1,0:T(4,128)S(1)} %get-tuple-element.15), channel_id=1, source_target_pairs={{0,1},{1,0},{2,3},{3,2},{4,5},{5,4},{6,7},{7,6},{8,9},{9,8},{10,11... | collective-permute-start | bytes 6152 | tf_op jit(solution)/shard_map/ppermute | solution.py:26
  46.6 3.7 %collective-permute-start.13 = (f32[4,128]{1,0:T(4,128)S(1)}, f32[4,128]{1,0:T(4,128)S(1)}, u32[]{:S(2)}, u32[]{:S(2)}) collective-permute-start(f32[4,128]{1,0:T(4,128)S(1)} %get-tuple-element.17), channel_id=1, source_target_pairs={{0,2},{2,0},{4,6},{6,4},{8,10},{10,8},{12,14},{14,12},{1,3},{3,1},... | collective-permute-start | bytes 6152 | tf_op jit(solution)/shard_map/ppermute | solution.py:26
  47.3 3.0 %collective-permute-start.14 = (f32[4,128]{1,0:T(4,128)S(1)}, f32[4,128]{1,0:T(4,128)S(1)}, u32[]{:S(2)}, u32[]{:S(2)}) collective-permute-start(f32[4,128]{1,0:T(4,128)S(1)} %get-tuple-element.16), channel_id=1, source_target_pairs={{0,3},{1,2},{2,1},{3,0},{4,7},{5,6},{6,5},{7,4},{8,11},{9,10},{10,... | collective-permute-start | bytes 6152 | tf_op jit(solution)/shard_map/ppermute | solution.py:32

commit v12 on v11

--- a/solution.py
+++ b/solution.py
@@ -9,6 +9,7 @@
 from jax.sharding import PartitionSpec as P
 
 LANES = 128
+TABLE = 16
 LOG2E = 1.4426950408889634
 DEAD = -1.0e30
 SMEM = pl.BlockSpec(memory_space=pltpu.SMEM)
@@ -44,21 +45,26 @@
     return pl.ds(pl.multiple_of(index * LANES, LANES), count * LANES)
 
 
-def table_kernel(
-    nhelper, helper_ref, clusters_ref, count_ref, live_ref, ids_ref, out_ref
-):
-    lane = lax.broadcasted_iota(jnp.int32, (1, LANES), 1)
-    chunks = ids_ref.shape[0] // nhelper
-    out_ref[...] = jnp.zeros_like(out_ref)
-    for c in range(chunks):
+def pack_kernel(nhelper, helper_ref, live_ref, ids_ref, r_ref, out_ref):
+    lane = lax.broadcasted_iota(jnp.int32, (TABLE, LANES), 1)
+    row = lax.broadcasted_iota(jnp.int32, (TABLE, LANES), 0)
+    table = jnp.full((TABLE, LANES), -1, jnp.int32)
+    height = r_ref.shape[0]
+    for c in range(height // LANES):
         tile = helper_ref[0] + nhelper * c
         ids = ids_ref[pl.ds(tile, 1), :]
-        out_ref[c : c + 1, :] = jnp.where(tile * LANES + lane < live_ref[0], ids, -1)
+        table = jnp.where(row == c, jnp.where(tile * LANES + lane < live_ref[0], ids, -1), table)
+    out_ref[pl.ds(0, height), :] = r_ref[...]
+    out_ref[pl.ds(height, TABLE), pl.ds(0, LANES)] = table.astype(jnp.float32).astype(jnp.bfloat16)
+
+
+def table_kernel(clusters_ref, count_ref, out_ref):
+    lane = lax.broadcasted_iota(jnp.int32, out_ref.shape, 1)
     qblocks = clusters_ref.shape[0]
     row = jnp.where(lane == qblocks, count_ref[0], 0)
     for k in range(qblocks):
         row = jnp.where(lane == k, clusters_ref[k], row)
-    out_ref[chunks : chunks + 1, :] = row
+    out_ref[...] = row
 
 
 def stage_kernel(*refs):
@@ -70,22 +76,21 @@
 def score_kernel(chunks, qblocks, first, wide, beta_ref, *refs):
     if first:
         (*given, out_ref, qv, info_out, q_list, ids_ref, other_ref, info, info_sem) = refs
-        q_refs, t_refs, given = given[:4], given[4:8], given[8:]
+        q_refs, t_refs, r_refs = given[:4], given[4:8], given[8:]
     else:
-        (info, qv, prev_ref, *given, out_ref, q_list, ids_ref, other_ref) = refs
-    r_refs, i_refs = given[: len(given) // 2], given[len(given) // 2 :]
+        (info, qv, prev_ref, *r_refs, out_ref, q_list, ids_ref, other_ref) = refs
     width = qv.shape[1]
     height = chunks * LANES
     if first:
         for s, t_ref in enumerate(t_refs):
-            info_out[s : s + 1, :] = t_ref[chunks : chunks + 1, :]
+            info_out[s : s + 1, :] = t_ref[0:1, :]
         copy = pltpu.make_async_copy(info_out, info, info_sem)
         copy.start()
 
-    for s, i_ref in enumerate(i_refs):
+    for s, r_ref in enumerate(r_refs):
+        table = r_ref[pl.ds(height, TABLE), pl.ds(0, LANES)].astype(jnp.float32)
         for c in range(chunks):
-            ids = i_ref[c : c + 1, :].astype(jnp.float32)
-            ids = jnp.broadcast_to(ids, (LANES, LANES)).T
+            ids = jnp.broadcast_to(table[c : c + 1, :], (LANES, LANES)).T
             rows = pl.ds(s * height + c * LANES, LANES)
             ids_ref[rows, :] = ids
             other_ref[rows, :] = jnp.where(ids < 0.0, DEAD, -4.0)
@@ -149,7 +154,7 @@
     lax.fori_loop(0, (q_count + wide - 1) // wide, query_blocks, 0)
 
 
-def score_call(chunks, qblocks, wide, beta, given, payloads, tables, first):
+def score_call(chunks, qblocks, wide, beta, given, payloads, first):
     width = payloads[0].shape[1]
     slots = 4 * qblocks
     height = chunks * LANES
@@ -158,7 +163,7 @@
     info_shape = jax.ShapeDtypeStruct((8, LANES), jnp.int32)
     spread = pltpu.VMEM((len(payloads) * height, LANES), jnp.float32)
     scratch = [pltpu.SMEM((slots, 2), jnp.int32), spread, spread]
-    specs = [VMEM] * (len(given) + len(payloads) + len(tables))
+    specs = [VMEM] * (len(given) + len(payloads))
     if first:
         scratch += [pltpu.SMEM((8, LANES), jnp.int32), pltpu.SemaphoreType.DMA]
     else:
@@ -171,7 +176,7 @@
         scratch_shapes=scratch,
         compiler_params=PARAMS,
         cost_estimate=cost(1, 1),
-    )(beta, *given, *payloads, *tables)
+    )(beta, *given, *payloads)
 
 
 def per_device(
@@ -195,30 +200,35 @@
     q_partner = swap(queries, "blk")
     by_chunk = references.reshape(chunks, nhelper, LANES, width)
     own = lax.dynamic_index_in_dim(by_chunk, helper, 1, keepdims=False)
-    own = own.reshape(chunks * LANES, width)
-
-    held, masks, mask = [own], [0], sources - 1
+    own = pl.pallas_call(
+        functools.partial(pack_kernel, nhelper),
+        out_shape=jax.ShapeDtypeStruct((chunks * LANES + TABLE, width), jnp.bfloat16),
+        in_specs=[SMEM] * 2 + [VMEM] * 2,
+        out_specs=VMEM,
+        compiler_params=PARAMS,
+        cost_estimate=cost(1, 1),
+    )(
+        helper[None],
+        ref_rows,
+        ref_cluster.reshape(tiles, LANES),
+        own.reshape(chunks * LANES, width),
+    )
+
+    held, mask = [own], sources - 1
     while mask:
         held = held + [trade(x, 2 * mask) for x in held]
-        masks, mask = masks + [m ^ mask for m in masks], mask // 2
+        mask //= 2
     q_helper = swap(queries, "helper")
 
     table = pl.pallas_call(
-        functools.partial(table_kernel, nhelper),
-        out_shape=jax.ShapeDtypeStruct((8 * ((chunks + 8) // 8), LANES), jnp.int32),
-        in_specs=[SMEM] * 4 + [VMEM],
+        table_kernel,
+        out_shape=jax.ShapeDtypeStruct((8, LANES), jnp.int32),
+        in_specs=[SMEM] * 2,
         out_specs=VMEM,
         compiler_params=PARAMS,
         cost_estimate=cost(1, 1),
-    )(
-        helper[None],
-        after(query_block_cluster, own),
-        block_count,
-        ref_rows,
-        ref_cluster.reshape(tiles, LANES),
-    )
-    r_tables = [table] + [trade(table, 2 * m) for m in masks[1:]]
-    q_tables = [table, swap(table, "helper"), swap(table, "blk"), swap_both(table)]
+    )(after(query_block_cluster, own), block_count)
+    q_tables = (table, swap(table, "helper"), swap(table, "blk"), swap_both(table))
     staged = pl.pallas_call(
         stage_kernel,
         out_shape=jax.ShapeDtypeStruct(queries.shape, queries.dtype),
@@ -227,7 +237,7 @@
         compiler_params=PARAMS,
         cost_estimate=cost(1, 1),
     )(queries)
-    q_both = swap(after(q_partner, staged, *held[1:-1], *r_tables, *q_tables), "helper")
+    q_both = swap(after(q_partner, staged, *held[1:-1], *q_tables), "helper")
 
     totals, packed, info = score_call(
         chunks,
@@ -236,7 +246,6 @@
         cluster_beta,
         (staged, q_helper, q_partner, q_both, *q_tables),
         held[:-1],
-        r_tables[:-1],
         True,
     )
     totals = score_call(
@@ -246,7 +255,6 @@
         cluster_beta,
         (info, packed, totals),
         held[-1:],
-        r_tables[-1:],
         False,
     )
     totals = totals.reshape(4, qblocks, LANES)

time: 51.4 us -> 45.4 us (0.88)
  waiting for transfers between devices: 25.7 us -> 21.4 us
  starting transfers between devices: 13.9 us -> 12 us
  Pallas kernels: 6 us -> 7.1 us
  local copies, waits for them, and re-layouts: 3.16 us -> 2.52 us
    ppermute x6 -> x3, waiting for transfers between devices: 20.8 us -> 11.1 us  [trade(): return lax.ppermute(value, 'blk', [(i, i ^ mask) for i in range(length)])]
    ppermute x7, waiting for transfers between devices: 3.93 us -> 10.2 us  [swap(): return lax.ppermute(value, axis, [(i, i ^ 1) for i in range(length)])]
    ppermute x6 -> x3, starting transfers between devices: 7.52 us -> 5.34 us  [trade(): return lax.ppermute(value, 'blk', [(i, i ^ mask) for i in range(length)])]
    pallas_call x2, Pallas kernels: 5.4 us -> 6.47 us  [score_call(): pl.pallas_call(functools.partial(score_kernel, chunks, qblocks, first, wi...]
    ppermute x2, waiting for transfers between devices: 0.91 us -> 0.09 us  [swap_both(): return lax.ppermute(value, ('blk', 'helper'), pairs)]
    unnamed x14 -> x16, local copies, waits for them, and re-layouts: 3.13 us -> 2.48 us
  transfers between devices with their start and end apart: 15 -> 12, of which waited for: 9 -> 7; matrix products, arithmetic and copies ran while one was open for 0% -> 0% of each run, Pallas kernels for 8% -> 11%
where the time goes in v12:
time: 45.4 us; the launch traced here: 45.2 us
  waiting for transfers between devices  21.4 us (47%)
  starting transfers between devices  12 us (26%)
  Pallas kernels  7.1 us (16%)
  local copies, waits for them, and re-layouts  2.52 us (6%)
  between operations  1.42 us (3%)
  other arithmetic  0.85 us (2%)
    ppermute x3, waiting for transfers between devices, trade(): return lax.ppermute(value, 'blk', [(i, i ^ mask) for i in range(length)])  11.1 us
    ppermute x7, waiting for transfers between devices, swap(): return lax.ppermute(value, axis, [(i, i ^ 1) for i in range(length)])  10.2 us
    pallas_call x2, Pallas kernels, score_call(): pl.pallas_call(functools.partial(score_kernel, chunks, qblocks, first, wi...  6.47 us
    ppermute x7, starting transfers between devices, swap(): return lax.ppermute(value, axis, [(i, i ^ 1) for i in range(length)])  5.5 us
    ppermute x3, starting transfers between devices, trade(): return lax.ppermute(value, 'blk', [(i, i ^ mask) for i in range(length)])  5.34 us
    unnamed x16, local copies, waits for them, and re-layouts  2.48 us
    ppermute x2, starting transfers between devices, swap_both(): return lax.ppermute(value, ('blk', 'helper'), pairs)  1.11 us
  transfers between devices with their start and end apart: 12, of which 7 were waited for; matrix products, arithmetic and copies ran while one was open for 0% of the time, Pallas kernels for 11%

profile of v12, /device:TPU:0, one launch (start us, length us, event | category | flops | bytes accessed | tf_op | source)
XLA Modules:
  0.0 45.2 jit_solution(3698430138299075111)
XLA Ops:
  0.0 3.0 %collective-permute-start.1 = (bf16[512,768]{1,0:T(8,128)(2,1)}, bf16[512,768]{1,0:T(8,128)(2,1)S(1)}, u32[]{:S(2)}, u32[]{:S(2)}) collective-permute-start(bf16[512,768]{1,0:T(8,128)(2,1)} %refs_0_.1), channel_id=1, source_target_pairs={{0,2},{2,0},{4,6},{6,4},{8,10},{10,8},{12,14},{14,12},{1,3},{3,1},... | collective-permute-start | bytes 2359304 | tf_op jit(solution)/shard_map/ppermute | solution.py:27
  3.8 0.7 %copy-done.3 = s32[512]{0:T(512)S(1)} copy-done((s32[512]{0:T(512)S(1)}, s32[512]{0:T(512)}, u32[]{:S(2)}) %copy-start.3) | copy-done | bytes 2072
  4.5 3.7 %collective-permute-start.2 = (bf16[272,768]{1,0:T(8,128)(2,1)S(1)}, bf16[272,768]{1,0:T(8,128)(2,1)S(1)}, u32[]{:S(2)}, u32[]{:S(2)}) collective-permute-start(bf16[272,768]{1,0:T(8,128)(2,1)S(1)} %shard_map.83.refs_8_), channel_id=1, source_target_pairs={{0,12},{2,14},{4,8},{6,10},{8,4},{10,6},{12,0},{14,2},{1,13},{3,15... | collective-permute-start | bytes 1253384 | tf_op jit(solution)/shard_map/ppermute | solution.py:22
  8.8 0.6 %copy-done.5 = s32[4]{0:T(128)S(1)} copy-done((s32[4]{0:T(128)S(1)}, s32[4]{0:T(128)}, u32[]{:S(2)}) %copy-start.5) | copy-done | bytes 40
  9.4 0.5 %shard_map.84.refs_4_ = s32[8,128]{1,0:T(8,128)S(1)} custom-call(s32[4]{0:T(128)S(1)} %copy-done.5, s32[1]{0:T(128)S(6)} %copy.12.count_ref), custom_call_target="tpu_custom_call" | custom-call | flops 1 | bytes 1 | tf_op jit(solution)/shard_map/pallas_call | solution.py:223
  10.0 0.1 collective-permute-start.4
  10.1 0.6 %collective-permute-start.5 = (s32[8,128]{1,0:T(8,128)S(1)}, s32[8,128]{1,0:T(8,128)S(1)}, u32[]{:S(2)}, u32[]{:S(2)}) collective-permute-start(s32[8,128]{1,0:T(8,128)S(1)} %shard_map.84.refs_4_), channel_id=1, source_target_pairs={{0,2},{2,0},{4,6},{6,4},{8,10},{10,8},{12,14},{14,12},{1,3},{3,1},... | collective-permute-start | bytes 12296 | tf_op jit(solution)/shard_map/ppermute | solution.py:27
  10.7 0.6 %collective-permute-done.4.refs_5_ = s32[8,128]{1,0:T(8,128)S(1)} collective-permute-done((s32[8,128]{1,0:T(8,128)S(1)}, s32[8,128]{1,0:T(8,128)S(1)}, u32[]{:S(2)}, u32[]{:S(2)}) %collective-permute-start.4) | collective-permute-done | bytes 4128 | tf_op jit(solution)/shard_map/ppermute | solution.py:27
  11.2 0.7 %collective-permute-start.6 = (s32[8,128]{1,0:T(8,128)S(1)}, s32[8,128]{1,0:T(8,128)S(1)}, u32[]{:S(2)}, u32[]{:S(2)}) collective-permute-start(s32[8,128]{1,0:T(8,128)S(1)} %shard_map.84.refs_4_), channel_id=1, source_target_pairs={{0,3},{1,2},{2,1},{3,0},{4,7},{5,6},{6,5},{7,4},{8,11},{9,10},{10,... | collective-permute-start | bytes 12296 | tf_op jit(solution)/shard_map/ppermute | solution.py:33
  11.9 1.1 %copy-done.1 = bf16[512,768]{1,0:T(8,128)(2,1)S(1)} copy-done((bf16[512,768]{1,0:T(8,128)(2,1)S(1)}, bf16[512,768]{1,0:T(8,128)(2,1)}, u32[]{:S(2)}) %copy-start.1) | copy-done | bytes 786456
  13.2 7.8 %collective-permute-done.5.refs_6_ = s32[8,128]{1,0:T(8,128)S(1)} collective-permute-done((s32[8,128]{1,0:T(8,128)S(1)}, s32[8,128]{1,0:T(8,128)S(1)}, u32[]{:S(2)}, u32[]{:S(2)}) %collective-permute-start.5) | collective-permute-done | bytes 4128 | tf_op jit(solution)/shard_map/ppermute | solution.py:27
  21.0 5.6 %collective-permute-done.3.refs_10_ = bf16[272,768]{1,0:T(8,128)(2,1)S(1)} collective-permute-done((bf16[272,768]{1,0:T(8,128)(2,1)S(1)}, bf16[272,768]{1,0:T(8,128)(2,1)S(1)}, u32[]{:S(2)}, u32[]{:S(2)}) %collective-permute-start.3) | collective-permute-done | bytes 417824 | tf_op jit(solution)/shard_map/ppermute | solution.py:22
  26.6 1.7 %collective-permute-start.8 = (bf16[272,768]{1,0:T(8,128)(2,1)S(1)}, bf16[272,768]{1,0:T(8,128)(2,1)S(1)}, u32[]{:S(2)}, u32[]{:S(2)}) collective-permute-start(bf16[272,768]{1,0:T(8,128)(2,1)S(1)} %collective-permute-done.2.refs_9_), channel_id=1, source_target_pairs={{0,4},{2,6},{4,0},{6,2},{8,12},{10,14},{12,8},{14,10},{1,5},{3,7},... | collective-permute-start | bytes 1253384 | tf_op jit(solution)/shard_map/ppermute | solution.py:22
  28.2 0.6 %collective-permute-done.7.refs_3_ = bf16[512,768]{1,0:T(8,128)(2,1)S(1)} collective-permute-done((bf16[512,768]{1,0:T(8,128)(2,1)S(1)}, bf16[512,768]{1,0:T(8,128)(2,1)S(1)}, u32[]{:S(2)}, u32[]{:S(2)}) %collective-permute-start.7) | collective-permute-done | bytes 786464 | tf_op jit(solution)/shard_map/ppermute | solution.py:27
  28.8 4.3 %shard_map.85 = (f32[16,128]{1,0:T(8,128)S(1)}, bf16[2048,768]{1,0:T(8,128)(2,1)S(1)}, s32[8,128]{1,0:T(8,128)S(1)}) custom-call(f32[64]{0:T(128)S(1)} %copy-done.4, bf16[512,768]{1,0:T(8,128)(2,1)S(1)} %shard_map.82.refs_0_, bf16[512,768]{1,0:T(8,128)(2,1)S(1)} %collective-permute-done.refs_1_, bf16[512,768]{1,0:T(8,128)(2,1)S(1)} %collective-permute-done.1.refs_2_, ...), custom_call_target="tpu_custom_call" | custom-call | flops 1 | bytes 1 | tf_op jit(solution)/shard_map/pallas_call | solution.py:171
  33.1 5.5 %collective-permute-done.8.refs_3_ = bf16[272,768]{1,0:T(8,128)(2,1)S(1)} collective-permute-done((bf16[272,768]{1,0:T(8,128)(2,1)S(1)}, bf16[272,768]{1,0:T(8,128)(2,1)S(1)}, u32[]{:S(2)}, u32[]{:S(2)}) %collective-permute-start.8) | collective-permute-done | bytes 417824 | tf_op jit(solution)/shard_map/ppermute | solution.py:22
  38.6 2.2 %shard_map.86 = f32[16,128]{1,0:T(8,128)S(1)} custom-call(f32[64]{0:T(128)S(1)} %copy-done.4, s32[8,128]{1,0:T(8,128)S(1)} %get-tuple-element.12.refs_0_, bf16[2048,768]{1,0:T(8,128)(2,1)S(1)} %get-tuple-element.13.refs_1_, f32[16,128]{1,0:T(8,128)S(1)} %get-tuple-element.14.refs_2_, bf16[272,768]{1,0:T(8,128)(2,1)S(1)} %collective-permute-done.8.refs_3_), custom_call_target="tpu_custom_call" | custom-call | flops 1 | bytes 1 | tf_op jit(solution)/shard_map/pallas_call | solution.py:171
  40.8 0.7 %collective-permute-start.10 = (f32[4,128]{1,0:T(4,128)S(1)}, f32[4,128]{1,0:T(4,128)S(1)}, u32[]{:S(2)}, u32[]{:S(2)}) collective-permute-start(f32[4,128]{1,0:T(4,128)S(1)} %get-tuple-element.17), channel_id=1, source_target_pairs={{0,2},{2,0},{4,6},{6,4},{8,10},{10,8},{12,14},{14,12},{1,3},{3,1},... | collective-permute-start | bytes 6152 | tf_op jit(solution)/shard_map/ppermute | solution.py:27
  41.6 0.4 collective-permute-start.11
  42.0 1.1 %collective-permute-start.9 = (f32[4,128]{1,0:T(4,128)S(1)}, f32[4,128]{1,0:T(4,128)S(1)}, u32[]{:S(2)}, u32[]{:S(2)}) collective-permute-start(f32[4,128]{1,0:T(4,128)S(1)} %get-tuple-element.15), channel_id=1, source_target_pairs={{0,1},{1,0},{2,3},{3,2},{4,5},{5,4},{6,7},{7,6},{8,9},{9,8},{10,11... | collective-permute-start | bytes 6152 | tf_op jit(solution)/shard_map/ppermute | solution.py:27
  43.0 0.2 select_reduce_fusion
  43.2 1.2 %collective-permute-done.10 = f32[4,128]{1,0:T(4,128)S(1)} collective-permute-done((f32[4,128]{1,0:T(4,128)S(1)}, f32[4,128]{1,0:T(4,128)S(1)}, u32[]{:S(2)}, u32[]{:S(2)}) %collective-permute-start.10) | collective-permute-done | bytes 2080 | tf_op jit(solution)/shard_map/ppermute | solution.py:27
  44.5 0.1 collective-permute-done.11
  44.6 0.7 %log-plus-one_bitcast_fusion = f32[512]{0:T(512)} fusion(f32[4,128]{1,0:T(4,128)S(1)} %collective-permute-done.11, f32[4,128]{1,0:T(4,128)S(1)} %collective-permute-done.10, f32[4,128]{1,0:T(4,128)S(1)} %collective-permute-done.9, f32[16,128]{1,0:T(8,128)S(1)} %shard_map.86, f32[4]{0:T(128)S(1)} %convert_element_type.7), kind=kLoop, calls=%fused_computation.4 | loop fusion | flops 2048 | bytes 10256 | tf_op jit(solution)/shard_map/reshape | solution.py:266
  (26 shorter events, 0.2 us)
Async XLA Ops:
  0.0 3.7 %copy-start = (bf16[512,768]{1,0:T(8,128)(2,1)S(1)}, bf16[512,768]{1,0:T(8,128)(2,1)}, u32[]{:S(2)}) copy-start(bf16[512,768]{1,0:T(8,128)(2,1)} %param.11) | copy-start | bytes 2359300
  0.0 20.9 %copy-start.2 = (bf16[512,768]{1,0:T(8,128)(2,1)S(1)}, bf16[512,768]{1,0:T(8,128)(2,1)}, u32[]{:S(2)}) copy-start(bf16[512,768]{1,0:T(8,128)(2,1)} %refs_0_.1) | copy-start | bytes 2359300
  0.0 28.8 %copy-start.4 = (f32[64]{0:T(128)S(1)}, f32[64]{0:T(128)}, u32[]{:S(2)}) copy-start(f32[64]{0:T(128)} %beta_ref.3) | copy-start | bytes 772
  0.0 26.5 %collective-permute-start.1 = (bf16[512,768]{1,0:T(8,128)(2,1)}, bf16[512,768]{1,0:T(8,128)(2,1)S(1)}, u32[]{:S(2)}, u32[]{:S(2)}) collective-permute-start(bf16[512,768]{1,0:T(8,128)(2,1)} %refs_0_.1), channel_id=1, source_target_pairs={{0,2},{2,0},{4,6},{6,4},{8,10},{10,8},{12,14},{14,12},{1,3},{3,1},... | collective-permute-start | bytes 2359304 | tf_op jit(solution)/shard_map/ppermute | solution.py:27
  3.7 0.7 %copy-start.3 = (s32[512]{0:T(512)S(1)}, s32[512]{0:T(512)}, u32[]{:S(2)}) copy-start(s32[512]{0:T(512)} %param.12) | copy-start | bytes 6148
  4.5 16.5 %collective-permute-start.2 = (bf16[272,768]{1,0:T(8,128)(2,1)S(1)}, bf16[272,768]{1,0:T(8,128)(2,1)S(1)}, u32[]{:S(2)}, u32[]{:S(2)}) collective-permute-start(bf16[272,768]{1,0:T(8,128)(2,1)S(1)} %shard_map.83.refs_8_), channel_id=1, source_target_pairs={{0,12},{2,14},{4,8},{6,10},{8,4},{10,6},{12,0},{14,2},{1,13},{3,15... | collective-permute-start | bytes 1253384 | tf_op jit(solution)/shard_map/ppermute | solution.py:22
  8.1 18.4 %collective-permute-start.3 = (bf16[272,768]{1,0:T(8,128)(2,1)S(1)}, bf16[272,768]{1,0:T(8,128)(2,1)S(1)}, u32[]{:S(2)}, u32[]{:S(2)}) collective-permute-start(bf16[272,768]{1,0:T(8,128)(2,1)S(1)} %shard_map.83.refs_8_), channel_id=1, source_target_pairs={{0,4},{2,6},{4,0},{6,2},{8,12},{10,14},{12,8},{14,10},{1,5},{3,7},... | collective-permute-start | bytes 1253384 | tf_op jit(solution)/shard_map/ppermute | solution.py:22
  8.8 0.7 %copy-start.5 = (s32[4]{0:T(128)S(1)}, s32[4]{0:T(128)}, u32[]{:S(2)}) copy-start(s32[4]{0:T(128)} %clusters_ref) | copy-start | bytes 52
  10.0 1.2 %collective-permute-start.4 = (s32[8,128]{1,0:T(8,128)S(1)}, s32[8,128]{1,0:T(8,128)S(1)}, u32[]{:S(2)}, u32[]{:S(2)}) collective-permute-start(s32[8,128]{1,0:T(8,128)S(1)} %shard_map.84.refs_4_), channel_id=1, source_target_pairs={{0,1},{1,0},{2,3},{3,2},{4,5},{5,4},{6,7},{7,6},{8,9},{9,8},{10,11... | collective-permute-start | bytes 12296 | tf_op jit(solution)/shard_map/ppermute | solution.py:27
  10.1 10.8 %collective-permute-start.5 = (s32[8,128]{1,0:T(8,128)S(1)}, s32[8,128]{1,0:T(8,128)S(1)}, u32[]{:S(2)}, u32[]{:S(2)}) collective-permute-start(s32[8,128]{1,0:T(8,128)S(1)} %shard_map.84.refs_4_), channel_id=1, source_target_pairs={{0,2},{2,0},{4,6},{6,4},{8,10},{10,8},{12,14},{14,12},{1,3},{3,1},... | collective-permute-start | bytes 12296 | tf_op jit(solution)/shard_map/ppermute | solution.py:27
  11.2 9.7 %collective-permute-start.6 = (s32[8,128]{1,0:T(8,128)S(1)}, s32[8,128]{1,0:T(8,128)S(1)}, u32[]{:S(2)}, u32[]{:S(2)}) collective-permute-start(s32[8,128]{1,0:T(8,128)S(1)} %shard_map.84.refs_4_), channel_id=1, source_target_pairs={{0,3},{1,2},{2,1},{3,0},{4,7},{5,6},{6,5},{7,4},{8,11},{9,10},{10,... | collective-permute-start | bytes 12296 | tf_op jit(solution)/shard_map/ppermute | solution.py:33
  11.9 1.1 %copy-start.1 = (bf16[512,768]{1,0:T(8,128)(2,1)S(1)}, bf16[512,768]{1,0:T(8,128)(2,1)}, u32[]{:S(2)}) copy-start(bf16[512,768]{1,0:T(8,128)(2,1)} %refs_0_.1) | copy-start | bytes 2359300
  13.1 29.9 %copy-start.6 = (s32[4]{0:T(128)S(1)}, s32[4]{0:T(128)}, u32[]{:S(2)}) copy-start(s32[4]{0:T(128)} %clusters_ref) | copy-start | bytes 52
  13.1 29.9 %copy-start.7 = (s32[64]{0:T(128)S(1)}, s32[64]{0:T(128)}, u32[]{:S(2)}) copy-start(s32[64]{0:T(128)} %param.15) | copy-start | bytes 772
  20.9 7.3 %collective-permute-start = (bf16[512,768]{1,0:T(8,128)(2,1)S(1)}, bf16[512,768]{1,0:T(8,128)(2,1)S(1)}, u32[]{:S(2)}, u32[]{:S(2)}) collective-permute-start(bf16[512,768]{1,0:T(8,128)(2,1)S(1)} %copy-done.2), channel_id=1, source_target_pairs={{0,1},{1,0},{2,3},{3,2},{4,5},{5,4},{6,7},{7,6},{8,9},{9,8},{10,11... | collective-permute-start | bytes 2359304 | tf_op jit(solution)/shard_map/ppermute | solution.py:27
  26.6 2.3 %collective-permute-start.7 = (bf16[512,768]{1,0:T(8,128)(2,1)S(1)}, bf16[512,768]{1,0:T(8,128)(2,1)S(1)}, u32[]{:S(2)}, u32[]{:S(2)}) collective-permute-start(bf16[512,768]{1,0:T(8,128)(2,1)S(1)} %collective-permute-done.1.refs_2_), channel_id=1, source_target_pairs={{0,1},{1,0},{2,3},{3,2},{4,5},{5,4},{6,7},{7,6},{8,9},{9,8},{10,11... | collective-permute-start | bytes 2359304 | tf_op jit(solution)/shard_map/ppermute | solution.py:27
  26.6 12.0 %collective-permute-start.8 = (bf16[272,768]{1,0:T(8,128)(2,1)S(1)}, bf16[272,768]{1,0:T(8,128)(2,1)S(1)}, u32[]{:S(2)}, u32[]{:S(2)}) collective-permute-start(bf16[272,768]{1,0:T(8,128)(2,1)S(1)} %collective-permute-done.2.refs_9_), channel_id=1, source_target_pairs={{0,4},{2,6},{4,0},{6,2},{8,12},{10,14},{12,8},{14,10},{1,5},{3,7},... | collective-permute-start | bytes 1253384 | tf_op jit(solution)/shard_map/ppermute | solution.py:22
  40.8 3.7 %collective-permute-start.10 = (f32[4,128]{1,0:T(4,128)S(1)}, f32[4,128]{1,0:T(4,128)S(1)}, u32[]{:S(2)}, u32[]{:S(2)}) collective-permute-start(f32[4,128]{1,0:T(4,128)S(1)} %get-tuple-element.17), channel_id=1, source_target_pairs={{0,2},{2,0},{4,6},{6,4},{8,10},{10,8},{12,14},{14,12},{1,3},{3,1},... | collective-permute-start | bytes 6152 | tf_op jit(solution)/shard_map/ppermute | solution.py:27
  41.6 3.0 %collective-permute-start.11 = (f32[4,128]{1,0:T(4,128)S(1)}, f32[4,128]{1,0:T(4,128)S(1)}, u32[]{:S(2)}, u32[]{:S(2)}) collective-permute-start(f32[4,128]{1,0:T(4,128)S(1)} %get-tuple-element.16), channel_id=1, source_target_pairs={{0,3},{1,2},{2,1},{3,0},{4,7},{5,6},{6,5},{7,4},{8,11},{9,10},{10,... | collective-permute-start | bytes 6152 | tf_op jit(solution)/shard_map/ppermute | solution.py:33
  42.0 2.6 %collective-permute-start.9 = (f32[4,128]{1,0:T(4,128)S(1)}, f32[4,128]{1,0:T(4,128)S(1)}, u32[]{:S(2)}, u32[]{:S(2)}) collective-permute-start(f32[4,128]{1,0:T(4,128)S(1)} %get-tuple-element.15), channel_id=1, source_target_pairs={{0,1},{1,0},{2,3},{3,2},{4,5},{5,4},{6,7},{7,6},{8,9},{9,8},{10,11... | collective-permute-start | bytes 6152 | tf_op jit(solution)/shard_map/ppermute | solution.py:27

commit v13 on v12

--- a/solution.py
+++ b/solution.py
@@ -9,7 +9,7 @@
 from jax.sharding import PartitionSpec as P
 
 LANES = 128
-TABLE = 16
+TABLE = 8
 LOG2E = 1.4426950408889634
 DEAD = -1.0e30
 SMEM = pl.BlockSpec(memory_space=pltpu.SMEM)
@@ -73,13 +73,17 @@
         out[...] = source[...]
 
 
-def score_kernel(chunks, qblocks, first, wide, beta_ref, *refs):
+def score_kernel(chunks, qblocks, pieces, first, wide, beta_ref, *refs):
     if first:
         (*given, out_ref, qv, info_out, q_list, ids_ref, other_ref, info, info_sem) = refs
-        q_refs, t_refs, r_refs = given[:4], given[4:8], given[8:]
+        q_refs = []
+        for n in pieces:
+            q_refs.append(given[:n])
+            given = given[n:]
+        t_refs, r_refs = given[:4], given[4:]
     else:
         (info, qv, prev_ref, *r_refs, out_ref, q_list, ids_ref, other_ref) = refs
-    width = qv.shape[1]
+    width = qv.shape[0]
     height = chunks * LANES
     if first:
         for s, t_ref in enumerate(t_refs):
@@ -102,13 +106,21 @@
         blocks = info[source, qblocks]
 
         def one_block(block, carry, source=source, q_count=q_count):
-            if first:
-                qv[rows_of(q_count + block), :] = q_refs[source][rows_of(block), :]
             q_list[q_count + block, 0] = source * qblocks + block
             q_list[q_count + block, 1] = info[source, block]
             return carry
 
         lax.fori_loop(0, blocks, one_block, 0)
+        start = 0
+        for piece in q_refs[source] if first else ():
+            each = piece.shape[0] // LANES
+
+            def move(block, carry, place=q_count + start, piece=piece):
+                qv[:, rows_of(place + block)] = piece[rows_of(block), :].T
+                return carry
+
+            lax.fori_loop(0, jnp.clip(blocks - start, 0, each), move, 0)
+            start += each
         q_count = q_count + blocks
 
     factor = LOG2E / math.sqrt(width)
@@ -130,8 +142,8 @@
             for pair in range(wide // 2):
                 score = lax.dot_general(
                     tile,
-                    qv[rows_of(wide * group + 2 * pair, 2), :],
-                    (((1,), (1,)), ((), ())),
+                    qv[:, rows_of(wide * group + 2 * pair, 2)],
+                    (((1,), (0,)), ((), ())),
                     preferred_element_type=jnp.float32,
                 )
                 for half in range(2):
@@ -154,12 +166,12 @@
     lax.fori_loop(0, (q_count + wide - 1) // wide, query_blocks, 0)
 
 
-def score_call(chunks, qblocks, wide, beta, given, payloads, first):
+def score_call(chunks, qblocks, pieces, wide, beta, given, payloads, first):
     width = payloads[0].shape[1]
     slots = 4 * qblocks
     height = chunks * LANES
     totals_shape = jax.ShapeDtypeStruct((slots, LANES), jnp.float32)
-    packed_shape = jax.ShapeDtypeStruct((slots * LANES, width), jnp.bfloat16)
+    packed_shape = jax.ShapeDtypeStruct((width, slots * LANES), jnp.bfloat16)
     info_shape = jax.ShapeDtypeStruct((8, LANES), jnp.int32)
     spread = pltpu.VMEM((len(payloads) * height, LANES), jnp.float32)
     scratch = [pltpu.SMEM((slots, 2), jnp.int32), spread, spread]
@@ -169,7 +181,7 @@
     else:
         specs[0] = SMEM
     return pl.pallas_call(
-        functools.partial(score_kernel, chunks, qblocks, first, wide),
+        functools.partial(score_kernel, chunks, qblocks, pieces, first, wide),
         out_shape=(totals_shape, packed_shape, info_shape) if first else totals_shape,
         in_specs=[SMEM] + specs,
         out_specs=(VMEM, VMEM, VMEM) if first else VMEM,
@@ -237,20 +249,26 @@
         compiler_params=PARAMS,
         cost_estimate=cost(1, 1),
     )(queries)
-    q_both = swap(after(q_partner, staged, *held[1:-1], *q_tables), "helper")
+    q_partner = after(q_partner, staged, *held[1:-1], *q_tables)
+    half = qblocks // 2 * LANES
+    q_both = [swap(q_partner[:half], "helper"), swap(q_partner[half:], "helper")]
+    queries = (staged, q_helper, q_partner, *q_both)
+    pieces = (1, 1, 1, 2)
 
     totals, packed, info = score_call(
         chunks,
         qblocks,
+        pieces,
         2,
         cluster_beta,
-        (staged, q_helper, q_partner, q_both, *q_tables),
+        (*queries, *q_tables),
         held[:-1],
         True,
     )
     totals = score_call(
         chunks,
         qblocks,
+        pieces,
         4,
         cluster_beta,
         (info, packed, totals),
@@ -263,7 +281,7 @@
     onehot = query_block_cluster[:, None] == columns[None, :]
     sizes = jnp.sum(jnp.where(onehot, cluster_member_count[None, :], 0), axis=1)
     density = jnp.log1p(total / sizes.astype(jnp.float32)[:, None])
-    return density.reshape(queries.shape[0])
+    return density.reshape(qblocks * LANES)
 
 
 def solution(mesh):

time: 45.4 us -> 42 us (0.925)
  waiting for transfers between devices: 21.4 us -> 14.4 us
  starting transfers between devices: 12 us -> 13.8 us
  Pallas kernels: 7.1 us -> 8.74 us
    ppermute x3, waiting for transfers between devices: 11.1 us -> 1.28 us  [trade(): return lax.ppermute(value, 'blk', [(i, i ^ mask) for i in range(length)])]
    ppermute x7 -> x8, waiting for transfers between devices: 10.2 us -> 13.2 us  [swap(): return lax.ppermute(value, axis, [(i, i ^ 1) for i in range(length)])]
    pallas_call x2, Pallas kernels: 6.47 us -> 8.11 us  [score_call(): pl.pallas_call(functools.partial(score_kernel, chunks, qblocks, pieces, f...]
    ppermute x3, starting transfers between devices: 5.34 us -> 6.92 us  [trade(): return lax.ppermute(value, 'blk', [(i, i ^ mask) for i in range(length)])]
    ppermute x2, starting transfers between devices: 1.11 us -> 1.77 us  [swap_both(): return lax.ppermute(value, ('blk', 'helper'), pairs)]
    ppermute x7 -> x8, starting transfers between devices: 5.5 us -> 5.09 us  [swap(): return lax.ppermute(value, axis, [(i, i ^ 1) for i in range(length)])]
    unnamed x16 -> x12, local copies, waits for them, and re-layouts: 2.48 us -> 2.47 us
  transfers between devices with their start and end apart: 12 -> 13, of which waited for: 7 -> 7; matrix products, arithmetic and copies ran while one was open for 0% -> 1% of each run, Pallas kernels for 11% -> 16%
where the time goes in v13:
time: 42 us; the launch traced here: 41.8 us
  waiting for transfers between devices  14.4 us (34%)
  starting transfers between devices  13.8 us (33%)
  Pallas kernels  8.74 us (21%)
  local copies, waits for them, and re-layouts  2.56 us (6%)
  between operations  1.42 us (3%)
  other arithmetic  0.85 us (2%)
    ppermute x8, waiting for transfers between devices, swap(): return lax.ppermute(value, axis, [(i, i ^ 1) for i in range(length)])  13.2 us
    pallas_call x2, Pallas kernels, score_call(): pl.pallas_call(functools.partial(score_kernel, chunks, qblocks, pieces, f...  8.11 us
    ppermute x3, starting transfers between devices, trade(): return lax.ppermute(value, 'blk', [(i, i ^ mask) for i in range(length)])  6.92 us
    ppermute x8, starting transfers between devices, swap(): return lax.ppermute(value, axis, [(i, i ^ 1) for i in range(length)])  5.09 us
    unnamed x12, local copies, waits for them, and re-layouts  2.47 us
    ppermute x2, starting transfers between devices, swap_both(): return lax.ppermute(value, ('blk', 'helper'), pairs)  1.77 us
    ppermute x3, waiting for transfers between devices, trade(): return lax.ppermute(value, 'blk', [(i, i ^ mask) for i in range(length)])  1.28 us
  transfers between devices with their start and end apart: 13, of which 7 were waited for; matrix products, arithmetic and copies ran while one was open for 1% of the time, Pallas kernels for 16%

profile of v13, /device:TPU:0, one launch (start us, length us, event | category | flops | bytes accessed | tf_op | source)
XLA Modules:
  0.0 41.8 jit_solution(1381197244010584249)
XLA Ops:
  0.0 3.0 %collective-permute-start.1 = (bf16[512,768]{1,0:T(8,128)(2,1)}, bf16[512,768]{1,0:T(8,128)(2,1)S(1)}, u32[]{:S(2)}, u32[]{:S(2)}) collective-permute-start(bf16[512,768]{1,0:T(8,128)(2,1)} %refs_0_.1), channel_id=1, source_target_pairs={{0,2},{2,0},{4,6},{6,4},{8,10},{10,8},{12,14},{14,12},{1,3},{3,1},... | collective-permute-start | bytes 2359304 | tf_op jit(solution)/shard_map/ppermute | solution.py:27
  3.7 0.7 %copy-done.2 = s32[512]{0:T(512)S(1)} copy-done((s32[512]{0:T(512)S(1)}, s32[512]{0:T(512)}, u32[]{:S(2)}) %copy-start.2) | copy-done | bytes 2072
  4.4 3.7 %collective-permute-start.2 = (bf16[264,768]{1,0:T(8,128)(2,1)S(1)}, bf16[264,768]{1,0:T(8,128)(2,1)S(1)}, u32[]{:S(2)}, u32[]{:S(2)}) collective-permute-start(bf16[264,768]{1,0:T(8,128)(2,1)S(1)} %shard_map.83.refs_9_), channel_id=1, source_target_pairs={{0,12},{2,14},{4,8},{6,10},{8,4},{10,6},{12,0},{14,2},{1,13},{3,15... | collective-permute-start | bytes 1216520 | tf_op jit(solution)/shard_map/ppermute | solution.py:22
  8.7 0.6 %copy-done.4 = s32[4]{0:T(128)S(1)} copy-done((s32[4]{0:T(128)S(1)}, s32[4]{0:T(128)}, u32[]{:S(2)}) %copy-start.4) | copy-done | bytes 40
  9.4 0.5 %shard_map.84.refs_5_ = s32[8,128]{1,0:T(8,128)S(1)} custom-call(s32[4]{0:T(128)S(1)} %copy-done.4, s32[1]{0:T(128)S(6)} %copy.12.count_ref), custom_call_target="tpu_custom_call" | custom-call | flops 1 | bytes 1 | tf_op jit(solution)/shard_map/pallas_call | solution.py:235
  9.9 0.6 %collective-permute-start.4 = (s32[8,128]{1,0:T(8,128)S(1)}, s32[8,128]{1,0:T(8,128)S(1)}, u32[]{:S(2)}, u32[]{:S(2)}) collective-permute-start(s32[8,128]{1,0:T(8,128)S(1)} %shard_map.84.refs_5_), channel_id=1, source_target_pairs={{0,1},{1,0},{2,3},{3,2},{4,5},{5,4},{6,7},{7,6},{8,9},{9,8},{10,11... | collective-permute-start | bytes 12296 | tf_op jit(solution)/shard_map/ppermute | solution.py:27
  10.5 0.8 %collective-permute-done.4.refs_6_ = s32[8,128]{1,0:T(8,128)S(1)} collective-permute-done((s32[8,128]{1,0:T(8,128)S(1)}, s32[8,128]{1,0:T(8,128)S(1)}, u32[]{:S(2)}, u32[]{:S(2)}) %collective-permute-start.4) | collective-permute-done | bytes 4128 | tf_op jit(solution)/shard_map/ppermute | solution.py:27
  11.3 0.5 %collective-permute-start.5 = (s32[8,128]{1,0:T(8,128)S(1)}, s32[8,128]{1,0:T(8,128)S(1)}, u32[]{:S(2)}, u32[]{:S(2)}) collective-permute-start(s32[8,128]{1,0:T(8,128)S(1)} %shard_map.84.refs_5_), channel_id=1, source_target_pairs={{0,2},{2,0},{4,6},{6,4},{8,10},{10,8},{12,14},{14,12},{1,3},{3,1},... | collective-permute-start | bytes 12296 | tf_op jit(solution)/shard_map/ppermute | solution.py:27
  11.8 9.0 %collective-permute-done.5.refs_7_ = s32[8,128]{1,0:T(8,128)S(1)} collective-permute-done((s32[8,128]{1,0:T(8,128)S(1)}, s32[8,128]{1,0:T(8,128)S(1)}, u32[]{:S(2)}, u32[]{:S(2)}) %collective-permute-start.5) | collective-permute-done | bytes 4128 | tf_op jit(solution)/shard_map/ppermute | solution.py:27
  20.8 0.3 collective-permute-start.6
  21.1 1.1 %copy-done.1 = bf16[512,768]{1,0:T(8,128)(2,1)S(1)} copy-done((bf16[512,768]{1,0:T(8,128)(2,1)S(1)}, bf16[512,768]{1,0:T(8,128)(2,1)}, u32[]{:S(2)}) %copy-start.1) | copy-done | bytes 786456
  22.3 3.2 %collective-permute-start.9 = (bf16[264,768]{1,0:T(8,128)(2,1)S(1)}, bf16[264,768]{1,0:T(8,128)(2,1)S(1)}, u32[]{:S(2)}, u32[]{:S(2)}) collective-permute-start(bf16[264,768]{1,0:T(8,128)(2,1)S(1)} %collective-permute-done.2.refs_10_), channel_id=1, source_target_pairs={{0,4},{2,6},{4,0},{6,2},{8,12},{10,14},{12,8},{14,10},{1,5},{3,7},... | collective-permute-start | bytes 1216520 | tf_op jit(solution)/shard_map/ppermute | solution.py:22
  25.6 0.4 collective-permute-done.3.refs_11_
  26.1 0.5 %collective-permute-start.8 = (bf16[256,768]{1,0:T(8,128)(2,1)S(1)}, bf16[256,768]{1,0:T(8,128)(2,1)S(1)}, u32[]{:S(2)}, u32[]{:S(2)}) collective-permute-start(bf16[256,768]{1,0:T(8,128)(2,1)S(1)} %get-tuple-element.15), channel_id=1, source_target_pairs={{0,1},{1,0},{2,3},{3,2},{4,5},{5,4},{6,7},{7,6},{8,9},{9,8},{10,11... | collective-permute-start | bytes 1179656 | tf_op jit(solution)/shard_map/ppermute | solution.py:27
  26.6 1.2 %collective-permute-done.7.refs_3_ = bf16[256,768]{1,0:T(8,128)(2,1)S(1)} collective-permute-done((bf16[256,768]{1,0:T(8,128)(2,1)S(1)}, bf16[256,768]{1,0:T(8,128)(2,1)S(1)}, u32[]{:S(2)}, u32[]{:S(2)}) %collective-permute-start.7) | collective-permute-done | bytes 393248 | tf_op jit(solution)/shard_map/ppermute | solution.py:27
  27.8 0.6 %collective-permute-done.8.refs_4_ = bf16[256,768]{1,0:T(8,128)(2,1)S(1)} collective-permute-done((bf16[256,768]{1,0:T(8,128)(2,1)S(1)}, bf16[256,768]{1,0:T(8,128)(2,1)S(1)}, u32[]{:S(2)}, u32[]{:S(2)}) %collective-permute-start.8) | collective-permute-done | bytes 393248 | tf_op jit(solution)/shard_map/ppermute | solution.py:27
  28.4 5.9 %shard_map.85 = (f32[16,128]{1,0:T(8,128)S(1)}, bf16[768,2048]{1,0:T(8,128)(2,1)S(1)}, s32[8,128]{1,0:T(8,128)S(1)}) custom-call(f32[64]{0:T(128)S(1)} %copy-done.3, bf16[512,768]{1,0:T(8,128)(2,1)S(1)} %shard_map.82.refs_0_, bf16[512,768]{1,0:T(8,128)(2,1)S(1)} %collective-permute-done.refs_1_, bf16[512,768]{1,0:T(8,128)(2,1)S(1)} %collective-permute-done.1.refs_2_, ...), custom_call_target="tpu_custom_call" | custom-call | flops 1 | bytes 1 | tf_op jit(solution)/shard_map/pallas_call | solution.py:183
  34.3 0.9 %collective-permute-done.9.refs_3_ = bf16[264,768]{1,0:T(8,128)(2,1)S(1)} collective-permute-done((bf16[264,768]{1,0:T(8,128)(2,1)S(1)}, bf16[264,768]{1,0:T(8,128)(2,1)S(1)}, u32[]{:S(2)}, u32[]{:S(2)}) %collective-permute-start.9) | collective-permute-done | bytes 405536 | tf_op jit(solution)/shard_map/ppermute | solution.py:22
  35.2 2.2 %shard_map.86 = f32[16,128]{1,0:T(8,128)S(1)} custom-call(f32[64]{0:T(128)S(1)} %copy-done.3, s32[8,128]{1,0:T(8,128)S(1)} %get-tuple-element.12.refs_0_, bf16[768,2048]{1,0:T(8,128)(2,1)S(1)} %get-tuple-element.13.refs_1_, f32[16,128]{1,0:T(8,128)S(1)} %get-tuple-element.14.refs_2_, bf16[264,768]{1,0:T(8,128)(2,1)S(1)} %collective-permute-done.9.refs_3_), custom_call_target="tpu_custom_call" | custom-call | flops 1 | bytes 1 | tf_op jit(solution)/shard_map/pallas_call | solution.py:183
  37.5 0.4 collective-permute-start.11
  37.9 1.5 %collective-permute-start.12 = (f32[4,128]{1,0:T(4,128)S(1)}, f32[4,128]{1,0:T(4,128)S(1)}, u32[]{:S(2)}, u32[]{:S(2)}) collective-permute-start(f32[4,128]{1,0:T(4,128)S(1)} %get-tuple-element.18), channel_id=1, source_target_pairs={{0,3},{1,2},{2,1},{3,0},{4,7},{5,6},{6,5},{7,4},{8,11},{9,10},{10,... | collective-permute-start | bytes 6152 | tf_op jit(solution)/shard_map/ppermute | solution.py:33
  39.3 0.2 select_reduce_fusion
  39.5 1.6 %collective-permute-done.11 = f32[4,128]{1,0:T(4,128)S(1)} collective-permute-done((f32[4,128]{1,0:T(4,128)S(1)}, f32[4,128]{1,0:T(4,128)S(1)}, u32[]{:S(2)}, u32[]{:S(2)}) %collective-permute-start.11) | collective-permute-done | bytes 2080 | tf_op jit(solution)/shard_map/ppermute | solution.py:27
  41.1 0.7 %log-plus-one_bitcast_fusion = f32[512]{0:T(512)} fusion(f32[4,128]{1,0:T(4,128)S(1)} %collective-permute-done.12, f32[4,128]{1,0:T(4,128)S(1)} %collective-permute-done.11, f32[4,128]{1,0:T(4,128)S(1)} %collective-permute-done.10, f32[16,128]{1,0:T(8,128)S(1)} %shard_map.86, f32[4]{0:T(128)S(1)} %convert_element_type.7), kind=kLoop, calls=%fused_computation.4 | loop fusion | flops 2048 | bytes 10256 | tf_op jit(solution)/shard_map/reshape | solution.py:284
  (25 shorter events, 0.4 us)
Async XLA Ops:
  0.0 3.6 %copy-start = (bf16[512,768]{1,0:T(8,128)(2,1)S(1)}, bf16[512,768]{1,0:T(8,128)(2,1)}, u32[]{:S(2)}) copy-start(bf16[512,768]{1,0:T(8,128)(2,1)} %param.11) | copy-start | bytes 2359300
  0.0 28.4 %copy-start.3 = (f32[64]{0:T(128)S(1)}, f32[64]{0:T(128)}, u32[]{:S(2)}) copy-start(f32[64]{0:T(128)} %beta_ref.3) | copy-start | bytes 772
  0.0 25.9 %collective-permute-start.1 = (bf16[512,768]{1,0:T(8,128)(2,1)}, bf16[512,768]{1,0:T(8,128)(2,1)S(1)}, u32[]{:S(2)}, u32[]{:S(2)}) collective-permute-start(bf16[512,768]{1,0:T(8,128)(2,1)} %refs_0_.1), channel_id=1, source_target_pairs={{0,2},{2,0},{4,6},{6,4},{8,10},{10,8},{12,14},{14,12},{1,3},{3,1},... | collective-permute-start | bytes 2359304 | tf_op jit(solution)/shard_map/ppermute | solution.py:27
  3.7 0.7 %copy-start.2 = (s32[512]{0:T(512)S(1)}, s32[512]{0:T(512)}, u32[]{:S(2)}) copy-start(s32[512]{0:T(512)} %param.12) | copy-start | bytes 6148
  4.4 17.9 %collective-permute-start.2 = (bf16[264,768]{1,0:T(8,128)(2,1)S(1)}, bf16[264,768]{1,0:T(8,128)(2,1)S(1)}, u32[]{:S(2)}, u32[]{:S(2)}) collective-permute-start(bf16[264,768]{1,0:T(8,128)(2,1)S(1)} %shard_map.83.refs_9_), channel_id=1, source_target_pairs={{0,12},{2,14},{4,8},{6,10},{8,4},{10,6},{12,0},{14,2},{1,13},{3,15... | collective-permute-start | bytes 1216520 | tf_op jit(solution)/shard_map/ppermute | solution.py:22
  8.1 17.9 %collective-permute-start.3 = (bf16[264,768]{1,0:T(8,128)(2,1)S(1)}, bf16[264,768]{1,0:T(8,128)(2,1)S(1)}, u32[]{:S(2)}, u32[]{:S(2)}) collective-permute-start(bf16[264,768]{1,0:T(8,128)(2,1)S(1)} %shard_map.83.refs_9_), channel_id=1, source_target_pairs={{0,4},{2,6},{4,0},{6,2},{8,12},{10,14},{12,8},{14,10},{1,5},{3,7},... | collective-permute-start | bytes 1216520 | tf_op jit(solution)/shard_map/ppermute | solution.py:22
  8.1 18.5 %collective-permute-start = (bf16[512,768]{1,0:T(8,128)(2,1)}, bf16[512,768]{1,0:T(8,128)(2,1)S(1)}, u32[]{:S(2)}, u32[]{:S(2)}) collective-permute-start(bf16[512,768]{1,0:T(8,128)(2,1)} %refs_0_.1), channel_id=1, source_target_pairs={{0,1},{1,0},{2,3},{3,2},{4,5},{5,4},{6,7},{7,6},{8,9},{9,8},{10,11... | collective-permute-start | bytes 2359304 | tf_op jit(solution)/shard_map/ppermute | solution.py:27
  8.7 0.7 %copy-start.4 = (s32[4]{0:T(128)S(1)}, s32[4]{0:T(128)}, u32[]{:S(2)}) copy-start(s32[4]{0:T(128)} %clusters_ref) | copy-start | bytes 52
  9.9 1.4 %collective-permute-start.4 = (s32[8,128]{1,0:T(8,128)S(1)}, s32[8,128]{1,0:T(8,128)S(1)}, u32[]{:S(2)}, u32[]{:S(2)}) collective-permute-start(s32[8,128]{1,0:T(8,128)S(1)} %shard_map.84.refs_5_), channel_id=1, source_target_pairs={{0,1},{1,0},{2,3},{3,2},{4,5},{5,4},{6,7},{7,6},{8,9},{9,8},{10,11... | collective-permute-start | bytes 12296 | tf_op jit(solution)/shard_map/ppermute | solution.py:27
  11.3 9.5 %collective-permute-start.5 = (s32[8,128]{1,0:T(8,128)S(1)}, s32[8,128]{1,0:T(8,128)S(1)}, u32[]{:S(2)}, u32[]{:S(2)}) collective-permute-start(s32[8,128]{1,0:T(8,128)S(1)} %shard_map.84.refs_5_), channel_id=1, source_target_pairs={{0,2},{2,0},{4,6},{6,4},{8,10},{10,8},{12,14},{14,12},{1,3},{3,1},... | collective-permute-start | bytes 12296 | tf_op jit(solution)/shard_map/ppermute | solution.py:27
  20.8 4.8 %collective-permute-start.6 = (s32[8,128]{1,0:T(8,128)S(1)}, s32[8,128]{1,0:T(8,128)S(1)}, u32[]{:S(2)}, u32[]{:S(2)}) collective-permute-start(s32[8,128]{1,0:T(8,128)S(1)} %shard_map.84.refs_5_), channel_id=1, source_target_pairs={{0,3},{1,2},{2,1},{3,0},{4,7},{5,6},{6,5},{7,4},{8,11},{9,10},{10,... | collective-permute-start | bytes 12296 | tf_op jit(solution)/shard_map/ppermute | solution.py:33
  21.1 1.1 %copy-start.1 = (bf16[512,768]{1,0:T(8,128)(2,1)S(1)}, bf16[512,768]{1,0:T(8,128)(2,1)}, u32[]{:S(2)}) copy-start(bf16[512,768]{1,0:T(8,128)(2,1)} %refs_0_.1) | copy-start | bytes 2359300
  22.3 12.9 %collective-permute-start.9 = (bf16[264,768]{1,0:T(8,128)(2,1)S(1)}, bf16[264,768]{1,0:T(8,128)(2,1)S(1)}, u32[]{:S(2)}, u32[]{:S(2)}) collective-permute-start(bf16[264,768]{1,0:T(8,128)(2,1)S(1)} %collective-permute-done.2.refs_10_), channel_id=1, source_target_pairs={{0,4},{2,6},{4,0},{6,2},{8,12},{10,14},{12,8},{14,10},{1,5},{3,7},... | collective-permute-start | bytes 1216520 | tf_op jit(solution)/shard_map/ppermute | solution.py:22
  26.0 1.8 %collective-permute-start.7 = (bf16[256,768]{1,0:T(8,128)(2,1)S(1)}, bf16[256,768]{1,0:T(8,128)(2,1)S(1)}, u32[]{:S(2)}, u32[]{:S(2)}) collective-permute-start(bf16[256,768]{1,0:T(8,128)(2,1)S(1)} %get-tuple-element.16), channel_id=1, source_target_pairs={{0,1},{1,0},{2,3},{3,2},{4,5},{5,4},{6,7},{7,6},{8,9},{9,8},{10,11... | collective-permute-start | bytes 1179656 | tf_op jit(solution)/shard_map/ppermute | solution.py:27
  26.1 13.3 %copy-start.5 = (s32[64]{0:T(128)S(1)}, s32[64]{0:T(128)}, u32[]{:S(2)}) copy-start(s32[64]{0:T(128)} %param.15) | copy-start | bytes 772
  26.1 2.3 %collective-permute-start.8 = (bf16[256,768]{1,0:T(8,128)(2,1)S(1)}, bf16[256,768]{1,0:T(8,128)(2,1)S(1)}, u32[]{:S(2)}, u32[]{:S(2)}) collective-permute-start(bf16[256,768]{1,0:T(8,128)(2,1)S(1)} %get-tuple-element.15), channel_id=1, source_target_pairs={{0,1},{1,0},{2,3},{3,2},{4,5},{5,4},{6,7},{7,6},{8,9},{9,8},{10,11... | collective-permute-start | bytes 1179656 | tf_op jit(solution)/shard_map/ppermute | solution.py:27
  37.4 2.1 %collective-permute-start.10 = (f32[4,128]{1,0:T(4,128)S(1)}, f32[4,128]{1,0:T(4,128)S(1)}, u32[]{:S(2)}, u32[]{:S(2)}) collective-permute-start(f32[4,128]{1,0:T(4,128)S(1)} %get-tuple-element.17), channel_id=1, source_target_pairs={{0,1},{1,0},{2,3},{3,2},{4,5},{5,4},{6,7},{7,6},{8,9},{9,8},{10,11... | collective-permute-start | bytes 6152 | tf_op jit(solution)/shard_map/ppermute | solution.py:27
  37.5 3.7 %collective-permute-start.11 = (f32[4,128]{1,0:T(4,128)S(1)}, f32[4,128]{1,0:T(4,128)S(1)}, u32[]{:S(2)}, u32[]{:S(2)}) collective-permute-start(f32[4,128]{1,0:T(4,128)S(1)} %get-tuple-element.19), channel_id=1, source_target_pairs={{0,2},{2,0},{4,6},{6,4},{8,10},{10,8},{12,14},{14,12},{1,3},{3,1},... | collective-permute-start | bytes 6152 | tf_op jit(solution)/shard_map/ppermute | solution.py:27
  37.9 3.2 %collective-permute-start.12 = (f32[4,128]{1,0:T(4,128)S(1)}, f32[4,128]{1,0:T(4,128)S(1)}, u32[]{:S(2)}, u32[]{:S(2)}) collective-permute-start(f32[4,128]{1,0:T(4,128)S(1)} %get-tuple-element.18), channel_id=1, source_target_pairs={{0,3},{1,2},{2,1},{3,0},{4,7},{5,6},{6,5},{7,4},{8,11},{9,10},{10,... | collective-permute-start | bytes 6152 | tf_op jit(solution)/shard_map/ppermute | solution.py:33

commit v14 on v13

--- a/solution.py
+++ b/solution.py
@@ -83,7 +83,7 @@
         t_refs, r_refs = given[:4], given[4:]
     else:
         (info, qv, prev_ref, *r_refs, out_ref, q_list, ids_ref, other_ref) = refs
-    width = qv.shape[0]
+    width = qv.shape[1]
     height = chunks * LANES
     if first:
         for s, t_ref in enumerate(t_refs):
@@ -116,7 +116,7 @@
             each = piece.shape[0] // LANES
 
             def move(block, carry, place=q_count + start, piece=piece):
-                qv[:, rows_of(place + block)] = piece[rows_of(block), :].T
+                qv[rows_of(place + block), :] = piece[rows_of(block), :]
                 return carry
 
             lax.fori_loop(0, jnp.clip(blocks - start, 0, each), move, 0)
@@ -142,8 +142,8 @@
             for pair in range(wide // 2):
                 score = lax.dot_general(
                     tile,
-                    qv[:, rows_of(wide * group + 2 * pair, 2)],
-                    (((1,), (0,)), ((), ())),
+                    qv[rows_of(wide * group + 2 * pair, 2), :],
+                    (((1,), (1,)), ((), ())),
                     preferred_element_type=jnp.float32,
                 )
                 for half in range(2):
@@ -171,7 +171,7 @@
     slots = 4 * qblocks
     height = chunks * LANES
     totals_shape = jax.ShapeDtypeStruct((slots, LANES), jnp.float32)
-    packed_shape = jax.ShapeDtypeStruct((width, slots * LANES), jnp.bfloat16)
+    packed_shape = jax.ShapeDtypeStruct((slots * LANES, width), jnp.bfloat16)
     info_shape = jax.ShapeDtypeStruct((8, LANES), jnp.int32)
     spread = pltpu.VMEM((len(payloads) * height, LANES), jnp.float32)
     scratch = [pltpu.SMEM((slots, 2), jnp.int32), spread, spread]
@@ -269,7 +269,7 @@
         chunks,
         qblocks,
         pieces,
-        4,
+        8,
         cluster_beta,
         (info, packed, totals),
         held[-1:],

time: 42 us -> 41.7 us (level)
  waiting for transfers between devices: 14.4 us -> 15.5 us
  Pallas kernels: 8.74 us -> 7.78 us
    ppermute x3, waiting for transfers between devices: 1.28 us -> 2.3 us  [trade(): return lax.ppermute(value, 'blk', [(i, i ^ mask) for i in range(length)])]
    pallas_call x2, Pallas kernels: 8.11 us -> 7.15 us  [score_call(): pl.pallas_call(functools.partial(score_kernel, chunks, qblocks, pieces, f...]
  transfers between devices with their start and end apart: 13 -> 13, of which waited for: 7 -> 7; matrix products, arithmetic and copies ran while one was open for 1% -> 1% of each run, Pallas kernels for 16% -> 13%
where the time goes in v14:
time: 41.7 us; the launch traced here: 41.9 us
  waiting for transfers between devices  15.5 us (37%)
  starting transfers between devices  13.8 us (33%)
  Pallas kernels  7.78 us (19%)
  local copies, waits for them, and re-layouts  2.56 us (6%)
  between operations  1.42 us (3%)
  other arithmetic  0.85 us (2%)
    ppermute x8, waiting for transfers between devices, swap(): return lax.ppermute(value, axis, [(i, i ^ 1) for i in range(length)])  13.2 us
    pallas_call x2, Pallas kernels, score_call(): pl.pallas_call(functools.partial(score_kernel, chunks, qblocks, pieces, f...  7.15 us
    ppermute x3, starting transfers between devices, trade(): return lax.ppermute(value, 'blk', [(i, i ^ mask) for i in range(length)])  6.92 us
    ppermute x8, starting transfers between devices, swap(): return lax.ppermute(value, axis, [(i, i ^ 1) for i in range(length)])  5.1 us
    unnamed x12, local copies, waits for them, and re-layouts  2.47 us
    ppermute x3, waiting for transfers between devices, trade(): return lax.ppermute(value, 'blk', [(i, i ^ mask) for i in range(length)])  2.3 us
    ppermute x2, starting transfers between devices, swap_both(): return lax.ppermute(value, ('blk', 'helper'), pairs)  1.76 us
  transfers between devices with their start and end apart: 13, of which 7 were waited for; matrix products, arithmetic and copies ran while one was open for 1% of the time, Pallas kernels for 13%

profile of v14, /device:TPU:0, one launch (start us, length us, event | category | flops | bytes accessed | tf_op | source)
XLA Modules:
  0.0 41.9 jit_solution(9321982344369689623)
XLA Ops:
  0.0 3.0 %collective-permute-start.1 = (bf16[512,768]{1,0:T(8,128)(2,1)}, bf16[512,768]{1,0:T(8,128)(2,1)S(1)}, u32[]{:S(2)}, u32[]{:S(2)}) collective-permute-start(bf16[512,768]{1,0:T(8,128)(2,1)} %refs_0_.1), channel_id=1, source_target_pairs={{0,2},{2,0},{4,6},{6,4},{8,10},{10,8},{12,14},{14,12},{1,3},{3,1},... | collective-permute-start | bytes 2359304 | tf_op jit(solution)/shard_map/ppermute | solution.py:27
  3.7 0.7 %copy-done.2 = s32[512]{0:T(512)S(1)} copy-done((s32[512]{0:T(512)S(1)}, s32[512]{0:T(512)}, u32[]{:S(2)}) %copy-start.2) | copy-done | bytes 2072
  4.4 3.7 %collective-permute-start.2 = (bf16[264,768]{1,0:T(8,128)(2,1)S(1)}, bf16[264,768]{1,0:T(8,128)(2,1)S(1)}, u32[]{:S(2)}, u32[]{:S(2)}) collective-permute-start(bf16[264,768]{1,0:T(8,128)(2,1)S(1)} %shard_map.83.refs_9_), channel_id=1, source_target_pairs={{0,12},{2,14},{4,8},{6,10},{8,4},{10,6},{12,0},{14,2},{1,13},{3,15... | collective-permute-start | bytes 1216520 | tf_op jit(solution)/shard_map/ppermute | solution.py:22
  8.7 0.6 %copy-done.4 = s32[4]{0:T(128)S(1)} copy-done((s32[4]{0:T(128)S(1)}, s32[4]{0:T(128)}, u32[]{:S(2)}) %copy-start.4) | copy-done | bytes 40
  9.4 0.5 %shard_map.84.refs_5_ = s32[8,128]{1,0:T(8,128)S(1)} custom-call(s32[4]{0:T(128)S(1)} %copy-done.4, s32[1]{0:T(128)S(6)} %copy.12.count_ref), custom_call_target="tpu_custom_call" | custom-call | flops 1 | bytes 1 | tf_op jit(solution)/shard_map/pallas_call | solution.py:235
  9.9 0.6 %collective-permute-start.4 = (s32[8,128]{1,0:T(8,128)S(1)}, s32[8,128]{1,0:T(8,128)S(1)}, u32[]{:S(2)}, u32[]{:S(2)}) collective-permute-start(s32[8,128]{1,0:T(8,128)S(1)} %shard_map.84.refs_5_), channel_id=1, source_target_pairs={{0,1},{1,0},{2,3},{3,2},{4,5},{5,4},{6,7},{7,6},{8,9},{9,8},{10,11... | collective-permute-start | bytes 12296 | tf_op jit(solution)/shard_map/ppermute | solution.py:27
  10.5 0.8 %collective-permute-done.4.refs_6_ = s32[8,128]{1,0:T(8,128)S(1)} collective-permute-done((s32[8,128]{1,0:T(8,128)S(1)}, s32[8,128]{1,0:T(8,128)S(1)}, u32[]{:S(2)}, u32[]{:S(2)}) %collective-permute-start.4) | collective-permute-done | bytes 4128 | tf_op jit(solution)/shard_map/ppermute | solution.py:27
  11.3 0.5 %collective-permute-start.5 = (s32[8,128]{1,0:T(8,128)S(1)}, s32[8,128]{1,0:T(8,128)S(1)}, u32[]{:S(2)}, u32[]{:S(2)}) collective-permute-start(s32[8,128]{1,0:T(8,128)S(1)} %shard_map.84.refs_5_), channel_id=1, source_target_pairs={{0,2},{2,0},{4,6},{6,4},{8,10},{10,8},{12,14},{14,12},{1,3},{3,1},... | collective-permute-start | bytes 12296 | tf_op jit(solution)/shard_map/ppermute | solution.py:27
  11.8 9.0 %collective-permute-done.5.refs_7_ = s32[8,128]{1,0:T(8,128)S(1)} collective-permute-done((s32[8,128]{1,0:T(8,128)S(1)}, s32[8,128]{1,0:T(8,128)S(1)}, u32[]{:S(2)}, u32[]{:S(2)}) %collective-permute-start.5) | collective-permute-done | bytes 4128 | tf_op jit(solution)/shard_map/ppermute | solution.py:27
  20.8 0.3 collective-permute-start.6
  21.1 1.1 %copy-done.1 = bf16[512,768]{1,0:T(8,128)(2,1)S(1)} copy-done((bf16[512,768]{1,0:T(8,128)(2,1)S(1)}, bf16[512,768]{1,0:T(8,128)(2,1)}, u32[]{:S(2)}) %copy-start.1) | copy-done | bytes 786456
  22.3 3.2 %collective-permute-start.9 = (bf16[264,768]{1,0:T(8,128)(2,1)S(1)}, bf16[264,768]{1,0:T(8,128)(2,1)S(1)}, u32[]{:S(2)}, u32[]{:S(2)}) collective-permute-start(bf16[264,768]{1,0:T(8,128)(2,1)S(1)} %collective-permute-done.2.refs_10_), channel_id=1, source_target_pairs={{0,4},{2,6},{4,0},{6,2},{8,12},{10,14},{12,8},{14,10},{1,5},{3,7},... | collective-permute-start | bytes 1216520 | tf_op jit(solution)/shard_map/ppermute | solution.py:22
  25.6 0.4 collective-permute-done.3.refs_11_
  26.1 0.5 %collective-permute-start.8 = (bf16[256,768]{1,0:T(8,128)(2,1)S(1)}, bf16[256,768]{1,0:T(8,128)(2,1)S(1)}, u32[]{:S(2)}, u32[]{:S(2)}) collective-permute-start(bf16[256,768]{1,0:T(8,128)(2,1)S(1)} %get-tuple-element.15), channel_id=1, source_target_pairs={{0,1},{1,0},{2,3},{3,2},{4,5},{5,4},{6,7},{7,6},{8,9},{9,8},{10,11... | collective-permute-start | bytes 1179656 | tf_op jit(solution)/shard_map/ppermute | solution.py:27
  26.6 1.2 %collective-permute-done.7.refs_3_ = bf16[256,768]{1,0:T(8,128)(2,1)S(1)} collective-permute-done((bf16[256,768]{1,0:T(8,128)(2,1)S(1)}, bf16[256,768]{1,0:T(8,128)(2,1)S(1)}, u32[]{:S(2)}, u32[]{:S(2)}) %collective-permute-start.7) | collective-permute-done | bytes 393248 | tf_op jit(solution)/shard_map/ppermute | solution.py:27
  27.8 0.6 %collective-permute-done.8.refs_4_ = bf16[256,768]{1,0:T(8,128)(2,1)S(1)} collective-permute-done((bf16[256,768]{1,0:T(8,128)(2,1)S(1)}, bf16[256,768]{1,0:T(8,128)(2,1)S(1)}, u32[]{:S(2)}, u32[]{:S(2)}) %collective-permute-start.8) | collective-permute-done | bytes 393248 | tf_op jit(solution)/shard_map/ppermute | solution.py:27
  28.4 4.9 %shard_map.85 = (f32[16,128]{1,0:T(8,128)S(1)}, bf16[2048,768]{1,0:T(8,128)(2,1)S(1)}, s32[8,128]{1,0:T(8,128)S(1)}) custom-call(f32[64]{0:T(128)S(1)} %copy-done.3, bf16[512,768]{1,0:T(8,128)(2,1)S(1)} %shard_map.82.refs_0_, bf16[512,768]{1,0:T(8,128)(2,1)S(1)} %collective-permute-done.refs_1_, bf16[512,768]{1,0:T(8,128)(2,1)S(1)} %collective-permute-done.1.refs_2_, ...), custom_call_target="tpu_custom_call" | custom-call | flops 1 | bytes 1 | tf_op jit(solution)/shard_map/pallas_call | solution.py:183
  33.3 1.9 %collective-permute-done.9.refs_3_ = bf16[264,768]{1,0:T(8,128)(2,1)S(1)} collective-permute-done((bf16[264,768]{1,0:T(8,128)(2,1)S(1)}, bf16[264,768]{1,0:T(8,128)(2,1)S(1)}, u32[]{:S(2)}, u32[]{:S(2)}) %collective-permute-start.9) | collective-permute-done | bytes 405536 | tf_op jit(solution)/shard_map/ppermute | solution.py:22
  35.2 2.2 %shard_map.86 = f32[16,128]{1,0:T(8,128)S(1)} custom-call(f32[64]{0:T(128)S(1)} %copy-done.3, s32[8,128]{1,0:T(8,128)S(1)} %get-tuple-element.12.refs_0_, bf16[2048,768]{1,0:T(8,128)(2,1)S(1)} %get-tuple-element.13.refs_1_, f32[16,128]{1,0:T(8,128)S(1)} %get-tuple-element.14.refs_2_, bf16[264,768]{1,0:T(8,128)(2,1)S(1)} %collective-permute-done.9.refs_3_), custom_call_target="tpu_custom_call" | custom-call | flops 1 | bytes 1 | tf_op jit(solution)/shard_map/pallas_call | solution.py:183
  37.5 0.4 collective-permute-start.11
  37.9 1.5 %collective-permute-start.12 = (f32[4,128]{1,0:T(4,128)S(1)}, f32[4,128]{1,0:T(4,128)S(1)}, u32[]{:S(2)}, u32[]{:S(2)}) collective-permute-start(f32[4,128]{1,0:T(4,128)S(1)} %get-tuple-element.18), channel_id=1, source_target_pairs={{0,3},{1,2},{2,1},{3,0},{4,7},{5,6},{6,5},{7,4},{8,11},{9,10},{10,... | collective-permute-start | bytes 6152 | tf_op jit(solution)/shard_map/ppermute | solution.py:33
  39.4 0.2 select_reduce_fusion
  39.6 1.6 %collective-permute-done.11 = f32[4,128]{1,0:T(4,128)S(1)} collective-permute-done((f32[4,128]{1,0:T(4,128)S(1)}, f32[4,128]{1,0:T(4,128)S(1)}, u32[]{:S(2)}, u32[]{:S(2)}) %collective-permute-start.11) | collective-permute-done | bytes 2080 | tf_op jit(solution)/shard_map/ppermute | solution.py:27
  41.2 0.7 %log-plus-one_bitcast_fusion = f32[512]{0:T(512)} fusion(f32[4,128]{1,0:T(4,128)S(1)} %collective-permute-done.12, f32[4,128]{1,0:T(4,128)S(1)} %collective-permute-done.11, f32[4,128]{1,0:T(4,128)S(1)} %collective-permute-done.10, f32[16,128]{1,0:T(8,128)S(1)} %shard_map.86, f32[4]{0:T(128)S(1)} %convert_element_type.7), kind=kLoop, calls=%fused_computation.4 | loop fusion | flops 2048 | bytes 10256 | tf_op jit(solution)/shard_map/reshape | solution.py:284
  (25 shorter events, 0.4 us)
Async XLA Ops:
  0.0 3.6 %copy-start = (bf16[512,768]{1,0:T(8,128)(2,1)S(1)}, bf16[512,768]{1,0:T(8,128)(2,1)}, u32[]{:S(2)}) copy-start(bf16[512,768]{1,0:T(8,128)(2,1)} %param.11) | copy-start | bytes 2359300
  0.0 28.4 %copy-start.3 = (f32[64]{0:T(128)S(1)}, f32[64]{0:T(128)}, u32[]{:S(2)}) copy-start(f32[64]{0:T(128)} %beta_ref.3) | copy-start | bytes 772
  0.0 25.9 %collective-permute-start.1 = (bf16[512,768]{1,0:T(8,128)(2,1)}, bf16[512,768]{1,0:T(8,128)(2,1)S(1)}, u32[]{:S(2)}, u32[]{:S(2)}) collective-permute-start(bf16[512,768]{1,0:T(8,128)(2,1)} %refs_0_.1), channel_id=1, source_target_pairs={{0,2},{2,0},{4,6},{6,4},{8,10},{10,8},{12,14},{14,12},{1,3},{3,1},... | collective-permute-start | bytes 2359304 | tf_op jit(solution)/shard_map/ppermute | solution.py:27
  3.7 0.7 %copy-start.2 = (s32[512]{0:T(512)S(1)}, s32[512]{0:T(512)}, u32[]{:S(2)}) copy-start(s32[512]{0:T(512)} %param.12) | copy-start | bytes 6148
  4.4 17.9 %collective-permute-start.2 = (bf16[264,768]{1,0:T(8,128)(2,1)S(1)}, bf16[264,768]{1,0:T(8,128)(2,1)S(1)}, u32[]{:S(2)}, u32[]{:S(2)}) collective-permute-start(bf16[264,768]{1,0:T(8,128)(2,1)S(1)} %shard_map.83.refs_9_), channel_id=1, source_target_pairs={{0,12},{2,14},{4,8},{6,10},{8,4},{10,6},{12,0},{14,2},{1,13},{3,15... | collective-permute-start | bytes 1216520 | tf_op jit(solution)/shard_map/ppermute | solution.py:22
  8.1 17.9 %collective-permute-start.3 = (bf16[264,768]{1,0:T(8,128)(2,1)S(1)}, bf16[264,768]{1,0:T(8,128)(2,1)S(1)}, u32[]{:S(2)}, u32[]{:S(2)}) collective-permute-start(bf16[264,768]{1,0:T(8,128)(2,1)S(1)} %shard_map.83.refs_9_), channel_id=1, source_target_pairs={{0,4},{2,6},{4,0},{6,2},{8,12},{10,14},{12,8},{14,10},{1,5},{3,7},... | collective-permute-start | bytes 1216520 | tf_op jit(solution)/shard_map/ppermute | solution.py:22
  8.1 18.5 %collective-permute-start = (bf16[512,768]{1,0:T(8,128)(2,1)}, bf16[512,768]{1,0:T(8,128)(2,1)S(1)}, u32[]{:S(2)}, u32[]{:S(2)}) collective-permute-start(bf16[512,768]{1,0:T(8,128)(2,1)} %refs_0_.1), channel_id=1, source_target_pairs={{0,1},{1,0},{2,3},{3,2},{4,5},{5,4},{6,7},{7,6},{8,9},{9,8},{10,11... | collective-permute-start | bytes 2359304 | tf_op jit(solution)/shard_map/ppermute | solution.py:27
  8.7 0.7 %copy-start.4 = (s32[4]{0:T(128)S(1)}, s32[4]{0:T(128)}, u32[]{:S(2)}) copy-start(s32[4]{0:T(128)} %clusters_ref) | copy-start | bytes 52
  9.9 1.4 %collective-permute-start.4 = (s32[8,128]{1,0:T(8,128)S(1)}, s32[8,128]{1,0:T(8,128)S(1)}, u32[]{:S(2)}, u32[]{:S(2)}) collective-permute-start(s32[8,128]{1,0:T(8,128)S(1)} %shard_map.84.refs_5_), channel_id=1, source_target_pairs={{0,1},{1,0},{2,3},{3,2},{4,5},{5,4},{6,7},{7,6},{8,9},{9,8},{10,11... | collective-permute-start | bytes 12296 | tf_op jit(solution)/shard_map/ppermute | solution.py:27
  11.3 9.5 %collective-permute-start.5 = (s32[8,128]{1,0:T(8,128)S(1)}, s32[8,128]{1,0:T(8,128)S(1)}, u32[]{:S(2)}, u32[]{:S(2)}) collective-permute-start(s32[8,128]{1,0:T(8,128)S(1)} %shard_map.84.refs_5_), channel_id=1, source_target_pairs={{0,2},{2,0},{4,6},{6,4},{8,10},{10,8},{12,14},{14,12},{1,3},{3,1},... | collective-permute-start | bytes 12296 | tf_op jit(solution)/shard_map/ppermute | solution.py:27
  20.8 4.8 %collective-permute-start.6 = (s32[8,128]{1,0:T(8,128)S(1)}, s32[8,128]{1,0:T(8,128)S(1)}, u32[]{:S(2)}, u32[]{:S(2)}) collective-permute-start(s32[8,128]{1,0:T(8,128)S(1)} %shard_map.84.refs_5_), channel_id=1, source_target_pairs={{0,3},{1,2},{2,1},{3,0},{4,7},{5,6},{6,5},{7,4},{8,11},{9,10},{10,... | collective-permute-start | bytes 12296 | tf_op jit(solution)/shard_map/ppermute | solution.py:33
  21.1 1.1 %copy-start.1 = (bf16[512,768]{1,0:T(8,128)(2,1)S(1)}, bf16[512,768]{1,0:T(8,128)(2,1)}, u32[]{:S(2)}) copy-start(bf16[512,768]{1,0:T(8,128)(2,1)} %refs_0_.1) | copy-start | bytes 2359300
  22.3 12.9 %collective-permute-start.9 = (bf16[264,768]{1,0:T(8,128)(2,1)S(1)}, bf16[264,768]{1,0:T(8,128)(2,1)S(1)}, u32[]{:S(2)}, u32[]{:S(2)}) collective-permute-start(bf16[264,768]{1,0:T(8,128)(2,1)S(1)} %collective-permute-done.2.refs_10_), channel_id=1, source_target_pairs={{0,4},{2,6},{4,0},{6,2},{8,12},{10,14},{12,8},{14,10},{1,5},{3,7},... | collective-permute-start | bytes 1216520 | tf_op jit(solution)/shard_map/ppermute | solution.py:22
  26.0 1.8 %collective-permute-start.7 = (bf16[256,768]{1,0:T(8,128)(2,1)S(1)}, bf16[256,768]{1,0:T(8,128)(2,1)S(1)}, u32[]{:S(2)}, u32[]{:S(2)}) collective-permute-start(bf16[256,768]{1,0:T(8,128)(2,1)S(1)} %get-tuple-element.16), channel_id=1, source_target_pairs={{0,1},{1,0},{2,3},{3,2},{4,5},{5,4},{6,7},{7,6},{8,9},{9,8},{10,11... | collective-permute-start | bytes 1179656 | tf_op jit(solution)/shard_map/ppermute | solution.py:27
  26.1 13.3 %copy-start.5 = (s32[64]{0:T(128)S(1)}, s32[64]{0:T(128)}, u32[]{:S(2)}) copy-start(s32[64]{0:T(128)} %param.15) | copy-start | bytes 772
  26.1 2.3 %collective-permute-start.8 = (bf16[256,768]{1,0:T(8,128)(2,1)S(1)}, bf16[256,768]{1,0:T(8,128)(2,1)S(1)}, u32[]{:S(2)}, u32[]{:S(2)}) collective-permute-start(bf16[256,768]{1,0:T(8,128)(2,1)S(1)} %get-tuple-element.15), channel_id=1, source_target_pairs={{0,1},{1,0},{2,3},{3,2},{4,5},{5,4},{6,7},{7,6},{8,9},{9,8},{10,11... | collective-permute-start | bytes 1179656 | tf_op jit(solution)/shard_map/ppermute | solution.py:27
  37.5 2.1 %collective-permute-start.10 = (f32[4,128]{1,0:T(4,128)S(1)}, f32[4,128]{1,0:T(4,128)S(1)}, u32[]{:S(2)}, u32[]{:S(2)}) collective-permute-start(f32[4,128]{1,0:T(4,128)S(1)} %get-tuple-element.17), channel_id=1, source_target_pairs={{0,1},{1,0},{2,3},{3,2},{4,5},{5,4},{6,7},{7,6},{8,9},{9,8},{10,11... | collective-permute-start | bytes 6152 | tf_op jit(solution)/shard_map/ppermute | solution.py:27
  37.5 3.7 %collective-permute-start.11 = (f32[4,128]{1,0:T(4,128)S(1)}, f32[4,128]{1,0:T(4,128)S(1)}, u32[]{:S(2)}, u32[]{:S(2)}) collective-permute-start(f32[4,128]{1,0:T(4,128)S(1)} %get-tuple-element.19), channel_id=1, source_target_pairs={{0,2},{2,0},{4,6},{6,4},{8,10},{10,8},{12,14},{14,12},{1,3},{3,1},... | collective-permute-start | bytes 6152 | tf_op jit(solution)/shard_map/ppermute | solution.py:27
  37.9 3.2 %collective-permute-start.12 = (f32[4,128]{1,0:T(4,128)S(1)}, f32[4,128]{1,0:T(4,128)S(1)}, u32[]{:S(2)}, u32[]{:S(2)}) collective-permute-start(f32[4,128]{1,0:T(4,128)S(1)} %get-tuple-element.18), channel_id=1, source_target_pairs={{0,3},{1,2},{2,1},{3,0},{4,7},{5,6},{6,5},{7,4},{8,11},{9,10},{10,... | collective-permute-start | bytes 6152 | tf_op jit(solution)/shard_map/ppermute | solution.py:33

commit v15 on v14

--- a/solution.py
+++ b/solution.py
@@ -10,6 +10,7 @@
 
 LANES = 128
 TABLE = 8
+LATE = 64
 LOG2E = 1.4426950408889634
 DEAD = -1.0e30
 SMEM = pl.BlockSpec(memory_space=pltpu.SMEM)
@@ -45,7 +46,7 @@
     return pl.ds(pl.multiple_of(index * LANES, LANES), count * LANES)
 
 
-def pack_kernel(nhelper, helper_ref, live_ref, ids_ref, r_ref, out_ref):
+def pack_kernel(nhelper, helper_ref, live_ref, ids_ref, r_ref, whole_ref, most_ref, late_ref):
     lane = lax.broadcasted_iota(jnp.int32, (TABLE, LANES), 1)
     row = lax.broadcasted_iota(jnp.int32, (TABLE, LANES), 0)
     table = jnp.full((TABLE, LANES), -1, jnp.int32)
@@ -54,8 +55,11 @@
         tile = helper_ref[0] + nhelper * c
         ids = ids_ref[pl.ds(tile, 1), :]
         table = jnp.where(row == c, jnp.where(tile * LANES + lane < live_ref[0], ids, -1), table)
-    out_ref[pl.ds(0, height), :] = r_ref[...]
-    out_ref[pl.ds(height, TABLE), pl.ds(0, LANES)] = table.astype(jnp.float32).astype(jnp.bfloat16)
+    table = table.astype(jnp.float32).astype(jnp.bfloat16)
+    for out_ref, count in ((whole_ref, height), (most_ref, height - LATE)):
+        out_ref[pl.ds(0, count), :] = r_ref[pl.ds(0, count), :]
+        out_ref[pl.ds(count, TABLE), pl.ds(0, LANES)] = table
+    late_ref[...] = r_ref[pl.ds(height - LATE, LATE), :]
 
 
 def table_kernel(clusters_ref, count_ref, out_ref):
@@ -73,7 +77,7 @@
         out[...] = source[...]
 
 
-def score_kernel(chunks, qblocks, pieces, first, wide, beta_ref, *refs):
+def score_kernel(spans, qblocks, pieces, first, wide, beta_ref, *refs):
     if first:
         (*given, out_ref, qv, info_out, q_list, ids_ref, other_ref, info, info_sem) = refs
         q_refs = []
@@ -84,20 +88,25 @@
     else:
         (info, qv, prev_ref, *r_refs, out_ref, q_list, ids_ref, other_ref) = refs
     width = qv.shape[1]
-    height = chunks * LANES
     if first:
         for s, t_ref in enumerate(t_refs):
             info_out[s : s + 1, :] = t_ref[0:1, :]
         copy = pltpu.make_async_copy(info_out, info, info_sem)
         copy.start()
 
-    for s, r_ref in enumerate(r_refs):
-        table = r_ref[pl.ds(height, TABLE), pl.ds(0, LANES)].astype(jnp.float32)
-        for c in range(chunks):
+    start = 0
+    for (begin, end, behind), r_ref in zip(spans, r_refs):
+        if behind is None:
+            r_ref, behind = r_refs[-1], r_refs[-1].shape[0] - TABLE
+        table = r_ref[pl.ds(behind, TABLE), pl.ds(0, LANES)].astype(jnp.float32)
+        for c in range(begin // LANES, -(-end // LANES)):
+            low, high = max(begin, c * LANES), min(end, (c + 1) * LANES)
             ids = jnp.broadcast_to(table[c : c + 1, :], (LANES, LANES)).T
-            rows = pl.ds(s * height + c * LANES, LANES)
+            ids = ids[low - c * LANES : high - c * LANES, :]
+            rows = pl.ds(start, high - low)
             ids_ref[rows, :] = ids
             other_ref[rows, :] = jnp.where(ids < 0.0, DEAD, -4.0)
+            start += high - low
     if first:
         copy.wait()
 
@@ -131,14 +140,17 @@
         for side in range(wide):
             entry = jnp.minimum(wide * group + side, q_count - 1)
             slot, cluster = q_list[entry, 0], q_list[entry, 1]
-            beta = beta_ref[cluster]
+            beta = beta_ref[0, cluster]
             sides.append(
                 (slot, cluster.astype(jnp.float32), beta * factor, beta * beta * (0.5 * LOG2E))
             )
         accs = [jnp.zeros((8, LANES), jnp.float32) for _ in range(wide)]
-        for s, r_ref in enumerate(r_refs):
+        start = 0
+        for (begin, end, _), r_ref in zip(spans, r_refs):
+            height = end - begin
             tile = r_ref[pl.ds(0, height), :]
-            rows = pl.ds(s * height, height)
+            rows = pl.ds(start, height)
+            start += height
             for pair in range(wide // 2):
                 score = lax.dot_general(
                     tile,
@@ -166,14 +178,14 @@
     lax.fori_loop(0, (q_count + wide - 1) // wide, query_blocks, 0)
 
 
-def score_call(chunks, qblocks, pieces, wide, beta, given, payloads, first):
+def score_call(spans, qblocks, pieces, wide, beta, given, payloads, first):
     width = payloads[0].shape[1]
     slots = 4 * qblocks
-    height = chunks * LANES
+    height = sum(end - begin for begin, end, _ in spans)
     totals_shape = jax.ShapeDtypeStruct((slots, LANES), jnp.float32)
     packed_shape = jax.ShapeDtypeStruct((slots * LANES, width), jnp.bfloat16)
     info_shape = jax.ShapeDtypeStruct((8, LANES), jnp.int32)
-    spread = pltpu.VMEM((len(payloads) * height, LANES), jnp.float32)
+    spread = pltpu.VMEM((height, LANES), jnp.float32)
     scratch = [pltpu.SMEM((slots, 2), jnp.int32), spread, spread]
     specs = [VMEM] * (len(given) + len(payloads))
     if first:
@@ -181,7 +193,7 @@
     else:
         specs[0] = SMEM
     return pl.pallas_call(
-        functools.partial(score_kernel, chunks, qblocks, pieces, first, wide),
+        functools.partial(score_kernel, spans, qblocks, pieces, first, wide),
         out_shape=(totals_shape, packed_shape, info_shape) if first else totals_shape,
         in_specs=[SMEM] + specs,
         out_specs=(VMEM, VMEM, VMEM) if first else VMEM,
@@ -212,11 +224,15 @@
     q_partner = swap(queries, "blk")
     by_chunk = references.reshape(chunks, nhelper, LANES, width)
     own = lax.dynamic_index_in_dim(by_chunk, helper, 1, keepdims=False)
-    own = pl.pallas_call(
+    height = chunks * LANES
+    own, most, late = pl.pallas_call(
         functools.partial(pack_kernel, nhelper),
-        out_shape=jax.ShapeDtypeStruct((chunks * LANES + TABLE, width), jnp.bfloat16),
+        out_shape=[
+            jax.ShapeDtypeStruct((n, width), jnp.bfloat16)
+            for n in (height + TABLE, height - LATE + TABLE, LATE)
+        ],
         in_specs=[SMEM] * 2 + [VMEM] * 2,
-        out_specs=VMEM,
+        out_specs=[VMEM] * 3,
         compiler_params=PARAMS,
         cost_estimate=cost(1, 1),
     )(
@@ -227,9 +243,13 @@
     )
 
     held, mask = [own], sources - 1
-    while mask:
-        held = held + [trade(x, 2 * mask) for x in held]
-        mask //= 2
+    while mask > 1:
+        held, mask = held + [trade(x, 2 * mask) for x in held], mask // 2
+    held += [trade(most, 2)] + [trade(x, 2) for x in held[1:]]
+    late = trade(late, 2)
+    spans = [(0, height, height)] * len(held)
+    spans[len(held) // 2] = (0, height - LATE, height - LATE)
+    tabled = held[len(held) // 2]
     q_helper = swap(queries, "helper")
 
     table = pl.pallas_call(
@@ -241,14 +261,15 @@
         cost_estimate=cost(1, 1),
     )(after(query_block_cluster, own), block_count)
     q_tables = (table, swap(table, "helper"), swap(table, "blk"), swap_both(table))
-    staged = pl.pallas_call(
+    beta = cluster_beta.reshape(1, -1)
+    staged, beta = pl.pallas_call(
         stage_kernel,
-        out_shape=jax.ShapeDtypeStruct(queries.shape, queries.dtype),
-        in_specs=[VMEM],
-        out_specs=VMEM,
+        out_shape=[jax.ShapeDtypeStruct(x.shape, x.dtype) for x in (queries, beta)],
+        in_specs=[VMEM] * 2,
+        out_specs=[VMEM] * 2,
         compiler_params=PARAMS,
         cost_estimate=cost(1, 1),
-    )(queries)
+    )(queries, beta)
     q_partner = after(q_partner, staged, *held[1:-1], *q_tables)
     half = qblocks // 2 * LANES
     q_both = [swap(q_partner[:half], "helper"), swap(q_partner[half:], "helper")]
@@ -256,25 +277,21 @@
     pieces = (1, 1, 1, 2)
 
     totals, packed, info = score_call(
-        chunks,
+        tuple(spans[:-1]),
         qblocks,
         pieces,
-        2,
-        cluster_beta,
+        4,
+        beta,
         (*queries, *q_tables),
         held[:-1],
         True,
     )
-    totals = score_call(
-        chunks,
-        qblocks,
-        pieces,
-        8,
-        cluster_beta,
-        (info, packed, totals),
-        held[-1:],
-        False,
-    )
+    for payloads, span in (
+        (held[-1:], spans[-1]),
+        ([late, tabled], (height - LATE, height, None)),
+    ):
+        given = (info, packed, totals)
+        totals = score_call((span,), qblocks, pieces, 8, beta, given, payloads, False)
     totals = totals.reshape(4, qblocks, LANES)
     total = totals[0] + swap(totals[1], "helper") + swap(totals[2], "blk") + swap_both(totals[3])
     columns = jnp.arange(cluster_member_count.shape[0], dtype=jnp.int32)

time: 41.7 us -> 45.1 us (1.082)
  Pallas kernels: 7.78 us -> 9.27 us
  waiting for transfers between devices: 15.5 us -> 16.7 us
  local copies, waits for them, and re-layouts: 2.56 us -> 3.22 us
    pallas_call x4 -> x5, Pallas kernels: 7.23 us -> 8.72 us  [the longest x3 8.62 us: score_call(): pl.pallas_call(functools.partial(score_kernel, spans, qblocks, pieces, fi...]
    ppermute x3 -> x4, waiting for transfers between devices: 2.3 us -> 3.5 us  [trade(): return lax.ppermute(value, 'blk', [(i, i ^ mask) for i in range(length)])]
    unnamed x12, local copies, waits for them, and re-layouts: 2.47 us -> 3.12 us
    ppermute x8, starting transfers between devices: 5.1 us -> 5.7 us  [swap(): return lax.ppermute(value, axis, [(i, i ^ 1) for i in range(length)])]
    ppermute x2, starting transfers between devices: 1.76 us -> 1.16 us  [swap_both(): return lax.ppermute(value, ('blk', 'helper'), pairs)]
    ppermute x3 -> x4, starting transfers between devices: 6.92 us -> 6.6 us  [trade(): return lax.ppermute(value, 'blk', [(i, i ^ mask) for i in range(length)])]
  transfers between devices with their start and end apart: 13 -> 14, of which waited for: 7 -> 7; matrix products, arithmetic and copies ran while one was open for 1% -> 1% of each run, Pallas kernels for 13% -> 16%
where the time goes in v15:
time: 45.1 us; the launch traced here: 44.9 us
  waiting for transfers between devices  16.7 us (37%)
  starting transfers between devices  13.5 us (30%)
  Pallas kernels  9.27 us (21%)
  local copies, waits for them, and re-layouts  3.22 us (7%)
  between operations  1.43 us (3%)
  other arithmetic  0.85 us (2%)
    ppermute x8, waiting for transfers between devices, swap(): return lax.ppermute(value, axis, [(i, i ^ 1) for i in range(length)])  13 us
    pallas_call x3, Pallas kernels, score_call(): pl.pallas_call(functools.partial(score_kernel, spans, qblocks, pieces, fi...  8.62 us
    ppermute x4, starting transfers between devices, trade(): return lax.ppermute(value, 'blk', [(i, i ^ mask) for i in range(length)])  6.6 us
    ppermute x8, starting transfers between devices, swap(): return lax.ppermute(value, axis, [(i, i ^ 1) for i in range(length)])  5.7 us
    ppermute x4, waiting for transfers between devices, trade(): return lax.ppermute(value, 'blk', [(i, i ^ mask) for i in range(length)])  3.5 us
    unnamed x12, local copies, waits for them, and re-layouts  3.12 us
    ppermute x2, starting transfers between devices, swap_both(): return lax.ppermute(value, ('blk', 'helper'), pairs)  1.16 us
  transfers between devices with their start and end apart: 14, of which 7 were waited for; matrix products, arithmetic and copies ran while one was open for 1% of the time, Pallas kernels for 16%

profile of v15, /device:TPU:0, one launch (start us, length us, event | category | flops | bytes accessed | tf_op | source)
XLA Modules:
  0.0 44.9 jit_solution(14644024731537048568)
XLA Ops:
  0.0 3.0 %collective-permute-start.1 = (bf16[512,768]{1,0:T(8,128)(2,1)}, bf16[512,768]{1,0:T(8,128)(2,1)S(1)}, u32[]{:S(2)}, u32[]{:S(2)}) collective-permute-start(bf16[512,768]{1,0:T(8,128)(2,1)} %refs_0_.1), channel_id=1, source_target_pairs={{0,2},{2,0},{4,6},{6,4},{8,10},{10,8},{12,14},{14,12},{1,3},{3,1},... | collective-permute-start | bytes 2359304 | tf_op jit(solution)/shard_map/ppermute | solution.py:28
  3.7 0.7 %copy-done.2 = s32[512]{0:T(512)S(1)} copy-done((s32[512]{0:T(512)S(1)}, s32[512]{0:T(512)}, u32[]{:S(2)}) %copy-start.2) | copy-done | bytes 2072
  4.4 3.7 %collective-permute-start.2 = (bf16[264,768]{1,0:T(8,128)(2,1)S(1)}, bf16[264,768]{1,0:T(8,128)(2,1)S(1)}, u32[]{:S(2)}, u32[]{:S(2)}) collective-permute-start(bf16[264,768]{1,0:T(8,128)(2,1)S(1)} %get-tuple-element.17.refs_9_), channel_id=1, source_target_pairs={{0,12},{2,14},{4,8},{6,10},{8,4},{10,6},{12,0},{14,2},{1,13},{3,15... | collective-permute-start | bytes 1216520 | tf_op jit(solution)/shard_map/ppermute | solution.py:23
  8.8 0.6 %copy-done.3 = s32[4]{0:T(128)S(1)} copy-done((s32[4]{0:T(128)S(1)}, s32[4]{0:T(128)}, u32[]{:S(2)}) %copy-start.3) | copy-done | bytes 40
  9.4 0.5 %shard_map.84.refs_5_ = s32[8,128]{1,0:T(8,128)S(1)} custom-call(s32[4]{0:T(128)S(1)} %copy-done.3, s32[1]{0:T(128)S(6)} %copy.12.count_ref), custom_call_target="tpu_custom_call" | custom-call | flops 1 | bytes 1 | tf_op jit(solution)/shard_map/pallas_call | solution.py:255
  10.0 0.6 %collective-permute-start.4 = (s32[8,128]{1,0:T(8,128)S(1)}, s32[8,128]{1,0:T(8,128)S(1)}, u32[]{:S(2)}, u32[]{:S(2)}) collective-permute-start(s32[8,128]{1,0:T(8,128)S(1)} %shard_map.84.refs_5_), channel_id=1, source_target_pairs={{0,1},{1,0},{2,3},{3,2},{4,5},{5,4},{6,7},{7,6},{8,9},{9,8},{10,11... | collective-permute-start | bytes 12296 | tf_op jit(solution)/shard_map/ppermute | solution.py:28
  10.5 0.8 %collective-permute-done.4.refs_6_ = s32[8,128]{1,0:T(8,128)S(1)} collective-permute-done((s32[8,128]{1,0:T(8,128)S(1)}, s32[8,128]{1,0:T(8,128)S(1)}, u32[]{:S(2)}, u32[]{:S(2)}) %collective-permute-start.4) | collective-permute-done | bytes 4128 | tf_op jit(solution)/shard_map/ppermute | solution.py:28
  11.3 0.5 %collective-permute-start.5 = (s32[8,128]{1,0:T(8,128)S(1)}, s32[8,128]{1,0:T(8,128)S(1)}, u32[]{:S(2)}, u32[]{:S(2)}) collective-permute-start(s32[8,128]{1,0:T(8,128)S(1)} %shard_map.84.refs_5_), channel_id=1, source_target_pairs={{0,2},{2,0},{4,6},{6,4},{8,10},{10,8},{12,14},{14,12},{1,3},{3,1},... | collective-permute-start | bytes 12296 | tf_op jit(solution)/shard_map/ppermute | solution.py:28
  11.9 8.9 %collective-permute-done.5.refs_7_ = s32[8,128]{1,0:T(8,128)S(1)} collective-permute-done((s32[8,128]{1,0:T(8,128)S(1)}, s32[8,128]{1,0:T(8,128)S(1)}, u32[]{:S(2)}, u32[]{:S(2)}) %collective-permute-start.5) | collective-permute-done | bytes 4128 | tf_op jit(solution)/shard_map/ppermute | solution.py:28
  21.1 1.1 %copy-done.1 = bf16[512,768]{1,0:T(8,128)(2,1)S(1)} copy-done((bf16[512,768]{1,0:T(8,128)(2,1)S(1)}, bf16[512,768]{1,0:T(8,128)(2,1)}, u32[]{:S(2)}) %copy-start.1) | copy-done | bytes 786456
  22.3 0.7 %copy-done.4 = f32[64]{0:T(128)S(1)} copy-done((f32[64]{0:T(128)S(1)}, f32[64]{0:T(128)}, u32[]{:S(2)}) %copy-start.4) | copy-done | bytes 280
  23.0 2.6 %collective-permute-start.9 = (bf16[264,768]{1,0:T(8,128)(2,1)S(1)}, bf16[264,768]{1,0:T(8,128)(2,1)S(1)}, u32[]{:S(2)}, u32[]{:S(2)}) collective-permute-start(bf16[264,768]{1,0:T(8,128)(2,1)S(1)} %collective-permute-done.2.refs_10_), channel_id=1, source_target_pairs={{0,4},{2,6},{4,0},{6,2},{8,12},{10,14},{12,8},{14,10},{1,5},{3,7},... | collective-permute-start | bytes 1216520 | tf_op jit(solution)/shard_map/ppermute | solution.py:23
  25.7 0.4 collective-permute-start.7
  26.2 0.3 collective-permute-start.10
  26.6 0.9 %collective-permute-done.7.refs_3_ = bf16[256,768]{1,0:T(8,128)(2,1)S(1)} collective-permute-done((bf16[256,768]{1,0:T(8,128)(2,1)S(1)}, bf16[256,768]{1,0:T(8,128)(2,1)S(1)}, u32[]{:S(2)}, u32[]{:S(2)}) %collective-permute-start.7) | collective-permute-done | bytes 393248 | tf_op jit(solution)/shard_map/ppermute | solution.py:28
  27.4 0.6 %collective-permute-done.8.refs_4_ = bf16[256,768]{1,0:T(8,128)(2,1)S(1)} collective-permute-done((bf16[256,768]{1,0:T(8,128)(2,1)S(1)}, bf16[256,768]{1,0:T(8,128)(2,1)S(1)}, u32[]{:S(2)}, u32[]{:S(2)}) %collective-permute-start.8) | collective-permute-done | bytes 393248 | tf_op jit(solution)/shard_map/ppermute | solution.py:28
  28.0 4.2 %shard_map.85 = (f32[16,128]{1,0:T(8,128)S(1)}, bf16[2048,768]{1,0:T(8,128)(2,1)S(1)}, s32[8,128]{1,0:T(8,128)S(1)}) custom-call(f32[1,64]{1,0:T(1,128)S(1)} %get-tuple-element.15.beta_ref, bf16[512,768]{1,0:T(8,128)(2,1)S(1)} %get-tuple-element.16.refs_0_, bf16[512,768]{1,0:T(8,128)(2,1)S(1)} %collective-permute-done.refs_1_, ...), custom_call_target="tpu_custom_call" | custom-call | flops 1 | bytes 1 | tf_op jit(solution)/shard_map/pallas_call | solution.py:195
  32.3 3.5 %collective-permute-done.9.refs_3_ = bf16[264,768]{1,0:T(8,128)(2,1)S(1)} collective-permute-done((bf16[264,768]{1,0:T(8,128)(2,1)S(1)}, bf16[264,768]{1,0:T(8,128)(2,1)S(1)}, u32[]{:S(2)}, u32[]{:S(2)}) %collective-permute-start.9) | collective-permute-done | bytes 405536 | tf_op jit(solution)/shard_map/ppermute | solution.py:23
  35.8 2.2 %shard_map.86.refs_2_ = f32[16,128]{1,0:T(8,128)S(1)} custom-call(f32[1,64]{1,0:T(1,128)S(1)} %get-tuple-element.15.beta_ref, s32[8,128]{1,0:T(8,128)S(1)} %get-tuple-element.21.refs_0_, bf16[2048,768]{1,0:T(8,128)(2,1)S(1)} %get-tuple-element.22.refs_1_, f32[16,128]{1,0:T(8,128)S(1)} %get-tuple-element.23.refs_2_, ...), custom_call_target="tpu_custom_call" | custom-call | flops 1 | bytes 1 | tf_op jit(solution)/shard_map/pallas_call | solution.py:195
  38.0 2.1 %shard_map.87 = f32[16,128]{1,0:T(8,128)S(1)} custom-call(f32[1,64]{1,0:T(1,128)S(1)} %get-tuple-element.15.beta_ref, s32[8,128]{1,0:T(8,128)S(1)} %get-tuple-element.21.refs_0_, bf16[2048,768]{1,0:T(8,128)(2,1)S(1)} %get-tuple-element.22.refs_1_, f32[16,128]{1,0:T(8,128)S(1)} %shard_map.86.refs_2_, bf16[64,768]{1,0:T(8,128)(2,1)S(1)} %collective-permute-done.10.refs_3_, ...), custom_call_target="tpu_custom_call" | custom-call | flops 1 | bytes 1 | tf_op jit(solution)/shard_map/pallas_call | solution.py:195
  40.5 0.8 %collective-permute-start.12 = (f32[4,128]{1,0:T(4,128)S(1)}, f32[4,128]{1,0:T(4,128)S(1)}, u32[]{:S(2)}, u32[]{:S(2)}) collective-permute-start(f32[4,128]{1,0:T(4,128)S(1)} %get-tuple-element.29), channel_id=1, source_target_pairs={{0,2},{2,0},{4,6},{6,4},{8,10},{10,8},{12,14},{14,12},{1,3},{3,1},... | collective-permute-start | bytes 6152 | tf_op jit(solution)/shard_map/ppermute | solution.py:28
  41.2 0.9 %collective-permute-start.13 = (f32[4,128]{1,0:T(4,128)S(1)}, f32[4,128]{1,0:T(4,128)S(1)}, u32[]{:S(2)}, u32[]{:S(2)}) collective-permute-start(f32[4,128]{1,0:T(4,128)S(1)} %get-tuple-element.28), channel_id=1, source_target_pairs={{0,3},{1,2},{2,1},{3,0},{4,7},{5,6},{6,5},{7,4},{8,11},{9,10},{10,... | collective-permute-start | bytes 6152 | tf_op jit(solution)/shard_map/ppermute | solution.py:34
  42.3 1.7 %collective-permute-done.12 = f32[4,128]{1,0:T(4,128)S(1)} collective-permute-done((f32[4,128]{1,0:T(4,128)S(1)}, f32[4,128]{1,0:T(4,128)S(1)}, u32[]{:S(2)}, u32[]{:S(2)}) %collective-permute-start.12) | collective-permute-done | bytes 2080 | tf_op jit(solution)/shard_map/ppermute | solution.py:28
  44.3 0.7 %log-plus-one_bitcast_fusion = f32[512]{0:T(512)} fusion(f32[4,128]{1,0:T(4,128)S(1)} %collective-permute-done.13, f32[4,128]{1,0:T(4,128)S(1)} %collective-permute-done.12, f32[4,128]{1,0:T(4,128)S(1)} %collective-permute-done.11, f32[16,128]{1,0:T(8,128)S(1)} %shard_map.87, f32[4]{0:T(128)S(1)} %convert_element_type.7), kind=kLoop, calls=%fused_computation.4 | loop fusion | flops 2048 | bytes 10256 | tf_op jit(solution)/shard_map/reshape | solution.py:301
  (28 shorter events, 1.5 us)
Async XLA Ops:
  0.0 3.6 %copy-start = (bf16[512,768]{1,0:T(8,128)(2,1)S(1)}, bf16[512,768]{1,0:T(8,128)(2,1)}, u32[]{:S(2)}) copy-start(bf16[512,768]{1,0:T(8,128)(2,1)} %param.11) | copy-start | bytes 2359300
  0.0 25.6 %collective-permute-start.1 = (bf16[512,768]{1,0:T(8,128)(2,1)}, bf16[512,768]{1,0:T(8,128)(2,1)S(1)}, u32[]{:S(2)}, u32[]{:S(2)}) collective-permute-start(bf16[512,768]{1,0:T(8,128)(2,1)} %refs_0_.1), channel_id=1, source_target_pairs={{0,2},{2,0},{4,6},{6,4},{8,10},{10,8},{12,14},{14,12},{1,3},{3,1},... | collective-permute-start | bytes 2359304 | tf_op jit(solution)/shard_map/ppermute | solution.py:28
  3.7 0.7 %copy-start.2 = (s32[512]{0:T(512)S(1)}, s32[512]{0:T(512)}, u32[]{:S(2)}) copy-start(s32[512]{0:T(512)} %param.12) | copy-start | bytes 6148
  4.4 18.6 %collective-permute-start.2 = (bf16[264,768]{1,0:T(8,128)(2,1)S(1)}, bf16[264,768]{1,0:T(8,128)(2,1)S(1)}, u32[]{:S(2)}, u32[]{:S(2)}) collective-permute-start(bf16[264,768]{1,0:T(8,128)(2,1)S(1)} %get-tuple-element.17.refs_9_), channel_id=1, source_target_pairs={{0,12},{2,14},{4,8},{6,10},{8,4},{10,6},{12,0},{14,2},{1,13},{3,15... | collective-permute-start | bytes 1216520 | tf_op jit(solution)/shard_map/ppermute | solution.py:23
  8.1 17.5 %collective-permute-start.3 = (bf16[200,768]{1,0:T(8,128)(2,1)S(1)}, bf16[200,768]{1,0:T(8,128)(2,1)S(1)}, u32[]{:S(2)}, u32[]{:S(2)}) collective-permute-start(bf16[200,768]{1,0:T(8,128)(2,1)S(1)} %get-tuple-element.18), channel_id=1, source_target_pairs={{0,4},{2,6},{4,0},{6,2},{8,12},{10,14},{12,8},{14,10},{1,5},{3,7},... | collective-permute-start | bytes 921608 | tf_op jit(solution)/shard_map/ppermute | solution.py:23
  8.1 18.5 %collective-permute-start = (bf16[512,768]{1,0:T(8,128)(2,1)}, bf16[512,768]{1,0:T(8,128)(2,1)S(1)}, u32[]{:S(2)}, u32[]{:S(2)}) collective-permute-start(bf16[512,768]{1,0:T(8,128)(2,1)} %refs_0_.1), channel_id=1, source_target_pairs={{0,1},{1,0},{2,3},{3,2},{4,5},{5,4},{6,7},{7,6},{8,9},{9,8},{10,11... | collective-permute-start | bytes 2359304 | tf_op jit(solution)/shard_map/ppermute | solution.py:28
  8.7 0.7 %copy-start.3 = (s32[4]{0:T(128)S(1)}, s32[4]{0:T(128)}, u32[]{:S(2)}) copy-start(s32[4]{0:T(128)} %clusters_ref) | copy-start | bytes 52
  10.0 1.4 %collective-permute-start.4 = (s32[8,128]{1,0:T(8,128)S(1)}, s32[8,128]{1,0:T(8,128)S(1)}, u32[]{:S(2)}, u32[]{:S(2)}) collective-permute-start(s32[8,128]{1,0:T(8,128)S(1)} %shard_map.84.refs_5_), channel_id=1, source_target_pairs={{0,1},{1,0},{2,3},{3,2},{4,5},{5,4},{6,7},{7,6},{8,9},{9,8},{10,11... | collective-permute-start | bytes 12296 | tf_op jit(solution)/shard_map/ppermute | solution.py:28
  11.3 9.5 %collective-permute-start.5 = (s32[8,128]{1,0:T(8,128)S(1)}, s32[8,128]{1,0:T(8,128)S(1)}, u32[]{:S(2)}, u32[]{:S(2)}) collective-permute-start(s32[8,128]{1,0:T(8,128)S(1)} %shard_map.84.refs_5_), channel_id=1, source_target_pairs={{0,2},{2,0},{4,6},{6,4},{8,10},{10,8},{12,14},{14,12},{1,3},{3,1},... | collective-permute-start | bytes 12296 | tf_op jit(solution)/shard_map/ppermute | solution.py:28
  20.8 4.8 %collective-permute-start.6 = (s32[8,128]{1,0:T(8,128)S(1)}, s32[8,128]{1,0:T(8,128)S(1)}, u32[]{:S(2)}, u32[]{:S(2)}) collective-permute-start(s32[8,128]{1,0:T(8,128)S(1)} %shard_map.84.refs_5_), channel_id=1, source_target_pairs={{0,3},{1,2},{2,1},{3,0},{4,7},{5,6},{6,5},{7,4},{8,11},{9,10},{10,... | collective-permute-start | bytes 12296 | tf_op jit(solution)/shard_map/ppermute | solution.py:34
  21.1 1.1 %copy-start.1 = (bf16[512,768]{1,0:T(8,128)(2,1)S(1)}, bf16[512,768]{1,0:T(8,128)(2,1)}, u32[]{:S(2)}) copy-start(bf16[512,768]{1,0:T(8,128)(2,1)} %refs_0_.1) | copy-start | bytes 2359300
  22.3 0.7 %copy-start.4 = (f32[64]{0:T(128)S(1)}, f32[64]{0:T(128)}, u32[]{:S(2)}) copy-start(f32[64]{0:T(128)} %param.14) | copy-start | bytes 772
  23.0 12.8 %collective-permute-start.9 = (bf16[264,768]{1,0:T(8,128)(2,1)S(1)}, bf16[264,768]{1,0:T(8,128)(2,1)S(1)}, u32[]{:S(2)}, u32[]{:S(2)}) collective-permute-start(bf16[264,768]{1,0:T(8,128)(2,1)S(1)} %collective-permute-done.2.refs_10_), channel_id=1, source_target_pairs={{0,4},{2,6},{4,0},{6,2},{8,12},{10,14},{12,8},{14,10},{1,5},{3,7},... | collective-permute-start | bytes 1216520 | tf_op jit(solution)/shard_map/ppermute | solution.py:23
  25.7 1.8 %collective-permute-start.7 = (bf16[256,768]{1,0:T(8,128)(2,1)S(1)}, bf16[256,768]{1,0:T(8,128)(2,1)S(1)}, u32[]{:S(2)}, u32[]{:S(2)}) collective-permute-start(bf16[256,768]{1,0:T(8,128)(2,1)S(1)} %get-tuple-element.26), channel_id=1, source_target_pairs={{0,1},{1,0},{2,3},{3,2},{4,5},{5,4},{6,7},{7,6},{8,9},{9,8},{10,11... | collective-permute-start | bytes 1179656 | tf_op jit(solution)/shard_map/ppermute | solution.py:28
  26.0 2.0 %collective-permute-start.8 = (bf16[256,768]{1,0:T(8,128)(2,1)S(1)}, bf16[256,768]{1,0:T(8,128)(2,1)S(1)}, u32[]{:S(2)}, u32[]{:S(2)}) collective-permute-start(bf16[256,768]{1,0:T(8,128)(2,1)S(1)} %get-tuple-element.25), channel_id=1, source_target_pairs={{0,1},{1,0},{2,3},{3,2},{4,5},{5,4},{6,7},{7,6},{8,9},{9,8},{10,11... | collective-permute-start | bytes 1179656 | tf_op jit(solution)/shard_map/ppermute | solution.py:28
  26.2 11.8 %collective-permute-start.10 = (bf16[64,768]{1,0:T(8,128)(2,1)S(1)}, bf16[64,768]{1,0:T(8,128)(2,1)S(1)}, u32[]{:S(2)}, u32[]{:S(2)}) collective-permute-start(bf16[64,768]{1,0:T(8,128)(2,1)S(1)} %get-tuple-element.24), channel_id=1, source_target_pairs={{0,4},{2,6},{4,0},{6,2},{8,12},{10,14},{12,8},{14,10},{1,5},{3,7},... | collective-permute-start | bytes 294920 | tf_op jit(solution)/shard_map/ppermute | solution.py:23
  35.8 6.3 %copy-start.5 = (s32[64]{0:T(128)S(1)}, s32[64]{0:T(128)}, u32[]{:S(2)}) copy-start(s32[64]{0:T(128)} %param.15) | copy-start | bytes 772
  40.2 2.1 %collective-permute-start.11 = (f32[4,128]{1,0:T(4,128)S(1)}, f32[4,128]{1,0:T(4,128)S(1)}, u32[]{:S(2)}, u32[]{:S(2)}) collective-permute-start(f32[4,128]{1,0:T(4,128)S(1)} %get-tuple-element.27), channel_id=1, source_target_pairs={{0,1},{1,0},{2,3},{3,2},{4,5},{5,4},{6,7},{7,6},{8,9},{9,8},{10,11... | collective-permute-start | bytes 6152 | tf_op jit(solution)/shard_map/ppermute | solution.py:28
  40.5 3.6 %collective-permute-start.12 = (f32[4,128]{1,0:T(4,128)S(1)}, f32[4,128]{1,0:T(4,128)S(1)}, u32[]{:S(2)}, u32[]{:S(2)}) collective-permute-start(f32[4,128]{1,0:T(4,128)S(1)} %get-tuple-element.29), channel_id=1, source_target_pairs={{0,2},{2,0},{4,6},{6,4},{8,10},{10,8},{12,14},{14,12},{1,3},{3,1},... | collective-permute-start | bytes 6152 | tf_op jit(solution)/shard_map/ppermute | solution.py:28
  41.2 3.0 %collective-permute-start.13 = (f32[4,128]{1,0:T(4,128)S(1)}, f32[4,128]{1,0:T(4,128)S(1)}, u32[]{:S(2)}, u32[]{:S(2)}) collective-permute-start(f32[4,128]{1,0:T(4,128)S(1)} %get-tuple-element.28), channel_id=1, source_target_pairs={{0,3},{1,2},{2,1},{3,0},{4,7},{5,6},{6,5},{7,4},{8,11},{9,10},{10,... | collective-permute-start | bytes 6152 | tf_op jit(solution)/shard_map/ppermute | solution.py:34

commit v16 on v14

--- a/solution.py
+++ b/solution.py
@@ -73,22 +73,23 @@
         out[...] = source[...]
 
 
-def score_kernel(chunks, qblocks, pieces, first, wide, beta_ref, *refs):
-    if first:
-        (*given, out_ref, qv, info_out, q_list, ids_ref, other_ref, info, info_sem) = refs
+def score_kernel(chunks, qblocks, pieces, first, wide, *refs):
+    if first:
+        (beta_ref, *given, out_ref, qv, slot_ref, number_ref, info_v, info, ids_ref, other_ref, info_sem) = refs
         q_refs = []
         for n in pieces:
             q_refs.append(given[:n])
             given = given[n:]
         t_refs, r_refs = given[:4], given[4:]
     else:
-        (info, qv, prev_ref, *r_refs, out_ref, q_list, ids_ref, other_ref) = refs
+        (slot_ref, number_ref, qv, prev_ref, *r_refs, out_ref, ids_ref, other_ref) = refs
     width = qv.shape[1]
     height = chunks * LANES
+    slots = 4 * qblocks
     if first:
         for s, t_ref in enumerate(t_refs):
-            info_out[s : s + 1, :] = t_ref[0:1, :]
-        copy = pltpu.make_async_copy(info_out, info, info_sem)
+            info_v[s : s + 1, :] = t_ref[0:1, :]
+        copy = pltpu.make_async_copy(info_v, info, info_sem)
         copy.start()
 
     for s, r_ref in enumerate(r_refs):
@@ -98,43 +99,53 @@
             rows = pl.ds(s * height + c * LANES, LANES)
             ids_ref[rows, :] = ids
             other_ref[rows, :] = jnp.where(ids < 0.0, DEAD, -4.0)
+
     if first:
         copy.wait()
-
-    q_count = jnp.int32(0)
-    for source in range(4):
-        blocks = info[source, qblocks]
-
-        def one_block(block, carry, source=source, q_count=q_count):
-            q_list[q_count + block, 0] = source * qblocks + block
-            q_list[q_count + block, 1] = info[source, block]
+        factor = LOG2E / math.sqrt(width)
+        q_count = jnp.int32(0)
+        for source in range(4):
+            blocks = info[source, qblocks]
+
+            def enter(block, carry, source=source, q_count=q_count):
+                entry = q_count + block
+                cluster = info[source, block]
+                beta = beta_ref[0, cluster]
+                slot_ref[entry] = source * qblocks + block
+                number_ref[3 * entry] = cluster.astype(jnp.float32)
+                number_ref[3 * entry + 1] = beta * factor
+                number_ref[3 * entry + 2] = beta * beta * (0.5 * LOG2E)
+                return carry
+
+            lax.fori_loop(0, blocks, enter, 0)
+            start = 0
+            for piece in q_refs[source]:
+                each = piece.shape[0] // LANES
+
+                def move(block, carry, place=q_count + start, piece=piece):
+                    qv[rows_of(place + block), :] = piece[rows_of(block), :]
+                    return carry
+
+                lax.fori_loop(0, jnp.clip(blocks - start, 0, each), move, 0)
+                start += each
+            q_count = q_count + blocks
+
+        def spare(entry, carry):
+            slot_ref[entry] = slots
+            for i in range(3):
+                number_ref[3 * entry + i] = 0.0
             return carry
 
-        lax.fori_loop(0, blocks, one_block, 0)
-        start = 0
-        for piece in q_refs[source] if first else ():
-            each = piece.shape[0] // LANES
-
-            def move(block, carry, place=q_count + start, piece=piece):
-                qv[rows_of(place + block), :] = piece[rows_of(block), :]
-                return carry
-
-            lax.fori_loop(0, jnp.clip(blocks - start, 0, each), move, 0)
-            start += each
-        q_count = q_count + blocks
-
-    factor = LOG2E / math.sqrt(width)
-    out_ref[...] = jnp.zeros_like(out_ref) if first else prev_ref[...]
+        lax.fori_loop(q_count, slots, spare, 0)
+        slot_ref[slots] = q_count
+        out_ref[...] = jnp.zeros_like(out_ref)
+    else:
+        q_count = slot_ref[slots]
+        out_ref[...] = prev_ref[...]
 
     def query_blocks(group, carry):
-        sides = []
-        for side in range(wide):
-            entry = jnp.minimum(wide * group + side, q_count - 1)
-            slot, cluster = q_list[entry, 0], q_list[entry, 1]
-            beta = beta_ref[cluster]
-            sides.append(
-                (slot, cluster.astype(jnp.float32), beta * factor, beta * beta * (0.5 * LOG2E))
-            )
+        sides = [wide * group + side for side in range(wide)]
+        numbers = [[number_ref[3 * entry + i] for i in range(3)] for entry in sides]
         accs = [jnp.zeros((8, LANES), jnp.float32) for _ in range(wide)]
         for s, r_ref in enumerate(r_refs):
             tile = r_ref[pl.ds(0, height), :]
@@ -148,47 +159,43 @@
                 )
                 for half in range(2):
                     side = 2 * pair + half
-                    _, cluster, scale, offset = sides[side]
+                    cluster, scale, offset = numbers[side]
                     part = score[:, half * LANES : (half + 1) * LANES]
                     weight = jnp.where(ids_ref[rows, :] == cluster, 0.0, other_ref[rows, :])
                     value = jnp.exp2((part * scale - offset) + weight)
                     accs[side] += jnp.sum(value.reshape(height // 8, 8, LANES), axis=0)
-        for side in range(wide):
-            total = jnp.sum(accs[side], axis=0, keepdims=True)
-
-            @pl.when(wide * group + side < q_count)
-            def _(side=side, total=total):
-                row = pl.ds(sides[side][0], 1)
-                out_ref[row, :] = out_ref[row, :] + total
-
+        for entry, acc in zip(sides, accs):
+            row = pl.ds(slot_ref[entry], 1)
+            out_ref[row, :] = out_ref[row, :] + jnp.sum(acc, axis=0, keepdims=True)
         return carry
 
     lax.fori_loop(0, (q_count + wide - 1) // wide, query_blocks, 0)
 
 
-def score_call(chunks, qblocks, pieces, wide, beta, given, payloads, first):
+def score_call(chunks, qblocks, pieces, wide, given, payloads, first):
     width = payloads[0].shape[1]
     slots = 4 * qblocks
-    height = chunks * LANES
-    totals_shape = jax.ShapeDtypeStruct((slots, LANES), jnp.float32)
+    rows = len(payloads) * chunks * LANES
+    totals_shape = jax.ShapeDtypeStruct((slots + 8, LANES), jnp.float32)
     packed_shape = jax.ShapeDtypeStruct((slots * LANES, width), jnp.bfloat16)
-    info_shape = jax.ShapeDtypeStruct((8, LANES), jnp.int32)
-    spread = pltpu.VMEM((len(payloads) * height, LANES), jnp.float32)
-    scratch = [pltpu.SMEM((slots, 2), jnp.int32), spread, spread]
-    specs = [VMEM] * (len(given) + len(payloads))
-    if first:
-        scratch += [pltpu.SMEM((8, LANES), jnp.int32), pltpu.SemaphoreType.DMA]
+    slot_shape = jax.ShapeDtypeStruct((slots + 8,), jnp.int32)
+    number_shape = jax.ShapeDtypeStruct((3 * slots,), jnp.float32)
+    scratch = [pltpu.VMEM((rows, LANES), jnp.float32)] * 2
+    if first:
+        scratch = [pltpu.VMEM((8, LANES), jnp.int32), pltpu.SMEM((8, LANES), jnp.int32)] + scratch
+        scratch.append(pltpu.SemaphoreType.DMA)
+        specs = [SMEM] + [VMEM] * (len(given) - 1 + len(payloads))
     else:
-        specs[0] = SMEM
+        specs = [SMEM] * 2 + [VMEM] * (len(given) - 2 + len(payloads))
     return pl.pallas_call(
         functools.partial(score_kernel, chunks, qblocks, pieces, first, wide),
-        out_shape=(totals_shape, packed_shape, info_shape) if first else totals_shape,
-        in_specs=[SMEM] + specs,
-        out_specs=(VMEM, VMEM, VMEM) if first else VMEM,
+        out_shape=(totals_shape, packed_shape, slot_shape, number_shape) if first else totals_shape,
+        in_specs=specs,
+        out_specs=(VMEM, VMEM, SMEM, SMEM) if first else VMEM,
         scratch_shapes=scratch,
         compiler_params=PARAMS,
         cost_estimate=cost(1, 1),
-    )(beta, *given, *payloads)
+    )(*given, *payloads)
 
 
 def per_device(
@@ -241,40 +248,26 @@
         cost_estimate=cost(1, 1),
     )(after(query_block_cluster, own), block_count)
     q_tables = (table, swap(table, "helper"), swap(table, "blk"), swap_both(table))
-    staged = pl.pallas_call(
+    beta = cluster_beta.reshape(1, -1)
+    staged, beta = pl.pallas_call(
         stage_kernel,
-        out_shape=jax.ShapeDtypeStruct(queries.shape, queries.dtype),
-        in_specs=[VMEM],
-        out_specs=VMEM,
-        compiler_params=PARAMS,
-        cost_estimate=cost(1, 1),
-    )(queries)
+        out_shape=[jax.ShapeDtypeStruct(x.shape, x.dtype) for x in (queries, beta)],
+        in_specs=[VMEM] * 2,
+        out_specs=[VMEM] * 2,
+        compiler_params=PARAMS,
+        cost_estimate=cost(1, 1),
+    )(queries, beta)
     q_partner = after(q_partner, staged, *held[1:-1], *q_tables)
     half = qblocks // 2 * LANES
     q_both = [swap(q_partner[:half], "helper"), swap(q_partner[half:], "helper")]
     queries = (staged, q_helper, q_partner, *q_both)
     pieces = (1, 1, 1, 2)
 
-    totals, packed, info = score_call(
-        chunks,
-        qblocks,
-        pieces,
-        2,
-        cluster_beta,
-        (*queries, *q_tables),
-        held[:-1],
-        True,
-    )
-    totals = score_call(
-        chunks,
-        qblocks,
-        pieces,
-        8,
-        cluster_beta,
-        (info, packed, totals),
-        held[-1:],
-        False,
-    )
+    given = (beta, *queries, *q_tables)
+    totals, packed, *plan = score_call(chunks, qblocks, pieces, 4, given, held[:-1], True)
+    given = (*plan, packed, totals)
+    totals = score_call(chunks, qblocks, pieces, 8, given, held[-1:], False)
+    totals = totals[: 4 * qblocks]
     totals = totals.reshape(4, qblocks, LANES)
     total = totals[0] + swap(totals[1], "helper") + swap(totals[2], "blk") + swap_both(totals[3])
     columns = jnp.arange(cluster_member_count.shape[0], dtype=jnp.int32)

time: 41.7 us -> 42.3 us (1.014)
  local copies, waits for them, and re-layouts: 2.56 us -> 3.21 us
  starting transfers between devices: 13.8 us -> 13.2 us
  waiting for transfers between devices: 15.5 us -> 16 us
    ppermute x3, starting transfers between devices: 6.92 us -> 6.26 us  [trade(): return lax.ppermute(value, 'blk', [(i, i ^ mask) for i in range(length)])]
    unnamed x12, local copies, waits for them, and re-layouts: 2.47 us -> 3.12 us
    ppermute x3, waiting for transfers between devices: 2.3 us -> 2.86 us  [trade(): return lax.ppermute(value, 'blk', [(i, i ^ mask) for i in range(length)])]
where the time goes in v16:
time: 42.3 us; the launch traced here: 42.1 us
  waiting for transfers between devices  16 us (38%)
  starting transfers between devices  13.2 us (31%)
  Pallas kernels  7.48 us (18%)
  local copies, waits for them, and re-layouts  3.21 us (8%)
  between operations  1.4 us (3%)
  other arithmetic  0.85 us (2%)
    ppermute x8, waiting for transfers between devices, swap(): return lax.ppermute(value, axis, [(i, i ^ 1) for i in range(length)])  13.2 us
    pallas_call x2, Pallas kernels, score_call(): pl.pallas_call(functools.partial(score_kernel, chunks, qblocks, pieces, f...  6.85 us
    ppermute x3, starting transfers between devices, trade(): return lax.ppermute(value, 'blk', [(i, i ^ mask) for i in range(length)])  6.26 us
    ppermute x8, starting transfers between devices, swap(): return lax.ppermute(value, axis, [(i, i ^ 1) for i in range(length)])  5.27 us
    unnamed x12, local copies, waits for them, and re-layouts  3.12 us
    ppermute x3, waiting for transfers between devices, trade(): return lax.ppermute(value, 'blk', [(i, i ^ mask) for i in range(length)])  2.86 us
    ppermute x2, starting transfers between devices, swap_both(): return lax.ppermute(value, ('blk', 'helper'), pairs)  1.63 us
  transfers between devices with their start and end apart: 13, of which 7 were waited for; matrix products, arithmetic and copies ran while one was open for 1% of the time, Pallas kernels for 13%

profile of v16, /device:TPU:0, one launch (start us, length us, event | category | flops | bytes accessed | tf_op | source)
XLA Modules:
  0.0 42.1 jit_solution(3189229710308488369)
XLA Ops:
  0.0 3.0 %collective-permute-start.1 = (bf16[512,768]{1,0:T(8,128)(2,1)}, bf16[512,768]{1,0:T(8,128)(2,1)S(1)}, u32[]{:S(2)}, u32[]{:S(2)}) collective-permute-start(bf16[512,768]{1,0:T(8,128)(2,1)} %refs_0_.1), channel_id=1, source_target_pairs={{0,2},{2,0},{4,6},{6,4},{8,10},{10,8},{12,14},{14,12},{1,3},{3,1},... | collective-permute-start | bytes 2359304 | tf_op jit(solution)/shard_map/ppermute | solution.py:27
  3.7 0.7 %copy-done.2 = s32[512]{0:T(512)S(1)} copy-done((s32[512]{0:T(512)S(1)}, s32[512]{0:T(512)}, u32[]{:S(2)}) %copy-start.2) | copy-done | bytes 2072
  4.4 3.7 %collective-permute-start.2 = (bf16[264,768]{1,0:T(8,128)(2,1)S(1)}, bf16[264,768]{1,0:T(8,128)(2,1)S(1)}, u32[]{:S(2)}, u32[]{:S(2)}) collective-permute-start(bf16[264,768]{1,0:T(8,128)(2,1)S(1)} %shard_map.83.refs_10_), channel_id=1, source_target_pairs={{0,12},{2,14},{4,8},{6,10},{8,4},{10,6},{12,0},{14,2},{1,13},{3,15... | collective-permute-start | bytes 1216520 | tf_op jit(solution)/shard_map/ppermute | solution.py:22
  8.7 0.6 %copy-done.3 = s32[4]{0:T(128)S(1)} copy-done((s32[4]{0:T(128)S(1)}, s32[4]{0:T(128)}, u32[]{:S(2)}) %copy-start.3) | copy-done | bytes 40
  9.4 0.5 %shard_map.84.refs_6_ = s32[8,128]{1,0:T(8,128)S(1)} custom-call(s32[4]{0:T(128)S(1)} %copy-done.3, s32[1]{0:T(128)S(6)} %copy.12.count_ref), custom_call_target="tpu_custom_call" | custom-call | flops 1 | bytes 1 | tf_op jit(solution)/shard_map/pallas_call | solution.py:242
  9.9 0.6 %collective-permute-start.4 = (s32[8,128]{1,0:T(8,128)S(1)}, s32[8,128]{1,0:T(8,128)S(1)}, u32[]{:S(2)}, u32[]{:S(2)}) collective-permute-start(s32[8,128]{1,0:T(8,128)S(1)} %shard_map.84.refs_6_), channel_id=1, source_target_pairs={{0,1},{1,0},{2,3},{3,2},{4,5},{5,4},{6,7},{7,6},{8,9},{9,8},{10,11... | collective-permute-start | bytes 12296 | tf_op jit(solution)/shard_map/ppermute | solution.py:27
  10.5 0.8 %collective-permute-done.4.refs_7_ = s32[8,128]{1,0:T(8,128)S(1)} collective-permute-done((s32[8,128]{1,0:T(8,128)S(1)}, s32[8,128]{1,0:T(8,128)S(1)}, u32[]{:S(2)}, u32[]{:S(2)}) %collective-permute-start.4) | collective-permute-done | bytes 4128 | tf_op jit(solution)/shard_map/ppermute | solution.py:27
  11.3 0.5 %collective-permute-start.5 = (s32[8,128]{1,0:T(8,128)S(1)}, s32[8,128]{1,0:T(8,128)S(1)}, u32[]{:S(2)}, u32[]{:S(2)}) collective-permute-start(s32[8,128]{1,0:T(8,128)S(1)} %shard_map.84.refs_6_), channel_id=1, source_target_pairs={{0,2},{2,0},{4,6},{6,4},{8,10},{10,8},{12,14},{14,12},{1,3},{3,1},... | collective-permute-start | bytes 12296 | tf_op jit(solution)/shard_map/ppermute | solution.py:27
  11.8 9.0 %collective-permute-done.5.refs_8_ = s32[8,128]{1,0:T(8,128)S(1)} collective-permute-done((s32[8,128]{1,0:T(8,128)S(1)}, s32[8,128]{1,0:T(8,128)S(1)}, u32[]{:S(2)}, u32[]{:S(2)}) %collective-permute-start.5) | collective-permute-done | bytes 4128 | tf_op jit(solution)/shard_map/ppermute | solution.py:27
  20.8 0.3 collective-permute-start.6
  21.1 1.1 %copy-done.1 = bf16[512,768]{1,0:T(8,128)(2,1)S(1)} copy-done((bf16[512,768]{1,0:T(8,128)(2,1)S(1)}, bf16[512,768]{1,0:T(8,128)(2,1)}, u32[]{:S(2)}) %copy-start.1) | copy-done | bytes 786456
  22.3 0.7 %copy-done.4 = f32[64]{0:T(128)S(1)} copy-done((f32[64]{0:T(128)S(1)}, f32[64]{0:T(128)}, u32[]{:S(2)}) %copy-start.4) | copy-done | bytes 280
  23.0 2.6 %collective-permute-start.9 = (bf16[264,768]{1,0:T(8,128)(2,1)S(1)}, bf16[264,768]{1,0:T(8,128)(2,1)S(1)}, u32[]{:S(2)}, u32[]{:S(2)}) collective-permute-start(bf16[264,768]{1,0:T(8,128)(2,1)S(1)} %collective-permute-done.2.refs_11_), channel_id=1, source_target_pairs={{0,4},{2,6},{4,0},{6,2},{8,12},{10,14},{12,8},{14,10},{1,5},{3,7},... | collective-permute-start | bytes 1216520 | tf_op jit(solution)/shard_map/ppermute | solution.py:22
  25.6 0.4 collective-permute-done.3.refs_12_
  26.1 0.5 %collective-permute-start.8 = (bf16[256,768]{1,0:T(8,128)(2,1)S(1)}, bf16[256,768]{1,0:T(8,128)(2,1)S(1)}, u32[]{:S(2)}, u32[]{:S(2)}) collective-permute-start(bf16[256,768]{1,0:T(8,128)(2,1)S(1)} %get-tuple-element.21), channel_id=1, source_target_pairs={{0,1},{1,0},{2,3},{3,2},{4,5},{5,4},{6,7},{7,6},{8,9},{9,8},{10,11... | collective-permute-start | bytes 1179656 | tf_op jit(solution)/shard_map/ppermute | solution.py:27
  26.6 1.2 %collective-permute-done.7.refs_4_ = bf16[256,768]{1,0:T(8,128)(2,1)S(1)} collective-permute-done((bf16[256,768]{1,0:T(8,128)(2,1)S(1)}, bf16[256,768]{1,0:T(8,128)(2,1)S(1)}, u32[]{:S(2)}, u32[]{:S(2)}) %collective-permute-start.7) | collective-permute-done | bytes 393248 | tf_op jit(solution)/shard_map/ppermute | solution.py:27
  27.8 0.6 %collective-permute-done.8.refs_5_ = bf16[256,768]{1,0:T(8,128)(2,1)S(1)} collective-permute-done((bf16[256,768]{1,0:T(8,128)(2,1)S(1)}, bf16[256,768]{1,0:T(8,128)(2,1)S(1)}, u32[]{:S(2)}, u32[]{:S(2)}) %collective-permute-start.8) | collective-permute-done | bytes 393248 | tf_op jit(solution)/shard_map/ppermute | solution.py:27
  28.4 4.9 %shard_map.85 = (f32[24,128]{1,0:T(8,128)S(1)}, bf16[2048,768]{1,0:T(8,128)(2,1)S(1)}, s32[24]{0:T(128)S(1)}, f32[48]{0:T(128)S(1)}) custom-call(f32[1,64]{1,0:T(1,128)S(1)} %get-tuple-element.13.refs_0_, bf16[512,768]{1,0:T(8,128)(2,1)S(1)} %get-tuple-element.14.refs_1_, bf16[512,768]{1,0:T(8,128)(2,1)S(1)} %collective-permute-done.refs_2_, ...), custom_call_target="tpu_custom_call" | custom-call | flops 1 | bytes 1 | tf_op jit(solution)/shard_map/pallas_call | solution.py:190
  33.2 2.5 %collective-permute-done.9.refs_4_ = bf16[264,768]{1,0:T(8,128)(2,1)S(1)} collective-permute-done((bf16[264,768]{1,0:T(8,128)(2,1)S(1)}, bf16[264,768]{1,0:T(8,128)(2,1)S(1)}, u32[]{:S(2)}, u32[]{:S(2)}) %collective-permute-start.9) | collective-permute-done | bytes 405536 | tf_op jit(solution)/shard_map/ppermute | solution.py:22
  35.7 2.0 %shard_map.86 = f32[24,128]{1,0:T(8,128)S(1)} custom-call(s32[24]{0:T(128)S(1)} %get-tuple-element.17.refs_0_, f32[48]{0:T(128)S(1)} %get-tuple-element.18.refs_1_, bf16[2048,768]{1,0:T(8,128)(2,1)S(1)} %get-tuple-element.19.refs_2_, f32[24,128]{1,0:T(8,128)S(1)} %get-tuple-element.20.refs_3_, bf16[264,768]{1,0:T(8,128)(2,1)S(1)} %collective-permute-done.9.refs_4_), custom_call_target="tpu_custom_call" | custom-call | flops 1 | bytes 1 | tf_op jit(solution)/shard_map/pallas_call | solution.py:190
  37.9 0.5 %collective-permute-start.11 = (f32[4,128]{1,0:T(4,128)S(1)}, f32[4,128]{1,0:T(4,128)S(1)}, u32[]{:S(2)}, u32[]{:S(2)}) collective-permute-start(f32[4,128]{1,0:T(4,128)S(1)} %get-tuple-element.25), channel_id=1, source_target_pairs={{0,2},{2,0},{4,6},{6,4},{8,10},{10,8},{12,14},{14,12},{1,3},{3,1},... | collective-permute-start | bytes 6152 | tf_op jit(solution)/shard_map/ppermute | solution.py:27
  38.4 1.3 %collective-permute-start.12 = (f32[4,128]{1,0:T(4,128)S(1)}, f32[4,128]{1,0:T(4,128)S(1)}, u32[]{:S(2)}, u32[]{:S(2)}) collective-permute-start(f32[4,128]{1,0:T(4,128)S(1)} %get-tuple-element.24), channel_id=1, source_target_pairs={{0,3},{1,2},{2,1},{3,0},{4,7},{5,6},{6,5},{7,4},{8,11},{9,10},{10,... | collective-permute-start | bytes 6152 | tf_op jit(solution)/shard_map/ppermute | solution.py:33
  39.9 1.6 %collective-permute-done.11 = f32[4,128]{1,0:T(4,128)S(1)} collective-permute-done((f32[4,128]{1,0:T(4,128)S(1)}, f32[4,128]{1,0:T(4,128)S(1)}, u32[]{:S(2)}, u32[]{:S(2)}) %collective-permute-start.11) | collective-permute-done | bytes 2080 | tf_op jit(solution)/shard_map/ppermute | solution.py:27
  41.5 0.7 %log-plus-one_bitcast_fusion = f32[512]{0:T(512)} fusion(f32[4,128]{1,0:T(4,128)S(1)} %collective-permute-done.12, f32[4,128]{1,0:T(4,128)S(1)} %collective-permute-done.11, f32[4,128]{1,0:T(4,128)S(1)} %collective-permute-done.10, f32[24,128]{1,0:T(8,128)S(1)} %shard_map.86, f32[4]{0:T(128)S(1)} %convert_element_type.7), kind=kLoop, calls=%fused_computation.4 | loop fusion | flops 2048 | bytes 10256 | tf_op jit(solution)/shard_map/reshape | solution.py:277
  (25 shorter events, 0.7 us)
Async XLA Ops:
  0.0 3.6 %copy-start = (bf16[512,768]{1,0:T(8,128)(2,1)S(1)}, bf16[512,768]{1,0:T(8,128)(2,1)}, u32[]{:S(2)}) copy-start(bf16[512,768]{1,0:T(8,128)(2,1)} %param.11) | copy-start | bytes 2359300
  0.0 25.9 %collective-permute-start.1 = (bf16[512,768]{1,0:T(8,128)(2,1)}, bf16[512,768]{1,0:T(8,128)(2,1)S(1)}, u32[]{:S(2)}, u32[]{:S(2)}) collective-permute-start(bf16[512,768]{1,0:T(8,128)(2,1)} %refs_0_.1), channel_id=1, source_target_pairs={{0,2},{2,0},{4,6},{6,4},{8,10},{10,8},{12,14},{14,12},{1,3},{3,1},... | collective-permute-start | bytes 2359304 | tf_op jit(solution)/shard_map/ppermute | solution.py:27
  3.7 0.7 %copy-start.2 = (s32[512]{0:T(512)S(1)}, s32[512]{0:T(512)}, u32[]{:S(2)}) copy-start(s32[512]{0:T(512)} %param.12) | copy-start | bytes 6148
  4.4 18.6 %collective-permute-start.2 = (bf16[264,768]{1,0:T(8,128)(2,1)S(1)}, bf16[264,768]{1,0:T(8,128)(2,1)S(1)}, u32[]{:S(2)}, u32[]{:S(2)}) collective-permute-start(bf16[264,768]{1,0:T(8,128)(2,1)S(1)} %shard_map.83.refs_10_), channel_id=1, source_target_pairs={{0,12},{2,14},{4,8},{6,10},{8,4},{10,6},{12,0},{14,2},{1,13},{3,15... | collective-permute-start | bytes 1216520 | tf_op jit(solution)/shard_map/ppermute | solution.py:22
  8.1 17.9 %collective-permute-start.3 = (bf16[264,768]{1,0:T(8,128)(2,1)S(1)}, bf16[264,768]{1,0:T(8,128)(2,1)S(1)}, u32[]{:S(2)}, u32[]{:S(2)}) collective-permute-start(bf16[264,768]{1,0:T(8,128)(2,1)S(1)} %shard_map.83.refs_10_), channel_id=1, source_target_pairs={{0,4},{2,6},{4,0},{6,2},{8,12},{10,14},{12,8},{14,10},{1,5},{3,7},... | collective-permute-start | bytes 1216520 | tf_op jit(solution)/shard_map/ppermute | solution.py:22
  8.1 18.5 %collective-permute-start = (bf16[512,768]{1,0:T(8,128)(2,1)}, bf16[512,768]{1,0:T(8,128)(2,1)S(1)}, u32[]{:S(2)}, u32[]{:S(2)}) collective-permute-start(bf16[512,768]{1,0:T(8,128)(2,1)} %refs_0_.1), channel_id=1, source_target_pairs={{0,1},{1,0},{2,3},{3,2},{4,5},{5,4},{6,7},{7,6},{8,9},{9,8},{10,11... | collective-permute-start | bytes 2359304 | tf_op jit(solution)/shard_map/ppermute | solution.py:27
  8.7 0.7 %copy-start.3 = (s32[4]{0:T(128)S(1)}, s32[4]{0:T(128)}, u32[]{:S(2)}) copy-start(s32[4]{0:T(128)} %clusters_ref) | copy-start | bytes 52
  9.9 1.4 %collective-permute-start.4 = (s32[8,128]{1,0:T(8,128)S(1)}, s32[8,128]{1,0:T(8,128)S(1)}, u32[]{:S(2)}, u32[]{:S(2)}) collective-permute-start(s32[8,128]{1,0:T(8,128)S(1)} %shard_map.84.refs_6_), channel_id=1, source_target_pairs={{0,1},{1,0},{2,3},{3,2},{4,5},{5,4},{6,7},{7,6},{8,9},{9,8},{10,11... | collective-permute-start | bytes 12296 | tf_op jit(solution)/shard_map/ppermute | solution.py:27
  11.3 9.5 %collective-permute-start.5 = (s32[8,128]{1,0:T(8,128)S(1)}, s32[8,128]{1,0:T(8,128)S(1)}, u32[]{:S(2)}, u32[]{:S(2)}) collective-permute-start(s32[8,128]{1,0:T(8,128)S(1)} %shard_map.84.refs_6_), channel_id=1, source_target_pairs={{0,2},{2,0},{4,6},{6,4},{8,10},{10,8},{12,14},{14,12},{1,3},{3,1},... | collective-permute-start | bytes 12296 | tf_op jit(solution)/shard_map/ppermute | solution.py:27
  20.8 4.8 %collective-permute-start.6 = (s32[8,128]{1,0:T(8,128)S(1)}, s32[8,128]{1,0:T(8,128)S(1)}, u32[]{:S(2)}, u32[]{:S(2)}) collective-permute-start(s32[8,128]{1,0:T(8,128)S(1)} %shard_map.84.refs_6_), channel_id=1, source_target_pairs={{0,3},{1,2},{2,1},{3,0},{4,7},{5,6},{6,5},{7,4},{8,11},{9,10},{10,... | collective-permute-start | bytes 12296 | tf_op jit(solution)/shard_map/ppermute | solution.py:33
  21.1 1.1 %copy-start.1 = (bf16[512,768]{1,0:T(8,128)(2,1)S(1)}, bf16[512,768]{1,0:T(8,128)(2,1)}, u32[]{:S(2)}) copy-start(bf16[512,768]{1,0:T(8,128)(2,1)} %refs_0_.1) | copy-start | bytes 2359300
  22.3 0.7 %copy-start.4 = (f32[64]{0:T(128)S(1)}, f32[64]{0:T(128)}, u32[]{:S(2)}) copy-start(f32[64]{0:T(128)} %param.14) | copy-start | bytes 772
  23.0 12.7 %collective-permute-start.9 = (bf16[264,768]{1,0:T(8,128)(2,1)S(1)}, bf16[264,768]{1,0:T(8,128)(2,1)S(1)}, u32[]{:S(2)}, u32[]{:S(2)}) collective-permute-start(bf16[264,768]{1,0:T(8,128)(2,1)S(1)} %collective-permute-done.2.refs_11_), channel_id=1, source_target_pairs={{0,4},{2,6},{4,0},{6,2},{8,12},{10,14},{12,8},{14,10},{1,5},{3,7},... | collective-permute-start | bytes 1216520 | tf_op jit(solution)/shard_map/ppermute | solution.py:22
  26.0 1.8 %collective-permute-start.7 = (bf16[256,768]{1,0:T(8,128)(2,1)S(1)}, bf16[256,768]{1,0:T(8,128)(2,1)S(1)}, u32[]{:S(2)}, u32[]{:S(2)}) collective-permute-start(bf16[256,768]{1,0:T(8,128)(2,1)S(1)} %get-tuple-element.22), channel_id=1, source_target_pairs={{0,1},{1,0},{2,3},{3,2},{4,5},{5,4},{6,7},{7,6},{8,9},{9,8},{10,11... | collective-permute-start | bytes 1179656 | tf_op jit(solution)/shard_map/ppermute | solution.py:27
  26.1 2.3 %collective-permute-start.8 = (bf16[256,768]{1,0:T(8,128)(2,1)S(1)}, bf16[256,768]{1,0:T(8,128)(2,1)S(1)}, u32[]{:S(2)}, u32[]{:S(2)}) collective-permute-start(bf16[256,768]{1,0:T(8,128)(2,1)S(1)} %get-tuple-element.21), channel_id=1, source_target_pairs={{0,1},{1,0},{2,3},{3,2},{4,5},{5,4},{6,7},{7,6},{8,9},{9,8},{10,11... | collective-permute-start | bytes 1179656 | tf_op jit(solution)/shard_map/ppermute | solution.py:27
  28.4 11.3 %copy-start.5 = (s32[64]{0:T(128)S(1)}, s32[64]{0:T(128)}, u32[]{:S(2)}) copy-start(s32[64]{0:T(128)} %param.15) | copy-start | bytes 772
  37.7 2.2 %collective-permute-start.10 = (f32[4,128]{1,0:T(4,128)S(1)}, f32[4,128]{1,0:T(4,128)S(1)}, u32[]{:S(2)}, u32[]{:S(2)}) collective-permute-start(f32[4,128]{1,0:T(4,128)S(1)} %get-tuple-element.23), channel_id=1, source_target_pairs={{0,1},{1,0},{2,3},{3,2},{4,5},{5,4},{6,7},{7,6},{8,9},{9,8},{10,11... | collective-permute-start | bytes 6152 | tf_op jit(solution)/shard_map/ppermute | solution.py:27
  37.9 3.6 %collective-permute-start.11 = (f32[4,128]{1,0:T(4,128)S(1)}, f32[4,128]{1,0:T(4,128)S(1)}, u32[]{:S(2)}, u32[]{:S(2)}) collective-permute-start(f32[4,128]{1,0:T(4,128)S(1)} %get-tuple-element.25), channel_id=1, source_target_pairs={{0,2},{2,0},{4,6},{6,4},{8,10},{10,8},{12,14},{14,12},{1,3},{3,1},... | collective-permute-start | bytes 6152 | tf_op jit(solution)/shard_map/ppermute | solution.py:27
  38.4 3.1 %collective-permute-start.12 = (f32[4,128]{1,0:T(4,128)S(1)}, f32[4,128]{1,0:T(4,128)S(1)}, u32[]{:S(2)}, u32[]{:S(2)}) collective-permute-start(f32[4,128]{1,0:T(4,128)S(1)} %get-tuple-element.24), channel_id=1, source_target_pairs={{0,3},{1,2},{2,1},{3,0},{4,7},{5,6},{6,5},{7,4},{8,11},{9,10},{10,... | collective-permute-start | bytes 6152 | tf_op jit(solution)/shard_map/ppermute | solution.py:33

commit v17 on v16

--- a/solution.py
+++ b/solution.py
@@ -172,6 +172,36 @@
     lax.fori_loop(0, (q_count + wide - 1) // wide, query_blocks, 0)
 
 
+def last_kernel(chunks, wide, slot_ref, number_ref, qv, prev_ref, r_ref, out_ref):
+    height = chunks * LANES
+    table = r_ref[pl.ds(height, TABLE), pl.ds(0, LANES)].astype(jnp.float32)
+    ids = [table[c : c + 1, :] for c in range(chunks)]
+    other = [jnp.where(row < 0.0, DEAD, -4.0) for row in ids]
+    out_ref[...] = prev_ref[...]
+
+    def query_blocks(group, carry):
+        score = lax.dot_general(
+            qv[rows_of(wide * group, wide), :],
+            r_ref[pl.ds(0, height), :],
+            (((1,), (1,)), ((), ())),
+            preferred_element_type=jnp.float32,
+        )
+        for side in range(wide):
+            entry = wide * group + side
+            cluster, scale, offset = (number_ref[3 * entry + i] for i in range(3))
+            acc = jnp.zeros((LANES, LANES), jnp.float32)
+            for c in range(chunks):
+                part = score[side * LANES : (side + 1) * LANES, c * LANES : (c + 1) * LANES]
+                bias = jnp.where(ids[c] == cluster, 0.0, other[c]) - offset
+                acc = acc + jnp.exp2(part * scale + bias)
+            row = pl.ds(slot_ref[entry], 1)
+            out_ref[row, :] = out_ref[row, :] + jnp.sum(acc.T, axis=0, keepdims=True)
+        return carry
+
+    q_count = slot_ref[slot_ref.shape[0] - 8]
+    lax.fori_loop(0, (q_count + wide - 1) // wide, query_blocks, 0)
+
+
 def score_call(chunks, qblocks, pieces, wide, given, payloads, first):
     width = payloads[0].shape[1]
     slots = 4 * qblocks
@@ -187,8 +217,11 @@
         specs = [SMEM] + [VMEM] * (len(given) - 1 + len(payloads))
     else:
         specs = [SMEM] * 2 + [VMEM] * (len(given) - 2 + len(payloads))
+    kernel = functools.partial(score_kernel, chunks, qblocks, pieces, first, wide)
+    if not first:
+        kernel, scratch = functools.partial(last_kernel, chunks, wide), []
     return pl.pallas_call(
-        functools.partial(score_kernel, chunks, qblocks, pieces, first, wide),
+        kernel,
         out_shape=(totals_shape, packed_shape, slot_shape, number_shape) if first else totals_shape,
         in_specs=specs,
         out_specs=(VMEM, VMEM, SMEM, SMEM) if first else VMEM,
@@ -239,15 +272,6 @@
         mask //= 2
     q_helper = swap(queries, "helper")
 
-    table = pl.pallas_call(
-        table_kernel,
-        out_shape=jax.ShapeDtypeStruct((8, LANES), jnp.int32),
-        in_specs=[SMEM] * 2,
-        out_specs=VMEM,
-        compiler_params=PARAMS,
-        cost_estimate=cost(1, 1),
-    )(after(query_block_cluster, own), block_count)
-    q_tables = (table, swap(table, "helper"), swap(table, "blk"), swap_both(table))
     beta = cluster_beta.reshape(1, -1)
     staged, beta = pl.pallas_call(
         stage_kernel,
@@ -257,6 +281,15 @@
         compiler_params=PARAMS,
         cost_estimate=cost(1, 1),
     )(queries, beta)
+    table = pl.pallas_call(
+        table_kernel,
+        out_shape=jax.ShapeDtypeStruct((8, LANES), jnp.int32),
+        in_specs=[SMEM] * 2,
+        out_specs=VMEM,
+        compiler_params=PARAMS,
+        cost_estimate=cost(1, 1),
+    )(after(query_block_cluster, own, staged), block_count)
+    q_tables = (table, swap(table, "helper"), swap(table, "blk"), swap_both(table))
     q_partner = after(q_partner, staged, *held[1:-1], *q_tables)
     half = qblocks // 2 * LANES
     q_both = [swap(q_partner[:half], "helper"), swap(q_partner[half:], "helper")]

time: 42.3 us -> 41 us (0.969)
  waiting for transfers between devices: 16 us -> 13.3 us
  starting transfers between devices: 13.2 us -> 15 us
    ppermute x8, waiting for transfers between devices: 13.2 us -> 11.3 us  [swap(): return lax.ppermute(value, axis, [(i, i ^ 1) for i in range(length)])]
    ppermute x3, starting transfers between devices: 6.26 us -> 8.11 us  [trade(): return lax.ppermute(value, 'blk', [(i, i ^ mask) for i in range(length)])]
    ppermute x3, waiting for transfers between devices: 2.86 us -> 1.78 us  [trade(): return lax.ppermute(value, 'blk', [(i, i ^ mask) for i in range(length)])]
  transfers between devices with their start and end apart: 13 -> 13, of which waited for: 7 -> 8; matrix products, arithmetic and copies ran while one was open for 1% -> 1% of each run, Pallas kernels for 13% -> 13%
where the time goes in v17:
time: 41 us; the launch traced here: 41.2 us
  starting transfers between devices  15 us (37%)
  waiting for transfers between devices  13.3 us (32%)
  Pallas kernels  7.45 us (18%)
  local copies, waits for them, and re-layouts  3.21 us (8%)
  between operations  1.41 us (3%)
  other arithmetic  0.85 us (2%)
    ppermute x8, waiting for transfers between devices, swap(): return lax.ppermute(value, axis, [(i, i ^ 1) for i in range(length)])  11.3 us
    ppermute x3, starting transfers between devices, trade(): return lax.ppermute(value, 'blk', [(i, i ^ mask) for i in range(length)])  8.11 us
    pallas_call x2, Pallas kernels, score_call(): pl.pallas_call(kernel, out_shape=(totals_shape, packed_shape, slot_shape,...  6.82 us
    ppermute x8, starting transfers between devices, swap(): return lax.ppermute(value, axis, [(i, i ^ 1) for i in range(length)])  5.49 us
    unnamed x12, local copies, waits for them, and re-layouts  3.12 us
    ppermute x3, waiting for transfers between devices, trade(): return lax.ppermute(value, 'blk', [(i, i ^ mask) for i in range(length)])  1.78 us
    ppermute x2, starting transfers between devices, swap_both(): return lax.ppermute(value, ('blk', 'helper'), pairs)  1.37 us
  transfers between devices with their start and end apart: 13, of which 8 were waited for; matrix products, arithmetic and copies ran while one was open for 1% of the time, Pallas kernels for 13%

profile of v17, /device:TPU:0, one launch (start us, length us, event | category | flops | bytes accessed | tf_op | source)
XLA Modules:
  0.0 41.2 jit_solution(7345160026689400242)
XLA Ops:
  0.0 3.0 %collective-permute-start.1 = (bf16[512,768]{1,0:T(8,128)(2,1)}, bf16[512,768]{1,0:T(8,128)(2,1)S(1)}, u32[]{:S(2)}, u32[]{:S(2)}) collective-permute-start(bf16[512,768]{1,0:T(8,128)(2,1)} %refs_0_.1), channel_id=1, source_target_pairs={{0,2},{2,0},{4,6},{6,4},{8,10},{10,8},{12,14},{14,12},{1,3},{3,1},... | collective-permute-start | bytes 2359304 | tf_op jit(solution)/shard_map/ppermute | solution.py:27
  3.7 0.7 %copy-done.2 = s32[512]{0:T(512)S(1)} copy-done((s32[512]{0:T(512)S(1)}, s32[512]{0:T(512)}, u32[]{:S(2)}) %copy-start.2) | copy-done | bytes 2072
  4.4 3.7 %collective-permute-start.2 = (bf16[264,768]{1,0:T(8,128)(2,1)S(1)}, bf16[264,768]{1,0:T(8,128)(2,1)S(1)}, u32[]{:S(2)}, u32[]{:S(2)}) collective-permute-start(bf16[264,768]{1,0:T(8,128)(2,1)S(1)} %shard_map.83.refs_10_), channel_id=1, source_target_pairs={{0,12},{2,14},{4,8},{6,10},{8,4},{10,6},{12,0},{14,2},{1,13},{3,15... | collective-permute-start | bytes 1216520 | tf_op jit(solution)/shard_map/ppermute | solution.py:22
  8.1 1.1 %copy-done.1 = bf16[512,768]{1,0:T(8,128)(2,1)S(1)} copy-done((bf16[512,768]{1,0:T(8,128)(2,1)S(1)}, bf16[512,768]{1,0:T(8,128)(2,1)}, u32[]{:S(2)}) %copy-start.1) | copy-done | bytes 786456
  9.2 0.7 %copy-done.4 = f32[64]{0:T(128)S(1)} copy-done((f32[64]{0:T(128)S(1)}, f32[64]{0:T(128)}, u32[]{:S(2)}) %copy-start.4) | copy-done | bytes 280
  10.6 0.6 %copy-done.3 = s32[4]{0:T(128)S(1)} copy-done((s32[4]{0:T(128)S(1)}, s32[4]{0:T(128)}, u32[]{:S(2)}) %copy-start.3) | copy-done | bytes 40
  11.2 0.5 %shard_map.84.refs_6_ = s32[8,128]{1,0:T(8,128)S(1)} custom-call(s32[4]{0:T(128)S(1)} %copy-done.3, s32[1]{0:T(128)S(6)} %copy.12.count_ref), custom_call_target="tpu_custom_call" | custom-call | flops 1 | bytes 1 | tf_op jit(solution)/shard_map/pallas_call | solution.py:284
  11.8 0.6 %collective-permute-start.4 = (s32[8,128]{1,0:T(8,128)S(1)}, s32[8,128]{1,0:T(8,128)S(1)}, u32[]{:S(2)}, u32[]{:S(2)}) collective-permute-start(s32[8,128]{1,0:T(8,128)S(1)} %shard_map.84.refs_6_), channel_id=1, source_target_pairs={{0,1},{1,0},{2,3},{3,2},{4,5},{5,4},{6,7},{7,6},{8,9},{9,8},{10,11... | collective-permute-start | bytes 12296 | tf_op jit(solution)/shard_map/ppermute | solution.py:27
  12.3 0.8 %collective-permute-done.4.refs_7_ = s32[8,128]{1,0:T(8,128)S(1)} collective-permute-done((s32[8,128]{1,0:T(8,128)S(1)}, s32[8,128]{1,0:T(8,128)S(1)}, u32[]{:S(2)}, u32[]{:S(2)}) %collective-permute-start.4) | collective-permute-done | bytes 4128 | tf_op jit(solution)/shard_map/ppermute | solution.py:27
  13.2 0.5 %collective-permute-start.5 = (s32[8,128]{1,0:T(8,128)S(1)}, s32[8,128]{1,0:T(8,128)S(1)}, u32[]{:S(2)}, u32[]{:S(2)}) collective-permute-start(s32[8,128]{1,0:T(8,128)S(1)} %shard_map.84.refs_6_), channel_id=1, source_target_pairs={{0,2},{2,0},{4,6},{6,4},{8,10},{10,8},{12,14},{14,12},{1,3},{3,1},... | collective-permute-start | bytes 12296 | tf_op jit(solution)/shard_map/ppermute | solution.py:27
  13.7 7.1 %collective-permute-done.5.refs_8_ = s32[8,128]{1,0:T(8,128)S(1)} collective-permute-done((s32[8,128]{1,0:T(8,128)S(1)}, s32[8,128]{1,0:T(8,128)S(1)}, u32[]{:S(2)}, u32[]{:S(2)}) %collective-permute-start.5) | collective-permute-done | bytes 4128 | tf_op jit(solution)/shard_map/ppermute | solution.py:27
  20.8 0.3 collective-permute-start.6
  21.1 4.4 %collective-permute-start.9 = (bf16[264,768]{1,0:T(8,128)(2,1)S(1)}, bf16[264,768]{1,0:T(8,128)(2,1)S(1)}, u32[]{:S(2)}, u32[]{:S(2)}) collective-permute-start(bf16[264,768]{1,0:T(8,128)(2,1)S(1)} %collective-permute-done.2.refs_11_), channel_id=1, source_target_pairs={{0,4},{2,6},{4,0},{6,2},{8,12},{10,14},{12,8},{14,10},{1,5},{3,7},... | collective-permute-start | bytes 1216520 | tf_op jit(solution)/shard_map/ppermute | solution.py:22
  25.6 0.5 %collective-permute-done.3.refs_12_ = bf16[264,768]{1,0:T(8,128)(2,1)S(1)} collective-permute-done((bf16[264,768]{1,0:T(8,128)(2,1)S(1)}, bf16[264,768]{1,0:T(8,128)(2,1)S(1)}, u32[]{:S(2)}, u32[]{:S(2)}) %collective-permute-start.3) | collective-permute-done | bytes 405536 | tf_op jit(solution)/shard_map/ppermute | solution.py:22
  26.2 0.5 %collective-permute-start.8 = (bf16[256,768]{1,0:T(8,128)(2,1)S(1)}, bf16[256,768]{1,0:T(8,128)(2,1)S(1)}, u32[]{:S(2)}, u32[]{:S(2)}) collective-permute-start(bf16[256,768]{1,0:T(8,128)(2,1)S(1)} %get-tuple-element.21), channel_id=1, source_target_pairs={{0,1},{1,0},{2,3},{3,2},{4,5},{5,4},{6,7},{7,6},{8,9},{9,8},{10,11... | collective-permute-start | bytes 1179656 | tf_op jit(solution)/shard_map/ppermute | solution.py:27
  26.7 1.2 %collective-permute-done.7.refs_4_ = bf16[256,768]{1,0:T(8,128)(2,1)S(1)} collective-permute-done((bf16[256,768]{1,0:T(8,128)(2,1)S(1)}, bf16[256,768]{1,0:T(8,128)(2,1)S(1)}, u32[]{:S(2)}, u32[]{:S(2)}) %collective-permute-start.7) | collective-permute-done | bytes 393248 | tf_op jit(solution)/shard_map/ppermute | solution.py:27
  27.9 0.6 %collective-permute-done.8.refs_5_ = bf16[256,768]{1,0:T(8,128)(2,1)S(1)} collective-permute-done((bf16[256,768]{1,0:T(8,128)(2,1)S(1)}, bf16[256,768]{1,0:T(8,128)(2,1)S(1)}, u32[]{:S(2)}, u32[]{:S(2)}) %collective-permute-start.8) | collective-permute-done | bytes 393248 | tf_op jit(solution)/shard_map/ppermute | solution.py:27
  28.5 4.9 %shard_map.85 = (f32[24,128]{1,0:T(8,128)S(1)}, bf16[2048,768]{1,0:T(8,128)(2,1)S(1)}, s32[24]{0:T(128)S(1)}, f32[48]{0:T(128)S(1)}) custom-call(f32[1,64]{1,0:T(1,128)S(1)} %get-tuple-element.13.refs_0_, bf16[512,768]{1,0:T(8,128)(2,1)S(1)} %get-tuple-element.14.refs_1_, bf16[512,768]{1,0:T(8,128)(2,1)S(1)} %collective-permute-done.refs_2_, ...), custom_call_target="tpu_custom_call" | custom-call | flops 1 | bytes 1 | tf_op jit(solution)/shard_map/pallas_call | solution.py:223
  33.3 1.3 %collective-permute-done.9.r_ref = bf16[264,768]{1,0:T(8,128)(2,1)S(1)} collective-permute-done((bf16[264,768]{1,0:T(8,128)(2,1)S(1)}, bf16[264,768]{1,0:T(8,128)(2,1)S(1)}, u32[]{:S(2)}, u32[]{:S(2)}) %collective-permute-start.9) | collective-permute-done | bytes 405536 | tf_op jit(solution)/shard_map/ppermute | solution.py:22
  34.6 2.0 %shard_map.86 = f32[24,128]{1,0:T(8,128)S(1)} custom-call(s32[24]{0:T(128)S(1)} %get-tuple-element.17.slot_ref, f32[48]{0:T(128)S(1)} %get-tuple-element.18.number_ref, bf16[2048,768]{1,0:T(8,128)(2,1)S(1)} %get-tuple-element.19.qv, f32[24,128]{1,0:T(8,128)S(1)} %get-tuple-element.20.prev_ref, bf16[264,768]{1,0:T(8,128)(2,1)S(1)} %collective-permute-done.9.r_ref), custom_call_target="tpu_custom_call" | custom-call | flops 1 | bytes 1 | tf_op jit(solution)/shard_map/pallas_call | solution.py:223
  36.7 0.8 %collective-permute-start.11 = (f32[4,128]{1,0:T(4,128)S(1)}, f32[4,128]{1,0:T(4,128)S(1)}, u32[]{:S(2)}, u32[]{:S(2)}) collective-permute-start(f32[4,128]{1,0:T(4,128)S(1)} %get-tuple-element.25), channel_id=1, source_target_pairs={{0,2},{2,0},{4,6},{6,4},{8,10},{10,8},{12,14},{14,12},{1,3},{3,1},... | collective-permute-start | bytes 6152 | tf_op jit(solution)/shard_map/ppermute | solution.py:27
  37.5 1.1 %collective-permute-start.12 = (f32[4,128]{1,0:T(4,128)S(1)}, f32[4,128]{1,0:T(4,128)S(1)}, u32[]{:S(2)}, u32[]{:S(2)}) collective-permute-start(f32[4,128]{1,0:T(4,128)S(1)} %get-tuple-element.24), channel_id=1, source_target_pairs={{0,3},{1,2},{2,1},{3,0},{4,7},{5,6},{6,5},{7,4},{8,11},{9,10},{10,... | collective-permute-start | bytes 6152 | tf_op jit(solution)/shard_map/ppermute | solution.py:33
  38.7 1.6 %collective-permute-done.11 = f32[4,128]{1,0:T(4,128)S(1)} collective-permute-done((f32[4,128]{1,0:T(4,128)S(1)}, f32[4,128]{1,0:T(4,128)S(1)}, u32[]{:S(2)}, u32[]{:S(2)}) %collective-permute-start.11) | collective-permute-done | bytes 2080 | tf_op jit(solution)/shard_map/ppermute | solution.py:27
  40.5 0.7 %log-plus-one_bitcast_fusion = f32[512]{0:T(512)} fusion(f32[4,128]{1,0:T(4,128)S(1)} %collective-permute-done.12, f32[4,128]{1,0:T(4,128)S(1)} %collective-permute-done.11, f32[4,128]{1,0:T(4,128)S(1)} %collective-permute-done.10, f32[24,128]{1,0:T(8,128)S(1)} %shard_map.86, f32[4]{0:T(128)S(1)} %convert_element_type.7), kind=kLoop, calls=%fused_computation.4 | loop fusion | flops 2048 | bytes 10256 | tf_op jit(solution)/shard_map/reshape | solution.py:310
  (25 shorter events, 0.7 us)
Async XLA Ops:
  0.0 3.6 %copy-start = (bf16[512,768]{1,0:T(8,128)(2,1)S(1)}, bf16[512,768]{1,0:T(8,128)(2,1)}, u32[]{:S(2)}) copy-start(bf16[512,768]{1,0:T(8,128)(2,1)} %param.11) | copy-start | bytes 2359300
  0.0 26.0 %collective-permute-start.1 = (bf16[512,768]{1,0:T(8,128)(2,1)}, bf16[512,768]{1,0:T(8,128)(2,1)S(1)}, u32[]{:S(2)}, u32[]{:S(2)}) collective-permute-start(bf16[512,768]{1,0:T(8,128)(2,1)} %refs_0_.1), channel_id=1, source_target_pairs={{0,2},{2,0},{4,6},{6,4},{8,10},{10,8},{12,14},{14,12},{1,3},{3,1},... | collective-permute-start | bytes 2359304 | tf_op jit(solution)/shard_map/ppermute | solution.py:27
  3.7 0.7 %copy-start.2 = (s32[512]{0:T(512)S(1)}, s32[512]{0:T(512)}, u32[]{:S(2)}) copy-start(s32[512]{0:T(512)} %param.12) | copy-start | bytes 6148
  4.4 16.7 %collective-permute-start.2 = (bf16[264,768]{1,0:T(8,128)(2,1)S(1)}, bf16[264,768]{1,0:T(8,128)(2,1)S(1)}, u32[]{:S(2)}, u32[]{:S(2)}) collective-permute-start(bf16[264,768]{1,0:T(8,128)(2,1)S(1)} %shard_map.83.refs_10_), channel_id=1, source_target_pairs={{0,12},{2,14},{4,8},{6,10},{8,4},{10,6},{12,0},{14,2},{1,13},{3,15... | collective-permute-start | bytes 1216520 | tf_op jit(solution)/shard_map/ppermute | solution.py:22
  8.1 18.0 %collective-permute-start.3 = (bf16[264,768]{1,0:T(8,128)(2,1)S(1)}, bf16[264,768]{1,0:T(8,128)(2,1)S(1)}, u32[]{:S(2)}, u32[]{:S(2)}) collective-permute-start(bf16[264,768]{1,0:T(8,128)(2,1)S(1)} %shard_map.83.refs_10_), channel_id=1, source_target_pairs={{0,4},{2,6},{4,0},{6,2},{8,12},{10,14},{12,8},{14,10},{1,5},{3,7},... | collective-permute-start | bytes 1216520 | tf_op jit(solution)/shard_map/ppermute | solution.py:22
  8.1 18.6 %collective-permute-start = (bf16[512,768]{1,0:T(8,128)(2,1)}, bf16[512,768]{1,0:T(8,128)(2,1)S(1)}, u32[]{:S(2)}, u32[]{:S(2)}) collective-permute-start(bf16[512,768]{1,0:T(8,128)(2,1)} %refs_0_.1), channel_id=1, source_target_pairs={{0,1},{1,0},{2,3},{3,2},{4,5},{5,4},{6,7},{7,6},{8,9},{9,8},{10,11... | collective-permute-start | bytes 2359304 | tf_op jit(solution)/shard_map/ppermute | solution.py:27
  8.1 1.1 %copy-start.1 = (bf16[512,768]{1,0:T(8,128)(2,1)S(1)}, bf16[512,768]{1,0:T(8,128)(2,1)}, u32[]{:S(2)}) copy-start(bf16[512,768]{1,0:T(8,128)(2,1)} %refs_0_.1) | copy-start | bytes 2359300
  9.2 0.7 %copy-start.4 = (f32[64]{0:T(128)S(1)}, f32[64]{0:T(128)}, u32[]{:S(2)}) copy-start(f32[64]{0:T(128)} %param.14) | copy-start | bytes 772
  10.6 0.7 %copy-start.3 = (s32[4]{0:T(128)S(1)}, s32[4]{0:T(128)}, u32[]{:S(2)}) copy-start(s32[4]{0:T(128)} %clusters_ref) | copy-start | bytes 52
  11.8 1.4 %collective-permute-start.4 = (s32[8,128]{1,0:T(8,128)S(1)}, s32[8,128]{1,0:T(8,128)S(1)}, u32[]{:S(2)}, u32[]{:S(2)}) collective-permute-start(s32[8,128]{1,0:T(8,128)S(1)} %shard_map.84.refs_6_), channel_id=1, source_target_pairs={{0,1},{1,0},{2,3},{3,2},{4,5},{5,4},{6,7},{7,6},{8,9},{9,8},{10,11... | collective-permute-start | bytes 12296 | tf_op jit(solution)/shard_map/ppermute | solution.py:27
  13.2 7.6 %collective-permute-start.5 = (s32[8,128]{1,0:T(8,128)S(1)}, s32[8,128]{1,0:T(8,128)S(1)}, u32[]{:S(2)}, u32[]{:S(2)}) collective-permute-start(s32[8,128]{1,0:T(8,128)S(1)} %shard_map.84.refs_6_), channel_id=1, source_target_pairs={{0,2},{2,0},{4,6},{6,4},{8,10},{10,8},{12,14},{14,12},{1,3},{3,1},... | collective-permute-start | bytes 12296 | tf_op jit(solution)/shard_map/ppermute | solution.py:27
  20.8 4.8 %collective-permute-start.6 = (s32[8,128]{1,0:T(8,128)S(1)}, s32[8,128]{1,0:T(8,128)S(1)}, u32[]{:S(2)}, u32[]{:S(2)}) collective-permute-start(s32[8,128]{1,0:T(8,128)S(1)} %shard_map.84.refs_6_), channel_id=1, source_target_pairs={{0,3},{1,2},{2,1},{3,0},{4,7},{5,6},{6,5},{7,4},{8,11},{9,10},{10,... | collective-permute-start | bytes 12296 | tf_op jit(solution)/shard_map/ppermute | solution.py:33
  21.1 13.5 %collective-permute-start.9 = (bf16[264,768]{1,0:T(8,128)(2,1)S(1)}, bf16[264,768]{1,0:T(8,128)(2,1)S(1)}, u32[]{:S(2)}, u32[]{:S(2)}) collective-permute-start(bf16[264,768]{1,0:T(8,128)(2,1)S(1)} %collective-permute-done.2.refs_11_), channel_id=1, source_target_pairs={{0,4},{2,6},{4,0},{6,2},{8,12},{10,14},{12,8},{14,10},{1,5},{3,7},... | collective-permute-start | bytes 1216520 | tf_op jit(solution)/shard_map/ppermute | solution.py:22
  26.1 1.8 %collective-permute-start.7 = (bf16[256,768]{1,0:T(8,128)(2,1)S(1)}, bf16[256,768]{1,0:T(8,128)(2,1)S(1)}, u32[]{:S(2)}, u32[]{:S(2)}) collective-permute-start(bf16[256,768]{1,0:T(8,128)(2,1)S(1)} %get-tuple-element.22), channel_id=1, source_target_pairs={{0,1},{1,0},{2,3},{3,2},{4,5},{5,4},{6,7},{7,6},{8,9},{9,8},{10,11... | collective-permute-start | bytes 1179656 | tf_op jit(solution)/shard_map/ppermute | solution.py:27
  26.2 2.3 %collective-permute-start.8 = (bf16[256,768]{1,0:T(8,128)(2,1)S(1)}, bf16[256,768]{1,0:T(8,128)(2,1)S(1)}, u32[]{:S(2)}, u32[]{:S(2)}) collective-permute-start(bf16[256,768]{1,0:T(8,128)(2,1)S(1)} %get-tuple-element.21), channel_id=1, source_target_pairs={{0,1},{1,0},{2,3},{3,2},{4,5},{5,4},{6,7},{7,6},{8,9},{9,8},{10,11... | collective-permute-start | bytes 1179656 | tf_op jit(solution)/shard_map/ppermute | solution.py:27
  28.5 10.1 %copy-start.5 = (s32[64]{0:T(128)S(1)}, s32[64]{0:T(128)}, u32[]{:S(2)}) copy-start(s32[64]{0:T(128)} %param.15) | copy-start | bytes 772
  36.6 2.1 %collective-permute-start.10 = (f32[4,128]{1,0:T(4,128)S(1)}, f32[4,128]{1,0:T(4,128)S(1)}, u32[]{:S(2)}, u32[]{:S(2)}) collective-permute-start(f32[4,128]{1,0:T(4,128)S(1)} %get-tuple-element.23), channel_id=1, source_target_pairs={{0,1},{1,0},{2,3},{3,2},{4,5},{5,4},{6,7},{7,6},{8,9},{9,8},{10,11... | collective-permute-start | bytes 6152 | tf_op jit(solution)/shard_map/ppermute | solution.py:27
  36.7 3.7 %collective-permute-start.11 = (f32[4,128]{1,0:T(4,128)S(1)}, f32[4,128]{1,0:T(4,128)S(1)}, u32[]{:S(2)}, u32[]{:S(2)}) collective-permute-start(f32[4,128]{1,0:T(4,128)S(1)} %get-tuple-element.25), channel_id=1, source_target_pairs={{0,2},{2,0},{4,6},{6,4},{8,10},{10,8},{12,14},{14,12},{1,3},{3,1},... | collective-permute-start | bytes 6152 | tf_op jit(solution)/shard_map/ppermute | solution.py:27
  37.5 3.0 %collective-permute-start.12 = (f32[4,128]{1,0:T(4,128)S(1)}, f32[4,128]{1,0:T(4,128)S(1)}, u32[]{:S(2)}, u32[]{:S(2)}) collective-permute-start(f32[4,128]{1,0:T(4,128)S(1)} %get-tuple-element.24), channel_id=1, source_target_pairs={{0,3},{1,2},{2,1},{3,0},{4,7},{5,6},{6,5},{7,4},{8,11},{9,10},{10,... | collective-permute-start | bytes 6152 | tf_op jit(solution)/shard_map/ppermute | solution.py:33

commit v18 on v17

--- a/solution.py
+++ b/solution.py
@@ -73,24 +73,20 @@
         out[...] = source[...]
 
 
-def score_kernel(chunks, qblocks, pieces, first, wide, *refs):
-    if first:
-        (beta_ref, *given, out_ref, qv, slot_ref, number_ref, info_v, info, ids_ref, other_ref, info_sem) = refs
-        q_refs = []
-        for n in pieces:
-            q_refs.append(given[:n])
-            given = given[n:]
-        t_refs, r_refs = given[:4], given[4:]
-    else:
-        (slot_ref, number_ref, qv, prev_ref, *r_refs, out_ref, ids_ref, other_ref) = refs
+def first_kernel(chunks, qblocks, pieces, wide, beta_ref, *refs):
+    *given, out_ref, qv, slot_ref, number_ref, info_v, info, ids_ref, other_ref, info_sem = refs
+    q_refs = []
+    for n in pieces:
+        q_refs.append(given[:n])
+        given = given[n:]
+    t_refs, r_refs = given[:4], given[4:]
     width = qv.shape[1]
     height = chunks * LANES
     slots = 4 * qblocks
-    if first:
-        for s, t_ref in enumerate(t_refs):
-            info_v[s : s + 1, :] = t_ref[0:1, :]
-        copy = pltpu.make_async_copy(info_v, info, info_sem)
-        copy.start()
+    for s, t_ref in enumerate(t_refs):
+        info_v[s : s + 1, :] = t_ref[0:1, :]
+    copy = pltpu.make_async_copy(info_v, info, info_sem)
+    copy.start()
 
     for s, r_ref in enumerate(r_refs):
         table = r_ref[pl.ds(height, TABLE), pl.ds(0, LANES)].astype(jnp.float32)
@@ -100,48 +96,44 @@
             ids_ref[rows, :] = ids
             other_ref[rows, :] = jnp.where(ids < 0.0, DEAD, -4.0)
 
-    if first:
-        copy.wait()
-        factor = LOG2E / math.sqrt(width)
-        q_count = jnp.int32(0)
-        for source in range(4):
-            blocks = info[source, qblocks]
-
-            def enter(block, carry, source=source, q_count=q_count):
-                entry = q_count + block
-                cluster = info[source, block]
-                beta = beta_ref[0, cluster]
-                slot_ref[entry] = source * qblocks + block
-                number_ref[3 * entry] = cluster.astype(jnp.float32)
-                number_ref[3 * entry + 1] = beta * factor
-                number_ref[3 * entry + 2] = beta * beta * (0.5 * LOG2E)
+    copy.wait()
+    factor = LOG2E / math.sqrt(width)
+    q_count = jnp.int32(0)
+    for source in range(4):
+        blocks = info[source, qblocks]
+
+        def enter(block, carry, source=source, q_count=q_count):
+            entry = q_count + block
+            cluster = info[source, block]
+            beta = beta_ref[0, cluster]
+            slot_ref[entry] = source * qblocks + block
+            number_ref[3 * entry] = cluster.astype(jnp.float32)
+            number_ref[3 * entry + 1] = beta * factor
+            number_ref[3 * entry + 2] = beta * beta * (0.5 * LOG2E)
+            return carry
+
+        lax.fori_loop(0, blocks, enter, 0)
+        start = 0
+        for piece in q_refs[source]:
+            each = piece.shape[0] // LANES
+
+            def move(block, carry, place=q_count + start, piece=piece):
+                qv[rows_of(place + block), :] = piece[rows_of(block), :]
                 return carry
 
-            lax.fori_loop(0, blocks, enter, 0)
-            start = 0
-            for piece in q_refs[source]:
-                each = piece.shape[0] // LANES
-
-                def move(block, carry, place=q_count + start, piece=piece):
-                    qv[rows_of(place + block), :] = piece[rows_of(block), :]
-                    return carry
-
-                lax.fori_loop(0, jnp.clip(blocks - start, 0, each), move, 0)
-                start += each
-            q_count = q_count + blocks
-
-        def spare(entry, carry):
-            slot_ref[entry] = slots
-            for i in range(3):
-                number_ref[3 * entry + i] = 0.0
-            return carry
-
-        lax.fori_loop(q_count, slots, spare, 0)
-        slot_ref[slots] = q_count
-        out_ref[...] = jnp.zeros_like(out_ref)
-    else:
-        q_count = slot_ref[slots]
-        out_ref[...] = prev_ref[...]
+            lax.fori_loop(0, jnp.clip(blocks - start, 0, each), move, 0)
+            start += each
+        q_count = q_count + blocks
+
+    def spare(entry, carry):
+        slot_ref[entry] = slots
+        for i in range(3):
+            number_ref[3 * entry + i] = 0.0
+        return carry
+
+    lax.fori_loop(q_count, slots, spare, 0)
+    slot_ref[slots] = q_count
+    out_ref[...] = jnp.zeros_like(out_ref)
 
     def query_blocks(group, carry):
         sides = [wide * group + side for side in range(wide)]
@@ -202,33 +194,41 @@
     lax.fori_loop(0, (q_count + wide - 1) // wide, query_blocks, 0)
 
 
-def score_call(chunks, qblocks, pieces, wide, given, payloads, first):
+def first_call(chunks, qblocks, pieces, wide, given, payloads):
     width = payloads[0].shape[1]
     slots = 4 * qblocks
     rows = len(payloads) * chunks * LANES
-    totals_shape = jax.ShapeDtypeStruct((slots + 8, LANES), jnp.float32)
-    packed_shape = jax.ShapeDtypeStruct((slots * LANES, width), jnp.bfloat16)
-    slot_shape = jax.ShapeDtypeStruct((slots + 8,), jnp.int32)
-    number_shape = jax.ShapeDtypeStruct((3 * slots,), jnp.float32)
-    scratch = [pltpu.VMEM((rows, LANES), jnp.float32)] * 2
-    if first:
-        scratch = [pltpu.VMEM((8, LANES), jnp.int32), pltpu.SMEM((8, LANES), jnp.int32)] + scratch
-        scratch.append(pltpu.SemaphoreType.DMA)
-        specs = [SMEM] + [VMEM] * (len(given) - 1 + len(payloads))
-    else:
-        specs = [SMEM] * 2 + [VMEM] * (len(given) - 2 + len(payloads))
-    kernel = functools.partial(score_kernel, chunks, qblocks, pieces, first, wide)
-    if not first:
-        kernel, scratch = functools.partial(last_kernel, chunks, wide), []
     return pl.pallas_call(
-        kernel,
-        out_shape=(totals_shape, packed_shape, slot_shape, number_shape) if first else totals_shape,
-        in_specs=specs,
-        out_specs=(VMEM, VMEM, SMEM, SMEM) if first else VMEM,
-        scratch_shapes=scratch,
+        functools.partial(first_kernel, chunks, qblocks, pieces, wide),
+        out_shape=(
+            jax.ShapeDtypeStruct((slots + 8, LANES), jnp.float32),
+            jax.ShapeDtypeStruct((slots * LANES, width), jnp.bfloat16),
+            jax.ShapeDtypeStruct((slots + 8,), jnp.int32),
+            jax.ShapeDtypeStruct((3 * slots,), jnp.float32),
+        ),
+        in_specs=[SMEM] + [VMEM] * (len(given) - 1 + len(payloads)),
+        out_specs=(VMEM, VMEM, SMEM, SMEM),
+        scratch_shapes=[
+            pltpu.VMEM((8, LANES), jnp.int32),
+            pltpu.SMEM((8, LANES), jnp.int32),
+            pltpu.VMEM((rows, LANES), jnp.float32),
+            pltpu.VMEM((rows, LANES), jnp.float32),
+            pltpu.SemaphoreType.DMA,
+        ],
         compiler_params=PARAMS,
         cost_estimate=cost(1, 1),
     )(*given, *payloads)
+
+
+def last_call(chunks, wide, slots, numbers, packed, totals, payload):
+    return pl.pallas_call(
+        functools.partial(last_kernel, chunks, wide),
+        out_shape=jax.ShapeDtypeStruct(totals.shape, jnp.float32),
+        in_specs=[SMEM] * 2 + [VMEM] * 3,
+        out_specs=VMEM,
+        compiler_params=PARAMS,
+        cost_estimate=cost(1, 1),
+    )(slots, numbers, packed, totals, payload)
 
 
 def per_device(
@@ -297,9 +297,8 @@
     pieces = (1, 1, 1, 2)
 
     given = (beta, *queries, *q_tables)
-    totals, packed, *plan = score_call(chunks, qblocks, pieces, 4, given, held[:-1], True)
-    given = (*plan, packed, totals)
-    totals = score_call(chunks, qblocks, pieces, 8, given, held[-1:], False)
+    totals, packed, *plan = first_call(chunks, qblocks, pieces, 4, given, held[:-1])
+    totals = last_call(chunks, 4, *plan, packed, totals, held[-1])
     totals = totals[: 4 * qblocks]
     totals = totals.reshape(4, qblocks, LANES)
     total = totals[0] + swap(totals[1], "helper") + swap(totals[2], "blk") + swap_both(totals[3])

time: 41 us -> 41.4 us (level)
  no operation moved by 1% of the time
where the time goes in v18:
time: 41.4 us; the launch traced here: 41.2 us
  starting transfers between devices  15 us (36%)
  waiting for transfers between devices  13.3 us (32%)
  Pallas kernels  7.51 us (18%)
  local copies, waits for them, and re-layouts  3.21 us (8%)
  between operations  1.41 us (3%)
  other arithmetic  0.85 us (2%)
    ppermute x8, waiting for transfers between devices, swap(): return lax.ppermute(value, axis, [(i, i ^ 1) for i in range(length)])  11.3 us
    ppermute x3, starting transfers between devices, trade(): return lax.ppermute(value, 'blk', [(i, i ^ mask) for i in range(length)])  8.11 us
    ppermute x8, starting transfers between devices, swap(): return lax.ppermute(value, axis, [(i, i ^ 1) for i in range(length)])  5.49 us
    pallas_call x1, Pallas kernels, first_call(): pl.pallas_call(functools.partial(first_kernel, chunks, qblocks, pieces, w...  4.86 us
    unnamed x12, local copies, waits for them, and re-layouts  3.12 us
    pallas_call x1, Pallas kernels, last_call(): pl.pallas_call(functools.partial(last_kernel, chunks, wide), out_shape=ja...  2.02 us
    ppermute x3, waiting for transfers between devices, trade(): return lax.ppermute(value, 'blk', [(i, i ^ mask) for i in range(length)])  1.79 us
    ppermute x2, starting transfers between devices, swap_both(): return lax.ppermute(value, ('blk', 'helper'), pairs)  1.37 us
  transfers between devices with their start and end apart: 13, of which 8 were waited for; matrix products, arithmetic and copies ran while one was open for 1% of the time, Pallas kernels for 13%

profile of v18, /device:TPU:0, one launch (start us, length us, event | category | flops | bytes accessed | tf_op | source)
XLA Modules:
  0.0 41.2 jit_solution(17243321897298377832)
XLA Ops:
  0.0 3.0 %collective-permute-start.1 = (bf16[512,768]{1,0:T(8,128)(2,1)}, bf16[512,768]{1,0:T(8,128)(2,1)S(1)}, u32[]{:S(2)}, u32[]{:S(2)}) collective-permute-start(bf16[512,768]{1,0:T(8,128)(2,1)} %refs_0_.1), channel_id=1, source_target_pairs={{0,2},{2,0},{4,6},{6,4},{8,10},{10,8},{12,14},{14,12},{1,3},{3,1},... | collective-permute-start | bytes 2359304 | tf_op jit(solution)/shard_map/ppermute | solution.py:27
  3.7 0.7 %copy-done.2 = s32[512]{0:T(512)S(1)} copy-done((s32[512]{0:T(512)S(1)}, s32[512]{0:T(512)}, u32[]{:S(2)}) %copy-start.2) | copy-done | bytes 2072
  4.4 3.7 %collective-permute-start.2 = (bf16[264,768]{1,0:T(8,128)(2,1)S(1)}, bf16[264,768]{1,0:T(8,128)(2,1)S(1)}, u32[]{:S(2)}, u32[]{:S(2)}) collective-permute-start(bf16[264,768]{1,0:T(8,128)(2,1)S(1)} %shard_map.83.refs_9_), channel_id=1, source_target_pairs={{0,12},{2,14},{4,8},{6,10},{8,4},{10,6},{12,0},{14,2},{1,13},{3,15... | collective-permute-start | bytes 1216520 | tf_op jit(solution)/shard_map/ppermute | solution.py:22
  8.1 1.1 %copy-done.1 = bf16[512,768]{1,0:T(8,128)(2,1)S(1)} copy-done((bf16[512,768]{1,0:T(8,128)(2,1)S(1)}, bf16[512,768]{1,0:T(8,128)(2,1)}, u32[]{:S(2)}) %copy-start.1) | copy-done | bytes 786456
  9.2 0.7 %copy-done.4 = f32[64]{0:T(128)S(1)} copy-done((f32[64]{0:T(128)S(1)}, f32[64]{0:T(128)}, u32[]{:S(2)}) %copy-start.4) | copy-done | bytes 280
  10.6 0.6 %copy-done.3 = s32[4]{0:T(128)S(1)} copy-done((s32[4]{0:T(128)S(1)}, s32[4]{0:T(128)}, u32[]{:S(2)}) %copy-start.3) | copy-done | bytes 40
  11.2 0.5 %shard_map.84.refs_5_ = s32[8,128]{1,0:T(8,128)S(1)} custom-call(s32[4]{0:T(128)S(1)} %copy-done.3, s32[1]{0:T(128)S(6)} %copy.12.count_ref), custom_call_target="tpu_custom_call" | custom-call | flops 1 | bytes 1 | tf_op jit(solution)/shard_map/pallas_call | solution.py:284
  11.8 0.6 %collective-permute-start.4 = (s32[8,128]{1,0:T(8,128)S(1)}, s32[8,128]{1,0:T(8,128)S(1)}, u32[]{:S(2)}, u32[]{:S(2)}) collective-permute-start(s32[8,128]{1,0:T(8,128)S(1)} %shard_map.84.refs_5_), channel_id=1, source_target_pairs={{0,1},{1,0},{2,3},{3,2},{4,5},{5,4},{6,7},{7,6},{8,9},{9,8},{10,11... | collective-permute-start | bytes 12296 | tf_op jit(solution)/shard_map/ppermute | solution.py:27
  12.3 0.8 %collective-permute-done.4.refs_6_ = s32[8,128]{1,0:T(8,128)S(1)} collective-permute-done((s32[8,128]{1,0:T(8,128)S(1)}, s32[8,128]{1,0:T(8,128)S(1)}, u32[]{:S(2)}, u32[]{:S(2)}) %collective-permute-start.4) | collective-permute-done | bytes 4128 | tf_op jit(solution)/shard_map/ppermute | solution.py:27
  13.2 0.5 %collective-permute-start.5 = (s32[8,128]{1,0:T(8,128)S(1)}, s32[8,128]{1,0:T(8,128)S(1)}, u32[]{:S(2)}, u32[]{:S(2)}) collective-permute-start(s32[8,128]{1,0:T(8,128)S(1)} %shard_map.84.refs_5_), channel_id=1, source_target_pairs={{0,2},{2,0},{4,6},{6,4},{8,10},{10,8},{12,14},{14,12},{1,3},{3,1},... | collective-permute-start | bytes 12296 | tf_op jit(solution)/shard_map/ppermute | solution.py:27
  13.7 7.1 %collective-permute-done.5.refs_7_ = s32[8,128]{1,0:T(8,128)S(1)} collective-permute-done((s32[8,128]{1,0:T(8,128)S(1)}, s32[8,128]{1,0:T(8,128)S(1)}, u32[]{:S(2)}, u32[]{:S(2)}) %collective-permute-start.5) | collective-permute-done | bytes 4128 | tf_op jit(solution)/shard_map/ppermute | solution.py:27
  20.8 0.3 collective-permute-start.6
  21.1 4.4 %collective-permute-start.9 = (bf16[264,768]{1,0:T(8,128)(2,1)S(1)}, bf16[264,768]{1,0:T(8,128)(2,1)S(1)}, u32[]{:S(2)}, u32[]{:S(2)}) collective-permute-start(bf16[264,768]{1,0:T(8,128)(2,1)S(1)} %collective-permute-done.2.refs_10_), channel_id=1, source_target_pairs={{0,4},{2,6},{4,0},{6,2},{8,12},{10,14},{12,8},{14,10},{1,5},{3,7},... | collective-permute-start | bytes 1216520 | tf_op jit(solution)/shard_map/ppermute | solution.py:22
  25.6 0.5 %collective-permute-done.3.refs_11_ = bf16[264,768]{1,0:T(8,128)(2,1)S(1)} collective-permute-done((bf16[264,768]{1,0:T(8,128)(2,1)S(1)}, bf16[264,768]{1,0:T(8,128)(2,1)S(1)}, u32[]{:S(2)}, u32[]{:S(2)}) %collective-permute-start.3) | collective-permute-done | bytes 405536 | tf_op jit(solution)/shard_map/ppermute | solution.py:22
  26.2 0.5 %collective-permute-start.8 = (bf16[256,768]{1,0:T(8,128)(2,1)S(1)}, bf16[256,768]{1,0:T(8,128)(2,1)S(1)}, u32[]{:S(2)}, u32[]{:S(2)}) collective-permute-start(bf16[256,768]{1,0:T(8,128)(2,1)S(1)} %get-tuple-element.21), channel_id=1, source_target_pairs={{0,1},{1,0},{2,3},{3,2},{4,5},{5,4},{6,7},{7,6},{8,9},{9,8},{10,11... | collective-permute-start | bytes 1179656 | tf_op jit(solution)/shard_map/ppermute | solution.py:27
  26.7 1.2 %collective-permute-done.7.refs_3_ = bf16[256,768]{1,0:T(8,128)(2,1)S(1)} collective-permute-done((bf16[256,768]{1,0:T(8,128)(2,1)S(1)}, bf16[256,768]{1,0:T(8,128)(2,1)S(1)}, u32[]{:S(2)}, u32[]{:S(2)}) %collective-permute-start.7) | collective-permute-done | bytes 393248 | tf_op jit(solution)/shard_map/ppermute | solution.py:27
  27.9 0.6 %collective-permute-done.8.refs_4_ = bf16[256,768]{1,0:T(8,128)(2,1)S(1)} collective-permute-done((bf16[256,768]{1,0:T(8,128)(2,1)S(1)}, bf16[256,768]{1,0:T(8,128)(2,1)S(1)}, u32[]{:S(2)}, u32[]{:S(2)}) %collective-permute-start.8) | collective-permute-done | bytes 393248 | tf_op jit(solution)/shard_map/ppermute | solution.py:27
  28.5 4.9 %shard_map.85 = (f32[24,128]{1,0:T(8,128)S(1)}, bf16[2048,768]{1,0:T(8,128)(2,1)S(1)}, s32[24]{0:T(128)S(1)}, f32[48]{0:T(128)S(1)}) custom-call(f32[1,64]{1,0:T(1,128)S(1)} %get-tuple-element.13.beta_ref, bf16[512,768]{1,0:T(8,128)(2,1)S(1)} %get-tuple-element.14.refs_0_, bf16[512,768]{1,0:T(8,128)(2,1)S(1)} %collective-permute-done.refs_1_, ...), custom_call_target="tpu_custom_call" | custom-call | flops 1 | bytes 1 | tf_op jit(solution)/shard_map/pallas_call | solution.py:201
  33.3 1.3 %collective-permute-done.9.r_ref = bf16[264,768]{1,0:T(8,128)(2,1)S(1)} collective-permute-done((bf16[264,768]{1,0:T(8,128)(2,1)S(1)}, bf16[264,768]{1,0:T(8,128)(2,1)S(1)}, u32[]{:S(2)}, u32[]{:S(2)}) %collective-permute-start.9) | collective-permute-done | bytes 405536 | tf_op jit(solution)/shard_map/ppermute | solution.py:22
  34.6 2.0 %shard_map.86 = f32[24,128]{1,0:T(8,128)S(1)} custom-call(s32[24]{0:T(128)S(1)} %get-tuple-element.17.slot_ref, f32[48]{0:T(128)S(1)} %get-tuple-element.18.number_ref, bf16[2048,768]{1,0:T(8,128)(2,1)S(1)} %get-tuple-element.19.qv, f32[24,128]{1,0:T(8,128)S(1)} %get-tuple-element.20.prev_ref, bf16[264,768]{1,0:T(8,128)(2,1)S(1)} %collective-permute-done.9.r_ref), custom_call_target="tpu_custom_call" | custom-call | flops 1 | bytes 1 | tf_op jit(solution)/shard_map/pallas_call | solution.py:224
  36.7 0.8 %collective-permute-start.11 = (f32[4,128]{1,0:T(4,128)S(1)}, f32[4,128]{1,0:T(4,128)S(1)}, u32[]{:S(2)}, u32[]{:S(2)}) collective-permute-start(f32[4,128]{1,0:T(4,128)S(1)} %get-tuple-element.25), channel_id=1, source_target_pairs={{0,2},{2,0},{4,6},{6,4},{8,10},{10,8},{12,14},{14,12},{1,3},{3,1},... | collective-permute-start | bytes 6152 | tf_op jit(solution)/shard_map/ppermute | solution.py:27
  37.5 1.1 %collective-permute-start.12 = (f32[4,128]{1,0:T(4,128)S(1)}, f32[4,128]{1,0:T(4,128)S(1)}, u32[]{:S(2)}, u32[]{:S(2)}) collective-permute-start(f32[4,128]{1,0:T(4,128)S(1)} %get-tuple-element.24), channel_id=1, source_target_pairs={{0,3},{1,2},{2,1},{3,0},{4,7},{5,6},{6,5},{7,4},{8,11},{9,10},{10,... | collective-permute-start | bytes 6152 | tf_op jit(solution)/shard_map/ppermute | solution.py:33
  38.8 1.6 %collective-permute-done.11 = f32[4,128]{1,0:T(4,128)S(1)} collective-permute-done((f32[4,128]{1,0:T(4,128)S(1)}, f32[4,128]{1,0:T(4,128)S(1)}, u32[]{:S(2)}, u32[]{:S(2)}) %collective-permute-start.11) | collective-permute-done | bytes 2080 | tf_op jit(solution)/shard_map/ppermute | solution.py:27
  40.6 0.7 %log-plus-one_bitcast_fusion = f32[512]{0:T(512)} fusion(f32[4,128]{1,0:T(4,128)S(1)} %collective-permute-done.12, f32[4,128]{1,0:T(4,128)S(1)} %collective-permute-done.11, f32[4,128]{1,0:T(4,128)S(1)} %collective-permute-done.10, f32[24,128]{1,0:T(8,128)S(1)} %shard_map.86, f32[4]{0:T(128)S(1)} %convert_element_type.7), kind=kLoop, calls=%fused_computation.4 | loop fusion | flops 2048 | bytes 10256 | tf_op jit(solution)/shard_map/reshape | solution.py:309
  (25 shorter events, 0.7 us)
Async XLA Ops:
  0.0 3.6 %copy-start = (bf16[512,768]{1,0:T(8,128)(2,1)S(1)}, bf16[512,768]{1,0:T(8,128)(2,1)}, u32[]{:S(2)}) copy-start(bf16[512,768]{1,0:T(8,128)(2,1)} %param.11) | copy-start | bytes 2359300
  0.0 26.0 %collective-permute-start.1 = (bf16[512,768]{1,0:T(8,128)(2,1)}, bf16[512,768]{1,0:T(8,128)(2,1)S(1)}, u32[]{:S(2)}, u32[]{:S(2)}) collective-permute-start(bf16[512,768]{1,0:T(8,128)(2,1)} %refs_0_.1), channel_id=1, source_target_pairs={{0,2},{2,0},{4,6},{6,4},{8,10},{10,8},{12,14},{14,12},{1,3},{3,1},... | collective-permute-start | bytes 2359304 | tf_op jit(solution)/shard_map/ppermute | solution.py:27
  3.7 0.7 %copy-start.2 = (s32[512]{0:T(512)S(1)}, s32[512]{0:T(512)}, u32[]{:S(2)}) copy-start(s32[512]{0:T(512)} %param.12) | copy-start | bytes 6148
  4.4 16.7 %collective-permute-start.2 = (bf16[264,768]{1,0:T(8,128)(2,1)S(1)}, bf16[264,768]{1,0:T(8,128)(2,1)S(1)}, u32[]{:S(2)}, u32[]{:S(2)}) collective-permute-start(bf16[264,768]{1,0:T(8,128)(2,1)S(1)} %shard_map.83.refs_9_), channel_id=1, source_target_pairs={{0,12},{2,14},{4,8},{6,10},{8,4},{10,6},{12,0},{14,2},{1,13},{3,15... | collective-permute-start | bytes 1216520 | tf_op jit(solution)/shard_map/ppermute | solution.py:22
  8.1 18.0 %collective-permute-start.3 = (bf16[264,768]{1,0:T(8,128)(2,1)S(1)}, bf16[264,768]{1,0:T(8,128)(2,1)S(1)}, u32[]{:S(2)}, u32[]{:S(2)}) collective-permute-start(bf16[264,768]{1,0:T(8,128)(2,1)S(1)} %shard_map.83.refs_9_), channel_id=1, source_target_pairs={{0,4},{2,6},{4,0},{6,2},{8,12},{10,14},{12,8},{14,10},{1,5},{3,7},... | collective-permute-start | bytes 1216520 | tf_op jit(solution)/shard_map/ppermute | solution.py:22
  8.1 18.6 %collective-permute-start = (bf16[512,768]{1,0:T(8,128)(2,1)}, bf16[512,768]{1,0:T(8,128)(2,1)S(1)}, u32[]{:S(2)}, u32[]{:S(2)}) collective-permute-start(bf16[512,768]{1,0:T(8,128)(2,1)} %refs_0_.1), channel_id=1, source_target_pairs={{0,1},{1,0},{2,3},{3,2},{4,5},{5,4},{6,7},{7,6},{8,9},{9,8},{10,11... | collective-permute-start | bytes 2359304 | tf_op jit(solution)/shard_map/ppermute | solution.py:27
  8.1 1.1 %copy-start.1 = (bf16[512,768]{1,0:T(8,128)(2,1)S(1)}, bf16[512,768]{1,0:T(8,128)(2,1)}, u32[]{:S(2)}) copy-start(bf16[512,768]{1,0:T(8,128)(2,1)} %refs_0_.1) | copy-start | bytes 2359300
  9.2 0.7 %copy-start.4 = (f32[64]{0:T(128)S(1)}, f32[64]{0:T(128)}, u32[]{:S(2)}) copy-start(f32[64]{0:T(128)} %param.14) | copy-start | bytes 772
  10.6 0.7 %copy-start.3 = (s32[4]{0:T(128)S(1)}, s32[4]{0:T(128)}, u32[]{:S(2)}) copy-start(s32[4]{0:T(128)} %clusters_ref) | copy-start | bytes 52
  11.8 1.4 %collective-permute-start.4 = (s32[8,128]{1,0:T(8,128)S(1)}, s32[8,128]{1,0:T(8,128)S(1)}, u32[]{:S(2)}, u32[]{:S(2)}) collective-permute-start(s32[8,128]{1,0:T(8,128)S(1)} %shard_map.84.refs_5_), channel_id=1, source_target_pairs={{0,1},{1,0},{2,3},{3,2},{4,5},{5,4},{6,7},{7,6},{8,9},{9,8},{10,11... | collective-permute-start | bytes 12296 | tf_op jit(solution)/shard_map/ppermute | solution.py:27
  13.2 7.6 %collective-permute-start.5 = (s32[8,128]{1,0:T(8,128)S(1)}, s32[8,128]{1,0:T(8,128)S(1)}, u32[]{:S(2)}, u32[]{:S(2)}) collective-permute-start(s32[8,128]{1,0:T(8,128)S(1)} %shard_map.84.refs_5_), channel_id=1, source_target_pairs={{0,2},{2,0},{4,6},{6,4},{8,10},{10,8},{12,14},{14,12},{1,3},{3,1},... | collective-permute-start | bytes 12296 | tf_op jit(solution)/shard_map/ppermute | solution.py:27
  20.8 4.8 %collective-permute-start.6 = (s32[8,128]{1,0:T(8,128)S(1)}, s32[8,128]{1,0:T(8,128)S(1)}, u32[]{:S(2)}, u32[]{:S(2)}) collective-permute-start(s32[8,128]{1,0:T(8,128)S(1)} %shard_map.84.refs_5_), channel_id=1, source_target_pairs={{0,3},{1,2},{2,1},{3,0},{4,7},{5,6},{6,5},{7,4},{8,11},{9,10},{10,... | collective-permute-start | bytes 12296 | tf_op jit(solution)/shard_map/ppermute | solution.py:33
  21.1 13.5 %collective-permute-start.9 = (bf16[264,768]{1,0:T(8,128)(2,1)S(1)}, bf16[264,768]{1,0:T(8,128)(2,1)S(1)}, u32[]{:S(2)}, u32[]{:S(2)}) collective-permute-start(bf16[264,768]{1,0:T(8,128)(2,1)S(1)} %collective-permute-done.2.refs_10_), channel_id=1, source_target_pairs={{0,4},{2,6},{4,0},{6,2},{8,12},{10,14},{12,8},{14,10},{1,5},{3,7},... | collective-permute-start | bytes 1216520 | tf_op jit(solution)/shard_map/ppermute | solution.py:22
  26.1 1.8 %collective-permute-start.7 = (bf16[256,768]{1,0:T(8,128)(2,1)S(1)}, bf16[256,768]{1,0:T(8,128)(2,1)S(1)}, u32[]{:S(2)}, u32[]{:S(2)}) collective-permute-start(bf16[256,768]{1,0:T(8,128)(2,1)S(1)} %get-tuple-element.22), channel_id=1, source_target_pairs={{0,1},{1,0},{2,3},{3,2},{4,5},{5,4},{6,7},{7,6},{8,9},{9,8},{10,11... | collective-permute-start | bytes 1179656 | tf_op jit(solution)/shard_map/ppermute | solution.py:27
  26.2 2.3 %collective-permute-start.8 = (bf16[256,768]{1,0:T(8,128)(2,1)S(1)}, bf16[256,768]{1,0:T(8,128)(2,1)S(1)}, u32[]{:S(2)}, u32[]{:S(2)}) collective-permute-start(bf16[256,768]{1,0:T(8,128)(2,1)S(1)} %get-tuple-element.21), channel_id=1, source_target_pairs={{0,1},{1,0},{2,3},{3,2},{4,5},{5,4},{6,7},{7,6},{8,9},{9,8},{10,11... | collective-permute-start | bytes 1179656 | tf_op jit(solution)/shard_map/ppermute | solution.py:27
  28.5 10.2 %copy-start.5 = (s32[64]{0:T(128)S(1)}, s32[64]{0:T(128)}, u32[]{:S(2)}) copy-start(s32[64]{0:T(128)} %param.15) | copy-start | bytes 772
  36.7 2.1 %collective-permute-start.10 = (f32[4,128]{1,0:T(4,128)S(1)}, f32[4,128]{1,0:T(4,128)S(1)}, u32[]{:S(2)}, u32[]{:S(2)}) collective-permute-start(f32[4,128]{1,0:T(4,128)S(1)} %get-tuple-element.23), channel_id=1, source_target_pairs={{0,1},{1,0},{2,3},{3,2},{4,5},{5,4},{6,7},{7,6},{8,9},{9,8},{10,11... | collective-permute-start | bytes 6152 | tf_op jit(solution)/shard_map/ppermute | solution.py:27
  36.7 3.7 %collective-permute-start.11 = (f32[4,128]{1,0:T(4,128)S(1)}, f32[4,128]{1,0:T(4,128)S(1)}, u32[]{:S(2)}, u32[]{:S(2)}) collective-permute-start(f32[4,128]{1,0:T(4,128)S(1)} %get-tuple-element.25), channel_id=1, source_target_pairs={{0,2},{2,0},{4,6},{6,4},{8,10},{10,8},{12,14},{14,12},{1,3},{3,1},... | collective-permute-start | bytes 6152 | tf_op jit(solution)/shard_map/ppermute | solution.py:27
  37.5 3.0 %collective-permute-start.12 = (f32[4,128]{1,0:T(4,128)S(1)}, f32[4,128]{1,0:T(4,128)S(1)}, u32[]{:S(2)}, u32[]{:S(2)}) collective-permute-start(f32[4,128]{1,0:T(4,128)S(1)} %get-tuple-element.24), channel_id=1, source_target_pairs={{0,3},{1,2},{2,1},{3,0},{4,7},{5,6},{6,5},{7,4},{8,11},{9,10},{10,... | collective-permute-start | bytes 6152 | tf_op jit(solution)/shard_map/ppermute | solution.py:33

commit v19 on v18

--- a/solution.py
+++ b/solution.py
@@ -171,9 +171,9 @@
     other = [jnp.where(row < 0.0, DEAD, -4.0) for row in ids]
     out_ref[...] = prev_ref[...]
 
-    def query_blocks(group, carry):
+    for group in range(number_ref.shape[0] // (3 * wide)):
         score = lax.dot_general(
-            qv[rows_of(wide * group, wide), :],
+            qv[wide * group * LANES : wide * (group + 1) * LANES, :],
             r_ref[pl.ds(0, height), :],
             (((1,), (1,)), ((), ())),
             preferred_element_type=jnp.float32,
@@ -188,10 +188,6 @@
                 acc = acc + jnp.exp2(part * scale + bias)
             row = pl.ds(slot_ref[entry], 1)
             out_ref[row, :] = out_ref[row, :] + jnp.sum(acc.T, axis=0, keepdims=True)
-        return carry
-
-    q_count = slot_ref[slot_ref.shape[0] - 8]
-    lax.fori_loop(0, (q_count + wide - 1) // wide, query_blocks, 0)
 
 
 def first_call(chunks, qblocks, pieces, wide, given, payloads):

time: 41.4 us -> 41.1 us (level)
  no operation moved by 1% of the time
where the time goes in v19:
time: 41.1 us; the launch traced here: 40.9 us
  starting transfers between devices  15 us (36%)
  waiting for transfers between devices  13.3 us (32%)
  Pallas kernels  7.18 us (17%)
  local copies, waits for them, and re-layouts  3.21 us (8%)
  between operations  1.41 us (3%)
  other arithmetic  0.85 us (2%)
    ppermute x8, waiting for transfers between devices, swap(): return lax.ppermute(value, axis, [(i, i ^ 1) for i in range(length)])  11.3 us
    ppermute x3, starting transfers between devices, trade(): return lax.ppermute(value, 'blk', [(i, i ^ mask) for i in range(length)])  8.11 us
    ppermute x8, starting transfers between devices, swap(): return lax.ppermute(value, axis, [(i, i ^ 1) for i in range(length)])  5.48 us
    pallas_call x1, Pallas kernels, first_call(): pl.pallas_call(functools.partial(first_kernel, chunks, qblocks, pieces, w...  4.86 us
    unnamed x12, local copies, waits for them, and re-layouts  3.12 us
    ppermute x3, waiting for transfers between devices, trade(): return lax.ppermute(value, 'blk', [(i, i ^ mask) for i in range(length)])  1.79 us
    pallas_call x1, Pallas kernels, last_call(): pl.pallas_call(functools.partial(last_kernel, chunks, wide), out_shape=ja...  1.69 us
    ppermute x2, starting transfers between devices, swap_both(): return lax.ppermute(value, ('blk', 'helper'), pairs)  1.37 us
  transfers between devices with their start and end apart: 13, of which 8 were waited for; matrix products, arithmetic and copies ran while one was open for 1% of the time, Pallas kernels for 13%

profile of v19, /device:TPU:0, one launch (start us, length us, event | category | flops | bytes accessed | tf_op | source)
XLA Modules:
  0.0 40.9 jit_solution(14578738041535929574)
XLA Ops:
  0.0 3.0 %collective-permute-start.1 = (bf16[512,768]{1,0:T(8,128)(2,1)}, bf16[512,768]{1,0:T(8,128)(2,1)S(1)}, u32[]{:S(2)}, u32[]{:S(2)}) collective-permute-start(bf16[512,768]{1,0:T(8,128)(2,1)} %refs_0_.1), channel_id=1, source_target_pairs={{0,2},{2,0},{4,6},{6,4},{8,10},{10,8},{12,14},{14,12},{1,3},{3,1},... | collective-permute-start | bytes 2359304 | tf_op jit(solution)/shard_map/ppermute | solution.py:27
  3.7 0.7 %copy-done.2 = s32[512]{0:T(512)S(1)} copy-done((s32[512]{0:T(512)S(1)}, s32[512]{0:T(512)}, u32[]{:S(2)}) %copy-start.2) | copy-done | bytes 2072
  4.4 3.7 %collective-permute-start.2 = (bf16[264,768]{1,0:T(8,128)(2,1)S(1)}, bf16[264,768]{1,0:T(8,128)(2,1)S(1)}, u32[]{:S(2)}, u32[]{:S(2)}) collective-permute-start(bf16[264,768]{1,0:T(8,128)(2,1)S(1)} %shard_map.83.refs_9_), channel_id=1, source_target_pairs={{0,12},{2,14},{4,8},{6,10},{8,4},{10,6},{12,0},{14,2},{1,13},{3,15... | collective-permute-start | bytes 1216520 | tf_op jit(solution)/shard_map/ppermute | solution.py:22
  8.1 1.1 %copy-done.1 = bf16[512,768]{1,0:T(8,128)(2,1)S(1)} copy-done((bf16[512,768]{1,0:T(8,128)(2,1)S(1)}, bf16[512,768]{1,0:T(8,128)(2,1)}, u32[]{:S(2)}) %copy-start.1) | copy-done | bytes 786456
  9.2 0.7 %copy-done.4 = f32[64]{0:T(128)S(1)} copy-done((f32[64]{0:T(128)S(1)}, f32[64]{0:T(128)}, u32[]{:S(2)}) %copy-start.4) | copy-done | bytes 280
  10.6 0.6 %copy-done.3 = s32[4]{0:T(128)S(1)} copy-done((s32[4]{0:T(128)S(1)}, s32[4]{0:T(128)}, u32[]{:S(2)}) %copy-start.3) | copy-done | bytes 40
  11.2 0.5 %shard_map.84.refs_5_ = s32[8,128]{1,0:T(8,128)S(1)} custom-call(s32[4]{0:T(128)S(1)} %copy-done.3, s32[1]{0:T(128)S(6)} %copy.12.count_ref), custom_call_target="tpu_custom_call" | custom-call | flops 1 | bytes 1 | tf_op jit(solution)/shard_map/pallas_call | solution.py:280
  11.8 0.6 %collective-permute-start.4 = (s32[8,128]{1,0:T(8,128)S(1)}, s32[8,128]{1,0:T(8,128)S(1)}, u32[]{:S(2)}, u32[]{:S(2)}) collective-permute-start(s32[8,128]{1,0:T(8,128)S(1)} %shard_map.84.refs_5_), channel_id=1, source_target_pairs={{0,1},{1,0},{2,3},{3,2},{4,5},{5,4},{6,7},{7,6},{8,9},{9,8},{10,11... | collective-permute-start | bytes 12296 | tf_op jit(solution)/shard_map/ppermute | solution.py:27
  12.3 0.8 %collective-permute-done.4.refs_6_ = s32[8,128]{1,0:T(8,128)S(1)} collective-permute-done((s32[8,128]{1,0:T(8,128)S(1)}, s32[8,128]{1,0:T(8,128)S(1)}, u32[]{:S(2)}, u32[]{:S(2)}) %collective-permute-start.4) | collective-permute-done | bytes 4128 | tf_op jit(solution)/shard_map/ppermute | solution.py:27
  13.2 0.5 %collective-permute-start.5 = (s32[8,128]{1,0:T(8,128)S(1)}, s32[8,128]{1,0:T(8,128)S(1)}, u32[]{:S(2)}, u32[]{:S(2)}) collective-permute-start(s32[8,128]{1,0:T(8,128)S(1)} %shard_map.84.refs_5_), channel_id=1, source_target_pairs={{0,2},{2,0},{4,6},{6,4},{8,10},{10,8},{12,14},{14,12},{1,3},{3,1},... | collective-permute-start | bytes 12296 | tf_op jit(solution)/shard_map/ppermute | solution.py:27
  13.7 7.1 %collective-permute-done.5.refs_7_ = s32[8,128]{1,0:T(8,128)S(1)} collective-permute-done((s32[8,128]{1,0:T(8,128)S(1)}, s32[8,128]{1,0:T(8,128)S(1)}, u32[]{:S(2)}, u32[]{:S(2)}) %collective-permute-start.5) | collective-permute-done | bytes 4128 | tf_op jit(solution)/shard_map/ppermute | solution.py:27
  20.8 0.3 collective-permute-start.6
  21.1 4.4 %collective-permute-start.9 = (bf16[264,768]{1,0:T(8,128)(2,1)S(1)}, bf16[264,768]{1,0:T(8,128)(2,1)S(1)}, u32[]{:S(2)}, u32[]{:S(2)}) collective-permute-start(bf16[264,768]{1,0:T(8,128)(2,1)S(1)} %collective-permute-done.2.refs_10_), channel_id=1, source_target_pairs={{0,4},{2,6},{4,0},{6,2},{8,12},{10,14},{12,8},{14,10},{1,5},{3,7},... | collective-permute-start | bytes 1216520 | tf_op jit(solution)/shard_map/ppermute | solution.py:22
  25.6 0.5 %collective-permute-done.3.refs_11_ = bf16[264,768]{1,0:T(8,128)(2,1)S(1)} collective-permute-done((bf16[264,768]{1,0:T(8,128)(2,1)S(1)}, bf16[264,768]{1,0:T(8,128)(2,1)S(1)}, u32[]{:S(2)}, u32[]{:S(2)}) %collective-permute-start.3) | collective-permute-done | bytes 405536 | tf_op jit(solution)/shard_map/ppermute | solution.py:22
  26.2 0.5 %collective-permute-start.8 = (bf16[256,768]{1,0:T(8,128)(2,1)S(1)}, bf16[256,768]{1,0:T(8,128)(2,1)S(1)}, u32[]{:S(2)}, u32[]{:S(2)}) collective-permute-start(bf16[256,768]{1,0:T(8,128)(2,1)S(1)} %get-tuple-element.21), channel_id=1, source_target_pairs={{0,1},{1,0},{2,3},{3,2},{4,5},{5,4},{6,7},{7,6},{8,9},{9,8},{10,11... | collective-permute-start | bytes 1179656 | tf_op jit(solution)/shard_map/ppermute | solution.py:27
  26.7 1.2 %collective-permute-done.7.refs_3_ = bf16[256,768]{1,0:T(8,128)(2,1)S(1)} collective-permute-done((bf16[256,768]{1,0:T(8,128)(2,1)S(1)}, bf16[256,768]{1,0:T(8,128)(2,1)S(1)}, u32[]{:S(2)}, u32[]{:S(2)}) %collective-permute-start.7) | collective-permute-done | bytes 393248 | tf_op jit(solution)/shard_map/ppermute | solution.py:27
  27.9 0.6 %collective-permute-done.8.refs_4_ = bf16[256,768]{1,0:T(8,128)(2,1)S(1)} collective-permute-done((bf16[256,768]{1,0:T(8,128)(2,1)S(1)}, bf16[256,768]{1,0:T(8,128)(2,1)S(1)}, u32[]{:S(2)}, u32[]{:S(2)}) %collective-permute-start.8) | collective-permute-done | bytes 393248 | tf_op jit(solution)/shard_map/ppermute | solution.py:27
  28.5 4.9 %shard_map.85 = (f32[24,128]{1,0:T(8,128)S(1)}, bf16[2048,768]{1,0:T(8,128)(2,1)S(1)}, s32[24]{0:T(128)S(1)}, f32[48]{0:T(128)S(1)}) custom-call(f32[1,64]{1,0:T(1,128)S(1)} %get-tuple-element.13.beta_ref, bf16[512,768]{1,0:T(8,128)(2,1)S(1)} %get-tuple-element.14.refs_0_, bf16[512,768]{1,0:T(8,128)(2,1)S(1)} %collective-permute-done.refs_1_, ...), custom_call_target="tpu_custom_call" | custom-call | flops 1 | bytes 1 | tf_op jit(solution)/shard_map/pallas_call | solution.py:197
  33.3 1.3 %collective-permute-done.9.r_ref = bf16[264,768]{1,0:T(8,128)(2,1)S(1)} collective-permute-done((bf16[264,768]{1,0:T(8,128)(2,1)S(1)}, bf16[264,768]{1,0:T(8,128)(2,1)S(1)}, u32[]{:S(2)}, u32[]{:S(2)}) %collective-permute-start.9) | collective-permute-done | bytes 405536 | tf_op jit(solution)/shard_map/ppermute | solution.py:22
  34.6 1.7 %shard_map.86 = f32[24,128]{1,0:T(8,128)S(1)} custom-call(s32[24]{0:T(128)S(1)} %get-tuple-element.17.slot_ref, f32[48]{0:T(128)S(1)} %get-tuple-element.18.number_ref, bf16[2048,768]{1,0:T(8,128)(2,1)S(1)} %get-tuple-element.19.qv, f32[24,128]{1,0:T(8,128)S(1)} %get-tuple-element.20.prev_ref, bf16[264,768]{1,0:T(8,128)(2,1)S(1)} %collective-permute-done.9.r_ref), custom_call_target="tpu_custom_call" | custom-call | flops 1 | bytes 1 | tf_op jit(solution)/shard_map/pallas_call | solution.py:220
  36.4 0.8 %collective-permute-start.11 = (f32[4,128]{1,0:T(4,128)S(1)}, f32[4,128]{1,0:T(4,128)S(1)}, u32[]{:S(2)}, u32[]{:S(2)}) collective-permute-start(f32[4,128]{1,0:T(4,128)S(1)} %get-tuple-element.25), channel_id=1, source_target_pairs={{0,2},{2,0},{4,6},{6,4},{8,10},{10,8},{12,14},{14,12},{1,3},{3,1},... | collective-permute-start | bytes 6152 | tf_op jit(solution)/shard_map/ppermute | solution.py:27
  37.2 1.1 %collective-permute-start.12 = (f32[4,128]{1,0:T(4,128)S(1)}, f32[4,128]{1,0:T(4,128)S(1)}, u32[]{:S(2)}, u32[]{:S(2)}) collective-permute-start(f32[4,128]{1,0:T(4,128)S(1)} %get-tuple-element.24), channel_id=1, source_target_pairs={{0,3},{1,2},{2,1},{3,0},{4,7},{5,6},{6,5},{7,4},{8,11},{9,10},{10,... | collective-permute-start | bytes 6152 | tf_op jit(solution)/shard_map/ppermute | solution.py:33
  38.5 1.6 %collective-permute-done.11 = f32[4,128]{1,0:T(4,128)S(1)} collective-permute-done((f32[4,128]{1,0:T(4,128)S(1)}, f32[4,128]{1,0:T(4,128)S(1)}, u32[]{:S(2)}, u32[]{:S(2)}) %collective-permute-start.11) | collective-permute-done | bytes 2080 | tf_op jit(solution)/shard_map/ppermute | solution.py:27
  40.2 0.7 %log-plus-one_bitcast_fusion = f32[512]{0:T(512)} fusion(f32[4,128]{1,0:T(4,128)S(1)} %collective-permute-done.12, f32[4,128]{1,0:T(4,128)S(1)} %collective-permute-done.11, f32[4,128]{1,0:T(4,128)S(1)} %collective-permute-done.10, f32[24,128]{1,0:T(8,128)S(1)} %shard_map.86, f32[4]{0:T(128)S(1)} %convert_element_type.7), kind=kLoop, calls=%fused_computation.4 | loop fusion | flops 2048 | bytes 10256 | tf_op jit(solution)/shard_map/reshape | solution.py:305
  (25 shorter events, 0.7 us)
Async XLA Ops:
  0.0 3.6 %copy-start = (bf16[512,768]{1,0:T(8,128)(2,1)S(1)}, bf16[512,768]{1,0:T(8,128)(2,1)}, u32[]{:S(2)}) copy-start(bf16[512,768]{1,0:T(8,128)(2,1)} %param.11) | copy-start | bytes 2359300
  0.0 26.0 %collective-permute-start.1 = (bf16[512,768]{1,0:T(8,128)(2,1)}, bf16[512,768]{1,0:T(8,128)(2,1)S(1)}, u32[]{:S(2)}, u32[]{:S(2)}) collective-permute-start(bf16[512,768]{1,0:T(8,128)(2,1)} %refs_0_.1), channel_id=1, source_target_pairs={{0,2},{2,0},{4,6},{6,4},{8,10},{10,8},{12,14},{14,12},{1,3},{3,1},... | collective-permute-start | bytes 2359304 | tf_op jit(solution)/shard_map/ppermute | solution.py:27
  3.7 0.7 %copy-start.2 = (s32[512]{0:T(512)S(1)}, s32[512]{0:T(512)}, u32[]{:S(2)}) copy-start(s32[512]{0:T(512)} %param.12) | copy-start | bytes 6148
  4.4 16.7 %collective-permute-start.2 = (bf16[264,768]{1,0:T(8,128)(2,1)S(1)}, bf16[264,768]{1,0:T(8,128)(2,1)S(1)}, u32[]{:S(2)}, u32[]{:S(2)}) collective-permute-start(bf16[264,768]{1,0:T(8,128)(2,1)S(1)} %shard_map.83.refs_9_), channel_id=1, source_target_pairs={{0,12},{2,14},{4,8},{6,10},{8,4},{10,6},{12,0},{14,2},{1,13},{3,15... | collective-permute-start | bytes 1216520 | tf_op jit(solution)/shard_map/ppermute | solution.py:22
  8.1 18.0 %collective-permute-start.3 = (bf16[264,768]{1,0:T(8,128)(2,1)S(1)}, bf16[264,768]{1,0:T(8,128)(2,1)S(1)}, u32[]{:S(2)}, u32[]{:S(2)}) collective-permute-start(bf16[264,768]{1,0:T(8,128)(2,1)S(1)} %shard_map.83.refs_9_), channel_id=1, source_target_pairs={{0,4},{2,6},{4,0},{6,2},{8,12},{10,14},{12,8},{14,10},{1,5},{3,7},... | collective-permute-start | bytes 1216520 | tf_op jit(solution)/shard_map/ppermute | solution.py:22
  8.1 18.6 %collective-permute-start = (bf16[512,768]{1,0:T(8,128)(2,1)}, bf16[512,768]{1,0:T(8,128)(2,1)S(1)}, u32[]{:S(2)}, u32[]{:S(2)}) collective-permute-start(bf16[512,768]{1,0:T(8,128)(2,1)} %refs_0_.1), channel_id=1, source_target_pairs={{0,1},{1,0},{2,3},{3,2},{4,5},{5,4},{6,7},{7,6},{8,9},{9,8},{10,11... | collective-permute-start | bytes 2359304 | tf_op jit(solution)/shard_map/ppermute | solution.py:27
  8.1 1.1 %copy-start.1 = (bf16[512,768]{1,0:T(8,128)(2,1)S(1)}, bf16[512,768]{1,0:T(8,128)(2,1)}, u32[]{:S(2)}) copy-start(bf16[512,768]{1,0:T(8,128)(2,1)} %refs_0_.1) | copy-start | bytes 2359300
  9.2 0.7 %copy-start.4 = (f32[64]{0:T(128)S(1)}, f32[64]{0:T(128)}, u32[]{:S(2)}) copy-start(f32[64]{0:T(128)} %param.14) | copy-start | bytes 772
  10.6 0.7 %copy-start.3 = (s32[4]{0:T(128)S(1)}, s32[4]{0:T(128)}, u32[]{:S(2)}) copy-start(s32[4]{0:T(128)} %clusters_ref) | copy-start | bytes 52
  11.8 1.4 %collective-permute-start.4 = (s32[8,128]{1,0:T(8,128)S(1)}, s32[8,128]{1,0:T(8,128)S(1)}, u32[]{:S(2)}, u32[]{:S(2)}) collective-permute-start(s32[8,128]{1,0:T(8,128)S(1)} %shard_map.84.refs_5_), channel_id=1, source_target_pairs={{0,1},{1,0},{2,3},{3,2},{4,5},{5,4},{6,7},{7,6},{8,9},{9,8},{10,11... | collective-permute-start | bytes 12296 | tf_op jit(solution)/shard_map/ppermute | solution.py:27
  13.2 7.6 %collective-permute-start.5 = (s32[8,128]{1,0:T(8,128)S(1)}, s32[8,128]{1,0:T(8,128)S(1)}, u32[]{:S(2)}, u32[]{:S(2)}) collective-permute-start(s32[8,128]{1,0:T(8,128)S(1)} %shard_map.84.refs_5_), channel_id=1, source_target_pairs={{0,2},{2,0},{4,6},{6,4},{8,10},{10,8},{12,14},{14,12},{1,3},{3,1},... | collective-permute-start | bytes 12296 | tf_op jit(solution)/shard_map/ppermute | solution.py:27
  20.8 4.8 %collective-permute-start.6 = (s32[8,128]{1,0:T(8,128)S(1)}, s32[8,128]{1,0:T(8,128)S(1)}, u32[]{:S(2)}, u32[]{:S(2)}) collective-permute-start(s32[8,128]{1,0:T(8,128)S(1)} %shard_map.84.refs_5_), channel_id=1, source_target_pairs={{0,3},{1,2},{2,1},{3,0},{4,7},{5,6},{6,5},{7,4},{8,11},{9,10},{10,... | collective-permute-start | bytes 12296 | tf_op jit(solution)/shard_map/ppermute | solution.py:33
  21.1 13.5 %collective-permute-start.9 = (bf16[264,768]{1,0:T(8,128)(2,1)S(1)}, bf16[264,768]{1,0:T(8,128)(2,1)S(1)}, u32[]{:S(2)}, u32[]{:S(2)}) collective-permute-start(bf16[264,768]{1,0:T(8,128)(2,1)S(1)} %collective-permute-done.2.refs_10_), channel_id=1, source_target_pairs={{0,4},{2,6},{4,0},{6,2},{8,12},{10,14},{12,8},{14,10},{1,5},{3,7},... | collective-permute-start | bytes 1216520 | tf_op jit(solution)/shard_map/ppermute | solution.py:22
  26.1 1.8 %collective-permute-start.7 = (bf16[256,768]{1,0:T(8,128)(2,1)S(1)}, bf16[256,768]{1,0:T(8,128)(2,1)S(1)}, u32[]{:S(2)}, u32[]{:S(2)}) collective-permute-start(bf16[256,768]{1,0:T(8,128)(2,1)S(1)} %get-tuple-element.22), channel_id=1, source_target_pairs={{0,1},{1,0},{2,3},{3,2},{4,5},{5,4},{6,7},{7,6},{8,9},{9,8},{10,11... | collective-permute-start | bytes 1179656 | tf_op jit(solution)/shard_map/ppermute | solution.py:27
  26.2 2.3 %collective-permute-start.8 = (bf16[256,768]{1,0:T(8,128)(2,1)S(1)}, bf16[256,768]{1,0:T(8,128)(2,1)S(1)}, u32[]{:S(2)}, u32[]{:S(2)}) collective-permute-start(bf16[256,768]{1,0:T(8,128)(2,1)S(1)} %get-tuple-element.21), channel_id=1, source_target_pairs={{0,1},{1,0},{2,3},{3,2},{4,5},{5,4},{6,7},{7,6},{8,9},{9,8},{10,11... | collective-permute-start | bytes 1179656 | tf_op jit(solution)/shard_map/ppermute | solution.py:27
  28.5 9.8 %copy-start.5 = (s32[64]{0:T(128)S(1)}, s32[64]{0:T(128)}, u32[]{:S(2)}) copy-start(s32[64]{0:T(128)} %param.15) | copy-start | bytes 772
  36.3 2.1 %collective-permute-start.10 = (f32[4,128]{1,0:T(4,128)S(1)}, f32[4,128]{1,0:T(4,128)S(1)}, u32[]{:S(2)}, u32[]{:S(2)}) collective-permute-start(f32[4,128]{1,0:T(4,128)S(1)} %get-tuple-element.23), channel_id=1, source_target_pairs={{0,1},{1,0},{2,3},{3,2},{4,5},{5,4},{6,7},{7,6},{8,9},{9,8},{10,11... | collective-permute-start | bytes 6152 | tf_op jit(solution)/shard_map/ppermute | solution.py:27
  36.4 3.7 %collective-permute-start.11 = (f32[4,128]{1,0:T(4,128)S(1)}, f32[4,128]{1,0:T(4,128)S(1)}, u32[]{:S(2)}, u32[]{:S(2)}) collective-permute-start(f32[4,128]{1,0:T(4,128)S(1)} %get-tuple-element.25), channel_id=1, source_target_pairs={{0,2},{2,0},{4,6},{6,4},{8,10},{10,8},{12,14},{14,12},{1,3},{3,1},... | collective-permute-start | bytes 6152 | tf_op jit(solution)/shard_map/ppermute | solution.py:27
  37.2 3.0 %collective-permute-start.12 = (f32[4,128]{1,0:T(4,128)S(1)}, f32[4,128]{1,0:T(4,128)S(1)}, u32[]{:S(2)}, u32[]{:S(2)}) collective-permute-start(f32[4,128]{1,0:T(4,128)S(1)} %get-tuple-element.24), channel_id=1, source_target_pairs={{0,3},{1,2},{2,1},{3,0},{4,7},{5,6},{6,5},{7,4},{8,11},{9,10},{10,... | collective-permute-start | bytes 6152 | tf_op jit(solution)/shard_map/ppermute | solution.py:33

commit v20 on v19

--- a/solution.py
+++ b/solution.py
@@ -262,7 +262,7 @@
         own.reshape(chunks * LANES, width),
     )
 
-    held, mask = [own], sources - 1
+    held, mask = [own], sources // 2
     while mask:
         held = held + [trade(x, 2 * mask) for x in held]
         mask //= 2

time: 41.1 us -> 41.7 us (1.015)
  waiting for transfers between devices: 13.3 us -> 18.1 us
  starting transfers between devices: 15 us -> 11.7 us
  Pallas kernels: 7.18 us -> 6.26 us
    ppermute x3, waiting for transfers between devices: 1.79 us -> 7.1 us  [trade(): return lax.ppermute(value, 'blk', [(i, i ^ mask) for i in range(length)])]
    ppermute x3, starting transfers between devices: 8.11 us -> 4.8 us  [trade(): return lax.ppermute(value, 'blk', [(i, i ^ mask) for i in range(length)])]
    pallas_call x1, Pallas kernels: 4.86 us -> 3.94 us  [first_call(): pl.pallas_call(functools.partial(first_kernel, chunks, qblocks, pieces, w...]
    ppermute x8, waiting for transfers between devices: 11.3 us -> 10.8 us  [swap(): return lax.ppermute(value, axis, [(i, i ^ 1) for i in range(length)])]
  transfers between devices with their start and end apart: 13 -> 13, of which waited for: 8 -> 8; matrix products, arithmetic and copies ran while one was open for 1% -> 1% of each run, Pallas kernels for 13% -> 11%
where the time goes in v20:
time: 41.7 us; the launch traced here: 41.5 us
  waiting for transfers between devices  18.1 us (43%)
  starting transfers between devices  11.7 us (28%)
  Pallas kernels  6.26 us (15%)
  local copies, waits for them, and re-layouts  3.22 us (8%)
  between operations  1.41 us (3%)
  other arithmetic  0.85 us (2%)
    ppermute x8, waiting for transfers between devices, swap(): return lax.ppermute(value, axis, [(i, i ^ 1) for i in range(length)])  10.8 us
    ppermute x3, waiting for transfers between devices, trade(): return lax.ppermute(value, 'blk', [(i, i ^ mask) for i in range(length)])  7.1 us
    ppermute x8, starting transfers between devices, swap(): return lax.ppermute(value, axis, [(i, i ^ 1) for i in range(length)])  5.57 us
    ppermute x3, starting transfers between devices, trade(): return lax.ppermute(value, 'blk', [(i, i ^ mask) for i in range(length)])  4.8 us
    pallas_call x1, Pallas kernels, first_call(): pl.pallas_call(functools.partial(first_kernel, chunks, qblocks, pieces, w...  3.94 us
    unnamed x12, local copies, waits for them, and re-layouts  3.12 us
    pallas_call x1, Pallas kernels, last_call(): pl.pallas_call(functools.partial(last_kernel, chunks, wide), out_shape=ja...  1.69 us
    ppermute x2, starting transfers between devices, swap_both(): return lax.ppermute(value, ('blk', 'helper'), pairs)  1.28 us
  transfers between devices with their start and end apart: 13, of which 8 were waited for; matrix products, arithmetic and copies ran while one was open for 1% of the time, Pallas kernels for 11%

profile of v20, /device:TPU:0, one launch (start us, length us, event | category | flops | bytes accessed | tf_op | source)
XLA Modules:
  0.0 41.5 jit_solution(14331773228197845198)
XLA Ops:
  0.0 3.0 %collective-permute-start.1 = (bf16[512,768]{1,0:T(8,128)(2,1)}, bf16[512,768]{1,0:T(8,128)(2,1)S(1)}, u32[]{:S(2)}, u32[]{:S(2)}) collective-permute-start(bf16[512,768]{1,0:T(8,128)(2,1)} %refs_0_.1), channel_id=1, source_target_pairs={{0,2},{2,0},{4,6},{6,4},{8,10},{10,8},{12,14},{14,12},{1,3},{3,1},... | collective-permute-start | bytes 2359304 | tf_op jit(solution)/shard_map/ppermute | solution.py:27
  3.7 0.7 %copy-done.2 = s32[512]{0:T(512)S(1)} copy-done((s32[512]{0:T(512)S(1)}, s32[512]{0:T(512)}, u32[]{:S(2)}) %copy-start.2) | copy-done | bytes 2072
  4.4 2.7 %collective-permute-start.2 = (bf16[264,768]{1,0:T(8,128)(2,1)S(1)}, bf16[264,768]{1,0:T(8,128)(2,1)S(1)}, u32[]{:S(2)}, u32[]{:S(2)}) collective-permute-start(bf16[264,768]{1,0:T(8,128)(2,1)S(1)} %shard_map.83.refs_9_), channel_id=1, source_target_pairs={{0,8},{2,10},{4,12},{6,14},{8,0},{10,2},{12,4},{14,6},{1,9},{3,11}... | collective-permute-start | bytes 1216520 | tf_op jit(solution)/shard_map/ppermute | solution.py:22
  7.0 1.6 %collective-permute-start.3 = (bf16[264,768]{1,0:T(8,128)(2,1)S(1)}, bf16[264,768]{1,0:T(8,128)(2,1)S(1)}, u32[]{:S(2)}, u32[]{:S(2)}) collective-permute-start(bf16[264,768]{1,0:T(8,128)(2,1)S(1)} %shard_map.83.refs_9_), channel_id=1, source_target_pairs={{0,4},{2,6},{4,0},{6,2},{8,12},{10,14},{12,8},{14,10},{1,5},{3,7},... | collective-permute-start | bytes 1216520 | tf_op jit(solution)/shard_map/ppermute | solution.py:22
  8.6 1.1 %copy-done.1 = bf16[512,768]{1,0:T(8,128)(2,1)S(1)} copy-done((bf16[512,768]{1,0:T(8,128)(2,1)S(1)}, bf16[512,768]{1,0:T(8,128)(2,1)}, u32[]{:S(2)}) %copy-start.1) | copy-done | bytes 786456
  9.8 0.7 %copy-done.4 = f32[64]{0:T(128)S(1)} copy-done((f32[64]{0:T(128)S(1)}, f32[64]{0:T(128)}, u32[]{:S(2)}) %copy-start.4) | copy-done | bytes 280
  11.1 0.6 %copy-done.3 = s32[4]{0:T(128)S(1)} copy-done((s32[4]{0:T(128)S(1)}, s32[4]{0:T(128)}, u32[]{:S(2)}) %copy-start.3) | copy-done | bytes 40
  11.8 0.5 %shard_map.84.refs_5_ = s32[8,128]{1,0:T(8,128)S(1)} custom-call(s32[4]{0:T(128)S(1)} %copy-done.3, s32[1]{0:T(128)S(6)} %copy.12.count_ref), custom_call_target="tpu_custom_call" | custom-call | flops 1 | bytes 1 | tf_op jit(solution)/shard_map/pallas_call | solution.py:280
  12.3 0.6 %collective-permute-start.4 = (s32[8,128]{1,0:T(8,128)S(1)}, s32[8,128]{1,0:T(8,128)S(1)}, u32[]{:S(2)}, u32[]{:S(2)}) collective-permute-start(s32[8,128]{1,0:T(8,128)S(1)} %shard_map.84.refs_5_), channel_id=1, source_target_pairs={{0,1},{1,0},{2,3},{3,2},{4,5},{5,4},{6,7},{7,6},{8,9},{9,8},{10,11... | collective-permute-start | bytes 12296 | tf_op jit(solution)/shard_map/ppermute | solution.py:27
  12.9 0.8 %collective-permute-done.4.refs_6_ = s32[8,128]{1,0:T(8,128)S(1)} collective-permute-done((s32[8,128]{1,0:T(8,128)S(1)}, s32[8,128]{1,0:T(8,128)S(1)}, u32[]{:S(2)}, u32[]{:S(2)}) %collective-permute-start.4) | collective-permute-done | bytes 4128 | tf_op jit(solution)/shard_map/ppermute | solution.py:27
  13.7 0.5 %collective-permute-start.5 = (s32[8,128]{1,0:T(8,128)S(1)}, s32[8,128]{1,0:T(8,128)S(1)}, u32[]{:S(2)}, u32[]{:S(2)}) collective-permute-start(s32[8,128]{1,0:T(8,128)S(1)} %shard_map.84.refs_5_), channel_id=1, source_target_pairs={{0,2},{2,0},{4,6},{6,4},{8,10},{10,8},{12,14},{14,12},{1,3},{3,1},... | collective-permute-start | bytes 12296 | tf_op jit(solution)/shard_map/ppermute | solution.py:27
  14.2 6.6 %collective-permute-done.5.refs_7_ = s32[8,128]{1,0:T(8,128)S(1)} collective-permute-done((s32[8,128]{1,0:T(8,128)S(1)}, s32[8,128]{1,0:T(8,128)S(1)}, u32[]{:S(2)}, u32[]{:S(2)}) %collective-permute-start.5) | collective-permute-done | bytes 4128 | tf_op jit(solution)/shard_map/ppermute | solution.py:27
  21.1 3.9 %collective-permute-done.2.refs_10_ = bf16[264,768]{1,0:T(8,128)(2,1)S(1)} collective-permute-done((bf16[264,768]{1,0:T(8,128)(2,1)S(1)}, bf16[264,768]{1,0:T(8,128)(2,1)S(1)}, u32[]{:S(2)}, u32[]{:S(2)}) %collective-permute-start.2) | collective-permute-done | bytes 405536 | tf_op jit(solution)/shard_map/ppermute | solution.py:22
  25.0 0.6 %collective-permute-start.9 = (bf16[264,768]{1,0:T(8,128)(2,1)S(1)}, bf16[264,768]{1,0:T(8,128)(2,1)S(1)}, u32[]{:S(2)}, u32[]{:S(2)}) collective-permute-start(bf16[264,768]{1,0:T(8,128)(2,1)S(1)} %collective-permute-done.2.refs_10_), channel_id=1, source_target_pairs={{0,4},{2,6},{4,0},{6,2},{8,12},{10,14},{12,8},{14,10},{1,5},{3,7},... | collective-permute-start | bytes 1216520 | tf_op jit(solution)/shard_map/ppermute | solution.py:22
  25.7 0.5 %collective-permute-start.8 = (bf16[256,768]{1,0:T(8,128)(2,1)S(1)}, bf16[256,768]{1,0:T(8,128)(2,1)S(1)}, u32[]{:S(2)}, u32[]{:S(2)}) collective-permute-start(bf16[256,768]{1,0:T(8,128)(2,1)S(1)} %get-tuple-element.21), channel_id=1, source_target_pairs={{0,1},{1,0},{2,3},{3,2},{4,5},{5,4},{6,7},{7,6},{8,9},{9,8},{10,11... | collective-permute-start | bytes 1179656 | tf_op jit(solution)/shard_map/ppermute | solution.py:27
  26.2 1.2 %collective-permute-done.7.refs_3_ = bf16[256,768]{1,0:T(8,128)(2,1)S(1)} collective-permute-done((bf16[256,768]{1,0:T(8,128)(2,1)S(1)}, bf16[256,768]{1,0:T(8,128)(2,1)S(1)}, u32[]{:S(2)}, u32[]{:S(2)}) %collective-permute-start.7) | collective-permute-done | bytes 393248 | tf_op jit(solution)/shard_map/ppermute | solution.py:27
  27.4 0.6 %collective-permute-done.8.refs_4_ = bf16[256,768]{1,0:T(8,128)(2,1)S(1)} collective-permute-done((bf16[256,768]{1,0:T(8,128)(2,1)S(1)}, bf16[256,768]{1,0:T(8,128)(2,1)S(1)}, u32[]{:S(2)}, u32[]{:S(2)}) %collective-permute-start.8) | collective-permute-done | bytes 393248 | tf_op jit(solution)/shard_map/ppermute | solution.py:27
  28.0 3.9 %shard_map.85 = (f32[24,128]{1,0:T(8,128)S(1)}, bf16[2048,768]{1,0:T(8,128)(2,1)S(1)}, s32[24]{0:T(128)S(1)}, f32[48]{0:T(128)S(1)}) custom-call(f32[1,64]{1,0:T(1,128)S(1)} %get-tuple-element.13.beta_ref, bf16[512,768]{1,0:T(8,128)(2,1)S(1)} %get-tuple-element.14.refs_0_, bf16[512,768]{1,0:T(8,128)(2,1)S(1)} %collective-permute-done.refs_1_, ...), custom_call_target="tpu_custom_call" | custom-call | flops 1 | bytes 1 | tf_op jit(solution)/shard_map/pallas_call | solution.py:197
  31.9 3.2 %collective-permute-done.9.r_ref = bf16[264,768]{1,0:T(8,128)(2,1)S(1)} collective-permute-done((bf16[264,768]{1,0:T(8,128)(2,1)S(1)}, bf16[264,768]{1,0:T(8,128)(2,1)S(1)}, u32[]{:S(2)}, u32[]{:S(2)}) %collective-permute-start.9) | collective-permute-done | bytes 405536 | tf_op jit(solution)/shard_map/ppermute | solution.py:22
  35.2 1.7 %shard_map.86 = f32[24,128]{1,0:T(8,128)S(1)} custom-call(s32[24]{0:T(128)S(1)} %get-tuple-element.17.slot_ref, f32[48]{0:T(128)S(1)} %get-tuple-element.18.number_ref, bf16[2048,768]{1,0:T(8,128)(2,1)S(1)} %get-tuple-element.19.qv, f32[24,128]{1,0:T(8,128)S(1)} %get-tuple-element.20.prev_ref, bf16[264,768]{1,0:T(8,128)(2,1)S(1)} %collective-permute-done.9.r_ref), custom_call_target="tpu_custom_call" | custom-call | flops 1 | bytes 1 | tf_op jit(solution)/shard_map/pallas_call | solution.py:220
  36.9 0.9 %collective-permute-start.11 = (f32[4,128]{1,0:T(4,128)S(1)}, f32[4,128]{1,0:T(4,128)S(1)}, u32[]{:S(2)}, u32[]{:S(2)}) collective-permute-start(f32[4,128]{1,0:T(4,128)S(1)} %get-tuple-element.25), channel_id=1, source_target_pairs={{0,2},{2,0},{4,6},{6,4},{8,10},{10,8},{12,14},{14,12},{1,3},{3,1},... | collective-permute-start | bytes 6152 | tf_op jit(solution)/shard_map/ppermute | solution.py:27
  37.8 1.0 %collective-permute-start.12 = (f32[4,128]{1,0:T(4,128)S(1)}, f32[4,128]{1,0:T(4,128)S(1)}, u32[]{:S(2)}, u32[]{:S(2)}) collective-permute-start(f32[4,128]{1,0:T(4,128)S(1)} %get-tuple-element.24), channel_id=1, source_target_pairs={{0,3},{1,2},{2,1},{3,0},{4,7},{5,6},{6,5},{7,4},{8,11},{9,10},{10,... | collective-permute-start | bytes 6152 | tf_op jit(solution)/shard_map/ppermute | solution.py:33
  39.0 1.6 %collective-permute-done.11 = f32[4,128]{1,0:T(4,128)S(1)} collective-permute-done((f32[4,128]{1,0:T(4,128)S(1)}, f32[4,128]{1,0:T(4,128)S(1)}, u32[]{:S(2)}, u32[]{:S(2)}) %collective-permute-start.11) | collective-permute-done | bytes 2080 | tf_op jit(solution)/shard_map/ppermute | solution.py:27
  40.8 0.7 %log-plus-one_bitcast_fusion = f32[512]{0:T(512)} fusion(f32[4,128]{1,0:T(4,128)S(1)} %collective-permute-done.12, f32[4,128]{1,0:T(4,128)S(1)} %collective-permute-done.11, f32[4,128]{1,0:T(4,128)S(1)} %collective-permute-done.10, f32[24,128]{1,0:T(8,128)S(1)} %shard_map.86, f32[4]{0:T(128)S(1)} %convert_element_type.7), kind=kLoop, calls=%fused_computation.4 | loop fusion | flops 2048 | bytes 10256 | tf_op jit(solution)/shard_map/reshape | solution.py:305
  (25 shorter events, 1.1 us)
Async XLA Ops:
  0.0 3.6 %copy-start = (bf16[512,768]{1,0:T(8,128)(2,1)S(1)}, bf16[512,768]{1,0:T(8,128)(2,1)}, u32[]{:S(2)}) copy-start(bf16[512,768]{1,0:T(8,128)(2,1)} %param.11) | copy-start | bytes 2359300
  0.0 25.6 %collective-permute-start.1 = (bf16[512,768]{1,0:T(8,128)(2,1)}, bf16[512,768]{1,0:T(8,128)(2,1)S(1)}, u32[]{:S(2)}, u32[]{:S(2)}) collective-permute-start(bf16[512,768]{1,0:T(8,128)(2,1)} %refs_0_.1), channel_id=1, source_target_pairs={{0,2},{2,0},{4,6},{6,4},{8,10},{10,8},{12,14},{14,12},{1,3},{3,1},... | collective-permute-start | bytes 2359304 | tf_op jit(solution)/shard_map/ppermute | solution.py:27
  3.7 0.7 %copy-start.2 = (s32[512]{0:T(512)S(1)}, s32[512]{0:T(512)}, u32[]{:S(2)}) copy-start(s32[512]{0:T(512)} %param.12) | copy-start | bytes 6148
  4.4 20.6 %collective-permute-start.2 = (bf16[264,768]{1,0:T(8,128)(2,1)S(1)}, bf16[264,768]{1,0:T(8,128)(2,1)S(1)}, u32[]{:S(2)}, u32[]{:S(2)}) collective-permute-start(bf16[264,768]{1,0:T(8,128)(2,1)S(1)} %shard_map.83.refs_9_), channel_id=1, source_target_pairs={{0,8},{2,10},{4,12},{6,14},{8,0},{10,2},{12,4},{14,6},{1,9},{3,11}... | collective-permute-start | bytes 1216520 | tf_op jit(solution)/shard_map/ppermute | solution.py:22
  7.0 18.5 %collective-permute-start.3 = (bf16[264,768]{1,0:T(8,128)(2,1)S(1)}, bf16[264,768]{1,0:T(8,128)(2,1)S(1)}, u32[]{:S(2)}, u32[]{:S(2)}) collective-permute-start(bf16[264,768]{1,0:T(8,128)(2,1)S(1)} %shard_map.83.refs_9_), channel_id=1, source_target_pairs={{0,4},{2,6},{4,0},{6,2},{8,12},{10,14},{12,8},{14,10},{1,5},{3,7},... | collective-permute-start | bytes 1216520 | tf_op jit(solution)/shard_map/ppermute | solution.py:22
  8.6 17.6 %collective-permute-start = (bf16[512,768]{1,0:T(8,128)(2,1)}, bf16[512,768]{1,0:T(8,128)(2,1)S(1)}, u32[]{:S(2)}, u32[]{:S(2)}) collective-permute-start(bf16[512,768]{1,0:T(8,128)(2,1)} %refs_0_.1), channel_id=1, source_target_pairs={{0,1},{1,0},{2,3},{3,2},{4,5},{5,4},{6,7},{7,6},{8,9},{9,8},{10,11... | collective-permute-start | bytes 2359304 | tf_op jit(solution)/shard_map/ppermute | solution.py:27
  8.6 1.1 %copy-start.1 = (bf16[512,768]{1,0:T(8,128)(2,1)S(1)}, bf16[512,768]{1,0:T(8,128)(2,1)}, u32[]{:S(2)}) copy-start(bf16[512,768]{1,0:T(8,128)(2,1)} %refs_0_.1) | copy-start | bytes 2359300
  9.8 0.7 %copy-start.4 = (f32[64]{0:T(128)S(1)}, f32[64]{0:T(128)}, u32[]{:S(2)}) copy-start(f32[64]{0:T(128)} %param.14) | copy-start | bytes 772
  11.1 0.7 %copy-start.3 = (s32[4]{0:T(128)S(1)}, s32[4]{0:T(128)}, u32[]{:S(2)}) copy-start(s32[4]{0:T(128)} %clusters_ref) | copy-start | bytes 52
  12.3 1.4 %collective-permute-start.4 = (s32[8,128]{1,0:T(8,128)S(1)}, s32[8,128]{1,0:T(8,128)S(1)}, u32[]{:S(2)}, u32[]{:S(2)}) collective-permute-start(s32[8,128]{1,0:T(8,128)S(1)} %shard_map.84.refs_5_), channel_id=1, source_target_pairs={{0,1},{1,0},{2,3},{3,2},{4,5},{5,4},{6,7},{7,6},{8,9},{9,8},{10,11... | collective-permute-start | bytes 12296 | tf_op jit(solution)/shard_map/ppermute | solution.py:27
  13.7 7.1 %collective-permute-start.5 = (s32[8,128]{1,0:T(8,128)S(1)}, s32[8,128]{1,0:T(8,128)S(1)}, u32[]{:S(2)}, u32[]{:S(2)}) collective-permute-start(s32[8,128]{1,0:T(8,128)S(1)} %shard_map.84.refs_5_), channel_id=1, source_target_pairs={{0,2},{2,0},{4,6},{6,4},{8,10},{10,8},{12,14},{14,12},{1,3},{3,1},... | collective-permute-start | bytes 12296 | tf_op jit(solution)/shard_map/ppermute | solution.py:27
  20.8 4.8 %collective-permute-start.6 = (s32[8,128]{1,0:T(8,128)S(1)}, s32[8,128]{1,0:T(8,128)S(1)}, u32[]{:S(2)}, u32[]{:S(2)}) collective-permute-start(s32[8,128]{1,0:T(8,128)S(1)} %shard_map.84.refs_5_), channel_id=1, source_target_pairs={{0,3},{1,2},{2,1},{3,0},{4,7},{5,6},{6,5},{7,4},{8,11},{9,10},{10,... | collective-permute-start | bytes 12296 | tf_op jit(solution)/shard_map/ppermute | solution.py:33
  25.0 10.2 %collective-permute-start.9 = (bf16[264,768]{1,0:T(8,128)(2,1)S(1)}, bf16[264,768]{1,0:T(8,128)(2,1)S(1)}, u32[]{:S(2)}, u32[]{:S(2)}) collective-permute-start(bf16[264,768]{1,0:T(8,128)(2,1)S(1)} %collective-permute-done.2.refs_10_), channel_id=1, source_target_pairs={{0,4},{2,6},{4,0},{6,2},{8,12},{10,14},{12,8},{14,10},{1,5},{3,7},... | collective-permute-start | bytes 1216520 | tf_op jit(solution)/shard_map/ppermute | solution.py:22
  25.6 1.8 %collective-permute-start.7 = (bf16[256,768]{1,0:T(8,128)(2,1)S(1)}, bf16[256,768]{1,0:T(8,128)(2,1)S(1)}, u32[]{:S(2)}, u32[]{:S(2)}) collective-permute-start(bf16[256,768]{1,0:T(8,128)(2,1)S(1)} %get-tuple-element.22), channel_id=1, source_target_pairs={{0,1},{1,0},{2,3},{3,2},{4,5},{5,4},{6,7},{7,6},{8,9},{9,8},{10,11... | collective-permute-start | bytes 1179656 | tf_op jit(solution)/shard_map/ppermute | solution.py:27
  25.7 2.3 %collective-permute-start.8 = (bf16[256,768]{1,0:T(8,128)(2,1)S(1)}, bf16[256,768]{1,0:T(8,128)(2,1)S(1)}, u32[]{:S(2)}, u32[]{:S(2)}) collective-permute-start(bf16[256,768]{1,0:T(8,128)(2,1)S(1)} %get-tuple-element.21), channel_id=1, source_target_pairs={{0,1},{1,0},{2,3},{3,2},{4,5},{5,4},{6,7},{7,6},{8,9},{9,8},{10,11... | collective-permute-start | bytes 1179656 | tf_op jit(solution)/shard_map/ppermute | solution.py:27
  28.0 10.8 %copy-start.5 = (s32[64]{0:T(128)S(1)}, s32[64]{0:T(128)}, u32[]{:S(2)}) copy-start(s32[64]{0:T(128)} %param.15) | copy-start | bytes 772
  36.9 2.1 %collective-permute-start.10 = (f32[4,128]{1,0:T(4,128)S(1)}, f32[4,128]{1,0:T(4,128)S(1)}, u32[]{:S(2)}, u32[]{:S(2)}) collective-permute-start(f32[4,128]{1,0:T(4,128)S(1)} %get-tuple-element.23), channel_id=1, source_target_pairs={{0,1},{1,0},{2,3},{3,2},{4,5},{5,4},{6,7},{7,6},{8,9},{9,8},{10,11... | collective-permute-start | bytes 6152 | tf_op jit(solution)/shard_map/ppermute | solution.py:27
  36.9 3.7 %collective-permute-start.11 = (f32[4,128]{1,0:T(4,128)S(1)}, f32[4,128]{1,0:T(4,128)S(1)}, u32[]{:S(2)}, u32[]{:S(2)}) collective-permute-start(f32[4,128]{1,0:T(4,128)S(1)} %get-tuple-element.25), channel_id=1, source_target_pairs={{0,2},{2,0},{4,6},{6,4},{8,10},{10,8},{12,14},{14,12},{1,3},{3,1},... | collective-permute-start | bytes 6152 | tf_op jit(solution)/shard_map/ppermute | solution.py:27
  37.8 3.0 %collective-permute-start.12 = (f32[4,128]{1,0:T(4,128)S(1)}, f32[4,128]{1,0:T(4,128)S(1)}, u32[]{:S(2)}, u32[]{:S(2)}) collective-permute-start(f32[4,128]{1,0:T(4,128)S(1)} %get-tuple-element.24), channel_id=1, source_target_pairs={{0,3},{1,2},{2,1},{3,0},{4,7},{5,6},{6,5},{7,4},{8,11},{9,10},{10,... | collective-permute-start | bytes 6152 | tf_op jit(solution)/shard_map/ppermute | solution.py:33

commit v21 on v19

--- a/solution.py
+++ b/solution.py
@@ -106,7 +106,7 @@
             entry = q_count + block
             cluster = info[source, block]
             beta = beta_ref[0, cluster]
-            slot_ref[entry] = source * qblocks + block
+            slot_ref[entry] = (0, 2, 1, 3)[source] * qblocks + block
             number_ref[3 * entry] = cluster.astype(jnp.float32)
             number_ref[3 * entry + 1] = beta * factor
             number_ref[3 * entry + 2] = beta * beta * (0.5 * LOG2E)
@@ -164,7 +164,7 @@
     lax.fori_loop(0, (q_count + wide - 1) // wide, query_blocks, 0)
 
 
-def last_kernel(chunks, wide, slot_ref, number_ref, qv, prev_ref, r_ref, out_ref):
+def last_kernel(chunks, wide, slot_ref, number_ref, qv, prev_ref, r_ref, keep_ref, give_ref, out_ref):
     height = chunks * LANES
     table = r_ref[pl.ds(height, TABLE), pl.ds(0, LANES)].astype(jnp.float32)
     ids = [table[c : c + 1, :] for c in range(chunks)]
@@ -188,6 +188,9 @@
                 acc = acc + jnp.exp2(part * scale + bias)
             row = pl.ds(slot_ref[entry], 1)
             out_ref[row, :] = out_ref[row, :] + jnp.sum(acc.T, axis=0, keepdims=True)
+    half = keep_ref.shape[0]
+    keep_ref[...] = out_ref[pl.ds(0, half), :]
+    give_ref[...] = out_ref[pl.ds(half, half), :]
 
 
 def first_call(chunks, qblocks, pieces, wide, given, payloads):
@@ -216,12 +219,14 @@
     )(*given, *payloads)
 
 
-def last_call(chunks, wide, slots, numbers, packed, totals, payload):
+def last_call(chunks, qblocks, wide, slots, numbers, packed, totals, payload):
+    half = jax.ShapeDtypeStruct((2 * qblocks, LANES), jnp.float32)
     return pl.pallas_call(
         functools.partial(last_kernel, chunks, wide),
-        out_shape=jax.ShapeDtypeStruct(totals.shape, jnp.float32),
+        out_shape=(half, half),
         in_specs=[SMEM] * 2 + [VMEM] * 3,
-        out_specs=VMEM,
+        out_specs=(VMEM, VMEM),
+        scratch_shapes=[pltpu.VMEM(totals.shape, jnp.float32)],
         compiler_params=PARAMS,
         cost_estimate=cost(1, 1),
     )(slots, numbers, packed, totals, payload)
@@ -294,10 +299,9 @@
 
     given = (beta, *queries, *q_tables)
     totals, packed, *plan = first_call(chunks, qblocks, pieces, 4, given, held[:-1])
-    totals = last_call(chunks, 4, *plan, packed, totals, held[-1])
-    totals = totals[: 4 * qblocks]
-    totals = totals.reshape(4, qblocks, LANES)
-    total = totals[0] + swap(totals[1], "helper") + swap(totals[2], "blk") + swap_both(totals[3])
+    keep, give = last_call(chunks, qblocks, 4, *plan, packed, totals, held[-1])
+    keep = keep + swap(give, "helper")
+    total = keep[:qblocks] + swap(keep, "blk")[qblocks:]
     columns = jnp.arange(cluster_member_count.shape[0], dtype=jnp.int32)
     onehot = query_block_cluster[:, None] == columns[None, :]
     sizes = jnp.sum(jnp.where(onehot, cluster_member_count[None, :], 0), axis=1)

time: 41.1 us -> 42 us (1.022)
  waiting for transfers between devices: 13.3 us -> 15.3 us
  starting transfers between devices: 15 us -> 13.8 us
    ppermute x8, waiting for transfers between devices: 11.3 us -> 13.6 us  [swap(): return lax.ppermute(value, axis, [(i, i ^ 1) for i in range(length)])]
    ppermute x2 -> x1, starting transfers between devices: 1.37 us -> 0.31 us  [swap_both(): return lax.ppermute(value, ('blk', 'helper'), pairs)]
    unnamed x12 -> x14, local copies, waits for them, and re-layouts: 3.12 us -> 3.12 us
  transfers between devices with their start and end apart: 13 -> 12, of which waited for: 8 -> 8; matrix products, arithmetic and copies ran while one was open for 1% -> 1% of each run, Pallas kernels for 13% -> 13%
where the time goes in v21:
time: 42 us; the launch traced here: 41.8 us
  waiting for transfers between devices  15.3 us (36%)
  starting transfers between devices  13.8 us (33%)
  Pallas kernels  7.2 us (17%)
  local copies, waits for them, and re-layouts  3.21 us (8%)
  between operations  1.4 us (3%)
  other arithmetic  0.85 us (2%)
    ppermute x8, waiting for transfers between devices, swap(): return lax.ppermute(value, axis, [(i, i ^ 1) for i in range(length)])  13.6 us
    ppermute x3, starting transfers between devices, trade(): return lax.ppermute(value, 'blk', [(i, i ^ mask) for i in range(length)])  8.11 us
    ppermute x8, starting transfers between devices, swap(): return lax.ppermute(value, axis, [(i, i ^ 1) for i in range(length)])  5.42 us
    pallas_call x1, Pallas kernels, first_call(): pl.pallas_call(functools.partial(first_kernel, chunks, qblocks, pieces, w...  4.88 us
    unnamed x14, local copies, waits for them, and re-layouts  3.12 us
    ppermute x3, waiting for transfers between devices, trade(): return lax.ppermute(value, 'blk', [(i, i ^ mask) for i in range(length)])  1.77 us
    pallas_call x1, Pallas kernels, last_call(): pl.pallas_call(functools.partial(last_kernel, chunks, wide), out_shape=(h...  1.69 us
  transfers between devices with their start and end apart: 12, of which 8 were waited for; matrix products, arithmetic and copies ran while one was open for 1% of the time, Pallas kernels for 13%

profile of v21, /device:TPU:0, one launch (start us, length us, event | category | flops | bytes accessed | tf_op | source)
XLA Modules:
  0.0 41.8 jit_solution(5052767363639498769)
XLA Ops:
  0.0 3.0 %collective-permute-start.1 = (bf16[512,768]{1,0:T(8,128)(2,1)}, bf16[512,768]{1,0:T(8,128)(2,1)S(1)}, u32[]{:S(2)}, u32[]{:S(2)}) collective-permute-start(bf16[512,768]{1,0:T(8,128)(2,1)} %refs_0_.1), channel_id=1, source_target_pairs={{0,2},{2,0},{4,6},{6,4},{8,10},{10,8},{12,14},{14,12},{1,3},{3,1},... | collective-permute-start | bytes 2359304 | tf_op jit(solution)/shard_map/ppermute | solution.py:27
  3.7 0.7 %copy-done.2 = s32[512]{0:T(512)S(1)} copy-done((s32[512]{0:T(512)S(1)}, s32[512]{0:T(512)}, u32[]{:S(2)}) %copy-start.2) | copy-done | bytes 2072
  4.4 3.7 %collective-permute-start.2 = (bf16[264,768]{1,0:T(8,128)(2,1)S(1)}, bf16[264,768]{1,0:T(8,128)(2,1)S(1)}, u32[]{:S(2)}, u32[]{:S(2)}) collective-permute-start(bf16[264,768]{1,0:T(8,128)(2,1)S(1)} %shard_map.83.refs_9_), channel_id=1, source_target_pairs={{0,12},{2,14},{4,8},{6,10},{8,4},{10,6},{12,0},{14,2},{1,13},{3,15... | collective-permute-start | bytes 1216520 | tf_op jit(solution)/shard_map/ppermute | solution.py:22
  8.1 1.1 %copy-done.1 = bf16[512,768]{1,0:T(8,128)(2,1)S(1)} copy-done((bf16[512,768]{1,0:T(8,128)(2,1)S(1)}, bf16[512,768]{1,0:T(8,128)(2,1)}, u32[]{:S(2)}) %copy-start.1) | copy-done | bytes 786456
  9.2 0.7 %copy-done.5 = f32[64]{0:T(128)S(1)} copy-done((f32[64]{0:T(128)S(1)}, f32[64]{0:T(128)}, u32[]{:S(2)}) %copy-start.5) | copy-done | bytes 280
  10.6 0.6 %copy-done.3 = s32[4]{0:T(128)S(1)} copy-done((s32[4]{0:T(128)S(1)}, s32[4]{0:T(128)}, u32[]{:S(2)}) %copy-start.3) | copy-done | bytes 40
  11.2 0.5 %shard_map.84.refs_5_ = s32[8,128]{1,0:T(8,128)S(1)} custom-call(s32[4]{0:T(128)S(1)} %copy-done.3, s32[1]{0:T(128)S(6)} %copy.12.count_ref), custom_call_target="tpu_custom_call" | custom-call | flops 1 | bytes 1 | tf_op jit(solution)/shard_map/pallas_call | solution.py:285
  11.8 0.6 %collective-permute-start.4 = (s32[8,128]{1,0:T(8,128)S(1)}, s32[8,128]{1,0:T(8,128)S(1)}, u32[]{:S(2)}, u32[]{:S(2)}) collective-permute-start(s32[8,128]{1,0:T(8,128)S(1)} %shard_map.84.refs_5_), channel_id=1, source_target_pairs={{0,1},{1,0},{2,3},{3,2},{4,5},{5,4},{6,7},{7,6},{8,9},{9,8},{10,11... | collective-permute-start | bytes 12296 | tf_op jit(solution)/shard_map/ppermute | solution.py:27
  12.3 0.8 %collective-permute-done.4.refs_6_ = s32[8,128]{1,0:T(8,128)S(1)} collective-permute-done((s32[8,128]{1,0:T(8,128)S(1)}, s32[8,128]{1,0:T(8,128)S(1)}, u32[]{:S(2)}, u32[]{:S(2)}) %collective-permute-start.4) | collective-permute-done | bytes 4128 | tf_op jit(solution)/shard_map/ppermute | solution.py:27
  13.2 0.5 %collective-permute-start.5 = (s32[8,128]{1,0:T(8,128)S(1)}, s32[8,128]{1,0:T(8,128)S(1)}, u32[]{:S(2)}, u32[]{:S(2)}) collective-permute-start(s32[8,128]{1,0:T(8,128)S(1)} %shard_map.84.refs_5_), channel_id=1, source_target_pairs={{0,2},{2,0},{4,6},{6,4},{8,10},{10,8},{12,14},{14,12},{1,3},{3,1},... | collective-permute-start | bytes 12296 | tf_op jit(solution)/shard_map/ppermute | solution.py:27
  13.7 7.1 %collective-permute-done.5.refs_7_ = s32[8,128]{1,0:T(8,128)S(1)} collective-permute-done((s32[8,128]{1,0:T(8,128)S(1)}, s32[8,128]{1,0:T(8,128)S(1)}, u32[]{:S(2)}, u32[]{:S(2)}) %collective-permute-start.5) | collective-permute-done | bytes 4128 | tf_op jit(solution)/shard_map/ppermute | solution.py:27
  20.8 0.3 collective-permute-start.6
  21.1 4.4 %collective-permute-start.9 = (bf16[264,768]{1,0:T(8,128)(2,1)S(1)}, bf16[264,768]{1,0:T(8,128)(2,1)S(1)}, u32[]{:S(2)}, u32[]{:S(2)}) collective-permute-start(bf16[264,768]{1,0:T(8,128)(2,1)S(1)} %collective-permute-done.2.refs_10_), channel_id=1, source_target_pairs={{0,4},{2,6},{4,0},{6,2},{8,12},{10,14},{12,8},{14,10},{1,5},{3,7},... | collective-permute-start | bytes 1216520 | tf_op jit(solution)/shard_map/ppermute | solution.py:22
  25.6 0.5 %collective-permute-done.3.refs_11_ = bf16[264,768]{1,0:T(8,128)(2,1)S(1)} collective-permute-done((bf16[264,768]{1,0:T(8,128)(2,1)S(1)}, bf16[264,768]{1,0:T(8,128)(2,1)S(1)}, u32[]{:S(2)}, u32[]{:S(2)}) %collective-permute-start.3) | collective-permute-done | bytes 405536 | tf_op jit(solution)/shard_map/ppermute | solution.py:22
  26.2 0.5 %collective-permute-start.8 = (bf16[256,768]{1,0:T(8,128)(2,1)S(1)}, bf16[256,768]{1,0:T(8,128)(2,1)S(1)}, u32[]{:S(2)}, u32[]{:S(2)}) collective-permute-start(bf16[256,768]{1,0:T(8,128)(2,1)S(1)} %get-tuple-element.25), channel_id=1, source_target_pairs={{0,1},{1,0},{2,3},{3,2},{4,5},{5,4},{6,7},{7,6},{8,9},{9,8},{10,11... | collective-permute-start | bytes 1179656 | tf_op jit(solution)/shard_map/ppermute | solution.py:27
  26.7 1.2 %collective-permute-done.7.refs_3_ = bf16[256,768]{1,0:T(8,128)(2,1)S(1)} collective-permute-done((bf16[256,768]{1,0:T(8,128)(2,1)S(1)}, bf16[256,768]{1,0:T(8,128)(2,1)S(1)}, u32[]{:S(2)}, u32[]{:S(2)}) %collective-permute-start.7) | collective-permute-done | bytes 393248 | tf_op jit(solution)/shard_map/ppermute | solution.py:27
  27.9 0.6 %collective-permute-done.8.refs_4_ = bf16[256,768]{1,0:T(8,128)(2,1)S(1)} collective-permute-done((bf16[256,768]{1,0:T(8,128)(2,1)S(1)}, bf16[256,768]{1,0:T(8,128)(2,1)S(1)}, u32[]{:S(2)}, u32[]{:S(2)}) %collective-permute-start.8) | collective-permute-done | bytes 393248 | tf_op jit(solution)/shard_map/ppermute | solution.py:27
  28.5 4.9 %shard_map.85 = (f32[24,128]{1,0:T(8,128)S(1)}, bf16[2048,768]{1,0:T(8,128)(2,1)S(1)}, s32[24]{0:T(128)S(1)}, f32[48]{0:T(128)S(1)}) custom-call(f32[1,64]{1,0:T(1,128)S(1)} %get-tuple-element.15.beta_ref, bf16[512,768]{1,0:T(8,128)(2,1)S(1)} %get-tuple-element.16.refs_0_, bf16[512,768]{1,0:T(8,128)(2,1)S(1)} %collective-permute-done.refs_1_, ...), custom_call_target="tpu_custom_call" | custom-call | flops 1 | bytes 1 | tf_op jit(solution)/shard_map/pallas_call | solution.py:200
  33.3 1.3 %collective-permute-done.9.r_ref = bf16[264,768]{1,0:T(8,128)(2,1)S(1)} collective-permute-done((bf16[264,768]{1,0:T(8,128)(2,1)S(1)}, bf16[264,768]{1,0:T(8,128)(2,1)S(1)}, u32[]{:S(2)}, u32[]{:S(2)}) %collective-permute-start.9) | collective-permute-done | bytes 405536 | tf_op jit(solution)/shard_map/ppermute | solution.py:22
  34.6 1.7 %shard_map.86 = (f32[8,128]{1,0:T(8,128)S(1)}, f32[8,128]{1,0:T(8,128)S(1)}) custom-call(s32[24]{0:T(128)S(1)} %get-tuple-element.19.slot_ref, f32[48]{0:T(128)S(1)} %get-tuple-element.20.number_ref, bf16[2048,768]{1,0:T(8,128)(2,1)S(1)} %get-tuple-element.21.qv, f32[24,128]{1,0:T(8,128)S(1)} %get-tuple-element.22.prev_ref, ...), custom_call_target="tpu_custom_call" | custom-call | flops 1 | bytes 1 | tf_op jit(solution)/shard_map/pallas_call | solution.py:224
  36.4 1.2 %collective-permute-done.10 = f32[8,128]{1,0:T(8,128)S(1)} collective-permute-done((f32[8,128]{1,0:T(8,128)S(1)}, f32[8,128]{1,0:T(8,128)S(1)}, u32[]{:S(2)}, u32[]{:S(2)}) %collective-permute-start.10) | collective-permute-done | bytes 4128 | tf_op jit(solution)/shard_map/ppermute | solution.py:27
  37.6 0.7 %collective-permute-start.11 = (f32[8,128]{1,0:T(8,128)S(1)}, f32[8,128]{1,0:T(8,128)S(1)}, u32[]{:S(2)}, u32[]{:S(2)}) collective-permute-start(f32[8,128]{1,0:T(8,128)S(1)} %add.11), channel_id=1, source_target_pairs={{0,2},{2,0},{4,6},{6,4},{8,10},{10,8},{12,14},{14,12},{1,3},{3,1},... | collective-permute-start | bytes 12296 | tf_op jit(solution)/shard_map/ppermute | solution.py:27
  38.5 2.7 %collective-permute-done.11 = f32[8,128]{1,0:T(8,128)S(1)} collective-permute-done((f32[8,128]{1,0:T(8,128)S(1)}, f32[8,128]{1,0:T(8,128)S(1)}, u32[]{:S(2)}, u32[]{:S(2)}) %collective-permute-start.11) | collective-permute-done | bytes 4128 | tf_op jit(solution)/shard_map/ppermute | solution.py:27
  41.2 0.7 %log-plus-one_bitcast_fusion = f32[512]{0:T(512)} fusion(f32[8,128]{1,0:T(8,128)S(1)} %collective-permute-done.11, f32[8,128]{1,0:T(8,128)S(1)} %add.11, f32[4]{0:T(128)S(1)} %convert_element_type.7), kind=kLoop, calls=%fused_computation | loop fusion | flops 1024 | bytes 6160 | tf_op jit(solution)/shard_map/reshape | solution.py:309
  (25 shorter events, 0.5 us)
Async XLA Ops:
  0.0 3.6 %copy-start = (bf16[512,768]{1,0:T(8,128)(2,1)S(1)}, bf16[512,768]{1,0:T(8,128)(2,1)}, u32[]{:S(2)}) copy-start(bf16[512,768]{1,0:T(8,128)(2,1)} %param.11) | copy-start | bytes 2359300
  0.0 26.0 %collective-permute-start.1 = (bf16[512,768]{1,0:T(8,128)(2,1)}, bf16[512,768]{1,0:T(8,128)(2,1)S(1)}, u32[]{:S(2)}, u32[]{:S(2)}) collective-permute-start(bf16[512,768]{1,0:T(8,128)(2,1)} %refs_0_.1), channel_id=1, source_target_pairs={{0,2},{2,0},{4,6},{6,4},{8,10},{10,8},{12,14},{14,12},{1,3},{3,1},... | collective-permute-start | bytes 2359304 | tf_op jit(solution)/shard_map/ppermute | solution.py:27
  3.7 0.7 %copy-start.2 = (s32[512]{0:T(512)S(1)}, s32[512]{0:T(512)}, u32[]{:S(2)}) copy-start(s32[512]{0:T(512)} %param.12) | copy-start | bytes 6148
  4.4 16.7 %collective-permute-start.2 = (bf16[264,768]{1,0:T(8,128)(2,1)S(1)}, bf16[264,768]{1,0:T(8,128)(2,1)S(1)}, u32[]{:S(2)}, u32[]{:S(2)}) collective-permute-start(bf16[264,768]{1,0:T(8,128)(2,1)S(1)} %shard_map.83.refs_9_), channel_id=1, source_target_pairs={{0,12},{2,14},{4,8},{6,10},{8,4},{10,6},{12,0},{14,2},{1,13},{3,15... | collective-permute-start | bytes 1216520 | tf_op jit(solution)/shard_map/ppermute | solution.py:22
  8.1 18.0 %collective-permute-start.3 = (bf16[264,768]{1,0:T(8,128)(2,1)S(1)}, bf16[264,768]{1,0:T(8,128)(2,1)S(1)}, u32[]{:S(2)}, u32[]{:S(2)}) collective-permute-start(bf16[264,768]{1,0:T(8,128)(2,1)S(1)} %shard_map.83.refs_9_), channel_id=1, source_target_pairs={{0,4},{2,6},{4,0},{6,2},{8,12},{10,14},{12,8},{14,10},{1,5},{3,7},... | collective-permute-start | bytes 1216520 | tf_op jit(solution)/shard_map/ppermute | solution.py:22
  8.1 18.6 %collective-permute-start = (bf16[512,768]{1,0:T(8,128)(2,1)}, bf16[512,768]{1,0:T(8,128)(2,1)S(1)}, u32[]{:S(2)}, u32[]{:S(2)}) collective-permute-start(bf16[512,768]{1,0:T(8,128)(2,1)} %refs_0_.1), channel_id=1, source_target_pairs={{0,1},{1,0},{2,3},{3,2},{4,5},{5,4},{6,7},{7,6},{8,9},{9,8},{10,11... | collective-permute-start | bytes 2359304 | tf_op jit(solution)/shard_map/ppermute | solution.py:27
  8.1 1.1 %copy-start.1 = (bf16[512,768]{1,0:T(8,128)(2,1)S(1)}, bf16[512,768]{1,0:T(8,128)(2,1)}, u32[]{:S(2)}) copy-start(bf16[512,768]{1,0:T(8,128)(2,1)} %refs_0_.1) | copy-start | bytes 2359300
  9.2 0.7 %copy-start.5 = (f32[64]{0:T(128)S(1)}, f32[64]{0:T(128)}, u32[]{:S(2)}) copy-start(f32[64]{0:T(128)} %param.14) | copy-start | bytes 772
  10.6 0.7 %copy-start.3 = (s32[4]{0:T(128)S(1)}, s32[4]{0:T(128)}, u32[]{:S(2)}) copy-start(s32[4]{0:T(128)} %clusters_ref) | copy-start | bytes 52
  11.8 1.4 %collective-permute-start.4 = (s32[8,128]{1,0:T(8,128)S(1)}, s32[8,128]{1,0:T(8,128)S(1)}, u32[]{:S(2)}, u32[]{:S(2)}) collective-permute-start(s32[8,128]{1,0:T(8,128)S(1)} %shard_map.84.refs_5_), channel_id=1, source_target_pairs={{0,1},{1,0},{2,3},{3,2},{4,5},{5,4},{6,7},{7,6},{8,9},{9,8},{10,11... | collective-permute-start | bytes 12296 | tf_op jit(solution)/shard_map/ppermute | solution.py:27
  13.2 7.6 %collective-permute-start.5 = (s32[8,128]{1,0:T(8,128)S(1)}, s32[8,128]{1,0:T(8,128)S(1)}, u32[]{:S(2)}, u32[]{:S(2)}) collective-permute-start(s32[8,128]{1,0:T(8,128)S(1)} %shard_map.84.refs_5_), channel_id=1, source_target_pairs={{0,2},{2,0},{4,6},{6,4},{8,10},{10,8},{12,14},{14,12},{1,3},{3,1},... | collective-permute-start | bytes 12296 | tf_op jit(solution)/shard_map/ppermute | solution.py:27
  20.8 4.8 %collective-permute-start.6 = (s32[8,128]{1,0:T(8,128)S(1)}, s32[8,128]{1,0:T(8,128)S(1)}, u32[]{:S(2)}, u32[]{:S(2)}) collective-permute-start(s32[8,128]{1,0:T(8,128)S(1)} %shard_map.84.refs_5_), channel_id=1, source_target_pairs={{0,3},{1,2},{2,1},{3,0},{4,7},{5,6},{6,5},{7,4},{8,11},{9,10},{10,... | collective-permute-start | bytes 12296 | tf_op jit(solution)/shard_map/ppermute | solution.py:33
  21.1 13.5 %collective-permute-start.9 = (bf16[264,768]{1,0:T(8,128)(2,1)S(1)}, bf16[264,768]{1,0:T(8,128)(2,1)S(1)}, u32[]{:S(2)}, u32[]{:S(2)}) collective-permute-start(bf16[264,768]{1,0:T(8,128)(2,1)S(1)} %collective-permute-done.2.refs_10_), channel_id=1, source_target_pairs={{0,4},{2,6},{4,0},{6,2},{8,12},{10,14},{12,8},{14,10},{1,5},{3,7},... | collective-permute-start | bytes 1216520 | tf_op jit(solution)/shard_map/ppermute | solution.py:22
  26.1 1.8 %collective-permute-start.7 = (bf16[256,768]{1,0:T(8,128)(2,1)S(1)}, bf16[256,768]{1,0:T(8,128)(2,1)S(1)}, u32[]{:S(2)}, u32[]{:S(2)}) collective-permute-start(bf16[256,768]{1,0:T(8,128)(2,1)S(1)} %get-tuple-element.26), channel_id=1, source_target_pairs={{0,1},{1,0},{2,3},{3,2},{4,5},{5,4},{6,7},{7,6},{8,9},{9,8},{10,11... | collective-permute-start | bytes 1179656 | tf_op jit(solution)/shard_map/ppermute | solution.py:27
  26.2 2.3 %collective-permute-start.8 = (bf16[256,768]{1,0:T(8,128)(2,1)S(1)}, bf16[256,768]{1,0:T(8,128)(2,1)S(1)}, u32[]{:S(2)}, u32[]{:S(2)}) collective-permute-start(bf16[256,768]{1,0:T(8,128)(2,1)S(1)} %get-tuple-element.25), channel_id=1, source_target_pairs={{0,1},{1,0},{2,3},{3,2},{4,5},{5,4},{6,7},{7,6},{8,9},{9,8},{10,11... | collective-permute-start | bytes 1179656 | tf_op jit(solution)/shard_map/ppermute | solution.py:27
  28.5 9.9 %copy-start.4 = (s32[4]{0:T(128)S(1)}, s32[4]{0:T(128)}, u32[]{:S(2)}) copy-start(s32[4]{0:T(128)} %clusters_ref) | copy-start | bytes 52
  28.5 9.9 %copy-start.6 = (s32[64]{0:T(128)S(1)}, s32[64]{0:T(128)}, u32[]{:S(2)}) copy-start(s32[64]{0:T(128)} %param.15) | copy-start | bytes 772
  36.3 1.2 %collective-permute-start.10 = (f32[8,128]{1,0:T(8,128)S(1)}, f32[8,128]{1,0:T(8,128)S(1)}, u32[]{:S(2)}, u32[]{:S(2)}) collective-permute-start(f32[8,128]{1,0:T(8,128)S(1)} %get-tuple-element.24), channel_id=1, source_target_pairs={{0,1},{1,0},{2,3},{3,2},{4,5},{5,4},{6,7},{7,6},{8,9},{9,8},{10,11... | collective-permute-start | bytes 12296 | tf_op jit(solution)/shard_map/ppermute | solution.py:27
  37.6 3.6 %collective-permute-start.11 = (f32[8,128]{1,0:T(8,128)S(1)}, f32[8,128]{1,0:T(8,128)S(1)}, u32[]{:S(2)}, u32[]{:S(2)}) collective-permute-start(f32[8,128]{1,0:T(8,128)S(1)} %add.11), channel_id=1, source_target_pairs={{0,2},{2,0},{4,6},{6,4},{8,10},{10,8},{12,14},{14,12},{1,3},{3,1},... | collective-permute-start | bytes 12296 | tf_op jit(solution)/shard_map/ppermute | solution.py:27

commit v22 on v19

--- a/solution.py
+++ b/solution.py
@@ -9,7 +9,7 @@
 from jax.sharding import PartitionSpec as P
 
 LANES = 128
-TABLE = 8
+TABLE = 16
 LOG2E = 1.4426950408889634
 DEAD = -1.0e30
 SMEM = pl.BlockSpec(memory_space=pltpu.SMEM)

time: 41.1 us -> 41.9 us (1.019)
  waiting for transfers between devices: 13.3 us -> 14.4 us
  Pallas kernels: 7.18 us -> 6.28 us
  starting transfers between devices: 15 us -> 15.5 us
    ppermute x3, waiting for transfers between devices: 1.79 us -> 2.97 us  [trade(): return lax.ppermute(value, 'blk', [(i, i ^ mask) for i in range(length)])]
    pallas_call x1, Pallas kernels: 4.86 us -> 3.94 us  [first_call(): pl.pallas_call(functools.partial(first_kernel, chunks, qblocks, pieces, w...]
    ppermute x3, starting transfers between devices: 8.11 us -> 8.64 us  [trade(): return lax.ppermute(value, 'blk', [(i, i ^ mask) for i in range(length)])]
    unnamed x12 -> x14, local copies, waits for them, and re-layouts: 3.12 us -> 3.12 us
  transfers between devices with their start and end apart: 13 -> 13, of which waited for: 8 -> 8; matrix products, arithmetic and copies ran while one was open for 1% -> 1% of each run, Pallas kernels for 13% -> 11%
where the time goes in v22:
time: 41.9 us; the launch traced here: 41.7 us
  starting transfers between devices  15.5 us (37%)
  waiting for transfers between devices  14.4 us (34%)
  Pallas kernels  6.28 us (15%)
  local copies, waits for them, and re-layouts  3.22 us (8%)
  between operations  1.41 us (3%)
  other arithmetic  0.85 us (2%)
    ppermute x8, waiting for transfers between devices, swap(): return lax.ppermute(value, axis, [(i, i ^ 1) for i in range(length)])  11.3 us
    ppermute x3, starting transfers between devices, trade(): return lax.ppermute(value, 'blk', [(i, i ^ mask) for i in range(length)])  8.64 us
    ppermute x8, starting transfers between devices, swap(): return lax.ppermute(value, axis, [(i, i ^ 1) for i in range(length)])  5.48 us
    pallas_call x1, Pallas kernels, first_call(): pl.pallas_call(functools.partial(first_kernel, chunks, qblocks, pieces, w...  3.94 us
    unnamed x14, local copies, waits for them, and re-layouts  3.12 us
    ppermute x3, waiting for transfers between devices, trade(): return lax.ppermute(value, 'blk', [(i, i ^ mask) for i in range(length)])  2.97 us
    pallas_call x1, Pallas kernels, last_call(): pl.pallas_call(functools.partial(last_kernel, chunks, wide), out_shape=ja...  1.71 us
    ppermute x2, starting transfers between devices, swap_both(): return lax.ppermute(value, ('blk', 'helper'), pairs)  1.38 us
  transfers between devices with their start and end apart: 13, of which 8 were waited for; matrix products, arithmetic and copies ran while one was open for 1% of the time, Pallas kernels for 11%

profile of v22, /device:TPU:0, one launch (start us, length us, event | category | flops | bytes accessed | tf_op | source)
XLA Modules:
  0.0 41.7 jit_solution(11449515467795132040)
XLA Ops:
  0.0 3.0 %collective-permute-start.1 = (bf16[512,768]{1,0:T(8,128)(2,1)}, bf16[512,768]{1,0:T(8,128)(2,1)S(1)}, u32[]{:S(2)}, u32[]{:S(2)}) collective-permute-start(bf16[512,768]{1,0:T(8,128)(2,1)} %refs_0_.1), channel_id=1, source_target_pairs={{0,2},{2,0},{4,6},{6,4},{8,10},{10,8},{12,14},{14,12},{1,3},{3,1},... | collective-permute-start | bytes 2359304 | tf_op jit(solution)/shard_map/ppermute | solution.py:27
  3.7 0.7 %copy-done.2 = s32[512]{0:T(512)S(1)} copy-done((s32[512]{0:T(512)S(1)}, s32[512]{0:T(512)}, u32[]{:S(2)}) %copy-start.2) | copy-done | bytes 2072
  4.4 3.7 %collective-permute-start.2 = (bf16[272,768]{1,0:T(8,128)(2,1)S(1)}, bf16[272,768]{1,0:T(8,128)(2,1)S(1)}, u32[]{:S(2)}, u32[]{:S(2)}) collective-permute-start(bf16[272,768]{1,0:T(8,128)(2,1)S(1)} %shard_map.83.refs_9_), channel_id=1, source_target_pairs={{0,12},{2,14},{4,8},{6,10},{8,4},{10,6},{12,0},{14,2},{1,13},{3,15... | collective-permute-start | bytes 1253384 | tf_op jit(solution)/shard_map/ppermute | solution.py:22
  8.1 1.1 %copy-done.1 = bf16[512,768]{1,0:T(8,128)(2,1)S(1)} copy-done((bf16[512,768]{1,0:T(8,128)(2,1)S(1)}, bf16[512,768]{1,0:T(8,128)(2,1)}, u32[]{:S(2)}) %copy-start.1) | copy-done | bytes 786456
  9.2 0.7 %copy-done.5 = f32[64]{0:T(128)S(1)} copy-done((f32[64]{0:T(128)S(1)}, f32[64]{0:T(128)}, u32[]{:S(2)}) %copy-start.5) | copy-done | bytes 280
  10.6 0.6 %copy-done.3 = s32[4]{0:T(128)S(1)} copy-done((s32[4]{0:T(128)S(1)}, s32[4]{0:T(128)}, u32[]{:S(2)}) %copy-start.3) | copy-done | bytes 40
  11.2 0.5 %shard_map.84.refs_5_ = s32[8,128]{1,0:T(8,128)S(1)} custom-call(s32[4]{0:T(128)S(1)} %copy-done.3, s32[1]{0:T(128)S(6)} %copy.12.count_ref), custom_call_target="tpu_custom_call" | custom-call | flops 1 | bytes 1 | tf_op jit(solution)/shard_map/pallas_call | solution.py:280
  11.8 0.6 %collective-permute-start.4 = (s32[8,128]{1,0:T(8,128)S(1)}, s32[8,128]{1,0:T(8,128)S(1)}, u32[]{:S(2)}, u32[]{:S(2)}) collective-permute-start(s32[8,128]{1,0:T(8,128)S(1)} %shard_map.84.refs_5_), channel_id=1, source_target_pairs={{0,1},{1,0},{2,3},{3,2},{4,5},{5,4},{6,7},{7,6},{8,9},{9,8},{10,11... | collective-permute-start | bytes 12296 | tf_op jit(solution)/shard_map/ppermute | solution.py:27
  12.3 0.8 %collective-permute-done.4.refs_6_ = s32[8,128]{1,0:T(8,128)S(1)} collective-permute-done((s32[8,128]{1,0:T(8,128)S(1)}, s32[8,128]{1,0:T(8,128)S(1)}, u32[]{:S(2)}, u32[]{:S(2)}) %collective-permute-start.4) | collective-permute-done | bytes 4128 | tf_op jit(solution)/shard_map/ppermute | solution.py:27
  13.2 0.5 %collective-permute-start.5 = (s32[8,128]{1,0:T(8,128)S(1)}, s32[8,128]{1,0:T(8,128)S(1)}, u32[]{:S(2)}, u32[]{:S(2)}) collective-permute-start(s32[8,128]{1,0:T(8,128)S(1)} %shard_map.84.refs_5_), channel_id=1, source_target_pairs={{0,2},{2,0},{4,6},{6,4},{8,10},{10,8},{12,14},{14,12},{1,3},{3,1},... | collective-permute-start | bytes 12296 | tf_op jit(solution)/shard_map/ppermute | solution.py:27
  13.7 7.1 %collective-permute-done.5.refs_7_ = s32[8,128]{1,0:T(8,128)S(1)} collective-permute-done((s32[8,128]{1,0:T(8,128)S(1)}, s32[8,128]{1,0:T(8,128)S(1)}, u32[]{:S(2)}, u32[]{:S(2)}) %collective-permute-start.5) | collective-permute-done | bytes 4128 | tf_op jit(solution)/shard_map/ppermute | solution.py:27
  20.8 0.3 collective-permute-start.6
  21.1 5.0 %collective-permute-start.9 = (bf16[272,768]{1,0:T(8,128)(2,1)S(1)}, bf16[272,768]{1,0:T(8,128)(2,1)S(1)}, u32[]{:S(2)}, u32[]{:S(2)}) collective-permute-start(bf16[272,768]{1,0:T(8,128)(2,1)S(1)} %collective-permute-done.2.refs_10_), channel_id=1, source_target_pairs={{0,4},{2,6},{4,0},{6,2},{8,12},{10,14},{12,8},{14,10},{1,5},{3,7},... | collective-permute-start | bytes 1253384 | tf_op jit(solution)/shard_map/ppermute | solution.py:22
  26.1 0.5 %collective-permute-done.3.refs_11_ = bf16[272,768]{1,0:T(8,128)(2,1)S(1)} collective-permute-done((bf16[272,768]{1,0:T(8,128)(2,1)S(1)}, bf16[272,768]{1,0:T(8,128)(2,1)S(1)}, u32[]{:S(2)}, u32[]{:S(2)}) %collective-permute-start.3) | collective-permute-done | bytes 417824 | tf_op jit(solution)/shard_map/ppermute | solution.py:22
  26.7 0.5 %collective-permute-start.8 = (bf16[256,768]{1,0:T(8,128)(2,1)S(1)}, bf16[256,768]{1,0:T(8,128)(2,1)S(1)}, u32[]{:S(2)}, u32[]{:S(2)}) collective-permute-start(bf16[256,768]{1,0:T(8,128)(2,1)S(1)} %get-tuple-element.21), channel_id=1, source_target_pairs={{0,1},{1,0},{2,3},{3,2},{4,5},{5,4},{6,7},{7,6},{8,9},{9,8},{10,11... | collective-permute-start | bytes 1179656 | tf_op jit(solution)/shard_map/ppermute | solution.py:27
  27.2 1.2 %collective-permute-done.7.refs_3_ = bf16[256,768]{1,0:T(8,128)(2,1)S(1)} collective-permute-done((bf16[256,768]{1,0:T(8,128)(2,1)S(1)}, bf16[256,768]{1,0:T(8,128)(2,1)S(1)}, u32[]{:S(2)}, u32[]{:S(2)}) %collective-permute-start.7) | collective-permute-done | bytes 393248 | tf_op jit(solution)/shard_map/ppermute | solution.py:27
  28.4 0.6 %collective-permute-done.8.refs_4_ = bf16[256,768]{1,0:T(8,128)(2,1)S(1)} collective-permute-done((bf16[256,768]{1,0:T(8,128)(2,1)S(1)}, bf16[256,768]{1,0:T(8,128)(2,1)S(1)}, u32[]{:S(2)}, u32[]{:S(2)}) %collective-permute-start.8) | collective-permute-done | bytes 393248 | tf_op jit(solution)/shard_map/ppermute | solution.py:27
  29.0 3.9 %shard_map.85 = (f32[24,128]{1,0:T(8,128)S(1)}, bf16[2048,768]{1,0:T(8,128)(2,1)S(1)}, s32[24]{0:T(128)S(1)}, f32[48]{0:T(128)S(1)}) custom-call(f32[1,64]{1,0:T(1,128)S(1)} %get-tuple-element.13.beta_ref, bf16[512,768]{1,0:T(8,128)(2,1)S(1)} %get-tuple-element.14.refs_0_, bf16[512,768]{1,0:T(8,128)(2,1)S(1)} %collective-permute-done.refs_1_, ...), custom_call_target="tpu_custom_call" | custom-call | flops 1 | bytes 1 | tf_op jit(solution)/shard_map/pallas_call | solution.py:197
  32.9 2.5 %collective-permute-done.9.r_ref = bf16[272,768]{1,0:T(8,128)(2,1)S(1)} collective-permute-done((bf16[272,768]{1,0:T(8,128)(2,1)S(1)}, bf16[272,768]{1,0:T(8,128)(2,1)S(1)}, u32[]{:S(2)}, u32[]{:S(2)}) %collective-permute-start.9) | collective-permute-done | bytes 417824 | tf_op jit(solution)/shard_map/ppermute | solution.py:22
  35.4 1.7 %shard_map.86 = f32[24,128]{1,0:T(8,128)S(1)} custom-call(s32[24]{0:T(128)S(1)} %get-tuple-element.17.slot_ref, f32[48]{0:T(128)S(1)} %get-tuple-element.18.number_ref, bf16[2048,768]{1,0:T(8,128)(2,1)S(1)} %get-tuple-element.19.qv, f32[24,128]{1,0:T(8,128)S(1)} %get-tuple-element.20.prev_ref, bf16[272,768]{1,0:T(8,128)(2,1)S(1)} %collective-permute-done.9.r_ref), custom_call_target="tpu_custom_call" | custom-call | flops 1 | bytes 1 | tf_op jit(solution)/shard_map/pallas_call | solution.py:220
  37.2 0.8 %collective-permute-start.11 = (f32[4,128]{1,0:T(4,128)S(1)}, f32[4,128]{1,0:T(4,128)S(1)}, u32[]{:S(2)}, u32[]{:S(2)}) collective-permute-start(f32[4,128]{1,0:T(4,128)S(1)} %get-tuple-element.25), channel_id=1, source_target_pairs={{0,2},{2,0},{4,6},{6,4},{8,10},{10,8},{12,14},{14,12},{1,3},{3,1},... | collective-permute-start | bytes 6152 | tf_op jit(solution)/shard_map/ppermute | solution.py:27
  38.0 1.1 %collective-permute-start.12 = (f32[4,128]{1,0:T(4,128)S(1)}, f32[4,128]{1,0:T(4,128)S(1)}, u32[]{:S(2)}, u32[]{:S(2)}) collective-permute-start(f32[4,128]{1,0:T(4,128)S(1)} %get-tuple-element.24), channel_id=1, source_target_pairs={{0,3},{1,2},{2,1},{3,0},{4,7},{5,6},{6,5},{7,4},{8,11},{9,10},{10,... | collective-permute-start | bytes 6152 | tf_op jit(solution)/shard_map/ppermute | solution.py:33
  39.3 1.6 %collective-permute-done.11 = f32[4,128]{1,0:T(4,128)S(1)} collective-permute-done((f32[4,128]{1,0:T(4,128)S(1)}, f32[4,128]{1,0:T(4,128)S(1)}, u32[]{:S(2)}, u32[]{:S(2)}) %collective-permute-start.11) | collective-permute-done | bytes 2080 | tf_op jit(solution)/shard_map/ppermute | solution.py:27
  41.0 0.7 %log-plus-one_bitcast_fusion = f32[512]{0:T(512)} fusion(f32[4,128]{1,0:T(4,128)S(1)} %collective-permute-done.12, f32[4,128]{1,0:T(4,128)S(1)} %collective-permute-done.11, f32[4,128]{1,0:T(4,128)S(1)} %collective-permute-done.10, f32[24,128]{1,0:T(8,128)S(1)} %shard_map.86, f32[4]{0:T(128)S(1)} %convert_element_type.7), kind=kLoop, calls=%fused_computation.4 | loop fusion | flops 2048 | bytes 10256 | tf_op jit(solution)/shard_map/reshape | solution.py:305
  (27 shorter events, 0.7 us)
Async XLA Ops:
  0.0 3.6 %copy-start = (bf16[512,768]{1,0:T(8,128)(2,1)S(1)}, bf16[512,768]{1,0:T(8,128)(2,1)}, u32[]{:S(2)}) copy-start(bf16[512,768]{1,0:T(8,128)(2,1)} %param.11) | copy-start | bytes 2359300
  0.0 26.6 %collective-permute-start.1 = (bf16[512,768]{1,0:T(8,128)(2,1)}, bf16[512,768]{1,0:T(8,128)(2,1)S(1)}, u32[]{:S(2)}, u32[]{:S(2)}) collective-permute-start(bf16[512,768]{1,0:T(8,128)(2,1)} %refs_0_.1), channel_id=1, source_target_pairs={{0,2},{2,0},{4,6},{6,4},{8,10},{10,8},{12,14},{14,12},{1,3},{3,1},... | collective-permute-start | bytes 2359304 | tf_op jit(solution)/shard_map/ppermute | solution.py:27
  3.7 0.7 %copy-start.2 = (s32[512]{0:T(512)S(1)}, s32[512]{0:T(512)}, u32[]{:S(2)}) copy-start(s32[512]{0:T(512)} %param.12) | copy-start | bytes 6148
  4.4 16.7 %collective-permute-start.2 = (bf16[272,768]{1,0:T(8,128)(2,1)S(1)}, bf16[272,768]{1,0:T(8,128)(2,1)S(1)}, u32[]{:S(2)}, u32[]{:S(2)}) collective-permute-start(bf16[272,768]{1,0:T(8,128)(2,1)S(1)} %shard_map.83.refs_9_), channel_id=1, source_target_pairs={{0,12},{2,14},{4,8},{6,10},{8,4},{10,6},{12,0},{14,2},{1,13},{3,15... | collective-permute-start | bytes 1253384 | tf_op jit(solution)/shard_map/ppermute | solution.py:22
  8.1 18.5 %collective-permute-start.3 = (bf16[272,768]{1,0:T(8,128)(2,1)S(1)}, bf16[272,768]{1,0:T(8,128)(2,1)S(1)}, u32[]{:S(2)}, u32[]{:S(2)}) collective-permute-start(bf16[272,768]{1,0:T(8,128)(2,1)S(1)} %shard_map.83.refs_9_), channel_id=1, source_target_pairs={{0,4},{2,6},{4,0},{6,2},{8,12},{10,14},{12,8},{14,10},{1,5},{3,7},... | collective-permute-start | bytes 1253384 | tf_op jit(solution)/shard_map/ppermute | solution.py:22
  8.1 19.1 %collective-permute-start = (bf16[512,768]{1,0:T(8,128)(2,1)}, bf16[512,768]{1,0:T(8,128)(2,1)S(1)}, u32[]{:S(2)}, u32[]{:S(2)}) collective-permute-start(bf16[512,768]{1,0:T(8,128)(2,1)} %refs_0_.1), channel_id=1, source_target_pairs={{0,1},{1,0},{2,3},{3,2},{4,5},{5,4},{6,7},{7,6},{8,9},{9,8},{10,11... | collective-permute-start | bytes 2359304 | tf_op jit(solution)/shard_map/ppermute | solution.py:27
  8.1 1.1 %copy-start.1 = (bf16[512,768]{1,0:T(8,128)(2,1)S(1)}, bf16[512,768]{1,0:T(8,128)(2,1)}, u32[]{:S(2)}) copy-start(bf16[512,768]{1,0:T(8,128)(2,1)} %refs_0_.1) | copy-start | bytes 2359300
  9.2 0.7 %copy-start.5 = (f32[64]{0:T(128)S(1)}, f32[64]{0:T(128)}, u32[]{:S(2)}) copy-start(f32[64]{0:T(128)} %param.14) | copy-start | bytes 772
  10.6 0.7 %copy-start.3 = (s32[4]{0:T(128)S(1)}, s32[4]{0:T(128)}, u32[]{:S(2)}) copy-start(s32[4]{0:T(128)} %clusters_ref) | copy-start | bytes 52
  11.8 1.4 %collective-permute-start.4 = (s32[8,128]{1,0:T(8,128)S(1)}, s32[8,128]{1,0:T(8,128)S(1)}, u32[]{:S(2)}, u32[]{:S(2)}) collective-permute-start(s32[8,128]{1,0:T(8,128)S(1)} %shard_map.84.refs_5_), channel_id=1, source_target_pairs={{0,1},{1,0},{2,3},{3,2},{4,5},{5,4},{6,7},{7,6},{8,9},{9,8},{10,11... | collective-permute-start | bytes 12296 | tf_op jit(solution)/shard_map/ppermute | solution.py:27
  13.2 7.6 %collective-permute-start.5 = (s32[8,128]{1,0:T(8,128)S(1)}, s32[8,128]{1,0:T(8,128)S(1)}, u32[]{:S(2)}, u32[]{:S(2)}) collective-permute-start(s32[8,128]{1,0:T(8,128)S(1)} %shard_map.84.refs_5_), channel_id=1, source_target_pairs={{0,2},{2,0},{4,6},{6,4},{8,10},{10,8},{12,14},{14,12},{1,3},{3,1},... | collective-permute-start | bytes 12296 | tf_op jit(solution)/shard_map/ppermute | solution.py:27
  20.8 5.3 %collective-permute-start.6 = (s32[8,128]{1,0:T(8,128)S(1)}, s32[8,128]{1,0:T(8,128)S(1)}, u32[]{:S(2)}, u32[]{:S(2)}) collective-permute-start(s32[8,128]{1,0:T(8,128)S(1)} %shard_map.84.refs_5_), channel_id=1, source_target_pairs={{0,3},{1,2},{2,1},{3,0},{4,7},{5,6},{6,5},{7,4},{8,11},{9,10},{10,... | collective-permute-start | bytes 12296 | tf_op jit(solution)/shard_map/ppermute | solution.py:33
  21.1 14.3 %collective-permute-start.9 = (bf16[272,768]{1,0:T(8,128)(2,1)S(1)}, bf16[272,768]{1,0:T(8,128)(2,1)S(1)}, u32[]{:S(2)}, u32[]{:S(2)}) collective-permute-start(bf16[272,768]{1,0:T(8,128)(2,1)S(1)} %collective-permute-done.2.refs_10_), channel_id=1, source_target_pairs={{0,4},{2,6},{4,0},{6,2},{8,12},{10,14},{12,8},{14,10},{1,5},{3,7},... | collective-permute-start | bytes 1253384 | tf_op jit(solution)/shard_map/ppermute | solution.py:22
  26.6 1.8 %collective-permute-start.7 = (bf16[256,768]{1,0:T(8,128)(2,1)S(1)}, bf16[256,768]{1,0:T(8,128)(2,1)S(1)}, u32[]{:S(2)}, u32[]{:S(2)}) collective-permute-start(bf16[256,768]{1,0:T(8,128)(2,1)S(1)} %get-tuple-element.22), channel_id=1, source_target_pairs={{0,1},{1,0},{2,3},{3,2},{4,5},{5,4},{6,7},{7,6},{8,9},{9,8},{10,11... | collective-permute-start | bytes 1179656 | tf_op jit(solution)/shard_map/ppermute | solution.py:27
  26.7 2.3 %collective-permute-start.8 = (bf16[256,768]{1,0:T(8,128)(2,1)S(1)}, bf16[256,768]{1,0:T(8,128)(2,1)S(1)}, u32[]{:S(2)}, u32[]{:S(2)}) collective-permute-start(bf16[256,768]{1,0:T(8,128)(2,1)S(1)} %get-tuple-element.21), channel_id=1, source_target_pairs={{0,1},{1,0},{2,3},{3,2},{4,5},{5,4},{6,7},{7,6},{8,9},{9,8},{10,11... | collective-permute-start | bytes 1179656 | tf_op jit(solution)/shard_map/ppermute | solution.py:27
  29.0 10.1 %copy-start.4 = (s32[4]{0:T(128)S(1)}, s32[4]{0:T(128)}, u32[]{:S(2)}) copy-start(s32[4]{0:T(128)} %clusters_ref) | copy-start | bytes 52
  29.0 10.1 %copy-start.6 = (s32[64]{0:T(128)S(1)}, s32[64]{0:T(128)}, u32[]{:S(2)}) copy-start(s32[64]{0:T(128)} %param.15) | copy-start | bytes 772
  37.1 2.1 %collective-permute-start.10 = (f32[4,128]{1,0:T(4,128)S(1)}, f32[4,128]{1,0:T(4,128)S(1)}, u32[]{:S(2)}, u32[]{:S(2)}) collective-permute-start(f32[4,128]{1,0:T(4,128)S(1)} %get-tuple-element.23), channel_id=1, source_target_pairs={{0,1},{1,0},{2,3},{3,2},{4,5},{5,4},{6,7},{7,6},{8,9},{9,8},{10,11... | collective-permute-start | bytes 6152 | tf_op jit(solution)/shard_map/ppermute | solution.py:27
  37.2 3.7 %collective-permute-start.11 = (f32[4,128]{1,0:T(4,128)S(1)}, f32[4,128]{1,0:T(4,128)S(1)}, u32[]{:S(2)}, u32[]{:S(2)}) collective-permute-start(f32[4,128]{1,0:T(4,128)S(1)} %get-tuple-element.25), channel_id=1, source_target_pairs={{0,2},{2,0},{4,6},{6,4},{8,10},{10,8},{12,14},{14,12},{1,3},{3,1},... | collective-permute-start | bytes 6152 | tf_op jit(solution)/shard_map/ppermute | solution.py:27
  38.0 3.0 %collective-permute-start.12 = (f32[4,128]{1,0:T(4,128)S(1)}, f32[4,128]{1,0:T(4,128)S(1)}, u32[]{:S(2)}, u32[]{:S(2)}) collective-permute-start(f32[4,128]{1,0:T(4,128)S(1)} %get-tuple-element.24), channel_id=1, source_target_pairs={{0,3},{1,2},{2,1},{3,0},{4,7},{5,6},{6,5},{7,4},{8,11},{9,10},{10,... | collective-permute-start | bytes 6152 | tf_op jit(solution)/shard_map/ppermute | solution.py:33

commit v23 on v22

--- a/solution.py
+++ b/solution.py
@@ -43,6 +43,15 @@
 
 def rows_of(index, count=1):
     return pl.ds(pl.multiple_of(index * LANES, LANES), count * LANES)
+
+
+def unfolded(payload_ref, height):
+    blocks = payload_ref.shape[0] // height
+    return jnp.concatenate([payload_ref[pl.ds(b * height, height), :] for b in range(blocks)], axis=1)
+
+
+def table_of(payload_ref):
+    return payload_ref[pl.ds(payload_ref.shape[0] - TABLE, TABLE), :].astype(jnp.float32)
 
 
 def pack_kernel(nhelper, helper_ref, live_ref, ids_ref, r_ref, out_ref):
@@ -54,8 +63,10 @@
         tile = helper_ref[0] + nhelper * c
         ids = ids_ref[pl.ds(tile, 1), :]
         table = jnp.where(row == c, jnp.where(tile * LANES + lane < live_ref[0], ids, -1), table)
-    out_ref[pl.ds(0, height), :] = r_ref[...]
-    out_ref[pl.ds(height, TABLE), pl.ds(0, LANES)] = table.astype(jnp.float32).astype(jnp.bfloat16)
+    blocks = r_ref.shape[1] // LANES
+    for b in range(blocks):
+        out_ref[pl.ds(b * height, height), :] = r_ref[:, pl.ds(b * LANES, LANES)]
+    out_ref[pl.ds(blocks * height, TABLE), :] = table.astype(jnp.float32).astype(jnp.bfloat16)
 
 
 def table_kernel(clusters_ref, count_ref, out_ref):
@@ -89,7 +100,7 @@
     copy.start()
 
     for s, r_ref in enumerate(r_refs):
-        table = r_ref[pl.ds(height, TABLE), pl.ds(0, LANES)].astype(jnp.float32)
+        table = table_of(r_ref)
         for c in range(chunks):
             ids = jnp.broadcast_to(table[c : c + 1, :], (LANES, LANES)).T
             rows = pl.ds(s * height + c * LANES, LANES)
@@ -140,7 +151,7 @@
         numbers = [[number_ref[3 * entry + i] for i in range(3)] for entry in sides]
         accs = [jnp.zeros((8, LANES), jnp.float32) for _ in range(wide)]
         for s, r_ref in enumerate(r_refs):
-            tile = r_ref[pl.ds(0, height), :]
+            tile = unfolded(r_ref, height)
             rows = pl.ds(s * height, height)
             for pair in range(wide // 2):
                 score = lax.dot_general(
@@ -166,15 +177,16 @@
 
 def last_kernel(chunks, wide, slot_ref, number_ref, qv, prev_ref, r_ref, out_ref):
     height = chunks * LANES
-    table = r_ref[pl.ds(height, TABLE), pl.ds(0, LANES)].astype(jnp.float32)
+    table = table_of(r_ref)
     ids = [table[c : c + 1, :] for c in range(chunks)]
     other = [jnp.where(row < 0.0, DEAD, -4.0) for row in ids]
+    tile = unfolded(r_ref, height)
     out_ref[...] = prev_ref[...]
 
     for group in range(number_ref.shape[0] // (3 * wide)):
         score = lax.dot_general(
             qv[wide * group * LANES : wide * (group + 1) * LANES, :],
-            r_ref[pl.ds(0, height), :],
+            tile,
             (((1,), (1,)), ((), ())),
             preferred_element_type=jnp.float32,
         )
@@ -191,7 +203,7 @@
 
 
 def first_call(chunks, qblocks, pieces, wide, given, payloads):
-    width = payloads[0].shape[1]
+    width = given[1].shape[1]
     slots = 4 * qblocks
     rows = len(payloads) * chunks * LANES
     return pl.pallas_call(
@@ -250,7 +262,7 @@
     own = lax.dynamic_index_in_dim(by_chunk, helper, 1, keepdims=False)
     own = pl.pallas_call(
         functools.partial(pack_kernel, nhelper),
-        out_shape=jax.ShapeDtypeStruct((chunks * LANES + TABLE, width), jnp.bfloat16),
+        out_shape=jax.ShapeDtypeStruct((width // LANES * chunks * LANES + TABLE, LANES), jnp.bfloat16),
         in_specs=[SMEM] * 2 + [VMEM] * 2,
         out_specs=VMEM,
         compiler_params=PARAMS,

time: 41.9 us -> 40.6 us (0.969)
  waiting for transfers between devices: 14.4 us -> 13 us
  Pallas kernels: 6.28 us -> 7.27 us
  starting transfers between devices: 15.5 us -> 14.7 us
    ppermute x3, waiting for transfers between devices: 2.97 us -> 1.58 us  [trade(): return lax.ppermute(value, 'blk', [(i, i ^ mask) for i in range(length)])]
    pallas_call x1, Pallas kernels: 3.94 us -> 4.9 us  [first_call(): pl.pallas_call(functools.partial(first_kernel, chunks, qblocks, pieces, w...]
    ppermute x3, starting transfers between devices: 8.64 us -> 7.8 us  [trade(): return lax.ppermute(value, 'blk', [(i, i ^ mask) for i in range(length)])]
    unnamed x14 -> x12, local copies, waits for them, and re-layouts: 3.12 us -> 3.12 us
  transfers between devices with their start and end apart: 13 -> 13, of which waited for: 8 -> 8; matrix products, arithmetic and copies ran while one was open for 1% -> 1% of each run, Pallas kernels for 11% -> 14%
where the time goes in v23:
time: 40.6 us; the launch traced here: 40.4 us
  starting transfers between devices  14.7 us (36%)
  waiting for transfers between devices  13 us (32%)
  Pallas kernels  7.27 us (18%)
  local copies, waits for them, and re-layouts  3.21 us (8%)
  between operations  1.41 us (3%)
  other arithmetic  0.85 us (2%)
    ppermute x8, waiting for transfers between devices, swap(): return lax.ppermute(value, axis, [(i, i ^ 1) for i in range(length)])  11.3 us
    ppermute x3, starting transfers between devices, trade(): return lax.ppermute(value, 'blk', [(i, i ^ mask) for i in range(length)])  7.8 us
    ppermute x8, starting transfers between devices, swap(): return lax.ppermute(value, axis, [(i, i ^ 1) for i in range(length)])  5.49 us
    pallas_call x1, Pallas kernels, first_call(): pl.pallas_call(functools.partial(first_kernel, chunks, qblocks, pieces, w...  4.9 us
    unnamed x12, local copies, waits for them, and re-layouts  3.12 us
    pallas_call x1, Pallas kernels, last_call(): pl.pallas_call(functools.partial(last_kernel, chunks, wide), out_shape=ja...  1.7 us
    ppermute x3, waiting for transfers between devices, trade(): return lax.ppermute(value, 'blk', [(i, i ^ mask) for i in range(length)])  1.58 us
    ppermute x2, starting transfers between devices, swap_both(): return lax.ppermute(value, ('blk', 'helper'), pairs)  1.37 us
  transfers between devices with their start and end apart: 13, of which 8 were waited for; matrix products, arithmetic and copies ran while one was open for 1% of the time, Pallas kernels for 14%

profile of v23, /device:TPU:0, one launch (start us, length us, event | category | flops | bytes accessed | tf_op | source)
XLA Modules:
  0.0 40.4 jit_solution(8749814678058169304)
XLA Ops:
  0.0 3.0 %collective-permute-start.1 = (bf16[512,768]{1,0:T(8,128)(2,1)}, bf16[512,768]{1,0:T(8,128)(2,1)S(1)}, u32[]{:S(2)}, u32[]{:S(2)}) collective-permute-start(bf16[512,768]{1,0:T(8,128)(2,1)} %refs_0_.1), channel_id=1, source_target_pairs={{0,2},{2,0},{4,6},{6,4},{8,10},{10,8},{12,14},{14,12},{1,3},{3,1},... | collective-permute-start | bytes 2359304 | tf_op jit(solution)/shard_map/ppermute | solution.py:27
  3.7 0.7 %copy-done.2 = s32[512]{0:T(512)S(1)} copy-done((s32[512]{0:T(512)S(1)}, s32[512]{0:T(512)}, u32[]{:S(2)}) %copy-start.2) | copy-done | bytes 2072
  4.4 3.7 %collective-permute-start.2 = (bf16[1552,128]{1,0:T(8,128)(2,1)S(1)}, bf16[1552,128]{1,0:T(8,128)(2,1)S(1)}, u32[]{:S(2)}, u32[]{:S(2)}) collective-permute-start(bf16[1552,128]{1,0:T(8,128)(2,1)S(1)} %shard_map.83.refs_9_), channel_id=1, source_target_pairs={{0,12},{2,14},{4,8},{6,10},{8,4},{10,6},{12,0},{14,2},{1,13},{3,15... | collective-permute-start | bytes 1191944 | tf_op jit(solution)/shard_map/ppermute | solution.py:22
  8.1 1.1 %copy-done.1 = bf16[512,768]{1,0:T(8,128)(2,1)S(1)} copy-done((bf16[512,768]{1,0:T(8,128)(2,1)S(1)}, bf16[512,768]{1,0:T(8,128)(2,1)}, u32[]{:S(2)}) %copy-start.1) | copy-done | bytes 786456
  9.2 0.7 %copy-done.4 = f32[64]{0:T(128)S(1)} copy-done((f32[64]{0:T(128)S(1)}, f32[64]{0:T(128)}, u32[]{:S(2)}) %copy-start.4) | copy-done | bytes 280
  10.6 0.6 %copy-done.3 = s32[4]{0:T(128)S(1)} copy-done((s32[4]{0:T(128)S(1)}, s32[4]{0:T(128)}, u32[]{:S(2)}) %copy-start.3) | copy-done | bytes 40
  11.3 0.5 %shard_map.84.refs_5_ = s32[8,128]{1,0:T(8,128)S(1)} custom-call(s32[4]{0:T(128)S(1)} %copy-done.3, s32[1]{0:T(128)S(6)} %copy.12.count_ref), custom_call_target="tpu_custom_call" | custom-call | flops 1 | bytes 1 | tf_op jit(solution)/shard_map/pallas_call | solution.py:292
  11.8 0.6 %collective-permute-start.4 = (s32[8,128]{1,0:T(8,128)S(1)}, s32[8,128]{1,0:T(8,128)S(1)}, u32[]{:S(2)}, u32[]{:S(2)}) collective-permute-start(s32[8,128]{1,0:T(8,128)S(1)} %shard_map.84.refs_5_), channel_id=1, source_target_pairs={{0,1},{1,0},{2,3},{3,2},{4,5},{5,4},{6,7},{7,6},{8,9},{9,8},{10,11... | collective-permute-start | bytes 12296 | tf_op jit(solution)/shard_map/ppermute | solution.py:27
  12.4 0.8 %collective-permute-done.4.refs_6_ = s32[8,128]{1,0:T(8,128)S(1)} collective-permute-done((s32[8,128]{1,0:T(8,128)S(1)}, s32[8,128]{1,0:T(8,128)S(1)}, u32[]{:S(2)}, u32[]{:S(2)}) %collective-permute-start.4) | collective-permute-done | bytes 4128 | tf_op jit(solution)/shard_map/ppermute | solution.py:27
  13.2 0.5 %collective-permute-start.5 = (s32[8,128]{1,0:T(8,128)S(1)}, s32[8,128]{1,0:T(8,128)S(1)}, u32[]{:S(2)}, u32[]{:S(2)}) collective-permute-start(s32[8,128]{1,0:T(8,128)S(1)} %shard_map.84.refs_5_), channel_id=1, source_target_pairs={{0,2},{2,0},{4,6},{6,4},{8,10},{10,8},{12,14},{14,12},{1,3},{3,1},... | collective-permute-start | bytes 12296 | tf_op jit(solution)/shard_map/ppermute | solution.py:27
  13.7 7.1 %collective-permute-done.5.refs_7_ = s32[8,128]{1,0:T(8,128)S(1)} collective-permute-done((s32[8,128]{1,0:T(8,128)S(1)}, s32[8,128]{1,0:T(8,128)S(1)}, u32[]{:S(2)}, u32[]{:S(2)}) %collective-permute-start.5) | collective-permute-done | bytes 4128 | tf_op jit(solution)/shard_map/ppermute | solution.py:27
  20.8 0.3 collective-permute-start.6
  21.1 4.1 %collective-permute-start.9 = (bf16[1552,128]{1,0:T(8,128)(2,1)S(1)}, bf16[1552,128]{1,0:T(8,128)(2,1)S(1)}, u32[]{:S(2)}, u32[]{:S(2)}) collective-permute-start(bf16[1552,128]{1,0:T(8,128)(2,1)S(1)} %collective-permute-done.2.refs_10_), channel_id=1, source_target_pairs={{0,4},{2,6},{4,0},{6,2},{8,12},{10,14},{12,8},{14,10},{1,5},{3,7},... | collective-permute-start | bytes 1191944 | tf_op jit(solution)/shard_map/ppermute | solution.py:22
  25.3 0.5 %collective-permute-done.3.refs_11_ = bf16[1552,128]{1,0:T(8,128)(2,1)S(1)} collective-permute-done((bf16[1552,128]{1,0:T(8,128)(2,1)S(1)}, bf16[1552,128]{1,0:T(8,128)(2,1)S(1)}, u32[]{:S(2)}, u32[]{:S(2)}) %collective-permute-start.3) | collective-permute-done | bytes 397344 | tf_op jit(solution)/shard_map/ppermute | solution.py:22
  25.9 0.5 %collective-permute-start.8 = (bf16[256,768]{1,0:T(8,128)(2,1)S(1)}, bf16[256,768]{1,0:T(8,128)(2,1)S(1)}, u32[]{:S(2)}, u32[]{:S(2)}) collective-permute-start(bf16[256,768]{1,0:T(8,128)(2,1)S(1)} %get-tuple-element.21), channel_id=1, source_target_pairs={{0,1},{1,0},{2,3},{3,2},{4,5},{5,4},{6,7},{7,6},{8,9},{9,8},{10,11... | collective-permute-start | bytes 1179656 | tf_op jit(solution)/shard_map/ppermute | solution.py:27
  26.4 1.2 %collective-permute-done.7.refs_3_ = bf16[256,768]{1,0:T(8,128)(2,1)S(1)} collective-permute-done((bf16[256,768]{1,0:T(8,128)(2,1)S(1)}, bf16[256,768]{1,0:T(8,128)(2,1)S(1)}, u32[]{:S(2)}, u32[]{:S(2)}) %collective-permute-start.7) | collective-permute-done | bytes 393248 | tf_op jit(solution)/shard_map/ppermute | solution.py:27
  27.6 0.6 %collective-permute-done.8.refs_4_ = bf16[256,768]{1,0:T(8,128)(2,1)S(1)} collective-permute-done((bf16[256,768]{1,0:T(8,128)(2,1)S(1)}, bf16[256,768]{1,0:T(8,128)(2,1)S(1)}, u32[]{:S(2)}, u32[]{:S(2)}) %collective-permute-start.8) | collective-permute-done | bytes 393248 | tf_op jit(solution)/shard_map/ppermute | solution.py:27
  28.1 4.9 %shard_map.85 = (f32[24,128]{1,0:T(8,128)S(1)}, bf16[2048,768]{1,0:T(8,128)(2,1)S(1)}, s32[24]{0:T(128)S(1)}, f32[48]{0:T(128)S(1)}) custom-call(f32[1,64]{1,0:T(1,128)S(1)} %get-tuple-element.13.beta_ref, bf16[512,768]{1,0:T(8,128)(2,1)S(1)} %get-tuple-element.14.refs_0_, bf16[512,768]{1,0:T(8,128)(2,1)S(1)} %collective-permute-done.refs_1_, ...), custom_call_target="tpu_custom_call" | custom-call | flops 1 | bytes 1 | tf_op jit(solution)/shard_map/pallas_call | solution.py:209
  33.1 1.1 %collective-permute-done.9.r_ref = bf16[1552,128]{1,0:T(8,128)(2,1)S(1)} collective-permute-done((bf16[1552,128]{1,0:T(8,128)(2,1)S(1)}, bf16[1552,128]{1,0:T(8,128)(2,1)S(1)}, u32[]{:S(2)}, u32[]{:S(2)}) %collective-permute-start.9) | collective-permute-done | bytes 397344 | tf_op jit(solution)/shard_map/ppermute | solution.py:22
  34.2 1.7 %shard_map.86 = f32[24,128]{1,0:T(8,128)S(1)} custom-call(s32[24]{0:T(128)S(1)} %get-tuple-element.17.slot_ref, f32[48]{0:T(128)S(1)} %get-tuple-element.18.number_ref, bf16[2048,768]{1,0:T(8,128)(2,1)S(1)} %get-tuple-element.19.qv, f32[24,128]{1,0:T(8,128)S(1)} %get-tuple-element.20.prev_ref, bf16[1552,128]{1,0:T(8,128)(2,1)S(1)} %collective-permute-done.9.r_ref), custom_call_target="tpu_custom_call" | custom-call | flops 1 | bytes 1 | tf_op jit(solution)/shard_map/pallas_call | solution.py:232
  35.9 0.8 %collective-permute-start.11 = (f32[4,128]{1,0:T(4,128)S(1)}, f32[4,128]{1,0:T(4,128)S(1)}, u32[]{:S(2)}, u32[]{:S(2)}) collective-permute-start(f32[4,128]{1,0:T(4,128)S(1)} %get-tuple-element.25), channel_id=1, source_target_pairs={{0,2},{2,0},{4,6},{6,4},{8,10},{10,8},{12,14},{14,12},{1,3},{3,1},... | collective-permute-start | bytes 6152 | tf_op jit(solution)/shard_map/ppermute | solution.py:27
  36.7 1.1 %collective-permute-start.12 = (f32[4,128]{1,0:T(4,128)S(1)}, f32[4,128]{1,0:T(4,128)S(1)}, u32[]{:S(2)}, u32[]{:S(2)}) collective-permute-start(f32[4,128]{1,0:T(4,128)S(1)} %get-tuple-element.24), channel_id=1, source_target_pairs={{0,3},{1,2},{2,1},{3,0},{4,7},{5,6},{6,5},{7,4},{8,11},{9,10},{10,... | collective-permute-start | bytes 6152 | tf_op jit(solution)/shard_map/ppermute | solution.py:33
  38.0 1.6 %collective-permute-done.11 = f32[4,128]{1,0:T(4,128)S(1)} collective-permute-done((f32[4,128]{1,0:T(4,128)S(1)}, f32[4,128]{1,0:T(4,128)S(1)}, u32[]{:S(2)}, u32[]{:S(2)}) %collective-permute-start.11) | collective-permute-done | bytes 2080 | tf_op jit(solution)/shard_map/ppermute | solution.py:27
  39.8 0.7 %log-plus-one_bitcast_fusion = f32[512]{0:T(512)} fusion(f32[4,128]{1,0:T(4,128)S(1)} %collective-permute-done.12, f32[4,128]{1,0:T(4,128)S(1)} %collective-permute-done.11, f32[4,128]{1,0:T(4,128)S(1)} %collective-permute-done.10, f32[24,128]{1,0:T(8,128)S(1)} %shard_map.86, f32[4]{0:T(128)S(1)} %convert_element_type.7), kind=kLoop, calls=%fused_computation.4 | loop fusion | flops 2048 | bytes 10256 | tf_op jit(solution)/shard_map/reshape | solution.py:317
  (25 shorter events, 0.7 us)
Async XLA Ops:
  0.0 3.6 %copy-start = (bf16[512,768]{1,0:T(8,128)(2,1)S(1)}, bf16[512,768]{1,0:T(8,128)(2,1)}, u32[]{:S(2)}) copy-start(bf16[512,768]{1,0:T(8,128)(2,1)} %param.11) | copy-start | bytes 2359300
  0.0 25.7 %collective-permute-start.1 = (bf16[512,768]{1,0:T(8,128)(2,1)}, bf16[512,768]{1,0:T(8,128)(2,1)S(1)}, u32[]{:S(2)}, u32[]{:S(2)}) collective-permute-start(bf16[512,768]{1,0:T(8,128)(2,1)} %refs_0_.1), channel_id=1, source_target_pairs={{0,2},{2,0},{4,6},{6,4},{8,10},{10,8},{12,14},{14,12},{1,3},{3,1},... | collective-permute-start | bytes 2359304 | tf_op jit(solution)/shard_map/ppermute | solution.py:27
  3.7 0.7 %copy-start.2 = (s32[512]{0:T(512)S(1)}, s32[512]{0:T(512)}, u32[]{:S(2)}) copy-start(s32[512]{0:T(512)} %param.12) | copy-start | bytes 6148
  4.4 16.7 %collective-permute-start.2 = (bf16[1552,128]{1,0:T(8,128)(2,1)S(1)}, bf16[1552,128]{1,0:T(8,128)(2,1)S(1)}, u32[]{:S(2)}, u32[]{:S(2)}) collective-permute-start(bf16[1552,128]{1,0:T(8,128)(2,1)S(1)} %shard_map.83.refs_9_), channel_id=1, source_target_pairs={{0,12},{2,14},{4,8},{6,10},{8,4},{10,6},{12,0},{14,2},{1,13},{3,15... | collective-permute-start | bytes 1191944 | tf_op jit(solution)/shard_map/ppermute | solution.py:22
  8.1 17.6 %collective-permute-start.3 = (bf16[1552,128]{1,0:T(8,128)(2,1)S(1)}, bf16[1552,128]{1,0:T(8,128)(2,1)S(1)}, u32[]{:S(2)}, u32[]{:S(2)}) collective-permute-start(bf16[1552,128]{1,0:T(8,128)(2,1)S(1)} %shard_map.83.refs_9_), channel_id=1, source_target_pairs={{0,4},{2,6},{4,0},{6,2},{8,12},{10,14},{12,8},{14,10},{1,5},{3,7},... | collective-permute-start | bytes 1191944 | tf_op jit(solution)/shard_map/ppermute | solution.py:22
  8.1 18.3 %collective-permute-start = (bf16[512,768]{1,0:T(8,128)(2,1)}, bf16[512,768]{1,0:T(8,128)(2,1)S(1)}, u32[]{:S(2)}, u32[]{:S(2)}) collective-permute-start(bf16[512,768]{1,0:T(8,128)(2,1)} %refs_0_.1), channel_id=1, source_target_pairs={{0,1},{1,0},{2,3},{3,2},{4,5},{5,4},{6,7},{7,6},{8,9},{9,8},{10,11... | collective-permute-start | bytes 2359304 | tf_op jit(solution)/shard_map/ppermute | solution.py:27
  8.1 1.1 %copy-start.1 = (bf16[512,768]{1,0:T(8,128)(2,1)S(1)}, bf16[512,768]{1,0:T(8,128)(2,1)}, u32[]{:S(2)}) copy-start(bf16[512,768]{1,0:T(8,128)(2,1)} %refs_0_.1) | copy-start | bytes 2359300
  9.2 0.7 %copy-start.4 = (f32[64]{0:T(128)S(1)}, f32[64]{0:T(128)}, u32[]{:S(2)}) copy-start(f32[64]{0:T(128)} %param.14) | copy-start | bytes 772
  10.6 0.7 %copy-start.3 = (s32[4]{0:T(128)S(1)}, s32[4]{0:T(128)}, u32[]{:S(2)}) copy-start(s32[4]{0:T(128)} %clusters_ref) | copy-start | bytes 52
  11.8 1.4 %collective-permute-start.4 = (s32[8,128]{1,0:T(8,128)S(1)}, s32[8,128]{1,0:T(8,128)S(1)}, u32[]{:S(2)}, u32[]{:S(2)}) collective-permute-start(s32[8,128]{1,0:T(8,128)S(1)} %shard_map.84.refs_5_), channel_id=1, source_target_pairs={{0,1},{1,0},{2,3},{3,2},{4,5},{5,4},{6,7},{7,6},{8,9},{9,8},{10,11... | collective-permute-start | bytes 12296 | tf_op jit(solution)/shard_map/ppermute | solution.py:27
  13.2 7.6 %collective-permute-start.5 = (s32[8,128]{1,0:T(8,128)S(1)}, s32[8,128]{1,0:T(8,128)S(1)}, u32[]{:S(2)}, u32[]{:S(2)}) collective-permute-start(s32[8,128]{1,0:T(8,128)S(1)} %shard_map.84.refs_5_), channel_id=1, source_target_pairs={{0,2},{2,0},{4,6},{6,4},{8,10},{10,8},{12,14},{14,12},{1,3},{3,1},... | collective-permute-start | bytes 12296 | tf_op jit(solution)/shard_map/ppermute | solution.py:27
  20.8 4.5 %collective-permute-start.6 = (s32[8,128]{1,0:T(8,128)S(1)}, s32[8,128]{1,0:T(8,128)S(1)}, u32[]{:S(2)}, u32[]{:S(2)}) collective-permute-start(s32[8,128]{1,0:T(8,128)S(1)} %shard_map.84.refs_5_), channel_id=1, source_target_pairs={{0,3},{1,2},{2,1},{3,0},{4,7},{5,6},{6,5},{7,4},{8,11},{9,10},{10,... | collective-permute-start | bytes 12296 | tf_op jit(solution)/shard_map/ppermute | solution.py:33
  21.1 13.0 %collective-permute-start.9 = (bf16[1552,128]{1,0:T(8,128)(2,1)S(1)}, bf16[1552,128]{1,0:T(8,128)(2,1)S(1)}, u32[]{:S(2)}, u32[]{:S(2)}) collective-permute-start(bf16[1552,128]{1,0:T(8,128)(2,1)S(1)} %collective-permute-done.2.refs_10_), channel_id=1, source_target_pairs={{0,4},{2,6},{4,0},{6,2},{8,12},{10,14},{12,8},{14,10},{1,5},{3,7},... | collective-permute-start | bytes 1191944 | tf_op jit(solution)/shard_map/ppermute | solution.py:22
  25.8 1.8 %collective-permute-start.7 = (bf16[256,768]{1,0:T(8,128)(2,1)S(1)}, bf16[256,768]{1,0:T(8,128)(2,1)S(1)}, u32[]{:S(2)}, u32[]{:S(2)}) collective-permute-start(bf16[256,768]{1,0:T(8,128)(2,1)S(1)} %get-tuple-element.22), channel_id=1, source_target_pairs={{0,1},{1,0},{2,3},{3,2},{4,5},{5,4},{6,7},{7,6},{8,9},{9,8},{10,11... | collective-permute-start | bytes 1179656 | tf_op jit(solution)/shard_map/ppermute | solution.py:27
  25.9 2.3 %collective-permute-start.8 = (bf16[256,768]{1,0:T(8,128)(2,1)S(1)}, bf16[256,768]{1,0:T(8,128)(2,1)S(1)}, u32[]{:S(2)}, u32[]{:S(2)}) collective-permute-start(bf16[256,768]{1,0:T(8,128)(2,1)S(1)} %get-tuple-element.21), channel_id=1, source_target_pairs={{0,1},{1,0},{2,3},{3,2},{4,5},{5,4},{6,7},{7,6},{8,9},{9,8},{10,11... | collective-permute-start | bytes 1179656 | tf_op jit(solution)/shard_map/ppermute | solution.py:27
  28.1 9.7 %copy-start.5 = (s32[64]{0:T(128)S(1)}, s32[64]{0:T(128)}, u32[]{:S(2)}) copy-start(s32[64]{0:T(128)} %param.15) | copy-start | bytes 772
  35.9 2.1 %collective-permute-start.10 = (f32[4,128]{1,0:T(4,128)S(1)}, f32[4,128]{1,0:T(4,128)S(1)}, u32[]{:S(2)}, u32[]{:S(2)}) collective-permute-start(f32[4,128]{1,0:T(4,128)S(1)} %get-tuple-element.23), channel_id=1, source_target_pairs={{0,1},{1,0},{2,3},{3,2},{4,5},{5,4},{6,7},{7,6},{8,9},{9,8},{10,11... | collective-permute-start | bytes 6152 | tf_op jit(solution)/shard_map/ppermute | solution.py:27
  35.9 3.7 %collective-permute-start.11 = (f32[4,128]{1,0:T(4,128)S(1)}, f32[4,128]{1,0:T(4,128)S(1)}, u32[]{:S(2)}, u32[]{:S(2)}) collective-permute-start(f32[4,128]{1,0:T(4,128)S(1)} %get-tuple-element.25), channel_id=1, source_target_pairs={{0,2},{2,0},{4,6},{6,4},{8,10},{10,8},{12,14},{14,12},{1,3},{3,1},... | collective-permute-start | bytes 6152 | tf_op jit(solution)/shard_map/ppermute | solution.py:27
  36.7 3.0 %collective-permute-start.12 = (f32[4,128]{1,0:T(4,128)S(1)}, f32[4,128]{1,0:T(4,128)S(1)}, u32[]{:S(2)}, u32[]{:S(2)}) collective-permute-start(f32[4,128]{1,0:T(4,128)S(1)} %get-tuple-element.24), channel_id=1, source_target_pairs={{0,3},{1,2},{2,1},{3,0},{4,7},{5,6},{6,5},{7,4},{8,11},{9,10},{10,... | collective-permute-start | bytes 6152 | tf_op jit(solution)/shard_map/ppermute | solution.py:33

commit v24 on v23

--- a/solution.py
+++ b/solution.py
@@ -85,7 +85,7 @@
 
 
 def first_kernel(chunks, qblocks, pieces, wide, beta_ref, *refs):
-    *given, out_ref, qv, slot_ref, number_ref, info_v, info, ids_ref, other_ref, info_sem = refs
+    *given, out_ref, qv, number_ref, info_v, info, ids_ref, other_ref, info_sem = refs
     q_refs = []
     for n in pieces:
         q_refs.append(given[:n])
@@ -117,10 +117,10 @@
             entry = q_count + block
             cluster = info[source, block]
             beta = beta_ref[0, cluster]
-            slot_ref[entry] = source * qblocks + block
-            number_ref[3 * entry] = cluster.astype(jnp.float32)
-            number_ref[3 * entry + 1] = beta * factor
-            number_ref[3 * entry + 2] = beta * beta * (0.5 * LOG2E)
+            number_ref[4 * entry] = cluster.astype(jnp.float32)
+            number_ref[4 * entry + 1] = beta * factor
+            number_ref[4 * entry + 2] = beta * beta * (0.5 * LOG2E)
+            number_ref[4 * entry + 3] = jnp.float32(source * qblocks) + block.astype(jnp.float32)
             return carry
 
         lax.fori_loop(0, blocks, enter, 0)
@@ -137,18 +137,17 @@
         q_count = q_count + blocks
 
     def spare(entry, carry):
-        slot_ref[entry] = slots
+        number_ref[4 * entry + 3] = float(slots)
         for i in range(3):
-            number_ref[3 * entry + i] = 0.0
+            number_ref[4 * entry + i] = 0.0
         return carry
 
     lax.fori_loop(q_count, slots, spare, 0)
-    slot_ref[slots] = q_count
     out_ref[...] = jnp.zeros_like(out_ref)
 
     def query_blocks(group, carry):
         sides = [wide * group + side for side in range(wide)]
-        numbers = [[number_ref[3 * entry + i] for i in range(3)] for entry in sides]
+        numbers = [[number_ref[4 * entry + i] for i in range(3)] for entry in sides]
         accs = [jnp.zeros((8, LANES), jnp.float32) for _ in range(wide)]
         for s, r_ref in enumerate(r_refs):
             tile = unfolded(r_ref, height)
@@ -168,14 +167,14 @@
                     value = jnp.exp2((part * scale - offset) + weight)
                     accs[side] += jnp.sum(value.reshape(height // 8, 8, LANES), axis=0)
         for entry, acc in zip(sides, accs):
-            row = pl.ds(slot_ref[entry], 1)
+            row = pl.ds(number_ref[4 * entry + 3].astype(jnp.int32), 1)
             out_ref[row, :] = out_ref[row, :] + jnp.sum(acc, axis=0, keepdims=True)
         return carry
 
     lax.fori_loop(0, (q_count + wide - 1) // wide, query_blocks, 0)
 
 
-def last_kernel(chunks, wide, slot_ref, number_ref, qv, prev_ref, r_ref, out_ref):
+def last_kernel(chunks, wide, number_ref, qv, prev_ref, r_ref, out_ref):
     height = chunks * LANES
     table = table_of(r_ref)
     ids = [table[c : c + 1, :] for c in range(chunks)]
@@ -183,7 +182,7 @@
     tile = unfolded(r_ref, height)
     out_ref[...] = prev_ref[...]
 
-    for group in range(number_ref.shape[0] // (3 * wide)):
+    for group in range(number_ref.shape[0] // (4 * wide)):
         score = lax.dot_general(
             qv[wide * group * LANES : wide * (group + 1) * LANES, :],
             tile,
@@ -192,13 +191,13 @@
         )
         for side in range(wide):
             entry = wide * group + side
-            cluster, scale, offset = (number_ref[3 * entry + i] for i in range(3))
+            cluster, scale, offset = (number_ref[4 * entry + i] for i in range(3))
             acc = jnp.zeros((LANES, LANES), jnp.float32)
             for c in range(chunks):
                 part = score[side * LANES : (side + 1) * LANES, c * LANES : (c + 1) * LANES]
                 bias = jnp.where(ids[c] == cluster, 0.0, other[c]) - offset
                 acc = acc + jnp.exp2(part * scale + bias)
-            row = pl.ds(slot_ref[entry], 1)
+            row = pl.ds(number_ref[4 * entry + 3].astype(jnp.int32), 1)
             out_ref[row, :] = out_ref[row, :] + jnp.sum(acc.T, axis=0, keepdims=True)
 
 
@@ -211,11 +210,10 @@
         out_shape=(
             jax.ShapeDtypeStruct((slots + 8, LANES), jnp.float32),
             jax.ShapeDtypeStruct((slots * LANES, width), jnp.bfloat16),
-            jax.ShapeDtypeStruct((slots + 8,), jnp.int32),
-            jax.ShapeDtypeStruct((3 * slots,), jnp.float32),
+            jax.ShapeDtypeStruct((4 * slots,), jnp.float32),
         ),
         in_specs=[SMEM] + [VMEM] * (len(given) - 1 + len(payloads)),
-        out_specs=(VMEM, VMEM, SMEM, SMEM),
+        out_specs=(VMEM, VMEM, SMEM),
         scratch_shapes=[
             pltpu.VMEM((8, LANES), jnp.int32),
             pltpu.SMEM((8, LANES), jnp.int32),
@@ -228,15 +226,15 @@
     )(*given, *payloads)
 
 
-def last_call(chunks, wide, slots, numbers, packed, totals, payload):
+def last_call(chunks, wide, numbers, packed, totals, payload):
     return pl.pallas_call(
         functools.partial(last_kernel, chunks, wide),
         out_shape=jax.ShapeDtypeStruct(totals.shape, jnp.float32),
-        in_specs=[SMEM] * 2 + [VMEM] * 3,
+        in_specs=[SMEM] + [VMEM] * 3,
         out_specs=VMEM,
         compiler_params=PARAMS,
         cost_estimate=cost(1, 1),
-    )(slots, numbers, packed, totals, payload)
+    )(numbers, packed, totals, payload)
 
 
 def per_device(
@@ -305,8 +303,8 @@
     pieces = (1, 1, 1, 2)
 
     given = (beta, *queries, *q_tables)
-    totals, packed, *plan = first_call(chunks, qblocks, pieces, 4, given, held[:-1])
-    totals = last_call(chunks, 4, *plan, packed, totals, held[-1])
+    totals, packed, numbers = first_call(chunks, qblocks, pieces, 4, given, held[:-1])
+    totals = last_call(chunks, 8, numbers, packed, totals, held[-1])
     totals = totals[: 4 * qblocks]
     totals = totals.reshape(4, qblocks, LANES)
     total = totals[0] + swap(totals[1], "helper") + swap(totals[2], "blk") + swap_both(totals[3])

time: 40.6 us -> 40.7 us (level)
  no operation moved by 1% of the time
where the time goes in v24:
time: 40.7 us; the launch traced here: 40.5 us
  starting transfers between devices  14.7 us (36%)
  waiting for transfers between devices  13.1 us (32%)
  Pallas kernels  7.29 us (18%)
  local copies, waits for them, and re-layouts  3.21 us (8%)
  between operations  1.41 us (3%)
  other arithmetic  0.85 us (2%)
    ppermute x8, waiting for transfers between devices, swap(): return lax.ppermute(value, axis, [(i, i ^ 1) for i in range(length)])  11.3 us
    ppermute x3, starting transfers between devices, trade(): return lax.ppermute(value, 'blk', [(i, i ^ mask) for i in range(length)])  7.8 us
    ppermute x8, starting transfers between devices, swap(): return lax.ppermute(value, axis, [(i, i ^ 1) for i in range(length)])  5.49 us
    pallas_call x1, Pallas kernels, first_call(): pl.pallas_call(functools.partial(first_kernel, chunks, qblocks, pieces, w...  4.87 us
    unnamed x12, local copies, waits for them, and re-layouts  3.12 us
    pallas_call x1, Pallas kernels, last_call(): pl.pallas_call(functools.partial(last_kernel, chunks, wide), out_shape=ja...  1.75 us
    ppermute x3, waiting for transfers between devices, trade(): return lax.ppermute(value, 'blk', [(i, i ^ mask) for i in range(length)])  1.61 us
    ppermute x2, starting transfers between devices, swap_both(): return lax.ppermute(value, ('blk', 'helper'), pairs)  1.37 us
  transfers between devices with their start and end apart: 13, of which 8 were waited for; matrix products, arithmetic and copies ran while one was open for 1% of the time, Pallas kernels for 14%

profile of v24, /device:TPU:0, one launch (start us, length us, event | category | flops | bytes accessed | tf_op | source)
XLA Modules:
  0.0 40.5 jit_solution(2539640913435639516)
XLA Ops:
  0.0 3.0 %collective-permute-start.1 = (bf16[512,768]{1,0:T(8,128)(2,1)}, bf16[512,768]{1,0:T(8,128)(2,1)S(1)}, u32[]{:S(2)}, u32[]{:S(2)}) collective-permute-start(bf16[512,768]{1,0:T(8,128)(2,1)} %refs_0_.1), channel_id=1, source_target_pairs={{0,2},{2,0},{4,6},{6,4},{8,10},{10,8},{12,14},{14,12},{1,3},{3,1},... | collective-permute-start | bytes 2359304 | tf_op jit(solution)/shard_map/ppermute | solution.py:27
  3.7 0.7 %copy-done.2 = s32[512]{0:T(512)S(1)} copy-done((s32[512]{0:T(512)S(1)}, s32[512]{0:T(512)}, u32[]{:S(2)}) %copy-start.2) | copy-done | bytes 2072
  4.4 3.7 %collective-permute-start.2 = (bf16[1552,128]{1,0:T(8,128)(2,1)S(1)}, bf16[1552,128]{1,0:T(8,128)(2,1)S(1)}, u32[]{:S(2)}, u32[]{:S(2)}) collective-permute-start(bf16[1552,128]{1,0:T(8,128)(2,1)S(1)} %shard_map.83.refs_9_), channel_id=1, source_target_pairs={{0,12},{2,14},{4,8},{6,10},{8,4},{10,6},{12,0},{14,2},{1,13},{3,15... | collective-permute-start | bytes 1191944 | tf_op jit(solution)/shard_map/ppermute | solution.py:22
  8.1 1.1 %copy-done.1 = bf16[512,768]{1,0:T(8,128)(2,1)S(1)} copy-done((bf16[512,768]{1,0:T(8,128)(2,1)S(1)}, bf16[512,768]{1,0:T(8,128)(2,1)}, u32[]{:S(2)}) %copy-start.1) | copy-done | bytes 786456
  9.2 0.7 %copy-done.4 = f32[64]{0:T(128)S(1)} copy-done((f32[64]{0:T(128)S(1)}, f32[64]{0:T(128)}, u32[]{:S(2)}) %copy-start.4) | copy-done | bytes 280
  10.6 0.6 %copy-done.3 = s32[4]{0:T(128)S(1)} copy-done((s32[4]{0:T(128)S(1)}, s32[4]{0:T(128)}, u32[]{:S(2)}) %copy-start.3) | copy-done | bytes 40
  11.3 0.5 %shard_map.84.refs_5_ = s32[8,128]{1,0:T(8,128)S(1)} custom-call(s32[4]{0:T(128)S(1)} %copy-done.3, s32[1]{0:T(128)S(6)} %copy.12.count_ref), custom_call_target="tpu_custom_call" | custom-call | flops 1 | bytes 1 | tf_op jit(solution)/shard_map/pallas_call | solution.py:290
  11.8 0.6 %collective-permute-start.4 = (s32[8,128]{1,0:T(8,128)S(1)}, s32[8,128]{1,0:T(8,128)S(1)}, u32[]{:S(2)}, u32[]{:S(2)}) collective-permute-start(s32[8,128]{1,0:T(8,128)S(1)} %shard_map.84.refs_5_), channel_id=1, source_target_pairs={{0,1},{1,0},{2,3},{3,2},{4,5},{5,4},{6,7},{7,6},{8,9},{9,8},{10,11... | collective-permute-start | bytes 12296 | tf_op jit(solution)/shard_map/ppermute | solution.py:27
  12.4 0.8 %collective-permute-done.4.refs_6_ = s32[8,128]{1,0:T(8,128)S(1)} collective-permute-done((s32[8,128]{1,0:T(8,128)S(1)}, s32[8,128]{1,0:T(8,128)S(1)}, u32[]{:S(2)}, u32[]{:S(2)}) %collective-permute-start.4) | collective-permute-done | bytes 4128 | tf_op jit(solution)/shard_map/ppermute | solution.py:27
  13.2 0.5 %collective-permute-start.5 = (s32[8,128]{1,0:T(8,128)S(1)}, s32[8,128]{1,0:T(8,128)S(1)}, u32[]{:S(2)}, u32[]{:S(2)}) collective-permute-start(s32[8,128]{1,0:T(8,128)S(1)} %shard_map.84.refs_5_), channel_id=1, source_target_pairs={{0,2},{2,0},{4,6},{6,4},{8,10},{10,8},{12,14},{14,12},{1,3},{3,1},... | collective-permute-start | bytes 12296 | tf_op jit(solution)/shard_map/ppermute | solution.py:27
  13.7 7.1 %collective-permute-done.5.refs_7_ = s32[8,128]{1,0:T(8,128)S(1)} collective-permute-done((s32[8,128]{1,0:T(8,128)S(1)}, s32[8,128]{1,0:T(8,128)S(1)}, u32[]{:S(2)}, u32[]{:S(2)}) %collective-permute-start.5) | collective-permute-done | bytes 4128 | tf_op jit(solution)/shard_map/ppermute | solution.py:27
  20.8 0.3 collective-permute-start.6
  21.1 4.1 %collective-permute-start.9 = (bf16[1552,128]{1,0:T(8,128)(2,1)S(1)}, bf16[1552,128]{1,0:T(8,128)(2,1)S(1)}, u32[]{:S(2)}, u32[]{:S(2)}) collective-permute-start(bf16[1552,128]{1,0:T(8,128)(2,1)S(1)} %collective-permute-done.2.refs_10_), channel_id=1, source_target_pairs={{0,4},{2,6},{4,0},{6,2},{8,12},{10,14},{12,8},{14,10},{1,5},{3,7},... | collective-permute-start | bytes 1191944 | tf_op jit(solution)/shard_map/ppermute | solution.py:22
  25.3 0.5 %collective-permute-done.3.refs_11_ = bf16[1552,128]{1,0:T(8,128)(2,1)S(1)} collective-permute-done((bf16[1552,128]{1,0:T(8,128)(2,1)S(1)}, bf16[1552,128]{1,0:T(8,128)(2,1)S(1)}, u32[]{:S(2)}, u32[]{:S(2)}) %collective-permute-start.3) | collective-permute-done | bytes 397344 | tf_op jit(solution)/shard_map/ppermute | solution.py:22
  25.9 0.5 %collective-permute-start.8 = (bf16[256,768]{1,0:T(8,128)(2,1)S(1)}, bf16[256,768]{1,0:T(8,128)(2,1)S(1)}, u32[]{:S(2)}, u32[]{:S(2)}) collective-permute-start(bf16[256,768]{1,0:T(8,128)(2,1)S(1)} %get-tuple-element.19), channel_id=1, source_target_pairs={{0,1},{1,0},{2,3},{3,2},{4,5},{5,4},{6,7},{7,6},{8,9},{9,8},{10,11... | collective-permute-start | bytes 1179656 | tf_op jit(solution)/shard_map/ppermute | solution.py:27
  26.4 1.2 %collective-permute-done.7.refs_3_ = bf16[256,768]{1,0:T(8,128)(2,1)S(1)} collective-permute-done((bf16[256,768]{1,0:T(8,128)(2,1)S(1)}, bf16[256,768]{1,0:T(8,128)(2,1)S(1)}, u32[]{:S(2)}, u32[]{:S(2)}) %collective-permute-start.7) | collective-permute-done | bytes 393248 | tf_op jit(solution)/shard_map/ppermute | solution.py:27
  27.6 0.6 %collective-permute-done.8.refs_4_ = bf16[256,768]{1,0:T(8,128)(2,1)S(1)} collective-permute-done((bf16[256,768]{1,0:T(8,128)(2,1)S(1)}, bf16[256,768]{1,0:T(8,128)(2,1)S(1)}, u32[]{:S(2)}, u32[]{:S(2)}) %collective-permute-start.8) | collective-permute-done | bytes 393248 | tf_op jit(solution)/shard_map/ppermute | solution.py:27
  28.1 4.9 %shard_map.85 = (f32[24,128]{1,0:T(8,128)S(1)}, bf16[2048,768]{1,0:T(8,128)(2,1)S(1)}, f32[64]{0:T(128)S(1)}) custom-call(f32[1,64]{1,0:T(1,128)S(1)} %get-tuple-element.12.beta_ref, bf16[512,768]{1,0:T(8,128)(2,1)S(1)} %get-tuple-element.13.refs_0_, bf16[512,768]{1,0:T(8,128)(2,1)S(1)} %collective-permute-done.refs_1_, ...), custom_call_target="tpu_custom_call" | custom-call | flops 1 | bytes 1 | tf_op jit(solution)/shard_map/pallas_call | solution.py:208
  33.0 1.1 %collective-permute-done.9.r_ref = bf16[1552,128]{1,0:T(8,128)(2,1)S(1)} collective-permute-done((bf16[1552,128]{1,0:T(8,128)(2,1)S(1)}, bf16[1552,128]{1,0:T(8,128)(2,1)S(1)}, u32[]{:S(2)}, u32[]{:S(2)}) %collective-permute-start.9) | collective-permute-done | bytes 397344 | tf_op jit(solution)/shard_map/ppermute | solution.py:22
  34.2 1.7 %shard_map.86 = f32[24,128]{1,0:T(8,128)S(1)} custom-call(f32[64]{0:T(128)S(1)} %get-tuple-element.16.number_ref, bf16[2048,768]{1,0:T(8,128)(2,1)S(1)} %get-tuple-element.17.qv, f32[24,128]{1,0:T(8,128)S(1)} %get-tuple-element.18.prev_ref, bf16[1552,128]{1,0:T(8,128)(2,1)S(1)} %collective-permute-done.9.r_ref), custom_call_target="tpu_custom_call" | custom-call | flops 1 | bytes 1 | tf_op jit(solution)/shard_map/pallas_call | solution.py:230
  36.0 0.8 %collective-permute-start.11 = (f32[4,128]{1,0:T(4,128)S(1)}, f32[4,128]{1,0:T(4,128)S(1)}, u32[]{:S(2)}, u32[]{:S(2)}) collective-permute-start(f32[4,128]{1,0:T(4,128)S(1)} %get-tuple-element.23), channel_id=1, source_target_pairs={{0,2},{2,0},{4,6},{6,4},{8,10},{10,8},{12,14},{14,12},{1,3},{3,1},... | collective-permute-start | bytes 6152 | tf_op jit(solution)/shard_map/ppermute | solution.py:27
  36.8 1.1 %collective-permute-start.12 = (f32[4,128]{1,0:T(4,128)S(1)}, f32[4,128]{1,0:T(4,128)S(1)}, u32[]{:S(2)}, u32[]{:S(2)}) collective-permute-start(f32[4,128]{1,0:T(4,128)S(1)} %get-tuple-element.22), channel_id=1, source_target_pairs={{0,3},{1,2},{2,1},{3,0},{4,7},{5,6},{6,5},{7,4},{8,11},{9,10},{10,... | collective-permute-start | bytes 6152 | tf_op jit(solution)/shard_map/ppermute | solution.py:33
  38.1 1.6 %collective-permute-done.11 = f32[4,128]{1,0:T(4,128)S(1)} collective-permute-done((f32[4,128]{1,0:T(4,128)S(1)}, f32[4,128]{1,0:T(4,128)S(1)}, u32[]{:S(2)}, u32[]{:S(2)}) %collective-permute-start.11) | collective-permute-done | bytes 2080 | tf_op jit(solution)/shard_map/ppermute | solution.py:27
  39.8 0.7 %log-plus-one_bitcast_fusion = f32[512]{0:T(512)} fusion(f32[4,128]{1,0:T(4,128)S(1)} %collective-permute-done.12, f32[4,128]{1,0:T(4,128)S(1)} %collective-permute-done.11, f32[4,128]{1,0:T(4,128)S(1)} %collective-permute-done.10, f32[24,128]{1,0:T(8,128)S(1)} %shard_map.86, f32[4]{0:T(128)S(1)} %convert_element_type.7), kind=kLoop, calls=%fused_computation.4 | loop fusion | flops 2048 | bytes 10256 | tf_op jit(solution)/shard_map/reshape | solution.py:315
  (25 shorter events, 0.8 us)
Async XLA Ops:
  0.0 3.6 %copy-start = (bf16[512,768]{1,0:T(8,128)(2,1)S(1)}, bf16[512,768]{1,0:T(8,128)(2,1)}, u32[]{:S(2)}) copy-start(bf16[512,768]{1,0:T(8,128)(2,1)} %param.11) | copy-start | bytes 2359300
  0.0 25.7 %collective-permute-start.1 = (bf16[512,768]{1,0:T(8,128)(2,1)}, bf16[512,768]{1,0:T(8,128)(2,1)S(1)}, u32[]{:S(2)}, u32[]{:S(2)}) collective-permute-start(bf16[512,768]{1,0:T(8,128)(2,1)} %refs_0_.1), channel_id=1, source_target_pairs={{0,2},{2,0},{4,6},{6,4},{8,10},{10,8},{12,14},{14,12},{1,3},{3,1},... | collective-permute-start | bytes 2359304 | tf_op jit(solution)/shard_map/ppermute | solution.py:27
  3.7 0.7 %copy-start.2 = (s32[512]{0:T(512)S(1)}, s32[512]{0:T(512)}, u32[]{:S(2)}) copy-start(s32[512]{0:T(512)} %param.12) | copy-start | bytes 6148
  4.4 16.7 %collective-permute-start.2 = (bf16[1552,128]{1,0:T(8,128)(2,1)S(1)}, bf16[1552,128]{1,0:T(8,128)(2,1)S(1)}, u32[]{:S(2)}, u32[]{:S(2)}) collective-permute-start(bf16[1552,128]{1,0:T(8,128)(2,1)S(1)} %shard_map.83.refs_9_), channel_id=1, source_target_pairs={{0,12},{2,14},{4,8},{6,10},{8,4},{10,6},{12,0},{14,2},{1,13},{3,15... | collective-permute-start | bytes 1191944 | tf_op jit(solution)/shard_map/ppermute | solution.py:22
  8.1 17.6 %collective-permute-start.3 = (bf16[1552,128]{1,0:T(8,128)(2,1)S(1)}, bf16[1552,128]{1,0:T(8,128)(2,1)S(1)}, u32[]{:S(2)}, u32[]{:S(2)}) collective-permute-start(bf16[1552,128]{1,0:T(8,128)(2,1)S(1)} %shard_map.83.refs_9_), channel_id=1, source_target_pairs={{0,4},{2,6},{4,0},{6,2},{8,12},{10,14},{12,8},{14,10},{1,5},{3,7},... | collective-permute-start | bytes 1191944 | tf_op jit(solution)/shard_map/ppermute | solution.py:22
  8.1 18.3 %collective-permute-start = (bf16[512,768]{1,0:T(8,128)(2,1)}, bf16[512,768]{1,0:T(8,128)(2,1)S(1)}, u32[]{:S(2)}, u32[]{:S(2)}) collective-permute-start(bf16[512,768]{1,0:T(8,128)(2,1)} %refs_0_.1), channel_id=1, source_target_pairs={{0,1},{1,0},{2,3},{3,2},{4,5},{5,4},{6,7},{7,6},{8,9},{9,8},{10,11... | collective-permute-start | bytes 2359304 | tf_op jit(solution)/shard_map/ppermute | solution.py:27
  8.1 1.1 %copy-start.1 = (bf16[512,768]{1,0:T(8,128)(2,1)S(1)}, bf16[512,768]{1,0:T(8,128)(2,1)}, u32[]{:S(2)}) copy-start(bf16[512,768]{1,0:T(8,128)(2,1)} %refs_0_.1) | copy-start | bytes 2359300
  9.2 0.7 %copy-start.4 = (f32[64]{0:T(128)S(1)}, f32[64]{0:T(128)}, u32[]{:S(2)}) copy-start(f32[64]{0:T(128)} %param.14) | copy-start | bytes 772
  10.6 0.7 %copy-start.3 = (s32[4]{0:T(128)S(1)}, s32[4]{0:T(128)}, u32[]{:S(2)}) copy-start(s32[4]{0:T(128)} %clusters_ref) | copy-start | bytes 52
  11.8 1.4 %collective-permute-start.4 = (s32[8,128]{1,0:T(8,128)S(1)}, s32[8,128]{1,0:T(8,128)S(1)}, u32[]{:S(2)}, u32[]{:S(2)}) collective-permute-start(s32[8,128]{1,0:T(8,128)S(1)} %shard_map.84.refs_5_), channel_id=1, source_target_pairs={{0,1},{1,0},{2,3},{3,2},{4,5},{5,4},{6,7},{7,6},{8,9},{9,8},{10,11... | collective-permute-start | bytes 12296 | tf_op jit(solution)/shard_map/ppermute | solution.py:27
  13.2 7.6 %collective-permute-start.5 = (s32[8,128]{1,0:T(8,128)S(1)}, s32[8,128]{1,0:T(8,128)S(1)}, u32[]{:S(2)}, u32[]{:S(2)}) collective-permute-start(s32[8,128]{1,0:T(8,128)S(1)} %shard_map.84.refs_5_), channel_id=1, source_target_pairs={{0,2},{2,0},{4,6},{6,4},{8,10},{10,8},{12,14},{14,12},{1,3},{3,1},... | collective-permute-start | bytes 12296 | tf_op jit(solution)/shard_map/ppermute | solution.py:27
  20.8 4.5 %collective-permute-start.6 = (s32[8,128]{1,0:T(8,128)S(1)}, s32[8,128]{1,0:T(8,128)S(1)}, u32[]{:S(2)}, u32[]{:S(2)}) collective-permute-start(s32[8,128]{1,0:T(8,128)S(1)} %shard_map.84.refs_5_), channel_id=1, source_target_pairs={{0,3},{1,2},{2,1},{3,0},{4,7},{5,6},{6,5},{7,4},{8,11},{9,10},{10,... | collective-permute-start | bytes 12296 | tf_op jit(solution)/shard_map/ppermute | solution.py:33
  21.1 13.0 %collective-permute-start.9 = (bf16[1552,128]{1,0:T(8,128)(2,1)S(1)}, bf16[1552,128]{1,0:T(8,128)(2,1)S(1)}, u32[]{:S(2)}, u32[]{:S(2)}) collective-permute-start(bf16[1552,128]{1,0:T(8,128)(2,1)S(1)} %collective-permute-done.2.refs_10_), channel_id=1, source_target_pairs={{0,4},{2,6},{4,0},{6,2},{8,12},{10,14},{12,8},{14,10},{1,5},{3,7},... | collective-permute-start | bytes 1191944 | tf_op jit(solution)/shard_map/ppermute | solution.py:22
  25.8 1.8 %collective-permute-start.7 = (bf16[256,768]{1,0:T(8,128)(2,1)S(1)}, bf16[256,768]{1,0:T(8,128)(2,1)S(1)}, u32[]{:S(2)}, u32[]{:S(2)}) collective-permute-start(bf16[256,768]{1,0:T(8,128)(2,1)S(1)} %get-tuple-element.20), channel_id=1, source_target_pairs={{0,1},{1,0},{2,3},{3,2},{4,5},{5,4},{6,7},{7,6},{8,9},{9,8},{10,11... | collective-permute-start | bytes 1179656 | tf_op jit(solution)/shard_map/ppermute | solution.py:27
  25.9 2.3 %collective-permute-start.8 = (bf16[256,768]{1,0:T(8,128)(2,1)S(1)}, bf16[256,768]{1,0:T(8,128)(2,1)S(1)}, u32[]{:S(2)}, u32[]{:S(2)}) collective-permute-start(bf16[256,768]{1,0:T(8,128)(2,1)S(1)} %get-tuple-element.19), channel_id=1, source_target_pairs={{0,1},{1,0},{2,3},{3,2},{4,5},{5,4},{6,7},{7,6},{8,9},{9,8},{10,11... | collective-permute-start | bytes 1179656 | tf_op jit(solution)/shard_map/ppermute | solution.py:27
  28.1 9.7 %copy-start.5 = (s32[64]{0:T(128)S(1)}, s32[64]{0:T(128)}, u32[]{:S(2)}) copy-start(s32[64]{0:T(128)} %param.15) | copy-start | bytes 772
  35.9 2.1 %collective-permute-start.10 = (f32[4,128]{1,0:T(4,128)S(1)}, f32[4,128]{1,0:T(4,128)S(1)}, u32[]{:S(2)}, u32[]{:S(2)}) collective-permute-start(f32[4,128]{1,0:T(4,128)S(1)} %get-tuple-element.21), channel_id=1, source_target_pairs={{0,1},{1,0},{2,3},{3,2},{4,5},{5,4},{6,7},{7,6},{8,9},{9,8},{10,11... | collective-permute-start | bytes 6152 | tf_op jit(solution)/shard_map/ppermute | solution.py:27
  36.0 3.7 %collective-permute-start.11 = (f32[4,128]{1,0:T(4,128)S(1)}, f32[4,128]{1,0:T(4,128)S(1)}, u32[]{:S(2)}, u32[]{:S(2)}) collective-permute-start(f32[4,128]{1,0:T(4,128)S(1)} %get-tuple-element.23), channel_id=1, source_target_pairs={{0,2},{2,0},{4,6},{6,4},{8,10},{10,8},{12,14},{14,12},{1,3},{3,1},... | collective-permute-start | bytes 6152 | tf_op jit(solution)/shard_map/ppermute | solution.py:27
  36.8 3.0 %collective-permute-start.12 = (f32[4,128]{1,0:T(4,128)S(1)}, f32[4,128]{1,0:T(4,128)S(1)}, u32[]{:S(2)}, u32[]{:S(2)}) collective-permute-start(f32[4,128]{1,0:T(4,128)S(1)} %get-tuple-element.22), channel_id=1, source_target_pairs={{0,3},{1,2},{2,1},{3,0},{4,7},{5,6},{6,5},{7,4},{8,11},{9,10},{10,... | collective-permute-start | bytes 6152 | tf_op jit(solution)/shard_map/ppermute | solution.py:33

commit v25 on v23

--- a/solution.py
+++ b/solution.py
@@ -183,6 +183,7 @@
     tile = unfolded(r_ref, height)
     out_ref[...] = prev_ref[...]
 
+    sums = []
     for group in range(number_ref.shape[0] // (3 * wide)):
         score = lax.dot_general(
             qv[wide * group * LANES : wide * (group + 1) * LANES, :],
@@ -198,8 +199,10 @@
                 part = score[side * LANES : (side + 1) * LANES, c * LANES : (c + 1) * LANES]
                 bias = jnp.where(ids[c] == cluster, 0.0, other[c]) - offset
                 acc = acc + jnp.exp2(part * scale + bias)
-            row = pl.ds(slot_ref[entry], 1)
-            out_ref[row, :] = out_ref[row, :] + jnp.sum(acc.T, axis=0, keepdims=True)
+            sums.append(jnp.sum(acc.T, axis=0, keepdims=True))
+    for entry, total in enumerate(sums):
+        row = pl.ds(slot_ref[entry], 1)
+        out_ref[row, :] = out_ref[row, :] + total
 
 
 def first_call(chunks, qblocks, pieces, wide, given, payloads):
@@ -306,7 +309,7 @@
 
     given = (beta, *queries, *q_tables)
     totals, packed, *plan = first_call(chunks, qblocks, pieces, 4, given, held[:-1])
-    totals = last_call(chunks, 4, *plan, packed, totals, held[-1])
+    totals = last_call(chunks, 2, *plan, packed, totals, held[-1])
     totals = totals[: 4 * qblocks]
     totals = totals.reshape(4, qblocks, LANES)
     total = totals[0] + swap(totals[1], "helper") + swap(totals[2], "blk") + swap_both(totals[3])

time: 40.6 us -> 40.6 us (level)
  no operation moved by 1% of the time
where the time goes in v25:
time: 40.6 us; the launch traced here: 40.4 us
  starting transfers between devices  14.7 us (36%)
  waiting for transfers between devices  13 us (32%)
  Pallas kernels  7.27 us (18%)
  local copies, waits for them, and re-layouts  3.21 us (8%)
  between operations  1.41 us (3%)
  other arithmetic  0.85 us (2%)
    ppermute x8, waiting for transfers between devices, swap(): return lax.ppermute(value, axis, [(i, i ^ 1) for i in range(length)])  11.3 us
    ppermute x3, starting transfers between devices, trade(): return lax.ppermute(value, 'blk', [(i, i ^ mask) for i in range(length)])  7.8 us
    ppermute x8, starting transfers between devices, swap(): return lax.ppermute(value, axis, [(i, i ^ 1) for i in range(length)])  5.47 us
    pallas_call x1, Pallas kernels, first_call(): pl.pallas_call(functools.partial(first_kernel, chunks, qblocks, pieces, w...  4.9 us
    unnamed x12, local copies, waits for them, and re-layouts  3.12 us
    pallas_call x1, Pallas kernels, last_call(): pl.pallas_call(functools.partial(last_kernel, chunks, wide), out_shape=ja...  1.7 us
    ppermute x3, waiting for transfers between devices, trade(): return lax.ppermute(value, 'blk', [(i, i ^ mask) for i in range(length)])  1.58 us
    ppermute x2, starting transfers between devices, swap_both(): return lax.ppermute(value, ('blk', 'helper'), pairs)  1.39 us
  transfers between devices with their start and end apart: 13, of which 8 were waited for; matrix products, arithmetic and copies ran while one was open for 1% of the time, Pallas kernels for 14%

profile of v25, /device:TPU:0, one launch (start us, length us, event | category | flops | bytes accessed | tf_op | source)
XLA Modules:
  0.0 40.4 jit_solution(6203667301936256313)
XLA Ops:
  0.0 3.0 %collective-permute-start.1 = (bf16[512,768]{1,0:T(8,128)(2,1)}, bf16[512,768]{1,0:T(8,128)(2,1)S(1)}, u32[]{:S(2)}, u32[]{:S(2)}) collective-permute-start(bf16[512,768]{1,0:T(8,128)(2,1)} %refs_0_.1), channel_id=1, source_target_pairs={{0,2},{2,0},{4,6},{6,4},{8,10},{10,8},{12,14},{14,12},{1,3},{3,1},... | collective-permute-start | bytes 2359304 | tf_op jit(solution)/shard_map/ppermute | solution.py:27
  3.7 0.7 %copy-done.2 = s32[512]{0:T(512)S(1)} copy-done((s32[512]{0:T(512)S(1)}, s32[512]{0:T(512)}, u32[]{:S(2)}) %copy-start.2) | copy-done | bytes 2072
  4.4 3.7 %collective-permute-start.2 = (bf16[1552,128]{1,0:T(8,128)(2,1)S(1)}, bf16[1552,128]{1,0:T(8,128)(2,1)S(1)}, u32[]{:S(2)}, u32[]{:S(2)}) collective-permute-start(bf16[1552,128]{1,0:T(8,128)(2,1)S(1)} %shard_map.83.refs_9_), channel_id=1, source_target_pairs={{0,12},{2,14},{4,8},{6,10},{8,4},{10,6},{12,0},{14,2},{1,13},{3,15... | collective-permute-start | bytes 1191944 | tf_op jit(solution)/shard_map/ppermute | solution.py:22
  8.1 1.1 %copy-done.1 = bf16[512,768]{1,0:T(8,128)(2,1)S(1)} copy-done((bf16[512,768]{1,0:T(8,128)(2,1)S(1)}, bf16[512,768]{1,0:T(8,128)(2,1)}, u32[]{:S(2)}) %copy-start.1) | copy-done | bytes 786456
  9.2 0.7 %copy-done.4 = f32[64]{0:T(128)S(1)} copy-done((f32[64]{0:T(128)S(1)}, f32[64]{0:T(128)}, u32[]{:S(2)}) %copy-start.4) | copy-done | bytes 280
  10.6 0.6 %copy-done.3 = s32[4]{0:T(128)S(1)} copy-done((s32[4]{0:T(128)S(1)}, s32[4]{0:T(128)}, u32[]{:S(2)}) %copy-start.3) | copy-done | bytes 40
  11.3 0.5 %shard_map.84.refs_5_ = s32[8,128]{1,0:T(8,128)S(1)} custom-call(s32[4]{0:T(128)S(1)} %copy-done.3, s32[1]{0:T(128)S(6)} %copy.12.count_ref), custom_call_target="tpu_custom_call" | custom-call | flops 1 | bytes 1 | tf_op jit(solution)/shard_map/pallas_call | solution.py:295
  11.8 0.6 %collective-permute-start.4 = (s32[8,128]{1,0:T(8,128)S(1)}, s32[8,128]{1,0:T(8,128)S(1)}, u32[]{:S(2)}, u32[]{:S(2)}) collective-permute-start(s32[8,128]{1,0:T(8,128)S(1)} %shard_map.84.refs_5_), channel_id=1, source_target_pairs={{0,1},{1,0},{2,3},{3,2},{4,5},{5,4},{6,7},{7,6},{8,9},{9,8},{10,11... | collective-permute-start | bytes 12296 | tf_op jit(solution)/shard_map/ppermute | solution.py:27
  12.4 0.8 %collective-permute-done.4.refs_6_ = s32[8,128]{1,0:T(8,128)S(1)} collective-permute-done((s32[8,128]{1,0:T(8,128)S(1)}, s32[8,128]{1,0:T(8,128)S(1)}, u32[]{:S(2)}, u32[]{:S(2)}) %collective-permute-start.4) | collective-permute-done | bytes 4128 | tf_op jit(solution)/shard_map/ppermute | solution.py:27
  13.2 0.5 %collective-permute-start.5 = (s32[8,128]{1,0:T(8,128)S(1)}, s32[8,128]{1,0:T(8,128)S(1)}, u32[]{:S(2)}, u32[]{:S(2)}) collective-permute-start(s32[8,128]{1,0:T(8,128)S(1)} %shard_map.84.refs_5_), channel_id=1, source_target_pairs={{0,2},{2,0},{4,6},{6,4},{8,10},{10,8},{12,14},{14,12},{1,3},{3,1},... | collective-permute-start | bytes 12296 | tf_op jit(solution)/shard_map/ppermute | solution.py:27
  13.7 7.1 %collective-permute-done.5.refs_7_ = s32[8,128]{1,0:T(8,128)S(1)} collective-permute-done((s32[8,128]{1,0:T(8,128)S(1)}, s32[8,128]{1,0:T(8,128)S(1)}, u32[]{:S(2)}, u32[]{:S(2)}) %collective-permute-start.5) | collective-permute-done | bytes 4128 | tf_op jit(solution)/shard_map/ppermute | solution.py:27
  20.8 0.3 collective-permute-start.6
  21.1 4.1 %collective-permute-start.9 = (bf16[1552,128]{1,0:T(8,128)(2,1)S(1)}, bf16[1552,128]{1,0:T(8,128)(2,1)S(1)}, u32[]{:S(2)}, u32[]{:S(2)}) collective-permute-start(bf16[1552,128]{1,0:T(8,128)(2,1)S(1)} %collective-permute-done.2.refs_10_), channel_id=1, source_target_pairs={{0,4},{2,6},{4,0},{6,2},{8,12},{10,14},{12,8},{14,10},{1,5},{3,7},... | collective-permute-start | bytes 1191944 | tf_op jit(solution)/shard_map/ppermute | solution.py:22
  25.3 0.5 %collective-permute-done.3.refs_11_ = bf16[1552,128]{1,0:T(8,128)(2,1)S(1)} collective-permute-done((bf16[1552,128]{1,0:T(8,128)(2,1)S(1)}, bf16[1552,128]{1,0:T(8,128)(2,1)S(1)}, u32[]{:S(2)}, u32[]{:S(2)}) %collective-permute-start.3) | collective-permute-done | bytes 397344 | tf_op jit(solution)/shard_map/ppermute | solution.py:22
  25.9 0.5 %collective-permute-start.8 = (bf16[256,768]{1,0:T(8,128)(2,1)S(1)}, bf16[256,768]{1,0:T(8,128)(2,1)S(1)}, u32[]{:S(2)}, u32[]{:S(2)}) collective-permute-start(bf16[256,768]{1,0:T(8,128)(2,1)S(1)} %get-tuple-element.21), channel_id=1, source_target_pairs={{0,1},{1,0},{2,3},{3,2},{4,5},{5,4},{6,7},{7,6},{8,9},{9,8},{10,11... | collective-permute-start | bytes 1179656 | tf_op jit(solution)/shard_map/ppermute | solution.py:27
  26.4 1.2 %collective-permute-done.7.refs_3_ = bf16[256,768]{1,0:T(8,128)(2,1)S(1)} collective-permute-done((bf16[256,768]{1,0:T(8,128)(2,1)S(1)}, bf16[256,768]{1,0:T(8,128)(2,1)S(1)}, u32[]{:S(2)}, u32[]{:S(2)}) %collective-permute-start.7) | collective-permute-done | bytes 393248 | tf_op jit(solution)/shard_map/ppermute | solution.py:27
  27.6 0.6 %collective-permute-done.8.refs_4_ = bf16[256,768]{1,0:T(8,128)(2,1)S(1)} collective-permute-done((bf16[256,768]{1,0:T(8,128)(2,1)S(1)}, bf16[256,768]{1,0:T(8,128)(2,1)S(1)}, u32[]{:S(2)}, u32[]{:S(2)}) %collective-permute-start.8) | collective-permute-done | bytes 393248 | tf_op jit(solution)/shard_map/ppermute | solution.py:27
  28.1 4.9 %shard_map.85 = (f32[24,128]{1,0:T(8,128)S(1)}, bf16[2048,768]{1,0:T(8,128)(2,1)S(1)}, s32[24]{0:T(128)S(1)}, f32[48]{0:T(128)S(1)}) custom-call(f32[1,64]{1,0:T(1,128)S(1)} %get-tuple-element.13.beta_ref, bf16[512,768]{1,0:T(8,128)(2,1)S(1)} %get-tuple-element.14.refs_0_, bf16[512,768]{1,0:T(8,128)(2,1)S(1)} %collective-permute-done.refs_1_, ...), custom_call_target="tpu_custom_call" | custom-call | flops 1 | bytes 1 | tf_op jit(solution)/shard_map/pallas_call | solution.py:212
  33.1 1.1 %collective-permute-done.9.r_ref = bf16[1552,128]{1,0:T(8,128)(2,1)S(1)} collective-permute-done((bf16[1552,128]{1,0:T(8,128)(2,1)S(1)}, bf16[1552,128]{1,0:T(8,128)(2,1)S(1)}, u32[]{:S(2)}, u32[]{:S(2)}) %collective-permute-start.9) | collective-permute-done | bytes 397344 | tf_op jit(solution)/shard_map/ppermute | solution.py:22
  34.2 1.7 %shard_map.86 = f32[24,128]{1,0:T(8,128)S(1)} custom-call(s32[24]{0:T(128)S(1)} %get-tuple-element.17.slot_ref, f32[48]{0:T(128)S(1)} %get-tuple-element.18.number_ref, bf16[2048,768]{1,0:T(8,128)(2,1)S(1)} %get-tuple-element.19.qv, f32[24,128]{1,0:T(8,128)S(1)} %get-tuple-element.20.prev_ref, bf16[1552,128]{1,0:T(8,128)(2,1)S(1)} %collective-permute-done.9.r_ref), custom_call_target="tpu_custom_call" | custom-call | flops 1 | bytes 1 | tf_op jit(solution)/shard_map/pallas_call | solution.py:235
  35.9 0.8 %collective-permute-start.11 = (f32[4,128]{1,0:T(4,128)S(1)}, f32[4,128]{1,0:T(4,128)S(1)}, u32[]{:S(2)}, u32[]{:S(2)}) collective-permute-start(f32[4,128]{1,0:T(4,128)S(1)} %get-tuple-element.25), channel_id=1, source_target_pairs={{0,2},{2,0},{4,6},{6,4},{8,10},{10,8},{12,14},{14,12},{1,3},{3,1},... | collective-permute-start | bytes 6152 | tf_op jit(solution)/shard_map/ppermute | solution.py:27
  36.7 1.1 %collective-permute-start.12 = (f32[4,128]{1,0:T(4,128)S(1)}, f32[4,128]{1,0:T(4,128)S(1)}, u32[]{:S(2)}, u32[]{:S(2)}) collective-permute-start(f32[4,128]{1,0:T(4,128)S(1)} %get-tuple-element.24), channel_id=1, source_target_pairs={{0,3},{1,2},{2,1},{3,0},{4,7},{5,6},{6,5},{7,4},{8,11},{9,10},{10,... | collective-permute-start | bytes 6152 | tf_op jit(solution)/shard_map/ppermute | solution.py:33
  38.0 1.6 %collective-permute-done.11 = f32[4,128]{1,0:T(4,128)S(1)} collective-permute-done((f32[4,128]{1,0:T(4,128)S(1)}, f32[4,128]{1,0:T(4,128)S(1)}, u32[]{:S(2)}, u32[]{:S(2)}) %collective-permute-start.11) | collective-permute-done | bytes 2080 | tf_op jit(solution)/shard_map/ppermute | solution.py:27
  39.7 0.7 %log-plus-one_bitcast_fusion = f32[512]{0:T(512)} fusion(f32[4,128]{1,0:T(4,128)S(1)} %collective-permute-done.12, f32[4,128]{1,0:T(4,128)S(1)} %collective-permute-done.11, f32[4,128]{1,0:T(4,128)S(1)} %collective-permute-done.10, f32[24,128]{1,0:T(8,128)S(1)} %shard_map.86, f32[4]{0:T(128)S(1)} %convert_element_type.7), kind=kLoop, calls=%fused_computation.4 | loop fusion | flops 2048 | bytes 10256 | tf_op jit(solution)/shard_map/reshape | solution.py:320
  (25 shorter events, 0.7 us)
Async XLA Ops:
  0.0 3.6 %copy-start = (bf16[512,768]{1,0:T(8,128)(2,1)S(1)}, bf16[512,768]{1,0:T(8,128)(2,1)}, u32[]{:S(2)}) copy-start(bf16[512,768]{1,0:T(8,128)(2,1)} %param.11) | copy-start | bytes 2359300
  0.0 25.7 %collective-permute-start.1 = (bf16[512,768]{1,0:T(8,128)(2,1)}, bf16[512,768]{1,0:T(8,128)(2,1)S(1)}, u32[]{:S(2)}, u32[]{:S(2)}) collective-permute-start(bf16[512,768]{1,0:T(8,128)(2,1)} %refs_0_.1), channel_id=1, source_target_pairs={{0,2},{2,0},{4,6},{6,4},{8,10},{10,8},{12,14},{14,12},{1,3},{3,1},... | collective-permute-start | bytes 2359304 | tf_op jit(solution)/shard_map/ppermute | solution.py:27
  3.7 0.7 %copy-start.2 = (s32[512]{0:T(512)S(1)}, s32[512]{0:T(512)}, u32[]{:S(2)}) copy-start(s32[512]{0:T(512)} %param.12) | copy-start | bytes 6148
  4.4 16.7 %collective-permute-start.2 = (bf16[1552,128]{1,0:T(8,128)(2,1)S(1)}, bf16[1552,128]{1,0:T(8,128)(2,1)S(1)}, u32[]{:S(2)}, u32[]{:S(2)}) collective-permute-start(bf16[1552,128]{1,0:T(8,128)(2,1)S(1)} %shard_map.83.refs_9_), channel_id=1, source_target_pairs={{0,12},{2,14},{4,8},{6,10},{8,4},{10,6},{12,0},{14,2},{1,13},{3,15... | collective-permute-start | bytes 1191944 | tf_op jit(solution)/shard_map/ppermute | solution.py:22
  8.1 17.6 %collective-permute-start.3 = (bf16[1552,128]{1,0:T(8,128)(2,1)S(1)}, bf16[1552,128]{1,0:T(8,128)(2,1)S(1)}, u32[]{:S(2)}, u32[]{:S(2)}) collective-permute-start(bf16[1552,128]{1,0:T(8,128)(2,1)S(1)} %shard_map.83.refs_9_), channel_id=1, source_target_pairs={{0,4},{2,6},{4,0},{6,2},{8,12},{10,14},{12,8},{14,10},{1,5},{3,7},... | collective-permute-start | bytes 1191944 | tf_op jit(solution)/shard_map/ppermute | solution.py:22
  8.1 18.3 %collective-permute-start = (bf16[512,768]{1,0:T(8,128)(2,1)}, bf16[512,768]{1,0:T(8,128)(2,1)S(1)}, u32[]{:S(2)}, u32[]{:S(2)}) collective-permute-start(bf16[512,768]{1,0:T(8,128)(2,1)} %refs_0_.1), channel_id=1, source_target_pairs={{0,1},{1,0},{2,3},{3,2},{4,5},{5,4},{6,7},{7,6},{8,9},{9,8},{10,11... | collective-permute-start | bytes 2359304 | tf_op jit(solution)/shard_map/ppermute | solution.py:27
  8.1 1.1 %copy-start.1 = (bf16[512,768]{1,0:T(8,128)(2,1)S(1)}, bf16[512,768]{1,0:T(8,128)(2,1)}, u32[]{:S(2)}) copy-start(bf16[512,768]{1,0:T(8,128)(2,1)} %refs_0_.1) | copy-start | bytes 2359300
  9.2 0.7 %copy-start.4 = (f32[64]{0:T(128)S(1)}, f32[64]{0:T(128)}, u32[]{:S(2)}) copy-start(f32[64]{0:T(128)} %param.14) | copy-start | bytes 772
  10.6 0.7 %copy-start.3 = (s32[4]{0:T(128)S(1)}, s32[4]{0:T(128)}, u32[]{:S(2)}) copy-start(s32[4]{0:T(128)} %clusters_ref) | copy-start | bytes 52
  11.8 1.4 %collective-permute-start.4 = (s32[8,128]{1,0:T(8,128)S(1)}, s32[8,128]{1,0:T(8,128)S(1)}, u32[]{:S(2)}, u32[]{:S(2)}) collective-permute-start(s32[8,128]{1,0:T(8,128)S(1)} %shard_map.84.refs_5_), channel_id=1, source_target_pairs={{0,1},{1,0},{2,3},{3,2},{4,5},{5,4},{6,7},{7,6},{8,9},{9,8},{10,11... | collective-permute-start | bytes 12296 | tf_op jit(solution)/shard_map/ppermute | solution.py:27
  13.2 7.6 %collective-permute-start.5 = (s32[8,128]{1,0:T(8,128)S(1)}, s32[8,128]{1,0:T(8,128)S(1)}, u32[]{:S(2)}, u32[]{:S(2)}) collective-permute-start(s32[8,128]{1,0:T(8,128)S(1)} %shard_map.84.refs_5_), channel_id=1, source_target_pairs={{0,2},{2,0},{4,6},{6,4},{8,10},{10,8},{12,14},{14,12},{1,3},{3,1},... | collective-permute-start | bytes 12296 | tf_op jit(solution)/shard_map/ppermute | solution.py:27
  20.8 4.5 %collective-permute-start.6 = (s32[8,128]{1,0:T(8,128)S(1)}, s32[8,128]{1,0:T(8,128)S(1)}, u32[]{:S(2)}, u32[]{:S(2)}) collective-permute-start(s32[8,128]{1,0:T(8,128)S(1)} %shard_map.84.refs_5_), channel_id=1, source_target_pairs={{0,3},{1,2},{2,1},{3,0},{4,7},{5,6},{6,5},{7,4},{8,11},{9,10},{10,... | collective-permute-start | bytes 12296 | tf_op jit(solution)/shard_map/ppermute | solution.py:33
  21.1 13.0 %collective-permute-start.9 = (bf16[1552,128]{1,0:T(8,128)(2,1)S(1)}, bf16[1552,128]{1,0:T(8,128)(2,1)S(1)}, u32[]{:S(2)}, u32[]{:S(2)}) collective-permute-start(bf16[1552,128]{1,0:T(8,128)(2,1)S(1)} %collective-permute-done.2.refs_10_), channel_id=1, source_target_pairs={{0,4},{2,6},{4,0},{6,2},{8,12},{10,14},{12,8},{14,10},{1,5},{3,7},... | collective-permute-start | bytes 1191944 | tf_op jit(solution)/shard_map/ppermute | solution.py:22
  25.8 1.8 %collective-permute-start.7 = (bf16[256,768]{1,0:T(8,128)(2,1)S(1)}, bf16[256,768]{1,0:T(8,128)(2,1)S(1)}, u32[]{:S(2)}, u32[]{:S(2)}) collective-permute-start(bf16[256,768]{1,0:T(8,128)(2,1)S(1)} %get-tuple-element.22), channel_id=1, source_target_pairs={{0,1},{1,0},{2,3},{3,2},{4,5},{5,4},{6,7},{7,6},{8,9},{9,8},{10,11... | collective-permute-start | bytes 1179656 | tf_op jit(solution)/shard_map/ppermute | solution.py:27
  25.9 2.3 %collective-permute-start.8 = (bf16[256,768]{1,0:T(8,128)(2,1)S(1)}, bf16[256,768]{1,0:T(8,128)(2,1)S(1)}, u32[]{:S(2)}, u32[]{:S(2)}) collective-permute-start(bf16[256,768]{1,0:T(8,128)(2,1)S(1)} %get-tuple-element.21), channel_id=1, source_target_pairs={{0,1},{1,0},{2,3},{3,2},{4,5},{5,4},{6,7},{7,6},{8,9},{9,8},{10,11... | collective-permute-start | bytes 1179656 | tf_op jit(solution)/shard_map/ppermute | solution.py:27
  28.1 9.7 %copy-start.5 = (s32[64]{0:T(128)S(1)}, s32[64]{0:T(128)}, u32[]{:S(2)}) copy-start(s32[64]{0:T(128)} %param.15) | copy-start | bytes 772
  35.9 2.1 %collective-permute-start.10 = (f32[4,128]{1,0:T(4,128)S(1)}, f32[4,128]{1,0:T(4,128)S(1)}, u32[]{:S(2)}, u32[]{:S(2)}) collective-permute-start(f32[4,128]{1,0:T(4,128)S(1)} %get-tuple-element.23), channel_id=1, source_target_pairs={{0,1},{1,0},{2,3},{3,2},{4,5},{5,4},{6,7},{7,6},{8,9},{9,8},{10,11... | collective-permute-start | bytes 6152 | tf_op jit(solution)/shard_map/ppermute | solution.py:27
  35.9 3.7 %collective-permute-start.11 = (f32[4,128]{1,0:T(4,128)S(1)}, f32[4,128]{1,0:T(4,128)S(1)}, u32[]{:S(2)}, u32[]{:S(2)}) collective-permute-start(f32[4,128]{1,0:T(4,128)S(1)} %get-tuple-element.25), channel_id=1, source_target_pairs={{0,2},{2,0},{4,6},{6,4},{8,10},{10,8},{12,14},{14,12},{1,3},{3,1},... | collective-permute-start | bytes 6152 | tf_op jit(solution)/shard_map/ppermute | solution.py:27
  36.7 3.0 %collective-permute-start.12 = (f32[4,128]{1,0:T(4,128)S(1)}, f32[4,128]{1,0:T(4,128)S(1)}, u32[]{:S(2)}, u32[]{:S(2)}) collective-permute-start(f32[4,128]{1,0:T(4,128)S(1)} %get-tuple-element.24), channel_id=1, source_target_pairs={{0,3},{1,2},{2,1},{3,0},{4,7},{5,6},{6,5},{7,4},{8,11},{9,10},{10,... | collective-permute-start | bytes 6152 | tf_op jit(solution)/shard_map/ppermute | solution.py:33

commit v26 on v23

--- a/solution.py
+++ b/solution.py
@@ -305,7 +305,7 @@
     pieces = (1, 1, 1, 2)
 
     given = (beta, *queries, *q_tables)
-    totals, packed, *plan = first_call(chunks, qblocks, pieces, 4, given, held[:-1])
+    totals, packed, *plan = first_call(chunks, qblocks, pieces, 2, given, held[:-1])
     totals = last_call(chunks, 4, *plan, packed, totals, held[-1])
     totals = totals[: 4 * qblocks]
     totals = totals.reshape(4, qblocks, LANES)

time: 40.6 us -> 40.6 us (level)
  no operation moved by 1% of the time
where the time goes in v26:
time: 40.6 us; the launch traced here: 40.4 us
  starting transfers between devices  14.7 us (36%)
  waiting for transfers between devices  12.9 us (32%)
  Pallas kernels  7.44 us (18%)
  local copies, waits for them, and re-layouts  3.21 us (8%)
  between operations  1.41 us (3%)
  other arithmetic  0.85 us (2%)
    ppermute x8, waiting for transfers between devices, swap(): return lax.ppermute(value, axis, [(i, i ^ 1) for i in range(length)])  11.3 us
    ppermute x3, starting transfers between devices, trade(): return lax.ppermute(value, 'blk', [(i, i ^ mask) for i in range(length)])  7.8 us
    ppermute x8, starting transfers between devices, swap(): return lax.ppermute(value, axis, [(i, i ^ 1) for i in range(length)])  5.49 us
    pallas_call x1, Pallas kernels, first_call(): pl.pallas_call(functools.partial(first_kernel, chunks, qblocks, pieces, w...  5.06 us
    unnamed x12, local copies, waits for them, and re-layouts  3.12 us
    pallas_call x1, Pallas kernels, last_call(): pl.pallas_call(functools.partial(last_kernel, chunks, wide), out_shape=ja...  1.7 us
    ppermute x3, waiting for transfers between devices, trade(): return lax.ppermute(value, 'blk', [(i, i ^ mask) for i in range(length)])  1.41 us
    ppermute x2, starting transfers between devices, swap_both(): return lax.ppermute(value, ('blk', 'helper'), pairs)  1.37 us
  transfers between devices with their start and end apart: 13, of which 8 were waited for; matrix products, arithmetic and copies ran while one was open for 1% of the time, Pallas kernels for 14%

profile of v26, /device:TPU:0, one launch (start us, length us, event | category | flops | bytes accessed | tf_op | source)
XLA Modules:
  0.0 40.4 jit_solution(4105733433180440743)
XLA Ops:
  0.0 3.0 %collective-permute-start.1 = (bf16[512,768]{1,0:T(8,128)(2,1)}, bf16[512,768]{1,0:T(8,128)(2,1)S(1)}, u32[]{:S(2)}, u32[]{:S(2)}) collective-permute-start(bf16[512,768]{1,0:T(8,128)(2,1)} %refs_0_.1), channel_id=1, source_target_pairs={{0,2},{2,0},{4,6},{6,4},{8,10},{10,8},{12,14},{14,12},{1,3},{3,1},... | collective-permute-start | bytes 2359304 | tf_op jit(solution)/shard_map/ppermute | solution.py:27
  3.7 0.7 %copy-done.2 = s32[512]{0:T(512)S(1)} copy-done((s32[512]{0:T(512)S(1)}, s32[512]{0:T(512)}, u32[]{:S(2)}) %copy-start.2) | copy-done | bytes 2072
  4.4 3.7 %collective-permute-start.2 = (bf16[1552,128]{1,0:T(8,128)(2,1)S(1)}, bf16[1552,128]{1,0:T(8,128)(2,1)S(1)}, u32[]{:S(2)}, u32[]{:S(2)}) collective-permute-start(bf16[1552,128]{1,0:T(8,128)(2,1)S(1)} %shard_map.83.refs_9_), channel_id=1, source_target_pairs={{0,12},{2,14},{4,8},{6,10},{8,4},{10,6},{12,0},{14,2},{1,13},{3,15... | collective-permute-start | bytes 1191944 | tf_op jit(solution)/shard_map/ppermute | solution.py:22
  8.1 1.1 %copy-done.1 = bf16[512,768]{1,0:T(8,128)(2,1)S(1)} copy-done((bf16[512,768]{1,0:T(8,128)(2,1)S(1)}, bf16[512,768]{1,0:T(8,128)(2,1)}, u32[]{:S(2)}) %copy-start.1) | copy-done | bytes 786456
  9.2 0.7 %copy-done.4 = f32[64]{0:T(128)S(1)} copy-done((f32[64]{0:T(128)S(1)}, f32[64]{0:T(128)}, u32[]{:S(2)}) %copy-start.4) | copy-done | bytes 280
  10.6 0.6 %copy-done.3 = s32[4]{0:T(128)S(1)} copy-done((s32[4]{0:T(128)S(1)}, s32[4]{0:T(128)}, u32[]{:S(2)}) %copy-start.3) | copy-done | bytes 40
  11.3 0.5 %shard_map.84.refs_5_ = s32[8,128]{1,0:T(8,128)S(1)} custom-call(s32[4]{0:T(128)S(1)} %copy-done.3, s32[1]{0:T(128)S(6)} %copy.12.count_ref), custom_call_target="tpu_custom_call" | custom-call | flops 1 | bytes 1 | tf_op jit(solution)/shard_map/pallas_call | solution.py:292
  11.8 0.6 %collective-permute-start.4 = (s32[8,128]{1,0:T(8,128)S(1)}, s32[8,128]{1,0:T(8,128)S(1)}, u32[]{:S(2)}, u32[]{:S(2)}) collective-permute-start(s32[8,128]{1,0:T(8,128)S(1)} %shard_map.84.refs_5_), channel_id=1, source_target_pairs={{0,1},{1,0},{2,3},{3,2},{4,5},{5,4},{6,7},{7,6},{8,9},{9,8},{10,11... | collective-permute-start | bytes 12296 | tf_op jit(solution)/shard_map/ppermute | solution.py:27
  12.4 0.8 %collective-permute-done.4.refs_6_ = s32[8,128]{1,0:T(8,128)S(1)} collective-permute-done((s32[8,128]{1,0:T(8,128)S(1)}, s32[8,128]{1,0:T(8,128)S(1)}, u32[]{:S(2)}, u32[]{:S(2)}) %collective-permute-start.4) | collective-permute-done | bytes 4128 | tf_op jit(solution)/shard_map/ppermute | solution.py:27
  13.2 0.5 %collective-permute-start.5 = (s32[8,128]{1,0:T(8,128)S(1)}, s32[8,128]{1,0:T(8,128)S(1)}, u32[]{:S(2)}, u32[]{:S(2)}) collective-permute-start(s32[8,128]{1,0:T(8,128)S(1)} %shard_map.84.refs_5_), channel_id=1, source_target_pairs={{0,2},{2,0},{4,6},{6,4},{8,10},{10,8},{12,14},{14,12},{1,3},{3,1},... | collective-permute-start | bytes 12296 | tf_op jit(solution)/shard_map/ppermute | solution.py:27
  13.7 7.1 %collective-permute-done.5.refs_7_ = s32[8,128]{1,0:T(8,128)S(1)} collective-permute-done((s32[8,128]{1,0:T(8,128)S(1)}, s32[8,128]{1,0:T(8,128)S(1)}, u32[]{:S(2)}, u32[]{:S(2)}) %collective-permute-start.5) | collective-permute-done | bytes 4128 | tf_op jit(solution)/shard_map/ppermute | solution.py:27
  20.8 0.3 collective-permute-start.6
  21.1 4.1 %collective-permute-start.9 = (bf16[1552,128]{1,0:T(8,128)(2,1)S(1)}, bf16[1552,128]{1,0:T(8,128)(2,1)S(1)}, u32[]{:S(2)}, u32[]{:S(2)}) collective-permute-start(bf16[1552,128]{1,0:T(8,128)(2,1)S(1)} %collective-permute-done.2.refs_10_), channel_id=1, source_target_pairs={{0,4},{2,6},{4,0},{6,2},{8,12},{10,14},{12,8},{14,10},{1,5},{3,7},... | collective-permute-start | bytes 1191944 | tf_op jit(solution)/shard_map/ppermute | solution.py:22
  25.3 0.5 %collective-permute-done.3.refs_11_ = bf16[1552,128]{1,0:T(8,128)(2,1)S(1)} collective-permute-done((bf16[1552,128]{1,0:T(8,128)(2,1)S(1)}, bf16[1552,128]{1,0:T(8,128)(2,1)S(1)}, u32[]{:S(2)}, u32[]{:S(2)}) %collective-permute-start.3) | collective-permute-done | bytes 397344 | tf_op jit(solution)/shard_map/ppermute | solution.py:22
  25.9 0.5 %collective-permute-start.8 = (bf16[256,768]{1,0:T(8,128)(2,1)S(1)}, bf16[256,768]{1,0:T(8,128)(2,1)S(1)}, u32[]{:S(2)}, u32[]{:S(2)}) collective-permute-start(bf16[256,768]{1,0:T(8,128)(2,1)S(1)} %get-tuple-element.21), channel_id=1, source_target_pairs={{0,1},{1,0},{2,3},{3,2},{4,5},{5,4},{6,7},{7,6},{8,9},{9,8},{10,11... | collective-permute-start | bytes 1179656 | tf_op jit(solution)/shard_map/ppermute | solution.py:27
  26.4 1.2 %collective-permute-done.7.refs_3_ = bf16[256,768]{1,0:T(8,128)(2,1)S(1)} collective-permute-done((bf16[256,768]{1,0:T(8,128)(2,1)S(1)}, bf16[256,768]{1,0:T(8,128)(2,1)S(1)}, u32[]{:S(2)}, u32[]{:S(2)}) %collective-permute-start.7) | collective-permute-done | bytes 393248 | tf_op jit(solution)/shard_map/ppermute | solution.py:27
  27.6 0.6 %collective-permute-done.8.refs_4_ = bf16[256,768]{1,0:T(8,128)(2,1)S(1)} collective-permute-done((bf16[256,768]{1,0:T(8,128)(2,1)S(1)}, bf16[256,768]{1,0:T(8,128)(2,1)S(1)}, u32[]{:S(2)}, u32[]{:S(2)}) %collective-permute-start.8) | collective-permute-done | bytes 393248 | tf_op jit(solution)/shard_map/ppermute | solution.py:27
  28.1 5.1 %shard_map.85 = (f32[24,128]{1,0:T(8,128)S(1)}, bf16[2048,768]{1,0:T(8,128)(2,1)S(1)}, s32[24]{0:T(128)S(1)}, f32[48]{0:T(128)S(1)}) custom-call(f32[1,64]{1,0:T(1,128)S(1)} %get-tuple-element.13.beta_ref, bf16[512,768]{1,0:T(8,128)(2,1)S(1)} %get-tuple-element.14.refs_0_, bf16[512,768]{1,0:T(8,128)(2,1)S(1)} %collective-permute-done.refs_1_, ...), custom_call_target="tpu_custom_call" | custom-call | flops 1 | bytes 1 | tf_op jit(solution)/shard_map/pallas_call | solution.py:209
  33.2 0.9 %collective-permute-done.9.r_ref = bf16[1552,128]{1,0:T(8,128)(2,1)S(1)} collective-permute-done((bf16[1552,128]{1,0:T(8,128)(2,1)S(1)}, bf16[1552,128]{1,0:T(8,128)(2,1)S(1)}, u32[]{:S(2)}, u32[]{:S(2)}) %collective-permute-start.9) | collective-permute-done | bytes 397344 | tf_op jit(solution)/shard_map/ppermute | solution.py:22
  34.2 1.7 %shard_map.86 = f32[24,128]{1,0:T(8,128)S(1)} custom-call(s32[24]{0:T(128)S(1)} %get-tuple-element.17.slot_ref, f32[48]{0:T(128)S(1)} %get-tuple-element.18.number_ref, bf16[2048,768]{1,0:T(8,128)(2,1)S(1)} %get-tuple-element.19.qv, f32[24,128]{1,0:T(8,128)S(1)} %get-tuple-element.20.prev_ref, bf16[1552,128]{1,0:T(8,128)(2,1)S(1)} %collective-permute-done.9.r_ref), custom_call_target="tpu_custom_call" | custom-call | flops 1 | bytes 1 | tf_op jit(solution)/shard_map/pallas_call | solution.py:232
  35.9 0.8 %collective-permute-start.11 = (f32[4,128]{1,0:T(4,128)S(1)}, f32[4,128]{1,0:T(4,128)S(1)}, u32[]{:S(2)}, u32[]{:S(2)}) collective-permute-start(f32[4,128]{1,0:T(4,128)S(1)} %get-tuple-element.25), channel_id=1, source_target_pairs={{0,2},{2,0},{4,6},{6,4},{8,10},{10,8},{12,14},{14,12},{1,3},{3,1},... | collective-permute-start | bytes 6152 | tf_op jit(solution)/shard_map/ppermute | solution.py:27
  36.7 1.1 %collective-permute-start.12 = (f32[4,128]{1,0:T(4,128)S(1)}, f32[4,128]{1,0:T(4,128)S(1)}, u32[]{:S(2)}, u32[]{:S(2)}) collective-permute-start(f32[4,128]{1,0:T(4,128)S(1)} %get-tuple-element.24), channel_id=1, source_target_pairs={{0,3},{1,2},{2,1},{3,0},{4,7},{5,6},{6,5},{7,4},{8,11},{9,10},{10,... | collective-permute-start | bytes 6152 | tf_op jit(solution)/shard_map/ppermute | solution.py:33
  38.0 1.6 %collective-permute-done.11 = f32[4,128]{1,0:T(4,128)S(1)} collective-permute-done((f32[4,128]{1,0:T(4,128)S(1)}, f32[4,128]{1,0:T(4,128)S(1)}, u32[]{:S(2)}, u32[]{:S(2)}) %collective-permute-start.11) | collective-permute-done | bytes 2080 | tf_op jit(solution)/shard_map/ppermute | solution.py:27
  39.8 0.7 %log-plus-one_bitcast_fusion = f32[512]{0:T(512)} fusion(f32[4,128]{1,0:T(4,128)S(1)} %collective-permute-done.12, f32[4,128]{1,0:T(4,128)S(1)} %collective-permute-done.11, f32[4,128]{1,0:T(4,128)S(1)} %collective-permute-done.10, f32[24,128]{1,0:T(8,128)S(1)} %shard_map.86, f32[4]{0:T(128)S(1)} %convert_element_type.7), kind=kLoop, calls=%fused_computation.4 | loop fusion | flops 2048 | bytes 10256 | tf_op jit(solution)/shard_map/reshape | solution.py:317
  (25 shorter events, 0.7 us)
Async XLA Ops:
  0.0 3.6 %copy-start = (bf16[512,768]{1,0:T(8,128)(2,1)S(1)}, bf16[512,768]{1,0:T(8,128)(2,1)}, u32[]{:S(2)}) copy-start(bf16[512,768]{1,0:T(8,128)(2,1)} %param.11) | copy-start | bytes 2359300
  0.0 25.7 %collective-permute-start.1 = (bf16[512,768]{1,0:T(8,128)(2,1)}, bf16[512,768]{1,0:T(8,128)(2,1)S(1)}, u32[]{:S(2)}, u32[]{:S(2)}) collective-permute-start(bf16[512,768]{1,0:T(8,128)(2,1)} %refs_0_.1), channel_id=1, source_target_pairs={{0,2},{2,0},{4,6},{6,4},{8,10},{10,8},{12,14},{14,12},{1,3},{3,1},... | collective-permute-start | bytes 2359304 | tf_op jit(solution)/shard_map/ppermute | solution.py:27
  3.7 0.7 %copy-start.2 = (s32[512]{0:T(512)S(1)}, s32[512]{0:T(512)}, u32[]{:S(2)}) copy-start(s32[512]{0:T(512)} %param.12) | copy-start | bytes 6148
  4.4 16.7 %collective-permute-start.2 = (bf16[1552,128]{1,0:T(8,128)(2,1)S(1)}, bf16[1552,128]{1,0:T(8,128)(2,1)S(1)}, u32[]{:S(2)}, u32[]{:S(2)}) collective-permute-start(bf16[1552,128]{1,0:T(8,128)(2,1)S(1)} %shard_map.83.refs_9_), channel_id=1, source_target_pairs={{0,12},{2,14},{4,8},{6,10},{8,4},{10,6},{12,0},{14,2},{1,13},{3,15... | collective-permute-start | bytes 1191944 | tf_op jit(solution)/shard_map/ppermute | solution.py:22
  8.1 17.6 %collective-permute-start.3 = (bf16[1552,128]{1,0:T(8,128)(2,1)S(1)}, bf16[1552,128]{1,0:T(8,128)(2,1)S(1)}, u32[]{:S(2)}, u32[]{:S(2)}) collective-permute-start(bf16[1552,128]{1,0:T(8,128)(2,1)S(1)} %shard_map.83.refs_9_), channel_id=1, source_target_pairs={{0,4},{2,6},{4,0},{6,2},{8,12},{10,14},{12,8},{14,10},{1,5},{3,7},... | collective-permute-start | bytes 1191944 | tf_op jit(solution)/shard_map/ppermute | solution.py:22
  8.1 18.3 %collective-permute-start = (bf16[512,768]{1,0:T(8,128)(2,1)}, bf16[512,768]{1,0:T(8,128)(2,1)S(1)}, u32[]{:S(2)}, u32[]{:S(2)}) collective-permute-start(bf16[512,768]{1,0:T(8,128)(2,1)} %refs_0_.1), channel_id=1, source_target_pairs={{0,1},{1,0},{2,3},{3,2},{4,5},{5,4},{6,7},{7,6},{8,9},{9,8},{10,11... | collective-permute-start | bytes 2359304 | tf_op jit(solution)/shard_map/ppermute | solution.py:27
  8.1 1.1 %copy-start.1 = (bf16[512,768]{1,0:T(8,128)(2,1)S(1)}, bf16[512,768]{1,0:T(8,128)(2,1)}, u32[]{:S(2)}) copy-start(bf16[512,768]{1,0:T(8,128)(2,1)} %refs_0_.1) | copy-start | bytes 2359300
  9.2 0.7 %copy-start.4 = (f32[64]{0:T(128)S(1)}, f32[64]{0:T(128)}, u32[]{:S(2)}) copy-start(f32[64]{0:T(128)} %param.14) | copy-start | bytes 772
  10.6 0.7 %copy-start.3 = (s32[4]{0:T(128)S(1)}, s32[4]{0:T(128)}, u32[]{:S(2)}) copy-start(s32[4]{0:T(128)} %clusters_ref) | copy-start | bytes 52
  11.8 1.4 %collective-permute-start.4 = (s32[8,128]{1,0:T(8,128)S(1)}, s32[8,128]{1,0:T(8,128)S(1)}, u32[]{:S(2)}, u32[]{:S(2)}) collective-permute-start(s32[8,128]{1,0:T(8,128)S(1)} %shard_map.84.refs_5_), channel_id=1, source_target_pairs={{0,1},{1,0},{2,3},{3,2},{4,5},{5,4},{6,7},{7,6},{8,9},{9,8},{10,11... | collective-permute-start | bytes 12296 | tf_op jit(solution)/shard_map/ppermute | solution.py:27
  13.2 7.6 %collective-permute-start.5 = (s32[8,128]{1,0:T(8,128)S(1)}, s32[8,128]{1,0:T(8,128)S(1)}, u32[]{:S(2)}, u32[]{:S(2)}) collective-permute-start(s32[8,128]{1,0:T(8,128)S(1)} %shard_map.84.refs_5_), channel_id=1, source_target_pairs={{0,2},{2,0},{4,6},{6,4},{8,10},{10,8},{12,14},{14,12},{1,3},{3,1},... | collective-permute-start | bytes 12296 | tf_op jit(solution)/shard_map/ppermute | solution.py:27
  20.8 4.5 %collective-permute-start.6 = (s32[8,128]{1,0:T(8,128)S(1)}, s32[8,128]{1,0:T(8,128)S(1)}, u32[]{:S(2)}, u32[]{:S(2)}) collective-permute-start(s32[8,128]{1,0:T(8,128)S(1)} %shard_map.84.refs_5_), channel_id=1, source_target_pairs={{0,3},{1,2},{2,1},{3,0},{4,7},{5,6},{6,5},{7,4},{8,11},{9,10},{10,... | collective-permute-start | bytes 12296 | tf_op jit(solution)/shard_map/ppermute | solution.py:33
  21.1 13.0 %collective-permute-start.9 = (bf16[1552,128]{1,0:T(8,128)(2,1)S(1)}, bf16[1552,128]{1,0:T(8,128)(2,1)S(1)}, u32[]{:S(2)}, u32[]{:S(2)}) collective-permute-start(bf16[1552,128]{1,0:T(8,128)(2,1)S(1)} %collective-permute-done.2.refs_10_), channel_id=1, source_target_pairs={{0,4},{2,6},{4,0},{6,2},{8,12},{10,14},{12,8},{14,10},{1,5},{3,7},... | collective-permute-start | bytes 1191944 | tf_op jit(solution)/shard_map/ppermute | solution.py:22
  25.8 1.8 %collective-permute-start.7 = (bf16[256,768]{1,0:T(8,128)(2,1)S(1)}, bf16[256,768]{1,0:T(8,128)(2,1)S(1)}, u32[]{:S(2)}, u32[]{:S(2)}) collective-permute-start(bf16[256,768]{1,0:T(8,128)(2,1)S(1)} %get-tuple-element.22), channel_id=1, source_target_pairs={{0,1},{1,0},{2,3},{3,2},{4,5},{5,4},{6,7},{7,6},{8,9},{9,8},{10,11... | collective-permute-start | bytes 1179656 | tf_op jit(solution)/shard_map/ppermute | solution.py:27
  25.9 2.3 %collective-permute-start.8 = (bf16[256,768]{1,0:T(8,128)(2,1)S(1)}, bf16[256,768]{1,0:T(8,128)(2,1)S(1)}, u32[]{:S(2)}, u32[]{:S(2)}) collective-permute-start(bf16[256,768]{1,0:T(8,128)(2,1)S(1)} %get-tuple-element.21), channel_id=1, source_target_pairs={{0,1},{1,0},{2,3},{3,2},{4,5},{5,4},{6,7},{7,6},{8,9},{9,8},{10,11... | collective-permute-start | bytes 1179656 | tf_op jit(solution)/shard_map/ppermute | solution.py:27
  28.1 9.7 %copy-start.5 = (s32[64]{0:T(128)S(1)}, s32[64]{0:T(128)}, u32[]{:S(2)}) copy-start(s32[64]{0:T(128)} %param.15) | copy-start | bytes 772
  35.9 2.1 %collective-permute-start.10 = (f32[4,128]{1,0:T(4,128)S(1)}, f32[4,128]{1,0:T(4,128)S(1)}, u32[]{:S(2)}, u32[]{:S(2)}) collective-permute-start(f32[4,128]{1,0:T(4,128)S(1)} %get-tuple-element.23), channel_id=1, source_target_pairs={{0,1},{1,0},{2,3},{3,2},{4,5},{5,4},{6,7},{7,6},{8,9},{9,8},{10,11... | collective-permute-start | bytes 6152 | tf_op jit(solution)/shard_map/ppermute | solution.py:27
  35.9 3.7 %collective-permute-start.11 = (f32[4,128]{1,0:T(4,128)S(1)}, f32[4,128]{1,0:T(4,128)S(1)}, u32[]{:S(2)}, u32[]{:S(2)}) collective-permute-start(f32[4,128]{1,0:T(4,128)S(1)} %get-tuple-element.25), channel_id=1, source_target_pairs={{0,2},{2,0},{4,6},{6,4},{8,10},{10,8},{12,14},{14,12},{1,3},{3,1},... | collective-permute-start | bytes 6152 | tf_op jit(solution)/shard_map/ppermute | solution.py:27
  36.7 3.0 %collective-permute-start.12 = (f32[4,128]{1,0:T(4,128)S(1)}, f32[4,128]{1,0:T(4,128)S(1)}, u32[]{:S(2)}, u32[]{:S(2)}) collective-permute-start(f32[4,128]{1,0:T(4,128)S(1)} %get-tuple-element.24), channel_id=1, source_target_pairs={{0,3},{1,2},{2,1},{3,0},{4,7},{5,6},{6,5},{7,4},{8,11},{9,10},{10,... | collective-permute-start | bytes 6152 | tf_op jit(solution)/shard_map/ppermute | solution.py:33
